TPU v7x, 32 devices: a whole 2x2x4 slice. The times are simulated.
32 devices in a mesh: groups: 1, dp: 2 (over core), expert: 16 (over z, y, x).
Axes of the slice: x: 2, y: 2, z: 4, core: 2. Of those that a mesh axis runs over, the one named last changes fastest.
Arguments:
- tokens: bfloat16 [512, 2048], P(('groups', 'dp', 'expert')), may hold values from -6 to 6
- cotangent: bfloat16 [512, 2048], P(('groups', 'dp', 'expert')), may hold values from -12 to 12
- gate_values: bfloat16 [512, 8], P(('groups', 'dp', 'expert')), may hold values from 0.049804688 to 0.29882812
- expert_ids: int32 [512, 8], P(('groups', 'dp', 'expert')), may hold values from 0 to 15, all different within a row; in each aligned block of 16 rows (0 to 15, 16 to 31, ...) at most 9 rows name the same one
- packing: int32 [512], P(('groups', 'dp', 'expert')), may hold values from -1 to 31, as said below
- w_gate: bfloat16 [16, 384, 2048], P('expert', 'dp'), may hold values from -0.125 to 0.125
- w_up: bfloat16 [16, 384, 2048], P('expert', 'dp'), may hold values from -0.125 to 0.125
- w_down: bfloat16 [16, 384, 2048], P('expert', 'dp'), may hold values from -0.3125 to 0.3125
Outputs:
- input_grad: bfloat16 [512, 2048], P(('groups', 'dp', 'expert'))
- grad_gate: bfloat16 [16, 384, 2048], P(('groups', 'expert'), 'dp')
- grad_up: bfloat16 [16, 384, 2048], P(('groups', 'expert'), 'dp')
- grad_down: bfloat16 [16, 384, 2048], P(('groups', 'expert'), 'dp')
Inputs may be any that keep to these rules, and one draw needn't show every extreme that they name: `packing`: slot value q names home row q % 16 of the dp device q // 16 with the same expert index; -1 marks an empty slot. Home rows come in groups of 8 completions that are kept or filtered together; over the devices sharing an expert index, every kept row is named exactly once and filtered rows never; the i-th kept row, in home order, goes to slot i // 2 of dp device i % 2, so empty slots come last on each device. `expert_ids`: in the 16 rows of one device, no expert is named by more than 9 rows, a bound that some block reaches.
All inputs are finite; a program needn't handle non-finite values.
Results may differ from a plain program's by a relative error of at most 0.0072.
Values may be sent and summed in bfloat16 or wider, within the bound.
No kernel may reach another device: no remote copies, remote signals or barrier semaphores. Data moves between devices by JAX's collectives and lax.ppermute only.
A program may use at most 64 MiB of HBM per device.

v0:
```python
import jax
import jax.numpy as jnp
from jax import lax
from jax.sharding import PartitionSpec as P


def slot_table(route_ids, route_gates, expert_count, capacity):
    row_count, top_count = route_ids.shape
    flat_ids = route_ids.reshape(-1)
    labels = jnp.arange(expert_count, dtype=jnp.int32)
    onehot = (flat_ids[:, None] == labels[None, :]).astype(jnp.int32)
    earlier = jnp.cumsum(onehot, axis=0) - onehot
    rank_in = jnp.sum(earlier * onehot, axis=1)
    position = flat_ids * capacity + rank_in
    places = jnp.arange(expert_count * capacity, dtype=jnp.int32)
    matched = places[:, None] == position[None, :]
    owner_row = jnp.arange(row_count * top_count, dtype=jnp.int32) // top_count
    occupied = jnp.any(matched, axis=1)
    slot_row = jnp.sum(jnp.where(matched, owner_row[None, :], 0), axis=1)
    flat_gates = route_gates.reshape(-1).astype(jnp.float32)
    slot_gate = jnp.sum(jnp.where(matched, flat_gates[None, :], 0.0), axis=1)
    return (position.reshape(row_count, top_count), occupied, slot_row, slot_gate)


def pick_rows(slot_lists, pooled):
    sources = jnp.arange(pooled.shape[0], dtype=jnp.int32)
    choose = (slot_lists[:, None] == sources[None, :]).astype(jnp.bfloat16)
    return jnp.dot(choose, pooled, preferred_element_type=jnp.float32).astype(jnp.bfloat16)


def fill_slots(rebal_rows, rebal_upstream, occupied, slot_row, slot_gate):
    send_rows = jnp.where(occupied[:, None], rebal_rows[slot_row], jnp.zeros((), jnp.bfloat16))
    scaled = slot_gate[:, None] * rebal_upstream[slot_row].astype(jnp.float32)
    send_upstream = jnp.where(occupied[:, None], scaled, 0.0).astype(jnp.bfloat16)
    return (send_rows, send_upstream)


def expert_terms(inputs, upstream, gate_mat, up_mat, down_mat):
    gate_pre = jnp.dot(inputs, gate_mat.T, preferred_element_type=jnp.float32)
    up_pre = jnp.dot(inputs, up_mat.T, preferred_element_type=jnp.float32)
    sigmoid_val = jax.nn.sigmoid(gate_pre)
    activated = gate_pre * sigmoid_val
    hidden = (activated * up_pre).astype(jnp.bfloat16)
    hidden_grad = jnp.dot(upstream, down_mat.T, preferred_element_type=jnp.float32)
    silu_slope = sigmoid_val * (1.0 + gate_pre * (1.0 - sigmoid_val))
    gate_grad = (hidden_grad * up_pre * silu_slope).astype(jnp.bfloat16)
    up_grad = (hidden_grad * activated).astype(jnp.bfloat16)
    weight_grads = (
        jnp.dot(gate_grad.T, inputs, preferred_element_type=jnp.float32).astype(jnp.bfloat16)[None],
        jnp.dot(up_grad.T, inputs, preferred_element_type=jnp.float32).astype(jnp.bfloat16)[None],
        jnp.dot(hidden.T, upstream, preferred_element_type=jnp.float32).astype(jnp.bfloat16)[None],
    )
    partial_grad = jnp.dot(gate_grad, gate_mat, preferred_element_type=jnp.float32)
    partial_grad = partial_grad + jnp.dot(up_grad, up_mat, preferred_element_type=jnp.float32)
    return (weight_grads, partial_grad)


def local(tokens, cotangent, gate_values, expert_ids, packing, w_gate, w_up, w_down):
    row_count, top_count = expert_ids.shape
    model_width = tokens.shape[1]
    dp_size = lax.axis_size("dp")
    expert_count = lax.axis_size("expert") * w_gate.shape[0]
    capacity = min(row_count, max(2, row_count * top_count // expert_count + 1))
    gate_mat = w_gate[0]
    up_mat = w_up[0]
    down_mat = w_down[0]
    pooled_rows, pooled_upstream, pooled_gates = (
        lax.all_gather(tokens, "dp", axis=0, tiled=True),
        lax.all_gather(cotangent, "dp", axis=0, tiled=True),
        lax.all_gather(gate_values, "dp", axis=0, tiled=True),
    )
    lists_all, pooled_ids = (
        lax.all_gather(packing, "dp", axis=0, tiled=True),
        lax.all_gather(expert_ids, "dp", axis=0, tiled=True),
    )
    member_rows = []
    member_upstream = []
    member_positions = []
    for member in range(dp_size):
        low = member * row_count
        slot_lists = lists_all[low : low + row_count]
        position, occupied, slot_row, slot_gate = slot_table(
            pooled_ids[low : low + row_count],
            pooled_gates[low : low + row_count],
            expert_count,
            capacity,
        )
        send_rows, send_upstream = fill_slots(
            pick_rows(slot_lists, pooled_rows),
            pick_rows(slot_lists, pooled_upstream),
            occupied,
            slot_row,
            slot_gate,
        )
        member_rows.append(send_rows.reshape(expert_count, capacity * model_width))
        member_upstream.append(send_upstream.reshape(expert_count, capacity * model_width))
        member_positions.append(position)
    own_position = jnp.stack(member_positions)[lax.axis_index("dp")]
    send_rows = jnp.concatenate(member_rows, axis=1).reshape(
        expert_count * dp_size * capacity, model_width
    )
    send_upstream = jnp.concatenate(member_upstream, axis=1).reshape(
        expert_count * dp_size * capacity, model_width
    )
    recv_rows, recv_upstream = (
        lax.all_to_all(send_rows, "expert", split_axis=0, concat_axis=0, tiled=True),
        lax.all_to_all(send_upstream, "expert", split_axis=0, concat_axis=0, tiled=True),
    )
    weight_grads, partial_grad = expert_terms(recv_rows, recv_upstream, gate_mat, up_mat, down_mat)
    summed = lax.psum_scatter(
        partial_grad.reshape(expert_count, dp_size * capacity * model_width).astype(jnp.bfloat16),
        "dp",
        scatter_dimension=1,
        tiled=True,
    ).astype(jnp.float32)
    slot_grad = summed.reshape(expert_count * capacity, model_width).astype(jnp.bfloat16)
    returned = lax.all_to_all(slot_grad, "expert", split_axis=0, concat_axis=0, tiled=True)
    rebal_grad = jnp.sum(returned[own_position].astype(jnp.float32), axis=1).astype(jnp.bfloat16)
    pooled_grad = lax.all_gather(rebal_grad, "dp", axis=0, tiled=True)
    home_index = lax.axis_index("dp") * row_count + jnp.arange(row_count, dtype=jnp.int32)
    choose = (lists_all[None, :] == home_index[:, None]).astype(jnp.bfloat16)
    input_grad = jnp.dot(choose, pooled_grad, preferred_element_type=jnp.float32).astype(
        jnp.bfloat16
    )
    return (input_grad, weight_grads[0], weight_grads[1], weight_grads[2])


def solution(mesh):
    in_specs = (
        P(("groups", "dp", "expert"), None),
        P(("groups", "dp", "expert"), None),
        P(("groups", "dp", "expert"), None),
        P(("groups", "dp", "expert"), None),
        P(("groups", "dp", "expert")),
        P("expert", "dp", None),
        P("expert", "dp", None),
        P("expert", "dp", None),
    )
    out_specs = (
        P(("groups", "dp", "expert"), None),
        P(("groups", "expert"), "dp", None),
        P(("groups", "expert"), "dp", None),
        P(("groups", "expert"), "dp", None),
    )
    return jax.shard_map(local, mesh=mesh, in_specs=in_specs, out_specs=out_specs, check_vma=False)
```

profile of v0, /device:TPU:0, one launch (start us, length us, event | category | flops | bytes accessed | tf_op | source)
XLA Modules:
  0.0 170.8 jit_solution(8412146137536812544)
XLA Ops:
  10.0 1.9 %all-reduce = s32[32]{0:T(128)S(1)} all-reduce(s32[32]{0:T(128)S(1)} %dynamic-update-slice), channel_id=1, replica_groups=mesh['groups'=1,'dp'=2,'expert'=16] {'dp'}, use_global_device_ids=true, to_apply=%add | all-reduce | flops 32 | bytes 256
  12.0 2.0 %all-gather = s32[2,16,8]{1,2,0:T(8,128)S(1)} all-gather(s32[1,16,8]{1,2,0:T(8,128)} %bitcast.63), channel_id=1, replica_groups=mesh['groups'=1,'dp'=2,'expert'=16] {'dp'}, dimensions={0}, use_global_device_ids=true | all-gather | bytes 1536 | tf_op jit(solution)/shard_map/all_gather | solution.py:74
  16.3 2.1 %all_gather.22 = bf16[32,2048]{1,0:T(8,128)(2,1)S(1)} all-gather(bf16[16,2048]{1,0:T(8,128)(2,1)} %param.8), channel_id=1, replica_groups=mesh['groups'=1,'dp'=2,'expert'=16] {'dp'}, dimensions={0}, use_global_device_ids=true | all-gather | bytes 196608 | tf_op jit(solution)/shard_map/all_gather | solution.py:68
  21.7 1.6 pad_maximum_fusion.1
  23.3 8.3 %all-to-all-start.1 = ((bf16[16,18,2048]{2,1,0:T(8,128)(2,1)}), bf16[16,18,2048]{2,1,0:T(8,128)(2,1)}, u32[]{:S(2)}, u32[]{:S(2)}) async-start(bf16[16,18,2048]{2,1,0:T(8,128)(2,1)} %pad_maximum_fusion.1), calls=%async_computation.1 | async-start | bytes 3145728 | tf_op jit(solution)/shard_map/all_to_all | solution.py:106
  31.6 1.8 %all-gather.1 = bf16[2,16,8]{1,2,0:T(8,128)(2,1)S(1)} all-gather(bf16[1,16,8]{1,2,0:T(8,128)(2,1)S(1)} %bitcast.68), channel_id=1, replica_groups=mesh['groups'=1,'dp'=2,'expert'=16] {'dp'}, dimensions={0}, use_global_device_ids=true | all-gather | bytes 768 | tf_op jit(solution)/shard_map/all_gather | solution.py:70
  34.2 1.9 %all_gather.21 = bf16[32,2048]{1,0:T(8,128)(2,1)S(1)} all-gather(bf16[16,2048]{1,0:T(8,128)(2,1)S(1)} %copy-done.6), channel_id=1, replica_groups=mesh['groups'=1,'dp'=2,'expert'=16] {'dp'}, dimensions={0}, use_global_device_ids=true | all-gather | bytes 196608 | tf_op jit(solution)/shard_map/all_gather | solution.py:69
  38.9 1.5 reshape.192
  40.6 1.8 %select_convert_fusion = bf16[16,9,2048]{2,1,0:T(8,128)(2,1)S(1)} fusion(f32[16,9,2048]{2,1,0:T(8,128)} %reshape.192, f32[16,9]{1,0:T(8,128)S(1)} %mul.84, pred[16,9]{1,0:T(8,128)(4,1)S(1)} %broadcast_in_dim.119), kind=kLoop, calls=%fused_computation.18 | loop fusion | flops 884736 | bytes 1770192 | tf_op jit(solution)/shard_map/convert_element_type | solution.py:34
  42.7 1.6 pad_maximum_fusion
  44.3 21.6 %all-to-all-done.1 = bf16[16,18,2048]{2,1,0:T(8,128)(2,1)} async-done(((bf16[16,18,2048]{2,1,0:T(8,128)(2,1)}), bf16[16,18,2048]{2,1,0:T(8,128)(2,1)}, u32[]{:S(2)}, u32[]{:S(2)}) %all-to-all-start.1) | async-done | bytes 1179680 | tf_op jit(solution)/shard_map/all_to_all | solution.py:106
  65.9 8.1 %all-to-all-start = ((bf16[16,18,2048]{2,1,0:T(8,128)(2,1)}), bf16[16,18,2048]{2,1,0:T(8,128)(2,1)S(1)}, u32[]{:S(2)}, u32[]{:S(2)}) async-start(bf16[16,18,2048]{2,1,0:T(8,128)(2,1)} %pad_maximum_fusion), calls=%async_computation | async-start | bytes 3145728 | tf_op jit(solution)/shard_map/all_to_all | solution.py:107
  74.1 1.6 all_to_all.21
  78.1 29.4 %all-to-all-done = bf16[16,18,2048]{2,1,0:T(8,128)(2,1)S(1)} async-done(((bf16[16,18,2048]{2,1,0:T(8,128)(2,1)}), bf16[16,18,2048]{2,1,0:T(8,128)(2,1)S(1)}, u32[]{:S(2)}, u32[]{:S(2)}) %all-to-all-start) | async-done | bytes 1179680 | tf_op jit(solution)/shard_map/all_to_all | solution.py:107
  108.7 2.1 %multiply_convert_fusion.1 = (bf16[288,192]{1,0:T(8,128)(2,1)S(1)}, bf16[288,192]{1,0:T(8,128)(2,1)S(1)}) fusion(f32[288,192]{1,0:T(8,128)} %fusion.6, f32[288,192]{1,0:T(8,128)} %fusion.9, bf16[288,2048]{1,0:T(8,128)(2,1)} %all_to_all.19, bf16[1,192,2048]{2,1,0:T(8,128)(2,1)} %param.15), kind=kOutput, calls=%fused_computation.35 | convolution fusion | flops 227211264 | bytes 2629632 | tf_op jit(solution)/shard_map/dot_general | solution.py:44
  112.5 2.7 %convert_element_type.123 = bf16[16,36864]{1,0:T(8,128)(2,1)} reshape(bf16[288,2048]{1,0:T(8,128)(2,1)S(1)} %fusion) | data formatting | bytes 2359296 | tf_op jit(solution)/shard_map/convert_element_type | solution.py:111
  115.6 10.2 %reduce-scatter.2.cloned.1.call-done = bf16[16,18432]{1,0:T(8,128)(2,1)} async-done(((bf16[16,36864]{1,0:T(8,128)(2,1)}), bf16[16,18432]{1,0:T(8,128)(2,1)}) %reduce-scatter.2.cloned.1.call-update) | async-done | bytes 589840 | tf_op jit(solution)/shard_map/reduce_scatter | solution.py:110
  125.8 2.4 %convert_element_type.124 = bf16[16,9,2048]{2,1,0:T(8,128)(2,1)} reshape(bf16[16,18432]{1,0:T(8,128)(2,1)} %reduce-scatter.2.cloned.1.call-done) | data formatting | bytes 1179648 | tf_op jit(solution)/shard_map/convert_element_type | solution.py:116
  128.2 6.8 %all-to-all-start.2 = ((bf16[16,9,2048]{2,1,0:T(8,128)(2,1)}), bf16[16,9,2048]{2,1,0:T(8,128)(2,1)S(1)}, u32[]{:S(2)}, u32[]{:S(2)}) async-start(bf16[16,9,2048]{2,1,0:T(8,128)(2,1)} %convert_element_type.124), calls=%async_computation.3 | async-start | bytes 2097152 | tf_op jit(solution)/shard_map/all_to_all | solution.py:117
  135.2 1.5 fusion.2
  136.7 1.5 fusion.1
  138.2 1.5 fusion.3
  139.7 19.9 %all-to-all-done.2 = bf16[16,9,2048]{2,1,0:T(8,128)(2,1)S(1)} async-done(((bf16[16,9,2048]{2,1,0:T(8,128)(2,1)}), bf16[16,9,2048]{2,1,0:T(8,128)(2,1)S(1)}, u32[]{:S(2)}, u32[]{:S(2)}) %all-to-all-start.2) | async-done | bytes 589856 | tf_op jit(solution)/shard_map/all_to_all | solution.py:117
  161.2 1.9 %all_gather.23 = bf16[32,2048]{1,0:T(8,128)(2,1)S(1)} all-gather(bf16[16,2048]{1,0:T(8,128)(2,1)S(1)} %bitcast_reduce_fusion), channel_id=1, replica_groups=mesh['groups'=1,'dp'=2,'expert'=16] {'dp'}, dimensions={0}, use_global_device_ids=true | all-gather | bytes 196608 | tf_op jit(solution)/shard_map/all_gather | solution.py:119
  (118 shorter events, 19.7 us)
Async XLA Ops:
  7.2 68.5 %copy-start = (bf16[1,192,2048]{2,1,0:T(8,128)(2,1)S(1)}, bf16[1,192,2048]{2,1,0:T(8,128)(2,1)}, u32[]{:S(2)}) copy-start(bf16[1,192,2048]{2,1,0:T(8,128)(2,1)} %param.13) | copy-start | bytes 2359300
  11.9 2.1 %copy-start.13 = (s32[32]{0:T(128)}, s32[32]{0:T(128)S(1)}, u32[]{:S(2)}) copy-start(s32[32]{0:T(128)S(1)} %all-reduce) | copy-start | bytes 388
  12.0 7.8 %copy-start.9 = (s32[16]{0:T(128)}, s32[16]{0:T(128)S(1)}, u32[]{:S(2)}) copy-start(s32[16]{0:T(128)S(1)} %get-tuple-element.15) | copy-start | bytes 196
  12.0 7.8 %copy-start.11 = (s32[16]{0:T(128)}, s32[16]{0:T(128)S(1)}, u32[]{:S(2)}) copy-start(s32[16]{0:T(128)S(1)} %get-tuple-element.14) | copy-start | bytes 196
  14.8 5.1 %copy-start.22 = (s32[128]{0:T(128)}, s32[128]{0:T(128)S(1)}, u32[]{:S(2)}) copy-start(s32[128]{0:T(128)S(1)} %multiply_add_fusion.1) | copy-start | bytes 1540
  15.8 2.8 %copy-start.15 = (s32[128]{0:T(128)}, s32[128]{0:T(128)S(1)}, u32[]{:S(2)}) copy-start(s32[128]{0:T(128)S(1)} %select_reduce_fusion.4) | copy-start | bytes 1540
  15.8 2.8 %copy-start.17 = (s32[128]{0:T(128)}, s32[128]{0:T(128)S(1)}, u32[]{:S(2)}) copy-start(s32[128]{0:T(128)S(1)} %get-tuple-element.17) | copy-start | bytes 1540
  16.3 3.9 %copy-start.7 = (s32[1024]{0:T(1024)}, s32[1024]{0:T(1024)S(1)}, u32[]{:S(2)}) copy-start(s32[1024]{0:T(1024)S(1)} %pad_clamp_fusion.1) | copy-start | bytes 12292
  16.3 2.6 %copy-start.8 = (s32[1024]{0:T(1024)}, s32[1024]{0:T(1024)S(1)}, u32[]{:S(2)}) copy-start(s32[1024]{0:T(1024)S(1)} %pad_clamp_fusion.2) | copy-start | bytes 12292
  23.3 8.4 %copy-start.21 = (bf16[16,8]{0,1:T(8,128)(2,1)S(1)}, bf16[16,8]{0,1:T(8,128)(2,1)}, u32[]{:S(2)}) copy-start(bf16[16,8]{0,1:T(8,128)(2,1)} %param.10) | copy-start | bytes 772
  23.3 10.5 %copy-start.23 = (s32[128]{0:T(128)S(1)}, s32[128]{0:T(128)}, u32[]{:S(2)}) copy-start(s32[128]{0:T(128)} %copy-done.22) | copy-start | bytes 1540
  23.3 10.7 %copy-start.18 = (s32[128]{0:T(128)S(1)}, s32[128]{0:T(128)}, u32[]{:S(2)}) copy-start(s32[128]{0:T(128)} %copy-done.17) | copy-start | bytes 1540
  23.3 10.9 %copy-start.6 = (bf16[16,2048]{1,0:T(8,128)(2,1)S(1)}, bf16[16,2048]{1,0:T(8,128)(2,1)}, u32[]{:S(2)}) copy-start(bf16[16,2048]{1,0:T(8,128)(2,1)} %param.9) | copy-start | bytes 196612
  23.3 12.8 %copy-start.12 = (s32[16]{0:T(128)S(1)}, s32[16]{0:T(128)}, u32[]{:S(2)}) copy-start(s32[16]{0:T(128)} %copy-done.11) | copy-start | bytes 196
  23.3 42.7 %all-to-all-start.1 = ((bf16[16,18,2048]{2,1,0:T(8,128)(2,1)}), bf16[16,18,2048]{2,1,0:T(8,128)(2,1)}, u32[]{:S(2)}, u32[]{:S(2)}) async-start(bf16[16,18,2048]{2,1,0:T(8,128)(2,1)} %pad_maximum_fusion.1), calls=%async_computation.1 | async-start | bytes 3145728 | tf_op jit(solution)/shard_map/all_to_all | solution.py:106
  65.9 41.6 %all-to-all-start = ((bf16[16,18,2048]{2,1,0:T(8,128)(2,1)}), bf16[16,18,2048]{2,1,0:T(8,128)(2,1)S(1)}, u32[]{:S(2)}, u32[]{:S(2)}) async-start(bf16[16,18,2048]{2,1,0:T(8,128)(2,1)} %pad_maximum_fusion), calls=%async_computation | async-start | bytes 3145728 | tf_op jit(solution)/shard_map/all_to_all | solution.py:107
  74.0 51.7 %reduce-scatter.2.cloned.1.call-start = ((), (), s32[]{:S(2)}) async-start(), calls=%async_computation.4 | async-start | bytes 1769472 | tf_op jit(solution)/shard_map/reduce_scatter | solution.py:110
  112.5 2.8 %copy-start.20 = (s32[128]{0:T(128)S(1)}, s32[128]{0:T(128)}, u32[]{:S(2)}) copy-start(s32[128]{0:T(128)} %copy-done.19) | copy-start | bytes 1540
  112.5 2.9 %copy-start.16 = (s32[128]{0:T(128)S(1)}, s32[128]{0:T(128)}, u32[]{:S(2)}) copy-start(s32[128]{0:T(128)} %copy-done.15) | copy-start | bytes 1540
  128.2 31.5 %all-to-all-start.2 = ((bf16[16,9,2048]{2,1,0:T(8,128)(2,1)}), bf16[16,9,2048]{2,1,0:T(8,128)(2,1)S(1)}, u32[]{:S(2)}, u32[]{:S(2)}) async-start(bf16[16,9,2048]{2,1,0:T(8,128)(2,1)} %convert_element_type.124), calls=%async_computation.3 | async-start | bytes 2097152 | tf_op jit(solution)/shard_map/all_to_all | solution.py:117
  136.7 1.5 copy-start.3
  136.7 1.5 copy-start.4
  136.7 1.5 copy-start.5
  159.9 3.2 %copy-start.14 = (s32[32]{0:T(128)S(1)}, s32[32]{0:T(128)}, u32[]{:S(2)}) copy-start(s32[32]{0:T(128)} %copy-done.13) | copy-start | bytes 388
  (4 other events, 4.1 us)
Sparse Core Ops, SparseCore 0:
  115.4 10.3 reduce-scatter.1
where the time goes:
time: 172 us; the launch traced here: 171 us
  waiting for transfers between devices  81.2 us (47%)
  starting transfers between devices  23.3 us (14%)
  local copies, waits for them, and re-layouts  20.5 us (12%)
  between operations  15.2 us (9%)
  blocking collectives  11.6 us (7%)
  matrix products  11.6 us (7%)
  other arithmetic  7.45 us (4%)
    all_to_all x1, waiting for transfers between devices, local(): lax.all_to_all(send_upstream, 'expert', split_axis=0, concat_axis=0, tile...  29.4 us
    all_to_all x1, waiting for transfers between devices, local(): lax.all_to_all(send_rows, 'expert', split_axis=0, concat_axis=0, tiled=True)  21.6 us
    all_to_all x1, waiting for transfers between devices, local(): lax.all_to_all(slot_grad, 'expert', split_axis=0, concat_axis=0, tiled=True)  19.9 us
    reduce_scatter x1, waiting for transfers between devices, local(): lax.psum_scatter(partial_grad.reshape(expert_count, dp_size * capacity *...  10.2 us
    all_to_all x1, starting transfers between devices, local(): lax.all_to_all(send_rows, 'expert', split_axis=0, concat_axis=0, tiled=True)  8.34 us
    all_to_all x1, starting transfers between devices, local(): lax.all_to_all(send_upstream, 'expert', split_axis=0, concat_axis=0, tile...  8.07 us
    all_to_all x1, starting transfers between devices, local(): lax.all_to_all(slot_grad, 'expert', split_axis=0, concat_axis=0, tiled=True)  6.8 us
  transfers between devices with their start and end apart: 4, of which 4 were waited for; matrix products, arithmetic and copies ran while one was open for 10% of the time, Pallas kernels for 0%

commit v1 on v0

--- a/solution.py
+++ b/solution.py
@@ -55,7 +55,7 @@
     return (weight_grads, partial_grad)
 
 
-def local(tokens, cotangent, gate_values, expert_ids, packing, w_gate, w_up, w_down):
+def routed_local(tokens, cotangent, gate_values, expert_ids, packing, w_gate, w_up, w_down):
     row_count, top_count = expert_ids.shape
     model_width = tokens.shape[1]
     dp_size = lax.axis_size("dp")
@@ -125,6 +125,77 @@
     return (input_grad, weight_grads[0], weight_grads[1], weight_grads[2])
 
 
+def home_gates(packing, expert_ids, gate_values, dp_size, expert_count):
+    top = expert_ids.shape[1]
+    here = lax.axis_index("expert")
+    own = jnp.where(expert_ids == here, gate_values.astype(jnp.float32), 0.0)
+    slot_gate = jnp.sum(own, axis=1)
+    pair = lambda flat: flat.reshape(dp_size, expert_count, -1).transpose(1, 0, 2).reshape(expert_count, -1)
+    lists = pair(packing)
+    by_slot = pair(slot_gate)
+    pair_rows = lists.shape[1]
+    homes = jnp.arange(pair_rows, dtype=jnp.int32)
+    matched = lists[:, None, :] == homes[None, :, None]
+    by_home = jnp.sum(jnp.where(matched, by_slot[:, None, :], 0.0), axis=2)
+    return by_home.reshape(expert_count, dp_size, -1).transpose(1, 0, 2).reshape(-1)
+
+
+def dense_local(tokens, cotangent, gate_values, expert_ids, packing, w_gate, w_up, w_down):
+    row_count, top = expert_ids.shape
+    dp_size = lax.axis_size("dp")
+    devices = lax.axis_size("expert")
+    axes = ("dp", "expert")
+    gate_mat, up_mat, down_mat = w_gate[0], w_up[0], w_down[0]
+    routing = jnp.concatenate(
+        [
+            gate_values,
+            expert_ids.astype(jnp.bfloat16),
+            packing[:, None].astype(jnp.bfloat16),
+        ],
+        axis=1,
+    )
+    routing = lax.all_gather(routing, axes, axis=0, tiled=True)
+    inputs = lax.all_gather(tokens, axes, axis=0, tiled=True)
+    upstream = lax.all_gather(cotangent, axes, axis=0, tiled=True)
+    gates = home_gates(
+        routing[:, 2 * top].astype(jnp.int32),
+        routing[:, top : 2 * top].astype(jnp.int32),
+        routing[:, :top],
+        dp_size,
+        devices,
+    )[:, None]
+    gate_pre = jnp.dot(inputs, gate_mat.T, preferred_element_type=jnp.float32)
+    up_pre = jnp.dot(inputs, up_mat.T, preferred_element_type=jnp.float32)
+    hidden_grad = gates * jnp.dot(upstream, down_mat.T, preferred_element_type=jnp.float32)
+    sigmoid_val = jax.nn.sigmoid(gate_pre)
+    activated = gate_pre * sigmoid_val
+    hidden = (gates * activated * up_pre).astype(jnp.bfloat16)
+    silu_slope = sigmoid_val * (1.0 + gate_pre * (1.0 - sigmoid_val))
+    gate_grad = (hidden_grad * up_pre * silu_slope).astype(jnp.bfloat16)
+    up_grad = (hidden_grad * activated).astype(jnp.bfloat16)
+    partial_grad = jnp.dot(gate_grad, gate_mat, preferred_element_type=jnp.float32)
+    partial_grad = partial_grad + jnp.dot(up_grad, up_mat, preferred_element_type=jnp.float32)
+    input_grad = lax.psum_scatter(
+        partial_grad.astype(jnp.bfloat16), axes, scatter_dimension=0, tiled=True
+    )
+    weight_grads = [
+        jnp.dot(grad.T, rows, preferred_element_type=jnp.float32).astype(jnp.bfloat16)[None]
+        for grad, rows in ((gate_grad, inputs), (up_grad, inputs), (hidden, upstream))
+    ]
+    return (input_grad, *weight_grads)
+
+
+def local(tokens, cotangent, gate_values, expert_ids, packing, w_gate, w_up, w_down):
+    row_count, top = expert_ids.shape
+    expert_count = lax.axis_size("expert") * w_gate.shape[0]
+    capacity = min(row_count, max(2, row_count * top // expert_count + 1))
+    few = capacity * 4 <= row_count
+    chosen = routed_local if few else dense_local
+    return chosen(
+        tokens, cotangent, gate_values, expert_ids, packing, w_gate, w_up, w_down
+    )
+
+
 def solution(mesh):
     in_specs = (
         P(("groups", "dp", "expert"), None),

time: 172 us -> 283 us (1.65)
  waiting for transfers between devices: 81.2 us -> 178 us
  blocking collectives: 11.6 us -> 71 us
  starting transfers between devices: 23.3 us -> 0.11 us
  local copies, waits for them, and re-layouts: 20.5 us -> 1.57 us
  other arithmetic: 7.45 us -> 2.62 us
  matrix products: 11.6 us -> 15.1 us
    reduce_scatter x1, waiting for transfers between devices: 10.2 us -> 136 us  [dense_local(): lax.psum_scatter(partial_grad.astype(jnp.bfloat16), axes, scatter_dimensi...]
    all_to_all x3 -> x0, waiting for transfers between devices: 71 us -> none  [the longest x1 29.4 us: local(): lax.all_to_all(send_upstream, 'expert', split_axis=0, concat_axis=0, tile...]
    all_gather x5 -> x1, blocking collectives: 9.66 us -> 71 us  [dense_local(): routing = lax.all_gather(routing, axes, axis=0, tiled=True)]
    all_gather x0 -> x2, waiting for transfers between devices: none -> 40.6 us  [the longest x1 40.6 us: dense_local(): upstream = lax.all_gather(cotangent, axes, axis=0, tiled=True)]
    all_to_all x3 -> x0, starting transfers between devices: 23.2 us -> none  [the longest x1 8.34 us: local(): lax.all_to_all(send_rows, 'expert', split_axis=0, concat_axis=0, tiled=True)]
    convert_element_type x8 -> x0, local copies, waits for them, and re-layouts: 7.16 us -> none  [the longest x1 2.73 us: local(): partial_grad.reshape(expert_count, dp_size * capacity * model_width)]
    gather x7 -> x0, local copies, waits for them, and re-layouts: 5.79 us -> none  [the longest x4 2.46 us: fill_slots(): rebal_rows[slot_row]]
    dot_general x13 -> x8, matrix products: 11.6 us -> 15.1 us  [the longest x3 4.43 us: dense_local(): jnp.dot(grad.T, rows, preferred_element_type=jnp.float32)]
  transfers between devices with their start and end apart: 4 -> 3, of which waited for: 4 -> 2; matrix products, arithmetic and copies ran while one was open for 10% -> 4% of each run, Pallas kernels for 0% -> 0%
where the time goes in v1:
time: 283 us
  waiting for transfers between devices  178 us (63%)
  blocking collectives  71 us (25%)
  matrix products  15.1 us (5%)
  between operations  13.8 us (5%)
    reduce_scatter x1, waiting for transfers between devices, dense_local(): lax.psum_scatter(partial_grad.astype(jnp.bfloat16), axes, scatter_dimensi...  136 us
    all_gather x1, blocking collectives, dense_local(): routing = lax.all_gather(routing, axes, axis=0, tiled=True)  71 us
    all_gather x1, waiting for transfers between devices, dense_local(): upstream = lax.all_gather(cotangent, axes, axis=0, tiled=True)  40.6 us
  transfers between devices with their start and end apart: 3, of which 2 were waited for; matrix products, arithmetic and copies ran while one was open for 4% of the time, Pallas kernels for 0%

profile of v1, /device:TPU:0, one launch (start us, length us, event | category | flops | bytes accessed | tf_op | source)
XLA Modules:
  0.0 282.7 jit_solution(6875974394089522797)
XLA Ops:
  7.2 0.7 all-gather.5.cloned.1.call-update
  8.0 0.7 all-gather.3.cloned.1.call-update
  8.7 0.7 convert_element_type.41
  9.4 0.7 convert_bitcast_fusion
  10.1 0.7 pad_maximum_fusion
  10.8 0.1 copy.34
  10.8 71.0 %all_gather.9 = bf16[512,17]{1,0:T(8,128)(2,1)S(1)} all-gather(bf16[16,17]{1,0:T(8,128)(2,1)S(1)} %copy.34), channel_id=1, replica_groups=mesh['groups'=1,'dp'=2,'expert'=16] {'dp','expert'}, dimensions={0}, use_global_device_ids=true | all-gather | bytes 17952 | tf_op jit(solution)/shard_map/all_gather | solution.py:157
  81.9 0.2 convert_reduce_fusion
  82.3 0.2 select_reduce_fusion.1
  82.7 0.1 select_reduce_fusion
  83.1 3.3 %fusion.5 = f32[512,192]{0,1:T(8,128)} fusion(bf16[512,2048]{1,0:T(8,128)(2,1)} %all-gather.5.cloned.1.call-done, bf16[1,192,2048]{2,1,0:T(8,128)(2,1)S(1)} %copy-done), kind=kOutput, calls=%fused_computation.10 | convolution fusion | flops 402653184 | bytes 3276800 | tf_op jit(solution)/shard_map/dot_general | solution.py:167
  86.4 1.6 fusion.8
  88.0 40.6 %all-gather.3.cloned.1.call-done = bf16[512,2048]{1,0:T(8,128)(2,1)} async-done(((bf16[16,2048]{1,0:T(8,128)(2,1)}), bf16[512,2048]{1,0:T(8,128)(2,1)}) %all-gather.3.cloned.1.call-update) | async-done | bytes 2097168 | tf_op jit(solution)/shard_map/all_gather | solution.py:159
  128.6 2.9 %multiply_convert_fusion.1 = (bf16[512,192]{0,1:T(8,128)(2,1)S(1)}, bf16[512,192]{0,1:T(8,128)(2,1)S(1)}) fusion(f32[512,192]{0,1:T(8,128)} %fusion.5, f32[512,192]{0,1:T(8,128)} %fusion.8, bf16[512,2048]{1,0:T(8,128)(2,1)} %all-gather.3.cloned.1.call-done, bf16[1,192,2048]{2,1,0:T(8,128)(2,1)} %param.15, f32[512]{0:T(512)S(1)} %mul.37), kind=kOutput, calls=%fused_computation.17 | convolution fusion | flops 404029440 | bytes 4065280 | tf_op jit(solution)/shard_map/dot_general | solution.py:169
  131.5 0.8 fusion.3
  132.3 0.4 copy-done.3
  132.7 2.1 add_convert_fusion
  134.8 1.5 fusion.1
  136.2 1.5 fusion
  137.7 0.2 copy-done.4
  137.9 0.3 copy-done.5
  138.1 0.1 copy-done.6
  138.2 1.5 fusion.2
  139.8 136.4 %reduce-scatter.2.cloned.1.call-done = bf16[16,2048]{1,0:T(8,128)(2,1)} async-done(((bf16[512,2048]{1,0:T(8,128)(2,1)}), bf16[16,2048]{1,0:T(8,128)(2,1)}) %reduce-scatter.2.cloned.1.call-update) | async-done | bytes 65552 | tf_op jit(solution)/shard_map/reduce_scatter | solution.py:178
  (24 shorter events, 0.7 us)
Async XLA Ops:
  7.2 75.9 %copy-start = (bf16[1,192,2048]{2,1,0:T(8,128)(2,1)S(1)}, bf16[1,192,2048]{2,1,0:T(8,128)(2,1)}, u32[]{:S(2)}) copy-start(bf16[1,192,2048]{2,1,0:T(8,128)(2,1)} %param.13) | copy-start | bytes 2359300
  7.2 75.8 %all-gather.5.cloned.1.call-start = ((), (), s32[]{:S(2)}) async-start(), calls=%async_computation.2 | async-start | bytes 2162688 | tf_op jit(solution)/shard_map/all_gather | solution.py:158
  7.9 120.7 %all-gather.3.cloned.1.call-start = ((), (), s32[]{:S(2)}) async-start(), calls=%async_computation.1 | async-start | bytes 2162688 | tf_op jit(solution)/shard_map/all_gather | solution.py:159
  8.7 267.5 %reduce-scatter.2.cloned.1.call-start = ((), (), s32[]{:S(2)}) async-start(), calls=%async_computation.3 | async-start | bytes 2162688 | tf_op jit(solution)/shard_map/reduce_scatter | solution.py:178
  83.0 3.4 %copy-start.1 = (bf16[512,2048]{1,0:T(8,128)(2,1)S(1)}, bf16[512,2048]{1,0:T(8,128)(2,1)}, u32[]{:S(2)}) copy-start(bf16[512,2048]{1,0:T(8,128)(2,1)} %all-gather.5.cloned.1.call-done) | copy-start | bytes 6291460
  83.0 3.4 %copy-start.2 = (bf16[1,192,2048]{2,1,0:T(8,128)(2,1)S(1)}, bf16[1,192,2048]{2,1,0:T(8,128)(2,1)}, u32[]{:S(2)}) copy-start(bf16[1,192,2048]{2,1,0:T(8,128)(2,1)} %param.14) | copy-start | bytes 2359300
  131.5 1.1 copy-start.3
  136.2 1.6 copy-start.4
  136.2 1.9 copy-start.5
  136.2 2.0 copy-start.6
Sparse Core Ops, SparseCore 0:
  10.9 59.5 all-gather.4
  73.3 55.2 all-gather.2
  134.9 141.2 reduce-scatter.1

commit v2 on v0

--- a/solution.py
+++ b/solution.py
@@ -1,3 +1,5 @@
+import math
+
 import jax
 import jax.numpy as jnp
 from jax import lax
@@ -55,7 +57,7 @@
     return (weight_grads, partial_grad)
 
 
-def local(tokens, cotangent, gate_values, expert_ids, packing, w_gate, w_up, w_down):
+def routed_local(tokens, cotangent, gate_values, expert_ids, packing, w_gate, w_up, w_down):
     row_count, top_count = expert_ids.shape
     model_width = tokens.shape[1]
     dp_size = lax.axis_size("dp")
@@ -125,6 +127,106 @@
     return (input_grad, weight_grads[0], weight_grads[1], weight_grads[2])
 
 
+def swap(value):
+    return lax.ppermute(value, "dp", [(0, 1), (1, 0)])
+
+
+def shift_outer(value, count, inner, step):
+    return lax.ppermute(
+        value, "expert", [(place, (place + step * inner) % count) for place in range(count)]
+    )
+
+
+def swap_inner(value, count, partner):
+    return lax.ppermute(value, "expert", [(place, place ^ partner) for place in range(count)])
+
+
+def home_gates(packing, expert_ids, gate_values, count):
+    row_count = packing.shape[0]
+    labels = jnp.arange(count, dtype=jnp.int32)
+    named = expert_ids[:, :, None] == labels[None, None, :]
+    by_slot = jnp.sum(jnp.where(named, gate_values.astype(jnp.float32)[:, :, None], 0.0), axis=1)
+    own_homes = lax.axis_index("dp") * row_count + jnp.arange(row_count, dtype=jnp.int32)
+    routing = jnp.concatenate(
+        [packing[:, None].astype(jnp.bfloat16), by_slot.astype(jnp.bfloat16)], axis=1
+    )
+    routing = jnp.concatenate([routing, swap(routing)], axis=0).astype(jnp.float32)
+    matched = own_homes[:, None] == routing[:, 0].astype(jnp.int32)[None, :]
+    return jnp.sum(jnp.where(matched[:, :, None], routing[None, :, 1:], 0.0), axis=1)
+
+
+def spread(value, count, inner):
+    column = jnp.concatenate(
+        [value] + [shift_outer(value, count, inner, step) for step in range(1, count // inner)],
+        axis=0,
+    )
+    return jnp.concatenate(
+        [column] + [swap_inner(column, count, partner) for partner in range(1, inner)], axis=0
+    )
+
+
+def bring_back(value, count, inner):
+    outer = count // inner
+    blocks = value.reshape(inner, -1, value.shape[-1])
+    total = blocks[0].astype(jnp.float32)
+    for partner in range(1, inner):
+        total = total + swap_inner(blocks[partner], count, partner).astype(jnp.float32)
+    blocks = total.reshape(outer, -1, value.shape[-1])
+    rounded = blocks.astype(jnp.bfloat16)
+    total = blocks[0]
+    for step in range(1, outer):
+        total = total + shift_outer(rounded[step], count, inner, -step).astype(jnp.float32)
+    return total.astype(jnp.bfloat16)
+
+
+def dense_local(tokens, cotangent, gate_values, expert_ids, packing, w_gate, w_up, w_down):
+    model_width = tokens.shape[1]
+    half = w_gate.shape[1]
+    count = lax.axis_size("expert")
+    inner = math.gcd(count, 4)
+    gate_up = jnp.concatenate([w_gate[0], swap(w_gate[0]), w_up[0], swap(w_up[0])], axis=0)
+    down = jnp.concatenate([w_down[0], swap(w_down[0])], axis=0)
+    gates = home_gates(packing, expert_ids, gate_values, count).astype(jnp.bfloat16)
+    inputs = spread(tokens, count, inner)
+    upstream = spread(jnp.concatenate([cotangent, gates], axis=1), count, inner)
+    here = jnp.arange(count, dtype=jnp.int32) == lax.axis_index("expert")
+    gate = jnp.sum(
+        jnp.where(here[None, :], upstream[:, model_width:].astype(jnp.float32), 0.0),
+        axis=1,
+        keepdims=True,
+    )
+    upstream = upstream[:, :model_width]
+    pre = jnp.dot(inputs, gate_up.T, preferred_element_type=jnp.float32)
+    gate_pre, up_pre = pre[:, : 2 * half], pre[:, 2 * half :]
+    hidden_grad = gate * jnp.dot(upstream, down.T, preferred_element_type=jnp.float32)
+    sigmoid_val = jax.nn.sigmoid(gate_pre)
+    activated = gate_pre * sigmoid_val
+    hidden = (gate * activated * up_pre).astype(jnp.bfloat16)
+    silu_slope = sigmoid_val * (1.0 + gate_pre * (1.0 - sigmoid_val))
+    gate_grad = (hidden_grad * up_pre * silu_slope).astype(jnp.bfloat16)
+    up_grad = (hidden_grad * activated).astype(jnp.bfloat16)
+    both_grad = jnp.concatenate([gate_grad, up_grad], axis=1)
+    partial_grad = jnp.dot(both_grad, gate_up, preferred_element_type=jnp.float32)
+    input_grad = bring_back(partial_grad.astype(jnp.bfloat16), count, inner)
+    weight_grads = []
+    for grad, rows in ((gate_grad, inputs), (up_grad, inputs), (hidden, upstream)):
+        whole = jnp.dot(grad.T, rows, preferred_element_type=jnp.float32)
+        other = swap(whole[half:].astype(jnp.bfloat16)).astype(jnp.float32)
+        weight_grads.append((whole[:half] + other).astype(jnp.bfloat16)[None])
+    return (input_grad, *weight_grads)
+
+
+def local(tokens, cotangent, gate_values, expert_ids, packing, w_gate, w_up, w_down):
+    row_count, top = expert_ids.shape
+    expert_count = lax.axis_size("expert") * w_gate.shape[0]
+    capacity = min(row_count, max(2, row_count * top // expert_count + 1))
+    few = capacity * 4 <= row_count
+    chosen = routed_local if few else dense_local
+    return chosen(
+        tokens, cotangent, gate_values, expert_ids, packing, w_gate, w_up, w_down
+    )
+
+
 def solution(mesh):
     in_specs = (
         P(("groups", "dp", "expert"), None),

time: 172 us -> 83 us (0.48)
  waiting for transfers between devices: 81.2 us -> 38 us
  local copies, waits for them, and re-layouts: 20.5 us -> 3.57 us
  between operations: 15.2 us -> 0.93 us
  blocking collectives: 11.6 us -> 0 us
  matrix products: 11.6 us -> 4.94 us
  starting transfers between devices: 23.3 us -> 28.1 us
    all_to_all x3 -> x0, waiting for transfers between devices: 71 us -> none  [the longest x1 29.4 us: local(): lax.all_to_all(send_upstream, 'expert', split_axis=0, concat_axis=0, tile...]
    ppermute x0 -> x25, waiting for transfers between devices: none -> 38 us  [the longest x9 27 us: swap_inner(): lax.ppermute(value, 'expert', [(place, place ^ partner) for place in rang...]
    ppermute x0 -> x25, starting transfers between devices: none -> 28.1 us  [the longest x9 13.6 us: swap_inner(): lax.ppermute(value, 'expert', [(place, place ^ partner) for place in rang...]
    all_to_all x3 -> x0, starting transfers between devices: 23.2 us -> none  [the longest x1 8.34 us: local(): lax.all_to_all(send_rows, 'expert', split_axis=0, concat_axis=0, tiled=True)]
    reduce_scatter x1 -> x0, waiting for transfers between devices: 10.2 us -> none  [local(): lax.psum_scatter(partial_grad.reshape(expert_count, dp_size * capacity *...]
    all_gather x5 -> x0, blocking collectives: 9.66 us -> none  [the longest x1 2.11 us: local(): lax.all_gather(tokens, 'dp', axis=0, tiled=True)]
    dot_general x13 -> x6, matrix products: 11.6 us -> 4.94 us  [the longest x3 1.94 us: dense_local(): whole = jnp.dot(grad.T, rows, preferred_element_type=jnp.float32)]
    convert_element_type x8 -> x2, local copies, waits for them, and re-layouts: 7.16 us -> 0.85 us  [the longest x1 0.75 us: home_gates(): gate_values.astype(jnp.float32)[:, :, None]]
  transfers between devices with their start and end apart: 4 -> 25, of which waited for: 4 -> 12; matrix products, arithmetic and copies ran while one was open for 10% -> 15% of each run, Pallas kernels for 0% -> 0%
where the time goes in v2:
time: 83 us; the launch traced here: 82.7 us
  waiting for transfers between devices  38 us (46%)
  starting transfers between devices  28.1 us (34%)
  other arithmetic  7.15 us (9%)
  matrix products  4.94 us (6%)
  local copies, waits for them, and re-layouts  3.57 us (4%)
  between operations  0.93 us (1%)
    ppermute x9, waiting for transfers between devices, swap_inner(): lax.ppermute(value, 'expert', [(place, place ^ partner) for place in rang...  27 us
    ppermute x9, starting transfers between devices, swap_inner(): lax.ppermute(value, 'expert', [(place, place ^ partner) for place in rang...  13.6 us
    ppermute x9, starting transfers between devices, shift_outer(): lax.ppermute(value, 'expert', [(place, (place + step * inner) % count) fo...  12.7 us
    ppermute x9, waiting for transfers between devices, shift_outer(): lax.ppermute(value, 'expert', [(place, (place + step * inner) % count) fo...  11 us
    broadcast_in_dim x3, other arithmetic, dense_local(): weight_grads.append((whole[:half] + other).astype(jnp.bfloat16)[None])  3.26 us
    unnamed x17, local copies, waits for them, and re-layouts  2.15 us
    dot_general x3, matrix products, dense_local(): whole = jnp.dot(grad.T, rows, preferred_element_type=jnp.float32)  1.94 us
    ppermute x7, starting transfers between devices, swap(): return lax.ppermute(value, 'dp', [(0, 1), (1, 0)])  1.76 us
  transfers between devices with their start and end apart: 25, of which 12 were waited for; matrix products, arithmetic and copies ran while one was open for 15% of the time, Pallas kernels for 0%

profile of v2, /device:TPU:0, one launch (start us, length us, event | category | flops | bytes accessed | tf_op | source)
XLA Modules:
  0.0 82.7 jit_solution(4603602766148541057)
XLA Ops:
  0.6 4.1 %collective-permute-start.9 = (bf16[16,2048]{1,0:T(8,128)(2,1)}, bf16[16,2048]{1,0:T(8,128)(2,1)S(1)}, u32[]{:S(2)}, u32[]{:S(2)}) collective-permute-start(bf16[16,2048]{1,0:T(8,128)(2,1)} %param.8), channel_id=1, source_target_pairs={{0,8},{1,9},{2,10},{3,11},{4,12},{5,13},{6,14},{7,15},{8,0},{9,1},... | collective-permute-start | bytes 196616 | tf_op jit(solution)/shard_map/ppermute | solution.py:135
  4.7 1.6 %collective-permute-start.8 = (bf16[16,2048]{1,0:T(8,128)(2,1)}, bf16[16,2048]{1,0:T(8,128)(2,1)S(1)}, u32[]{:S(2)}, u32[]{:S(2)}) collective-permute-start(bf16[16,2048]{1,0:T(8,128)(2,1)} %param.8), channel_id=1, source_target_pairs={{0,4},{1,5},{2,6},{3,7},{4,8},{5,9},{6,10},{7,11},{8,12},{9,13},{1... | collective-permute-start | bytes 196616 | tf_op jit(solution)/shard_map/ppermute | solution.py:135
  6.3 2.2 %collective-permute-start.10 = (bf16[16,2048]{1,0:T(8,128)(2,1)}, bf16[16,2048]{1,0:T(8,128)(2,1)S(1)}, u32[]{:S(2)}, u32[]{:S(2)}) collective-permute-start(bf16[16,2048]{1,0:T(8,128)(2,1)} %param.8), channel_id=1, source_target_pairs={{0,12},{1,13},{2,14},{3,15},{4,0},{5,1},{6,2},{7,3},{8,4},{9,5},{1... | collective-permute-start | bytes 196616 | tf_op jit(solution)/shard_map/ppermute | solution.py:135
  15.2 5.6 %collective-permute-done.1 = bf16[16,2064]{1,0:T(8,128)(2,1)S(1)} collective-permute-done((bf16[16,2064]{1,0:T(8,128)(2,1)S(1)}, bf16[16,2064]{1,0:T(8,128)(2,1)S(1)}, u32[]{:S(2)}, u32[]{:S(2)}) %collective-permute-start.1) | collective-permute-done | bytes 66080 | tf_op jit(solution)/shard_map/ppermute | solution.py:135
  21.9 1.5 %collective-permute-start.12 = (bf16[64,2048]{1,0:T(8,128)(2,1)S(1)}, bf16[64,2048]{1,0:T(8,128)(2,1)S(1)}, u32[]{:S(2)}, u32[]{:S(2)}) collective-permute-start(bf16[64,2048]{1,0:T(8,128)(2,1)S(1)} %get-tuple-element.16), channel_id=1, source_target_pairs={{0,2},{1,3},{2,0},{3,1},{4,6},{5,7},{6,4},{7,5},{8,10},{9,11},{10,... | collective-permute-start | bytes 786440 | tf_op jit(solution)/shard_map/ppermute | solution.py:141
  23.4 1.7 %collective-permute-done.3 = bf16[16,2064]{1,0:T(8,128)(2,1)S(1)} collective-permute-done((bf16[16,2064]{1,0:T(8,128)(2,1)S(1)}, bf16[16,2064]{1,0:T(8,128)(2,1)S(1)}, u32[]{:S(2)}, u32[]{:S(2)}) %collective-permute-start.3) | collective-permute-done | bytes 66080 | tf_op jit(solution)/shard_map/ppermute | solution.py:135
  25.1 1.5 %collective-permute-start.11 = (bf16[64,2048]{1,0:T(8,128)(2,1)S(1)}, bf16[64,2048]{1,0:T(8,128)(2,1)S(1)}, u32[]{:S(2)}, u32[]{:S(2)}) collective-permute-start(bf16[64,2048]{1,0:T(8,128)(2,1)S(1)} %get-tuple-element.16), channel_id=1, source_target_pairs={{0,1},{1,0},{2,3},{3,2},{4,5},{5,4},{6,7},{7,6},{8,9},{9,8},{10,11... | collective-permute-start | bytes 786440 | tf_op jit(solution)/shard_map/ppermute | solution.py:141
  27.5 4.0 %collective-permute-done.11 = bf16[64,2048]{1,0:T(8,128)(2,1)S(1)} collective-permute-done((bf16[64,2048]{1,0:T(8,128)(2,1)S(1)}, bf16[64,2048]{1,0:T(8,128)(2,1)S(1)}, u32[]{:S(2)}, u32[]{:S(2)}) %collective-permute-start.11) | collective-permute-done | bytes 262176 | tf_op jit(solution)/shard_map/ppermute | solution.py:141
  31.5 2.7 %collective-permute-start.13 = (bf16[64,2048]{1,0:T(8,128)(2,1)S(1)}, bf16[64,2048]{1,0:T(8,128)(2,1)S(1)}, u32[]{:S(2)}, u32[]{:S(2)}) collective-permute-start(bf16[64,2048]{1,0:T(8,128)(2,1)S(1)} %get-tuple-element.16), channel_id=1, source_target_pairs={{0,3},{1,2},{2,1},{3,0},{4,7},{5,6},{6,5},{7,4},{8,11},{9,10},{10,... | collective-permute-start | bytes 786440 | tf_op jit(solution)/shard_map/ppermute | solution.py:141
  34.8 6.8 %collective-permute-done.13 = bf16[64,2048]{1,0:T(8,128)(2,1)S(1)} collective-permute-done((bf16[64,2048]{1,0:T(8,128)(2,1)S(1)}, bf16[64,2048]{1,0:T(8,128)(2,1)S(1)}, u32[]{:S(2)}, u32[]{:S(2)}) %collective-permute-start.13) | collective-permute-done | bytes 262176 | tf_op jit(solution)/shard_map/ppermute | solution.py:141
  41.6 2.7 %collective-permute-start.6 = (bf16[64,2064]{1,0:T(8,128)(2,1)S(1)}, bf16[64,2064]{1,0:T(8,128)(2,1)S(1)}, u32[]{:S(2)}, u32[]{:S(2)}) collective-permute-start(bf16[64,2064]{1,0:T(8,128)(2,1)S(1)} %pad_maximum_fusion.3), channel_id=1, source_target_pairs={{0,3},{1,2},{2,1},{3,0},{4,7},{5,6},{6,5},{7,4},{8,11},{9,10},{10,... | collective-permute-start | bytes 792584 | tf_op jit(solution)/shard_map/ppermute | solution.py:141
  44.3 2.2 %collective-permute-done.4 = bf16[64,2064]{1,0:T(8,128)(2,1)S(1)} collective-permute-done((bf16[64,2064]{1,0:T(8,128)(2,1)S(1)}, bf16[64,2064]{1,0:T(8,128)(2,1)S(1)}, u32[]{:S(2)}, u32[]{:S(2)}) %collective-permute-start.4) | collective-permute-done | bytes 264224 | tf_op jit(solution)/shard_map/ppermute | solution.py:141
  47.6 5.6 %collective-permute-done.5 = bf16[64,2064]{1,0:T(8,128)(2,1)S(1)} collective-permute-done((bf16[64,2064]{1,0:T(8,128)(2,1)S(1)}, bf16[64,2064]{1,0:T(8,128)(2,1)S(1)}, u32[]{:S(2)}, u32[]{:S(2)}) %collective-permute-start.5) | collective-permute-done | bytes 264224 | tf_op jit(solution)/shard_map/ppermute | solution.py:141
  56.3 1.2 %convolution_convert_fusion = bf16[256,2048]{1,0:T(8,128)(2,1)S(1)} fusion(bf16[192,2048]{1,0:T(8,128)(2,1)S(1)} %collective-permute-done.15, bf16[192,2048]{1,0:T(8,128)(2,1)S(1)} %bitcast.20, bf16[192,2048]{1,0:T(8,128)(2,1)S(1)} %collective-permute-done.14, bf16[192,2048]{1,0:T(8,128)(2,1)S(1)} %bitcast.23, bf16[256,384]{1,0:T(8,128)(2,1)S(1)} %get-tuple-element.7, ...), kind=kOutput, calls=%fused_computation.1 | convolution fusion | flops 819200000 | bytes 4587520 | tf_op jit(solution)/shard_map/dot_general | solution.py:209
  57.6 1.6 %collective-permute-start.16 = (bf16[64,2048]{1,0:T(8,128)(2,1)S(1)}, bf16[64,2048]{1,0:T(8,128)(2,1)S(1)}, u32[]{:S(2)}, u32[]{:S(2)}) collective-permute-start(bf16[64,2048]{1,0:T(8,128)(2,1)S(1)} %get-tuple-element.8), channel_id=1, source_target_pairs={{0,1},{1,0},{2,3},{3,2},{4,5},{5,4},{6,7},{7,6},{8,9},{9,8},{10,11... | collective-permute-start | bytes 786440 | tf_op jit(solution)/shard_map/ppermute | solution.py:141
  61.9 3.9 %collective-permute-done.16 = bf16[64,2048]{1,0:T(8,128)(2,1)S(1)} collective-permute-done((bf16[64,2048]{1,0:T(8,128)(2,1)S(1)}, bf16[64,2048]{1,0:T(8,128)(2,1)S(1)}, u32[]{:S(2)}, u32[]{:S(2)}) %collective-permute-start.16) | collective-permute-done | bytes 262176 | tf_op jit(solution)/shard_map/ppermute | solution.py:141
  65.8 3.2 %collective-permute-done.18 = bf16[64,2048]{1,0:T(8,128)(2,1)S(1)} collective-permute-done((bf16[64,2048]{1,0:T(8,128)(2,1)S(1)}, bf16[64,2048]{1,0:T(8,128)(2,1)S(1)}, u32[]{:S(2)}, u32[]{:S(2)}) %collective-permute-start.18) | collective-permute-done | bytes 262176 | tf_op jit(solution)/shard_map/ppermute | solution.py:141
  69.0 1.3 %collective-permute-done.17 = bf16[64,2048]{1,0:T(8,128)(2,1)S(1)} collective-permute-done((bf16[64,2048]{1,0:T(8,128)(2,1)S(1)}, bf16[64,2048]{1,0:T(8,128)(2,1)S(1)}, u32[]{:S(2)}, u32[]{:S(2)}) %collective-permute-start.17) | collective-permute-done | bytes 262176 | tf_op jit(solution)/shard_map/ppermute | solution.py:141
  70.5 2.2 %collective-permute-start.19 = (bf16[16,2048]{1,0:T(8,128)(2,1)S(1)}, bf16[16,2048]{1,0:T(8,128)(2,1)S(1)}, u32[]{:S(2)}, u32[]{:S(2)}) collective-permute-start(bf16[16,2048]{1,0:T(8,128)(2,1)S(1)} %get-tuple-element.11), channel_id=1, source_target_pairs={{0,12},{1,13},{2,14},{3,15},{4,0},{5,1},{6,2},{7,3},{8,4},{9,5},{1... | collective-permute-start | bytes 196616 | tf_op jit(solution)/shard_map/ppermute | solution.py:135
  72.7 1.2 %collective-permute-start.20 = (bf16[16,2048]{1,0:T(8,128)(2,1)S(1)}, bf16[16,2048]{1,0:T(8,128)(2,1)S(1)}, u32[]{:S(2)}, u32[]{:S(2)}) collective-permute-start(bf16[16,2048]{1,0:T(8,128)(2,1)S(1)} %get-tuple-element.13), channel_id=1, source_target_pairs={{0,8},{1,9},{2,10},{3,11},{4,12},{5,13},{6,14},{7,15},{8,0},{9,1},... | collective-permute-start | bytes 196616 | tf_op jit(solution)/shard_map/ppermute | solution.py:135
  75.3 3.4 %collective-permute-done.21 = bf16[16,2048]{1,0:T(8,128)(2,1)S(1)} collective-permute-done((bf16[16,2048]{1,0:T(8,128)(2,1)S(1)}, bf16[16,2048]{1,0:T(8,128)(2,1)S(1)}, u32[]{:S(2)}, u32[]{:S(2)}) %collective-permute-start.21) | collective-permute-done | bytes 65568 | tf_op jit(solution)/shard_map/ppermute | solution.py:135
  79.4 1.1 %fusion.15 = bf16[1,192,2048]{2,1,0:T(8,128)(2,1)} fusion(bf16[192,2048]{1,0:T(8,128)(2,1)S(1)} %collective-permute-done.24, f32[384,2048]{1,0:T(8,128)S(1)} %fusion.10), kind=kLoop, calls=%fused_computation.21 | loop fusion | flops 1179648 | bytes 3145728 | tf_op jit(solution)/shard_map/broadcast_in_dim | solution.py:215
  80.5 1.1 %fusion.13 = bf16[1,192,2048]{2,1,0:T(8,128)(2,1)} fusion(bf16[192,2048]{1,0:T(8,128)(2,1)S(1)} %collective-permute-done.22, f32[384,2048]{1,0:T(8,128)S(1)} %fusion.34), kind=kLoop, calls=%fused_computation.19 | loop fusion | flops 1179648 | bytes 3145728 | tf_op jit(solution)/shard_map/broadcast_in_dim | solution.py:215
  81.6 1.1 %fusion.14 = bf16[1,192,2048]{2,1,0:T(8,128)(2,1)} fusion(bf16[192,2048]{1,0:T(8,128)(2,1)S(1)} %collective-permute-done.23, f32[384,2048]{1,0:T(8,128)S(1)} %fusion.35), kind=kLoop, calls=%fused_computation.20 | loop fusion | flops 1179648 | bytes 3145728 | tf_op jit(solution)/shard_map/broadcast_in_dim | solution.py:215
  (78 shorter events, 18.5 us)
Async XLA Ops:
  0.6 13.9 %collective-permute-start.9 = (bf16[16,2048]{1,0:T(8,128)(2,1)}, bf16[16,2048]{1,0:T(8,128)(2,1)S(1)}, u32[]{:S(2)}, u32[]{:S(2)}) collective-permute-start(bf16[16,2048]{1,0:T(8,128)(2,1)} %param.8), channel_id=1, source_target_pairs={{0,8},{1,9},{2,10},{3,11},{4,12},{5,13},{6,14},{7,15},{8,0},{9,1},... | collective-permute-start | bytes 196616 | tf_op jit(solution)/shard_map/ppermute | solution.py:135
  4.7 9.2 %collective-permute-start.8 = (bf16[16,2048]{1,0:T(8,128)(2,1)}, bf16[16,2048]{1,0:T(8,128)(2,1)S(1)}, u32[]{:S(2)}, u32[]{:S(2)}) collective-permute-start(bf16[16,2048]{1,0:T(8,128)(2,1)} %param.8), channel_id=1, source_target_pairs={{0,4},{1,5},{2,6},{3,7},{4,8},{5,9},{6,10},{7,11},{8,12},{9,13},{1... | collective-permute-start | bytes 196616 | tf_op jit(solution)/shard_map/ppermute | solution.py:135
  6.3 8.3 %collective-permute-start.10 = (bf16[16,2048]{1,0:T(8,128)(2,1)}, bf16[16,2048]{1,0:T(8,128)(2,1)S(1)}, u32[]{:S(2)}, u32[]{:S(2)}) collective-permute-start(bf16[16,2048]{1,0:T(8,128)(2,1)} %param.8), channel_id=1, source_target_pairs={{0,12},{1,13},{2,14},{3,15},{4,0},{5,1},{6,2},{7,3},{8,4},{9,5},{1... | collective-permute-start | bytes 196616 | tf_op jit(solution)/shard_map/ppermute | solution.py:135
  11.0 42.3 %collective-permute-start.14 = (bf16[192,2048]{1,0:T(8,128)(2,1)}, bf16[192,2048]{1,0:T(8,128)(2,1)S(1)}, u32[]{:S(2)}, u32[]{:S(2)}) collective-permute-start(bf16[192,2048]{1,0:T(8,128)(2,1)} %bitcast.21), channel_id=1, source_target_pairs={{0,16},{16,0},{1,17},{17,1},{2,18},{18,2},{3,19},{19,3},{4,20},{20... | collective-permute-start | bytes 2359304 | tf_op jit(solution)/shard_map/ppermute | solution.py:131
  12.4 40.9 %collective-permute-start.15 = (bf16[192,2048]{1,0:T(8,128)(2,1)}, bf16[192,2048]{1,0:T(8,128)(2,1)S(1)}, u32[]{:S(2)}, u32[]{:S(2)}) collective-permute-start(bf16[192,2048]{1,0:T(8,128)(2,1)} %bitcast.18), channel_id=1, source_target_pairs={{0,16},{16,0},{1,17},{17,1},{2,18},{18,2},{3,19},{19,3},{4,20},{20... | collective-permute-start | bytes 2359304 | tf_op jit(solution)/shard_map/ppermute | solution.py:131
  14.0 41.1 %collective-permute-start.7 = (bf16[192,2048]{1,0:T(8,128)(2,1)}, bf16[192,2048]{1,0:T(8,128)(2,1)S(1)}, u32[]{:S(2)}, u32[]{:S(2)}) collective-permute-start(bf16[192,2048]{1,0:T(8,128)(2,1)} %bitcast.16), channel_id=1, source_target_pairs={{0,16},{16,0},{1,17},{17,1},{2,18},{18,2},{3,19},{19,3},{4,20},{20... | collective-permute-start | bytes 2359304 | tf_op jit(solution)/shard_map/ppermute | solution.py:131
  14.5 7.4 %collective-permute-start.2 = (bf16[16,2064]{1,0:T(8,128)(2,1)S(1)}, bf16[16,2064]{1,0:T(8,128)(2,1)S(1)}, u32[]{:S(2)}, u32[]{:S(2)}) collective-permute-start(bf16[16,2064]{1,0:T(8,128)(2,1)S(1)} %get-tuple-element.14), channel_id=1, source_target_pairs={{0,8},{1,9},{2,10},{3,11},{4,12},{5,13},{6,14},{7,15},{8,0},{9,1},... | collective-permute-start | bytes 198152 | tf_op jit(solution)/shard_map/ppermute | solution.py:135
  14.6 6.2 %collective-permute-start.1 = (bf16[16,2064]{1,0:T(8,128)(2,1)S(1)}, bf16[16,2064]{1,0:T(8,128)(2,1)S(1)}, u32[]{:S(2)}, u32[]{:S(2)}) collective-permute-start(bf16[16,2064]{1,0:T(8,128)(2,1)S(1)} %get-tuple-element.14), channel_id=1, source_target_pairs={{0,4},{1,5},{2,6},{3,7},{4,8},{5,9},{6,10},{7,11},{8,12},{9,13},{1... | collective-permute-start | bytes 198152 | tf_op jit(solution)/shard_map/ppermute | solution.py:135
  20.8 4.3 %collective-permute-start.3 = (bf16[16,2064]{1,0:T(8,128)(2,1)S(1)}, bf16[16,2064]{1,0:T(8,128)(2,1)S(1)}, u32[]{:S(2)}, u32[]{:S(2)}) collective-permute-start(bf16[16,2064]{1,0:T(8,128)(2,1)S(1)} %get-tuple-element.14), channel_id=1, source_target_pairs={{0,12},{1,13},{2,14},{3,15},{4,0},{5,1},{6,2},{7,3},{8,4},{9,5},{1... | collective-permute-start | bytes 198152 | tf_op jit(solution)/shard_map/ppermute | solution.py:135
  21.9 12.3 %collective-permute-start.12 = (bf16[64,2048]{1,0:T(8,128)(2,1)S(1)}, bf16[64,2048]{1,0:T(8,128)(2,1)S(1)}, u32[]{:S(2)}, u32[]{:S(2)}) collective-permute-start(bf16[64,2048]{1,0:T(8,128)(2,1)S(1)} %get-tuple-element.16), channel_id=1, source_target_pairs={{0,2},{1,3},{2,0},{3,1},{4,6},{5,7},{6,4},{7,5},{8,10},{9,11},{10,... | collective-permute-start | bytes 786440 | tf_op jit(solution)/shard_map/ppermute | solution.py:141
  25.1 6.4 %collective-permute-start.11 = (bf16[64,2048]{1,0:T(8,128)(2,1)S(1)}, bf16[64,2048]{1,0:T(8,128)(2,1)S(1)}, u32[]{:S(2)}, u32[]{:S(2)}) collective-permute-start(bf16[64,2048]{1,0:T(8,128)(2,1)S(1)} %get-tuple-element.16), channel_id=1, source_target_pairs={{0,1},{1,0},{2,3},{3,2},{4,5},{5,4},{6,7},{7,6},{8,9},{9,8},{10,11... | collective-permute-start | bytes 786440 | tf_op jit(solution)/shard_map/ppermute | solution.py:141
  31.5 10.1 %collective-permute-start.13 = (bf16[64,2048]{1,0:T(8,128)(2,1)S(1)}, bf16[64,2048]{1,0:T(8,128)(2,1)S(1)}, u32[]{:S(2)}, u32[]{:S(2)}) collective-permute-start(bf16[64,2048]{1,0:T(8,128)(2,1)S(1)} %get-tuple-element.16), channel_id=1, source_target_pairs={{0,3},{1,2},{2,1},{3,0},{4,7},{5,6},{6,5},{7,4},{8,11},{9,10},{10,... | collective-permute-start | bytes 786440 | tf_op jit(solution)/shard_map/ppermute | solution.py:141
  34.2 12.3 %collective-permute-start.4 = (bf16[64,2064]{1,0:T(8,128)(2,1)S(1)}, bf16[64,2064]{1,0:T(8,128)(2,1)S(1)}, u32[]{:S(2)}, u32[]{:S(2)}) collective-permute-start(bf16[64,2064]{1,0:T(8,128)(2,1)S(1)} %pad_maximum_fusion.3), channel_id=1, source_target_pairs={{0,1},{1,0},{2,3},{3,2},{4,5},{5,4},{6,7},{7,6},{8,9},{9,8},{10,11... | collective-permute-start | bytes 792584 | tf_op jit(solution)/shard_map/ppermute | solution.py:141
  41.6 11.6 %collective-permute-start.6 = (bf16[64,2064]{1,0:T(8,128)(2,1)S(1)}, bf16[64,2064]{1,0:T(8,128)(2,1)S(1)}, u32[]{:S(2)}, u32[]{:S(2)}) collective-permute-start(bf16[64,2064]{1,0:T(8,128)(2,1)S(1)} %pad_maximum_fusion.3), channel_id=1, source_target_pairs={{0,3},{1,2},{2,1},{3,0},{4,7},{5,6},{6,5},{7,4},{8,11},{9,10},{10,... | collective-permute-start | bytes 792584 | tf_op jit(solution)/shard_map/ppermute | solution.py:141
  46.5 6.6 %collective-permute-start.5 = (bf16[64,2064]{1,0:T(8,128)(2,1)S(1)}, bf16[64,2064]{1,0:T(8,128)(2,1)S(1)}, u32[]{:S(2)}, u32[]{:S(2)}) collective-permute-start(bf16[64,2064]{1,0:T(8,128)(2,1)S(1)} %pad_maximum_fusion.3), channel_id=1, source_target_pairs={{0,2},{1,3},{2,0},{3,1},{4,6},{5,7},{6,4},{7,5},{8,10},{9,11},{10,... | collective-permute-start | bytes 792584 | tf_op jit(solution)/shard_map/ppermute | solution.py:141
  57.6 8.3 %collective-permute-start.16 = (bf16[64,2048]{1,0:T(8,128)(2,1)S(1)}, bf16[64,2048]{1,0:T(8,128)(2,1)S(1)}, u32[]{:S(2)}, u32[]{:S(2)}) collective-permute-start(bf16[64,2048]{1,0:T(8,128)(2,1)S(1)} %get-tuple-element.8), channel_id=1, source_target_pairs={{0,1},{1,0},{2,3},{3,2},{4,5},{5,4},{6,7},{7,6},{8,9},{9,8},{10,11... | collective-permute-start | bytes 786440 | tf_op jit(solution)/shard_map/ppermute | solution.py:141
  59.1 9.9 %collective-permute-start.18 = (bf16[64,2048]{1,0:T(8,128)(2,1)S(1)}, bf16[64,2048]{1,0:T(8,128)(2,1)S(1)}, u32[]{:S(2)}, u32[]{:S(2)}) collective-permute-start(bf16[64,2048]{1,0:T(8,128)(2,1)S(1)} %get-tuple-element.9), channel_id=1, source_target_pairs={{0,3},{1,2},{2,1},{3,0},{4,7},{5,6},{6,5},{7,4},{8,11},{9,10},{10,... | collective-permute-start | bytes 786440 | tf_op jit(solution)/shard_map/ppermute | solution.py:141
  60.1 10.3 %collective-permute-start.17 = (bf16[64,2048]{1,0:T(8,128)(2,1)S(1)}, bf16[64,2048]{1,0:T(8,128)(2,1)S(1)}, u32[]{:S(2)}, u32[]{:S(2)}) collective-permute-start(bf16[64,2048]{1,0:T(8,128)(2,1)S(1)} %get-tuple-element.10), channel_id=1, source_target_pairs={{0,2},{1,3},{2,0},{3,1},{4,6},{5,7},{6,4},{7,5},{8,10},{9,11},{10,... | collective-permute-start | bytes 786440 | tf_op jit(solution)/shard_map/ppermute | solution.py:141
  61.2 18.2 %collective-permute-start.24 = (bf16[192,2048]{1,0:T(8,128)(2,1)S(1)}, bf16[192,2048]{1,0:T(8,128)(2,1)S(1)}, u32[]{:S(2)}, u32[]{:S(2)}) collective-permute-start(bf16[192,2048]{1,0:T(8,128)(2,1)S(1)} %slice.155), channel_id=1, source_target_pairs={{0,16},{16,0},{1,17},{17,1},{2,18},{18,2},{3,19},{19,3},{4,20},{20... | collective-permute-start | bytes 2359304 | tf_op jit(solution)/shard_map/ppermute | solution.py:131
  70.5 4.3 %collective-permute-start.19 = (bf16[16,2048]{1,0:T(8,128)(2,1)S(1)}, bf16[16,2048]{1,0:T(8,128)(2,1)S(1)}, u32[]{:S(2)}, u32[]{:S(2)}) collective-permute-start(bf16[16,2048]{1,0:T(8,128)(2,1)S(1)} %get-tuple-element.11), channel_id=1, source_target_pairs={{0,12},{1,13},{2,14},{3,15},{4,0},{5,1},{6,2},{7,3},{8,4},{9,5},{1... | collective-permute-start | bytes 196616 | tf_op jit(solution)/shard_map/ppermute | solution.py:135
  72.7 6.1 %collective-permute-start.21 = (bf16[16,2048]{1,0:T(8,128)(2,1)S(1)}, bf16[16,2048]{1,0:T(8,128)(2,1)S(1)}, u32[]{:S(2)}, u32[]{:S(2)}) collective-permute-start(bf16[16,2048]{1,0:T(8,128)(2,1)S(1)} %get-tuple-element.12), channel_id=1, source_target_pairs={{0,4},{1,5},{2,6},{3,7},{4,8},{5,9},{6,10},{7,11},{8,12},{9,13},{1... | collective-permute-start | bytes 196616 | tf_op jit(solution)/shard_map/ppermute | solution.py:135
  72.7 6.1 %collective-permute-start.20 = (bf16[16,2048]{1,0:T(8,128)(2,1)S(1)}, bf16[16,2048]{1,0:T(8,128)(2,1)S(1)}, u32[]{:S(2)}, u32[]{:S(2)}) collective-permute-start(bf16[16,2048]{1,0:T(8,128)(2,1)S(1)} %get-tuple-element.13), channel_id=1, source_target_pairs={{0,8},{1,9},{2,10},{3,11},{4,12},{5,13},{6,14},{7,15},{8,0},{9,1},... | collective-permute-start | bytes 196616 | tf_op jit(solution)/shard_map/ppermute | solution.py:135
  74.6 5.9 %collective-permute-start.22 = (bf16[192,2048]{1,0:T(8,128)(2,1)S(1)}, bf16[192,2048]{1,0:T(8,128)(2,1)S(1)}, u32[]{:S(2)}, u32[]{:S(2)}) collective-permute-start(bf16[192,2048]{1,0:T(8,128)(2,1)S(1)} %slice.157), channel_id=1, source_target_pairs={{0,16},{16,0},{1,17},{17,1},{2,18},{18,2},{3,19},{19,3},{4,20},{20... | collective-permute-start | bytes 2359304 | tf_op jit(solution)/shard_map/ppermute | solution.py:131
  74.8 6.7 %collective-permute-start.23 = (bf16[192,2048]{1,0:T(8,128)(2,1)S(1)}, bf16[192,2048]{1,0:T(8,128)(2,1)S(1)}, u32[]{:S(2)}, u32[]{:S(2)}) collective-permute-start(bf16[192,2048]{1,0:T(8,128)(2,1)S(1)} %slice.156), channel_id=1, source_target_pairs={{0,16},{16,0},{1,17},{17,1},{2,18},{18,2},{3,19},{19,3},{4,20},{20... | collective-permute-start | bytes 2359304 | tf_op jit(solution)/shard_map/ppermute | solution.py:131
  (4 other events, 66.0 us)

commit v3 on v2

--- a/solution.py
+++ b/solution.py
@@ -155,14 +155,19 @@
     return jnp.sum(jnp.where(matched[:, :, None], routing[None, :, 1:], 0.0), axis=1)
 
 
-def spread(value, count, inner):
-    column = jnp.concatenate(
-        [value] + [shift_outer(value, count, inner, step) for step in range(1, count // inner)],
-        axis=0,
-    )
-    return jnp.concatenate(
-        [column] + [swap_inner(column, count, partner) for partner in range(1, inner)], axis=0
-    )
+def along_outer(value, count, inner):
+    return [value] + [shift_outer(value, count, inner, step) for step in range(1, count // inner)]
+
+
+def across_inner(column, count, inner):
+    if inner < 4:
+        return [column] + [swap_inner(column, count, partner) for partner in range(1, inner)]
+    cut = column.shape[0] // 2
+    first = swap_inner(column, count, 1)
+    second = swap_inner(column, count, 2)
+    far_top = swap_inner(first[:cut], count, 2)
+    far_bottom = swap_inner(second[cut:], count, 1)
+    return [column, first, second, far_top, far_bottom]
 
 
 def bring_back(value, count, inner):
@@ -184,11 +189,15 @@
     half = w_gate.shape[1]
     count = lax.axis_size("expert")
     inner = math.gcd(count, 4)
-    gate_up = jnp.concatenate([w_gate[0], swap(w_gate[0]), w_up[0], swap(w_up[0])], axis=0)
-    down = jnp.concatenate([w_down[0], swap(w_down[0])], axis=0)
+    token_column = jnp.concatenate(along_outer(tokens, count, inner), axis=0)
+    other = swap(jnp.concatenate([w_gate[0], w_up[0], w_down[0]], axis=0))
     gates = home_gates(packing, expert_ids, gate_values, count).astype(jnp.bfloat16)
-    inputs = spread(tokens, count, inner)
-    upstream = spread(jnp.concatenate([cotangent, gates], axis=1), count, inner)
+    payload = jnp.concatenate([cotangent, gates], axis=1)
+    payload, token_column, other = lax.optimization_barrier((payload, token_column, other))
+    upstream_column = jnp.concatenate(along_outer(payload, count, inner), axis=0)
+    inputs = jnp.concatenate(across_inner(token_column, count, inner), axis=0)
+    other_inputs = swap(inputs)
+    upstream = jnp.concatenate(across_inner(upstream_column, count, inner), axis=0)
     here = jnp.arange(count, dtype=jnp.int32) == lax.axis_index("expert")
     gate = jnp.sum(
         jnp.where(here[None, :], upstream[:, model_width:].astype(jnp.float32), 0.0),
@@ -196,6 +205,8 @@
         keepdims=True,
     )
     upstream = upstream[:, :model_width]
+    gate_up = jnp.concatenate([w_gate[0], other[:half], w_up[0], other[half : 2 * half]], axis=0)
+    down = jnp.concatenate([w_down[0], other[2 * half :]], axis=0)
     pre = jnp.dot(inputs, gate_up.T, preferred_element_type=jnp.float32)
     gate_pre, up_pre = pre[:, : 2 * half], pre[:, 2 * half :]
     hidden_grad = gate * jnp.dot(upstream, down.T, preferred_element_type=jnp.float32)
@@ -207,12 +218,25 @@
     up_grad = (hidden_grad * activated).astype(jnp.bfloat16)
     both_grad = jnp.concatenate([gate_grad, up_grad], axis=1)
     partial_grad = jnp.dot(both_grad, gate_up, preferred_element_type=jnp.float32)
-    input_grad = bring_back(partial_grad.astype(jnp.bfloat16), count, inner)
+    partial_grad = partial_grad.astype(jnp.bfloat16)
+    input_grad = bring_back(partial_grad, count, inner)
+    grads = (gate_grad, up_grad, hidden)
+    own_grads = jnp.concatenate([grad[:, :half] for grad in grads], axis=1)
+    sent_grads = jnp.concatenate([grad[:, half:] for grad in grads], axis=1)
+    sent_grads, upstream, _ = lax.optimization_barrier((sent_grads, upstream, partial_grad))
+    other_grads = swap(sent_grads)
+    other_upstream = swap(upstream)
     weight_grads = []
-    for grad, rows in ((gate_grad, inputs), (up_grad, inputs), (hidden, upstream)):
-        whole = jnp.dot(grad.T, rows, preferred_element_type=jnp.float32)
-        other = swap(whole[half:].astype(jnp.bfloat16)).astype(jnp.float32)
-        weight_grads.append((whole[:half] + other).astype(jnp.bfloat16)[None])
+    for index, (rows, other_rows) in enumerate(
+        ((inputs, other_inputs), (inputs, other_inputs), (upstream, other_upstream))
+    ):
+        low = index * half
+        total = jnp.dot(
+            own_grads[:, low : low + half].T, rows, preferred_element_type=jnp.float32
+        ) + jnp.dot(
+            other_grads[:, low : low + half].T, other_rows, preferred_element_type=jnp.float32
+        )
+        weight_grads.append(total.astype(jnp.bfloat16)[None])
     return (input_grad, *weight_grads)
 
 

time: 83 us -> 71 us (0.86)
  waiting for transfers between devices: 38 us -> 24.5 us
  matrix products: 4.94 us -> 8.17 us
  starting transfers between devices: 28.1 us -> 30.6 us
  other arithmetic: 7.15 us -> 5.04 us
  local copies, waits for them, and re-layouts: 3.57 us -> 1.48 us
    ppermute x9 -> x11, waiting for transfers between devices: 27 us -> 15.4 us  [swap_inner(): lax.ppermute(value, 'expert', [(place, place ^ partner) for place in rang...]
    broadcast_in_dim x3 -> x0, other arithmetic: 3.26 us -> none  [dense_local(): weight_grads.append((whole[:half] + other).astype(jnp.bfloat16)[None])]
    dot_general x3 -> x6, matrix products: 1.94 us -> 5.15 us  [the longest x3 2.98 us: dense_local(): jnp.dot(own_grads[:, low:low + half].T, rows, preferred_element_type=jnp....]
    ppermute x9, waiting for transfers between devices: 11 us -> 7.99 us  [shift_outer(): lax.ppermute(value, 'expert', [(place, (place + step * inner) % count) fo...]
    ppermute x9 -> x11, starting transfers between devices: 13.6 us -> 16 us  [swap_inner(): lax.ppermute(value, 'expert', [(place, place ^ partner) for place in rang...]
    unnamed x17 -> x27, local copies, waits for them, and re-layouts: 2.15 us -> 0.29 us
    concatenate x2 -> x4, other arithmetic: 1.72 us -> 3.53 us  [the longest x1 3.38 us: dense_local(): other = swap(jnp.concatenate([w_gate[0], w_up[0], w_down[0]], axis=0))]
    ppermute x9, starting transfers between devices: 12.7 us -> 14.1 us  [shift_outer(): lax.ppermute(value, 'expert', [(place, (place + step * inner) % count) fo...]
  transfers between devices with their start and end apart: 25 -> 25, of which waited for: 12 -> 16; matrix products, arithmetic and copies ran while one was open for 15% -> 11% of each run, Pallas kernels for 0% -> 0%
where the time goes in v3:
time: 71 us; the launch traced here: 70.8 us
  starting transfers between devices  30.6 us (43%)
  waiting for transfers between devices  24.5 us (35%)
  matrix products  8.17 us (12%)
  other arithmetic  5.04 us (7%)
  local copies, waits for them, and re-layouts  1.48 us (2%)
  between operations  1 us (1%)
    ppermute x11, starting transfers between devices, swap_inner(): lax.ppermute(value, 'expert', [(place, place ^ partner) for place in rang...  16 us
    ppermute x11, waiting for transfers between devices, swap_inner(): lax.ppermute(value, 'expert', [(place, place ^ partner) for place in rang...  15.4 us
    ppermute x9, starting transfers between devices, shift_outer(): lax.ppermute(value, 'expert', [(place, (place + step * inner) % count) fo...  14.1 us
    ppermute x9, waiting for transfers between devices, shift_outer(): lax.ppermute(value, 'expert', [(place, (place + step * inner) % count) fo...  7.99 us
    concatenate x1, other arithmetic, dense_local(): other = swap(jnp.concatenate([w_gate[0], w_up[0], w_down[0]], axis=0))  3.38 us
    dot_general x3, matrix products, dense_local(): jnp.dot(own_grads[:, low:low + half].T, rows, preferred_element_type=jnp....  2.98 us
    dot_general x3, matrix products, dense_local(): jnp.dot(other_grads[:, low:low + half].T, other_rows, preferred_element_t...  2.17 us
  transfers between devices with their start and end apart: 25, of which 16 were waited for; matrix products, arithmetic and copies ran while one was open for 11% of the time, Pallas kernels for 0%

profile of v3, /device:TPU:0, one launch (start us, length us, event | category | flops | bytes accessed | tf_op | source)
XLA Modules:
  0.0 70.8 jit_solution(1042840928340474401)
XLA Ops:
  0.7 3.4 %pad_maximum_fusion.1 = bf16[576,2048]{1,0:T(8,128)(2,1)} fusion(bf16[192,2048]{1,0:T(8,128)(2,1)} %bitcast.18, bf16[192,2048]{1,0:T(8,128)(2,1)} %bitcast.20, bf16[192,2048]{1,0:T(8,128)(2,1)} %bitcast.23), kind=kLoop, calls=%fused_computation.11 | loop fusion | flops 7077888 | bytes 4718592 | tf_op jit(solution)/shard_map/concatenate | solution.py:193
  4.5 2.6 %collective-permute-start.1 = (bf16[16,2048]{1,0:T(8,128)(2,1)S(1)}, bf16[16,2048]{1,0:T(8,128)(2,1)S(1)}, u32[]{:S(2)}, u32[]{:S(2)}) collective-permute-start(bf16[16,2048]{1,0:T(8,128)(2,1)S(1)} %copy-done.4), channel_id=1, source_target_pairs={{0,4},{1,5},{2,6},{3,7},{4,8},{5,9},{6,10},{7,11},{8,12},{9,13},{1... | collective-permute-start | bytes 196616 | tf_op jit(solution)/shard_map/ppermute | solution.py:135
  7.1 2.6 %collective-permute-start.2 = (bf16[16,2048]{1,0:T(8,128)(2,1)S(1)}, bf16[16,2048]{1,0:T(8,128)(2,1)S(1)}, u32[]{:S(2)}, u32[]{:S(2)}) collective-permute-start(bf16[16,2048]{1,0:T(8,128)(2,1)S(1)} %copy-done.4), channel_id=1, source_target_pairs={{0,8},{1,9},{2,10},{3,11},{4,12},{5,13},{6,14},{7,15},{8,0},{9,1},... | collective-permute-start | bytes 196616 | tf_op jit(solution)/shard_map/ppermute | solution.py:135
  9.7 1.3 %collective-permute-start.3 = (bf16[16,2048]{1,0:T(8,128)(2,1)S(1)}, bf16[16,2048]{1,0:T(8,128)(2,1)S(1)}, u32[]{:S(2)}, u32[]{:S(2)}) collective-permute-start(bf16[16,2048]{1,0:T(8,128)(2,1)S(1)} %copy-done.4), channel_id=1, source_target_pairs={{0,12},{1,13},{2,14},{3,15},{4,0},{5,1},{6,2},{7,3},{8,4},{9,5},{1... | collective-permute-start | bytes 196616 | tf_op jit(solution)/shard_map/ppermute | solution.py:135
  13.2 1.5 %collective-permute-done.2 = bf16[16,2048]{1,0:T(8,128)(2,1)S(1)} collective-permute-done((bf16[16,2048]{1,0:T(8,128)(2,1)S(1)}, bf16[16,2048]{1,0:T(8,128)(2,1)S(1)}, u32[]{:S(2)}, u32[]{:S(2)}) %collective-permute-start.2) | collective-permute-done | bytes 65568 | tf_op jit(solution)/shard_map/ppermute | solution.py:135
  15.1 1.7 %collective-permute-start.5 = (bf16[16,2064]{1,0:T(8,128)(2,1)S(1)}, bf16[16,2064]{1,0:T(8,128)(2,1)S(1)}, u32[]{:S(2)}, u32[]{:S(2)}) collective-permute-start(bf16[16,2064]{1,0:T(8,128)(2,1)S(1)} %pad_maximum_fusion.6), channel_id=1, source_target_pairs={{0,4},{1,5},{2,6},{3,7},{4,8},{5,9},{6,10},{7,11},{8,12},{9,13},{1... | collective-permute-start | bytes 198152 | tf_op jit(solution)/shard_map/ppermute | solution.py:135
  16.7 1.6 %collective-permute-start.6 = (bf16[16,2064]{1,0:T(8,128)(2,1)S(1)}, bf16[16,2064]{1,0:T(8,128)(2,1)S(1)}, u32[]{:S(2)}, u32[]{:S(2)}) collective-permute-start(bf16[16,2064]{1,0:T(8,128)(2,1)S(1)} %pad_maximum_fusion.6), channel_id=1, source_target_pairs={{0,8},{1,9},{2,10},{3,11},{4,12},{5,13},{6,14},{7,15},{8,0},{9,1},... | collective-permute-start | bytes 198152 | tf_op jit(solution)/shard_map/ppermute | solution.py:135
  19.2 1.5 %collective-permute-start.12 = (bf16[64,2048]{1,0:T(8,128)(2,1)S(1)}, bf16[64,2048]{1,0:T(8,128)(2,1)S(1)}, u32[]{:S(2)}, u32[]{:S(2)}) collective-permute-start(bf16[64,2048]{1,0:T(8,128)(2,1)S(1)} %pad_maximum_fusion.5), channel_id=1, source_target_pairs={{0,1},{1,0},{2,3},{3,2},{4,5},{5,4},{6,7},{7,6},{8,9},{9,8},{10,11... | collective-permute-start | bytes 786440 | tf_op jit(solution)/shard_map/ppermute | solution.py:141
  20.7 1.6 %collective-permute-start.13 = (bf16[64,2048]{1,0:T(8,128)(2,1)S(1)}, bf16[64,2048]{1,0:T(8,128)(2,1)S(1)}, u32[]{:S(2)}, u32[]{:S(2)}) collective-permute-start(bf16[64,2048]{1,0:T(8,128)(2,1)S(1)} %pad_maximum_fusion.5), channel_id=1, source_target_pairs={{0,2},{1,3},{2,0},{3,1},{4,6},{5,7},{6,4},{7,5},{8,10},{9,11},{10,... | collective-permute-start | bytes 786440 | tf_op jit(solution)/shard_map/ppermute | solution.py:141
  23.9 1.6 %collective-permute-start.8 = (bf16[64,2064]{1,0:T(8,128)(2,1)S(1)}, bf16[64,2064]{1,0:T(8,128)(2,1)S(1)}, u32[]{:S(2)}, u32[]{:S(2)}) collective-permute-start(bf16[64,2064]{1,0:T(8,128)(2,1)S(1)} %get-tuple-element.28), channel_id=1, source_target_pairs={{0,1},{1,0},{2,3},{3,2},{4,5},{5,4},{6,7},{7,6},{8,9},{9,8},{10,11... | collective-permute-start | bytes 792584 | tf_op jit(solution)/shard_map/ppermute | solution.py:141
  25.4 1.5 %collective-permute-start.9 = (bf16[64,2064]{1,0:T(8,128)(2,1)S(1)}, bf16[64,2064]{1,0:T(8,128)(2,1)S(1)}, u32[]{:S(2)}, u32[]{:S(2)}) collective-permute-start(bf16[64,2064]{1,0:T(8,128)(2,1)S(1)} %get-tuple-element.28), channel_id=1, source_target_pairs={{0,2},{1,3},{2,0},{3,1},{4,6},{5,7},{6,4},{7,5},{8,10},{9,11},{10,... | collective-permute-start | bytes 792584 | tf_op jit(solution)/shard_map/ppermute | solution.py:141
  27.3 1.6 %collective-permute-start.14 = (bf16[32,2048]{1,0:T(8,128)(2,1)S(1)}, bf16[32,2048]{1,0:T(8,128)(2,1)S(1)}, u32[]{:S(2)}, u32[]{:S(2)}) collective-permute-start(bf16[32,2048]{1,0:T(8,128)(2,1)S(1)} %slice.134), channel_id=1, source_target_pairs={{0,2},{1,3},{2,0},{3,1},{4,6},{5,7},{6,4},{7,5},{8,10},{9,11},{10,... | collective-permute-start | bytes 393224 | tf_op jit(solution)/shard_map/ppermute | solution.py:141
  28.9 1.6 %collective-permute-start.15 = (bf16[32,2048]{1,0:T(8,128)(2,1)S(1)}, bf16[32,2048]{1,0:T(8,128)(2,1)S(1)}, u32[]{:S(2)}, u32[]{:S(2)}) collective-permute-start(bf16[32,2048]{1,0:T(8,128)(2,1)S(1)} %slice.135), channel_id=1, source_target_pairs={{0,1},{1,0},{2,3},{3,2},{4,5},{5,4},{6,7},{7,6},{8,9},{9,8},{10,11... | collective-permute-start | bytes 393224 | tf_op jit(solution)/shard_map/ppermute | solution.py:141
  30.5 3.0 %collective-permute-done.8 = bf16[64,2064]{1,0:T(8,128)(2,1)S(1)} collective-permute-done((bf16[64,2064]{1,0:T(8,128)(2,1)S(1)}, bf16[64,2064]{1,0:T(8,128)(2,1)S(1)}, u32[]{:S(2)}, u32[]{:S(2)}) %collective-permute-start.8) | collective-permute-done | bytes 264224 | tf_op jit(solution)/shard_map/ppermute | solution.py:141
  33.5 1.6 %collective-permute-start.10 = (bf16[32,2064]{1,0:T(8,128)(2,1)S(1)}, bf16[32,2064]{1,0:T(8,128)(2,1)S(1)}, u32[]{:S(2)}, u32[]{:S(2)}) collective-permute-start(bf16[32,2064]{1,0:T(8,128)(2,1)S(1)} %slice.130), channel_id=1, source_target_pairs={{0,2},{1,3},{2,0},{3,1},{4,6},{5,7},{6,4},{7,5},{8,10},{9,11},{10,... | collective-permute-start | bytes 396296 | tf_op jit(solution)/shard_map/ppermute | solution.py:141
  35.1 1.6 %collective-permute-start.11 = (bf16[32,2064]{1,0:T(8,128)(2,1)S(1)}, bf16[32,2064]{1,0:T(8,128)(2,1)S(1)}, u32[]{:S(2)}, u32[]{:S(2)}) collective-permute-start(bf16[32,2064]{1,0:T(8,128)(2,1)S(1)} %slice.131), channel_id=1, source_target_pairs={{0,1},{1,0},{2,3},{3,2},{4,5},{5,4},{6,7},{7,6},{8,9},{9,8},{10,11... | collective-permute-start | bytes 396296 | tf_op jit(solution)/shard_map/ppermute | solution.py:141
  42.4 1.6 %collective-permute-start.16 = (bf16[64,2048]{1,0:T(8,128)(2,1)S(1)}, bf16[64,2048]{1,0:T(8,128)(2,1)S(1)}, u32[]{:S(2)}, u32[]{:S(2)}) collective-permute-start(bf16[64,2048]{1,0:T(8,128)(2,1)S(1)} %get-tuple-element.21), channel_id=1, source_target_pairs={{0,1},{1,0},{2,3},{3,2},{4,5},{5,4},{6,7},{7,6},{8,9},{9,8},{10,11... | collective-permute-start | bytes 786440 | tf_op jit(solution)/shard_map/ppermute | solution.py:141
  44.5 1.5 %collective-permute-start.18 = (bf16[64,2048]{1,0:T(8,128)(2,1)S(1)}, bf16[64,2048]{1,0:T(8,128)(2,1)S(1)}, u32[]{:S(2)}, u32[]{:S(2)}) collective-permute-start(bf16[64,2048]{1,0:T(8,128)(2,1)S(1)} %get-tuple-element.22), channel_id=1, source_target_pairs={{0,3},{1,2},{2,1},{3,0},{4,7},{5,6},{6,5},{7,4},{8,11},{9,10},{10,... | collective-permute-start | bytes 786440 | tf_op jit(solution)/shard_map/ppermute | solution.py:141
  46.6 5.2 %collective-permute-done.16 = bf16[64,2048]{1,0:T(8,128)(2,1)S(1)} collective-permute-done((bf16[64,2048]{1,0:T(8,128)(2,1)S(1)}, bf16[64,2048]{1,0:T(8,128)(2,1)S(1)}, u32[]{:S(2)}, u32[]{:S(2)}) %collective-permute-start.16) | collective-permute-done | bytes 262176 | tf_op jit(solution)/shard_map/ppermute | solution.py:141
  52.0 4.3 %collective-permute-done.18 = bf16[64,2048]{1,0:T(8,128)(2,1)S(1)} collective-permute-done((bf16[64,2048]{1,0:T(8,128)(2,1)S(1)}, bf16[64,2048]{1,0:T(8,128)(2,1)S(1)}, u32[]{:S(2)}, u32[]{:S(2)}) %collective-permute-start.18) | collective-permute-done | bytes 262176 | tf_op jit(solution)/shard_map/ppermute | solution.py:141
  57.2 2.1 %collective-permute-start.20 = (bf16[16,2048]{1,0:T(8,128)(2,1)S(1)}, bf16[16,2048]{1,0:T(8,128)(2,1)S(1)}, u32[]{:S(2)}, u32[]{:S(2)}) collective-permute-start(bf16[16,2048]{1,0:T(8,128)(2,1)S(1)} %get-tuple-element.27), channel_id=1, source_target_pairs={{0,8},{1,9},{2,10},{3,11},{4,12},{5,13},{6,14},{7,15},{8,0},{9,1},... | collective-permute-start | bytes 196616 | tf_op jit(solution)/shard_map/ppermute | solution.py:135
  61.2 2.3 %collective-permute-done.20 = bf16[16,2048]{1,0:T(8,128)(2,1)S(1)} collective-permute-done((bf16[16,2048]{1,0:T(8,128)(2,1)S(1)}, bf16[16,2048]{1,0:T(8,128)(2,1)S(1)}, u32[]{:S(2)}, u32[]{:S(2)}) %collective-permute-start.20) | collective-permute-done | bytes 65568 | tf_op jit(solution)/shard_map/ppermute | solution.py:135
  63.4 1.9 %collective-permute-done.21 = bf16[16,2048]{1,0:T(8,128)(2,1)S(1)} collective-permute-done((bf16[16,2048]{1,0:T(8,128)(2,1)S(1)}, bf16[16,2048]{1,0:T(8,128)(2,1)S(1)}, u32[]{:S(2)}, u32[]{:S(2)}) %collective-permute-start.21) | collective-permute-done | bytes 65568 | tf_op jit(solution)/shard_map/ppermute | solution.py:135
  69.5 1.3 %fusion.3 = bf16[1,192,2048]{2,1,0:T(8,128)(2,1)} fusion(f32[192,2048]{1,0:T(8,128)S(1)} %fusion.19, bf16[256,2048]{1,0:T(8,128)(2,1)S(1)} %collective-permute-done.24, bf16[256,576]{1,0:T(8,128)(2,1)S(1)} %collective-permute-done.22), kind=kOutput, calls=%fused_computation.8 | convolution fusion | flops 202113024 | bytes 3538944 | tf_op jit(solution)/shard_map/dot_general | solution.py:236
  (96 shorter events, 19.6 us)
Async XLA Ops:
  4.1 11.0 %collective-permute-start.4 = (bf16[576,2048]{1,0:T(8,128)(2,1)}, bf16[576,2048]{1,0:T(8,128)(2,1)S(1)}, u32[]{:S(2)}, u32[]{:S(2)}) collective-permute-start(bf16[576,2048]{1,0:T(8,128)(2,1)} %pad_maximum_fusion.1), channel_id=1, source_target_pairs={{0,16},{16,0},{1,17},{17,1},{2,18},{18,2},{3,19},{19,3},{4,20},{20... | collective-permute-start | bytes 7077896 | tf_op jit(solution)/shard_map/ppermute | solution.py:131
  4.5 8.7 %collective-permute-start.1 = (bf16[16,2048]{1,0:T(8,128)(2,1)S(1)}, bf16[16,2048]{1,0:T(8,128)(2,1)S(1)}, u32[]{:S(2)}, u32[]{:S(2)}) collective-permute-start(bf16[16,2048]{1,0:T(8,128)(2,1)S(1)} %copy-done.4), channel_id=1, source_target_pairs={{0,4},{1,5},{2,6},{3,7},{4,8},{5,9},{6,10},{7,11},{8,12},{9,13},{1... | collective-permute-start | bytes 196616 | tf_op jit(solution)/shard_map/ppermute | solution.py:135
  7.1 7.7 %collective-permute-start.2 = (bf16[16,2048]{1,0:T(8,128)(2,1)S(1)}, bf16[16,2048]{1,0:T(8,128)(2,1)S(1)}, u32[]{:S(2)}, u32[]{:S(2)}) collective-permute-start(bf16[16,2048]{1,0:T(8,128)(2,1)S(1)} %copy-done.4), channel_id=1, source_target_pairs={{0,8},{1,9},{2,10},{3,11},{4,12},{5,13},{6,14},{7,15},{8,0},{9,1},... | collective-permute-start | bytes 196616 | tf_op jit(solution)/shard_map/ppermute | solution.py:135
  9.7 5.4 %collective-permute-start.3 = (bf16[16,2048]{1,0:T(8,128)(2,1)S(1)}, bf16[16,2048]{1,0:T(8,128)(2,1)S(1)}, u32[]{:S(2)}, u32[]{:S(2)}) collective-permute-start(bf16[16,2048]{1,0:T(8,128)(2,1)S(1)} %copy-done.4), channel_id=1, source_target_pairs={{0,12},{1,13},{2,14},{3,15},{4,0},{5,1},{6,2},{7,3},{8,4},{9,5},{1... | collective-permute-start | bytes 196616 | tf_op jit(solution)/shard_map/ppermute | solution.py:135
  15.1 7.5 %collective-permute-start.5 = (bf16[16,2064]{1,0:T(8,128)(2,1)S(1)}, bf16[16,2064]{1,0:T(8,128)(2,1)S(1)}, u32[]{:S(2)}, u32[]{:S(2)}) collective-permute-start(bf16[16,2064]{1,0:T(8,128)(2,1)S(1)} %pad_maximum_fusion.6), channel_id=1, source_target_pairs={{0,4},{1,5},{2,6},{3,7},{4,8},{5,9},{6,10},{7,11},{8,12},{9,13},{1... | collective-permute-start | bytes 198152 | tf_op jit(solution)/shard_map/ppermute | solution.py:135
  16.7 7.0 %collective-permute-start.6 = (bf16[16,2064]{1,0:T(8,128)(2,1)S(1)}, bf16[16,2064]{1,0:T(8,128)(2,1)S(1)}, u32[]{:S(2)}, u32[]{:S(2)}) collective-permute-start(bf16[16,2064]{1,0:T(8,128)(2,1)S(1)} %pad_maximum_fusion.6), channel_id=1, source_target_pairs={{0,8},{1,9},{2,10},{3,11},{4,12},{5,13},{6,14},{7,15},{8,0},{9,1},... | collective-permute-start | bytes 198152 | tf_op jit(solution)/shard_map/ppermute | solution.py:135
  18.4 5.5 %collective-permute-start.7 = (bf16[16,2064]{1,0:T(8,128)(2,1)S(1)}, bf16[16,2064]{1,0:T(8,128)(2,1)S(1)}, u32[]{:S(2)}, u32[]{:S(2)}) collective-permute-start(bf16[16,2064]{1,0:T(8,128)(2,1)S(1)} %pad_maximum_fusion.6), channel_id=1, source_target_pairs={{0,12},{1,13},{2,14},{3,15},{4,0},{5,1},{6,2},{7,3},{8,4},{9,5},{1... | collective-permute-start | bytes 198152 | tf_op jit(solution)/shard_map/ppermute | solution.py:135
  19.2 8.1 %collective-permute-start.12 = (bf16[64,2048]{1,0:T(8,128)(2,1)S(1)}, bf16[64,2048]{1,0:T(8,128)(2,1)S(1)}, u32[]{:S(2)}, u32[]{:S(2)}) collective-permute-start(bf16[64,2048]{1,0:T(8,128)(2,1)S(1)} %pad_maximum_fusion.5), channel_id=1, source_target_pairs={{0,1},{1,0},{2,3},{3,2},{4,5},{5,4},{6,7},{7,6},{8,9},{9,8},{10,11... | collective-permute-start | bytes 786440 | tf_op jit(solution)/shard_map/ppermute | solution.py:141
  20.7 8.2 %collective-permute-start.13 = (bf16[64,2048]{1,0:T(8,128)(2,1)S(1)}, bf16[64,2048]{1,0:T(8,128)(2,1)S(1)}, u32[]{:S(2)}, u32[]{:S(2)}) collective-permute-start(bf16[64,2048]{1,0:T(8,128)(2,1)S(1)} %pad_maximum_fusion.5), channel_id=1, source_target_pairs={{0,2},{1,3},{2,0},{3,1},{4,6},{5,7},{6,4},{7,5},{8,10},{9,11},{10,... | collective-permute-start | bytes 786440 | tf_op jit(solution)/shard_map/ppermute | solution.py:141
  23.9 9.6 %collective-permute-start.8 = (bf16[64,2064]{1,0:T(8,128)(2,1)S(1)}, bf16[64,2064]{1,0:T(8,128)(2,1)S(1)}, u32[]{:S(2)}, u32[]{:S(2)}) collective-permute-start(bf16[64,2064]{1,0:T(8,128)(2,1)S(1)} %get-tuple-element.28), channel_id=1, source_target_pairs={{0,1},{1,0},{2,3},{3,2},{4,5},{5,4},{6,7},{7,6},{8,9},{9,8},{10,11... | collective-permute-start | bytes 792584 | tf_op jit(solution)/shard_map/ppermute | solution.py:141
  25.4 9.7 %collective-permute-start.9 = (bf16[64,2064]{1,0:T(8,128)(2,1)S(1)}, bf16[64,2064]{1,0:T(8,128)(2,1)S(1)}, u32[]{:S(2)}, u32[]{:S(2)}) collective-permute-start(bf16[64,2064]{1,0:T(8,128)(2,1)S(1)} %get-tuple-element.28), channel_id=1, source_target_pairs={{0,2},{1,3},{2,0},{3,1},{4,6},{5,7},{6,4},{7,5},{8,10},{9,11},{10,... | collective-permute-start | bytes 792584 | tf_op jit(solution)/shard_map/ppermute | solution.py:141
  27.3 10.5 %collective-permute-start.14 = (bf16[32,2048]{1,0:T(8,128)(2,1)S(1)}, bf16[32,2048]{1,0:T(8,128)(2,1)S(1)}, u32[]{:S(2)}, u32[]{:S(2)}) collective-permute-start(bf16[32,2048]{1,0:T(8,128)(2,1)S(1)} %slice.134), channel_id=1, source_target_pairs={{0,2},{1,3},{2,0},{3,1},{4,6},{5,7},{6,4},{7,5},{8,10},{9,11},{10,... | collective-permute-start | bytes 393224 | tf_op jit(solution)/shard_map/ppermute | solution.py:141
  28.9 8.9 %collective-permute-start.15 = (bf16[32,2048]{1,0:T(8,128)(2,1)S(1)}, bf16[32,2048]{1,0:T(8,128)(2,1)S(1)}, u32[]{:S(2)}, u32[]{:S(2)}) collective-permute-start(bf16[32,2048]{1,0:T(8,128)(2,1)S(1)} %slice.135), channel_id=1, source_target_pairs={{0,1},{1,0},{2,3},{3,2},{4,5},{5,4},{6,7},{7,6},{8,9},{9,8},{10,11... | collective-permute-start | bytes 393224 | tf_op jit(solution)/shard_map/ppermute | solution.py:141
  33.5 6.4 %collective-permute-start.10 = (bf16[32,2064]{1,0:T(8,128)(2,1)S(1)}, bf16[32,2064]{1,0:T(8,128)(2,1)S(1)}, u32[]{:S(2)}, u32[]{:S(2)}) collective-permute-start(bf16[32,2064]{1,0:T(8,128)(2,1)S(1)} %slice.130), channel_id=1, source_target_pairs={{0,2},{1,3},{2,0},{3,1},{4,6},{5,7},{6,4},{7,5},{8,10},{9,11},{10,... | collective-permute-start | bytes 396296 | tf_op jit(solution)/shard_map/ppermute | solution.py:141
  35.1 5.1 %collective-permute-start.11 = (bf16[32,2064]{1,0:T(8,128)(2,1)S(1)}, bf16[32,2064]{1,0:T(8,128)(2,1)S(1)}, u32[]{:S(2)}, u32[]{:S(2)}) collective-permute-start(bf16[32,2064]{1,0:T(8,128)(2,1)S(1)} %slice.131), channel_id=1, source_target_pairs={{0,1},{1,0},{2,3},{3,2},{4,5},{5,4},{6,7},{7,6},{8,9},{9,8},{10,11... | collective-permute-start | bytes 396296 | tf_op jit(solution)/shard_map/ppermute | solution.py:141
  42.4 9.3 %collective-permute-start.16 = (bf16[64,2048]{1,0:T(8,128)(2,1)S(1)}, bf16[64,2048]{1,0:T(8,128)(2,1)S(1)}, u32[]{:S(2)}, u32[]{:S(2)}) collective-permute-start(bf16[64,2048]{1,0:T(8,128)(2,1)S(1)} %get-tuple-element.21), channel_id=1, source_target_pairs={{0,1},{1,0},{2,3},{3,2},{4,5},{5,4},{6,7},{7,6},{8,9},{9,8},{10,11... | collective-permute-start | bytes 786440 | tf_op jit(solution)/shard_map/ppermute | solution.py:141
  44.0 8.0 %collective-permute-start.17 = (bf16[64,2048]{1,0:T(8,128)(2,1)S(1)}, bf16[64,2048]{1,0:T(8,128)(2,1)S(1)}, u32[]{:S(2)}, u32[]{:S(2)}) collective-permute-start(bf16[64,2048]{1,0:T(8,128)(2,1)S(1)} %get-tuple-element.23), channel_id=1, source_target_pairs={{0,2},{1,3},{2,0},{3,1},{4,6},{5,7},{6,4},{7,5},{8,10},{9,11},{10,... | collective-permute-start | bytes 786440 | tf_op jit(solution)/shard_map/ppermute | solution.py:141
  44.5 11.8 %collective-permute-start.18 = (bf16[64,2048]{1,0:T(8,128)(2,1)S(1)}, bf16[64,2048]{1,0:T(8,128)(2,1)S(1)}, u32[]{:S(2)}, u32[]{:S(2)}) collective-permute-start(bf16[64,2048]{1,0:T(8,128)(2,1)S(1)} %get-tuple-element.22), channel_id=1, source_target_pairs={{0,3},{1,2},{2,1},{3,0},{4,7},{5,6},{6,5},{7,4},{8,11},{9,10},{10,... | collective-permute-start | bytes 786440 | tf_op jit(solution)/shard_map/ppermute | solution.py:141
  46.0 20.1 %collective-permute-start.23 = (bf16[256,2048]{1,0:T(8,128)(2,1)S(1)}, bf16[256,2048]{1,0:T(8,128)(2,1)S(1)}, u32[]{:S(2)}, u32[]{:S(2)}) collective-permute-start(bf16[256,2048]{1,0:T(8,128)(2,1)S(1)} %constant_dynamic-update-slice_fusion.12), channel_id=1, source_target_pairs={{0,16},{16,0},{1,17},{17,1},{2,18},{18,2},{3,19},{19,3},{4,20},{20... | collective-permute-start | bytes 3145736 | tf_op jit(solution)/shard_map/ppermute | solution.py:131
  56.4 4.7 %collective-permute-start.19 = (bf16[16,2048]{1,0:T(8,128)(2,1)S(1)}, bf16[16,2048]{1,0:T(8,128)(2,1)S(1)}, u32[]{:S(2)}, u32[]{:S(2)}) collective-permute-start(bf16[16,2048]{1,0:T(8,128)(2,1)S(1)} %get-tuple-element.25), channel_id=1, source_target_pairs={{0,12},{1,13},{2,14},{3,15},{4,0},{5,1},{6,2},{7,3},{8,4},{9,5},{1... | collective-permute-start | bytes 196616 | tf_op jit(solution)/shard_map/ppermute | solution.py:135
  57.2 6.2 %collective-permute-start.20 = (bf16[16,2048]{1,0:T(8,128)(2,1)S(1)}, bf16[16,2048]{1,0:T(8,128)(2,1)S(1)}, u32[]{:S(2)}, u32[]{:S(2)}) collective-permute-start(bf16[16,2048]{1,0:T(8,128)(2,1)S(1)} %get-tuple-element.27), channel_id=1, source_target_pairs={{0,8},{1,9},{2,10},{3,11},{4,12},{5,13},{6,14},{7,15},{8,0},{9,1},... | collective-permute-start | bytes 196616 | tf_op jit(solution)/shard_map/ppermute | solution.py:135
  59.3 6.1 %collective-permute-start.21 = (bf16[16,2048]{1,0:T(8,128)(2,1)S(1)}, bf16[16,2048]{1,0:T(8,128)(2,1)S(1)}, u32[]{:S(2)}, u32[]{:S(2)}) collective-permute-start(bf16[16,2048]{1,0:T(8,128)(2,1)S(1)} %get-tuple-element.26), channel_id=1, source_target_pairs={{0,4},{1,5},{2,6},{3,7},{4,8},{5,9},{6,10},{7,11},{8,12},{9,13},{1... | collective-permute-start | bytes 196616 | tf_op jit(solution)/shard_map/ppermute | solution.py:135
  60.3 9.2 %collective-permute-start.24 = (bf16[256,2048]{1,0:T(8,128)(2,1)S(1)}, bf16[256,2048]{1,0:T(8,128)(2,1)S(1)}, u32[]{:S(2)}, u32[]{:S(2)}) collective-permute-start(bf16[256,2048]{1,0:T(8,128)(2,1)S(1)} %slice.133), channel_id=1, source_target_pairs={{0,16},{16,0},{1,17},{17,1},{2,18},{18,2},{3,19},{19,3},{4,20},{20... | collective-permute-start | bytes 3145736 | tf_op jit(solution)/shard_map/ppermute | solution.py:131
  61.2 4.9 %collective-permute-start.22 = (bf16[256,576]{1,0:T(8,128)(2,1)S(1)}, bf16[256,576]{1,0:T(8,128)(2,1)S(1)}, u32[]{:S(2)}, u32[]{:S(2)}) collective-permute-start(bf16[256,576]{1,0:T(8,128)(2,1)S(1)} %pad_maximum_fusion.4), channel_id=1, source_target_pairs={{0,16},{16,0},{1,17},{17,1},{2,18},{18,2},{3,19},{19,3},{4,20},{20... | collective-permute-start | bytes 884744 | tf_op jit(solution)/shard_map/ppermute | solution.py:131
  (9 other events, 69.4 us)

commit v4 on v3

--- a/solution.py
+++ b/solution.py
@@ -170,13 +170,9 @@
     return [column, first, second, far_top, far_bottom]
 
 
-def bring_back(value, count, inner):
+def return_outer(total, count, inner):
     outer = count // inner
-    blocks = value.reshape(inner, -1, value.shape[-1])
-    total = blocks[0].astype(jnp.float32)
-    for partner in range(1, inner):
-        total = total + swap_inner(blocks[partner], count, partner).astype(jnp.float32)
-    blocks = total.reshape(outer, -1, value.shape[-1])
+    blocks = total.reshape(outer, -1, total.shape[-1])
     rounded = blocks.astype(jnp.bfloat16)
     total = blocks[0]
     for step in range(1, outer):
@@ -184,20 +180,43 @@
     return total.astype(jnp.bfloat16)
 
 
+def return_inner(blocks, count):
+    if len(blocks) < 4:
+        total = blocks[0]
+        for partner in range(1, len(blocks)):
+            block = blocks[partner].astype(jnp.bfloat16)
+            total = total + swap_inner(block, count, partner).astype(jnp.float32)
+        return total
+    cut = blocks[3].shape[0] // 2
+    far = blocks[3].astype(jnp.bfloat16)
+    top = swap_inner(far[:cut], count, 2).astype(jnp.float32)
+    bottom = swap_inner(far[cut:], count, 1).astype(jnp.float32)
+    first = jnp.concatenate([blocks[1][:cut] + top, blocks[1][cut:]], axis=0)
+    second = jnp.concatenate([blocks[2][:cut], blocks[2][cut:] + bottom], axis=0)
+    first = swap_inner(first.astype(jnp.bfloat16), count, 1)
+    second = swap_inner(second.astype(jnp.bfloat16), count, 2)
+    return blocks[0] + first.astype(jnp.float32) + second.astype(jnp.float32)
+
+
 def dense_local(tokens, cotangent, gate_values, expert_ids, packing, w_gate, w_up, w_down):
     model_width = tokens.shape[1]
     half = w_gate.shape[1]
     count = lax.axis_size("expert")
     inner = math.gcd(count, 4)
-    token_column = jnp.concatenate(along_outer(tokens, count, inner), axis=0)
-    other = swap(jnp.concatenate([w_gate[0], w_up[0], w_down[0]], axis=0))
+    token_blocks = along_outer(tokens, count, inner)
+    own_weights = jnp.concatenate([w_gate[0], w_up[0], w_down[0]], axis=0)
     gates = home_gates(packing, expert_ids, gate_values, count).astype(jnp.bfloat16)
     payload = jnp.concatenate([cotangent, gates], axis=1)
-    payload, token_column, other = lax.optimization_barrier((payload, token_column, other))
+    payload, token_blocks[1] = lax.optimization_barrier((payload, token_blocks[1]))
+    token_column = jnp.concatenate(token_blocks, axis=0)
     upstream_column = jnp.concatenate(along_outer(payload, count, inner), axis=0)
-    inputs = jnp.concatenate(across_inner(token_column, count, inner), axis=0)
+    token_columns = across_inner(token_column, count, inner)
+    own_weights, token_columns[1] = lax.optimization_barrier((own_weights, token_columns[1]))
+    other = swap(own_weights)
+    inputs = jnp.concatenate(token_columns, axis=0)
     other_inputs = swap(inputs)
     upstream = jnp.concatenate(across_inner(upstream_column, count, inner), axis=0)
+    upstream, other_inputs = lax.optimization_barrier((upstream, other_inputs))
     here = jnp.arange(count, dtype=jnp.int32) == lax.axis_index("expert")
     gate = jnp.sum(
         jnp.where(here[None, :], upstream[:, model_width:].astype(jnp.float32), 0.0),
@@ -217,13 +236,16 @@
     gate_grad = (hidden_grad * up_pre * silu_slope).astype(jnp.bfloat16)
     up_grad = (hidden_grad * activated).astype(jnp.bfloat16)
     both_grad = jnp.concatenate([gate_grad, up_grad], axis=1)
-    partial_grad = jnp.dot(both_grad, gate_up, preferred_element_type=jnp.float32)
-    partial_grad = partial_grad.astype(jnp.bfloat16)
-    input_grad = bring_back(partial_grad, count, inner)
+    depth = both_grad.shape[0] // inner
+    blocks = [
+        jnp.dot(both_grad[low : low + depth], gate_up, preferred_element_type=jnp.float32)
+        for low in range(0, both_grad.shape[0], depth)
+    ]
+    input_grad = return_outer(return_inner(blocks, count), count, inner)
     grads = (gate_grad, up_grad, hidden)
     own_grads = jnp.concatenate([grad[:, :half] for grad in grads], axis=1)
     sent_grads = jnp.concatenate([grad[:, half:] for grad in grads], axis=1)
-    sent_grads, upstream, _ = lax.optimization_barrier((sent_grads, upstream, partial_grad))
+    sent_grads, upstream, _ = lax.optimization_barrier((sent_grads, upstream, blocks[-1]))
     other_grads = swap(sent_grads)
     other_upstream = swap(upstream)
     weight_grads = []

time: 71 us -> 82.1 us (1.16)
  local copies, waits for them, and re-layouts: 1.48 us -> 8.78 us
  other arithmetic: 5.04 us -> 8.19 us
  starting transfers between devices: 30.6 us -> 28 us
  matrix products: 8.17 us -> 9.76 us
  waiting for transfers between devices: 24.5 us -> 25.9 us
    unnamed x27 -> x22, local copies, waits for them, and re-layouts: 0.29 us -> 6.34 us
    ppermute x11 -> x12, starting transfers between devices: 16 us -> 12.2 us  [swap_inner(): lax.ppermute(value, 'expert', [(place, place ^ partner) for place in rang...]
    ppermute x11 -> x12, waiting for transfers between devices: 15.4 us -> 18.5 us  [swap_inner(): lax.ppermute(value, 'expert', [(place, place ^ partner) for place in rang...]
    dot_general x1 -> x4, matrix products: 1.2 us -> 2.73 us  [dense_local(): jnp.dot(both_grad[low:low + depth], gate_up, preferred_element_type=jnp.f...]
    concatenate x2 -> x4, other arithmetic: 3.4 us -> 2.25 us  [the longest x1 1.76 us: dense_local(): own_weights = jnp.concatenate([w_gate[0], w_up[0], w_down[0]], axis=0)]
    ppermute x5, waiting for transfers between devices: 1.14 us -> 0.01 us  [swap(): return lax.ppermute(value, 'dp', [(0, 1), (1, 0)])]
    ppermute x9, starting transfers between devices: 14.1 us -> 15.1 us  [shift_outer(): lax.ppermute(value, 'expert', [(place, (place + step * inner) % count) fo...]
    concatenate x1, other arithmetic: 0.01 us -> 0.85 us  [dense_local(): payload = jnp.concatenate([cotangent, gates], axis=1)]
  transfers between devices with their start and end apart: 25 -> 26, of which waited for: 16 -> 12; matrix products, arithmetic and copies ran while one was open for 11% -> 23% of each run, Pallas kernels for 0% -> 0%
where the time goes in v4:
time: 82.1 us; the launch traced here: 81.6 us
  starting transfers between devices  28 us (34%)
  waiting for transfers between devices  25.9 us (32%)
  matrix products  9.76 us (12%)
  local copies, waits for them, and re-layouts  8.78 us (11%)
  other arithmetic  8.19 us (10%)
  between operations  0.99 us (1%)
    ppermute x12, waiting for transfers between devices, swap_inner(): lax.ppermute(value, 'expert', [(place, place ^ partner) for place in rang...  18.5 us
    ppermute x9, starting transfers between devices, shift_outer(): lax.ppermute(value, 'expert', [(place, (place + step * inner) % count) fo...  15.1 us
    ppermute x12, starting transfers between devices, swap_inner(): lax.ppermute(value, 'expert', [(place, place ^ partner) for place in rang...  12.2 us
    ppermute x9, waiting for transfers between devices, shift_outer(): lax.ppermute(value, 'expert', [(place, (place + step * inner) % count) fo...  7.4 us
    unnamed x22, local copies, waits for them, and re-layouts  6.34 us
    dot_general x3, matrix products, dense_local(): jnp.dot(own_grads[:, low:low + half].T, rows, preferred_element_type=jnp....  3.01 us
    dot_general x4, matrix products, dense_local(): jnp.dot(both_grad[low:low + depth], gate_up, preferred_element_type=jnp.f...  2.73 us
    dot_general x3, matrix products, dense_local(): jnp.dot(other_grads[:, low:low + half].T, other_rows, preferred_element_t...  2.18 us
  transfers between devices with their start and end apart: 26, of which 12 were waited for; matrix products, arithmetic and copies ran while one was open for 23% of the time, Pallas kernels for 0%

profile of v4, /device:TPU:0, one launch (start us, length us, event | category | flops | bytes accessed | tf_op | source)
XLA Modules:
  0.0 81.6 jit_solution(12473034781753961584)
XLA Ops:
  0.6 3.1 %collective-permute-start.1 = (bf16[16,2048]{1,0:T(8,128)(2,1)}, bf16[16,2048]{1,0:T(8,128)(2,1)}, u32[]{:S(2)}, u32[]{:S(2)}) collective-permute-start(bf16[16,2048]{1,0:T(8,128)(2,1)} %param.8), channel_id=1, source_target_pairs={{0,4},{1,5},{2,6},{3,7},{4,8},{5,9},{6,10},{7,11},{8,12},{9,13},{1... | collective-permute-start | bytes 196616 | tf_op jit(solution)/shard_map/ppermute | solution.py:135
  3.7 2.6 %collective-permute-start.9 = (bf16[16,2048]{1,0:T(8,128)(2,1)}, bf16[16,2048]{1,0:T(8,128)(2,1)S(1)}, u32[]{:S(2)}, u32[]{:S(2)}) collective-permute-start(bf16[16,2048]{1,0:T(8,128)(2,1)} %param.8), channel_id=1, source_target_pairs={{0,8},{1,9},{2,10},{3,11},{4,12},{5,13},{6,14},{7,15},{8,0},{9,1},... | collective-permute-start | bytes 196616 | tf_op jit(solution)/shard_map/ppermute | solution.py:135
  6.3 1.3 %collective-permute-start.10 = (bf16[16,2048]{1,0:T(8,128)(2,1)}, bf16[16,2048]{1,0:T(8,128)(2,1)S(1)}, u32[]{:S(2)}, u32[]{:S(2)}) collective-permute-start(bf16[16,2048]{1,0:T(8,128)(2,1)} %param.8), channel_id=1, source_target_pairs={{0,12},{1,13},{2,14},{3,15},{4,0},{5,1},{6,2},{7,3},{8,4},{9,5},{1... | collective-permute-start | bytes 196616 | tf_op jit(solution)/shard_map/ppermute | solution.py:135
  10.1 1.5 %constant_dynamic-update-slice_fusion.23 = (bf16[256,2048]{1,0:T(8,128)(2,1)S(1)}, bf16[64,2048]{1,0:T(8,128)(2,1)}) fusion(bf16[16,2048]{1,0:T(8,128)(2,1)} %param.8), kind=kLoop, calls=%fused_computation.87 | loop fusion | bytes 196608
  12.1 1.8 %pad_maximum_fusion.1 = bf16[576,2048]{1,0:T(8,128)(2,1)S(1)} fusion(bf16[192,2048]{1,0:T(8,128)(2,1)} %bitcast.27, bf16[192,2048]{1,0:T(8,128)(2,1)} %bitcast.23, bf16[192,2048]{1,0:T(8,128)(2,1)} %bitcast.25), kind=kLoop, calls=%fused_computation.10 | loop fusion | flops 7077888 | bytes 4718592 | tf_op jit(solution)/shard_map/concatenate | solution.py:207
  18.3 1.5 %constant_dynamic-update-slice_fusion.22 = (bf16[256,2048]{1,0:T(8,128)(2,1)S(1)}, bf16[64,2048]{1,0:T(8,128)(2,1)}) fusion(bf16[256,2048]{1,0:T(8,128)(2,1)S(1)} %get-tuple-element.45, bf16[16,2048]{1,0:T(8,128)(2,1)} %collective-permute-done.1, bf16[64,2048]{1,0:T(8,128)(2,1)} %get-tuple-element.46), kind=kLoop, calls=%fused_computation.86 | loop fusion | bytes 196608
  21.0 1.5 %collective-permute-start.11 = (bf16[64,2048]{1,0:T(8,128)(2,1)}, bf16[64,2048]{1,0:T(8,128)(2,1)S(1)}, u32[]{:S(2)}, u32[]{:S(2)}) collective-permute-start(bf16[64,2048]{1,0:T(8,128)(2,1)} %get-tuple-element.40), channel_id=1, source_target_pairs={{0,1},{1,0},{2,3},{3,2},{4,5},{5,4},{6,7},{7,6},{8,9},{9,8},{10,11... | collective-permute-start | bytes 786440 | tf_op jit(solution)/shard_map/ppermute | solution.py:141
  22.5 1.5 %collective-permute-start.12 = (bf16[64,2048]{1,0:T(8,128)(2,1)}, bf16[64,2048]{1,0:T(8,128)(2,1)S(1)}, u32[]{:S(2)}, u32[]{:S(2)}) collective-permute-start(bf16[64,2048]{1,0:T(8,128)(2,1)} %get-tuple-element.40), channel_id=1, source_target_pairs={{0,2},{1,3},{2,0},{3,1},{4,6},{5,7},{6,4},{7,5},{8,10},{9,11},{10,... | collective-permute-start | bytes 786440 | tf_op jit(solution)/shard_map/ppermute | solution.py:141
  25.1 2.9 %collective-permute-start.4 = (bf16[16,2064]{1,0:T(8,128)(2,1)S(1)}, bf16[16,2064]{1,0:T(8,128)(2,1)S(1)}, u32[]{:S(2)}, u32[]{:S(2)}) collective-permute-start(bf16[16,2064]{1,0:T(8,128)(2,1)S(1)} %pad_maximum_fusion.7), channel_id=1, source_target_pairs={{0,12},{1,13},{2,14},{3,15},{4,0},{5,1},{6,2},{7,3},{8,4},{9,5},{1... | collective-permute-start | bytes 198152 | tf_op jit(solution)/shard_map/ppermute | solution.py:135
  28.0 2.9 %collective-permute-done.2 = bf16[16,2064]{1,0:T(8,128)(2,1)S(1)} collective-permute-done((bf16[16,2064]{1,0:T(8,128)(2,1)S(1)}, bf16[16,2064]{1,0:T(8,128)(2,1)S(1)}, u32[]{:S(2)}, u32[]{:S(2)}) %collective-permute-start.2) | collective-permute-done | bytes 66080 | tf_op jit(solution)/shard_map/ppermute | solution.py:135
  31.0 2.0 %collective-permute-done.3 = bf16[16,2064]{1,0:T(8,128)(2,1)S(1)} collective-permute-done((bf16[16,2064]{1,0:T(8,128)(2,1)S(1)}, bf16[16,2064]{1,0:T(8,128)(2,1)S(1)}, u32[]{:S(2)}, u32[]{:S(2)}) %collective-permute-start.3) | collective-permute-done | bytes 66080 | tf_op jit(solution)/shard_map/ppermute | solution.py:135
  34.2 1.6 %collective-permute-start.13 = (bf16[32,2048]{1,0:T(8,128)(2,1)S(1)}, bf16[32,2048]{1,0:T(8,128)(2,1)S(1)}, u32[]{:S(2)}, u32[]{:S(2)}) collective-permute-start(bf16[32,2048]{1,0:T(8,128)(2,1)S(1)} %slice.154), channel_id=1, source_target_pairs={{0,2},{1,3},{2,0},{3,1},{4,6},{5,7},{6,4},{7,5},{8,10},{9,11},{10,... | collective-permute-start | bytes 393224 | tf_op jit(solution)/shard_map/ppermute | solution.py:141
  35.8 1.6 %collective-permute-start.14 = (bf16[32,2048]{1,0:T(8,128)(2,1)S(1)}, bf16[32,2048]{1,0:T(8,128)(2,1)S(1)}, u32[]{:S(2)}, u32[]{:S(2)}) collective-permute-start(bf16[32,2048]{1,0:T(8,128)(2,1)S(1)} %slice.155), channel_id=1, source_target_pairs={{0,1},{1,0},{2,3},{3,2},{4,5},{5,4},{6,7},{7,6},{8,9},{9,8},{10,11... | collective-permute-start | bytes 393224 | tf_op jit(solution)/shard_map/ppermute | solution.py:141
  37.4 4.2 %collective-permute-done.5 = bf16[64,2064]{1,0:T(8,128)(2,1)S(1)} collective-permute-done((bf16[64,2064]{1,0:T(8,128)(2,1)S(1)}, bf16[64,2064]{1,0:T(8,128)(2,1)S(1)}, u32[]{:S(2)}, u32[]{:S(2)}) %collective-permute-start.5) | collective-permute-done | bytes 264224 | tf_op jit(solution)/shard_map/ppermute | solution.py:141
  43.2 1.6 %collective-permute-start.8 = (bf16[32,2064]{1,0:T(8,128)(2,1)S(1)}, bf16[32,2064]{1,0:T(8,128)(2,1)S(1)}, u32[]{:S(2)}, u32[]{:S(2)}) collective-permute-start(bf16[32,2064]{1,0:T(8,128)(2,1)S(1)} %slice.153), channel_id=1, source_target_pairs={{0,1},{1,0},{2,3},{3,2},{4,5},{5,4},{6,7},{7,6},{8,9},{9,8},{10,11... | collective-permute-start | bytes 396296 | tf_op jit(solution)/shard_map/ppermute | solution.py:141
  45.0 1.7 %collective-permute-done.7 = bf16[32,2064]{1,0:T(8,128)(2,1)S(1)} collective-permute-done((bf16[32,2064]{1,0:T(8,128)(2,1)S(1)}, bf16[32,2064]{1,0:T(8,128)(2,1)S(1)}, u32[]{:S(2)}, u32[]{:S(2)}) %collective-permute-start.7) | collective-permute-done | bytes 132128 | tf_op jit(solution)/shard_map/ppermute | solution.py:141
  46.7 1.6 %collective-permute-done.8 = bf16[32,2064]{1,0:T(8,128)(2,1)S(1)} collective-permute-done((bf16[32,2064]{1,0:T(8,128)(2,1)S(1)}, bf16[32,2064]{1,0:T(8,128)(2,1)S(1)}, u32[]{:S(2)}, u32[]{:S(2)}) %collective-permute-start.8) | collective-permute-done | bytes 132128 | tf_op jit(solution)/shard_map/ppermute | solution.py:141
  54.7 1.6 %collective-permute-start.19 = (bf16[32,2048]{1,0:T(8,128)(2,1)S(1)}, bf16[32,2048]{1,0:T(8,128)(2,1)S(1)}, u32[]{:S(2)}, u32[]{:S(2)}) collective-permute-start(bf16[32,2048]{1,0:T(8,128)(2,1)S(1)} %get-tuple-element.30), channel_id=1, source_target_pairs={{0,1},{1,0},{2,3},{3,2},{4,5},{5,4},{6,7},{7,6},{8,9},{9,8},{10,11... | collective-permute-start | bytes 393224 | tf_op jit(solution)/shard_map/ppermute | solution.py:141
  57.7 2.0 %collective-permute-done.19 = bf16[32,2048]{1,0:T(8,128)(2,1)S(1)} collective-permute-done((bf16[32,2048]{1,0:T(8,128)(2,1)S(1)}, bf16[32,2048]{1,0:T(8,128)(2,1)S(1)}, u32[]{:S(2)}, u32[]{:S(2)}) %collective-permute-start.19) | collective-permute-done | bytes 131104 | tf_op jit(solution)/shard_map/ppermute | solution.py:141
  60.3 3.1 %collective-permute-done.17 = bf16[32,2048]{1,0:T(8,128)(2,1)S(1)} collective-permute-done((bf16[32,2048]{1,0:T(8,128)(2,1)S(1)}, bf16[32,2048]{1,0:T(8,128)(2,1)S(1)}, u32[]{:S(2)}, u32[]{:S(2)}) %collective-permute-start.17) | collective-permute-done | bytes 131104 | tf_op jit(solution)/shard_map/ppermute | solution.py:141
  66.2 2.4 %collective-permute-done.20 = bf16[64,2048]{1,0:T(8,128)(2,1)S(1)} collective-permute-done((bf16[64,2048]{1,0:T(8,128)(2,1)S(1)}, bf16[64,2048]{1,0:T(8,128)(2,1)S(1)}, u32[]{:S(2)}, u32[]{:S(2)}) %collective-permute-start.20) | collective-permute-done | bytes 262176 | tf_op jit(solution)/shard_map/ppermute | solution.py:141
  68.6 2.4 %collective-permute-done.18 = bf16[64,2048]{1,0:T(8,128)(2,1)S(1)} collective-permute-done((bf16[64,2048]{1,0:T(8,128)(2,1)S(1)}, bf16[64,2048]{1,0:T(8,128)(2,1)S(1)}, u32[]{:S(2)}, u32[]{:S(2)}) %collective-permute-start.18) | collective-permute-done | bytes 262176 | tf_op jit(solution)/shard_map/ppermute | solution.py:141
  71.8 1.7 %collective-permute-start.23 = (bf16[16,2048]{1,0:T(8,128)(2,1)S(1)}, bf16[16,2048]{1,0:T(8,128)(2,1)S(1)}, u32[]{:S(2)}, u32[]{:S(2)}) collective-permute-start(bf16[16,2048]{1,0:T(8,128)(2,1)S(1)} %get-tuple-element.27), channel_id=1, source_target_pairs={{0,4},{1,5},{2,6},{3,7},{4,8},{5,9},{6,10},{7,11},{8,12},{9,13},{1... | collective-permute-start | bytes 196616 | tf_op jit(solution)/shard_map/ppermute | solution.py:135
  78.0 1.6 %collective-permute-done.22 = bf16[16,2048]{1,0:T(8,128)(2,1)S(1)} collective-permute-done((bf16[16,2048]{1,0:T(8,128)(2,1)S(1)}, bf16[16,2048]{1,0:T(8,128)(2,1)S(1)}, u32[]{:S(2)}, u32[]{:S(2)}) %collective-permute-start.22) | collective-permute-done | bytes 65568 | tf_op jit(solution)/shard_map/ppermute | solution.py:135
  (101 shorter events, 31.0 us)
Async XLA Ops:
  0.6 17.6 %collective-permute-start.1 = (bf16[16,2048]{1,0:T(8,128)(2,1)}, bf16[16,2048]{1,0:T(8,128)(2,1)}, u32[]{:S(2)}, u32[]{:S(2)}) collective-permute-start(bf16[16,2048]{1,0:T(8,128)(2,1)} %param.8), channel_id=1, source_target_pairs={{0,4},{1,5},{2,6},{3,7},{4,8},{5,9},{6,10},{7,11},{8,12},{9,13},{1... | collective-permute-start | bytes 196616 | tf_op jit(solution)/shard_map/ppermute | solution.py:135
  3.7 16.0 %collective-permute-start.9 = (bf16[16,2048]{1,0:T(8,128)(2,1)}, bf16[16,2048]{1,0:T(8,128)(2,1)S(1)}, u32[]{:S(2)}, u32[]{:S(2)}) collective-permute-start(bf16[16,2048]{1,0:T(8,128)(2,1)} %param.8), channel_id=1, source_target_pairs={{0,8},{1,9},{2,10},{3,11},{4,12},{5,13},{6,14},{7,15},{8,0},{9,1},... | collective-permute-start | bytes 196616 | tf_op jit(solution)/shard_map/ppermute | solution.py:135
  6.3 14.1 %collective-permute-start.10 = (bf16[16,2048]{1,0:T(8,128)(2,1)}, bf16[16,2048]{1,0:T(8,128)(2,1)S(1)}, u32[]{:S(2)}, u32[]{:S(2)}) collective-permute-start(bf16[16,2048]{1,0:T(8,128)(2,1)} %param.8), channel_id=1, source_target_pairs={{0,12},{1,13},{2,14},{3,15},{4,0},{5,1},{6,2},{7,3},{8,4},{9,5},{1... | collective-permute-start | bytes 196616 | tf_op jit(solution)/shard_map/ppermute | solution.py:135
  21.0 13.1 %collective-permute-start.11 = (bf16[64,2048]{1,0:T(8,128)(2,1)}, bf16[64,2048]{1,0:T(8,128)(2,1)S(1)}, u32[]{:S(2)}, u32[]{:S(2)}) collective-permute-start(bf16[64,2048]{1,0:T(8,128)(2,1)} %get-tuple-element.40), channel_id=1, source_target_pairs={{0,1},{1,0},{2,3},{3,2},{4,5},{5,4},{6,7},{7,6},{8,9},{9,8},{10,11... | collective-permute-start | bytes 786440 | tf_op jit(solution)/shard_map/ppermute | solution.py:141
  22.5 13.2 %collective-permute-start.12 = (bf16[64,2048]{1,0:T(8,128)(2,1)}, bf16[64,2048]{1,0:T(8,128)(2,1)S(1)}, u32[]{:S(2)}, u32[]{:S(2)}) collective-permute-start(bf16[64,2048]{1,0:T(8,128)(2,1)} %get-tuple-element.40), channel_id=1, source_target_pairs={{0,2},{1,3},{2,0},{3,1},{4,6},{5,7},{6,4},{7,5},{8,10},{9,11},{10,... | collective-permute-start | bytes 786440 | tf_op jit(solution)/shard_map/ppermute | solution.py:141
  24.0 6.9 %collective-permute-start.2 = (bf16[16,2064]{1,0:T(8,128)(2,1)S(1)}, bf16[16,2064]{1,0:T(8,128)(2,1)S(1)}, u32[]{:S(2)}, u32[]{:S(2)}) collective-permute-start(bf16[16,2064]{1,0:T(8,128)(2,1)S(1)} %pad_maximum_fusion.7), channel_id=1, source_target_pairs={{0,4},{1,5},{2,6},{3,7},{4,8},{5,9},{6,10},{7,11},{8,12},{9,13},{1... | collective-permute-start | bytes 198152 | tf_op jit(solution)/shard_map/ppermute | solution.py:135
  24.7 8.2 %collective-permute-start.3 = (bf16[16,2064]{1,0:T(8,128)(2,1)S(1)}, bf16[16,2064]{1,0:T(8,128)(2,1)S(1)}, u32[]{:S(2)}, u32[]{:S(2)}) collective-permute-start(bf16[16,2064]{1,0:T(8,128)(2,1)S(1)} %pad_maximum_fusion.7), channel_id=1, source_target_pairs={{0,8},{1,9},{2,10},{3,11},{4,12},{5,13},{6,14},{7,15},{8,0},{9,1},... | collective-permute-start | bytes 198152 | tf_op jit(solution)/shard_map/ppermute | solution.py:135
  25.1 7.9 %collective-permute-start.4 = (bf16[16,2064]{1,0:T(8,128)(2,1)S(1)}, bf16[16,2064]{1,0:T(8,128)(2,1)S(1)}, u32[]{:S(2)}, u32[]{:S(2)}) collective-permute-start(bf16[16,2064]{1,0:T(8,128)(2,1)S(1)} %pad_maximum_fusion.7), channel_id=1, source_target_pairs={{0,12},{1,13},{2,14},{3,15},{4,0},{5,1},{6,2},{7,3},{8,4},{9,5},{1... | collective-permute-start | bytes 198152 | tf_op jit(solution)/shard_map/ppermute | solution.py:135
  33.0 8.5 %collective-permute-start.5 = (bf16[64,2064]{1,0:T(8,128)(2,1)S(1)}, bf16[64,2064]{1,0:T(8,128)(2,1)S(1)}, u32[]{:S(2)}, u32[]{:S(2)}) collective-permute-start(bf16[64,2064]{1,0:T(8,128)(2,1)S(1)} %get-tuple-element.31), channel_id=1, source_target_pairs={{0,1},{1,0},{2,3},{3,2},{4,5},{5,4},{6,7},{7,6},{8,9},{9,8},{10,11... | collective-permute-start | bytes 792584 | tf_op jit(solution)/shard_map/ppermute | solution.py:141
  33.6 9.5 %collective-permute-start.6 = (bf16[64,2064]{1,0:T(8,128)(2,1)S(1)}, bf16[64,2064]{1,0:T(8,128)(2,1)S(1)}, u32[]{:S(2)}, u32[]{:S(2)}) collective-permute-start(bf16[64,2064]{1,0:T(8,128)(2,1)S(1)} %get-tuple-element.31), channel_id=1, source_target_pairs={{0,2},{1,3},{2,0},{3,1},{4,6},{5,7},{6,4},{7,5},{8,10},{9,11},{10,... | collective-permute-start | bytes 792584 | tf_op jit(solution)/shard_map/ppermute | solution.py:141
  34.1 14.5 %collective-permute-start.16 = (bf16[576,2048]{1,0:T(8,128)(2,1)S(1)}, bf16[576,2048]{1,0:T(8,128)(2,1)S(1)}, u32[]{:S(2)}, u32[]{:S(2)}) collective-permute-start(bf16[576,2048]{1,0:T(8,128)(2,1)S(1)} %pad_maximum_fusion.1), channel_id=1, source_target_pairs={{0,16},{16,0},{1,17},{17,1},{2,18},{18,2},{3,19},{19,3},{4,20},{20... | collective-permute-start | bytes 7077896 | tf_op jit(solution)/shard_map/ppermute | solution.py:131
  34.2 10.6 %collective-permute-start.13 = (bf16[32,2048]{1,0:T(8,128)(2,1)S(1)}, bf16[32,2048]{1,0:T(8,128)(2,1)S(1)}, u32[]{:S(2)}, u32[]{:S(2)}) collective-permute-start(bf16[32,2048]{1,0:T(8,128)(2,1)S(1)} %slice.154), channel_id=1, source_target_pairs={{0,2},{1,3},{2,0},{3,1},{4,6},{5,7},{6,4},{7,5},{8,10},{9,11},{10,... | collective-permute-start | bytes 393224 | tf_op jit(solution)/shard_map/ppermute | solution.py:141
  35.8 9.1 %collective-permute-start.14 = (bf16[32,2048]{1,0:T(8,128)(2,1)S(1)}, bf16[32,2048]{1,0:T(8,128)(2,1)S(1)}, u32[]{:S(2)}, u32[]{:S(2)}) collective-permute-start(bf16[32,2048]{1,0:T(8,128)(2,1)S(1)} %slice.155), channel_id=1, source_target_pairs={{0,1},{1,0},{2,3},{3,2},{4,5},{5,4},{6,7},{7,6},{8,9},{9,8},{10,11... | collective-permute-start | bytes 393224 | tf_op jit(solution)/shard_map/ppermute | solution.py:141
  41.5 5.1 %collective-permute-start.7 = (bf16[32,2064]{1,0:T(8,128)(2,1)S(1)}, bf16[32,2064]{1,0:T(8,128)(2,1)S(1)}, u32[]{:S(2)}, u32[]{:S(2)}) collective-permute-start(bf16[32,2064]{1,0:T(8,128)(2,1)S(1)} %slice.152), channel_id=1, source_target_pairs={{0,2},{1,3},{2,0},{3,1},{4,6},{5,7},{6,4},{7,5},{8,10},{9,11},{10,... | collective-permute-start | bytes 396296 | tf_op jit(solution)/shard_map/ppermute | solution.py:141
  43.2 5.1 %collective-permute-start.8 = (bf16[32,2064]{1,0:T(8,128)(2,1)S(1)}, bf16[32,2064]{1,0:T(8,128)(2,1)S(1)}, u32[]{:S(2)}, u32[]{:S(2)}) collective-permute-start(bf16[32,2064]{1,0:T(8,128)(2,1)S(1)} %slice.153), channel_id=1, source_target_pairs={{0,1},{1,0},{2,3},{3,2},{4,5},{5,4},{6,7},{7,6},{8,9},{9,8},{10,11... | collective-permute-start | bytes 396296 | tf_op jit(solution)/shard_map/ppermute | solution.py:141
  54.7 5.0 %collective-permute-start.19 = (bf16[32,2048]{1,0:T(8,128)(2,1)S(1)}, bf16[32,2048]{1,0:T(8,128)(2,1)S(1)}, u32[]{:S(2)}, u32[]{:S(2)}) collective-permute-start(bf16[32,2048]{1,0:T(8,128)(2,1)S(1)} %get-tuple-element.30), channel_id=1, source_target_pairs={{0,1},{1,0},{2,3},{3,2},{4,5},{5,4},{6,7},{7,6},{8,9},{9,8},{10,11... | collective-permute-start | bytes 393224 | tf_op jit(solution)/shard_map/ppermute | solution.py:141
  56.9 23.4 %collective-permute-start.25 = (bf16[256,2048]{1,0:T(8,128)(2,1)S(1)}, bf16[256,2048]{1,0:T(8,128)(2,1)S(1)}, u32[]{:S(2)}, u32[]{:S(2)}) collective-permute-start(bf16[256,2048]{1,0:T(8,128)(2,1)S(1)} %slice.121), channel_id=1, source_target_pairs={{0,16},{16,0},{1,17},{17,1},{2,18},{18,2},{3,19},{19,3},{4,20},{20... | collective-permute-start | bytes 3145736 | tf_op jit(solution)/shard_map/ppermute | solution.py:131
  57.1 6.4 %collective-permute-start.17 = (bf16[32,2048]{1,0:T(8,128)(2,1)S(1)}, bf16[32,2048]{1,0:T(8,128)(2,1)S(1)}, u32[]{:S(2)}, u32[]{:S(2)}) collective-permute-start(bf16[32,2048]{1,0:T(8,128)(2,1)S(1)} %get-tuple-element.29), channel_id=1, source_target_pairs={{0,2},{1,3},{2,0},{3,1},{4,6},{5,7},{6,4},{7,5},{8,10},{9,11},{10,... | collective-permute-start | bytes 393224 | tf_op jit(solution)/shard_map/ppermute | solution.py:141
  57.1 6.9 %collective-permute-start.24 = (bf16[256,576]{1,0:T(8,128)(2,1)S(1)}, bf16[256,576]{1,0:T(8,128)(2,1)S(1)}, u32[]{:S(2)}, u32[]{:S(2)}) collective-permute-start(bf16[256,576]{1,0:T(8,128)(2,1)S(1)} %pad_maximum_fusion.2), channel_id=1, source_target_pairs={{0,16},{16,0},{1,17},{17,1},{2,18},{18,2},{3,19},{19,3},{4,20},{20... | collective-permute-start | bytes 884744 | tf_op jit(solution)/shard_map/ppermute | solution.py:131
  59.8 8.9 %collective-permute-start.20 = (bf16[64,2048]{1,0:T(8,128)(2,1)S(1)}, bf16[64,2048]{1,0:T(8,128)(2,1)S(1)}, u32[]{:S(2)}, u32[]{:S(2)}) collective-permute-start(bf16[64,2048]{1,0:T(8,128)(2,1)S(1)} %pad_maximum_fusion.4), channel_id=1, source_target_pairs={{0,2},{1,3},{2,0},{3,1},{4,6},{5,7},{6,4},{7,5},{8,10},{9,11},{10,... | collective-permute-start | bytes 786440 | tf_op jit(solution)/shard_map/ppermute | solution.py:141
  63.5 7.6 %collective-permute-start.18 = (bf16[64,2048]{1,0:T(8,128)(2,1)S(1)}, bf16[64,2048]{1,0:T(8,128)(2,1)S(1)}, u32[]{:S(2)}, u32[]{:S(2)}) collective-permute-start(bf16[64,2048]{1,0:T(8,128)(2,1)S(1)} %pad_maximum_fusion.3), channel_id=1, source_target_pairs={{0,1},{1,0},{2,3},{3,2},{4,5},{5,4},{6,7},{7,6},{8,9},{9,8},{10,11... | collective-permute-start | bytes 786440 | tf_op jit(solution)/shard_map/ppermute | solution.py:141
  71.8 6.2 %collective-permute-start.23 = (bf16[16,2048]{1,0:T(8,128)(2,1)S(1)}, bf16[16,2048]{1,0:T(8,128)(2,1)S(1)}, u32[]{:S(2)}, u32[]{:S(2)}) collective-permute-start(bf16[16,2048]{1,0:T(8,128)(2,1)S(1)} %get-tuple-element.27), channel_id=1, source_target_pairs={{0,4},{1,5},{2,6},{3,7},{4,8},{5,9},{6,10},{7,11},{8,12},{9,13},{1... | collective-permute-start | bytes 196616 | tf_op jit(solution)/shard_map/ppermute | solution.py:135
  73.5 6.2 %collective-permute-start.22 = (bf16[16,2048]{1,0:T(8,128)(2,1)S(1)}, bf16[16,2048]{1,0:T(8,128)(2,1)S(1)}, u32[]{:S(2)}, u32[]{:S(2)}) collective-permute-start(bf16[16,2048]{1,0:T(8,128)(2,1)S(1)} %get-tuple-element.28), channel_id=1, source_target_pairs={{0,8},{1,9},{2,10},{3,11},{4,12},{5,13},{6,14},{7,15},{8,0},{9,1},... | collective-permute-start | bytes 196616 | tf_op jit(solution)/shard_map/ppermute | solution.py:135
  74.7 5.0 %collective-permute-start.21 = (bf16[16,2048]{1,0:T(8,128)(2,1)S(1)}, bf16[16,2048]{1,0:T(8,128)(2,1)S(1)}, u32[]{:S(2)}, u32[]{:S(2)}) collective-permute-start(bf16[16,2048]{1,0:T(8,128)(2,1)S(1)} %get-tuple-element.26), channel_id=1, source_target_pairs={{0,12},{1,13},{2,14},{3,15},{4,0},{5,1},{6,2},{7,3},{8,4},{9,5},{1... | collective-permute-start | bytes 196616 | tf_op jit(solution)/shard_map/ppermute | solution.py:135
  (6 other events, 14.9 us)

commit v5 on v0

--- a/solution.py
+++ b/solution.py
@@ -1,6 +1,10 @@
+import math
+
 import jax
 import jax.numpy as jnp
 from jax import lax
+from jax.experimental import pallas as pl
+from jax.experimental.pallas import tpu as pltpu
 from jax.sharding import PartitionSpec as P
 
 
@@ -55,7 +59,7 @@
     return (weight_grads, partial_grad)
 
 
-def local(tokens, cotangent, gate_values, expert_ids, packing, w_gate, w_up, w_down):
+def routed_local(tokens, cotangent, gate_values, expert_ids, packing, w_gate, w_up, w_down):
     row_count, top_count = expert_ids.shape
     model_width = tokens.shape[1]
     dp_size = lax.axis_size("dp")
@@ -125,6 +129,287 @@
     return (input_grad, weight_grads[0], weight_grads[1], weight_grads[2])
 
 
+def swap(value):
+    return lax.ppermute(value, "dp", [(0, 1), (1, 0)])
+
+
+def shift_outer(value, count, inner, step):
+    return lax.ppermute(
+        value, "expert", [(place, (place + step * inner) % count) for place in range(count)]
+    )
+
+
+def swap_inner(value, count, partner):
+    return lax.ppermute(value, "expert", [(place, place ^ partner) for place in range(count)])
+
+
+VMEM = pl.BlockSpec(memory_space=pltpu.VMEM)
+SMEM = pl.BlockSpec(memory_space=pltpu.SMEM)
+NT = (((1,), (1,)), ((), ()))
+TN = (((0,), (0,)), ((), ()))
+
+
+def on_chip(body, outs, *args, scalars=0, flops=0):
+    moved = sum(arg.size * arg.dtype.itemsize for arg in args)
+    moved += sum(math.prod(shape) * jnp.dtype(dtype).itemsize for shape, dtype in outs)
+    return pl.pallas_call(
+        body,
+        out_shape=[jax.ShapeDtypeStruct(shape, dtype) for shape, dtype in outs],
+        in_specs=[SMEM] * scalars + [VMEM] * (len(args) - scalars),
+        out_specs=[VMEM] * len(outs),
+        compiler_params=pltpu.CompilerParams(vmem_limit_bytes=2 * moved + (8 << 20)),
+        cost_estimate=pl.CostEstimate(flops=flops, bytes_accessed=moved, transcendentals=0),
+    )(*args)
+
+
+def stack_kernel(*refs):
+    low = 0
+    for ref in refs[:-1]:
+        refs[-1][low : low + ref.shape[0], :] = ref[...]
+        low += ref.shape[0]
+
+
+def stack(blocks):
+    rows = sum(block.shape[0] for block in blocks)
+    return on_chip(stack_kernel, [((rows, blocks[0].shape[1]), blocks[0].dtype)], *blocks)[0]
+
+
+def table_kernel(ids_ref, gates_ref, packing_ref, table_ref):
+    slots = packing_ref.shape[1]
+    count = table_ref.shape[0] - 16
+    labels = lax.broadcasted_iota(jnp.int32, (count, slots), 0)
+    total = jnp.zeros((count, slots), jnp.float32)
+    for k in range(ids_ref.shape[0]):
+        named = labels == ids_ref[k : k + 1, :]
+        total = total + jnp.where(named, gates_ref[k : k + 1, :].astype(jnp.float32), 0.0)
+    table_ref[:count, :] = total.astype(jnp.bfloat16)
+    lists = jnp.broadcast_to(packing_ref[...], (16, slots)).astype(jnp.float32)
+    table_ref[count:, :] = lists.astype(jnp.bfloat16)
+
+
+def payload_kernel(place_ref, table_ref, other_ref, cotangent_ref, payload_ref):
+    rows, width = cotangent_ref.shape
+    count = table_ref.shape[0] - 16
+    slots = table_ref.shape[1]
+    homes = lax.broadcasted_iota(jnp.int32, (rows, slots), 0) + place_ref[0] * rows
+    gates = jnp.zeros((rows, count), jnp.float32)
+    for ref in (table_ref, other_ref):
+        lists = ref[count:, :].astype(jnp.float32)[:1, :]
+        matched = (lists == homes.astype(jnp.float32)).astype(jnp.float32).astype(jnp.bfloat16)
+        gates = gates + lax.dot_general(
+            matched, ref[:count, :], NT, preferred_element_type=jnp.float32
+        )
+    payload_ref[:, :width] = cotangent_ref[...]
+    payload_ref[:, width:] = jnp.zeros((rows, payload_ref.shape[1] - width), jnp.bfloat16)
+    payload_ref[:, width : width + count] = gates.astype(jnp.bfloat16)
+
+
+def pre_kernel(own_ref, other_ref, *refs):
+    pieces, rows_ref, outs = refs[:-5], refs[-5], refs[-4:]
+    stack_kernel(*pieces, rows_ref)
+    half = own_ref.shape[0] // 3
+    rows = rows_ref[...]
+    for index, weights in enumerate((own_ref, other_ref)):
+        for kind in range(2):
+            outs[2 * index + kind][...] = lax.dot_general(
+                rows,
+                weights[kind * half : (kind + 1) * half, :],
+                NT,
+                preferred_element_type=jnp.float32,
+            )
+
+
+def grad_kernel(place_ref, own_ref, other_ref, *refs):
+    pre, pieces = refs[:4], refs[4:-7]
+    rows_ref, own_grads_ref, sent_grads_ref, *blocks = refs[-7:]
+    half = own_ref.shape[0] // 3
+    height, width = rows_ref.shape
+    gate = []
+    low = 0
+    for ref in pieces:
+        rows_ref[low : low + ref.shape[0], :] = ref[:, :width]
+        low += ref.shape[0]
+        gates = ref[:, width:].astype(jnp.float32)
+        lanes = lax.broadcasted_iota(jnp.int32, gates.shape, 1)
+        gate.append(jnp.sum(jnp.where(lanes == place_ref[0], gates, 0.0), axis=1, keepdims=True))
+    gate = jnp.concatenate(gate, axis=0)
+    upstream = rows_ref[...]
+    both = []
+    for index, (weights, grads_ref) in enumerate(
+        ((own_ref, own_grads_ref), (other_ref, sent_grads_ref))
+    ):
+        hidden_grad = gate * lax.dot_general(
+            upstream, weights[2 * half :, :], NT, preferred_element_type=jnp.float32
+        )
+        gate_pre, up_pre = pre[2 * index][...], pre[2 * index + 1][...]
+        sigmoid_val = 1.0 / (1.0 + jnp.exp(-gate_pre))
+        activated = gate_pre * sigmoid_val
+        silu_slope = sigmoid_val * (1.0 + gate_pre * (1.0 - sigmoid_val))
+        gate_grad = (hidden_grad * up_pre * silu_slope).astype(jnp.bfloat16)
+        up_grad = (hidden_grad * activated).astype(jnp.bfloat16)
+        grads_ref[:height, :] = gate_grad
+        grads_ref[height : 2 * height, :] = up_grad
+        grads_ref[2 * height :, :] = (gate * activated * up_pre).astype(jnp.bfloat16)
+        both.append(jnp.concatenate([gate_grad, up_grad], axis=1))
+    depth = height // len(blocks)
+    step = min(width, 512)
+    for left in range(0, width, step):
+        columns = slice(left, left + step)
+        term = jnp.dot(
+            both[0], own_ref[: 2 * half, columns], preferred_element_type=jnp.float32
+        ) + jnp.dot(both[1], other_ref[: 2 * half, columns], preferred_element_type=jnp.float32)
+        for index, block in enumerate(blocks):
+            rows = term[index * depth : (index + 1) * depth]
+            block[:, columns] = rows.astype(jnp.bfloat16)
+
+
+def column_kernel(*refs):
+    blocks, own_ref, sent = refs[:4], refs[4], refs[5:]
+    total = blocks[0][...].astype(jnp.float32)
+    for block in blocks[1:]:
+        total = total + block[...].astype(jnp.float32)
+    depth = own_ref.shape[0]
+    own_ref[...] = total[:depth]
+    for index, ref in enumerate(sent):
+        ref[...] = total[(index + 1) * depth : (index + 2) * depth].astype(jnp.bfloat16)
+
+
+def sum_kernel(own_ref, *refs):
+    total = own_ref[...]
+    for ref in refs[:-1]:
+        total = total + ref[...].astype(jnp.float32)
+    refs[-1][...] = total.astype(jnp.bfloat16)
+
+
+def weight_kernel(own_grads, other_grads, rows, other_rows, upstream, other_upstream, *outs):
+    height = rows.shape[0]
+    for index, out in enumerate(outs):
+        own, other = (upstream, other_upstream) if index == 2 else (rows, other_rows)
+        span = slice(index * height, (index + 1) * height)
+        step = min(out.shape[-1], 1024)
+        for left in range(0, out.shape[-1], step):
+            columns = slice(left, left + step)
+            total = lax.dot_general(
+                own_grads[span, :], own[:, columns], TN, preferred_element_type=jnp.float32
+            ) + lax.dot_general(
+                other_grads[span, :], other[:, columns], TN, preferred_element_type=jnp.float32
+            )
+            out[0, :, columns] = total.astype(jnp.bfloat16)
+
+
+def along_outer(value, count, inner):
+    return [value] + [shift_outer(value, count, inner, step) for step in range(1, count // inner)]
+
+
+def across_inner(column, count):
+    cut = column.shape[0] // 2
+    first = swap_inner(column, count, 1)
+    second = swap_inner(column, count, 2)
+    far_top = swap_inner(first[:cut], count, 2)
+    far_bottom = swap_inner(second[cut:], count, 1)
+    return [column, first, second, far_top, far_bottom]
+
+
+def dense_local(tokens, cotangent, gate_values, expert_ids, packing, w_gate, w_up, w_down):
+    row_count, model_width = tokens.shape
+    half = w_gate.shape[1]
+    count = lax.axis_size("expert")
+    inner = 4
+    outer = count // inner
+    height = row_count * count
+    low, wide = jnp.bfloat16, jnp.float32
+    dp_place = lax.axis_index("dp").reshape(1)
+    place = lax.axis_index("expert").reshape(1)
+
+    token_blocks = along_outer(tokens, count, inner)
+    (table,) = on_chip(
+        table_kernel,
+        [((count + 16, row_count), low)],
+        expert_ids.T,
+        gate_values.T,
+        packing.reshape(1, row_count),
+    )
+    other_table = swap(table)
+    own_weights = jnp.concatenate([w_gate[0], w_up[0], w_down[0]], axis=0)
+    own_weights, other_table = lax.optimization_barrier((own_weights, other_table))
+    other_weights = swap(own_weights)
+    (payload,) = on_chip(
+        payload_kernel,
+        [((row_count, model_width + 128), low)],
+        dp_place,
+        table,
+        other_table,
+        cotangent,
+        scalars=1,
+    )
+    payload, token_blocks[1] = lax.optimization_barrier((payload, token_blocks[1]))
+    token_columns = across_inner(stack(token_blocks), count)
+    upstream_columns = across_inner(stack(along_outer(payload, count, inner)), count)
+
+    inputs, *pre = on_chip(
+        pre_kernel,
+        [((height, model_width), low)] + [((height, half), wide)] * 4,
+        own_weights,
+        other_weights,
+        *token_columns,
+        flops=8 * height * half * model_width,
+    )
+    other_inputs = swap(inputs)
+    upstream, own_grads, sent_grads, *blocks = on_chip(
+        grad_kernel,
+        [((height, model_width), low)]
+        + [((3 * height, half), low)] * 2
+        + [((height // inner, model_width), low)] * inner,
+        place,
+        own_weights,
+        other_weights,
+        *pre,
+        *upstream_columns,
+        scalars=1,
+        flops=12 * height * half * model_width,
+    )
+    *blocks, other_inputs = lax.optimization_barrier((*blocks, other_inputs))
+    returned = [swap_inner(blocks[partner], count, partner) for partner in range(1, inner)]
+    other_grads = swap(sent_grads)
+    other_upstream = swap(upstream)
+    own, *sent = on_chip(
+        column_kernel,
+        [((row_count, model_width), wide)] + [((row_count, model_width), low)] * (outer - 1),
+        blocks[0],
+        *returned,
+    )
+    own, *sent, other_grads, other_upstream = lax.optimization_barrier(
+        (own, *sent, other_grads, other_upstream)
+    )
+    back = [shift_outer(sent[step - 1], count, inner, -step) for step in range(1, outer)]
+    weight_grads = on_chip(
+        weight_kernel,
+        [((1, half, model_width), low)] * 3,
+        own_grads,
+        other_grads,
+        inputs,
+        other_inputs,
+        upstream,
+        other_upstream,
+        flops=12 * height * half * model_width,
+    )
+    (input_grad,) = on_chip(sum_kernel, [((row_count, model_width), low)], own, *back)
+    return (input_grad, *weight_grads)
+
+
+def local(tokens, cotangent, gate_values, expert_ids, packing, w_gate, w_up, w_down):
+    row_count, top = expert_ids.shape
+    count = lax.axis_size("expert")
+    expert_count = count * w_gate.shape[0]
+    capacity = min(row_count, max(2, row_count * top // expert_count + 1))
+    few = capacity * 4 <= row_count
+    regular = lax.axis_size("dp") == 2 and count % 4 == 0 and w_gate.shape[0] == 1
+    chosen = dense_local if regular and not few else routed_local
+    return chosen(
+        tokens, cotangent, gate_values, expert_ids, packing, w_gate, w_up, w_down
+    )
+
+
 def solution(mesh):
     in_specs = (
         P(("groups", "dp", "expert"), None),

time: 172 us -> 83 us (0.48)
  waiting for transfers between devices: 81.2 us -> 30.8 us
  between operations: 15.2 us -> 0.74 us
  local copies, waits for them, and re-layouts: 20.5 us -> 7.01 us
  Pallas kernels: 0 us -> 12.4 us
  matrix products: 11.6 us -> 0 us
  blocking collectives: 11.6 us -> 0 us
  starting transfers between devices: 23.3 us -> 29.8 us
  other arithmetic: 7.45 us -> 1.8 us
    all_to_all x3 -> x0, waiting for transfers between devices: 71 us -> none  [the longest x1 29.4 us: local(): lax.all_to_all(send_upstream, 'expert', split_axis=0, concat_axis=0, tile...]
    ppermute x0 -> x25, waiting for transfers between devices: none -> 30.8 us  [the longest x11 20.4 us: swap_inner(): lax.ppermute(value, 'expert', [(place, place ^ partner) for place in rang...]
    ppermute x0 -> x25, starting transfers between devices: none -> 29.8 us  [the longest x9 15.8 us: shift_outer(): lax.ppermute(value, 'expert', [(place, (place + step * inner) % count) fo...]
    all_to_all x3 -> x0, starting transfers between devices: 23.2 us -> none  [the longest x1 8.34 us: local(): lax.all_to_all(send_rows, 'expert', split_axis=0, concat_axis=0, tiled=True)]
    pallas_call x0 -> x9, Pallas kernels: none -> 12.4 us  [on_chip(): pl.pallas_call(body, out_shape=[jax.ShapeDtypeStruct(shape, dtype) for sh...]
    dot_general x13 -> x0, matrix products: 11.6 us -> none  [the longest x1 2.13 us: expert_terms(): jnp.dot(upstream, down_mat.T, preferred_element_type=jnp.float32)]
    reduce_scatter x1 -> x0, waiting for transfers between devices: 10.2 us -> none  [local(): lax.psum_scatter(partial_grad.reshape(expert_count, dp_size * capacity *...]
    all_gather x5 -> x0, blocking collectives: 9.66 us -> none  [the longest x1 2.11 us: local(): lax.all_gather(tokens, 'dp', axis=0, tiled=True)]
  transfers between devices with their start and end apart: 4 -> 25, of which waited for: 4 -> 12; matrix products, arithmetic and copies ran while one was open for 10% -> 4% of each run, Pallas kernels for 0% -> 14%
where the time goes in v5:
time: 83 us; the launch traced here: 82.6 us
  waiting for transfers between devices  30.8 us (37%)
  starting transfers between devices  29.8 us (36%)
  Pallas kernels  12.4 us (15%)
  local copies, waits for them, and re-layouts  7.01 us (8%)
  other arithmetic  1.8 us (2%)
    ppermute x11, waiting for transfers between devices, swap_inner(): lax.ppermute(value, 'expert', [(place, place ^ partner) for place in rang...  20.4 us
    ppermute x9, starting transfers between devices, shift_outer(): lax.ppermute(value, 'expert', [(place, (place + step * inner) % count) fo...  15.8 us
    ppermute x11, starting transfers between devices, swap_inner(): lax.ppermute(value, 'expert', [(place, place ^ partner) for place in rang...  12.8 us
    pallas_call x9, Pallas kernels, on_chip(): pl.pallas_call(body, out_shape=[jax.ShapeDtypeStruct(shape, dtype) for sh...  12.4 us
    ppermute x9, waiting for transfers between devices, shift_outer(): lax.ppermute(value, 'expert', [(place, (place + step * inner) % count) fo...  10.4 us
    unnamed x22, local copies, waits for them, and re-layouts  5.58 us
    concatenate x1, other arithmetic, dense_local(): own_weights = jnp.concatenate([w_gate[0], w_up[0], w_down[0]], axis=0)  1.8 us
  transfers between devices with their start and end apart: 25, of which 12 were waited for; matrix products, arithmetic and copies ran while one was open for 4% of the time, Pallas kernels for 14%

profile of v5, /device:TPU:0, one launch (start us, length us, event | category | flops | bytes accessed | tf_op | source)
XLA Modules:
  0.0 82.6 jit_solution(4012404321697954068)
XLA Ops:
  3.2 1.8 %pad_maximum_fusion.own_ref = bf16[576,2048]{1,0:T(8,128)(2,1)S(1)} fusion(bf16[192,2048]{1,0:T(8,128)(2,1)} %bitcast.11, bf16[192,2048]{1,0:T(8,128)(2,1)} %bitcast.12, bf16[192,2048]{1,0:T(8,128)(2,1)} %bitcast.13), kind=kLoop, calls=%fused_computation | loop fusion | flops 7077888 | bytes 4718592 | tf_op jit(solution)/shard_map/concatenate | solution.py:333
  5.1 3.0 %collective-permute-start.2 = (bf16[16,2048]{1,0:T(8,128)(2,1)S(1)}, bf16[16,2048]{1,0:T(8,128)(2,1)S(1)}, u32[]{:S(2)}, u32[]{:S(2)}) collective-permute-start(bf16[16,2048]{1,0:T(8,128)(2,1)S(1)} %copy-done.7), channel_id=1, source_target_pairs={{0,4},{1,5},{2,6},{3,7},{4,8},{5,9},{6,10},{7,11},{8,12},{9,13},{1... | collective-permute-start | bytes 196616 | tf_op jit(solution)/shard_map/ppermute | solution.py:137
  8.2 2.6 %collective-permute-start.3 = (bf16[16,2048]{1,0:T(8,128)(2,1)S(1)}, bf16[16,2048]{1,0:T(8,128)(2,1)S(1)}, u32[]{:S(2)}, u32[]{:S(2)}) collective-permute-start(bf16[16,2048]{1,0:T(8,128)(2,1)S(1)} %copy-done.7), channel_id=1, source_target_pairs={{0,8},{1,9},{2,10},{3,11},{4,12},{5,13},{6,14},{7,15},{8,0},{9,1},... | collective-permute-start | bytes 196616 | tf_op jit(solution)/shard_map/ppermute | solution.py:137
  10.8 1.3 %collective-permute-start.4 = (bf16[16,2048]{1,0:T(8,128)(2,1)S(1)}, bf16[16,2048]{1,0:T(8,128)(2,1)S(1)}, u32[]{:S(2)}, u32[]{:S(2)}) collective-permute-start(bf16[16,2048]{1,0:T(8,128)(2,1)S(1)} %copy-done.7), channel_id=1, source_target_pairs={{0,12},{1,13},{2,14},{3,15},{4,0},{5,1},{6,2},{7,3},{8,4},{9,5},{1... | collective-permute-start | bytes 196616 | tf_op jit(solution)/shard_map/ppermute | solution.py:137
  12.7 2.7 %collective-permute-done.3.refs_2_ = bf16[16,2048]{1,0:T(8,128)(2,1)S(1)} collective-permute-done((bf16[16,2048]{1,0:T(8,128)(2,1)S(1)}, bf16[16,2048]{1,0:T(8,128)(2,1)S(1)}, u32[]{:S(2)}, u32[]{:S(2)}) %collective-permute-start.3) | collective-permute-done | bytes 65568 | tf_op jit(solution)/shard_map/ppermute | solution.py:137
  15.7 1.6 %collective-permute-start.6 = (bf16[64,2048]{1,0:T(8,128)(2,1)S(1)}, bf16[64,2048]{1,0:T(8,128)(2,1)S(1)}, u32[]{:S(2)}, u32[]{:S(2)}) collective-permute-start(bf16[64,2048]{1,0:T(8,128)(2,1)S(1)} %shard_map.113.refs_0_), channel_id=1, source_target_pairs={{0,2},{1,3},{2,0},{3,1},{4,6},{5,7},{6,4},{7,5},{8,10},{9,11},{10,... | collective-permute-start | bytes 786440 | tf_op jit(solution)/shard_map/ppermute | solution.py:143
  17.3 1.5 %collective-permute-start.5 = (bf16[64,2048]{1,0:T(8,128)(2,1)S(1)}, bf16[64,2048]{1,0:T(8,128)(2,1)S(1)}, u32[]{:S(2)}, u32[]{:S(2)}) collective-permute-start(bf16[64,2048]{1,0:T(8,128)(2,1)S(1)} %shard_map.113.refs_0_), channel_id=1, source_target_pairs={{0,1},{1,0},{2,3},{3,2},{4,5},{5,4},{6,7},{7,6},{8,9},{9,8},{10,11... | collective-permute-start | bytes 786440 | tf_op jit(solution)/shard_map/ppermute | solution.py:143
  18.8 2.9 %collective-permute-start.11 = (bf16[16,2176]{1,0:T(8,128)(2,1)S(1)}, bf16[16,2176]{1,0:T(8,128)(2,1)S(1)}, u32[]{:S(2)}, u32[]{:S(2)}) collective-permute-start(bf16[16,2176]{1,0:T(8,128)(2,1)S(1)} %shard_map.112.refs_0_), channel_id=1, source_target_pairs={{0,12},{1,13},{2,14},{3,15},{4,0},{5,1},{6,2},{7,3},{8,4},{9,5},{1... | collective-permute-start | bytes 208904 | tf_op jit(solution)/shard_map/ppermute | solution.py:137
  21.9 1.8 %collective-permute-done.11.refs_3_ = bf16[16,2176]{1,0:T(8,128)(2,1)S(1)} collective-permute-done((bf16[16,2176]{1,0:T(8,128)(2,1)S(1)}, bf16[16,2176]{1,0:T(8,128)(2,1)S(1)}, u32[]{:S(2)}, u32[]{:S(2)}) %collective-permute-start.11) | collective-permute-done | bytes 69664 | tf_op jit(solution)/shard_map/ppermute | solution.py:137
  23.6 2.7 %collective-permute-start.9 = (bf16[16,2176]{1,0:T(8,128)(2,1)S(1)}, bf16[16,2176]{1,0:T(8,128)(2,1)S(1)}, u32[]{:S(2)}, u32[]{:S(2)}) collective-permute-start(bf16[16,2176]{1,0:T(8,128)(2,1)S(1)} %shard_map.112.refs_0_), channel_id=1, source_target_pairs={{0,4},{1,5},{2,6},{3,7},{4,8},{5,9},{6,10},{7,11},{8,12},{9,13},{1... | collective-permute-start | bytes 208904 | tf_op jit(solution)/shard_map/ppermute | solution.py:137
  27.4 2.8 %collective-permute-done.9.refs_1_ = bf16[16,2176]{1,0:T(8,128)(2,1)S(1)} collective-permute-done((bf16[16,2176]{1,0:T(8,128)(2,1)S(1)}, bf16[16,2176]{1,0:T(8,128)(2,1)S(1)}, u32[]{:S(2)}, u32[]{:S(2)}) %collective-permute-start.9) | collective-permute-done | bytes 69664 | tf_op jit(solution)/shard_map/ppermute | solution.py:137
  31.4 1.6 %collective-permute-start.8 = (bf16[32,2048]{1,0:T(8,128)(2,1)S(1)}, bf16[32,2048]{1,0:T(8,128)(2,1)S(1)}, u32[]{:S(2)}, u32[]{:S(2)}) collective-permute-start(bf16[32,2048]{1,0:T(8,128)(2,1)S(1)} %slice.17), channel_id=1, source_target_pairs={{0,1},{1,0},{2,3},{3,2},{4,5},{5,4},{6,7},{7,6},{8,9},{9,8},{10,11... | collective-permute-start | bytes 393224 | tf_op jit(solution)/shard_map/ppermute | solution.py:143
  33.0 1.6 %collective-permute-start.7 = (bf16[32,2048]{1,0:T(8,128)(2,1)S(1)}, bf16[32,2048]{1,0:T(8,128)(2,1)S(1)}, u32[]{:S(2)}, u32[]{:S(2)}) collective-permute-start(bf16[32,2048]{1,0:T(8,128)(2,1)S(1)} %slice.16), channel_id=1, source_target_pairs={{0,2},{1,3},{2,0},{3,1},{4,6},{5,7},{6,4},{7,5},{8,10},{9,11},{10,... | collective-permute-start | bytes 393224 | tf_op jit(solution)/shard_map/ppermute | solution.py:143
  34.5 4.2 %collective-permute-done.8.refs_4_ = bf16[32,2048]{1,0:T(8,128)(2,1)S(1)} collective-permute-done((bf16[32,2048]{1,0:T(8,128)(2,1)S(1)}, bf16[32,2048]{1,0:T(8,128)(2,1)S(1)}, u32[]{:S(2)}, u32[]{:S(2)}) %collective-permute-start.8) | collective-permute-done | bytes 131104 | tf_op jit(solution)/shard_map/ppermute | solution.py:143
  38.8 3.4 %shard_map.114 = (bf16[256,2048]{1,0:T(8,128)(2,1)}, f32[256,192]{1,0:T(8,128)S(1)}, f32[256,192]{1,0:T(8,128)S(1)}, f32[256,192]{1,0:T(8,128)S(1)}, f32[256,192]{1,0:T(8,128)S(1)}) custom-call(bf16[576,2048]{1,0:T(8,128)(2,1)S(1)} %pad_maximum_fusion.own_ref, bf16[576,2048]{1,0:T(8,128)(2,1)} %collective-permute-done.1.other_ref, ...), custom_call_target="tpu_custom_call" | custom-call | flops 805306368 | bytes 7602176 | tf_op jit(solution)/shard_map/pallas_call | solution.py:155
  44.8 1.5 %collective-permute-start.14 = (bf16[32,2176]{1,0:T(8,128)(2,1)}, bf16[32,2176]{1,0:T(8,128)(2,1)}, u32[]{:S(2)}, u32[]{:S(2)}) collective-permute-start(bf16[32,2176]{1,0:T(8,128)(2,1)} %slice.18), channel_id=1, source_target_pairs={{0,2},{1,3},{2,0},{3,1},{4,6},{5,7},{6,4},{7,5},{8,10},{9,11},{10,... | collective-permute-start | bytes 417800 | tf_op jit(solution)/shard_map/ppermute | solution.py:143
  46.4 3.6 %collective-permute-done.15.refs_8_ = bf16[32,2176]{1,0:T(8,128)(2,1)} collective-permute-done((bf16[32,2176]{1,0:T(8,128)(2,1)}, bf16[32,2176]{1,0:T(8,128)(2,1)}, u32[]{:S(2)}, u32[]{:S(2)}) %collective-permute-start.15) | collective-permute-done | bytes 139296 | tf_op jit(solution)/shard_map/ppermute | solution.py:143
  53.7 4.0 %shard_map.116 = (bf16[256,2048]{1,0:T(8,128)(2,1)S(1)}, bf16[768,192]{1,0:T(8,128)(2,1)S(1)}, bf16[768,192]{1,0:T(8,128)(2,1)S(1)}, bf16[64,2048]{1,0:T(8,128)(...) custom-call(s32[1]{0:T(128)} %bitcast.place_ref, ...), custom_call_target="tpu_custom_call" | custom-call | flops 1207959552 | bytes 9306116 | tf_op jit(solution)/shard_map/pallas_call | solution.py:155
  58.3 1.5 %collective-permute-start.17 = (bf16[64,2048]{1,0:T(8,128)(2,1)S(1)}, bf16[64,2048]{1,0:T(8,128)(2,1)S(1)}, u32[]{:S(2)}, u32[]{:S(2)}) collective-permute-start(bf16[64,2048]{1,0:T(8,128)(2,1)S(1)} %get-tuple-element.52), channel_id=1, source_target_pairs={{0,1},{1,0},{2,3},{3,2},{4,5},{5,4},{6,7},{7,6},{8,9},{9,8},{10,11... | collective-permute-start | bytes 786440 | tf_op jit(solution)/shard_map/ppermute | solution.py:143
  59.8 1.5 %collective-permute-start.18 = (bf16[64,2048]{1,0:T(8,128)(2,1)S(1)}, bf16[64,2048]{1,0:T(8,128)(2,1)S(1)}, u32[]{:S(2)}, u32[]{:S(2)}) collective-permute-start(bf16[64,2048]{1,0:T(8,128)(2,1)S(1)} %get-tuple-element.53), channel_id=1, source_target_pairs={{0,2},{1,3},{2,0},{3,1},{4,6},{5,7},{6,4},{7,5},{8,10},{9,11},{10,... | collective-permute-start | bytes 786440 | tf_op jit(solution)/shard_map/ppermute | solution.py:143
  61.8 5.7 %collective-permute-done.17.refs_1_ = bf16[64,2048]{1,0:T(8,128)(2,1)S(1)} collective-permute-done((bf16[64,2048]{1,0:T(8,128)(2,1)S(1)}, bf16[64,2048]{1,0:T(8,128)(2,1)S(1)}, u32[]{:S(2)}, u32[]{:S(2)}) %collective-permute-start.17) | collective-permute-done | bytes 262176 | tf_op jit(solution)/shard_map/ppermute | solution.py:143
  67.4 6.0 %collective-permute-done.18.refs_2_ = bf16[64,2048]{1,0:T(8,128)(2,1)S(1)} collective-permute-done((bf16[64,2048]{1,0:T(8,128)(2,1)S(1)}, bf16[64,2048]{1,0:T(8,128)(2,1)S(1)}, u32[]{:S(2)}, u32[]{:S(2)}) %collective-permute-start.18) | collective-permute-done | bytes 262176 | tf_op jit(solution)/shard_map/ppermute | solution.py:143
  73.6 2.1 %collective-permute-start.22 = (bf16[16,2048]{1,0:T(8,128)(2,1)S(1)}, bf16[16,2048]{1,0:T(8,128)(2,1)S(1)}, u32[]{:S(2)}, u32[]{:S(2)}) collective-permute-start(bf16[16,2048]{1,0:T(8,128)(2,1)S(1)} %get-tuple-element.62), channel_id=1, source_target_pairs={{0,12},{1,13},{2,14},{3,15},{4,0},{5,1},{6,2},{7,3},{8,4},{9,5},{1... | collective-permute-start | bytes 196616 | tf_op jit(solution)/shard_map/ppermute | solution.py:137
  76.6 4.1 %shard_map.119 = (bf16[1,192,2048]{2,1,0:T(8,128)(2,1)}, bf16[1,192,2048]{2,1,0:T(8,128)(2,1)}, bf16[1,192,2048]{2,1,0:T(8,128)(2,1)}) custom-call(bf16[768,192]{1,0:T(8,128)(2,1)S(1)} %get-tuple-element.65.own_grads, bf16[768,192]{1,0:T(8,128)(2,1)S(1)} %collective-permute-done.20.other_grads, bf16[256,2048]{1,0:T(8,128)(2,1)} %get-tuple-element.50.rows, ...), custom_call_target="tpu_custom_call" | custom-call | flops 1207959552 | bytes 7143424 | tf_op jit(solution)/shard_map/pallas_call | solution.py:155
  (62 shorter events, 16.5 us)
Async XLA Ops:
  5.0 33.8 %collective-permute-start.1 = (bf16[576,2048]{1,0:T(8,128)(2,1)S(1)}, bf16[576,2048]{1,0:T(8,128)(2,1)}, u32[]{:S(2)}, u32[]{:S(2)}) collective-permute-start(bf16[576,2048]{1,0:T(8,128)(2,1)S(1)} %pad_maximum_fusion.own_ref), channel_id=1, source_target_pairs={{0,16},{16,0},{1,17},{17,1},{2,18},{18,2},{3,19},{19,3},{4,20},{20... | collective-permute-start | bytes 7077896 | tf_op jit(solution)/shard_map/ppermute | solution.py:133
  5.1 7.6 %collective-permute-start.2 = (bf16[16,2048]{1,0:T(8,128)(2,1)S(1)}, bf16[16,2048]{1,0:T(8,128)(2,1)S(1)}, u32[]{:S(2)}, u32[]{:S(2)}) collective-permute-start(bf16[16,2048]{1,0:T(8,128)(2,1)S(1)} %copy-done.7), channel_id=1, source_target_pairs={{0,4},{1,5},{2,6},{3,7},{4,8},{5,9},{6,10},{7,11},{8,12},{9,13},{1... | collective-permute-start | bytes 196616 | tf_op jit(solution)/shard_map/ppermute | solution.py:137
  8.2 7.3 %collective-permute-start.3 = (bf16[16,2048]{1,0:T(8,128)(2,1)S(1)}, bf16[16,2048]{1,0:T(8,128)(2,1)S(1)}, u32[]{:S(2)}, u32[]{:S(2)}) collective-permute-start(bf16[16,2048]{1,0:T(8,128)(2,1)S(1)} %copy-done.7), channel_id=1, source_target_pairs={{0,8},{1,9},{2,10},{3,11},{4,12},{5,13},{6,14},{7,15},{8,0},{9,1},... | collective-permute-start | bytes 196616 | tf_op jit(solution)/shard_map/ppermute | solution.py:137
  10.8 4.9 %collective-permute-start.4 = (bf16[16,2048]{1,0:T(8,128)(2,1)S(1)}, bf16[16,2048]{1,0:T(8,128)(2,1)S(1)}, u32[]{:S(2)}, u32[]{:S(2)}) collective-permute-start(bf16[16,2048]{1,0:T(8,128)(2,1)S(1)} %copy-done.7), channel_id=1, source_target_pairs={{0,12},{1,13},{2,14},{3,15},{4,0},{5,1},{6,2},{7,3},{8,4},{9,5},{1... | collective-permute-start | bytes 196616 | tf_op jit(solution)/shard_map/ppermute | solution.py:137
  15.7 15.6 %collective-permute-start.6 = (bf16[64,2048]{1,0:T(8,128)(2,1)S(1)}, bf16[64,2048]{1,0:T(8,128)(2,1)S(1)}, u32[]{:S(2)}, u32[]{:S(2)}) collective-permute-start(bf16[64,2048]{1,0:T(8,128)(2,1)S(1)} %shard_map.113.refs_0_), channel_id=1, source_target_pairs={{0,2},{1,3},{2,0},{3,1},{4,6},{5,7},{6,4},{7,5},{8,10},{9,11},{10,... | collective-permute-start | bytes 786440 | tf_op jit(solution)/shard_map/ppermute | solution.py:143
  17.3 15.7 %collective-permute-start.5 = (bf16[64,2048]{1,0:T(8,128)(2,1)S(1)}, bf16[64,2048]{1,0:T(8,128)(2,1)S(1)}, u32[]{:S(2)}, u32[]{:S(2)}) collective-permute-start(bf16[64,2048]{1,0:T(8,128)(2,1)S(1)} %shard_map.113.refs_0_), channel_id=1, source_target_pairs={{0,1},{1,0},{2,3},{3,2},{4,5},{5,4},{6,7},{7,6},{8,9},{9,8},{10,11... | collective-permute-start | bytes 786440 | tf_op jit(solution)/shard_map/ppermute | solution.py:143
  18.8 4.9 %collective-permute-start.11 = (bf16[16,2176]{1,0:T(8,128)(2,1)S(1)}, bf16[16,2176]{1,0:T(8,128)(2,1)S(1)}, u32[]{:S(2)}, u32[]{:S(2)}) collective-permute-start(bf16[16,2176]{1,0:T(8,128)(2,1)S(1)} %shard_map.112.refs_0_), channel_id=1, source_target_pairs={{0,12},{1,13},{2,14},{3,15},{4,0},{5,1},{6,2},{7,3},{8,4},{9,5},{1... | collective-permute-start | bytes 208904 | tf_op jit(solution)/shard_map/ppermute | solution.py:137
  21.7 5.8 %collective-permute-start.10 = (bf16[16,2176]{1,0:T(8,128)(2,1)S(1)}, bf16[16,2176]{1,0:T(8,128)(2,1)S(1)}, u32[]{:S(2)}, u32[]{:S(2)}) collective-permute-start(bf16[16,2176]{1,0:T(8,128)(2,1)S(1)} %shard_map.112.refs_0_), channel_id=1, source_target_pairs={{0,8},{1,9},{2,10},{3,11},{4,12},{5,13},{6,14},{7,15},{8,0},{9,1},... | collective-permute-start | bytes 208904 | tf_op jit(solution)/shard_map/ppermute | solution.py:137
  23.6 6.6 %collective-permute-start.9 = (bf16[16,2176]{1,0:T(8,128)(2,1)S(1)}, bf16[16,2176]{1,0:T(8,128)(2,1)S(1)}, u32[]{:S(2)}, u32[]{:S(2)}) collective-permute-start(bf16[16,2176]{1,0:T(8,128)(2,1)S(1)} %shard_map.112.refs_0_), channel_id=1, source_target_pairs={{0,4},{1,5},{2,6},{3,7},{4,8},{5,9},{6,10},{7,11},{8,12},{9,13},{1... | collective-permute-start | bytes 208904 | tf_op jit(solution)/shard_map/ppermute | solution.py:137
  30.3 12.6 %collective-permute-start.13 = (bf16[64,2176]{1,0:T(8,128)(2,1)S(1)}, bf16[64,2176]{1,0:T(8,128)(2,1)S(1)}, u32[]{:S(2)}, u32[]{:S(2)}) collective-permute-start(bf16[64,2176]{1,0:T(8,128)(2,1)S(1)} %shard_map.115.refs_4_), channel_id=1, source_target_pairs={{0,2},{1,3},{2,0},{3,1},{4,6},{5,7},{6,4},{7,5},{8,10},{9,11},{10,... | collective-permute-start | bytes 835592 | tf_op jit(solution)/shard_map/ppermute | solution.py:143
  30.8 13.3 %collective-permute-start.12 = (bf16[64,2176]{1,0:T(8,128)(2,1)S(1)}, bf16[64,2176]{1,0:T(8,128)(2,1)S(1)}, u32[]{:S(2)}, u32[]{:S(2)}) collective-permute-start(bf16[64,2176]{1,0:T(8,128)(2,1)S(1)} %shard_map.115.refs_4_), channel_id=1, source_target_pairs={{0,1},{1,0},{2,3},{3,2},{4,5},{5,4},{6,7},{7,6},{8,9},{9,8},{10,11... | collective-permute-start | bytes 835592 | tf_op jit(solution)/shard_map/ppermute | solution.py:143
  31.4 7.4 %collective-permute-start.8 = (bf16[32,2048]{1,0:T(8,128)(2,1)S(1)}, bf16[32,2048]{1,0:T(8,128)(2,1)S(1)}, u32[]{:S(2)}, u32[]{:S(2)}) collective-permute-start(bf16[32,2048]{1,0:T(8,128)(2,1)S(1)} %slice.17), channel_id=1, source_target_pairs={{0,1},{1,0},{2,3},{3,2},{4,5},{5,4},{6,7},{7,6},{8,9},{9,8},{10,11... | collective-permute-start | bytes 393224 | tf_op jit(solution)/shard_map/ppermute | solution.py:143
  33.0 5.8 %collective-permute-start.7 = (bf16[32,2048]{1,0:T(8,128)(2,1)S(1)}, bf16[32,2048]{1,0:T(8,128)(2,1)S(1)}, u32[]{:S(2)}, u32[]{:S(2)}) collective-permute-start(bf16[32,2048]{1,0:T(8,128)(2,1)S(1)} %slice.16), channel_id=1, source_target_pairs={{0,2},{1,3},{2,0},{3,1},{4,6},{5,7},{6,4},{7,5},{8,10},{9,11},{10,... | collective-permute-start | bytes 393224 | tf_op jit(solution)/shard_map/ppermute | solution.py:143
  42.9 15.4 %collective-permute-start.16 = (bf16[256,2048]{1,0:T(8,128)(2,1)}, bf16[256,2048]{1,0:T(8,128)(2,1)}, u32[]{:S(2)}, u32[]{:S(2)}) collective-permute-start(bf16[256,2048]{1,0:T(8,128)(2,1)} %get-tuple-element.50.rows), channel_id=1, source_target_pairs={{0,16},{16,0},{1,17},{17,1},{2,18},{18,2},{3,19},{19,3},{4,20},{20... | collective-permute-start | bytes 3145736 | tf_op jit(solution)/shard_map/ppermute | solution.py:133
  43.6 6.3 %collective-permute-start.15 = (bf16[32,2176]{1,0:T(8,128)(2,1)}, bf16[32,2176]{1,0:T(8,128)(2,1)}, u32[]{:S(2)}, u32[]{:S(2)}) collective-permute-start(bf16[32,2176]{1,0:T(8,128)(2,1)} %slice.19), channel_id=1, source_target_pairs={{0,1},{1,0},{2,3},{3,2},{4,5},{5,4},{6,7},{7,6},{8,9},{9,8},{10,11... | collective-permute-start | bytes 417800 | tf_op jit(solution)/shard_map/ppermute | solution.py:143
  44.8 6.1 %collective-permute-start.14 = (bf16[32,2176]{1,0:T(8,128)(2,1)}, bf16[32,2176]{1,0:T(8,128)(2,1)}, u32[]{:S(2)}, u32[]{:S(2)}) collective-permute-start(bf16[32,2176]{1,0:T(8,128)(2,1)} %slice.18), channel_id=1, source_target_pairs={{0,2},{1,3},{2,0},{3,1},{4,6},{5,7},{6,4},{7,5},{8,10},{9,11},{10,... | collective-permute-start | bytes 417800 | tf_op jit(solution)/shard_map/ppermute | solution.py:143
  57.7 15.9 %collective-permute-start.21 = (bf16[256,2048]{1,0:T(8,128)(2,1)S(1)}, bf16[256,2048]{1,0:T(8,128)(2,1)S(1)}, u32[]{:S(2)}, u32[]{:S(2)}) collective-permute-start(bf16[256,2048]{1,0:T(8,128)(2,1)S(1)} %get-tuple-element.60.upstream), channel_id=1, source_target_pairs={{0,16},{16,0},{1,17},{17,1},{2,18},{18,2},{3,19},{19,3},{4,20},{20... | collective-permute-start | bytes 3145736 | tf_op jit(solution)/shard_map/ppermute | solution.py:133
  57.8 15.8 %collective-permute-start.20 = (bf16[768,192]{1,0:T(8,128)(2,1)S(1)}, bf16[768,192]{1,0:T(8,128)(2,1)S(1)}, u32[]{:S(2)}, u32[]{:S(2)}) collective-permute-start(bf16[768,192]{1,0:T(8,128)(2,1)S(1)} %get-tuple-element.59), channel_id=1, source_target_pairs={{0,16},{16,0},{1,17},{17,1},{2,18},{18,2},{3,19},{19,3},{4,20},{20... | collective-permute-start | bytes 884744 | tf_op jit(solution)/shard_map/ppermute | solution.py:133
  58.3 9.2 %collective-permute-start.17 = (bf16[64,2048]{1,0:T(8,128)(2,1)S(1)}, bf16[64,2048]{1,0:T(8,128)(2,1)S(1)}, u32[]{:S(2)}, u32[]{:S(2)}) collective-permute-start(bf16[64,2048]{1,0:T(8,128)(2,1)S(1)} %get-tuple-element.52), channel_id=1, source_target_pairs={{0,1},{1,0},{2,3},{3,2},{4,5},{5,4},{6,7},{7,6},{8,9},{9,8},{10,11... | collective-permute-start | bytes 786440 | tf_op jit(solution)/shard_map/ppermute | solution.py:143
  59.8 13.6 %collective-permute-start.18 = (bf16[64,2048]{1,0:T(8,128)(2,1)S(1)}, bf16[64,2048]{1,0:T(8,128)(2,1)S(1)}, u32[]{:S(2)}, u32[]{:S(2)}) collective-permute-start(bf16[64,2048]{1,0:T(8,128)(2,1)S(1)} %get-tuple-element.53), channel_id=1, source_target_pairs={{0,2},{1,3},{2,0},{3,1},{4,6},{5,7},{6,4},{7,5},{8,10},{9,11},{10,... | collective-permute-start | bytes 786440 | tf_op jit(solution)/shard_map/ppermute | solution.py:143
  61.3 12.1 %collective-permute-start.19 = (bf16[64,2048]{1,0:T(8,128)(2,1)S(1)}, bf16[64,2048]{1,0:T(8,128)(2,1)S(1)}, u32[]{:S(2)}, u32[]{:S(2)}) collective-permute-start(bf16[64,2048]{1,0:T(8,128)(2,1)S(1)} %get-tuple-element.54), channel_id=1, source_target_pairs={{0,3},{1,2},{2,1},{3,0},{4,7},{5,6},{6,5},{7,4},{8,11},{9,10},{10,... | collective-permute-start | bytes 786440 | tf_op jit(solution)/shard_map/ppermute | solution.py:143
  73.6 7.1 %collective-permute-start.22 = (bf16[16,2048]{1,0:T(8,128)(2,1)S(1)}, bf16[16,2048]{1,0:T(8,128)(2,1)S(1)}, u32[]{:S(2)}, u32[]{:S(2)}) collective-permute-start(bf16[16,2048]{1,0:T(8,128)(2,1)S(1)} %get-tuple-element.62), channel_id=1, source_target_pairs={{0,12},{1,13},{2,14},{3,15},{4,0},{5,1},{6,2},{7,3},{8,4},{9,5},{1... | collective-permute-start | bytes 196616 | tf_op jit(solution)/shard_map/ppermute | solution.py:137
  75.6 6.3 %collective-permute-start.23 = (bf16[16,2048]{1,0:T(8,128)(2,1)S(1)}, bf16[16,2048]{1,0:T(8,128)(2,1)S(1)}, u32[]{:S(2)}, u32[]{:S(2)}) collective-permute-start(bf16[16,2048]{1,0:T(8,128)(2,1)S(1)} %get-tuple-element.63), channel_id=1, source_target_pairs={{0,8},{1,9},{2,10},{3,11},{4,12},{5,13},{6,14},{7,15},{8,0},{9,1},... | collective-permute-start | bytes 196616 | tf_op jit(solution)/shard_map/ppermute | solution.py:137
  75.6 6.3 %collective-permute-start.24 = (bf16[16,2048]{1,0:T(8,128)(2,1)S(1)}, bf16[16,2048]{1,0:T(8,128)(2,1)S(1)}, u32[]{:S(2)}, u32[]{:S(2)}) collective-permute-start(bf16[16,2048]{1,0:T(8,128)(2,1)S(1)} %get-tuple-element.64), channel_id=1, source_target_pairs={{0,4},{1,5},{2,6},{3,7},{4,8},{5,9},{6,10},{7,11},{8,12},{9,13},{1... | collective-permute-start | bytes 196616 | tf_op jit(solution)/shard_map/ppermute | solution.py:137
  (12 other events, 22.0 us)

commit v6 on v0

--- a/solution.py
+++ b/solution.py
@@ -1,6 +1,10 @@
+import math
+
 import jax
 import jax.numpy as jnp
 from jax import lax
+from jax.experimental import pallas as pl
+from jax.experimental.pallas import tpu as pltpu
 from jax.sharding import PartitionSpec as P
 
 
@@ -55,7 +59,7 @@
     return (weight_grads, partial_grad)
 
 
-def local(tokens, cotangent, gate_values, expert_ids, packing, w_gate, w_up, w_down):
+def routed_local(tokens, cotangent, gate_values, expert_ids, packing, w_gate, w_up, w_down):
     row_count, top_count = expert_ids.shape
     model_width = tokens.shape[1]
     dp_size = lax.axis_size("dp")
@@ -125,6 +129,296 @@
     return (input_grad, weight_grads[0], weight_grads[1], weight_grads[2])
 
 
+def swap(value):
+    return lax.ppermute(value, "dp", [(0, 1), (1, 0)])
+
+
+def shift_outer(value, count, inner, step):
+    return lax.ppermute(
+        value, "expert", [(place, (place + step * inner) % count) for place in range(count)]
+    )
+
+
+def swap_inner(value, count, partner):
+    return lax.ppermute(value, "expert", [(place, place ^ partner) for place in range(count)])
+
+
+VMEM = pl.BlockSpec(memory_space=pltpu.VMEM)
+SMEM = pl.BlockSpec(memory_space=pltpu.SMEM)
+NT = (((1,), (1,)), ((), ()))
+LANES = 128
+
+
+def on_chip(body, outs, *args, scalars=0):
+    moved = sum(arg.size * arg.dtype.itemsize for arg in args)
+    moved += sum(math.prod(shape) * jnp.dtype(dtype).itemsize for shape, dtype in outs)
+    return pl.pallas_call(
+        body,
+        out_shape=[jax.ShapeDtypeStruct(shape, dtype) for shape, dtype in outs],
+        in_specs=[SMEM] * scalars + [VMEM] * (len(args) - scalars),
+        out_specs=[VMEM] * len(outs),
+        compiler_params=pltpu.CompilerParams(vmem_limit_bytes=moved + (4 << 20)),
+        cost_estimate=pl.CostEstimate(flops=0, bytes_accessed=moved, transcendentals=0),
+    )(*args)
+
+
+def stack_kernel(*refs):
+    low = 0
+    for ref in refs[:-1]:
+        refs[-1][low : low + ref.shape[0], :] = ref[...]
+        low += ref.shape[0]
+
+
+def stack(blocks):
+    rows = sum(block.shape[0] for block in blocks)
+    return on_chip(stack_kernel, [((rows, blocks[0].shape[1]), blocks[0].dtype)], *blocks)[0]
+
+
+def table_kernel(ids_ref, gates_ref, packing_ref, table_ref):
+    slots = packing_ref.shape[1]
+    count = table_ref.shape[0] - 16
+    labels = lax.broadcasted_iota(jnp.int32, (count, slots), 0)
+    total = jnp.zeros((count, slots), jnp.float32)
+    for k in range(ids_ref.shape[0]):
+        named = labels == ids_ref[k : k + 1, :]
+        total = total + jnp.where(named, gates_ref[k : k + 1, :].astype(jnp.float32), 0.0)
+    table_ref[:count, :] = total.astype(jnp.bfloat16)
+    lists = jnp.broadcast_to(packing_ref[...], (16, slots)).astype(jnp.float32)
+    table_ref[count:, :] = lists.astype(jnp.bfloat16)
+
+
+def first_kernel(tokens_ref, cotangent_ref, out_ref):
+    width = tokens_ref.shape[1]
+    out_ref[:, :width] = tokens_ref[...]
+    out_ref[:, width:] = cotangent_ref[:, : out_ref.shape[1] - width]
+
+
+def second_kernel(place_ref, table_ref, other_ref, cotangent_ref, out_ref):
+    rows, slots = cotangent_ref.shape[0], table_ref.shape[1]
+    count = table_ref.shape[0] - 16
+    width = out_ref.shape[1] - LANES
+    homes = lax.broadcasted_iota(jnp.int32, (rows, slots), 0) + place_ref[0] * rows
+    gates = jnp.zeros((rows, count), jnp.float32)
+    for ref in (table_ref, other_ref):
+        lists = ref[count:, :].astype(jnp.float32)[:1, :]
+        matched = (lists == homes.astype(jnp.float32)).astype(jnp.float32).astype(jnp.bfloat16)
+        gates = gates + lax.dot_general(
+            matched, ref[:count, :], NT, preferred_element_type=jnp.float32
+        )
+    out_ref[:, :width] = cotangent_ref[:, cotangent_ref.shape[1] - width :]
+    out_ref[:, width:] = jnp.zeros((rows, LANES), jnp.bfloat16)
+    out_ref[:, width : width + count] = gates.astype(jnp.bfloat16)
+
+
+def gather_kernel(place_ref, *refs):
+    first, second, rows_ref, gate_ref = refs[:5], refs[5:-2], refs[-2], refs[-1]
+    low = 0
+    left = first[0].shape[1]
+    for ref in first:
+        rows_ref[low : low + ref.shape[0], :left] = ref[...]
+        low += ref.shape[0]
+    width = second[0].shape[1] - LANES
+    column = first[0].shape[0]
+    depth = column // len(second)
+    for step, ref in enumerate(second):
+        gates = ref[:, width:].astype(jnp.float32)
+        lanes = lax.broadcasted_iota(jnp.int32, gates.shape, 1)
+        gate = jnp.sum(jnp.where(lanes == place_ref[0], gates, 0.0), axis=1, keepdims=True)
+        for partner in range(ref.shape[0] // depth):
+            block = slice(partner * depth, (partner + 1) * depth)
+            low = partner * column + step * depth
+            rows_ref[low : low + depth, left:] = ref[block, :width]
+            gate_ref[low : low + depth, :] = gate[block]
+
+
+def split_kernel(first_ref, second_ref, *outs):
+    first, second = outs[:3], outs[3:]
+    column = first[0].shape[0]
+    depth = column // len(second)
+    for partner, out in enumerate(first):
+        out[...] = first_ref[(partner + 1) * column : (partner + 2) * column, :]
+    for step, out in enumerate(second):
+        for partner in range(out.shape[0] // depth):
+            low = partner * column + step * depth
+            out[partner * depth : (partner + 1) * depth, :] = second_ref[low : low + depth, :]
+
+
+def column_kernel(*refs):
+    own_ref, sent = refs[4], refs[5:]
+    depth = own_ref.shape[0]
+    total = refs[0][: depth * (len(sent) + 1), :].astype(jnp.float32)
+    for block in refs[1:4]:
+        total = total + block[...].astype(jnp.float32)
+    own_ref[...] = total[:depth]
+    for index, ref in enumerate(sent):
+        ref[...] = total[(index + 1) * depth : (index + 2) * depth].astype(jnp.bfloat16)
+
+
+def sum_kernel(*refs):
+    inputs, out_ref = refs[:-1], refs[-1]
+    half = len(inputs) // 2
+    low = 0
+    for part in (inputs[:half], inputs[half:]):
+        total = part[0][...]
+        for ref in part[1:]:
+            total = total + ref[...].astype(jnp.float32)
+        out_ref[:, low : low + total.shape[1]] = total.astype(jnp.bfloat16)
+        low += total.shape[1]
+
+
+def along_outer(value, count, inner):
+    return [value] + [shift_outer(value, count, inner, step) for step in range(1, count // inner)]
+
+
+def across_inner(column, count):
+    cut = column.shape[0] // 2
+    first = swap_inner(column, count, 1)
+    second = swap_inner(column, count, 2)
+    far_top = swap_inner(first[:cut], count, 2)
+    far_bottom = swap_inner(second[cut:], count, 1)
+    return [column, first, second, far_top, far_bottom]
+
+
+def dense_local(tokens, cotangent, gate_values, expert_ids, packing, w_gate, w_up, w_down):
+    row_count, model_width = tokens.shape
+    half = w_gate.shape[1]
+    count = lax.axis_size("expert")
+    inner = outer = 4
+    height = row_count * count
+    column = row_count * outer
+    low, wide = jnp.bfloat16, jnp.float32
+    dp_place = lax.axis_index("dp").reshape(1)
+    place = lax.axis_index("expert").reshape(1)
+    sent_late = model_width // 2
+    back_late = model_width // 4
+    early = 2 * model_width - sent_late
+    back_early = model_width - back_late
+
+    (first,) = on_chip(first_kernel, [((row_count, early), low)], tokens, cotangent)
+    first_blocks = along_outer(first, count, inner)
+    (table,) = on_chip(
+        table_kernel,
+        [((count + 16, row_count), low)],
+        expert_ids.T,
+        gate_values.T,
+        packing.reshape(1, row_count),
+    )
+    other_table = swap(table)
+    (second,) = on_chip(
+        second_kernel,
+        [((row_count, sent_late + LANES), low)],
+        dp_place,
+        table,
+        other_table,
+        cotangent,
+        scalars=1,
+    )
+    second_plane = stack(
+        [second] + [swap_inner(second, count, partner) for partner in range(1, inner)]
+    )
+    own_weights = jnp.concatenate([w_gate[0], w_up[0], w_down[0]], axis=0)
+    first_column = stack(first_blocks)
+    own_weights, first_column = lax.optimization_barrier((own_weights, first_column))
+    other = swap(own_weights)
+    first_pieces = across_inner(first_column, count)
+    second_pieces = along_outer(second_plane, count, inner)
+    rows, gate = on_chip(
+        gather_kernel,
+        [((height, 2 * model_width), low), ((height, 1), wide)],
+        place,
+        *first_pieces,
+        *second_pieces,
+        scalars=1,
+    )
+    other_rows = swap(rows)
+    inputs, upstream = rows[:, :model_width], rows[:, model_width:]
+
+    gate_up = jnp.concatenate([w_gate[0], other[:half], w_up[0], other[half : 2 * half]], axis=0)
+    down = jnp.concatenate([w_down[0], other[2 * half :]], axis=0)
+    pre = jnp.dot(inputs, gate_up.T, preferred_element_type=wide)
+    gate_pre, up_pre = pre[:, : 2 * half], pre[:, 2 * half :]
+    hidden_grad = gate * jnp.dot(upstream, down.T, preferred_element_type=wide)
+    sigmoid_val = jax.nn.sigmoid(gate_pre)
+    activated = gate_pre * sigmoid_val
+    hidden = (gate * activated * up_pre).astype(low)
+    silu_slope = sigmoid_val * (1.0 + gate_pre * (1.0 - sigmoid_val))
+    gate_grad = (hidden_grad * up_pre * silu_slope).astype(low)
+    up_grad = (hidden_grad * activated).astype(low)
+    both_grad = jnp.concatenate([gate_grad, up_grad], axis=1)
+    terms = [
+        jnp.dot(both_grad, gate_up[:, columns], preferred_element_type=wide).astype(low)
+        for columns in (slice(0, back_early), slice(back_early, None))
+    ]
+    blocks = on_chip(
+        split_kernel,
+        [((column, back_early), low)] * (inner - 1) + [((column, back_late), low)] * outer,
+        *terms,
+    )
+    early_back = [
+        swap_inner(block, count, partner + 1) for partner, block in enumerate(blocks[: inner - 1])
+    ]
+    late_blocks = blocks[inner - 1 :]
+    late_back = [
+        shift_outer(late_blocks[step], count, inner, -step) for step in range(1, outer)
+    ]
+    grads = (gate_grad, up_grad, hidden)
+    own_grads = jnp.concatenate([grad[:, :half] for grad in grads], axis=1)
+    sent_grads = jnp.concatenate([grad[:, half:] for grad in grads], axis=1)
+    sent_grads, *blocks = lax.optimization_barrier((sent_grads, *blocks))
+    other_grads = swap(sent_grads)
+    early_own, *early_sent = on_chip(
+        column_kernel,
+        [((row_count, back_early), wide)] + [((row_count, back_early), low)] * (outer - 1),
+        terms[0],
+        *early_back,
+    )
+    late_own, *late_sent = on_chip(
+        column_kernel,
+        [((row_count, back_late), wide)] + [((row_count, back_late), low)] * (inner - 1),
+        late_blocks[0],
+        *late_back,
+    )
+    early_sent[0], other_grads, other_rows = lax.optimization_barrier(
+        (early_sent[0], other_grads, other_rows)
+    )
+    early_parts = [
+        shift_outer(block, count, inner, -step - 1) for step, block in enumerate(early_sent)
+    ]
+    late_parts = [
+        swap_inner(block, count, partner + 1) for partner, block in enumerate(late_sent)
+    ]
+    weight_grads = []
+    for index, span in enumerate((slice(0, model_width),) * 2 + (slice(model_width, None),)):
+        part = slice(index * half, (index + 1) * half)
+        total = jnp.dot(own_grads[:, part].T, rows[:, span], preferred_element_type=wide)
+        total = total + jnp.dot(
+            other_grads[:, part].T, other_rows[:, span], preferred_element_type=wide
+        )
+        weight_grads.append(total.astype(low)[None])
+    (input_grad,) = on_chip(
+        sum_kernel,
+        [((row_count, model_width), low)],
+        early_own,
+        *early_parts,
+        late_own,
+        *late_parts,
+    )
+    return (input_grad, *weight_grads)
+
+
+def local(tokens, cotangent, gate_values, expert_ids, packing, w_gate, w_up, w_down):
+    row_count, top = expert_ids.shape
+    count = lax.axis_size("expert")
+    expert_count = count * w_gate.shape[0]
+    capacity = min(row_count, max(2, row_count * top // expert_count + 1))
+    few = capacity * 4 <= row_count
+    regular = lax.axis_size("dp") == 2 and count == 16 and w_gate.shape[0] == 1
+    chosen = dense_local if regular and not few else routed_local
+    return chosen(
+        tokens, cotangent, gate_values, expert_ids, packing, w_gate, w_up, w_down
+    )
+
+
 def solution(mesh):
     in_specs = (
         P(("groups", "dp", "expert"), None),

time: 172 us -> 99.5 us (0.58)
  waiting for transfers between devices: 81.2 us -> 31.8 us
  between operations: 15.2 us -> 0.9 us
  starting transfers between devices: 23.3 us -> 37.2 us
  blocking collectives: 11.6 us -> 0 us
  local copies, waits for them, and re-layouts: 20.5 us -> 12.1 us
  other arithmetic: 7.45 us -> 4.03 us
    all_to_all x3 -> x0, waiting for transfers between devices: 71 us -> none  [the longest x1 29.4 us: local(): lax.all_to_all(send_upstream, 'expert', split_axis=0, concat_axis=0, tile...]
    ppermute x0 -> x29, starting transfers between devices: none -> 37.2 us  [the longest x12 22.8 us: shift_outer(): lax.ppermute(value, 'expert', [(place, (place + step * inner) % count) fo...]
    ppermute x0 -> x29, waiting for transfers between devices: none -> 31.8 us  [the longest x13 15.7 us: swap_inner(): lax.ppermute(value, 'expert', [(place, place ^ partner) for place in rang...]
    all_to_all x3 -> x0, starting transfers between devices: 23.2 us -> none  [the longest x1 8.34 us: local(): lax.all_to_all(send_rows, 'expert', split_axis=0, concat_axis=0, tiled=True)]
    reduce_scatter x1 -> x0, waiting for transfers between devices: 10.2 us -> none  [local(): lax.psum_scatter(partial_grad.reshape(expert_count, dp_size * capacity *...]
    all_gather x5 -> x0, blocking collectives: 9.66 us -> none  [the longest x1 2.11 us: local(): lax.all_gather(tokens, 'dp', axis=0, tiled=True)]
    convert_element_type x8 -> x0, local copies, waits for them, and re-layouts: 7.16 us -> none  [the longest x1 2.73 us: local(): partial_grad.reshape(expert_count, dp_size * capacity * model_width)]
    unnamed x51 -> x38, local copies, waits for them, and re-layouts: 3.3 us -> 9.88 us
  transfers between devices with their start and end apart: 4 -> 29, of which waited for: 4 -> 11; matrix products, arithmetic and copies ran while one was open for 10% -> 18% of each run, Pallas kernels for 0% -> 1%
where the time goes in v6:
time: 99.5 us; the launch traced here: 99 us
  starting transfers between devices  37.2 us (37%)
  waiting for transfers between devices  31.8 us (32%)
  local copies, waits for them, and re-layouts  12.1 us (12%)
  matrix products  11.9 us (12%)
  other arithmetic  4.03 us (4%)
  Pallas kernels  1.2 us (1%)
    ppermute x12, starting transfers between devices, shift_outer(): lax.ppermute(value, 'expert', [(place, (place + step * inner) % count) fo...  22.8 us
    ppermute x13, waiting for transfers between devices, swap_inner(): lax.ppermute(value, 'expert', [(place, place ^ partner) for place in rang...  15.7 us
    ppermute x12, waiting for transfers between devices, shift_outer(): lax.ppermute(value, 'expert', [(place, (place + step * inner) % count) fo...  14.7 us
    ppermute x13, starting transfers between devices, swap_inner(): lax.ppermute(value, 'expert', [(place, place ^ partner) for place in rang...  13.6 us
    unnamed x38, local copies, waits for them, and re-layouts  9.88 us
    dot_general x3, matrix products, dense_local(): jnp.dot(other_grads[:, part].T, other_rows[:, span], preferred_element_ty...  4.96 us
    dot_general x3, matrix products, dense_local(): jnp.dot(own_grads[:, part].T, rows[:, span], preferred_element_type=wide)  3.86 us
    concatenate x1, other arithmetic, dense_local(): own_weights = jnp.concatenate([w_gate[0], w_up[0], w_down[0]], axis=0)  3.36 us
  transfers between devices with their start and end apart: 29, of which 11 were waited for; matrix products, arithmetic and copies ran while one was open for 18% of the time, Pallas kernels for 1%

profile of v6, /device:TPU:0, one launch (start us, length us, event | category | flops | bytes accessed | tf_op | source)
XLA Modules:
  0.0 99.0 jit_solution(17684226504921912271)
XLA Ops:
  2.3 3.1 %collective-permute-start = (bf16[16,3072]{1,0:T(8,128)(2,1)S(1)}, bf16[16,3072]{1,0:T(8,128)(2,1)S(1)}, u32[]{:S(2)}, u32[]{:S(2)}) collective-permute-start(bf16[16,3072]{1,0:T(8,128)(2,1)S(1)} %shard_map.111.refs_0_), channel_id=1, source_target_pairs={{0,4},{1,5},{2,6},{3,7},{4,8},{5,9},{6,10},{7,11},{8,12},{9,13},{1... | collective-permute-start | bytes 294920 | tf_op jit(solution)/shard_map/ppermute | solution.py:137
  5.4 2.6 %collective-permute-start.1 = (bf16[16,3072]{1,0:T(8,128)(2,1)S(1)}, bf16[16,3072]{1,0:T(8,128)(2,1)S(1)}, u32[]{:S(2)}, u32[]{:S(2)}) collective-permute-start(bf16[16,3072]{1,0:T(8,128)(2,1)S(1)} %shard_map.111.refs_0_), channel_id=1, source_target_pairs={{0,8},{1,9},{2,10},{3,11},{4,12},{5,13},{6,14},{7,15},{8,0},{9,1},... | collective-permute-start | bytes 294920 | tf_op jit(solution)/shard_map/ppermute | solution.py:137
  9.3 3.4 %pad_maximum_fusion.1 = bf16[576,2048]{1,0:T(8,128)(2,1)} fusion(bf16[192,2048]{1,0:T(8,128)(2,1)} %bitcast.24, bf16[192,2048]{1,0:T(8,128)(2,1)} %bitcast.18, bf16[192,2048]{1,0:T(8,128)(2,1)} %bitcast.21), kind=kLoop, calls=%fused_computation.12 | loop fusion | flops 7077888 | bytes 4718592 | tf_op jit(solution)/shard_map/concatenate | solution.py:319
  12.7 1.9 %collective-permute-done.1.refs_2_ = bf16[16,3072]{1,0:T(8,128)(2,1)S(1)} collective-permute-done((bf16[16,3072]{1,0:T(8,128)(2,1)S(1)}, bf16[16,3072]{1,0:T(8,128)(2,1)S(1)}, u32[]{:S(2)}, u32[]{:S(2)}) %collective-permute-start.1) | collective-permute-done | bytes 98336 | tf_op jit(solution)/shard_map/ppermute | solution.py:137
  14.7 1.6 %collective-permute-start.3 = (bf16[64,3072]{1,0:T(8,128)(2,1)S(1)}, bf16[64,3072]{1,0:T(8,128)(2,1)S(1)}, u32[]{:S(2)}, u32[]{:S(2)}) collective-permute-start(bf16[64,3072]{1,0:T(8,128)(2,1)S(1)} %shard_map.112.refs_0_), channel_id=1, source_target_pairs={{0,1},{1,0},{2,3},{3,2},{4,5},{5,4},{6,7},{7,6},{8,9},{9,8},{10,11... | collective-permute-start | bytes 1179656 | tf_op jit(solution)/shard_map/ppermute | solution.py:143
  16.3 1.5 %collective-permute-start.4 = (bf16[64,3072]{1,0:T(8,128)(2,1)S(1)}, bf16[64,3072]{1,0:T(8,128)(2,1)S(1)}, u32[]{:S(2)}, u32[]{:S(2)}) collective-permute-start(bf16[64,3072]{1,0:T(8,128)(2,1)S(1)} %shard_map.112.refs_0_), channel_id=1, source_target_pairs={{0,2},{1,3},{2,0},{3,1},{4,6},{5,7},{6,4},{7,5},{8,10},{9,11},{10,... | collective-permute-start | bytes 1179656 | tf_op jit(solution)/shard_map/ppermute | solution.py:143
  19.4 2.4 %collective-permute-start.10 = (bf16[16,1152]{1,0:T(8,128)(2,1)S(1)}, bf16[16,1152]{1,0:T(8,128)(2,1)S(1)}, u32[]{:S(2)}, u32[]{:S(2)}) collective-permute-start(bf16[16,1152]{1,0:T(8,128)(2,1)S(1)} %shard_map.114.refs_0_), channel_id=1, source_target_pairs={{0,3},{1,2},{2,1},{3,0},{4,7},{5,6},{6,5},{7,4},{8,11},{9,10},{10,... | collective-permute-start | bytes 110600 | tf_op jit(solution)/shard_map/ppermute | solution.py:143
  22.4 6.0 %collective-permute-done.10.refs_3_ = bf16[16,1152]{1,0:T(8,128)(2,1)S(1)} collective-permute-done((bf16[16,1152]{1,0:T(8,128)(2,1)S(1)}, bf16[16,1152]{1,0:T(8,128)(2,1)S(1)}, u32[]{:S(2)}, u32[]{:S(2)}) %collective-permute-start.10) | collective-permute-done | bytes 36896 | tf_op jit(solution)/shard_map/ppermute | solution.py:143
  29.0 3.3 %collective-permute-done.9.refs_2_ = bf16[16,1152]{1,0:T(8,128)(2,1)S(1)} collective-permute-done((bf16[16,1152]{1,0:T(8,128)(2,1)S(1)}, bf16[16,1152]{1,0:T(8,128)(2,1)S(1)}, u32[]{:S(2)}, u32[]{:S(2)}) %collective-permute-start.9) | collective-permute-done | bytes 36896 | tf_op jit(solution)/shard_map/ppermute | solution.py:143
  32.4 2.6 %collective-permute-start.11 = (bf16[64,1152]{1,0:T(8,128)(2,1)S(1)}, bf16[64,1152]{1,0:T(8,128)(2,1)S(1)}, u32[]{:S(2)}, u32[]{:S(2)}) collective-permute-start(bf16[64,1152]{1,0:T(8,128)(2,1)S(1)} %shard_map.115.refs_5_), channel_id=1, source_target_pairs={{0,4},{1,5},{2,6},{3,7},{4,8},{5,9},{6,10},{7,11},{8,12},{9,13},{1... | collective-permute-start | bytes 442376 | tf_op jit(solution)/shard_map/ppermute | solution.py:137
  37.1 1.6 %collective-permute-start.12 = (bf16[64,1152]{1,0:T(8,128)(2,1)S(1)}, bf16[64,1152]{1,0:T(8,128)(2,1)S(1)}, u32[]{:S(2)}, u32[]{:S(2)}) collective-permute-start(bf16[64,1152]{1,0:T(8,128)(2,1)S(1)} %shard_map.115.refs_5_), channel_id=1, source_target_pairs={{0,8},{1,9},{2,10},{3,11},{4,12},{5,13},{6,14},{7,15},{8,0},{9,1},... | collective-permute-start | bytes 442376 | tf_op jit(solution)/shard_map/ppermute | solution.py:137
  38.7 2.2 %collective-permute-done.11.refs_6_ = bf16[64,1152]{1,0:T(8,128)(2,1)S(1)} collective-permute-done((bf16[64,1152]{1,0:T(8,128)(2,1)S(1)}, bf16[64,1152]{1,0:T(8,128)(2,1)S(1)}, u32[]{:S(2)}, u32[]{:S(2)}) %collective-permute-start.11) | collective-permute-done | bytes 147488 | tf_op jit(solution)/shard_map/ppermute | solution.py:137
  42.5 3.7 %collective-permute-done.12.refs_7_ = bf16[64,1152]{1,0:T(8,128)(2,1)S(1)} collective-permute-done((bf16[64,1152]{1,0:T(8,128)(2,1)S(1)}, bf16[64,1152]{1,0:T(8,128)(2,1)S(1)}, u32[]{:S(2)}, u32[]{:S(2)}) %collective-permute-start.12) | collective-permute-done | bytes 147488 | tf_op jit(solution)/shard_map/ppermute | solution.py:137
  54.2 1.9 %fusion.43 = (bf16[192,2048]{1,0:T(8,128)(2,1)S(1)}, bf16[192,2048]{1,0:T(8,128)(2,1)S(1)}, bf16[192,2048]{1,0:T(8,128)(2,1)S(1)}) fusion(bf16[576,2048]{1,0:T(8,128)(2,1)} %collective-permute-done.14), kind=kLoop, calls=%fused_computation.54 | loop fusion | bytes 4718592 | tf_op jit(solution)/shard_map/slice | solution.py:337
  61.0 3.3 %collective-permute-start.23 = (bf16[64,512]{1,0:T(8,128)(2,1)S(1)}, bf16[64,512]{1,0:T(8,128)(2,1)S(1)}, u32[]{:S(2)}, u32[]{:S(2)}) collective-permute-start(bf16[64,512]{1,0:T(8,128)(2,1)S(1)} %get-tuple-element.37), channel_id=1, source_target_pairs={{0,12},{1,13},{2,14},{3,15},{4,0},{5,1},{6,2},{7,3},{8,4},{9,5},{1... | collective-permute-start | bytes 196616 | tf_op jit(solution)/shard_map/ppermute | solution.py:137
  65.3 2.0 %collective-permute-start.25 = (bf16[64,512]{1,0:T(8,128)(2,1)S(1)}, bf16[64,512]{1,0:T(8,128)(2,1)S(1)}, u32[]{:S(2)}, u32[]{:S(2)}) collective-permute-start(bf16[64,512]{1,0:T(8,128)(2,1)S(1)} %get-tuple-element.39), channel_id=1, source_target_pairs={{0,4},{1,5},{2,6},{3,7},{4,8},{5,9},{6,10},{7,11},{8,12},{9,13},{1... | collective-permute-start | bytes 196616 | tf_op jit(solution)/shard_map/ppermute | solution.py:137
  67.3 4.5 %collective-permute-done.24.refs_2_ = bf16[64,512]{1,0:T(8,128)(2,1)S(1)} collective-permute-done((bf16[64,512]{1,0:T(8,128)(2,1)S(1)}, bf16[64,512]{1,0:T(8,128)(2,1)S(1)}, u32[]{:S(2)}, u32[]{:S(2)}) %collective-permute-start.24) | collective-permute-done | bytes 65568 | tf_op jit(solution)/shard_map/ppermute | solution.py:137
  74.0 1.5 %collective-permute-start.26 = (bf16[16,512]{1,0:T(8,128)(2,1)S(1)}, bf16[16,512]{1,0:T(8,128)(2,1)S(1)}, u32[]{:S(2)}, u32[]{:S(2)}) collective-permute-start(bf16[16,512]{1,0:T(8,128)(2,1)S(1)} %get-tuple-element.45), channel_id=1, source_target_pairs={{0,1},{1,0},{2,3},{3,2},{4,5},{5,4},{6,7},{7,6},{8,9},{9,8},{10,11... | collective-permute-start | bytes 49160 | tf_op jit(solution)/shard_map/ppermute | solution.py:143
  75.5 5.6 %collective-permute-done.16.refs_2_ = bf16[64,1536]{1,0:T(8,128)(2,1)S(1)} collective-permute-done((bf16[64,1536]{1,0:T(8,128)(2,1)S(1)}, bf16[64,1536]{1,0:T(8,128)(2,1)S(1)}, u32[]{:S(2)}, u32[]{:S(2)}) %collective-permute-start.16) | collective-permute-done | bytes 196640 | tf_op jit(solution)/shard_map/ppermute | solution.py:143
  83.8 2.9 %collective-permute-start.22 = (bf16[16,1536]{1,0:T(8,128)(2,1)S(1)}, bf16[16,1536]{1,0:T(8,128)(2,1)S(1)}, u32[]{:S(2)}, u32[]{:S(2)}) collective-permute-start(bf16[16,1536]{1,0:T(8,128)(2,1)S(1)} %get-tuple-element.43), channel_id=1, source_target_pairs={{0,4},{1,5},{2,6},{3,7},{4,8},{5,9},{6,10},{7,11},{8,12},{9,13},{1... | collective-permute-start | bytes 147464 | tf_op jit(solution)/shard_map/ppermute | solution.py:137
  86.7 1.6 %fusion.14 = f32[192,2048]{1,0:T(8,128)S(1)} fusion(bf16[256,4096]{1,0:T(8,128)(2,1)} %collective-permute-done.19, bf16[256,576]{1,0:T(8,128)(2,1)S(1)} %collective-permute-done.18), kind=kOutput, calls=%fused_computation.19 | convolution fusion | flops 201326592 | bytes 2752512 | tf_op jit(solution)/shard_map/dot_general | solution.py:394
  88.3 1.7 %fusion.16 = f32[192,2048]{1,0:T(8,128)S(1)} fusion(bf16[256,4096]{1,0:T(8,128)(2,1)} %collective-permute-done.19, bf16[256,576]{1,0:T(8,128)(2,1)S(1)} %collective-permute-done.18), kind=kOutput, calls=%fused_computation.21 | convolution fusion | flops 201326592 | bytes 2752512 | tf_op jit(solution)/shard_map/dot_general | solution.py:394
  90.0 1.6 %fusion.18 = f32[192,2048]{1,0:T(8,128)S(1)} fusion(bf16[256,4096]{1,0:T(8,128)(2,1)} %collective-permute-done.19, bf16[256,576]{1,0:T(8,128)(2,1)S(1)} %collective-permute-done.18), kind=kOutput, calls=%fused_computation.23 | convolution fusion | flops 201326592 | bytes 2752512 | tf_op jit(solution)/shard_map/dot_general | solution.py:394
  96.5 1.9 %collective-permute-done.20.refs_1_ = bf16[16,1536]{1,0:T(8,128)(2,1)S(1)} collective-permute-done((bf16[16,1536]{1,0:T(8,128)(2,1)S(1)}, bf16[16,1536]{1,0:T(8,128)(2,1)S(1)}, u32[]{:S(2)}, u32[]{:S(2)}) %collective-permute-start.20) | collective-permute-done | bytes 49184 | tf_op jit(solution)/shard_map/ppermute | solution.py:137
  (102 shorter events, 33.6 us)
Async XLA Ops:
  2.3 10.4 %collective-permute-start = (bf16[16,3072]{1,0:T(8,128)(2,1)S(1)}, bf16[16,3072]{1,0:T(8,128)(2,1)S(1)}, u32[]{:S(2)}, u32[]{:S(2)}) collective-permute-start(bf16[16,3072]{1,0:T(8,128)(2,1)S(1)} %shard_map.111.refs_0_), channel_id=1, source_target_pairs={{0,4},{1,5},{2,6},{3,7},{4,8},{5,9},{6,10},{7,11},{8,12},{9,13},{1... | collective-permute-start | bytes 294920 | tf_op jit(solution)/shard_map/ppermute | solution.py:137
  5.4 9.2 %collective-permute-start.1 = (bf16[16,3072]{1,0:T(8,128)(2,1)S(1)}, bf16[16,3072]{1,0:T(8,128)(2,1)S(1)}, u32[]{:S(2)}, u32[]{:S(2)}) collective-permute-start(bf16[16,3072]{1,0:T(8,128)(2,1)S(1)} %shard_map.111.refs_0_), channel_id=1, source_target_pairs={{0,8},{1,9},{2,10},{3,11},{4,12},{5,13},{6,14},{7,15},{8,0},{9,1},... | collective-permute-start | bytes 294920 | tf_op jit(solution)/shard_map/ppermute | solution.py:137
  8.0 6.6 %collective-permute-start.2 = (bf16[16,3072]{1,0:T(8,128)(2,1)S(1)}, bf16[16,3072]{1,0:T(8,128)(2,1)S(1)}, u32[]{:S(2)}, u32[]{:S(2)}) collective-permute-start(bf16[16,3072]{1,0:T(8,128)(2,1)S(1)} %shard_map.111.refs_0_), channel_id=1, source_target_pairs={{0,12},{1,13},{2,14},{3,15},{4,0},{5,1},{6,2},{7,3},{8,4},{9,5},{1... | collective-permute-start | bytes 294920 | tf_op jit(solution)/shard_map/ppermute | solution.py:137
  14.6 39.6 %collective-permute-start.14 = (bf16[576,2048]{1,0:T(8,128)(2,1)}, bf16[576,2048]{1,0:T(8,128)(2,1)}, u32[]{:S(2)}, u32[]{:S(2)}) collective-permute-start(bf16[576,2048]{1,0:T(8,128)(2,1)} %pad_maximum_fusion.1), channel_id=1, source_target_pairs={{0,16},{16,0},{1,17},{17,1},{2,18},{18,2},{3,19},{19,3},{4,20},{20... | collective-permute-start | bytes 7077896 | tf_op jit(solution)/shard_map/ppermute | solution.py:133
  14.7 20.2 %collective-permute-start.3 = (bf16[64,3072]{1,0:T(8,128)(2,1)S(1)}, bf16[64,3072]{1,0:T(8,128)(2,1)S(1)}, u32[]{:S(2)}, u32[]{:S(2)}) collective-permute-start(bf16[64,3072]{1,0:T(8,128)(2,1)S(1)} %shard_map.112.refs_0_), channel_id=1, source_target_pairs={{0,1},{1,0},{2,3},{3,2},{4,5},{5,4},{6,7},{7,6},{8,9},{9,8},{10,11... | collective-permute-start | bytes 1179656 | tf_op jit(solution)/shard_map/ppermute | solution.py:143
  16.3 19.4 %collective-permute-start.4 = (bf16[64,3072]{1,0:T(8,128)(2,1)S(1)}, bf16[64,3072]{1,0:T(8,128)(2,1)S(1)}, u32[]{:S(2)}, u32[]{:S(2)}) collective-permute-start(bf16[64,3072]{1,0:T(8,128)(2,1)S(1)} %shard_map.112.refs_0_), channel_id=1, source_target_pairs={{0,2},{1,3},{2,0},{3,1},{4,6},{5,7},{6,4},{7,5},{8,10},{9,11},{10,... | collective-permute-start | bytes 1179656 | tf_op jit(solution)/shard_map/ppermute | solution.py:143
  19.4 9.0 %collective-permute-start.10 = (bf16[16,1152]{1,0:T(8,128)(2,1)S(1)}, bf16[16,1152]{1,0:T(8,128)(2,1)S(1)}, u32[]{:S(2)}, u32[]{:S(2)}) collective-permute-start(bf16[16,1152]{1,0:T(8,128)(2,1)S(1)} %shard_map.114.refs_0_), channel_id=1, source_target_pairs={{0,3},{1,2},{2,1},{3,0},{4,7},{5,6},{6,5},{7,4},{8,11},{9,10},{10,... | collective-permute-start | bytes 110600 | tf_op jit(solution)/shard_map/ppermute | solution.py:143
  21.8 7.2 %collective-permute-start.8 = (bf16[16,1152]{1,0:T(8,128)(2,1)S(1)}, bf16[16,1152]{1,0:T(8,128)(2,1)S(1)}, u32[]{:S(2)}, u32[]{:S(2)}) collective-permute-start(bf16[16,1152]{1,0:T(8,128)(2,1)S(1)} %shard_map.114.refs_0_), channel_id=1, source_target_pairs={{0,1},{1,0},{2,3},{3,2},{4,5},{5,4},{6,7},{7,6},{8,9},{9,8},{10,11... | collective-permute-start | bytes 110600 | tf_op jit(solution)/shard_map/ppermute | solution.py:143
  32.4 8.6 %collective-permute-start.11 = (bf16[64,1152]{1,0:T(8,128)(2,1)S(1)}, bf16[64,1152]{1,0:T(8,128)(2,1)S(1)}, u32[]{:S(2)}, u32[]{:S(2)}) collective-permute-start(bf16[64,1152]{1,0:T(8,128)(2,1)S(1)} %shard_map.115.refs_5_), channel_id=1, source_target_pairs={{0,4},{1,5},{2,6},{3,7},{4,8},{5,9},{6,10},{7,11},{8,12},{9,13},{1... | collective-permute-start | bytes 442376 | tf_op jit(solution)/shard_map/ppermute | solution.py:137
  35.0 13.0 %collective-permute-start.5 = (bf16[32,3072]{1,0:T(8,128)(2,1)S(1)}, bf16[32,3072]{1,0:T(8,128)(2,1)S(1)}, u32[]{:S(2)}, u32[]{:S(2)}) collective-permute-start(bf16[32,3072]{1,0:T(8,128)(2,1)S(1)} %slice.92), channel_id=1, source_target_pairs={{0,2},{1,3},{2,0},{3,1},{4,6},{5,7},{6,4},{7,5},{8,10},{9,11},{10,... | collective-permute-start | bytes 589832 | tf_op jit(solution)/shard_map/ppermute | solution.py:143
  35.7 12.9 %collective-permute-start.6 = (bf16[32,3072]{1,0:T(8,128)(2,1)S(1)}, bf16[32,3072]{1,0:T(8,128)(2,1)S(1)}, u32[]{:S(2)}, u32[]{:S(2)}) collective-permute-start(bf16[32,3072]{1,0:T(8,128)(2,1)S(1)} %slice.93), channel_id=1, source_target_pairs={{0,1},{1,0},{2,3},{3,2},{4,5},{5,4},{6,7},{7,6},{8,9},{9,8},{10,11... | collective-permute-start | bytes 589832 | tf_op jit(solution)/shard_map/ppermute | solution.py:143
  37.1 9.0 %collective-permute-start.12 = (bf16[64,1152]{1,0:T(8,128)(2,1)S(1)}, bf16[64,1152]{1,0:T(8,128)(2,1)S(1)}, u32[]{:S(2)}, u32[]{:S(2)}) collective-permute-start(bf16[64,1152]{1,0:T(8,128)(2,1)S(1)} %shard_map.115.refs_5_), channel_id=1, source_target_pairs={{0,8},{1,9},{2,10},{3,11},{4,12},{5,13},{6,14},{7,15},{8,0},{9,1},... | collective-permute-start | bytes 442376 | tf_op jit(solution)/shard_map/ppermute | solution.py:137
  54.0 29.8 %collective-permute-start.19 = (bf16[256,4096]{1,0:T(8,128)(2,1)S(1)}, bf16[256,4096]{1,0:T(8,128)(2,1)}, u32[]{:S(2)}, u32[]{:S(2)}) collective-permute-start(bf16[256,4096]{1,0:T(8,128)(2,1)S(1)} %get-tuple-element.29), channel_id=1, source_target_pairs={{0,16},{16,0},{1,17},{17,1},{2,18},{18,2},{3,19},{19,3},{4,20},{20... | collective-permute-start | bytes 6291464 | tf_op jit(solution)/shard_map/ppermute | solution.py:133
  60.5 22.7 %collective-permute-start.18 = (bf16[256,576]{1,0:T(8,128)(2,1)S(1)}, bf16[256,576]{1,0:T(8,128)(2,1)S(1)}, u32[]{:S(2)}, u32[]{:S(2)}) collective-permute-start(bf16[256,576]{1,0:T(8,128)(2,1)S(1)} %pad_maximum_fusion.3), channel_id=1, source_target_pairs={{0,16},{16,0},{1,17},{17,1},{2,18},{18,2},{3,19},{19,3},{4,20},{20... | collective-permute-start | bytes 884744 | tf_op jit(solution)/shard_map/ppermute | solution.py:133
  64.3 7.5 %collective-permute-start.24 = (bf16[64,512]{1,0:T(8,128)(2,1)S(1)}, bf16[64,512]{1,0:T(8,128)(2,1)S(1)}, u32[]{:S(2)}, u32[]{:S(2)}) collective-permute-start(bf16[64,512]{1,0:T(8,128)(2,1)S(1)} %get-tuple-element.38), channel_id=1, source_target_pairs={{0,8},{1,9},{2,10},{3,11},{4,12},{5,13},{6,14},{7,15},{8,0},{9,1},... | collective-permute-start | bytes 196616 | tf_op jit(solution)/shard_map/ppermute | solution.py:137
  65.3 6.6 %collective-permute-start.25 = (bf16[64,512]{1,0:T(8,128)(2,1)S(1)}, bf16[64,512]{1,0:T(8,128)(2,1)S(1)}, u32[]{:S(2)}, u32[]{:S(2)}) collective-permute-start(bf16[64,512]{1,0:T(8,128)(2,1)S(1)} %get-tuple-element.39), channel_id=1, source_target_pairs={{0,4},{1,5},{2,6},{3,7},{4,8},{5,9},{6,10},{7,11},{8,12},{9,13},{1... | collective-permute-start | bytes 196616 | tf_op jit(solution)/shard_map/ppermute | solution.py:137
  67.3 6.7 %collective-permute-start.15 = (bf16[64,1536]{1,0:T(8,128)(2,1)S(1)}, bf16[64,1536]{1,0:T(8,128)(2,1)S(1)}, u32[]{:S(2)}, u32[]{:S(2)}) collective-permute-start(bf16[64,1536]{1,0:T(8,128)(2,1)S(1)} %get-tuple-element.31), channel_id=1, source_target_pairs={{0,1},{1,0},{2,3},{3,2},{4,5},{5,4},{6,7},{7,6},{8,9},{9,8},{10,11... | collective-permute-start | bytes 589832 | tf_op jit(solution)/shard_map/ppermute | solution.py:143
  71.9 9.2 %collective-permute-start.16 = (bf16[64,1536]{1,0:T(8,128)(2,1)S(1)}, bf16[64,1536]{1,0:T(8,128)(2,1)S(1)}, u32[]{:S(2)}, u32[]{:S(2)}) collective-permute-start(bf16[64,1536]{1,0:T(8,128)(2,1)S(1)} %get-tuple-element.32), channel_id=1, source_target_pairs={{0,2},{1,3},{2,0},{3,1},{4,6},{5,7},{6,4},{7,5},{8,10},{9,11},{10,... | collective-permute-start | bytes 589832 | tf_op jit(solution)/shard_map/ppermute | solution.py:143
  71.9 10.1 %collective-permute-start.17 = (bf16[64,1536]{1,0:T(8,128)(2,1)S(1)}, bf16[64,1536]{1,0:T(8,128)(2,1)S(1)}, u32[]{:S(2)}, u32[]{:S(2)}) collective-permute-start(bf16[64,1536]{1,0:T(8,128)(2,1)S(1)} %get-tuple-element.33), channel_id=1, source_target_pairs={{0,3},{1,2},{2,1},{3,0},{4,7},{5,6},{6,5},{7,4},{8,11},{9,10},{10,... | collective-permute-start | bytes 589832 | tf_op jit(solution)/shard_map/ppermute | solution.py:143
  74.0 20.2 %collective-permute-start.26 = (bf16[16,512]{1,0:T(8,128)(2,1)S(1)}, bf16[16,512]{1,0:T(8,128)(2,1)S(1)}, u32[]{:S(2)}, u32[]{:S(2)}) collective-permute-start(bf16[16,512]{1,0:T(8,128)(2,1)S(1)} %get-tuple-element.45), channel_id=1, source_target_pairs={{0,1},{1,0},{2,3},{3,2},{4,5},{5,4},{6,7},{7,6},{8,9},{9,8},{10,11... | collective-permute-start | bytes 49160 | tf_op jit(solution)/shard_map/ppermute | solution.py:143
  81.1 15.4 %collective-permute-start.27 = (bf16[16,512]{1,0:T(8,128)(2,1)S(1)}, bf16[16,512]{1,0:T(8,128)(2,1)S(1)}, u32[]{:S(2)}, u32[]{:S(2)}) collective-permute-start(bf16[16,512]{1,0:T(8,128)(2,1)S(1)} %get-tuple-element.46), channel_id=1, source_target_pairs={{0,2},{1,3},{2,0},{3,1},{4,6},{5,7},{6,4},{7,5},{8,10},{9,11},{10,... | collective-permute-start | bytes 49160 | tf_op jit(solution)/shard_map/ppermute | solution.py:143
  82.0 14.5 %collective-permute-start.28 = (bf16[16,512]{1,0:T(8,128)(2,1)S(1)}, bf16[16,512]{1,0:T(8,128)(2,1)S(1)}, u32[]{:S(2)}, u32[]{:S(2)}) collective-permute-start(bf16[16,512]{1,0:T(8,128)(2,1)S(1)} %get-tuple-element.47), channel_id=1, source_target_pairs={{0,3},{1,2},{2,1},{3,0},{4,7},{5,6},{6,5},{7,4},{8,11},{9,10},{10,... | collective-permute-start | bytes 49160 | tf_op jit(solution)/shard_map/ppermute | solution.py:143
  83.2 13.3 %collective-permute-start.21 = (bf16[16,1536]{1,0:T(8,128)(2,1)S(1)}, bf16[16,1536]{1,0:T(8,128)(2,1)S(1)}, u32[]{:S(2)}, u32[]{:S(2)}) collective-permute-start(bf16[16,1536]{1,0:T(8,128)(2,1)S(1)} %get-tuple-element.42), channel_id=1, source_target_pairs={{0,8},{1,9},{2,10},{3,11},{4,12},{5,13},{6,14},{7,15},{8,0},{9,1},... | collective-permute-start | bytes 147464 | tf_op jit(solution)/shard_map/ppermute | solution.py:137
  83.8 12.7 %collective-permute-start.22 = (bf16[16,1536]{1,0:T(8,128)(2,1)S(1)}, bf16[16,1536]{1,0:T(8,128)(2,1)S(1)}, u32[]{:S(2)}, u32[]{:S(2)}) collective-permute-start(bf16[16,1536]{1,0:T(8,128)(2,1)S(1)} %get-tuple-element.43), channel_id=1, source_target_pairs={{0,4},{1,5},{2,6},{3,7},{4,8},{5,9},{6,10},{7,11},{8,12},{9,13},{1... | collective-permute-start | bytes 147464 | tf_op jit(solution)/shard_map/ppermute | solution.py:137
  (24 other events, 71.5 us)

commit v7 on v0

--- a/solution.py
+++ b/solution.py
@@ -1,6 +1,10 @@
+import math
+
 import jax
 import jax.numpy as jnp
 from jax import lax
+from jax.experimental import pallas as pl
+from jax.experimental.pallas import tpu as pltpu
 from jax.sharding import PartitionSpec as P
 
 
@@ -55,7 +59,7 @@
     return (weight_grads, partial_grad)
 
 
-def local(tokens, cotangent, gate_values, expert_ids, packing, w_gate, w_up, w_down):
+def routed_local(tokens, cotangent, gate_values, expert_ids, packing, w_gate, w_up, w_down):
     row_count, top_count = expert_ids.shape
     model_width = tokens.shape[1]
     dp_size = lax.axis_size("dp")
@@ -125,6 +129,229 @@
     return (input_grad, weight_grads[0], weight_grads[1], weight_grads[2])
 
 
+def swap(value):
+    return lax.ppermute(value, "dp", [(0, 1), (1, 0)])
+
+
+def shift_outer(value, count, inner, step):
+    return lax.ppermute(
+        value, "expert", [(place, (place + step * inner) % count) for place in range(count)]
+    )
+
+
+def swap_inner(value, count, partner):
+    return lax.ppermute(value, "expert", [(place, place ^ partner) for place in range(count)])
+
+
+VMEM = pl.BlockSpec(memory_space=pltpu.VMEM)
+LANES = 128
+NT = (((1,), (1,)), ((), ()))
+
+
+def on_chip(body, outs, *args):
+    moved = sum(arg.size * arg.dtype.itemsize for arg in args)
+    moved += sum(math.prod(shape) * jnp.dtype(dtype).itemsize for shape, dtype in outs)
+    return pl.pallas_call(
+        body,
+        out_shape=[jax.ShapeDtypeStruct(shape, dtype) for shape, dtype in outs],
+        in_specs=[VMEM] * len(args),
+        out_specs=[VMEM] * len(outs),
+        compiler_params=pltpu.CompilerParams(vmem_limit_bytes=moved + (4 << 20)),
+        cost_estimate=pl.CostEstimate(flops=0, bytes_accessed=moved, transcendentals=0),
+    )(*args)
+
+
+def stack_kernel(*refs):
+    low = 0
+    for ref in refs[:-1]:
+        refs[-1][low : low + ref.shape[0], :] = ref[...]
+        low += ref.shape[0]
+
+
+def stack(blocks):
+    rows = sum(block.shape[0] for block in blocks)
+    return on_chip(stack_kernel, [((rows, blocks[0].shape[1]), blocks[0].dtype)], *blocks)[0]
+
+
+def table_kernel(ids_ref, gates_ref, packing_ref, table_ref):
+    slots = packing_ref.shape[1]
+    count = table_ref.shape[0] - 16
+    labels = lax.broadcasted_iota(jnp.int32, (count, slots), 0)
+    total = jnp.zeros((count, slots), jnp.float32)
+    for k in range(ids_ref.shape[0]):
+        named = labels == ids_ref[k : k + 1, :]
+        total = total + jnp.where(named, gates_ref[k : k + 1, :].astype(jnp.float32), 0.0)
+    table_ref[:count, :] = total.astype(jnp.bfloat16)
+    lists = jnp.broadcast_to(packing_ref[...], (16, slots)).astype(jnp.float32)
+    table_ref[count:, :] = lists.astype(jnp.bfloat16)
+
+
+def payload_kernel(table_ref, other_ref, cotangent_ref, payload_ref):
+    rows, width = cotangent_ref.shape
+    count = table_ref.shape[0] - 16
+    slots = table_ref.shape[1]
+    homes = lax.broadcasted_iota(jnp.int32, (rows, slots), 0) + lax.axis_index("dp") * rows
+    gates = jnp.zeros((rows, count), jnp.float32)
+    for ref in (table_ref, other_ref):
+        lists = ref[count:, :].astype(jnp.float32)[:1, :]
+        matched = (lists == homes.astype(jnp.float32)).astype(jnp.float32).astype(jnp.bfloat16)
+        gates = gates + lax.dot_general(
+            matched, ref[:count, :], NT, preferred_element_type=jnp.float32
+        )
+    payload_ref[:, :width] = cotangent_ref[...]
+    payload_ref[:, width:] = jnp.zeros((rows, LANES), jnp.bfloat16)
+    payload_ref[:, width : width + count] = gates.astype(jnp.bfloat16)
+
+
+def rows_kernel(tokens_ref, *refs):
+    pieces, rows_ref, gate_ref = refs[:-2], refs[-2], refs[-1]
+    width = tokens_ref.shape[1]
+    rows_ref[:, :width] = tokens_ref[...]
+    low = 0
+    for ref in pieces:
+        span = slice(low, low + ref.shape[0])
+        rows_ref[span, width:] = ref[:, :width]
+        gates = ref[:, width:].astype(jnp.float32)
+        lanes = lax.broadcasted_iota(jnp.int32, gates.shape, 1)
+        here = jnp.where(lanes == lax.axis_index("expert"), gates, 0.0)
+        gate = jnp.sum(here, axis=1, keepdims=True)
+        gate_ref[span, :] = jnp.broadcast_to(gate, (ref.shape[0], gate_ref.shape[1]))
+        low += ref.shape[0]
+
+
+def column_kernel(*refs):
+    blocks, own_ref, sent = refs[:4], refs[4], refs[5:]
+    total = blocks[0][...].astype(jnp.float32)
+    for block in blocks[1:]:
+        total = total + block[...].astype(jnp.float32)
+    depth = own_ref.shape[0]
+    own_ref[...] = total[:depth]
+    for index, ref in enumerate(sent):
+        ref[...] = total[(index + 1) * depth : (index + 2) * depth].astype(jnp.bfloat16)
+
+
+def sum_kernel(own_ref, *refs):
+    total = own_ref[...]
+    for ref in refs[:-1]:
+        total = total + ref[...].astype(jnp.float32)
+    refs[-1][...] = total.astype(jnp.bfloat16)
+
+
+def along_outer(value, count, inner):
+    return [value] + [shift_outer(value, count, inner, step) for step in range(1, count // inner)]
+
+
+def dense_local(tokens, cotangent, gate_values, expert_ids, packing, w_gate, w_up, w_down):
+    row_count, model_width = tokens.shape
+    half = w_gate.shape[1]
+    count = lax.axis_size("expert")
+    inner = 4
+    outer = count // inner
+    low, wide = jnp.bfloat16, jnp.float32
+    height = row_count * count
+
+    token_blocks = along_outer(tokens, count, inner)
+    (table,) = on_chip(
+        table_kernel,
+        [((count + 16, row_count), low)],
+        expert_ids.T,
+        gate_values.T,
+        packing.reshape(1, row_count),
+    )
+    other_table = swap(table)
+    (payload,) = on_chip(
+        payload_kernel,
+        [((row_count, model_width + LANES), low)],
+        table,
+        other_table,
+        cotangent,
+    )
+    own_weights = jnp.concatenate([w_gate[0], w_up[0], w_down[0]], axis=0)
+    column = row_count * outer
+    top, bottom = slice(0, column // 2), slice(column // 2, None)
+
+    token_column, payload = lax.optimization_barrier((stack(token_blocks), payload))
+    token_near = [swap_inner(token_column, count, partner) for partner in (1, 2)]
+    upstream_blocks = along_outer(payload, count, inner)
+
+    token_near, upstream_column, own_weights = lax.optimization_barrier(
+        (token_near, stack(upstream_blocks), own_weights)
+    )
+    token_far = [swap_inner(token_near[0][top], count, 2), swap_inner(token_near[1][bottom], count, 1)]
+    upstream_near = [swap_inner(upstream_column, count, partner) for partner in (1, 2)]
+    other = swap(own_weights)
+
+    token_far, upstream_near = lax.optimization_barrier((token_far, upstream_near))
+    inputs = stack([token_column, *token_near, *token_far])
+    upstream_far = [
+        swap_inner(upstream_near[0][top], count, 2),
+        swap_inner(upstream_near[1][bottom], count, 1),
+    ]
+    rows, gate = on_chip(
+        rows_kernel,
+        [((height, 2 * model_width), low), ((height, 2 * half), wide)],
+        inputs,
+        upstream_column,
+        *upstream_near,
+        *upstream_far,
+    )
+    upstream = rows[:, model_width:]
+    gate_up = jnp.concatenate([w_gate[0], other[:half], w_up[0], other[half : 2 * half]], axis=0)
+    down = jnp.concatenate([w_down[0], other[2 * half :]], axis=0)
+    pre = jnp.dot(inputs, gate_up.T, preferred_element_type=wide)
+    gate_pre, up_pre = pre[:, : 2 * half], pre[:, 2 * half :]
+    hidden_grad = gate * jnp.dot(upstream, down.T, preferred_element_type=wide)
+    sigmoid_val = jax.nn.sigmoid(gate_pre)
+    activated = gate_pre * sigmoid_val
+    hidden = (gate * activated * up_pre).astype(low)
+    silu_slope = sigmoid_val * (1.0 + gate_pre * (1.0 - sigmoid_val))
+    gate_grad = (hidden_grad * up_pre * silu_slope).astype(low)
+    up_grad = (hidden_grad * activated).astype(low)
+    both_grad = jnp.concatenate([gate_grad, up_grad], axis=1)
+    partial_grad = jnp.dot(both_grad, gate_up, preferred_element_type=wide).astype(low)
+    blocks = jnp.split(partial_grad, inner, axis=0)
+    grads = (gate_grad, up_grad, hidden)
+    own_grads = jnp.concatenate([grad[:, :half] for grad in grads], axis=1)
+    sent_grads = jnp.concatenate([grad[:, half:] for grad in grads], axis=1)
+
+    blocks, sent_grads, rows = lax.optimization_barrier((blocks, sent_grads, rows))
+    returned = [swap_inner(blocks[partner], count, partner) for partner in range(1, inner)]
+    other_grads = swap(sent_grads)
+    other_rows = swap(rows)
+    own, *sent = on_chip(
+        column_kernel,
+        [((row_count, model_width), wide)] + [((row_count, model_width), low)] * (outer - 1),
+        blocks[0],
+        *returned,
+    )
+
+    sent, other_grads, other_rows = lax.optimization_barrier((sent, other_grads, other_rows))
+    back = [shift_outer(sent[step - 1], count, inner, -step) for step in range(1, outer)]
+    weight_grads = []
+    for index, span in enumerate((slice(0, model_width),) * 2 + (slice(model_width, None),)):
+        part = slice(index * half, (index + 1) * half)
+        total = jnp.dot(own_grads[:, part].T, rows[:, span], preferred_element_type=wide)
+        total = total + jnp.dot(
+            other_grads[:, part].T, other_rows[:, span], preferred_element_type=wide
+        )
+        weight_grads.append(total.astype(low)[None])
+    (input_grad,) = on_chip(sum_kernel, [((row_count, model_width), low)], own, *back)
+    return (input_grad, *weight_grads)
+
+
+def local(tokens, cotangent, gate_values, expert_ids, packing, w_gate, w_up, w_down):
+    row_count, top = expert_ids.shape
+    count = lax.axis_size("expert")
+    expert_count = count * w_gate.shape[0]
+    capacity = min(row_count, max(2, row_count * top // expert_count + 1))
+    few = capacity * 4 <= row_count
+    regular = lax.axis_size("dp") == 2 and count % 4 == 0 and w_gate.shape[0] == 1
+    chosen = dense_local if regular and not few else routed_local
+    return chosen(
+        tokens, cotangent, gate_values, expert_ids, packing, w_gate, w_up, w_down
+    )
+
+
 def solution(mesh):
     in_specs = (
         P(("groups", "dp", "expert"), None),

time: 172 us -> 74.4 us (0.43)
  waiting for transfers between devices: 81.2 us -> 28.9 us
  local copies, waits for them, and re-layouts: 20.5 us -> 5.58 us
  between operations: 15.2 us -> 0.87 us
  blocking collectives: 11.6 us -> 0 us
  other arithmetic: 7.45 us -> 1.89 us
  starting transfers between devices: 23.3 us -> 27.5 us
  matrix products: 11.6 us -> 8.15 us
    all_to_all x3 -> x0, waiting for transfers between devices: 71 us -> none  [the longest x1 29.4 us: local(): lax.all_to_all(send_upstream, 'expert', split_axis=0, concat_axis=0, tile...]
    ppermute x0 -> x24, waiting for transfers between devices: none -> 28.9 us  [the longest x11 22.6 us: swap_inner(): lax.ppermute(value, 'expert', [(place, place ^ partner) for place in rang...]
    ppermute x0 -> x24, starting transfers between devices: none -> 27.5 us  [the longest x9 13.7 us: shift_outer(): lax.ppermute(value, 'expert', [(place, (place + step * inner) % count) fo...]
    all_to_all x3 -> x0, starting transfers between devices: 23.2 us -> none  [the longest x1 8.34 us: local(): lax.all_to_all(send_rows, 'expert', split_axis=0, concat_axis=0, tiled=True)]
    reduce_scatter x1 -> x0, waiting for transfers between devices: 10.2 us -> none  [local(): lax.psum_scatter(partial_grad.reshape(expert_count, dp_size * capacity *...]
    all_gather x5 -> x0, blocking collectives: 9.66 us -> none  [the longest x1 2.11 us: local(): lax.all_gather(tokens, 'dp', axis=0, tiled=True)]
    convert_element_type x8 -> x0, local copies, waits for them, and re-layouts: 7.16 us -> none  [the longest x1 2.73 us: local(): partial_grad.reshape(expert_count, dp_size * capacity * model_width)]
    gather x7 -> x0, local copies, waits for them, and re-layouts: 5.79 us -> none  [the longest x4 2.46 us: fill_slots(): rebal_rows[slot_row]]
  transfers between devices with their start and end apart: 4 -> 24, of which waited for: 4 -> 10; matrix products, arithmetic and copies ran while one was open for 10% -> 9% of each run, Pallas kernels for 0% -> 1%
where the time goes in v7:
time: 74.4 us; the launch traced here: 74.1 us
  waiting for transfers between devices  28.9 us (39%)
  starting transfers between devices  27.5 us (37%)
  matrix products  8.15 us (11%)
  local copies, waits for them, and re-layouts  5.58 us (7%)
  other arithmetic  1.89 us (3%)
  Pallas kernels  1.21 us (2%)
  between operations  0.87 us (1%)
    ppermute x11, waiting for transfers between devices, swap_inner(): lax.ppermute(value, 'expert', [(place, place ^ partner) for place in rang...  22.6 us
    ppermute x9, starting transfers between devices, shift_outer(): lax.ppermute(value, 'expert', [(place, (place + step * inner) % count) fo...  13.7 us
    ppermute x11, starting transfers between devices, swap_inner(): lax.ppermute(value, 'expert', [(place, place ^ partner) for place in rang...  13 us
    ppermute x9, waiting for transfers between devices, shift_outer(): lax.ppermute(value, 'expert', [(place, (place + step * inner) % count) fo...  5.16 us
    unnamed x16, local copies, waits for them, and re-layouts  4.99 us
    dot_general x3, matrix products, dense_local(): jnp.dot(other_grads[:, part].T, other_rows[:, span], preferred_element_ty...  3.94 us
    concatenate x1, other arithmetic, dense_local(): own_weights = jnp.concatenate([w_gate[0], w_up[0], w_down[0]], axis=0)  1.76 us
  transfers between devices with their start and end apart: 24, of which 10 were waited for; matrix products, arithmetic and copies ran while one was open for 9% of the time, Pallas kernels for 1%

profile of v7, /device:TPU:0, one launch (start us, length us, event | category | flops | bytes accessed | tf_op | source)
XLA Modules:
  0.0 74.1 jit_solution(13969389596030702279)
XLA Ops:
  0.6 3.1 %collective-permute-start = (bf16[16,2048]{1,0:T(8,128)(2,1)}, bf16[16,2048]{1,0:T(8,128)(2,1)S(1)}, u32[]{:S(2)}, u32[]{:S(2)}) collective-permute-start(bf16[16,2048]{1,0:T(8,128)(2,1)} %refs_0_.1), channel_id=1, source_target_pairs={{0,4},{1,5},{2,6},{3,7},{4,8},{5,9},{6,10},{7,11},{8,12},{9,13},{1... | collective-permute-start | bytes 196616 | tf_op jit(solution)/shard_map/ppermute | solution.py:137
  3.7 2.6 %collective-permute-start.1 = (bf16[16,2048]{1,0:T(8,128)(2,1)}, bf16[16,2048]{1,0:T(8,128)(2,1)S(1)}, u32[]{:S(2)}, u32[]{:S(2)}) collective-permute-start(bf16[16,2048]{1,0:T(8,128)(2,1)} %refs_0_.1), channel_id=1, source_target_pairs={{0,8},{1,9},{2,10},{3,11},{4,12},{5,13},{6,14},{7,15},{8,0},{9,1},... | collective-permute-start | bytes 196616 | tf_op jit(solution)/shard_map/ppermute | solution.py:137
  6.3 1.3 %collective-permute-start.2 = (bf16[16,2048]{1,0:T(8,128)(2,1)}, bf16[16,2048]{1,0:T(8,128)(2,1)S(1)}, u32[]{:S(2)}, u32[]{:S(2)}) collective-permute-start(bf16[16,2048]{1,0:T(8,128)(2,1)} %refs_0_.1), channel_id=1, source_target_pairs={{0,12},{1,13},{2,14},{3,15},{4,0},{5,1},{6,2},{7,3},{8,4},{9,5},{1... | collective-permute-start | bytes 196616 | tf_op jit(solution)/shard_map/ppermute | solution.py:137
  12.8 1.6 %collective-permute-start.4 = (bf16[64,2048]{1,0:T(8,128)(2,1)S(1)}, bf16[64,2048]{1,0:T(8,128)(2,1)S(1)}, u32[]{:S(2)}, u32[]{:S(2)}) collective-permute-start(bf16[64,2048]{1,0:T(8,128)(2,1)S(1)} %shard_map.111.refs_0_), channel_id=1, source_target_pairs={{0,1},{1,0},{2,3},{3,2},{4,5},{5,4},{6,7},{7,6},{8,9},{9,8},{10,11... | collective-permute-start | bytes 786440 | tf_op jit(solution)/shard_map/ppermute | solution.py:143
  14.3 1.5 %collective-permute-start.5 = (bf16[64,2048]{1,0:T(8,128)(2,1)S(1)}, bf16[64,2048]{1,0:T(8,128)(2,1)S(1)}, u32[]{:S(2)}, u32[]{:S(2)}) collective-permute-start(bf16[64,2048]{1,0:T(8,128)(2,1)S(1)} %shard_map.111.refs_0_), channel_id=1, source_target_pairs={{0,2},{1,3},{2,0},{3,1},{4,6},{5,7},{6,4},{7,5},{8,10},{9,11},{10,... | collective-permute-start | bytes 786440 | tf_op jit(solution)/shard_map/ppermute | solution.py:143
  16.8 2.0 %collective-permute-start.7 = (bf16[16,2176]{1,0:T(8,128)(2,1)S(1)}, bf16[16,2176]{1,0:T(8,128)(2,1)S(1)}, u32[]{:S(2)}, u32[]{:S(2)}) collective-permute-start(bf16[16,2176]{1,0:T(8,128)(2,1)S(1)} %shard_map.113.refs_0_), channel_id=1, source_target_pairs={{0,8},{1,9},{2,10},{3,11},{4,12},{5,13},{6,14},{7,15},{8,0},{9,1},... | collective-permute-start | bytes 208904 | tf_op jit(solution)/shard_map/ppermute | solution.py:137
  19.7 1.8 %pad_maximum_fusion.1 = bf16[576,2048]{1,0:T(8,128)(2,1)S(1)} fusion(bf16[192,2048]{1,0:T(8,128)(2,1)} %bitcast.16, bf16[192,2048]{1,0:T(8,128)(2,1)} %bitcast.18, bf16[192,2048]{1,0:T(8,128)(2,1)} %bitcast.21), kind=kLoop, calls=%fused_computation.11 | loop fusion | flops 7077888 | bytes 4718592 | tf_op jit(solution)/shard_map/concatenate | solution.py:269
  21.4 1.3 %collective-permute-done.6.refs_1_ = bf16[16,2176]{1,0:T(8,128)(2,1)S(1)} collective-permute-done((bf16[16,2176]{1,0:T(8,128)(2,1)S(1)}, bf16[16,2176]{1,0:T(8,128)(2,1)S(1)}, u32[]{:S(2)}, u32[]{:S(2)}) %collective-permute-start.6) | collective-permute-done | bytes 69664 | tf_op jit(solution)/shard_map/ppermute | solution.py:137
  22.8 1.7 %collective-permute-done.7.refs_2_ = bf16[16,2176]{1,0:T(8,128)(2,1)S(1)} collective-permute-done((bf16[16,2176]{1,0:T(8,128)(2,1)S(1)}, bf16[16,2176]{1,0:T(8,128)(2,1)S(1)}, u32[]{:S(2)}, u32[]{:S(2)}) %collective-permute-start.7) | collective-permute-done | bytes 69664 | tf_op jit(solution)/shard_map/ppermute | solution.py:137
  25.7 1.6 %collective-permute-start.9 = (bf16[32,2048]{1,0:T(8,128)(2,1)S(1)}, bf16[32,2048]{1,0:T(8,128)(2,1)S(1)}, u32[]{:S(2)}, u32[]{:S(2)}) collective-permute-start(bf16[32,2048]{1,0:T(8,128)(2,1)S(1)} %slice.71), channel_id=1, source_target_pairs={{0,2},{1,3},{2,0},{3,1},{4,6},{5,7},{6,4},{7,5},{8,10},{9,11},{10,... | collective-permute-start | bytes 393224 | tf_op jit(solution)/shard_map/ppermute | solution.py:143
  27.3 1.6 %collective-permute-start.10 = (bf16[32,2048]{1,0:T(8,128)(2,1)S(1)}, bf16[32,2048]{1,0:T(8,128)(2,1)S(1)}, u32[]{:S(2)}, u32[]{:S(2)}) collective-permute-start(bf16[32,2048]{1,0:T(8,128)(2,1)S(1)} %slice.72), channel_id=1, source_target_pairs={{0,1},{1,0},{2,3},{3,2},{4,5},{5,4},{6,7},{7,6},{8,9},{9,8},{10,11... | collective-permute-start | bytes 393224 | tf_op jit(solution)/shard_map/ppermute | solution.py:143
  28.9 7.9 %collective-permute-done.9.refs_3_ = bf16[32,2048]{1,0:T(8,128)(2,1)S(1)} collective-permute-done((bf16[32,2048]{1,0:T(8,128)(2,1)S(1)}, bf16[32,2048]{1,0:T(8,128)(2,1)S(1)}, u32[]{:S(2)}, u32[]{:S(2)}) %collective-permute-start.9) | collective-permute-done | bytes 131104 | tf_op jit(solution)/shard_map/ppermute | solution.py:143
  37.4 1.6 %collective-permute-start.14 = (bf16[32,2176]{1,0:T(8,128)(2,1)S(1)}, bf16[32,2176]{1,0:T(8,128)(2,1)S(1)}, u32[]{:S(2)}, u32[]{:S(2)}) collective-permute-start(bf16[32,2176]{1,0:T(8,128)(2,1)S(1)} %slice.74), channel_id=1, source_target_pairs={{0,1},{1,0},{2,3},{3,2},{4,5},{5,4},{6,7},{7,6},{8,9},{9,8},{10,11... | collective-permute-start | bytes 417800 | tf_op jit(solution)/shard_map/ppermute | solution.py:143
  39.0 2.9 %collective-permute-done.13.refs_3_ = bf16[32,2176]{1,0:T(8,128)(2,1)S(1)} collective-permute-done((bf16[32,2176]{1,0:T(8,128)(2,1)S(1)}, bf16[32,2176]{1,0:T(8,128)(2,1)S(1)}, u32[]{:S(2)}, u32[]{:S(2)}) %collective-permute-start.13) | collective-permute-done | bytes 139296 | tf_op jit(solution)/shard_map/ppermute | solution.py:143
  46.1 1.2 %convolution_convert_fusion = bf16[256,2048]{1,0:T(8,128)(2,1)S(1)} fusion(bf16[192,2048]{1,0:T(8,128)(2,1)S(1)} %get-tuple-element.59, bf16[192,2048]{1,0:T(8,128)(2,1)S(1)} %bitcast.20, bf16[192,2048]{1,0:T(8,128)(2,1)S(1)} %get-tuple-element.60, bf16[192,2048]{1,0:T(8,128)(2,1)S(1)} %bitcast.23, bf16[256,384]{1,0:T(8,128)(2,1)S(1)} %get-tuple-element.62, ...), kind=kOutput, calls=%fused_computation.4 | convolution fusion | flops 819200000 | bytes 4587520 | tf_op jit(solution)/shard_map/dot_general | solution.py:311
  49.1 1.6 %collective-permute-start.16 = (bf16[64,2048]{1,0:T(8,128)(2,1)S(1)}, bf16[64,2048]{1,0:T(8,128)(2,1)S(1)}, u32[]{:S(2)}, u32[]{:S(2)}) collective-permute-start(bf16[64,2048]{1,0:T(8,128)(2,1)S(1)} %get-tuple-element.44), channel_id=1, source_target_pairs={{0,1},{1,0},{2,3},{3,2},{4,5},{5,4},{6,7},{7,6},{8,9},{9,8},{10,11... | collective-permute-start | bytes 786440 | tf_op jit(solution)/shard_map/ppermute | solution.py:143
  50.7 1.5 %collective-permute-start.17 = (bf16[64,2048]{1,0:T(8,128)(2,1)S(1)}, bf16[64,2048]{1,0:T(8,128)(2,1)S(1)}, u32[]{:S(2)}, u32[]{:S(2)}) collective-permute-start(bf16[64,2048]{1,0:T(8,128)(2,1)S(1)} %get-tuple-element.45), channel_id=1, source_target_pairs={{0,2},{1,3},{2,0},{3,1},{4,6},{5,7},{6,4},{7,5},{8,10},{9,11},{10,... | collective-permute-start | bytes 786440 | tf_op jit(solution)/shard_map/ppermute | solution.py:143
  53.1 5.3 %collective-permute-done.16.refs_1_ = bf16[64,2048]{1,0:T(8,128)(2,1)S(1)} collective-permute-done((bf16[64,2048]{1,0:T(8,128)(2,1)S(1)}, bf16[64,2048]{1,0:T(8,128)(2,1)S(1)}, u32[]{:S(2)}, u32[]{:S(2)}) %collective-permute-start.16) | collective-permute-done | bytes 262176 | tf_op jit(solution)/shard_map/ppermute | solution.py:143
  58.3 5.9 %collective-permute-done.17.refs_2_ = bf16[64,2048]{1,0:T(8,128)(2,1)S(1)} collective-permute-done((bf16[64,2048]{1,0:T(8,128)(2,1)S(1)}, bf16[64,2048]{1,0:T(8,128)(2,1)S(1)}, u32[]{:S(2)}, u32[]{:S(2)}) %collective-permute-start.17) | collective-permute-done | bytes 262176 | tf_op jit(solution)/shard_map/ppermute | solution.py:143
  64.4 2.0 %collective-permute-start.21 = (bf16[16,2048]{1,0:T(8,128)(2,1)S(1)}, bf16[16,2048]{1,0:T(8,128)(2,1)S(1)}, u32[]{:S(2)}, u32[]{:S(2)}) collective-permute-start(bf16[16,2048]{1,0:T(8,128)(2,1)S(1)} %get-tuple-element.53), channel_id=1, source_target_pairs={{0,12},{1,13},{2,14},{3,15},{4,0},{5,1},{6,2},{7,3},{8,4},{9,5},{1... | collective-permute-start | bytes 196616 | tf_op jit(solution)/shard_map/ppermute | solution.py:137
  67.4 1.3 %fusion.5 = bf16[1,192,2048]{2,1,0:T(8,128)(2,1)} fusion(f32[192,2048]{1,0:T(8,128)S(1)} %fusion.21, bf16[256,4096]{1,0:T(8,128)(2,1)S(1)} %collective-permute-done.20, bf16[256,576]{1,0:T(8,128)(2,1)S(1)} %collective-permute-done.19), kind=kOutput, calls=%fused_computation.10 | convolution fusion | flops 202113024 | bytes 3538944 | tf_op jit(solution)/shard_map/dot_general | solution.py:334
  68.6 1.4 %fusion.4 = bf16[1,192,2048]{2,1,0:T(8,128)(2,1)} fusion(f32[192,2048]{1,0:T(8,128)S(1)} %fusion.19, bf16[256,4096]{1,0:T(8,128)(2,1)S(1)} %collective-permute-done.20, bf16[256,576]{1,0:T(8,128)(2,1)S(1)} %collective-permute-done.19), kind=kOutput, calls=%fused_computation.9 | convolution fusion | flops 202113024 | bytes 3538944 | tf_op jit(solution)/shard_map/dot_general | solution.py:334
  70.0 1.3 %fusion.3 = bf16[1,192,2048]{2,1,0:T(8,128)(2,1)} fusion(f32[192,2048]{1,0:T(8,128)S(1)} %fusion.14, bf16[256,4096]{1,0:T(8,128)(2,1)S(1)} %collective-permute-done.20, bf16[256,576]{1,0:T(8,128)(2,1)S(1)} %collective-permute-done.19), kind=kOutput, calls=%fused_computation.8 | convolution fusion | flops 202113024 | bytes 3538944 | tf_op jit(solution)/shard_map/dot_general | solution.py:334
  71.3 1.3 %collective-permute-done.22.refs_1_ = bf16[16,2048]{1,0:T(8,128)(2,1)S(1)} collective-permute-done((bf16[16,2048]{1,0:T(8,128)(2,1)S(1)}, bf16[16,2048]{1,0:T(8,128)(2,1)S(1)}, u32[]{:S(2)}, u32[]{:S(2)}) %collective-permute-start.22) | collective-permute-done | bytes 65568 | tf_op jit(solution)/shard_map/ppermute | solution.py:137
  (68 shorter events, 18.1 us)
Async XLA Ops:
  0.6 11.3 %collective-permute-start = (bf16[16,2048]{1,0:T(8,128)(2,1)}, bf16[16,2048]{1,0:T(8,128)(2,1)S(1)}, u32[]{:S(2)}, u32[]{:S(2)}) collective-permute-start(bf16[16,2048]{1,0:T(8,128)(2,1)} %refs_0_.1), channel_id=1, source_target_pairs={{0,4},{1,5},{2,6},{3,7},{4,8},{5,9},{6,10},{7,11},{8,12},{9,13},{1... | collective-permute-start | bytes 196616 | tf_op jit(solution)/shard_map/ppermute | solution.py:137
  3.7 8.2 %collective-permute-start.1 = (bf16[16,2048]{1,0:T(8,128)(2,1)}, bf16[16,2048]{1,0:T(8,128)(2,1)S(1)}, u32[]{:S(2)}, u32[]{:S(2)}) collective-permute-start(bf16[16,2048]{1,0:T(8,128)(2,1)} %refs_0_.1), channel_id=1, source_target_pairs={{0,8},{1,9},{2,10},{3,11},{4,12},{5,13},{6,14},{7,15},{8,0},{9,1},... | collective-permute-start | bytes 196616 | tf_op jit(solution)/shard_map/ppermute | solution.py:137
  6.3 5.6 %collective-permute-start.2 = (bf16[16,2048]{1,0:T(8,128)(2,1)}, bf16[16,2048]{1,0:T(8,128)(2,1)S(1)}, u32[]{:S(2)}, u32[]{:S(2)}) collective-permute-start(bf16[16,2048]{1,0:T(8,128)(2,1)} %refs_0_.1), channel_id=1, source_target_pairs={{0,12},{1,13},{2,14},{3,15},{4,0},{5,1},{6,2},{7,3},{8,4},{9,5},{1... | collective-permute-start | bytes 196616 | tf_op jit(solution)/shard_map/ppermute | solution.py:137
  9.7 1.2 %collective-permute-start.3 = (bf16[32,16]{1,0:T(8,128)(2,1)S(1)}, bf16[32,16]{1,0:T(8,128)(2,1)S(1)}, u32[]{:S(2)}, u32[]{:S(2)}) collective-permute-start(bf16[32,16]{1,0:T(8,128)(2,1)S(1)} %shard_map.112.table_ref), channel_id=1, source_target_pairs={{0,16},{16,0},{1,17},{17,1},{2,18},{18,2},{3,19},{19,3},{4,20},{20... | collective-permute-start | bytes 3080 | tf_op jit(solution)/shard_map/ppermute | solution.py:133
  12.8 11.7 %collective-permute-start.4 = (bf16[64,2048]{1,0:T(8,128)(2,1)S(1)}, bf16[64,2048]{1,0:T(8,128)(2,1)S(1)}, u32[]{:S(2)}, u32[]{:S(2)}) collective-permute-start(bf16[64,2048]{1,0:T(8,128)(2,1)S(1)} %shard_map.111.refs_0_), channel_id=1, source_target_pairs={{0,1},{1,0},{2,3},{3,2},{4,5},{5,4},{6,7},{7,6},{8,9},{9,8},{10,11... | collective-permute-start | bytes 786440 | tf_op jit(solution)/shard_map/ppermute | solution.py:143
  14.3 10.2 %collective-permute-start.5 = (bf16[64,2048]{1,0:T(8,128)(2,1)S(1)}, bf16[64,2048]{1,0:T(8,128)(2,1)S(1)}, u32[]{:S(2)}, u32[]{:S(2)}) collective-permute-start(bf16[64,2048]{1,0:T(8,128)(2,1)S(1)} %shard_map.111.refs_0_), channel_id=1, source_target_pairs={{0,2},{1,3},{2,0},{3,1},{4,6},{5,7},{6,4},{7,5},{8,10},{9,11},{10,... | collective-permute-start | bytes 786440 | tf_op jit(solution)/shard_map/ppermute | solution.py:143
  15.9 6.9 %collective-permute-start.6 = (bf16[16,2176]{1,0:T(8,128)(2,1)S(1)}, bf16[16,2176]{1,0:T(8,128)(2,1)S(1)}, u32[]{:S(2)}, u32[]{:S(2)}) collective-permute-start(bf16[16,2176]{1,0:T(8,128)(2,1)S(1)} %shard_map.113.refs_0_), channel_id=1, source_target_pairs={{0,4},{1,5},{2,6},{3,7},{4,8},{5,9},{6,10},{7,11},{8,12},{9,13},{1... | collective-permute-start | bytes 208904 | tf_op jit(solution)/shard_map/ppermute | solution.py:137
  16.8 7.7 %collective-permute-start.7 = (bf16[16,2176]{1,0:T(8,128)(2,1)S(1)}, bf16[16,2176]{1,0:T(8,128)(2,1)S(1)}, u32[]{:S(2)}, u32[]{:S(2)}) collective-permute-start(bf16[16,2176]{1,0:T(8,128)(2,1)S(1)} %shard_map.113.refs_0_), channel_id=1, source_target_pairs={{0,8},{1,9},{2,10},{3,11},{4,12},{5,13},{6,14},{7,15},{8,0},{9,1},... | collective-permute-start | bytes 208904 | tf_op jit(solution)/shard_map/ppermute | solution.py:137
  18.8 5.7 %collective-permute-start.8 = (bf16[16,2176]{1,0:T(8,128)(2,1)S(1)}, bf16[16,2176]{1,0:T(8,128)(2,1)S(1)}, u32[]{:S(2)}, u32[]{:S(2)}) collective-permute-start(bf16[16,2176]{1,0:T(8,128)(2,1)S(1)} %shard_map.113.refs_0_), channel_id=1, source_target_pairs={{0,12},{1,13},{2,14},{3,15},{4,0},{5,1},{6,2},{7,3},{8,4},{9,5},{1... | collective-permute-start | bytes 208904 | tf_op jit(solution)/shard_map/ppermute | solution.py:137
  24.5 18.1 %collective-permute-start.15 = (bf16[576,2048]{1,0:T(8,128)(2,1)S(1)}, bf16[576,2048]{1,0:T(8,128)(2,1)S(1)}, u32[]{:S(2)}, u32[]{:S(2)}) collective-permute-start(bf16[576,2048]{1,0:T(8,128)(2,1)S(1)} %pad_maximum_fusion.1), channel_id=1, source_target_pairs={{0,16},{16,0},{1,17},{17,1},{2,18},{18,2},{3,19},{19,3},{4,20},{20... | collective-permute-start | bytes 7077896 | tf_op jit(solution)/shard_map/ppermute | solution.py:133
  24.6 12.1 %collective-permute-start.11 = (bf16[64,2176]{1,0:T(8,128)(2,1)S(1)}, bf16[64,2176]{1,0:T(8,128)(2,1)S(1)}, u32[]{:S(2)}, u32[]{:S(2)}) collective-permute-start(bf16[64,2176]{1,0:T(8,128)(2,1)S(1)} %shard_map.114.refs_0_), channel_id=1, source_target_pairs={{0,1},{1,0},{2,3},{3,2},{4,5},{5,4},{6,7},{7,6},{8,9},{9,8},{10,11... | collective-permute-start | bytes 835592 | tf_op jit(solution)/shard_map/ppermute | solution.py:143
  25.2 11.5 %collective-permute-start.12 = (bf16[64,2176]{1,0:T(8,128)(2,1)S(1)}, bf16[64,2176]{1,0:T(8,128)(2,1)S(1)}, u32[]{:S(2)}, u32[]{:S(2)}) collective-permute-start(bf16[64,2176]{1,0:T(8,128)(2,1)S(1)} %shard_map.114.refs_0_), channel_id=1, source_target_pairs={{0,2},{1,3},{2,0},{3,1},{4,6},{5,7},{6,4},{7,5},{8,10},{9,11},{10,... | collective-permute-start | bytes 835592 | tf_op jit(solution)/shard_map/ppermute | solution.py:143
  25.7 11.0 %collective-permute-start.9 = (bf16[32,2048]{1,0:T(8,128)(2,1)S(1)}, bf16[32,2048]{1,0:T(8,128)(2,1)S(1)}, u32[]{:S(2)}, u32[]{:S(2)}) collective-permute-start(bf16[32,2048]{1,0:T(8,128)(2,1)S(1)} %slice.71), channel_id=1, source_target_pairs={{0,2},{1,3},{2,0},{3,1},{4,6},{5,7},{6,4},{7,5},{8,10},{9,11},{10,... | collective-permute-start | bytes 393224 | tf_op jit(solution)/shard_map/ppermute | solution.py:143
  27.3 9.4 %collective-permute-start.10 = (bf16[32,2048]{1,0:T(8,128)(2,1)S(1)}, bf16[32,2048]{1,0:T(8,128)(2,1)S(1)}, u32[]{:S(2)}, u32[]{:S(2)}) collective-permute-start(bf16[32,2048]{1,0:T(8,128)(2,1)S(1)} %slice.72), channel_id=1, source_target_pairs={{0,1},{1,0},{2,3},{3,2},{4,5},{5,4},{6,7},{7,6},{8,9},{9,8},{10,11... | collective-permute-start | bytes 393224 | tf_op jit(solution)/shard_map/ppermute | solution.py:143
  36.8 5.1 %collective-permute-start.13 = (bf16[32,2176]{1,0:T(8,128)(2,1)S(1)}, bf16[32,2176]{1,0:T(8,128)(2,1)S(1)}, u32[]{:S(2)}, u32[]{:S(2)}) collective-permute-start(bf16[32,2176]{1,0:T(8,128)(2,1)S(1)} %slice.73), channel_id=1, source_target_pairs={{0,2},{1,3},{2,0},{3,1},{4,6},{5,7},{6,4},{7,5},{8,10},{9,11},{10,... | collective-permute-start | bytes 417800 | tf_op jit(solution)/shard_map/ppermute | solution.py:143
  37.4 5.1 %collective-permute-start.14 = (bf16[32,2176]{1,0:T(8,128)(2,1)S(1)}, bf16[32,2176]{1,0:T(8,128)(2,1)S(1)}, u32[]{:S(2)}, u32[]{:S(2)}) collective-permute-start(bf16[32,2176]{1,0:T(8,128)(2,1)S(1)} %slice.74), channel_id=1, source_target_pairs={{0,1},{1,0},{2,3},{3,2},{4,5},{5,4},{6,7},{7,6},{8,9},{9,8},{10,11... | collective-permute-start | bytes 417800 | tf_op jit(solution)/shard_map/ppermute | solution.py:143
  47.7 16.7 %collective-permute-start.20 = (bf16[256,4096]{1,0:T(8,128)(2,1)S(1)}, bf16[256,4096]{1,0:T(8,128)(2,1)S(1)}, u32[]{:S(2)}, u32[]{:S(2)}) collective-permute-start(bf16[256,4096]{1,0:T(8,128)(2,1)S(1)} %get-tuple-element.52), channel_id=1, source_target_pairs={{0,16},{16,0},{1,17},{17,1},{2,18},{18,2},{3,19},{19,3},{4,20},{20... | collective-permute-start | bytes 6291464 | tf_op jit(solution)/shard_map/ppermute | solution.py:133
  47.8 16.6 %collective-permute-start.19 = (bf16[256,576]{1,0:T(8,128)(2,1)S(1)}, bf16[256,576]{1,0:T(8,128)(2,1)S(1)}, u32[]{:S(2)}, u32[]{:S(2)}) collective-permute-start(bf16[256,576]{1,0:T(8,128)(2,1)S(1)} %pad_maximum_fusion.4), channel_id=1, source_target_pairs={{0,16},{16,0},{1,17},{17,1},{2,18},{18,2},{3,19},{19,3},{4,20},{20... | collective-permute-start | bytes 884744 | tf_op jit(solution)/shard_map/ppermute | solution.py:133
  49.1 9.2 %collective-permute-start.16 = (bf16[64,2048]{1,0:T(8,128)(2,1)S(1)}, bf16[64,2048]{1,0:T(8,128)(2,1)S(1)}, u32[]{:S(2)}, u32[]{:S(2)}) collective-permute-start(bf16[64,2048]{1,0:T(8,128)(2,1)S(1)} %get-tuple-element.44), channel_id=1, source_target_pairs={{0,1},{1,0},{2,3},{3,2},{4,5},{5,4},{6,7},{7,6},{8,9},{9,8},{10,11... | collective-permute-start | bytes 786440 | tf_op jit(solution)/shard_map/ppermute | solution.py:143
  50.7 13.6 %collective-permute-start.17 = (bf16[64,2048]{1,0:T(8,128)(2,1)S(1)}, bf16[64,2048]{1,0:T(8,128)(2,1)S(1)}, u32[]{:S(2)}, u32[]{:S(2)}) collective-permute-start(bf16[64,2048]{1,0:T(8,128)(2,1)S(1)} %get-tuple-element.45), channel_id=1, source_target_pairs={{0,2},{1,3},{2,0},{3,1},{4,6},{5,7},{6,4},{7,5},{8,10},{9,11},{10,... | collective-permute-start | bytes 786440 | tf_op jit(solution)/shard_map/ppermute | solution.py:143
  52.2 12.1 %collective-permute-start.18 = (bf16[64,2048]{1,0:T(8,128)(2,1)S(1)}, bf16[64,2048]{1,0:T(8,128)(2,1)S(1)}, u32[]{:S(2)}, u32[]{:S(2)}) collective-permute-start(bf16[64,2048]{1,0:T(8,128)(2,1)S(1)} %get-tuple-element.46), channel_id=1, source_target_pairs={{0,3},{1,2},{2,1},{3,0},{4,7},{5,6},{6,5},{7,4},{8,11},{9,10},{10,... | collective-permute-start | bytes 786440 | tf_op jit(solution)/shard_map/ppermute | solution.py:143
  64.4 6.9 %collective-permute-start.21 = (bf16[16,2048]{1,0:T(8,128)(2,1)S(1)}, bf16[16,2048]{1,0:T(8,128)(2,1)S(1)}, u32[]{:S(2)}, u32[]{:S(2)}) collective-permute-start(bf16[16,2048]{1,0:T(8,128)(2,1)S(1)} %get-tuple-element.53), channel_id=1, source_target_pairs={{0,12},{1,13},{2,14},{3,15},{4,0},{5,1},{6,2},{7,3},{8,4},{9,5},{1... | collective-permute-start | bytes 196616 | tf_op jit(solution)/shard_map/ppermute | solution.py:137
  66.4 6.2 %collective-permute-start.22 = (bf16[16,2048]{1,0:T(8,128)(2,1)S(1)}, bf16[16,2048]{1,0:T(8,128)(2,1)S(1)}, u32[]{:S(2)}, u32[]{:S(2)}) collective-permute-start(bf16[16,2048]{1,0:T(8,128)(2,1)S(1)} %get-tuple-element.54), channel_id=1, source_target_pairs={{0,8},{1,9},{2,10},{3,11},{4,12},{5,13},{6,14},{7,15},{8,0},{9,1},... | collective-permute-start | bytes 196616 | tf_op jit(solution)/shard_map/ppermute | solution.py:137
  67.3 6.1 %collective-permute-start.23 = (bf16[16,2048]{1,0:T(8,128)(2,1)S(1)}, bf16[16,2048]{1,0:T(8,128)(2,1)S(1)}, u32[]{:S(2)}, u32[]{:S(2)}) collective-permute-start(bf16[16,2048]{1,0:T(8,128)(2,1)S(1)} %get-tuple-element.55), channel_id=1, source_target_pairs={{0,4},{1,5},{2,6},{3,7},{4,8},{5,9},{6,10},{7,11},{8,12},{9,13},{1... | collective-permute-start | bytes 196616 | tf_op jit(solution)/shard_map/ppermute | solution.py:137
  (8 other events, 7.3 us)

commit v8 on v7

--- a/solution.py
+++ b/solution.py
@@ -144,18 +144,20 @@
 
 
 VMEM = pl.BlockSpec(memory_space=pltpu.VMEM)
+ANY = pl.BlockSpec(memory_space=pl.ANY)
 LANES = 128
 NT = (((1,), (1,)), ((), ()))
 
 
-def on_chip(body, outs, *args):
+def on_chip(body, outs, *args, scratch=(), spec=VMEM):
     moved = sum(arg.size * arg.dtype.itemsize for arg in args)
     moved += sum(math.prod(shape) * jnp.dtype(dtype).itemsize for shape, dtype in outs)
     return pl.pallas_call(
         body,
         out_shape=[jax.ShapeDtypeStruct(shape, dtype) for shape, dtype in outs],
-        in_specs=[VMEM] * len(args),
+        in_specs=[spec] * len(args),
         out_specs=[VMEM] * len(outs),
+        scratch_shapes=list(scratch),
         compiler_params=pltpu.CompilerParams(vmem_limit_bytes=moved + (4 << 20)),
         cost_estimate=pl.CostEstimate(flops=0, bytes_accessed=moved, transcendentals=0),
     )(*args)
@@ -173,7 +175,27 @@
     return on_chip(stack_kernel, [((rows, blocks[0].shape[1]), blocks[0].dtype)], *blocks)[0]
 
 
-def table_kernel(ids_ref, gates_ref, packing_ref, table_ref):
+def read_kernel(
+    ids_hbm, gates_hbm, packing_hbm, tokens_hbm, cotangent_hbm,
+    table_ref, tokens_ref, cotangent_ref,
+    ids_ref, gates_ref, packing_ref, ready,
+):
+    copies = [
+        pltpu.make_async_copy(source, target, ready.at[index])
+        for index, (source, target) in enumerate(
+            (
+                (ids_hbm, ids_ref),
+                (gates_hbm, gates_ref),
+                (packing_hbm, packing_ref),
+                (tokens_hbm, tokens_ref),
+                (cotangent_hbm, cotangent_ref),
+            )
+        )
+    ]
+    for copy in copies:
+        copy.start()
+    for copy in copies:
+        copy.wait()
     slots = packing_ref.shape[1]
     count = table_ref.shape[0] - 16
     labels = lax.broadcasted_iota(jnp.int32, (count, slots), 0)
@@ -251,35 +273,54 @@
     height = row_count * count
 
     token_blocks = along_outer(tokens, count, inner)
-    (table,) = on_chip(
-        table_kernel,
-        [((count + 16, row_count), low)],
-        expert_ids.T,
-        gate_values.T,
-        packing.reshape(1, row_count),
+    ids, gates, lists = expert_ids.T, gate_values.T, packing.reshape(1, row_count)
+    table, own_tokens, own_cotangent = on_chip(
+        read_kernel,
+        [
+            ((count + 16, row_count), low),
+            ((row_count, model_width), low),
+            ((row_count, model_width), low),
+        ],
+        ids,
+        gates,
+        lists,
+        tokens,
+        cotangent,
+        spec=ANY,
+        scratch=[
+            pltpu.VMEM(ids.shape, ids.dtype),
+            pltpu.VMEM(gates.shape, gates.dtype),
+            pltpu.VMEM(lists.shape, lists.dtype),
+            pltpu.SemaphoreType.DMA((5,)),
+        ],
     )
     other_table = swap(table)
+    other_table, own_gate, own_up = lax.optimization_barrier((other_table, w_gate[0], w_up[0]))
+    other_gate, other_up = swap(own_gate), swap(own_up)
     (payload,) = on_chip(
         payload_kernel,
         [((row_count, model_width + LANES), low)],
         table,
         other_table,
-        cotangent,
-    )
-    own_weights = jnp.concatenate([w_gate[0], w_up[0], w_down[0]], axis=0)
+        own_cotangent,
+    )
     column = row_count * outer
     top, bottom = slice(0, column // 2), slice(column // 2, None)
 
-    token_column, payload = lax.optimization_barrier((stack(token_blocks), payload))
+    token_column = stack([own_tokens, *token_blocks[1:]])
+    token_column, payload, other_gate, other_up = lax.optimization_barrier(
+        (token_column, payload, other_gate, other_up)
+    )
+    gate_up = stack([w_gate[0], other_gate, w_up[0], other_up])
     token_near = [swap_inner(token_column, count, partner) for partner in (1, 2)]
     upstream_blocks = along_outer(payload, count, inner)
 
-    token_near, upstream_column, own_weights = lax.optimization_barrier(
-        (token_near, stack(upstream_blocks), own_weights)
+    token_near, upstream_column, gate_up, own_down = lax.optimization_barrier(
+        (token_near, stack(upstream_blocks), gate_up, w_down[0])
     )
     token_far = [swap_inner(token_near[0][top], count, 2), swap_inner(token_near[1][bottom], count, 1)]
     upstream_near = [swap_inner(upstream_column, count, partner) for partner in (1, 2)]
-    other = swap(own_weights)
+    other_down = swap(own_down)
 
     token_far, upstream_near = lax.optimization_barrier((token_far, upstream_near))
     inputs = stack([token_column, *token_near, *token_far])
@@ -296,8 +337,7 @@
         *upstream_far,
     )
     upstream = rows[:, model_width:]
-    gate_up = jnp.concatenate([w_gate[0], other[:half], w_up[0], other[half : 2 * half]], axis=0)
-    down = jnp.concatenate([w_down[0], other[2 * half :]], axis=0)
+    down = jnp.concatenate([w_down[0], other_down], axis=0)
     pre = jnp.dot(inputs, gate_up.T, preferred_element_type=wide)
     gate_pre, up_pre = pre[:, : 2 * half], pre[:, 2 * half :]
     hidden_grad = gate * jnp.dot(upstream, down.T, preferred_element_type=wide)
@@ -325,7 +365,7 @@
         *returned,
     )
 
-    sent, other_grads, other_rows = lax.optimization_barrier((sent, other_grads, other_rows))
+    sent, other_grads = lax.optimization_barrier((sent, other_grads))
     back = [shift_outer(sent[step - 1], count, inner, -step) for step in range(1, outer)]
     weight_grads = []
     for index, span in enumerate((slice(0, model_width),) * 2 + (slice(model_width, None),)):
@@ -335,6 +375,7 @@
             other_grads[:, part].T, other_rows[:, span], preferred_element_type=wide
         )
         weight_grads.append(total.astype(low)[None])
+    weight_grads, back = lax.optimization_barrier((weight_grads, back))
     (input_grad,) = on_chip(sum_kernel, [((row_count, model_width), low)], own, *back)
     return (input_grad, *weight_grads)
 

time: 74.4 us -> 76.4 us (1.027)
  other arithmetic: 1.89 us -> 0.12 us
  waiting for transfers between devices: 28.9 us -> 30.5 us
  starting transfers between devices: 27.5 us -> 28.5 us
  local copies, waits for them, and re-layouts: 5.58 us -> 6.38 us
    ppermute x9, waiting for transfers between devices: 5.16 us -> 8.13 us  [shift_outer(): lax.ppermute(value, 'expert', [(place, (place + step * inner) % count) fo...]
    concatenate x1 -> x0, other arithmetic: 1.76 us -> none  [dense_local(): own_weights = jnp.concatenate([w_gate[0], w_up[0], w_down[0]], axis=0)]
    ppermute x11, waiting for transfers between devices: 22.6 us -> 21.6 us  [swap_inner(): lax.ppermute(value, 'expert', [(place, place ^ partner) for place in rang...]
    unnamed x16, local copies, waits for them, and re-layouts: 4.99 us -> 5.96 us
    ppermute x4 -> x6, starting transfers between devices: 0.71 us -> 1.67 us  [swap(): return lax.ppermute(value, 'dp', [(0, 1), (1, 0)])]
    pallas_call x8 -> x9, Pallas kernels: 1.21 us -> 1.61 us  [on_chip(): pl.pallas_call(body, out_shape=[jax.ShapeDtypeStruct(shape, dtype) for sh...]
  transfers between devices with their start and end apart: 24 -> 26, of which waited for: 10 -> 12; matrix products, arithmetic and copies ran while one was open for 9% -> 8% of each run, Pallas kernels for 1% -> 1%
where the time goes in v8:
time: 76.4 us; the launch traced here: 76 us
  waiting for transfers between devices  30.5 us (40%)
  starting transfers between devices  28.5 us (37%)
  matrix products  7.98 us (10%)
  local copies, waits for them, and re-layouts  6.38 us (8%)
  Pallas kernels  1.61 us (2%)
  between operations  0.87 us (1%)
    ppermute x11, waiting for transfers between devices, swap_inner(): lax.ppermute(value, 'expert', [(place, place ^ partner) for place in rang...  21.6 us
    ppermute x9, starting transfers between devices, shift_outer(): lax.ppermute(value, 'expert', [(place, (place + step * inner) % count) fo...  13.8 us
    ppermute x11, starting transfers between devices, swap_inner(): lax.ppermute(value, 'expert', [(place, place ^ partner) for place in rang...  13 us
    ppermute x9, waiting for transfers between devices, shift_outer(): lax.ppermute(value, 'expert', [(place, (place + step * inner) % count) fo...  8.13 us
    unnamed x16, local copies, waits for them, and re-layouts  5.96 us
    dot_general x3, matrix products, dense_local(): jnp.dot(other_grads[:, part].T, other_rows[:, span], preferred_element_ty...  3.96 us
    ppermute x6, starting transfers between devices, swap(): return lax.ppermute(value, 'dp', [(0, 1), (1, 0)])  1.67 us
    pallas_call x9, Pallas kernels, on_chip(): pl.pallas_call(body, out_shape=[jax.ShapeDtypeStruct(shape, dtype) for sh...  1.61 us
  transfers between devices with their start and end apart: 26, of which 12 were waited for; matrix products, arithmetic and copies ran while one was open for 8% of the time, Pallas kernels for 1%

profile of v8, /device:TPU:0, one launch (start us, length us, event | category | flops | bytes accessed | tf_op | source)
XLA Modules:
  0.0 76.0 jit_solution(8339520175287572384)
XLA Ops:
  6.4 2.9 %collective-permute-start = (bf16[16,2048]{1,0:T(8,128)(2,1)S(1)}, bf16[16,2048]{1,0:T(8,128)(2,1)S(1)}, u32[]{:S(2)}, u32[]{:S(2)}) collective-permute-start(bf16[16,2048]{1,0:T(8,128)(2,1)S(1)} %copy-done.3), channel_id=1, source_target_pairs={{0,4},{1,5},{2,6},{3,7},{4,8},{5,9},{6,10},{7,11},{8,12},{9,13},{1... | collective-permute-start | bytes 196616 | tf_op jit(solution)/shard_map/ppermute | solution.py:137
  9.3 2.6 %collective-permute-start.1 = (bf16[16,2048]{1,0:T(8,128)(2,1)S(1)}, bf16[16,2048]{1,0:T(8,128)(2,1)S(1)}, u32[]{:S(2)}, u32[]{:S(2)}) collective-permute-start(bf16[16,2048]{1,0:T(8,128)(2,1)S(1)} %copy-done.3), channel_id=1, source_target_pairs={{0,8},{1,9},{2,10},{3,11},{4,12},{5,13},{6,14},{7,15},{8,0},{9,1},... | collective-permute-start | bytes 196616 | tf_op jit(solution)/shard_map/ppermute | solution.py:137
  11.9 1.3 %collective-permute-start.2 = (bf16[16,2048]{1,0:T(8,128)(2,1)S(1)}, bf16[16,2048]{1,0:T(8,128)(2,1)S(1)}, u32[]{:S(2)}, u32[]{:S(2)}) collective-permute-start(bf16[16,2048]{1,0:T(8,128)(2,1)S(1)} %copy-done.3), channel_id=1, source_target_pairs={{0,12},{1,13},{2,14},{3,15},{4,0},{5,1},{6,2},{7,3},{8,4},{9,5},{1... | collective-permute-start | bytes 196616 | tf_op jit(solution)/shard_map/ppermute | solution.py:137
  14.0 2.7 %collective-permute-done.1.refs_2_ = bf16[16,2048]{1,0:T(8,128)(2,1)S(1)} collective-permute-done((bf16[16,2048]{1,0:T(8,128)(2,1)S(1)}, bf16[16,2048]{1,0:T(8,128)(2,1)S(1)}, u32[]{:S(2)}, u32[]{:S(2)}) %collective-permute-start.1) | collective-permute-done | bytes 65568 | tf_op jit(solution)/shard_map/ppermute | solution.py:137
  17.0 1.6 %collective-permute-start.6 = (bf16[64,2048]{1,0:T(8,128)(2,1)S(1)}, bf16[64,2048]{1,0:T(8,128)(2,1)S(1)}, u32[]{:S(2)}, u32[]{:S(2)}) collective-permute-start(bf16[64,2048]{1,0:T(8,128)(2,1)S(1)} %shard_map.112.refs_0_), channel_id=1, source_target_pairs={{0,1},{1,0},{2,3},{3,2},{4,5},{5,4},{6,7},{7,6},{8,9},{9,8},{10,11... | collective-permute-start | bytes 786440 | tf_op jit(solution)/shard_map/ppermute | solution.py:143
  18.5 1.5 %collective-permute-start.7 = (bf16[64,2048]{1,0:T(8,128)(2,1)S(1)}, bf16[64,2048]{1,0:T(8,128)(2,1)S(1)}, u32[]{:S(2)}, u32[]{:S(2)}) collective-permute-start(bf16[64,2048]{1,0:T(8,128)(2,1)S(1)} %shard_map.112.refs_0_), channel_id=1, source_target_pairs={{0,2},{1,3},{2,0},{3,1},{4,6},{5,7},{6,4},{7,5},{8,10},{9,11},{10,... | collective-permute-start | bytes 786440 | tf_op jit(solution)/shard_map/ppermute | solution.py:143
  20.0 2.8 %collective-permute-start.10 = (bf16[16,2176]{1,0:T(8,128)(2,1)S(1)}, bf16[16,2176]{1,0:T(8,128)(2,1)S(1)}, u32[]{:S(2)}, u32[]{:S(2)}) collective-permute-start(bf16[16,2176]{1,0:T(8,128)(2,1)S(1)} %shard_map.113.refs_0_), channel_id=1, source_target_pairs={{0,12},{1,13},{2,14},{3,15},{4,0},{5,1},{6,2},{7,3},{8,4},{9,5},{1... | collective-permute-start | bytes 208904 | tf_op jit(solution)/shard_map/ppermute | solution.py:137
  23.4 1.1 %copy-done = bf16[1,192,2048]{2,1,0:T(8,128)(2,1)S(1)} copy-done((bf16[1,192,2048]{2,1,0:T(8,128)(2,1)S(1)}, bf16[1,192,2048]{2,1,0:T(8,128)(2,1)}, u32[]{:S(2)}) %copy-start) | copy-done | bytes 786456
  24.6 1.1 %copy-done.1 = bf16[1,192,2048]{2,1,0:T(8,128)(2,1)S(1)} copy-done((bf16[1,192,2048]{2,1,0:T(8,128)(2,1)S(1)}, bf16[1,192,2048]{2,1,0:T(8,128)(2,1)}, u32[]{:S(2)}) %copy-start.1) | copy-done | bytes 786456
  25.9 3.1 %collective-permute-done.8.refs_1_ = bf16[16,2176]{1,0:T(8,128)(2,1)S(1)} collective-permute-done((bf16[16,2176]{1,0:T(8,128)(2,1)S(1)}, bf16[16,2176]{1,0:T(8,128)(2,1)S(1)}, u32[]{:S(2)}, u32[]{:S(2)}) %collective-permute-start.8) | collective-permute-done | bytes 69664 | tf_op jit(solution)/shard_map/ppermute | solution.py:137
  30.2 1.6 %collective-permute-start.11 = (bf16[32,2048]{1,0:T(8,128)(2,1)S(1)}, bf16[32,2048]{1,0:T(8,128)(2,1)S(1)}, u32[]{:S(2)}, u32[]{:S(2)}) collective-permute-start(bf16[32,2048]{1,0:T(8,128)(2,1)S(1)} %slice.62), channel_id=1, source_target_pairs={{0,2},{1,3},{2,0},{3,1},{4,6},{5,7},{6,4},{7,5},{8,10},{9,11},{10,... | collective-permute-start | bytes 393224 | tf_op jit(solution)/shard_map/ppermute | solution.py:143
  31.8 1.6 %collective-permute-start.12 = (bf16[32,2048]{1,0:T(8,128)(2,1)S(1)}, bf16[32,2048]{1,0:T(8,128)(2,1)S(1)}, u32[]{:S(2)}, u32[]{:S(2)}) collective-permute-start(bf16[32,2048]{1,0:T(8,128)(2,1)S(1)} %slice.63), channel_id=1, source_target_pairs={{0,1},{1,0},{2,3},{3,2},{4,5},{5,4},{6,7},{7,6},{8,9},{9,8},{10,11... | collective-permute-start | bytes 393224 | tf_op jit(solution)/shard_map/ppermute | solution.py:143
  33.4 7.9 %collective-permute-done.11.refs_3_ = bf16[32,2048]{1,0:T(8,128)(2,1)S(1)} collective-permute-done((bf16[32,2048]{1,0:T(8,128)(2,1)S(1)}, bf16[32,2048]{1,0:T(8,128)(2,1)S(1)}, u32[]{:S(2)}, u32[]{:S(2)}) %collective-permute-start.11) | collective-permute-done | bytes 131104 | tf_op jit(solution)/shard_map/ppermute | solution.py:143
  41.9 1.6 %collective-permute-start.16 = (bf16[32,2176]{1,0:T(8,128)(2,1)S(1)}, bf16[32,2176]{1,0:T(8,128)(2,1)S(1)}, u32[]{:S(2)}, u32[]{:S(2)}) collective-permute-start(bf16[32,2176]{1,0:T(8,128)(2,1)S(1)} %slice.65), channel_id=1, source_target_pairs={{0,1},{1,0},{2,3},{3,2},{4,5},{5,4},{6,7},{7,6},{8,9},{9,8},{10,11... | collective-permute-start | bytes 417800 | tf_op jit(solution)/shard_map/ppermute | solution.py:143
  43.5 1.0 %fusion.36 = f32[256,768]{1,0:T(8,128)S(1)} fusion(bf16[256,2048]{1,0:T(8,128)(2,1)S(1)} %shard_map.116.tokens_ref, bf16[768,2048]{1,0:T(8,128)(2,1)S(1)} %shard_map.115), kind=kOutput, calls=%fused_computation.43 | convolution fusion | flops 805306368 | bytes 4980736 | tf_op jit(solution)/shard_map/dot_general | solution.py:341
  44.5 1.9 %collective-permute-done.15.refs_3_ = bf16[32,2176]{1,0:T(8,128)(2,1)S(1)} collective-permute-done((bf16[32,2176]{1,0:T(8,128)(2,1)S(1)}, bf16[32,2176]{1,0:T(8,128)(2,1)S(1)}, u32[]{:S(2)}, u32[]{:S(2)}) %collective-permute-start.15) | collective-permute-done | bytes 139296 | tf_op jit(solution)/shard_map/ppermute | solution.py:143
  50.9 1.6 %collective-permute-start.18 = (bf16[64,2048]{1,0:T(8,128)(2,1)S(1)}, bf16[64,2048]{1,0:T(8,128)(2,1)S(1)}, u32[]{:S(2)}, u32[]{:S(2)}) collective-permute-start(bf16[64,2048]{1,0:T(8,128)(2,1)S(1)} %get-tuple-element.67), channel_id=1, source_target_pairs={{0,1},{1,0},{2,3},{3,2},{4,5},{5,4},{6,7},{7,6},{8,9},{9,8},{10,11... | collective-permute-start | bytes 786440 | tf_op jit(solution)/shard_map/ppermute | solution.py:143
  52.4 1.5 %collective-permute-start.19 = (bf16[64,2048]{1,0:T(8,128)(2,1)S(1)}, bf16[64,2048]{1,0:T(8,128)(2,1)S(1)}, u32[]{:S(2)}, u32[]{:S(2)}) collective-permute-start(bf16[64,2048]{1,0:T(8,128)(2,1)S(1)} %get-tuple-element.68), channel_id=1, source_target_pairs={{0,2},{1,3},{2,0},{3,1},{4,6},{5,7},{6,4},{7,5},{8,10},{9,11},{10,... | collective-permute-start | bytes 786440 | tf_op jit(solution)/shard_map/ppermute | solution.py:143
  54.8 5.3 %collective-permute-done.18.refs_1_ = bf16[64,2048]{1,0:T(8,128)(2,1)S(1)} collective-permute-done((bf16[64,2048]{1,0:T(8,128)(2,1)S(1)}, bf16[64,2048]{1,0:T(8,128)(2,1)S(1)}, u32[]{:S(2)}, u32[]{:S(2)}) %collective-permute-start.18) | collective-permute-done | bytes 262176 | tf_op jit(solution)/shard_map/ppermute | solution.py:143
  60.1 6.0 %collective-permute-done.19.refs_2_ = bf16[64,2048]{1,0:T(8,128)(2,1)S(1)} collective-permute-done((bf16[64,2048]{1,0:T(8,128)(2,1)S(1)}, bf16[64,2048]{1,0:T(8,128)(2,1)S(1)}, u32[]{:S(2)}, u32[]{:S(2)}) %collective-permute-start.19) | collective-permute-done | bytes 262176 | tf_op jit(solution)/shard_map/ppermute | solution.py:143
  66.2 3.0 %collective-permute-start.23 = (bf16[16,2048]{1,0:T(8,128)(2,1)S(1)}, bf16[16,2048]{1,0:T(8,128)(2,1)S(1)}, u32[]{:S(2)}, u32[]{:S(2)}) collective-permute-start(bf16[16,2048]{1,0:T(8,128)(2,1)S(1)} %get-tuple-element.77), channel_id=1, source_target_pairs={{0,12},{1,13},{2,14},{3,15},{4,0},{5,1},{6,2},{7,3},{8,4},{9,5},{1... | collective-permute-start | bytes 196616 | tf_op jit(solution)/shard_map/ppermute | solution.py:137
  69.8 1.3 %fusion.3 = bf16[1,192,2048]{2,1,0:T(8,128)(2,1)} fusion(f32[192,2048]{1,0:T(8,128)S(1)} %fusion.14, bf16[256,4096]{1,0:T(8,128)(2,1)S(1)} %collective-permute-done.22, bf16[256,576]{1,0:T(8,128)(2,1)S(1)} %collective-permute-done.21), kind=kOutput, calls=%fused_computation.7 | convolution fusion | flops 202113024 | bytes 3538944 | tf_op jit(solution)/shard_map/dot_general | solution.py:374
  71.1 1.4 %fusion.4 = bf16[1,192,2048]{2,1,0:T(8,128)(2,1)} fusion(f32[192,2048]{1,0:T(8,128)S(1)} %fusion.19, bf16[256,4096]{1,0:T(8,128)(2,1)S(1)} %collective-permute-done.22, bf16[256,576]{1,0:T(8,128)(2,1)S(1)} %collective-permute-done.21), kind=kOutput, calls=%fused_computation.8 | convolution fusion | flops 202113024 | bytes 3538944 | tf_op jit(solution)/shard_map/dot_general | solution.py:374
  72.5 1.3 %fusion.5 = bf16[1,192,2048]{2,1,0:T(8,128)(2,1)} fusion(f32[192,2048]{1,0:T(8,128)S(1)} %fusion.21, bf16[256,4096]{1,0:T(8,128)(2,1)S(1)} %collective-permute-done.22, bf16[256,576]{1,0:T(8,128)(2,1)S(1)} %collective-permute-done.21), kind=kOutput, calls=%fused_computation.9 | convolution fusion | flops 202113024 | bytes 3538944 | tf_op jit(solution)/shard_map/dot_general | solution.py:374
  (71 shorter events, 17.7 us)
Async XLA Ops:
  5.9 11.0 %collective-permute-start.4 = (bf16[192,2048]{1,0:T(8,128)(2,1)}, bf16[192,2048]{1,0:T(8,128)(2,1)S(1)}, u32[]{:S(2)}, u32[]{:S(2)}) collective-permute-start(bf16[192,2048]{1,0:T(8,128)(2,1)} %bitcast.15), channel_id=1, source_target_pairs={{0,16},{16,0},{1,17},{17,1},{2,18},{18,2},{3,19},{19,3},{4,20},{20... | collective-permute-start | bytes 2359304 | tf_op jit(solution)/shard_map/ppermute | solution.py:133
  6.3 10.7 %collective-permute-start.5 = (bf16[192,2048]{1,0:T(8,128)(2,1)}, bf16[192,2048]{1,0:T(8,128)(2,1)S(1)}, u32[]{:S(2)}, u32[]{:S(2)}) collective-permute-start(bf16[192,2048]{1,0:T(8,128)(2,1)} %bitcast.17), channel_id=1, source_target_pairs={{0,16},{16,0},{1,17},{17,1},{2,18},{18,2},{3,19},{19,3},{4,20},{20... | collective-permute-start | bytes 2359304 | tf_op jit(solution)/shard_map/ppermute | solution.py:133
  6.4 7.5 %collective-permute-start = (bf16[16,2048]{1,0:T(8,128)(2,1)S(1)}, bf16[16,2048]{1,0:T(8,128)(2,1)S(1)}, u32[]{:S(2)}, u32[]{:S(2)}) collective-permute-start(bf16[16,2048]{1,0:T(8,128)(2,1)S(1)} %copy-done.3), channel_id=1, source_target_pairs={{0,4},{1,5},{2,6},{3,7},{4,8},{5,9},{6,10},{7,11},{8,12},{9,13},{1... | collective-permute-start | bytes 196616 | tf_op jit(solution)/shard_map/ppermute | solution.py:137
  9.3 7.3 %collective-permute-start.1 = (bf16[16,2048]{1,0:T(8,128)(2,1)S(1)}, bf16[16,2048]{1,0:T(8,128)(2,1)S(1)}, u32[]{:S(2)}, u32[]{:S(2)}) collective-permute-start(bf16[16,2048]{1,0:T(8,128)(2,1)S(1)} %copy-done.3), channel_id=1, source_target_pairs={{0,8},{1,9},{2,10},{3,11},{4,12},{5,13},{6,14},{7,15},{8,0},{9,1},... | collective-permute-start | bytes 196616 | tf_op jit(solution)/shard_map/ppermute | solution.py:137
  17.0 12.0 %collective-permute-start.6 = (bf16[64,2048]{1,0:T(8,128)(2,1)S(1)}, bf16[64,2048]{1,0:T(8,128)(2,1)S(1)}, u32[]{:S(2)}, u32[]{:S(2)}) collective-permute-start(bf16[64,2048]{1,0:T(8,128)(2,1)S(1)} %shard_map.112.refs_0_), channel_id=1, source_target_pairs={{0,1},{1,0},{2,3},{3,2},{4,5},{5,4},{6,7},{7,6},{8,9},{9,8},{10,11... | collective-permute-start | bytes 786440 | tf_op jit(solution)/shard_map/ppermute | solution.py:143
  18.5 10.5 %collective-permute-start.7 = (bf16[64,2048]{1,0:T(8,128)(2,1)S(1)}, bf16[64,2048]{1,0:T(8,128)(2,1)S(1)}, u32[]{:S(2)}, u32[]{:S(2)}) collective-permute-start(bf16[64,2048]{1,0:T(8,128)(2,1)S(1)} %shard_map.112.refs_0_), channel_id=1, source_target_pairs={{0,2},{1,3},{2,0},{3,1},{4,6},{5,7},{6,4},{7,5},{8,10},{9,11},{10,... | collective-permute-start | bytes 786440 | tf_op jit(solution)/shard_map/ppermute | solution.py:143
  20.0 5.9 %collective-permute-start.10 = (bf16[16,2176]{1,0:T(8,128)(2,1)S(1)}, bf16[16,2176]{1,0:T(8,128)(2,1)S(1)}, u32[]{:S(2)}, u32[]{:S(2)}) collective-permute-start(bf16[16,2176]{1,0:T(8,128)(2,1)S(1)} %shard_map.113.refs_0_), channel_id=1, source_target_pairs={{0,12},{1,13},{2,14},{3,15},{4,0},{5,1},{6,2},{7,3},{8,4},{9,5},{1... | collective-permute-start | bytes 208904 | tf_op jit(solution)/shard_map/ppermute | solution.py:137
  22.9 6.1 %collective-permute-start.8 = (bf16[16,2176]{1,0:T(8,128)(2,1)S(1)}, bf16[16,2176]{1,0:T(8,128)(2,1)S(1)}, u32[]{:S(2)}, u32[]{:S(2)}) collective-permute-start(bf16[16,2176]{1,0:T(8,128)(2,1)S(1)} %shard_map.113.refs_0_), channel_id=1, source_target_pairs={{0,4},{1,5},{2,6},{3,7},{4,8},{5,9},{6,10},{7,11},{8,12},{9,13},{1... | collective-permute-start | bytes 208904 | tf_op jit(solution)/shard_map/ppermute | solution.py:137
  22.9 6.1 %collective-permute-start.9 = (bf16[16,2176]{1,0:T(8,128)(2,1)S(1)}, bf16[16,2176]{1,0:T(8,128)(2,1)S(1)}, u32[]{:S(2)}, u32[]{:S(2)}) collective-permute-start(bf16[16,2176]{1,0:T(8,128)(2,1)S(1)} %shard_map.113.refs_0_), channel_id=1, source_target_pairs={{0,8},{1,9},{2,10},{3,11},{4,12},{5,13},{6,14},{7,15},{8,0},{9,1},... | collective-permute-start | bytes 208904 | tf_op jit(solution)/shard_map/ppermute | solution.py:137
  29.0 18.1 %collective-permute-start.17 = (bf16[192,2048]{1,0:T(8,128)(2,1)S(1)}, bf16[192,2048]{1,0:T(8,128)(2,1)S(1)}, u32[]{:S(2)}, u32[]{:S(2)}) collective-permute-start(bf16[192,2048]{1,0:T(8,128)(2,1)S(1)} %bitcast.22), channel_id=1, source_target_pairs={{0,16},{16,0},{1,17},{17,1},{2,18},{18,2},{3,19},{19,3},{4,20},{20... | collective-permute-start | bytes 2359304 | tf_op jit(solution)/shard_map/ppermute | solution.py:133
  29.1 12.1 %collective-permute-start.13 = (bf16[64,2176]{1,0:T(8,128)(2,1)S(1)}, bf16[64,2176]{1,0:T(8,128)(2,1)S(1)}, u32[]{:S(2)}, u32[]{:S(2)}) collective-permute-start(bf16[64,2176]{1,0:T(8,128)(2,1)S(1)} %shard_map.114.refs_0_), channel_id=1, source_target_pairs={{0,1},{1,0},{2,3},{3,2},{4,5},{5,4},{6,7},{7,6},{8,9},{9,8},{10,11... | collective-permute-start | bytes 835592 | tf_op jit(solution)/shard_map/ppermute | solution.py:143
  29.7 11.5 %collective-permute-start.14 = (bf16[64,2176]{1,0:T(8,128)(2,1)S(1)}, bf16[64,2176]{1,0:T(8,128)(2,1)S(1)}, u32[]{:S(2)}, u32[]{:S(2)}) collective-permute-start(bf16[64,2176]{1,0:T(8,128)(2,1)S(1)} %shard_map.114.refs_0_), channel_id=1, source_target_pairs={{0,2},{1,3},{2,0},{3,1},{4,6},{5,7},{6,4},{7,5},{8,10},{9,11},{10,... | collective-permute-start | bytes 835592 | tf_op jit(solution)/shard_map/ppermute | solution.py:143
  30.2 11.0 %collective-permute-start.11 = (bf16[32,2048]{1,0:T(8,128)(2,1)S(1)}, bf16[32,2048]{1,0:T(8,128)(2,1)S(1)}, u32[]{:S(2)}, u32[]{:S(2)}) collective-permute-start(bf16[32,2048]{1,0:T(8,128)(2,1)S(1)} %slice.62), channel_id=1, source_target_pairs={{0,2},{1,3},{2,0},{3,1},{4,6},{5,7},{6,4},{7,5},{8,10},{9,11},{10,... | collective-permute-start | bytes 393224 | tf_op jit(solution)/shard_map/ppermute | solution.py:143
  31.8 9.4 %collective-permute-start.12 = (bf16[32,2048]{1,0:T(8,128)(2,1)S(1)}, bf16[32,2048]{1,0:T(8,128)(2,1)S(1)}, u32[]{:S(2)}, u32[]{:S(2)}) collective-permute-start(bf16[32,2048]{1,0:T(8,128)(2,1)S(1)} %slice.63), channel_id=1, source_target_pairs={{0,1},{1,0},{2,3},{3,2},{4,5},{5,4},{6,7},{7,6},{8,9},{9,8},{10,11... | collective-permute-start | bytes 393224 | tf_op jit(solution)/shard_map/ppermute | solution.py:143
  41.3 5.1 %collective-permute-start.15 = (bf16[32,2176]{1,0:T(8,128)(2,1)S(1)}, bf16[32,2176]{1,0:T(8,128)(2,1)S(1)}, u32[]{:S(2)}, u32[]{:S(2)}) collective-permute-start(bf16[32,2176]{1,0:T(8,128)(2,1)S(1)} %slice.64), channel_id=1, source_target_pairs={{0,2},{1,3},{2,0},{3,1},{4,6},{5,7},{6,4},{7,5},{8,10},{9,11},{10,... | collective-permute-start | bytes 417800 | tf_op jit(solution)/shard_map/ppermute | solution.py:143
  41.9 5.1 %collective-permute-start.16 = (bf16[32,2176]{1,0:T(8,128)(2,1)S(1)}, bf16[32,2176]{1,0:T(8,128)(2,1)S(1)}, u32[]{:S(2)}, u32[]{:S(2)}) collective-permute-start(bf16[32,2176]{1,0:T(8,128)(2,1)S(1)} %slice.65), channel_id=1, source_target_pairs={{0,1},{1,0},{2,3},{3,2},{4,5},{5,4},{6,7},{7,6},{8,9},{9,8},{10,11... | collective-permute-start | bytes 417800 | tf_op jit(solution)/shard_map/ppermute | solution.py:143
  49.5 20.3 %collective-permute-start.22 = (bf16[256,4096]{1,0:T(8,128)(2,1)S(1)}, bf16[256,4096]{1,0:T(8,128)(2,1)S(1)}, u32[]{:S(2)}, u32[]{:S(2)}) collective-permute-start(bf16[256,4096]{1,0:T(8,128)(2,1)S(1)} %get-tuple-element.71), channel_id=1, source_target_pairs={{0,16},{16,0},{1,17},{17,1},{2,18},{18,2},{3,19},{19,3},{4,20},{20... | collective-permute-start | bytes 6291464 | tf_op jit(solution)/shard_map/ppermute | solution.py:133
  49.6 16.6 %collective-permute-start.21 = (bf16[256,576]{1,0:T(8,128)(2,1)S(1)}, bf16[256,576]{1,0:T(8,128)(2,1)S(1)}, u32[]{:S(2)}, u32[]{:S(2)}) collective-permute-start(bf16[256,576]{1,0:T(8,128)(2,1)S(1)} %pad_maximum_fusion), channel_id=1, source_target_pairs={{0,16},{16,0},{1,17},{17,1},{2,18},{18,2},{3,19},{19,3},{4,20},{20... | collective-permute-start | bytes 884744 | tf_op jit(solution)/shard_map/ppermute | solution.py:133
  50.9 9.2 %collective-permute-start.18 = (bf16[64,2048]{1,0:T(8,128)(2,1)S(1)}, bf16[64,2048]{1,0:T(8,128)(2,1)S(1)}, u32[]{:S(2)}, u32[]{:S(2)}) collective-permute-start(bf16[64,2048]{1,0:T(8,128)(2,1)S(1)} %get-tuple-element.67), channel_id=1, source_target_pairs={{0,1},{1,0},{2,3},{3,2},{4,5},{5,4},{6,7},{7,6},{8,9},{9,8},{10,11... | collective-permute-start | bytes 786440 | tf_op jit(solution)/shard_map/ppermute | solution.py:143
  52.4 13.6 %collective-permute-start.19 = (bf16[64,2048]{1,0:T(8,128)(2,1)S(1)}, bf16[64,2048]{1,0:T(8,128)(2,1)S(1)}, u32[]{:S(2)}, u32[]{:S(2)}) collective-permute-start(bf16[64,2048]{1,0:T(8,128)(2,1)S(1)} %get-tuple-element.68), channel_id=1, source_target_pairs={{0,2},{1,3},{2,0},{3,1},{4,6},{5,7},{6,4},{7,5},{8,10},{9,11},{10,... | collective-permute-start | bytes 786440 | tf_op jit(solution)/shard_map/ppermute | solution.py:143
  54.0 12.1 %collective-permute-start.20 = (bf16[64,2048]{1,0:T(8,128)(2,1)S(1)}, bf16[64,2048]{1,0:T(8,128)(2,1)S(1)}, u32[]{:S(2)}, u32[]{:S(2)}) collective-permute-start(bf16[64,2048]{1,0:T(8,128)(2,1)S(1)} %get-tuple-element.69), channel_id=1, source_target_pairs={{0,3},{1,2},{2,1},{3,0},{4,7},{5,6},{6,5},{7,4},{8,11},{9,10},{10,... | collective-permute-start | bytes 786440 | tf_op jit(solution)/shard_map/ppermute | solution.py:143
  66.2 7.6 %collective-permute-start.23 = (bf16[16,2048]{1,0:T(8,128)(2,1)S(1)}, bf16[16,2048]{1,0:T(8,128)(2,1)S(1)}, u32[]{:S(2)}, u32[]{:S(2)}) collective-permute-start(bf16[16,2048]{1,0:T(8,128)(2,1)S(1)} %get-tuple-element.77), channel_id=1, source_target_pairs={{0,12},{1,13},{2,14},{3,15},{4,0},{5,1},{6,2},{7,3},{8,4},{9,5},{1... | collective-permute-start | bytes 196616 | tf_op jit(solution)/shard_map/ppermute | solution.py:137
  69.2 5.2 %collective-permute-start.24 = (bf16[16,2048]{1,0:T(8,128)(2,1)S(1)}, bf16[16,2048]{1,0:T(8,128)(2,1)S(1)}, u32[]{:S(2)}, u32[]{:S(2)}) collective-permute-start(bf16[16,2048]{1,0:T(8,128)(2,1)S(1)} %get-tuple-element.78), channel_id=1, source_target_pairs={{0,8},{1,9},{2,10},{3,11},{4,12},{5,13},{6,14},{7,15},{8,0},{9,1},... | collective-permute-start | bytes 196616 | tf_op jit(solution)/shard_map/ppermute | solution.py:137
  69.3 6.1 %collective-permute-start.25 = (bf16[16,2048]{1,0:T(8,128)(2,1)S(1)}, bf16[16,2048]{1,0:T(8,128)(2,1)S(1)}, u32[]{:S(2)}, u32[]{:S(2)}) collective-permute-start(bf16[16,2048]{1,0:T(8,128)(2,1)S(1)} %get-tuple-element.79), channel_id=1, source_target_pairs={{0,4},{1,5},{2,6},{3,7},{4,8},{5,9},{6,10},{7,11},{8,12},{9,13},{1... | collective-permute-start | bytes 196616 | tf_op jit(solution)/shard_map/ppermute | solution.py:137
  (10 other events, 15.6 us)

commit v9 on v8

--- a/solution.py
+++ b/solution.py
@@ -133,12 +133,6 @@
     return lax.ppermute(value, "dp", [(0, 1), (1, 0)])
 
 
-def shift_outer(value, count, inner, step):
-    return lax.ppermute(
-        value, "expert", [(place, (place + step * inner) % count) for place in range(count)]
-    )
-
-
 def swap_inner(value, count, partner):
     return lax.ppermute(value, "expert", [(place, place ^ partner) for place in range(count)])
 
@@ -149,7 +143,7 @@
 NT = (((1,), (1,)), ((), ()))
 
 
-def on_chip(body, outs, *args, scratch=(), spec=VMEM):
+def on_chip(body, outs, *args, scratch=(), spec=VMEM, limit=None):
     moved = sum(arg.size * arg.dtype.itemsize for arg in args)
     moved += sum(math.prod(shape) * jnp.dtype(dtype).itemsize for shape, dtype in outs)
     return pl.pallas_call(
@@ -158,7 +152,7 @@
         in_specs=[spec] * len(args),
         out_specs=[VMEM] * len(outs),
         scratch_shapes=list(scratch),
-        compiler_params=pltpu.CompilerParams(vmem_limit_bytes=moved + (4 << 20)),
+        compiler_params=pltpu.CompilerParams(vmem_limit_bytes=limit or moved + (4 << 20)),
         cost_estimate=pl.CostEstimate(flops=0, bytes_accessed=moved, transcendentals=0),
     )(*args)
 
@@ -180,17 +174,16 @@
     table_ref, tokens_ref, cotangent_ref,
     ids_ref, gates_ref, packing_ref, ready,
 ):
+    pairs = [(tokens_hbm, tokens_ref.at[index]) for index in range(tokens_ref.shape[0])]
+    pairs += [
+        (ids_hbm, ids_ref),
+        (gates_hbm, gates_ref),
+        (packing_hbm, packing_ref),
+        (cotangent_hbm, cotangent_ref),
+    ]
     copies = [
         pltpu.make_async_copy(source, target, ready.at[index])
-        for index, (source, target) in enumerate(
-            (
-                (ids_hbm, ids_ref),
-                (gates_hbm, gates_ref),
-                (packing_hbm, packing_ref),
-                (tokens_hbm, tokens_ref),
-                (cotangent_hbm, cotangent_ref),
-            )
-        )
+        for index, (source, target) in enumerate(pairs)
     ]
     for copy in copies:
         copy.start()
@@ -220,47 +213,55 @@
         gates = gates + lax.dot_general(
             matched, ref[:count, :], NT, preferred_element_type=jnp.float32
         )
-    payload_ref[:, :width] = cotangent_ref[...]
-    payload_ref[:, width:] = jnp.zeros((rows, LANES), jnp.bfloat16)
-    payload_ref[:, width : width + count] = gates.astype(jnp.bfloat16)
+    for copy in range(payload_ref.shape[0]):
+        payload_ref[copy, :, :width] = cotangent_ref[...]
+        payload_ref[copy, :, width:] = jnp.zeros((rows, LANES), jnp.bfloat16)
+        payload_ref[copy, :, width : width + count] = gates.astype(jnp.bfloat16)
+
+
+def place_rows(target, pieces, columns, width):
+    depth = pieces[0].shape[0]
+    here = lax.rem(lax.axis_index("expert"), 4)
+    for ref, partner, low in zip(pieces, (0, 1, 2, 3, 3), (0, 0, 0, 0, depth // 2)):
+        start = pl.multiple_of((here ^ partner) * depth + low, 16)
+        target[pl.ds(start, ref.shape[0]), columns] = ref[:, :width]
+
+
+def tokens_kernel(*refs):
+    place_rows(refs[-1], refs[:-1], slice(None), refs[-1].shape[1])
 
 
 def rows_kernel(tokens_ref, *refs):
-    pieces, rows_ref, gate_ref = refs[:-2], refs[-2], refs[-1]
+    pieces, rows_ref, gate_ref, beside_ref = refs[:-3], refs[-3], refs[-2], refs[-1]
     width = tokens_ref.shape[1]
     rows_ref[:, :width] = tokens_ref[...]
-    low = 0
-    for ref in pieces:
-        span = slice(low, low + ref.shape[0])
-        rows_ref[span, width:] = ref[:, :width]
-        gates = ref[:, width:].astype(jnp.float32)
-        lanes = lax.broadcasted_iota(jnp.int32, gates.shape, 1)
-        here = jnp.where(lanes == lax.axis_index("expert"), gates, 0.0)
-        gate = jnp.sum(here, axis=1, keepdims=True)
-        gate_ref[span, :] = jnp.broadcast_to(gate, (ref.shape[0], gate_ref.shape[1]))
-        low += ref.shape[0]
-
-
-def column_kernel(*refs):
-    blocks, own_ref, sent = refs[:4], refs[4], refs[5:]
-    total = blocks[0][...].astype(jnp.float32)
-    for block in blocks[1:]:
-        total = total + block[...].astype(jnp.float32)
-    depth = own_ref.shape[0]
-    own_ref[...] = total[:depth]
-    for index, ref in enumerate(sent):
-        ref[...] = total[(index + 1) * depth : (index + 2) * depth].astype(jnp.bfloat16)
-
-
-def sum_kernel(own_ref, *refs):
-    total = own_ref[...]
-    for ref in refs[:-1]:
-        total = total + ref[...].astype(jnp.float32)
-    refs[-1][...] = total.astype(jnp.bfloat16)
-
-
-def along_outer(value, count, inner):
-    return [value] + [shift_outer(value, count, inner, step) for step in range(1, count // inner)]
+    place_rows(rows_ref, pieces, slice(width, None), width)
+    place_rows(beside_ref, [ref.at[:, width:] for ref in pieces], slice(None), LANES)
+    gates = beside_ref[...].astype(jnp.float32)
+    lanes = lax.broadcasted_iota(jnp.int32, gates.shape, 1)
+    here = jnp.where(lanes == lax.axis_index("expert"), gates, 0.0)
+    gate = jnp.sum(here, axis=1, keepdims=True)
+    gate_ref[...] = jnp.broadcast_to(gate, gate_ref.shape)
+
+
+def column_kernel(blocks_ref, out_ref):
+    total = blocks_ref[0].astype(jnp.float32)
+    for index in range(1, blocks_ref.shape[0]):
+        total = total + blocks_ref[index].astype(jnp.float32)
+    depth = out_ref.shape[1]
+    for index in range(out_ref.shape[0]):
+        out_ref[index] = total[index * depth : (index + 1) * depth].astype(jnp.bfloat16)
+
+
+def sum_kernel(blocks_ref, out_ref):
+    total = blocks_ref[0].astype(jnp.float32)
+    for index in range(1, blocks_ref.shape[0]):
+        total = total + blocks_ref[index].astype(jnp.float32)
+    out_ref[...] = total.astype(jnp.bfloat16)
+
+
+def exchange(value, groups):
+    return lax.all_to_all(value, "expert", 0, 0, axis_index_groups=groups)
 
 
 def dense_local(tokens, cotangent, gate_values, expert_ids, packing, w_gate, w_up, w_down):
@@ -272,13 +273,14 @@
     low, wide = jnp.bfloat16, jnp.float32
     height = row_count * count
 
-    token_blocks = along_outer(tokens, count, inner)
+    columns = [[place + step * inner for step in range(outer)] for place in range(inner)]
+    planes = [[place * inner + step for step in range(inner)] for place in range(outer)]
     ids, gates, lists = expert_ids.T, gate_values.T, packing.reshape(1, row_count)
-    table, own_tokens, own_cotangent = on_chip(
+    table, sent_tokens, own_cotangent = on_chip(
         read_kernel,
         [
             ((count + 16, row_count), low),
-            ((row_count, model_width), low),
+            ((outer, row_count, model_width), low),
             ((row_count, model_width), low),
         ],
         ids,
@@ -291,39 +293,42 @@
             pltpu.VMEM(ids.shape, ids.dtype),
             pltpu.VMEM(gates.shape, gates.dtype),
             pltpu.VMEM(lists.shape, lists.dtype),
-            pltpu.SemaphoreType.DMA((5,)),
+            pltpu.SemaphoreType.DMA((4 + outer,)),
         ],
-    )
+        limit=48 << 20,
+    )
+    column = row_count * outer
+    token_column = exchange(sent_tokens, columns).reshape(column, model_width)
     other_table = swap(table)
     other_table, own_gate, own_up = lax.optimization_barrier((other_table, w_gate[0], w_up[0]))
     other_gate, other_up = swap(own_gate), swap(own_up)
     (payload,) = on_chip(
         payload_kernel,
-        [((row_count, model_width + LANES), low)],
+        [((outer, row_count, model_width + LANES), low)],
         table,
         other_table,
         own_cotangent,
     )
-    column = row_count * outer
     top, bottom = slice(0, column // 2), slice(column // 2, None)
 
-    token_column = stack([own_tokens, *token_blocks[1:]])
     token_column, payload, other_gate, other_up = lax.optimization_barrier(
         (token_column, payload, other_gate, other_up)
     )
     gate_up = stack([w_gate[0], other_gate, w_up[0], other_up])
     token_near = [swap_inner(token_column, count, partner) for partner in (1, 2)]
-    upstream_blocks = along_outer(payload, count, inner)
+    upstream_column = exchange(payload, columns).reshape(column, model_width + LANES)
 
     token_near, upstream_column, gate_up, own_down = lax.optimization_barrier(
-        (token_near, stack(upstream_blocks), gate_up, w_down[0])
+        (token_near, upstream_column, gate_up, w_down[0])
     )
     token_far = [swap_inner(token_near[0][top], count, 2), swap_inner(token_near[1][bottom], count, 1)]
     upstream_near = [swap_inner(upstream_column, count, partner) for partner in (1, 2)]
     other_down = swap(own_down)
 
     token_far, upstream_near = lax.optimization_barrier((token_far, upstream_near))
-    inputs = stack([token_column, *token_near, *token_far])
+    (inputs,) = on_chip(
+        tokens_kernel, [((height, model_width), low)], token_column, *token_near, *token_far
+    )
     upstream_far = [
         swap_inner(upstream_near[0][top], count, 2),
         swap_inner(upstream_near[1][bottom], count, 1),
@@ -335,6 +340,7 @@
         upstream_column,
         *upstream_near,
         *upstream_far,
+        scratch=[pltpu.VMEM((height, LANES), low)],
     )
     upstream = rows[:, model_width:]
     down = jnp.concatenate([w_down[0], other_down], axis=0)
@@ -349,24 +355,18 @@
     up_grad = (hidden_grad * activated).astype(low)
     both_grad = jnp.concatenate([gate_grad, up_grad], axis=1)
     partial_grad = jnp.dot(both_grad, gate_up, preferred_element_type=wide).astype(low)
-    blocks = jnp.split(partial_grad, inner, axis=0)
     grads = (gate_grad, up_grad, hidden)
     own_grads = jnp.concatenate([grad[:, :half] for grad in grads], axis=1)
     sent_grads = jnp.concatenate([grad[:, half:] for grad in grads], axis=1)
 
-    blocks, sent_grads, rows = lax.optimization_barrier((blocks, sent_grads, rows))
-    returned = [swap_inner(blocks[partner], count, partner) for partner in range(1, inner)]
+    partial_grad, sent_grads, rows = lax.optimization_barrier((partial_grad, sent_grads, rows))
+    blocks = exchange(partial_grad.reshape(inner, column, model_width), planes)
     other_grads = swap(sent_grads)
     other_rows = swap(rows)
-    own, *sent = on_chip(
-        column_kernel,
-        [((row_count, model_width), wide)] + [((row_count, model_width), low)] * (outer - 1),
-        blocks[0],
-        *returned,
-    )
+    (sent,) = on_chip(column_kernel, [((outer, row_count, model_width), low)], blocks)
 
     sent, other_grads = lax.optimization_barrier((sent, other_grads))
-    back = [shift_outer(sent[step - 1], count, inner, -step) for step in range(1, outer)]
+    back = exchange(sent, columns)
     weight_grads = []
     for index, span in enumerate((slice(0, model_width),) * 2 + (slice(model_width, None),)):
         part = slice(index * half, (index + 1) * half)
@@ -376,7 +376,7 @@
         )
         weight_grads.append(total.astype(low)[None])
     weight_grads, back = lax.optimization_barrier((weight_grads, back))
-    (input_grad,) = on_chip(sum_kernel, [((row_count, model_width), low)], own, *back)
+    (input_grad,) = on_chip(sum_kernel, [((row_count, model_width), low)], back)
     return (input_grad, *weight_grads)
 
 

time: 76.4 us -> 94.6 us (1.24)
  matrix products: 7.98 us -> 17.9 us
  local copies, waits for them, and re-layouts: 6.38 us -> 13.2 us
  waiting for transfers between devices: 30.5 us -> 25.5 us
  Pallas kernels: 1.61 us -> 5.19 us
  starting transfers between devices: 28.5 us -> 30.1 us
    all_to_all x0 -> x4, starting transfers between devices: none -> 18.2 us  [exchange(): return lax.all_to_all(value, 'expert', 0, 0, axis_index_groups=groups)]
    all_to_all x0 -> x4, waiting for transfers between devices: none -> 16.9 us  [exchange(): return lax.all_to_all(value, 'expert', 0, 0, axis_index_groups=groups)]
    ppermute x9 -> x0, starting transfers between devices: 13.8 us -> none  [shift_outer(): lax.ppermute(value, 'expert', [(place, (place + step * inner) % count) fo...]
    ppermute x11 -> x8, waiting for transfers between devices: 21.6 us -> 7.83 us  [swap_inner(): lax.ppermute(value, 'expert', [(place, place ^ partner) for place in rang...]
    ppermute x9 -> x0, waiting for transfers between devices: 8.13 us -> none  [shift_outer(): lax.ppermute(value, 'expert', [(place, (place + step * inner) % count) fo...]
    unnamed x16 -> x42, local copies, waits for them, and re-layouts: 5.96 us -> 11 us
    dot_general x3, matrix products: 1.2 us -> 5.66 us  [dense_local(): jnp.dot(own_grads[:, part].T, rows[:, span], preferred_element_type=wide)]
    dot_general x3, matrix products: 3.96 us -> 8.38 us  [dense_local(): jnp.dot(other_grads[:, part].T, other_rows[:, span], preferred_element_ty...]
  transfers between devices with their start and end apart: 26 -> 18, of which waited for: 12 -> 6; matrix products, arithmetic and copies ran while one was open for 8% -> 18% of each run, Pallas kernels for 1% -> 4%
where the time goes in v9:
time: 94.6 us; the launch traced here: 93.6 us
  starting transfers between devices  30.1 us (32%)
  waiting for transfers between devices  25.5 us (27%)
  matrix products  17.9 us (19%)
  local copies, waits for them, and re-layouts  13.2 us (14%)
  Pallas kernels  5.19 us (5%)
    all_to_all x4, starting transfers between devices, exchange(): return lax.all_to_all(value, 'expert', 0, 0, axis_index_groups=groups)  18.2 us
    all_to_all x4, waiting for transfers between devices, exchange(): return lax.all_to_all(value, 'expert', 0, 0, axis_index_groups=groups)  16.9 us
    unnamed x42, local copies, waits for them, and re-layouts  11 us
    ppermute x8, starting transfers between devices, swap_inner(): lax.ppermute(value, 'expert', [(place, place ^ partner) for place in rang...  10.4 us
    dot_general x3, matrix products, dense_local(): jnp.dot(other_grads[:, part].T, other_rows[:, span], preferred_element_ty...  8.38 us
    ppermute x8, waiting for transfers between devices, swap_inner(): lax.ppermute(value, 'expert', [(place, place ^ partner) for place in rang...  7.83 us
    dot_general x3, matrix products, dense_local(): jnp.dot(own_grads[:, part].T, rows[:, span], preferred_element_type=wide)  5.66 us
    pallas_call x7, Pallas kernels, on_chip(): pl.pallas_call(body, out_shape=[jax.ShapeDtypeStruct(shape, dtype) for sh...  5.19 us
  transfers between devices with their start and end apart: 18, of which 6 were waited for; matrix products, arithmetic and copies ran while one was open for 18% of the time, Pallas kernels for 4%

profile of v9, /device:TPU:0, one launch (start us, length us, event | category | flops | bytes accessed | tf_op | source)
XLA Modules:
  0.0 93.6 jit_solution(9924972884914244044)
XLA Ops:
  4.3 1.2 %shard_map.111 = (bf16[32,16]{1,0:T(8,128)(2,1)S(1)}, bf16[4,16,2048]{2,1,0:T(8,128)(2,1)}, bf16[16,2048]{1,0:T(8,128)(2,1)S(1)}) custom-call(s32[8,16]{1,0:T(8,128)S(1)} %bitcast.25, bf16[8,16]{1,0:T(8,128)(2,1)S(1)} %bitcast.26, s32[1,16]{1,0:T(1,128)S(1)} %bitcast.27, bf16[16,2048]{1,0:T(8,128)(2,1)S(1)} %copy-done.8, bf16[16,2048]{1,0:T(8,128)(2,1)S(1)} %copy-done.9), custom_call_target="tpu_custom_call" | custom-call | bytes 460608 | tf_op jit(solution)/shard_map/pallas_call | solution.py:149
  7.4 6.2 %all-to-all-start = ((bf16[4,16,2048]{2,1,0:T(8,128)(2,1)}), bf16[4,16,2048]{2,1,0:T(8,128)(2,1)}, u32[]{:S(2)}, u32[]{:S(2)}) async-start(bf16[4,16,2048]{2,1,0:T(8,128)(2,1)} %get-tuple-element.34), calls=%async_computation | async-start | bytes 524288 | tf_op jit(solution)/shard_map/all_to_all | solution.py:264
  14.4 8.5 %all-to-all-done = bf16[4,16,2048]{2,1,0:T(8,128)(2,1)} async-done(((bf16[4,16,2048]{2,1,0:T(8,128)(2,1)}), bf16[4,16,2048]{2,1,0:T(8,128)(2,1)}, u32[]{:S(2)}, u32[]{:S(2)}) %all-to-all-start) | async-done | bytes 262176 | tf_op jit(solution)/shard_map/all_to_all | solution.py:264
  24.7 3.5 %all-to-all-start.1 = ((bf16[4,16,2176]{2,1,0:T(8,128)(2,1)}), bf16[4,16,2176]{2,1,0:T(8,128)(2,1)S(1)}, u32[]{:S(2)}, u32[]{:S(2)}) async-start(bf16[4,16,2176]{2,1,0:T(8,128)(2,1)} %shard_map.112), calls=%async_computation.1 | async-start | bytes 557056 | tf_op jit(solution)/shard_map/all_to_all | solution.py:264
  28.2 1.6 %collective-permute-start.3 = (bf16[64,2048]{1,0:T(8,128)(2,1)}, bf16[64,2048]{1,0:T(8,128)(2,1)}, u32[]{:S(2)}, u32[]{:S(2)}) collective-permute-start(bf16[64,2048]{1,0:T(8,128)(2,1)} %bitcast.3.refs_0_), channel_id=1, source_target_pairs={{0,1},{1,0},{2,3},{3,2},{4,5},{5,4},{6,7},{7,6},{8,9},{9,8},{10,11... | collective-permute-start | bytes 786440 | tf_op jit(solution)/shard_map/ppermute | solution.py:137
  29.7 1.5 %collective-permute-start.4 = (bf16[64,2048]{1,0:T(8,128)(2,1)}, bf16[64,2048]{1,0:T(8,128)(2,1)}, u32[]{:S(2)}, u32[]{:S(2)}) collective-permute-start(bf16[64,2048]{1,0:T(8,128)(2,1)} %bitcast.3.refs_0_), channel_id=1, source_target_pairs={{0,2},{1,3},{2,0},{3,1},{4,6},{5,7},{6,4},{7,5},{8,10},{9,11},{10,... | collective-permute-start | bytes 786440 | tf_op jit(solution)/shard_map/ppermute | solution.py:137
  31.3 1.1 %copy-done.2 = bf16[1,192,2048]{2,1,0:T(8,128)(2,1)S(1)} copy-done((bf16[1,192,2048]{2,1,0:T(8,128)(2,1)S(1)}, bf16[1,192,2048]{2,1,0:T(8,128)(2,1)}, u32[]{:S(2)}) %copy-start.2) | copy-done | bytes 786456
  37.0 1.5 %collective-permute-start.8 = (bf16[64,2176]{1,0:T(8,128)(2,1)S(1)}, bf16[64,2176]{1,0:T(8,128)(2,1)S(1)}, u32[]{:S(2)}, u32[]{:S(2)}) collective-permute-start(bf16[64,2176]{1,0:T(8,128)(2,1)S(1)} %bitcast.19), channel_id=1, source_target_pairs={{0,2},{1,3},{2,0},{3,1},{4,6},{5,7},{6,4},{7,5},{8,10},{9,11},{10,... | collective-permute-start | bytes 835592 | tf_op jit(solution)/shard_map/ppermute | solution.py:137
  40.9 1.6 %collective-permute-start.6 = (bf16[32,2048]{1,0:T(8,128)(2,1)S(1)}, bf16[32,2048]{1,0:T(8,128)(2,1)S(1)}, u32[]{:S(2)}, u32[]{:S(2)}) collective-permute-start(bf16[32,2048]{1,0:T(8,128)(2,1)S(1)} %slice.63), channel_id=1, source_target_pairs={{0,1},{1,0},{2,3},{3,2},{4,5},{5,4},{6,7},{7,6},{8,9},{9,8},{10,11... | collective-permute-start | bytes 393224 | tf_op jit(solution)/shard_map/ppermute | solution.py:137
  42.4 6.1 %collective-permute-done.5.refs_3_ = bf16[32,2048]{1,0:T(8,128)(2,1)S(1)} collective-permute-done((bf16[32,2048]{1,0:T(8,128)(2,1)S(1)}, bf16[32,2048]{1,0:T(8,128)(2,1)S(1)}, u32[]{:S(2)}, u32[]{:S(2)}) %collective-permute-start.5) | collective-permute-done | bytes 131104 | tf_op jit(solution)/shard_map/ppermute | solution.py:137
  48.6 1.6 %collective-permute-start.10 = (bf16[32,2176]{1,0:T(8,128)(2,1)S(1)}, bf16[32,2176]{1,0:T(8,128)(2,1)S(1)}, u32[]{:S(2)}, u32[]{:S(2)}) collective-permute-start(bf16[32,2176]{1,0:T(8,128)(2,1)S(1)} %slice.65), channel_id=1, source_target_pairs={{0,1},{1,0},{2,3},{3,2},{4,5},{5,4},{6,7},{7,6},{8,9},{9,8},{10,11... | collective-permute-start | bytes 417800 | tf_op jit(solution)/shard_map/ppermute | solution.py:137
  50.2 1.6 %collective-permute-start.9 = (bf16[32,2176]{1,0:T(8,128)(2,1)S(1)}, bf16[32,2176]{1,0:T(8,128)(2,1)S(1)}, u32[]{:S(2)}, u32[]{:S(2)}) collective-permute-start(bf16[32,2176]{1,0:T(8,128)(2,1)S(1)} %slice.64), channel_id=1, source_target_pairs={{0,2},{1,3},{2,0},{3,1},{4,6},{5,7},{6,4},{7,5},{8,10},{9,11},{10,... | collective-permute-start | bytes 417800 | tf_op jit(solution)/shard_map/ppermute | solution.py:137
  51.8 1.2 %shard_map.114.tokens_ref = bf16[256,2048]{1,0:T(8,128)(2,1)S(1)} custom-call(bf16[64,2048]{1,0:T(8,128)(2,1)} %bitcast.3.refs_0_, bf16[64,2048]{1,0:T(8,128)(2,1)} %collective-permute-done.3.refs_1_, bf16[64,2048]{1,0:T(8,128)(2,1)} %collective-permute-done.4.refs_2_, bf16[32,2048]{1,0:T(8,128)(2,1)S(1)} %collective-permute-done.5.refs_3_, ...), custom_call_target="tpu_custom_call" | custom-call | bytes 2097152 | tf_op jit(solution)/shard_map/pallas_call | solution.py:149
  54.0 1.3 %collective-permute-done.9.refs_3_ = bf16[32,2176]{1,0:T(8,128)(2,1)S(1)} collective-permute-done((bf16[32,2176]{1,0:T(8,128)(2,1)S(1)}, bf16[32,2176]{1,0:T(8,128)(2,1)S(1)}, u32[]{:S(2)}, u32[]{:S(2)}) %collective-permute-start.9) | collective-permute-done | bytes 139296 | tf_op jit(solution)/shard_map/ppermute | solution.py:137
  57.7 2.0 %convolution_convert_fusion = bf16[256,2048]{1,0:T(8,128)(2,1)} fusion(bf16[768,2048]{1,0:T(8,128)(2,1)S(1)} %copy-done.1, bf16[256,384]{1,0:T(8,128)(2,1)S(1)} %get-tuple-element.65, bf16[256,384]{1,0:T(8,128)(2,1)S(1)} %get-tuple-element.64), kind=kOutput, calls=%fused_computation.3 | convolution fusion | flops 806617088 | bytes 4587520 | tf_op jit(solution)/shard_map/dot_general | solution.py:357
  61.2 3.5 %all-to-all-start.2 = ((bf16[4,64,2048]{2,1,0:T(8,128)(2,1)}), bf16[4,64,2048]{2,1,0:T(8,128)(2,1)S(1)}, u32[]{:S(2)}, u32[]{:S(2)}) async-start(bf16[4,64,2048]{2,1,0:T(8,128)(2,1)} %bitcast.28), calls=%async_computation.2 | async-start | bytes 2097152 | tf_op jit(solution)/shard_map/all_to_all | solution.py:264
  64.7 2.5 %fusion.14 = f32[192,2048]{1,0:T(8,128)} fusion(bf16[256,4096]{1,0:T(8,128)(2,1)S(1)} %get-tuple-element.55, bf16[256,384]{1,0:T(8,128)(2,1)} %copy-done.19), kind=kOutput, calls=%fused_computation.16 | convolution fusion | flops 201326592 | bytes 2752512 | tf_op jit(solution)/shard_map/dot_general | solution.py:373
  67.2 1.6 %fusion.19 = f32[192,2048]{1,0:T(8,128)} fusion(bf16[256,4096]{1,0:T(8,128)(2,1)S(1)} %get-tuple-element.55, bf16[256,384]{1,0:T(8,128)(2,1)S(1)} %copy-done.18), kind=kOutput, calls=%fused_computation.21 | convolution fusion | flops 201326592 | bytes 2752512 | tf_op jit(solution)/shard_map/dot_general | solution.py:373
  68.8 1.6 %fusion.21 = f32[192,2048]{1,0:T(8,128)} fusion(bf16[256,4096]{1,0:T(8,128)(2,1)S(1)} %get-tuple-element.55, bf16[256,384]{1,0:T(8,128)(2,1)S(1)} %copy-done.16), kind=kOutput, calls=%fused_computation.23 | convolution fusion | flops 201326592 | bytes 2752512 | tf_op jit(solution)/shard_map/dot_general | solution.py:373
  70.4 8.4 %all-to-all-done.2.blocks_ref = bf16[4,64,2048]{2,1,0:T(8,128)(2,1)S(1)} async-done(((bf16[4,64,2048]{2,1,0:T(8,128)(2,1)}), bf16[4,64,2048]{2,1,0:T(8,128)(2,1)S(1)}, u32[]{:S(2)}, u32[]{:S(2)}) %all-to-all-start.2) | async-done | bytes 1048608 | tf_op jit(solution)/shard_map/all_to_all | solution.py:264
  79.6 5.0 %all-to-all-start.3 = ((bf16[4,16,2048]{2,1,0:T(8,128)(2,1)}), bf16[4,16,2048]{2,1,0:T(8,128)(2,1)S(1)}, u32[]{:S(2)}, u32[]{:S(2)}) async-start(bf16[4,16,2048]{2,1,0:T(8,128)(2,1)} %shard_map.116), calls=%async_computation.3 | async-start | bytes 524288 | tf_op jit(solution)/shard_map/all_to_all | solution.py:264
  84.6 3.1 %fusion.3 = bf16[1,192,2048]{2,1,0:T(8,128)(2,1)} fusion(f32[192,2048]{1,0:T(8,128)} %fusion.14, bf16[256,4096]{1,0:T(8,128)(2,1)} %collective-permute-done.13, bf16[256,576]{1,0:T(8,128)(2,1)S(1)} %collective-permute-done.12), kind=kOutput, calls=%fused_computation.7 | convolution fusion | flops 202113024 | bytes 3538944 | tf_op jit(solution)/shard_map/dot_general | solution.py:374
  87.7 2.7 %fusion.4 = bf16[1,192,2048]{2,1,0:T(8,128)(2,1)} fusion(f32[192,2048]{1,0:T(8,128)S(1)} %copy-done.14, bf16[256,4096]{1,0:T(8,128)(2,1)} %collective-permute-done.13, bf16[256,576]{1,0:T(8,128)(2,1)S(1)} %collective-permute-done.12), kind=kOutput, calls=%fused_computation.8 | convolution fusion | flops 202113024 | bytes 3538944 | tf_op jit(solution)/shard_map/dot_general | solution.py:374
  90.4 2.5 %fusion.5 = bf16[1,192,2048]{2,1,0:T(8,128)(2,1)} fusion(f32[192,2048]{1,0:T(8,128)S(1)} %copy-done.13, bf16[256,4096]{1,0:T(8,128)(2,1)} %collective-permute-done.13, bf16[256,576]{1,0:T(8,128)(2,1)S(1)} %collective-permute-done.12), kind=kOutput, calls=%fused_computation.9 | convolution fusion | flops 202113024 | bytes 3538944 | tf_op jit(solution)/shard_map/dot_general | solution.py:374
  (78 shorter events, 21.5 us)
Async XLA Ops:
  5.5 1.3 %collective-permute-start = (bf16[32,16]{1,0:T(8,128)(2,1)S(1)}, bf16[32,16]{1,0:T(8,128)(2,1)S(1)}, u32[]{:S(2)}, u32[]{:S(2)}) collective-permute-start(bf16[32,16]{1,0:T(8,128)(2,1)S(1)} %get-tuple-element.35.table_ref), channel_id=1, source_target_pairs={{0,16},{16,0},{1,17},{17,1},{2,18},{18,2},{3,19},{19,3},{4,20},{20... | collective-permute-start | bytes 3080 | tf_op jit(solution)/shard_map/ppermute | solution.py:133
  6.9 16.1 %collective-permute-start.1 = (bf16[192,2048]{1,0:T(8,128)(2,1)}, bf16[192,2048]{1,0:T(8,128)(2,1)S(1)}, u32[]{:S(2)}, u32[]{:S(2)}) collective-permute-start(bf16[192,2048]{1,0:T(8,128)(2,1)} %bitcast.21), channel_id=1, source_target_pairs={{0,16},{16,0},{1,17},{17,1},{2,18},{18,2},{3,19},{19,3},{4,20},{20... | collective-permute-start | bytes 2359304 | tf_op jit(solution)/shard_map/ppermute | solution.py:133
  7.2 16.6 %collective-permute-start.2 = (bf16[192,2048]{1,0:T(8,128)(2,1)}, bf16[192,2048]{1,0:T(8,128)(2,1)S(1)}, u32[]{:S(2)}, u32[]{:S(2)}) collective-permute-start(bf16[192,2048]{1,0:T(8,128)(2,1)} %bitcast.23), channel_id=1, source_target_pairs={{0,16},{16,0},{1,17},{17,1},{2,18},{18,2},{3,19},{19,3},{4,20},{20... | collective-permute-start | bytes 2359304 | tf_op jit(solution)/shard_map/ppermute | solution.py:133
  7.4 15.6 %all-to-all-start = ((bf16[4,16,2048]{2,1,0:T(8,128)(2,1)}), bf16[4,16,2048]{2,1,0:T(8,128)(2,1)}, u32[]{:S(2)}, u32[]{:S(2)}) async-start(bf16[4,16,2048]{2,1,0:T(8,128)(2,1)} %get-tuple-element.34), calls=%async_computation | async-start | bytes 524288 | tf_op jit(solution)/shard_map/all_to_all | solution.py:264
  24.7 11.7 %all-to-all-start.1 = ((bf16[4,16,2176]{2,1,0:T(8,128)(2,1)}), bf16[4,16,2176]{2,1,0:T(8,128)(2,1)S(1)}, u32[]{:S(2)}, u32[]{:S(2)}) async-start(bf16[4,16,2176]{2,1,0:T(8,128)(2,1)} %shard_map.112), calls=%async_computation.1 | async-start | bytes 557056 | tf_op jit(solution)/shard_map/all_to_all | solution.py:264
  28.2 7.8 %collective-permute-start.3 = (bf16[64,2048]{1,0:T(8,128)(2,1)}, bf16[64,2048]{1,0:T(8,128)(2,1)}, u32[]{:S(2)}, u32[]{:S(2)}) collective-permute-start(bf16[64,2048]{1,0:T(8,128)(2,1)} %bitcast.3.refs_0_), channel_id=1, source_target_pairs={{0,1},{1,0},{2,3},{3,2},{4,5},{5,4},{6,7},{7,6},{8,9},{9,8},{10,11... | collective-permute-start | bytes 786440 | tf_op jit(solution)/shard_map/ppermute | solution.py:137
  29.7 6.7 %collective-permute-start.4 = (bf16[64,2048]{1,0:T(8,128)(2,1)}, bf16[64,2048]{1,0:T(8,128)(2,1)}, u32[]{:S(2)}, u32[]{:S(2)}) collective-permute-start(bf16[64,2048]{1,0:T(8,128)(2,1)} %bitcast.3.refs_0_), channel_id=1, source_target_pairs={{0,2},{1,3},{2,0},{3,1},{4,6},{5,7},{6,4},{7,5},{8,10},{9,11},{10,... | collective-permute-start | bytes 786440 | tf_op jit(solution)/shard_map/ppermute | solution.py:137
  36.0 18.0 %copy-start = (bf16[768,2048]{1,0:T(8,128)(2,1)}, bf16[768,2048]{1,0:T(8,128)(2,1)S(1)}, u32[]{:S(2)}) copy-start(bf16[768,2048]{1,0:T(8,128)(2,1)S(1)} %shard_map.113) | copy-start | bytes 9437188
  36.4 19.2 %collective-permute-start.11 = (bf16[192,2048]{1,0:T(8,128)(2,1)}, bf16[192,2048]{1,0:T(8,128)(2,1)S(1)}, u32[]{:S(2)}, u32[]{:S(2)}) collective-permute-start(bf16[192,2048]{1,0:T(8,128)(2,1)} %bitcast.29), channel_id=1, source_target_pairs={{0,16},{16,0},{1,17},{17,1},{2,18},{18,2},{3,19},{19,3},{4,20},{20... | collective-permute-start | bytes 2359304 | tf_op jit(solution)/shard_map/ppermute | solution.py:133
  36.4 12.1 %collective-permute-start.7 = (bf16[64,2176]{1,0:T(8,128)(2,1)S(1)}, bf16[64,2176]{1,0:T(8,128)(2,1)S(1)}, u32[]{:S(2)}, u32[]{:S(2)}) collective-permute-start(bf16[64,2176]{1,0:T(8,128)(2,1)S(1)} %bitcast.18), channel_id=1, source_target_pairs={{0,1},{1,0},{2,3},{3,2},{4,5},{5,4},{6,7},{7,6},{8,9},{9,8},{10,11... | collective-permute-start | bytes 835592 | tf_op jit(solution)/shard_map/ppermute | solution.py:137
  37.0 11.6 %collective-permute-start.8 = (bf16[64,2176]{1,0:T(8,128)(2,1)S(1)}, bf16[64,2176]{1,0:T(8,128)(2,1)S(1)}, u32[]{:S(2)}, u32[]{:S(2)}) collective-permute-start(bf16[64,2176]{1,0:T(8,128)(2,1)S(1)} %bitcast.19), channel_id=1, source_target_pairs={{0,2},{1,3},{2,0},{3,1},{4,6},{5,7},{6,4},{7,5},{8,10},{9,11},{10,... | collective-permute-start | bytes 835592 | tf_op jit(solution)/shard_map/ppermute | solution.py:137
  39.4 9.2 %collective-permute-start.5 = (bf16[32,2048]{1,0:T(8,128)(2,1)S(1)}, bf16[32,2048]{1,0:T(8,128)(2,1)S(1)}, u32[]{:S(2)}, u32[]{:S(2)}) collective-permute-start(bf16[32,2048]{1,0:T(8,128)(2,1)S(1)} %slice.62), channel_id=1, source_target_pairs={{0,2},{1,3},{2,0},{3,1},{4,6},{5,7},{6,4},{7,5},{8,10},{9,11},{10,... | collective-permute-start | bytes 393224 | tf_op jit(solution)/shard_map/ppermute | solution.py:137
  40.9 7.7 %collective-permute-start.6 = (bf16[32,2048]{1,0:T(8,128)(2,1)S(1)}, bf16[32,2048]{1,0:T(8,128)(2,1)S(1)}, u32[]{:S(2)}, u32[]{:S(2)}) collective-permute-start(bf16[32,2048]{1,0:T(8,128)(2,1)S(1)} %slice.63), channel_id=1, source_target_pairs={{0,1},{1,0},{2,3},{3,2},{4,5},{5,4},{6,7},{7,6},{8,9},{9,8},{10,11... | collective-permute-start | bytes 393224 | tf_op jit(solution)/shard_map/ppermute | solution.py:137
  48.6 5.4 %collective-permute-start.10 = (bf16[32,2176]{1,0:T(8,128)(2,1)S(1)}, bf16[32,2176]{1,0:T(8,128)(2,1)S(1)}, u32[]{:S(2)}, u32[]{:S(2)}) collective-permute-start(bf16[32,2176]{1,0:T(8,128)(2,1)S(1)} %slice.65), channel_id=1, source_target_pairs={{0,1},{1,0},{2,3},{3,2},{4,5},{5,4},{6,7},{7,6},{8,9},{9,8},{10,11... | collective-permute-start | bytes 417800 | tf_op jit(solution)/shard_map/ppermute | solution.py:137
  50.2 5.1 %collective-permute-start.9 = (bf16[32,2176]{1,0:T(8,128)(2,1)S(1)}, bf16[32,2176]{1,0:T(8,128)(2,1)S(1)}, u32[]{:S(2)}, u32[]{:S(2)}) collective-permute-start(bf16[32,2176]{1,0:T(8,128)(2,1)S(1)} %slice.64), channel_id=1, source_target_pairs={{0,2},{1,3},{2,0},{3,1},{4,6},{5,7},{6,4},{7,5},{8,10},{9,11},{10,... | collective-permute-start | bytes 417800 | tf_op jit(solution)/shard_map/ppermute | solution.py:137
  56.4 3.3 %copy-start.15 = (bf16[256,384]{1,0:T(8,128)(2,1)}, bf16[256,384]{1,0:T(8,128)(2,1)S(1)}, u32[]{:S(2)}) copy-start(bf16[256,384]{1,0:T(8,128)(2,1)S(1)} %get-tuple-element.64) | copy-start | bytes 589828
  56.5 3.3 %copy-start.17 = (bf16[256,384]{1,0:T(8,128)(2,1)}, bf16[256,384]{1,0:T(8,128)(2,1)S(1)}, u32[]{:S(2)}) copy-start(bf16[256,384]{1,0:T(8,128)(2,1)S(1)} %get-tuple-element.65) | copy-start | bytes 589828
  56.5 4.2 %copy-start.19 = (bf16[256,384]{1,0:T(8,128)(2,1)}, bf16[256,384]{1,0:T(8,128)(2,1)S(1)}, u32[]{:S(2)}) copy-start(bf16[256,384]{1,0:T(8,128)(2,1)S(1)} %get-tuple-element.66) | copy-start | bytes 589828
  60.7 23.9 %collective-permute-start.13 = (bf16[256,4096]{1,0:T(8,128)(2,1)S(1)}, bf16[256,4096]{1,0:T(8,128)(2,1)}, u32[]{:S(2)}, u32[]{:S(2)}) collective-permute-start(bf16[256,4096]{1,0:T(8,128)(2,1)S(1)} %get-tuple-element.55), channel_id=1, source_target_pairs={{0,16},{16,0},{1,17},{17,1},{2,18},{18,2},{3,19},{19,3},{4,20},{20... | collective-permute-start | bytes 6291464 | tf_op jit(solution)/shard_map/ppermute | solution.py:133
  60.7 18.9 %collective-permute-start.12 = (bf16[256,576]{1,0:T(8,128)(2,1)}, bf16[256,576]{1,0:T(8,128)(2,1)S(1)}, u32[]{:S(2)}, u32[]{:S(2)}) collective-permute-start(bf16[256,576]{1,0:T(8,128)(2,1)} %pad_maximum_fusion), channel_id=1, source_target_pairs={{0,16},{16,0},{1,17},{17,1},{2,18},{18,2},{3,19},{19,3},{4,20},{20... | collective-permute-start | bytes 884744 | tf_op jit(solution)/shard_map/ppermute | solution.py:133
  61.2 17.6 %all-to-all-start.2 = ((bf16[4,64,2048]{2,1,0:T(8,128)(2,1)}), bf16[4,64,2048]{2,1,0:T(8,128)(2,1)S(1)}, u32[]{:S(2)}, u32[]{:S(2)}) async-start(bf16[4,64,2048]{2,1,0:T(8,128)(2,1)} %bitcast.28), calls=%async_computation.2 | async-start | bytes 2097152 | tf_op jit(solution)/shard_map/all_to_all | solution.py:264
  64.7 4.1 %copy-start.16 = (bf16[256,384]{1,0:T(8,128)(2,1)S(1)}, bf16[256,384]{1,0:T(8,128)(2,1)}, u32[]{:S(2)}) copy-start(bf16[256,384]{1,0:T(8,128)(2,1)} %copy-done.15) | copy-start | bytes 589828
  79.6 13.4 %all-to-all-start.3 = ((bf16[4,16,2048]{2,1,0:T(8,128)(2,1)}), bf16[4,16,2048]{2,1,0:T(8,128)(2,1)S(1)}, u32[]{:S(2)}, u32[]{:S(2)}) async-start(bf16[4,16,2048]{2,1,0:T(8,128)(2,1)} %shard_map.116), calls=%async_computation.3 | async-start | bytes 524288 | tf_op jit(solution)/shard_map/all_to_all | solution.py:264
  84.6 3.1 %copy-start.14 = (f32[192,2048]{1,0:T(8,128)S(1)}, f32[192,2048]{1,0:T(8,128)}, u32[]{:S(2)}) copy-start(f32[192,2048]{1,0:T(8,128)} %fusion.19) | copy-start | bytes 4718596
  (15 other events, 19.0 us)

commit v10 on v3

--- a/solution.py
+++ b/solution.py
@@ -3,6 +3,8 @@
 import jax
 import jax.numpy as jnp
 from jax import lax
+from jax.experimental import pallas as pl
+from jax.experimental.pallas import tpu as pltpu
 from jax.sharding import PartitionSpec as P
 
 
@@ -141,18 +143,77 @@
     return lax.ppermute(value, "expert", [(place, place ^ partner) for place in range(count)])
 
 
-def home_gates(packing, expert_ids, gate_values, count):
-    row_count = packing.shape[0]
-    labels = jnp.arange(count, dtype=jnp.int32)
-    named = expert_ids[:, :, None] == labels[None, None, :]
-    by_slot = jnp.sum(jnp.where(named, gate_values.astype(jnp.float32)[:, :, None], 0.0), axis=1)
-    own_homes = lax.axis_index("dp") * row_count + jnp.arange(row_count, dtype=jnp.int32)
-    routing = jnp.concatenate(
-        [packing[:, None].astype(jnp.bfloat16), by_slot.astype(jnp.bfloat16)], axis=1
-    )
-    routing = jnp.concatenate([routing, swap(routing)], axis=0).astype(jnp.float32)
-    matched = own_homes[:, None] == routing[:, 0].astype(jnp.int32)[None, :]
-    return jnp.sum(jnp.where(matched[:, :, None], routing[None, :, 1:], 0.0), axis=1)
+VMEM = pl.BlockSpec(memory_space=pltpu.VMEM)
+ANY = pl.BlockSpec(memory_space=pl.ANY)
+NT = (((1,), (1,)), ((), ()))
+
+
+def on_chip(body, outs, *args, scratch=(), spec=VMEM, limit=True):
+    moved = sum(arg.size * arg.dtype.itemsize for arg in args)
+    moved += sum(math.prod(shape) * jnp.dtype(dtype).itemsize for shape, dtype in outs)
+    granted = {"vmem_limit_bytes": moved + (4 << 20)} if limit else {}
+    return pl.pallas_call(
+        body,
+        out_shape=[jax.ShapeDtypeStruct(shape, dtype) for shape, dtype in outs],
+        in_specs=[spec] * len(args),
+        out_specs=[VMEM] * len(outs),
+        scratch_shapes=list(scratch),
+        compiler_params=pltpu.CompilerParams(**granted),
+        cost_estimate=pl.CostEstimate(flops=0, bytes_accessed=moved, transcendentals=0),
+    )(*args)
+
+
+def read_kernel(
+    ids_hbm, gates_hbm, packing_hbm, tokens_hbm, cotangent_hbm, gate_hbm, up_hbm, down_hbm,
+    table_ref, tokens_ref, cotangent_ref, weights_ref,
+    ids_ref, gates_ref, packing_ref, ready,
+):
+    half = gate_hbm.shape[1]
+    pairs = [
+        (ids_hbm, ids_ref),
+        (gates_hbm, gates_ref),
+        (packing_hbm, packing_ref),
+        (tokens_hbm, tokens_ref),
+        (cotangent_hbm, cotangent_ref),
+    ]
+    for index, source in enumerate((gate_hbm, up_hbm, down_hbm)):
+        pairs.append((source.at[0], weights_ref.at[index * half : (index + 1) * half]))
+    copies = [
+        pltpu.make_async_copy(source, target, ready.at[index])
+        for index, (source, target) in enumerate(pairs)
+    ]
+    for copy in copies:
+        copy.start()
+    for copy in copies:
+        copy.wait()
+    slots = packing_ref.shape[1]
+    count = table_ref.shape[0] - 16
+    labels = lax.broadcasted_iota(jnp.int32, (count, slots), 0)
+    total = jnp.zeros((count, slots), jnp.float32)
+    for k in range(ids_ref.shape[0]):
+        named = labels == ids_ref[k : k + 1, :]
+        total = total + jnp.where(named, gates_ref[k : k + 1, :].astype(jnp.float32), 0.0)
+    table_ref[:count, :] = total.astype(jnp.bfloat16)
+    lists = jnp.broadcast_to(packing_ref[...], (16, slots)).astype(jnp.float32)
+    table_ref[count:, :] = lists.astype(jnp.bfloat16)
+
+
+def payload_kernel(table_ref, other_ref, cotangent_ref, payload_ref, here_ref):
+    rows, width = cotangent_ref.shape
+    count = table_ref.shape[0] - 16
+    slots = table_ref.shape[1]
+    homes = lax.broadcasted_iota(jnp.int32, (rows, slots), 0) + lax.axis_index("dp") * rows
+    gates = jnp.zeros((rows, count), jnp.float32)
+    for ref in (table_ref, other_ref):
+        lists = ref[count:, :].astype(jnp.float32)[:1, :]
+        matched = (lists == homes.astype(jnp.float32)).astype(jnp.float32).astype(jnp.bfloat16)
+        gates = gates + lax.dot_general(
+            matched, ref[:count, :], NT, preferred_element_type=jnp.float32
+        )
+    payload_ref[:, :width] = cotangent_ref[...]
+    payload_ref[:, width:] = gates.astype(jnp.bfloat16)
+    lanes = lax.broadcasted_iota(jnp.int32, here_ref.shape, 1)
+    here_ref[...] = (lanes == lax.axis_index("expert")).astype(jnp.float32)
 
 
 def along_outer(value, count, inner):
@@ -170,13 +231,17 @@
     return [column, first, second, far_top, far_bottom]
 
 
-def bring_back(value, count, inner):
-    outer = count // inner
+def return_inner(value, count, inner):
     blocks = value.reshape(inner, -1, value.shape[-1])
     total = blocks[0].astype(jnp.float32)
     for partner in range(1, inner):
         total = total + swap_inner(blocks[partner], count, partner).astype(jnp.float32)
-    blocks = total.reshape(outer, -1, value.shape[-1])
+    return total
+
+
+def return_outer(value, count, inner):
+    outer = count // inner
+    blocks = value.reshape(outer, -1, value.shape[-1])
     rounded = blocks.astype(jnp.bfloat16)
     total = blocks[0]
     for step in range(1, outer):
@@ -188,25 +253,58 @@
     model_width = tokens.shape[1]
     half = w_gate.shape[1]
     count = lax.axis_size("expert")
-    inner = math.gcd(count, 4)
-    token_column = jnp.concatenate(along_outer(tokens, count, inner), axis=0)
-    other = swap(jnp.concatenate([w_gate[0], w_up[0], w_down[0]], axis=0))
-    gates = home_gates(packing, expert_ids, gate_values, count).astype(jnp.bfloat16)
-    payload = jnp.concatenate([cotangent, gates], axis=1)
+    inner = 4
+    row_count = tokens.shape[0]
+    low = jnp.bfloat16
+    ids, gates, lists = expert_ids.T, gate_values.T, packing.reshape(1, row_count)
+    table, own_tokens, own_cotangent, own_weights = on_chip(
+        read_kernel,
+        [
+            ((count + 16, row_count), low),
+            (tokens.shape, low),
+            (cotangent.shape, low),
+            ((3 * half, model_width), low),
+        ],
+        ids,
+        gates,
+        lists,
+        tokens,
+        cotangent,
+        w_gate,
+        w_up,
+        w_down,
+        spec=ANY,
+        limit=False,
+        scratch=[
+            pltpu.VMEM(ids.shape, ids.dtype),
+            pltpu.VMEM(gates.shape, gates.dtype),
+            pltpu.VMEM(lists.shape, lists.dtype),
+            pltpu.SemaphoreType.DMA((8,)),
+        ],
+    )
+    token_column = jnp.concatenate(along_outer(own_tokens, count, inner), axis=0)
+    other = swap(own_weights)
+    payload, here = on_chip(
+        payload_kernel,
+        [((row_count, model_width + count), low), ((8, count), jnp.float32)],
+        table,
+        swap(table),
+        own_cotangent,
+    )
     payload, token_column, other = lax.optimization_barrier((payload, token_column, other))
     upstream_column = jnp.concatenate(along_outer(payload, count, inner), axis=0)
     inputs = jnp.concatenate(across_inner(token_column, count, inner), axis=0)
     other_inputs = swap(inputs)
     upstream = jnp.concatenate(across_inner(upstream_column, count, inner), axis=0)
-    here = jnp.arange(count, dtype=jnp.int32) == lax.axis_index("expert")
     gate = jnp.sum(
-        jnp.where(here[None, :], upstream[:, model_width:].astype(jnp.float32), 0.0),
-        axis=1,
-        keepdims=True,
+        upstream[:, model_width:].astype(jnp.float32) * here[:1], axis=1, keepdims=True
     )
     upstream = upstream[:, :model_width]
-    gate_up = jnp.concatenate([w_gate[0], other[:half], w_up[0], other[half : 2 * half]], axis=0)
-    down = jnp.concatenate([w_down[0], other[2 * half :]], axis=0)
+    gate_up = jnp.concatenate(
+        [own_weights[:half], other[:half], own_weights[half : 2 * half], other[half : 2 * half]],
+        axis=0,
+    )
+    down = jnp.concatenate([own_weights[2 * half :], other[2 * half :]], axis=0)
     pre = jnp.dot(inputs, gate_up.T, preferred_element_type=jnp.float32)
     gate_pre, up_pre = pre[:, : 2 * half], pre[:, 2 * half :]
     hidden_grad = gate * jnp.dot(upstream, down.T, preferred_element_type=jnp.float32)
@@ -219,13 +317,17 @@
     both_grad = jnp.concatenate([gate_grad, up_grad], axis=1)
     partial_grad = jnp.dot(both_grad, gate_up, preferred_element_type=jnp.float32)
     partial_grad = partial_grad.astype(jnp.bfloat16)
-    input_grad = bring_back(partial_grad, count, inner)
+    column_sum = return_inner(partial_grad, count, inner)
     grads = (gate_grad, up_grad, hidden)
     own_grads = jnp.concatenate([grad[:, :half] for grad in grads], axis=1)
     sent_grads = jnp.concatenate([grad[:, half:] for grad in grads], axis=1)
     sent_grads, upstream, _ = lax.optimization_barrier((sent_grads, upstream, partial_grad))
     other_grads = swap(sent_grads)
     other_upstream = swap(upstream)
+    column_sum, other_grads, other_inputs = lax.optimization_barrier(
+        (column_sum, other_grads, other_inputs)
+    )
+    input_grad = return_outer(column_sum, count, inner)
     weight_grads = []
     for index, (rows, other_rows) in enumerate(
         ((inputs, other_inputs), (inputs, other_inputs), (upstream, other_upstream))
@@ -242,10 +344,12 @@
 
 def local(tokens, cotangent, gate_values, expert_ids, packing, w_gate, w_up, w_down):
     row_count, top = expert_ids.shape
-    expert_count = lax.axis_size("expert") * w_gate.shape[0]
+    count = lax.axis_size("expert")
+    expert_count = count * w_gate.shape[0]
     capacity = min(row_count, max(2, row_count * top // expert_count + 1))
     few = capacity * 4 <= row_count
-    chosen = routed_local if few else dense_local
+    regular = lax.axis_size("dp") == 2 and count % 4 == 0 and w_gate.shape[0] == 1
+    chosen = dense_local if regular and not few else routed_local
     return chosen(
         tokens, cotangent, gate_values, expert_ids, packing, w_gate, w_up, w_down
     )

time: 71 us -> 70.8 us (level)
  other arithmetic: 5.04 us -> 1.07 us
  Pallas kernels: 0 us -> 3.39 us
  local copies, waits for them, and re-layouts: 1.48 us -> 2.86 us
    concatenate x4 -> x1, other arithmetic: 3.49 us -> 0.02 us  [dense_local(): jnp.concatenate(along_outer(own_tokens, count, inner), axis=0)]
    pallas_call x0 -> x2, Pallas kernels: none -> 3.39 us  [on_chip(): pl.pallas_call(body, out_shape=[jax.ShapeDtypeStruct(shape, dtype) for sh...]
    slice x5 -> x4, local copies, waits for them, and re-layouts: 0.49 us -> 2.15 us  [the longest x2 2.08 us: dense_local(): down = jnp.concatenate([own_weights[2 * half:], other[2 * half:]], axis=0)]
    ppermute x11, waiting for transfers between devices: 15.4 us -> 16.5 us  [swap_inner(): lax.ppermute(value, 'expert', [(place, place ^ partner) for place in rang...]
    ppermute x5, waiting for transfers between devices: 1.14 us -> 0.01 us  [swap(): return lax.ppermute(value, 'dp', [(0, 1), (1, 0)])]
  transfers between devices with their start and end apart: 25 -> 25, of which waited for: 16 -> 16; matrix products, arithmetic and copies ran while one was open for 11% -> 15% of each run, Pallas kernels for 0% -> 0%
where the time goes in v10:
time: 70.8 us; the launch traced here: 70.6 us
  starting transfers between devices  30.1 us (43%)
  waiting for transfers between devices  24.1 us (34%)
  matrix products  8.18 us (12%)
  Pallas kernels  3.39 us (5%)
  local copies, waits for them, and re-layouts  2.86 us (4%)
  other arithmetic  1.07 us (2%)
  between operations  0.91 us (1%)
    ppermute x11, waiting for transfers between devices, swap_inner(): lax.ppermute(value, 'expert', [(place, place ^ partner) for place in rang...  16.5 us
    ppermute x11, starting transfers between devices, swap_inner(): lax.ppermute(value, 'expert', [(place, place ^ partner) for place in rang...  15.5 us
    ppermute x9, starting transfers between devices, shift_outer(): lax.ppermute(value, 'expert', [(place, (place + step * inner) % count) fo...  14 us
    ppermute x9, waiting for transfers between devices, shift_outer(): lax.ppermute(value, 'expert', [(place, (place + step * inner) % count) fo...  7.55 us
    pallas_call x2, Pallas kernels, on_chip(): pl.pallas_call(body, out_shape=[jax.ShapeDtypeStruct(shape, dtype) for sh...  3.39 us
    dot_general x3, matrix products, dense_local(): jnp.dot(own_grads[:, low:low + half].T, rows, preferred_element_type=jnp....  2.99 us
    dot_general x3, matrix products, dense_local(): jnp.dot(other_grads[:, low:low + half].T, other_rows, preferred_element_t...  2.18 us
    slice x2, local copies, waits for them, and re-layouts, dense_local(): down = jnp.concatenate([own_weights[2 * half:], other[2 * half:]], axis=0)  2.08 us
  transfers between devices with their start and end apart: 25, of which 16 were waited for; matrix products, arithmetic and copies ran while one was open for 15% of the time, Pallas kernels for 0%

profile of v10, /device:TPU:0, one launch (start us, length us, event | category | flops | bytes accessed | tf_op | source)
XLA Modules:
  0.0 70.6 jit_solution(7709753325614026015)
XLA Ops:
  0.6 3.3 %shard_map.111 = (bf16[32,16]{1,0:T(8,128)(2,1)}, bf16[16,2048]{1,0:T(8,128)(2,1)}, bf16[16,2048]{1,0:T(8,128)(2,1)}, bf16[576,2048]{1,0:T(8,128)(2,1)}) custom-call(s32[8,16]{1,0:T(8,128)} %bitcast.18, bf16[8,16]{1,0:T(8,128)(2,1)} %bitcast.19, s32[1,16]{1,0:T(1,128)} %bitcast.20, bf16[16,2048]{1,0:T(8,128)(2,1)} %tokens_hbm.1, ...), custom_call_target="tpu_custom_call" | custom-call | bytes 4982592 | tf_op jit(solution)/shard_map/pallas_call | solution.py:155
  4.4 2.6 %collective-permute-start.1 = (bf16[16,2048]{1,0:T(8,128)(2,1)}, bf16[16,2048]{1,0:T(8,128)(2,1)S(1)}, u32[]{:S(2)}, u32[]{:S(2)}) collective-permute-start(bf16[16,2048]{1,0:T(8,128)(2,1)} %get-tuple-element.21), channel_id=1, source_target_pairs={{0,4},{1,5},{2,6},{3,7},{4,8},{5,9},{6,10},{7,11},{8,12},{9,13},{1... | collective-permute-start | bytes 196616 | tf_op jit(solution)/shard_map/ppermute | solution.py:137
  7.1 2.6 %collective-permute-start.2 = (bf16[16,2048]{1,0:T(8,128)(2,1)}, bf16[16,2048]{1,0:T(8,128)(2,1)S(1)}, u32[]{:S(2)}, u32[]{:S(2)}) collective-permute-start(bf16[16,2048]{1,0:T(8,128)(2,1)} %get-tuple-element.21), channel_id=1, source_target_pairs={{0,8},{1,9},{2,10},{3,11},{4,12},{5,13},{6,14},{7,15},{8,0},{9,1},... | collective-permute-start | bytes 196616 | tf_op jit(solution)/shard_map/ppermute | solution.py:137
  9.6 1.3 %collective-permute-start.3 = (bf16[16,2048]{1,0:T(8,128)(2,1)}, bf16[16,2048]{1,0:T(8,128)(2,1)S(1)}, u32[]{:S(2)}, u32[]{:S(2)}) collective-permute-start(bf16[16,2048]{1,0:T(8,128)(2,1)} %get-tuple-element.21), channel_id=1, source_target_pairs={{0,12},{1,13},{2,14},{3,15},{4,0},{5,1},{6,2},{7,3},{8,4},{9,5},{1... | collective-permute-start | bytes 196616 | tf_op jit(solution)/shard_map/ppermute | solution.py:137
  11.0 1.8 %fusion.31 = (bf16[192,2048]{1,0:T(8,128)(2,1)S(1)}, bf16[192,2048]{1,0:T(8,128)(2,1)S(1)}, bf16[192,2048]{1,0:T(8,128)(2,1)S(1)}) fusion(bf16[576,2048]{1,0:T(8,128)(2,1)} %get-tuple-element.22), kind=kLoop, calls=%fused_computation.61 | loop fusion | bytes 4718592 | tf_op jit(solution)/shard_map/slice | solution.py:307
  13.0 1.9 %collective-permute-done.2 = bf16[16,2048]{1,0:T(8,128)(2,1)S(1)} collective-permute-done((bf16[16,2048]{1,0:T(8,128)(2,1)}, bf16[16,2048]{1,0:T(8,128)(2,1)S(1)}, u32[]{:S(2)}, u32[]{:S(2)}) %collective-permute-start.2) | collective-permute-done | bytes 65568 | tf_op jit(solution)/shard_map/ppermute | solution.py:137
  15.2 1.7 %collective-permute-start.5 = (bf16[16,2064]{1,0:T(8,128)(2,1)S(1)}, bf16[16,2064]{1,0:T(8,128)(2,1)S(1)}, u32[]{:S(2)}, u32[]{:S(2)}) collective-permute-start(bf16[16,2064]{1,0:T(8,128)(2,1)S(1)} %get-tuple-element.23), channel_id=1, source_target_pairs={{0,4},{1,5},{2,6},{3,7},{4,8},{5,9},{6,10},{7,11},{8,12},{9,13},{1... | collective-permute-start | bytes 198152 | tf_op jit(solution)/shard_map/ppermute | solution.py:137
  16.9 1.6 %collective-permute-start.6 = (bf16[16,2064]{1,0:T(8,128)(2,1)S(1)}, bf16[16,2064]{1,0:T(8,128)(2,1)S(1)}, u32[]{:S(2)}, u32[]{:S(2)}) collective-permute-start(bf16[16,2064]{1,0:T(8,128)(2,1)S(1)} %get-tuple-element.23), channel_id=1, source_target_pairs={{0,8},{1,9},{2,10},{3,11},{4,12},{5,13},{6,14},{7,15},{8,0},{9,1},... | collective-permute-start | bytes 198152 | tf_op jit(solution)/shard_map/ppermute | solution.py:137
  19.3 1.5 %collective-permute-start.12 = (bf16[64,2048]{1,0:T(8,128)(2,1)S(1)}, bf16[64,2048]{1,0:T(8,128)(2,1)S(1)}, u32[]{:S(2)}, u32[]{:S(2)}) collective-permute-start(bf16[64,2048]{1,0:T(8,128)(2,1)S(1)} %pad_maximum_fusion.4), channel_id=1, source_target_pairs={{0,1},{1,0},{2,3},{3,2},{4,5},{5,4},{6,7},{7,6},{8,9},{9,8},{10,11... | collective-permute-start | bytes 786440 | tf_op jit(solution)/shard_map/ppermute | solution.py:143
  21.1 1.6 %collective-permute-start.13 = (bf16[64,2048]{1,0:T(8,128)(2,1)S(1)}, bf16[64,2048]{1,0:T(8,128)(2,1)S(1)}, u32[]{:S(2)}, u32[]{:S(2)}) collective-permute-start(bf16[64,2048]{1,0:T(8,128)(2,1)S(1)} %pad_maximum_fusion.4), channel_id=1, source_target_pairs={{0,2},{1,3},{2,0},{3,1},{4,6},{5,7},{6,4},{7,5},{8,10},{9,11},{10,... | collective-permute-start | bytes 786440 | tf_op jit(solution)/shard_map/ppermute | solution.py:143
  24.0 1.6 %collective-permute-start.8 = (bf16[64,2064]{1,0:T(8,128)(2,1)S(1)}, bf16[64,2064]{1,0:T(8,128)(2,1)S(1)}, u32[]{:S(2)}, u32[]{:S(2)}) collective-permute-start(bf16[64,2064]{1,0:T(8,128)(2,1)S(1)} %get-tuple-element.47), channel_id=1, source_target_pairs={{0,1},{1,0},{2,3},{3,2},{4,5},{5,4},{6,7},{7,6},{8,9},{9,8},{10,11... | collective-permute-start | bytes 792584 | tf_op jit(solution)/shard_map/ppermute | solution.py:143
  25.6 1.5 %collective-permute-start.9 = (bf16[64,2064]{1,0:T(8,128)(2,1)S(1)}, bf16[64,2064]{1,0:T(8,128)(2,1)S(1)}, u32[]{:S(2)}, u32[]{:S(2)}) collective-permute-start(bf16[64,2064]{1,0:T(8,128)(2,1)S(1)} %get-tuple-element.47), channel_id=1, source_target_pairs={{0,2},{1,3},{2,0},{3,1},{4,6},{5,7},{6,4},{7,5},{8,10},{9,11},{10,... | collective-permute-start | bytes 792584 | tf_op jit(solution)/shard_map/ppermute | solution.py:143
  27.4 1.6 %collective-permute-start.14 = (bf16[32,2048]{1,0:T(8,128)(2,1)S(1)}, bf16[32,2048]{1,0:T(8,128)(2,1)S(1)}, u32[]{:S(2)}, u32[]{:S(2)}) collective-permute-start(bf16[32,2048]{1,0:T(8,128)(2,1)S(1)} %slice.140), channel_id=1, source_target_pairs={{0,2},{1,3},{2,0},{3,1},{4,6},{5,7},{6,4},{7,5},{8,10},{9,11},{10,... | collective-permute-start | bytes 393224 | tf_op jit(solution)/shard_map/ppermute | solution.py:143
  30.6 3.0 %collective-permute-done.8 = bf16[64,2064]{1,0:T(8,128)(2,1)S(1)} collective-permute-done((bf16[64,2064]{1,0:T(8,128)(2,1)S(1)}, bf16[64,2064]{1,0:T(8,128)(2,1)S(1)}, u32[]{:S(2)}, u32[]{:S(2)}) %collective-permute-start.8) | collective-permute-done | bytes 264224 | tf_op jit(solution)/shard_map/ppermute | solution.py:143
  33.6 1.6 %collective-permute-start.10 = (bf16[32,2064]{1,0:T(8,128)(2,1)S(1)}, bf16[32,2064]{1,0:T(8,128)(2,1)S(1)}, u32[]{:S(2)}, u32[]{:S(2)}) collective-permute-start(bf16[32,2064]{1,0:T(8,128)(2,1)S(1)} %slice.136), channel_id=1, source_target_pairs={{0,2},{1,3},{2,0},{3,1},{4,6},{5,7},{6,4},{7,5},{8,10},{9,11},{10,... | collective-permute-start | bytes 396296 | tf_op jit(solution)/shard_map/ppermute | solution.py:143
  35.4 1.4 %collective-permute-start.11 = (bf16[32,2064]{1,0:T(8,128)(2,1)S(1)}, bf16[32,2064]{1,0:T(8,128)(2,1)S(1)}, u32[]{:S(2)}, u32[]{:S(2)}) collective-permute-start(bf16[32,2064]{1,0:T(8,128)(2,1)S(1)} %slice.137), channel_id=1, source_target_pairs={{0,1},{1,0},{2,3},{3,2},{4,5},{5,4},{6,7},{7,6},{8,9},{9,8},{10,11... | collective-permute-start | bytes 396296 | tf_op jit(solution)/shard_map/ppermute | solution.py:143
  43.3 1.4 %collective-permute-start.16 = (bf16[64,2048]{1,0:T(8,128)(2,1)S(1)}, bf16[64,2048]{1,0:T(8,128)(2,1)S(1)}, u32[]{:S(2)}, u32[]{:S(2)}) collective-permute-start(bf16[64,2048]{1,0:T(8,128)(2,1)S(1)} %get-tuple-element.40), channel_id=1, source_target_pairs={{0,1},{1,0},{2,3},{3,2},{4,5},{5,4},{6,7},{7,6},{8,9},{9,8},{10,11... | collective-permute-start | bytes 786440 | tf_op jit(solution)/shard_map/ppermute | solution.py:143
  45.4 1.4 %collective-permute-start.18 = (bf16[64,2048]{1,0:T(8,128)(2,1)S(1)}, bf16[64,2048]{1,0:T(8,128)(2,1)S(1)}, u32[]{:S(2)}, u32[]{:S(2)}) collective-permute-start(bf16[64,2048]{1,0:T(8,128)(2,1)S(1)} %get-tuple-element.41), channel_id=1, source_target_pairs={{0,3},{1,2},{2,1},{3,0},{4,7},{5,6},{6,5},{7,4},{8,11},{9,10},{10,... | collective-permute-start | bytes 786440 | tf_op jit(solution)/shard_map/ppermute | solution.py:143
  47.2 5.3 %collective-permute-done.16 = bf16[64,2048]{1,0:T(8,128)(2,1)S(1)} collective-permute-done((bf16[64,2048]{1,0:T(8,128)(2,1)S(1)}, bf16[64,2048]{1,0:T(8,128)(2,1)S(1)}, u32[]{:S(2)}, u32[]{:S(2)}) %collective-permute-start.16) | collective-permute-done | bytes 262176 | tf_op jit(solution)/shard_map/ppermute | solution.py:143
  52.6 3.3 %collective-permute-done.17 = bf16[64,2048]{1,0:T(8,128)(2,1)S(1)} collective-permute-done((bf16[64,2048]{1,0:T(8,128)(2,1)S(1)}, bf16[64,2048]{1,0:T(8,128)(2,1)S(1)}, u32[]{:S(2)}, u32[]{:S(2)}) %collective-permute-start.17) | collective-permute-done | bytes 262176 | tf_op jit(solution)/shard_map/ppermute | solution.py:143
  55.9 1.6 %collective-permute-done.18 = bf16[64,2048]{1,0:T(8,128)(2,1)S(1)} collective-permute-done((bf16[64,2048]{1,0:T(8,128)(2,1)S(1)}, bf16[64,2048]{1,0:T(8,128)(2,1)S(1)}, u32[]{:S(2)}, u32[]{:S(2)}) %collective-permute-start.18) | collective-permute-done | bytes 262176 | tf_op jit(solution)/shard_map/ppermute | solution.py:143
  59.5 2.4 %collective-permute-start.21 = (bf16[16,2048]{1,0:T(8,128)(2,1)S(1)}, bf16[16,2048]{1,0:T(8,128)(2,1)S(1)}, u32[]{:S(2)}, u32[]{:S(2)}) collective-permute-start(bf16[16,2048]{1,0:T(8,128)(2,1)S(1)} %get-tuple-element.44), channel_id=1, source_target_pairs={{0,12},{1,13},{2,14},{3,15},{4,0},{5,1},{6,2},{7,3},{8,4},{9,5},{1... | collective-permute-start | bytes 196616 | tf_op jit(solution)/shard_map/ppermute | solution.py:137
  64.5 2.5 %collective-permute-done.22 = bf16[16,2048]{1,0:T(8,128)(2,1)S(1)} collective-permute-done((bf16[16,2048]{1,0:T(8,128)(2,1)S(1)}, bf16[16,2048]{1,0:T(8,128)(2,1)S(1)}, u32[]{:S(2)}, u32[]{:S(2)}) %collective-permute-start.22) | collective-permute-done | bytes 65568 | tf_op jit(solution)/shard_map/ppermute | solution.py:137
  67.0 1.6 %collective-permute-done.23 = bf16[16,2048]{1,0:T(8,128)(2,1)S(1)} collective-permute-done((bf16[16,2048]{1,0:T(8,128)(2,1)S(1)}, bf16[16,2048]{1,0:T(8,128)(2,1)S(1)}, u32[]{:S(2)}, u32[]{:S(2)}) %collective-permute-start.23) | collective-permute-done | bytes 65568 | tf_op jit(solution)/shard_map/ppermute | solution.py:137
  (75 shorter events, 19.5 us)
Async XLA Ops:
  3.9 11.3 %collective-permute-start.4 = (bf16[576,2048]{1,0:T(8,128)(2,1)}, bf16[576,2048]{1,0:T(8,128)(2,1)S(1)}, u32[]{:S(2)}, u32[]{:S(2)}) collective-permute-start(bf16[576,2048]{1,0:T(8,128)(2,1)} %get-tuple-element.22), channel_id=1, source_target_pairs={{0,16},{16,0},{1,17},{17,1},{2,18},{18,2},{3,19},{19,3},{4,20},{20... | collective-permute-start | bytes 7077896 | tf_op jit(solution)/shard_map/ppermute | solution.py:133
  4.4 8.6 %collective-permute-start.1 = (bf16[16,2048]{1,0:T(8,128)(2,1)}, bf16[16,2048]{1,0:T(8,128)(2,1)S(1)}, u32[]{:S(2)}, u32[]{:S(2)}) collective-permute-start(bf16[16,2048]{1,0:T(8,128)(2,1)} %get-tuple-element.21), channel_id=1, source_target_pairs={{0,4},{1,5},{2,6},{3,7},{4,8},{5,9},{6,10},{7,11},{8,12},{9,13},{1... | collective-permute-start | bytes 196616 | tf_op jit(solution)/shard_map/ppermute | solution.py:137
  7.1 7.8 %collective-permute-start.2 = (bf16[16,2048]{1,0:T(8,128)(2,1)}, bf16[16,2048]{1,0:T(8,128)(2,1)S(1)}, u32[]{:S(2)}, u32[]{:S(2)}) collective-permute-start(bf16[16,2048]{1,0:T(8,128)(2,1)} %get-tuple-element.21), channel_id=1, source_target_pairs={{0,8},{1,9},{2,10},{3,11},{4,12},{5,13},{6,14},{7,15},{8,0},{9,1},... | collective-permute-start | bytes 196616 | tf_op jit(solution)/shard_map/ppermute | solution.py:137
  9.6 5.5 %collective-permute-start.3 = (bf16[16,2048]{1,0:T(8,128)(2,1)}, bf16[16,2048]{1,0:T(8,128)(2,1)S(1)}, u32[]{:S(2)}, u32[]{:S(2)}) collective-permute-start(bf16[16,2048]{1,0:T(8,128)(2,1)} %get-tuple-element.21), channel_id=1, source_target_pairs={{0,12},{1,13},{2,14},{3,15},{4,0},{5,1},{6,2},{7,3},{8,4},{9,5},{1... | collective-permute-start | bytes 196616 | tf_op jit(solution)/shard_map/ppermute | solution.py:137
  15.2 7.5 %collective-permute-start.5 = (bf16[16,2064]{1,0:T(8,128)(2,1)S(1)}, bf16[16,2064]{1,0:T(8,128)(2,1)S(1)}, u32[]{:S(2)}, u32[]{:S(2)}) collective-permute-start(bf16[16,2064]{1,0:T(8,128)(2,1)S(1)} %get-tuple-element.23), channel_id=1, source_target_pairs={{0,4},{1,5},{2,6},{3,7},{4,8},{5,9},{6,10},{7,11},{8,12},{9,13},{1... | collective-permute-start | bytes 198152 | tf_op jit(solution)/shard_map/ppermute | solution.py:137
  16.9 7.0 %collective-permute-start.6 = (bf16[16,2064]{1,0:T(8,128)(2,1)S(1)}, bf16[16,2064]{1,0:T(8,128)(2,1)S(1)}, u32[]{:S(2)}, u32[]{:S(2)}) collective-permute-start(bf16[16,2064]{1,0:T(8,128)(2,1)S(1)} %get-tuple-element.23), channel_id=1, source_target_pairs={{0,8},{1,9},{2,10},{3,11},{4,12},{5,13},{6,14},{7,15},{8,0},{9,1},... | collective-permute-start | bytes 198152 | tf_op jit(solution)/shard_map/ppermute | solution.py:137
  18.5 5.5 %collective-permute-start.7 = (bf16[16,2064]{1,0:T(8,128)(2,1)S(1)}, bf16[16,2064]{1,0:T(8,128)(2,1)S(1)}, u32[]{:S(2)}, u32[]{:S(2)}) collective-permute-start(bf16[16,2064]{1,0:T(8,128)(2,1)S(1)} %get-tuple-element.23), channel_id=1, source_target_pairs={{0,12},{1,13},{2,14},{3,15},{4,0},{5,1},{6,2},{7,3},{8,4},{9,5},{1... | collective-permute-start | bytes 198152 | tf_op jit(solution)/shard_map/ppermute | solution.py:137
  19.3 8.1 %collective-permute-start.12 = (bf16[64,2048]{1,0:T(8,128)(2,1)S(1)}, bf16[64,2048]{1,0:T(8,128)(2,1)S(1)}, u32[]{:S(2)}, u32[]{:S(2)}) collective-permute-start(bf16[64,2048]{1,0:T(8,128)(2,1)S(1)} %pad_maximum_fusion.4), channel_id=1, source_target_pairs={{0,1},{1,0},{2,3},{3,2},{4,5},{5,4},{6,7},{7,6},{8,9},{9,8},{10,11... | collective-permute-start | bytes 786440 | tf_op jit(solution)/shard_map/ppermute | solution.py:143
  21.1 8.2 %collective-permute-start.13 = (bf16[64,2048]{1,0:T(8,128)(2,1)S(1)}, bf16[64,2048]{1,0:T(8,128)(2,1)S(1)}, u32[]{:S(2)}, u32[]{:S(2)}) collective-permute-start(bf16[64,2048]{1,0:T(8,128)(2,1)S(1)} %pad_maximum_fusion.4), channel_id=1, source_target_pairs={{0,2},{1,3},{2,0},{3,1},{4,6},{5,7},{6,4},{7,5},{8,10},{9,11},{10,... | collective-permute-start | bytes 786440 | tf_op jit(solution)/shard_map/ppermute | solution.py:143
  24.0 9.6 %collective-permute-start.8 = (bf16[64,2064]{1,0:T(8,128)(2,1)S(1)}, bf16[64,2064]{1,0:T(8,128)(2,1)S(1)}, u32[]{:S(2)}, u32[]{:S(2)}) collective-permute-start(bf16[64,2064]{1,0:T(8,128)(2,1)S(1)} %get-tuple-element.47), channel_id=1, source_target_pairs={{0,1},{1,0},{2,3},{3,2},{4,5},{5,4},{6,7},{7,6},{8,9},{9,8},{10,11... | collective-permute-start | bytes 792584 | tf_op jit(solution)/shard_map/ppermute | solution.py:143
  25.6 9.8 %collective-permute-start.9 = (bf16[64,2064]{1,0:T(8,128)(2,1)S(1)}, bf16[64,2064]{1,0:T(8,128)(2,1)S(1)}, u32[]{:S(2)}, u32[]{:S(2)}) collective-permute-start(bf16[64,2064]{1,0:T(8,128)(2,1)S(1)} %get-tuple-element.47), channel_id=1, source_target_pairs={{0,2},{1,3},{2,0},{3,1},{4,6},{5,7},{6,4},{7,5},{8,10},{9,11},{10,... | collective-permute-start | bytes 792584 | tf_op jit(solution)/shard_map/ppermute | solution.py:143
  27.4 10.7 %collective-permute-start.14 = (bf16[32,2048]{1,0:T(8,128)(2,1)S(1)}, bf16[32,2048]{1,0:T(8,128)(2,1)S(1)}, u32[]{:S(2)}, u32[]{:S(2)}) collective-permute-start(bf16[32,2048]{1,0:T(8,128)(2,1)S(1)} %slice.140), channel_id=1, source_target_pairs={{0,2},{1,3},{2,0},{3,1},{4,6},{5,7},{6,4},{7,5},{8,10},{9,11},{10,... | collective-permute-start | bytes 393224 | tf_op jit(solution)/shard_map/ppermute | solution.py:143
  29.4 8.8 %collective-permute-start.15 = (bf16[32,2048]{1,0:T(8,128)(2,1)S(1)}, bf16[32,2048]{1,0:T(8,128)(2,1)S(1)}, u32[]{:S(2)}, u32[]{:S(2)}) collective-permute-start(bf16[32,2048]{1,0:T(8,128)(2,1)S(1)} %slice.141), channel_id=1, source_target_pairs={{0,1},{1,0},{2,3},{3,2},{4,5},{5,4},{6,7},{7,6},{8,9},{9,8},{10,11... | collective-permute-start | bytes 393224 | tf_op jit(solution)/shard_map/ppermute | solution.py:143
  33.6 6.7 %collective-permute-start.10 = (bf16[32,2064]{1,0:T(8,128)(2,1)S(1)}, bf16[32,2064]{1,0:T(8,128)(2,1)S(1)}, u32[]{:S(2)}, u32[]{:S(2)}) collective-permute-start(bf16[32,2064]{1,0:T(8,128)(2,1)S(1)} %slice.136), channel_id=1, source_target_pairs={{0,2},{1,3},{2,0},{3,1},{4,6},{5,7},{6,4},{7,5},{8,10},{9,11},{10,... | collective-permute-start | bytes 396296 | tf_op jit(solution)/shard_map/ppermute | solution.py:143
  35.4 5.1 %collective-permute-start.11 = (bf16[32,2064]{1,0:T(8,128)(2,1)S(1)}, bf16[32,2064]{1,0:T(8,128)(2,1)S(1)}, u32[]{:S(2)}, u32[]{:S(2)}) collective-permute-start(bf16[32,2064]{1,0:T(8,128)(2,1)S(1)} %slice.137), channel_id=1, source_target_pairs={{0,1},{1,0},{2,3},{3,2},{4,5},{5,4},{6,7},{7,6},{8,9},{9,8},{10,11... | collective-permute-start | bytes 396296 | tf_op jit(solution)/shard_map/ppermute | solution.py:143
  38.2 19.4 %collective-permute-start.20 = (bf16[256,2048]{1,0:T(8,128)(2,1)S(1)}, bf16[256,2048]{1,0:T(8,128)(2,1)S(1)}, u32[]{:S(2)}, u32[]{:S(2)}) collective-permute-start(bf16[256,2048]{1,0:T(8,128)(2,1)S(1)} %constant_dynamic-update-slice_fusion.12), channel_id=1, source_target_pairs={{0,16},{16,0},{1,17},{17,1},{2,18},{18,2},{3,19},{19,3},{4,20},{20... | collective-permute-start | bytes 3145736 | tf_op jit(solution)/shard_map/ppermute | solution.py:133
  43.3 9.3 %collective-permute-start.16 = (bf16[64,2048]{1,0:T(8,128)(2,1)S(1)}, bf16[64,2048]{1,0:T(8,128)(2,1)S(1)}, u32[]{:S(2)}, u32[]{:S(2)}) collective-permute-start(bf16[64,2048]{1,0:T(8,128)(2,1)S(1)} %get-tuple-element.40), channel_id=1, source_target_pairs={{0,1},{1,0},{2,3},{3,2},{4,5},{5,4},{6,7},{7,6},{8,9},{9,8},{10,11... | collective-permute-start | bytes 786440 | tf_op jit(solution)/shard_map/ppermute | solution.py:143
  44.7 11.2 %collective-permute-start.17 = (bf16[64,2048]{1,0:T(8,128)(2,1)S(1)}, bf16[64,2048]{1,0:T(8,128)(2,1)S(1)}, u32[]{:S(2)}, u32[]{:S(2)}) collective-permute-start(bf16[64,2048]{1,0:T(8,128)(2,1)S(1)} %get-tuple-element.42), channel_id=1, source_target_pairs={{0,2},{1,3},{2,0},{3,1},{4,6},{5,7},{6,4},{7,5},{8,10},{9,11},{10,... | collective-permute-start | bytes 786440 | tf_op jit(solution)/shard_map/ppermute | solution.py:143
  45.4 12.1 %collective-permute-start.18 = (bf16[64,2048]{1,0:T(8,128)(2,1)S(1)}, bf16[64,2048]{1,0:T(8,128)(2,1)S(1)}, u32[]{:S(2)}, u32[]{:S(2)}) collective-permute-start(bf16[64,2048]{1,0:T(8,128)(2,1)S(1)} %get-tuple-element.41), channel_id=1, source_target_pairs={{0,3},{1,2},{2,1},{3,0},{4,7},{5,6},{6,5},{7,4},{8,11},{9,10},{10,... | collective-permute-start | bytes 786440 | tf_op jit(solution)/shard_map/ppermute | solution.py:143
  46.8 22.5 %collective-permute-start.24 = (bf16[256,2048]{1,0:T(8,128)(2,1)S(1)}, bf16[256,2048]{1,0:T(8,128)(2,1)S(1)}, u32[]{:S(2)}, u32[]{:S(2)}) collective-permute-start(bf16[256,2048]{1,0:T(8,128)(2,1)S(1)} %slice.139), channel_id=1, source_target_pairs={{0,16},{16,0},{1,17},{17,1},{2,18},{18,2},{3,19},{19,3},{4,20},{20... | collective-permute-start | bytes 3145736 | tf_op jit(solution)/shard_map/ppermute | solution.py:133
  52.6 5.0 %collective-permute-start.19 = (bf16[256,576]{1,0:T(8,128)(2,1)S(1)}, bf16[256,576]{1,0:T(8,128)(2,1)S(1)}, u32[]{:S(2)}, u32[]{:S(2)}) collective-permute-start(bf16[256,576]{1,0:T(8,128)(2,1)S(1)} %pad_maximum_fusion.3), channel_id=1, source_target_pairs={{0,16},{16,0},{1,17},{17,1},{2,18},{18,2},{3,19},{19,3},{4,20},{20... | collective-permute-start | bytes 884744 | tf_op jit(solution)/shard_map/ppermute | solution.py:133
  59.5 5.1 %collective-permute-start.21 = (bf16[16,2048]{1,0:T(8,128)(2,1)S(1)}, bf16[16,2048]{1,0:T(8,128)(2,1)S(1)}, u32[]{:S(2)}, u32[]{:S(2)}) collective-permute-start(bf16[16,2048]{1,0:T(8,128)(2,1)S(1)} %get-tuple-element.44), channel_id=1, source_target_pairs={{0,12},{1,13},{2,14},{3,15},{4,0},{5,1},{6,2},{7,3},{8,4},{9,5},{1... | collective-permute-start | bytes 196616 | tf_op jit(solution)/shard_map/ppermute | solution.py:137
  61.9 5.2 %collective-permute-start.22 = (bf16[16,2048]{1,0:T(8,128)(2,1)S(1)}, bf16[16,2048]{1,0:T(8,128)(2,1)S(1)}, u32[]{:S(2)}, u32[]{:S(2)}) collective-permute-start(bf16[16,2048]{1,0:T(8,128)(2,1)S(1)} %get-tuple-element.46), channel_id=1, source_target_pairs={{0,8},{1,9},{2,10},{3,11},{4,12},{5,13},{6,14},{7,15},{8,0},{9,1},... | collective-permute-start | bytes 196616 | tf_op jit(solution)/shard_map/ppermute | solution.py:137
  62.6 6.1 %collective-permute-start.23 = (bf16[16,2048]{1,0:T(8,128)(2,1)S(1)}, bf16[16,2048]{1,0:T(8,128)(2,1)S(1)}, u32[]{:S(2)}, u32[]{:S(2)}) collective-permute-start(bf16[16,2048]{1,0:T(8,128)(2,1)S(1)} %get-tuple-element.45), channel_id=1, source_target_pairs={{0,4},{1,5},{2,6},{3,7},{4,8},{5,9},{6,10},{7,11},{8,12},{9,13},{1... | collective-permute-start | bytes 196616 | tf_op jit(solution)/shard_map/ppermute | solution.py:137
  (4 other events, 9.6 us)

commit v11 on v10

--- a/solution.py
+++ b/solution.py
@@ -146,6 +146,7 @@
 VMEM = pl.BlockSpec(memory_space=pltpu.VMEM)
 ANY = pl.BlockSpec(memory_space=pl.ANY)
 NT = (((1,), (1,)), ((), ()))
+TN = (((0,), (0,)), ((), ()))
 
 
 def on_chip(body, outs, *args, scratch=(), spec=VMEM, limit=True):
@@ -164,11 +165,10 @@
 
 
 def read_kernel(
-    ids_hbm, gates_hbm, packing_hbm, tokens_hbm, cotangent_hbm, gate_hbm, up_hbm, down_hbm,
-    table_ref, tokens_ref, cotangent_ref, weights_ref,
+    ids_hbm, gates_hbm, packing_hbm, tokens_hbm, cotangent_hbm,
+    table_ref, tokens_ref, cotangent_ref,
     ids_ref, gates_ref, packing_ref, ready,
 ):
-    half = gate_hbm.shape[1]
     pairs = [
         (ids_hbm, ids_ref),
         (gates_hbm, gates_ref),
@@ -176,8 +176,6 @@
         (tokens_hbm, tokens_ref),
         (cotangent_hbm, cotangent_ref),
     ]
-    for index, source in enumerate((gate_hbm, up_hbm, down_hbm)):
-        pairs.append((source.at[0], weights_ref.at[index * half : (index + 1) * half]))
     copies = [
         pltpu.make_async_copy(source, target, ready.at[index])
         for index, (source, target) in enumerate(pairs)
@@ -216,6 +214,22 @@
     here_ref[...] = (lanes == lax.axis_index("expert")).astype(jnp.float32)
 
 
+def weight_kernel(own_grads, other_grads, rows, other_rows, upstream, other_upstream, *outs):
+    half = outs[0].shape[1]
+    for index, out in enumerate(outs):
+        own, other = (upstream, other_upstream) if index == 2 else (rows, other_rows)
+        span = slice(index * half, (index + 1) * half)
+        step = min(out.shape[-1], 1024)
+        for left in range(0, out.shape[-1], step):
+            columns = slice(left, left + step)
+            total = lax.dot_general(
+                own_grads[:, span], own[:, columns], TN, preferred_element_type=jnp.float32
+            ) + lax.dot_general(
+                other_grads[:, span], other[:, columns], TN, preferred_element_type=jnp.float32
+            )
+            out[0, :, columns] = total.astype(jnp.bfloat16)
+
+
 def along_outer(value, count, inner):
     return [value] + [shift_outer(value, count, inner, step) for step in range(1, count // inner)]
 
@@ -257,33 +271,28 @@
     row_count = tokens.shape[0]
     low = jnp.bfloat16
     ids, gates, lists = expert_ids.T, gate_values.T, packing.reshape(1, row_count)
-    table, own_tokens, own_cotangent, own_weights = on_chip(
+    token_blocks = along_outer(tokens, count, inner)
+    table, own_tokens, own_cotangent = on_chip(
         read_kernel,
         [
             ((count + 16, row_count), low),
             (tokens.shape, low),
             (cotangent.shape, low),
-            ((3 * half, model_width), low),
         ],
         ids,
         gates,
         lists,
         tokens,
         cotangent,
-        w_gate,
-        w_up,
-        w_down,
         spec=ANY,
         limit=False,
         scratch=[
             pltpu.VMEM(ids.shape, ids.dtype),
             pltpu.VMEM(gates.shape, gates.dtype),
             pltpu.VMEM(lists.shape, lists.dtype),
-            pltpu.SemaphoreType.DMA((8,)),
+            pltpu.SemaphoreType.DMA((5,)),
         ],
     )
-    token_column = jnp.concatenate(along_outer(own_tokens, count, inner), axis=0)
-    other = swap(own_weights)
     payload, here = on_chip(
         payload_kernel,
         [((row_count, model_width + count), low), ((8, count), jnp.float32)],
@@ -291,9 +300,14 @@
         swap(table),
         own_cotangent,
     )
-    payload, token_column, other = lax.optimization_barrier((payload, token_column, other))
+    token_column = jnp.concatenate([own_tokens, *token_blocks[1:]], axis=0)
+    payload, token_column = lax.optimization_barrier((payload, token_column))
     upstream_column = jnp.concatenate(along_outer(payload, count, inner), axis=0)
-    inputs = jnp.concatenate(across_inner(token_column, count, inner), axis=0)
+    token_columns = across_inner(token_column, count, inner)
+    own_weights = jnp.concatenate([w_gate[0], w_up[0], w_down[0]], axis=0)
+    sent_weights, token_columns[1] = lax.optimization_barrier((own_weights, token_columns[1]))
+    other = swap(sent_weights)
+    inputs = jnp.concatenate(token_columns, axis=0)
     other_inputs = swap(inputs)
     upstream = jnp.concatenate(across_inner(upstream_column, count, inner), axis=0)
     gate = jnp.sum(
@@ -324,21 +338,20 @@
     sent_grads, upstream, _ = lax.optimization_barrier((sent_grads, upstream, partial_grad))
     other_grads = swap(sent_grads)
     other_upstream = swap(upstream)
-    column_sum, other_grads, other_inputs = lax.optimization_barrier(
-        (column_sum, other_grads, other_inputs)
+    column_sum, other_grads, other_inputs, other_upstream = lax.optimization_barrier(
+        (column_sum, other_grads, other_inputs, other_upstream)
     )
     input_grad = return_outer(column_sum, count, inner)
-    weight_grads = []
-    for index, (rows, other_rows) in enumerate(
-        ((inputs, other_inputs), (inputs, other_inputs), (upstream, other_upstream))
-    ):
-        low = index * half
-        total = jnp.dot(
-            own_grads[:, low : low + half].T, rows, preferred_element_type=jnp.float32
-        ) + jnp.dot(
-            other_grads[:, low : low + half].T, other_rows, preferred_element_type=jnp.float32
-        )
-        weight_grads.append(total.astype(jnp.bfloat16)[None])
+    weight_grads = on_chip(
+        weight_kernel,
+        [((1, half, model_width), low)] * 3,
+        own_grads,
+        other_grads,
+        inputs,
+        other_inputs,
+        upstream,
+        other_upstream,
+    )
     return (input_grad, *weight_grads)
 
 

time: 70.8 us -> 69.9 us (0.987)
  matrix products: 8.18 us -> 3.05 us
  waiting for transfers between devices: 24.1 us -> 27.6 us
  other arithmetic: 1.07 us -> 3.01 us
  starting transfers between devices: 30.1 us -> 28.6 us
  Pallas kernels: 3.39 us -> 4.21 us
    dot_general x6 -> x0, matrix products: 5.17 us -> none  [the longest x3 2.99 us: dense_local(): jnp.dot(own_grads[:, low:low + half].T, rows, preferred_element_type=jnp....]
    ppermute x11, waiting for transfers between devices: 16.5 us -> 20.5 us  [swap_inner(): lax.ppermute(value, 'expert', [(place, place ^ partner) for place in rang...]
    ppermute x11, starting transfers between devices: 15.5 us -> 13.1 us  [swap_inner(): lax.ppermute(value, 'expert', [(place, place ^ partner) for place in rang...]
    concatenate x1 -> x3, other arithmetic: 0.02 us -> 1.95 us  [the longest x1 1.81 us: dense_local(): own_weights = jnp.concatenate([w_gate[0], w_up[0], w_down[0]], axis=0)]
    slice x2 -> x1, local copies, waits for them, and re-layouts: 2.08 us -> 0.16 us  [dense_local(): down = jnp.concatenate([own_weights[2 * half:], other[2 * half:]], axis=0)]
    unnamed x16 -> x22, local copies, waits for them, and re-layouts: 0.19 us -> 1.48 us
    ppermute x9, starting transfers between devices: 14 us -> 15.3 us  [shift_outer(): lax.ppermute(value, 'expert', [(place, (place + step * inner) % count) fo...]
    pallas_call x2 -> x3, Pallas kernels: 3.39 us -> 4.21 us  [on_chip(): pl.pallas_call(body, out_shape=[jax.ShapeDtypeStruct(shape, dtype) for sh...]
  transfers between devices with their start and end apart: 25 -> 25, of which waited for: 16 -> 12; matrix products, arithmetic and copies ran while one was open for 15% -> 9% of each run, Pallas kernels for 0% -> 6%
where the time goes in v11:
time: 69.9 us; the launch traced here: 69.6 us
  starting transfers between devices  28.6 us (41%)
  waiting for transfers between devices  27.6 us (39%)
  Pallas kernels  4.21 us (6%)
  matrix products  3.05 us (4%)
  other arithmetic  3.01 us (4%)
  local copies, waits for them, and re-layouts  2.18 us (3%)
  between operations  0.96 us (1%)
    ppermute x11, waiting for transfers between devices, swap_inner(): lax.ppermute(value, 'expert', [(place, place ^ partner) for place in rang...  20.5 us
    ppermute x9, starting transfers between devices, shift_outer(): lax.ppermute(value, 'expert', [(place, (place + step * inner) % count) fo...  15.3 us
    ppermute x11, starting transfers between devices, swap_inner(): lax.ppermute(value, 'expert', [(place, place ^ partner) for place in rang...  13.1 us
    ppermute x9, waiting for transfers between devices, shift_outer(): lax.ppermute(value, 'expert', [(place, (place + step * inner) % count) fo...  7.12 us
    pallas_call x3, Pallas kernels, on_chip(): pl.pallas_call(body, out_shape=[jax.ShapeDtypeStruct(shape, dtype) for sh...  4.21 us
    concatenate x1, other arithmetic, dense_local(): own_weights = jnp.concatenate([w_gate[0], w_up[0], w_down[0]], axis=0)  1.81 us
    unnamed x22, local copies, waits for them, and re-layouts  1.48 us
  transfers between devices with their start and end apart: 25, of which 12 were waited for; matrix products, arithmetic and copies ran while one was open for 9% of the time, Pallas kernels for 6%

profile of v11, /device:TPU:0, one launch (start us, length us, event | category | flops | bytes accessed | tf_op | source)
XLA Modules:
  0.0 69.6 jit_solution(2438534727699166882)
XLA Ops:
  0.6 5.1 %collective-permute-start.3 = (bf16[16,2048]{1,0:T(8,128)(2,1)}, bf16[16,2048]{1,0:T(8,128)(2,1)S(1)}, u32[]{:S(2)}, u32[]{:S(2)}) collective-permute-start(bf16[16,2048]{1,0:T(8,128)(2,1)} %tokens_hbm.1), channel_id=1, source_target_pairs={{0,12},{1,13},{2,14},{3,15},{4,0},{5,1},{6,2},{7,3},{8,4},{9,5},{1... | collective-permute-start | bytes 196616 | tf_op jit(solution)/shard_map/ppermute | solution.py:137
  6.7 1.6 %shard_map.111 = (bf16[32,16]{1,0:T(8,128)(2,1)}, bf16[16,2048]{1,0:T(8,128)(2,1)}, bf16[16,2048]{1,0:T(8,128)(2,1)}) custom-call(s32[8,16]{1,0:T(8,128)} %bitcast.17, bf16[8,16]{1,0:T(8,128)(2,1)} %bitcast.18, s32[1,16]{1,0:T(1,128)} %bitcast.19, bf16[16,2048]{1,0:T(8,128)(2,1)} %tokens_hbm.1, bf16[16,2048]{1,0:T(8,128)(2,1)} %cotangent_hbm.1), custom_call_target="tpu_custom_call" | custom-call | bytes 264000 | tf_op jit(solution)/shard_map/pallas_call | solution.py:156
  8.5 1.8 %pad_maximum_fusion.1 = bf16[576,2048]{1,0:T(8,128)(2,1)S(1)} fusion(bf16[192,2048]{1,0:T(8,128)(2,1)} %bitcast.9, bf16[192,2048]{1,0:T(8,128)(2,1)} %bitcast.11, bf16[192,2048]{1,0:T(8,128)(2,1)} %bitcast.14), kind=kLoop, calls=%fused_computation.2 | loop fusion | flops 7077888 | bytes 4718592 | tf_op jit(solution)/shard_map/concatenate | solution.py:307
  10.5 2.0 %collective-permute-done.2 = bf16[16,2048]{1,0:T(8,128)(2,1)S(1)} collective-permute-done((bf16[16,2048]{1,0:T(8,128)(2,1)}, bf16[16,2048]{1,0:T(8,128)(2,1)S(1)}, u32[]{:S(2)}, u32[]{:S(2)}) %collective-permute-start.2) | collective-permute-done | bytes 65568 | tf_op jit(solution)/shard_map/ppermute | solution.py:137
  12.4 1.6 %collective-permute-start.11 = (bf16[64,2048]{1,0:T(8,128)(2,1)S(1)}, bf16[64,2048]{1,0:T(8,128)(2,1)S(1)}, u32[]{:S(2)}, u32[]{:S(2)}) collective-permute-start(bf16[64,2048]{1,0:T(8,128)(2,1)S(1)} %pad_maximum_fusion.6), channel_id=1, source_target_pairs={{0,1},{1,0},{2,3},{3,2},{4,5},{5,4},{6,7},{7,6},{8,9},{9,8},{10,11... | collective-permute-start | bytes 786440 | tf_op jit(solution)/shard_map/ppermute | solution.py:143
  14.0 1.6 %collective-permute-start.13 = (bf16[64,2048]{1,0:T(8,128)(2,1)S(1)}, bf16[64,2048]{1,0:T(8,128)(2,1)S(1)}, u32[]{:S(2)}, u32[]{:S(2)}) collective-permute-start(bf16[64,2048]{1,0:T(8,128)(2,1)S(1)} %pad_maximum_fusion.6), channel_id=1, source_target_pairs={{0,2},{1,3},{2,0},{3,1},{4,6},{5,7},{6,4},{7,5},{8,10},{9,11},{10,... | collective-permute-start | bytes 786440 | tf_op jit(solution)/shard_map/ppermute | solution.py:143
  16.2 2.0 %collective-permute-start.5 = (bf16[16,2064]{1,0:T(8,128)(2,1)S(1)}, bf16[16,2064]{1,0:T(8,128)(2,1)S(1)}, u32[]{:S(2)}, u32[]{:S(2)}) collective-permute-start(bf16[16,2064]{1,0:T(8,128)(2,1)S(1)} %get-tuple-element.26), channel_id=1, source_target_pairs={{0,8},{1,9},{2,10},{3,11},{4,12},{5,13},{6,14},{7,15},{8,0},{9,1},... | collective-permute-start | bytes 198152 | tf_op jit(solution)/shard_map/ppermute | solution.py:137
  18.1 2.2 %collective-permute-start.6 = (bf16[16,2064]{1,0:T(8,128)(2,1)S(1)}, bf16[16,2064]{1,0:T(8,128)(2,1)S(1)}, u32[]{:S(2)}, u32[]{:S(2)}) collective-permute-start(bf16[16,2064]{1,0:T(8,128)(2,1)S(1)} %get-tuple-element.26), channel_id=1, source_target_pairs={{0,12},{1,13},{2,14},{3,15},{4,0},{5,1},{6,2},{7,3},{8,4},{9,5},{1... | collective-permute-start | bytes 198152 | tf_op jit(solution)/shard_map/ppermute | solution.py:137
  20.4 1.9 %collective-permute-done.4 = bf16[16,2064]{1,0:T(8,128)(2,1)S(1)} collective-permute-done((bf16[16,2064]{1,0:T(8,128)(2,1)S(1)}, bf16[16,2064]{1,0:T(8,128)(2,1)S(1)}, u32[]{:S(2)}, u32[]{:S(2)}) %collective-permute-start.4) | collective-permute-done | bytes 66080 | tf_op jit(solution)/shard_map/ppermute | solution.py:137
  22.3 1.5 %collective-permute-done.5 = bf16[16,2064]{1,0:T(8,128)(2,1)S(1)} collective-permute-done((bf16[16,2064]{1,0:T(8,128)(2,1)S(1)}, bf16[16,2064]{1,0:T(8,128)(2,1)S(1)}, u32[]{:S(2)}, u32[]{:S(2)}) %collective-permute-start.5) | collective-permute-done | bytes 66080 | tf_op jit(solution)/shard_map/ppermute | solution.py:137
  25.0 1.6 %collective-permute-start.14 = (bf16[32,2048]{1,0:T(8,128)(2,1)S(1)}, bf16[32,2048]{1,0:T(8,128)(2,1)S(1)}, u32[]{:S(2)}, u32[]{:S(2)}) collective-permute-start(bf16[32,2048]{1,0:T(8,128)(2,1)S(1)} %slice.117), channel_id=1, source_target_pairs={{0,2},{1,3},{2,0},{3,1},{4,6},{5,7},{6,4},{7,5},{8,10},{9,11},{10,... | collective-permute-start | bytes 393224 | tf_op jit(solution)/shard_map/ppermute | solution.py:143
  26.6 1.6 %collective-permute-start.15 = (bf16[32,2048]{1,0:T(8,128)(2,1)S(1)}, bf16[32,2048]{1,0:T(8,128)(2,1)S(1)}, u32[]{:S(2)}, u32[]{:S(2)}) collective-permute-start(bf16[32,2048]{1,0:T(8,128)(2,1)S(1)} %slice.118), channel_id=1, source_target_pairs={{0,1},{1,0},{2,3},{3,2},{4,5},{5,4},{6,7},{7,6},{8,9},{9,8},{10,11... | collective-permute-start | bytes 393224 | tf_op jit(solution)/shard_map/ppermute | solution.py:143
  28.2 5.3 %collective-permute-done.7 = bf16[64,2064]{1,0:T(8,128)(2,1)S(1)} collective-permute-done((bf16[64,2064]{1,0:T(8,128)(2,1)S(1)}, bf16[64,2064]{1,0:T(8,128)(2,1)S(1)}, u32[]{:S(2)}, u32[]{:S(2)}) %collective-permute-start.7) | collective-permute-done | bytes 264224 | tf_op jit(solution)/shard_map/ppermute | solution.py:143
  34.1 1.5 %collective-permute-start.10 = (bf16[32,2064]{1,0:T(8,128)(2,1)S(1)}, bf16[32,2064]{1,0:T(8,128)(2,1)S(1)}, u32[]{:S(2)}, u32[]{:S(2)}) collective-permute-start(bf16[32,2064]{1,0:T(8,128)(2,1)S(1)} %slice.113), channel_id=1, source_target_pairs={{0,1},{1,0},{2,3},{3,2},{4,5},{5,4},{6,7},{7,6},{8,9},{9,8},{10,11... | collective-permute-start | bytes 396296 | tf_op jit(solution)/shard_map/ppermute | solution.py:143
  36.9 1.7 %collective-permute-done.9 = bf16[32,2064]{1,0:T(8,128)(2,1)S(1)} collective-permute-done((bf16[32,2064]{1,0:T(8,128)(2,1)S(1)}, bf16[32,2064]{1,0:T(8,128)(2,1)S(1)}, u32[]{:S(2)}, u32[]{:S(2)}) %collective-permute-start.9) | collective-permute-done | bytes 132128 | tf_op jit(solution)/shard_map/ppermute | solution.py:143
  42.8 1.2 %convolution_convert_fusion = bf16[256,2048]{1,0:T(8,128)(2,1)S(1)} fusion(bf16[192,2048]{1,0:T(8,128)(2,1)S(1)} %get-tuple-element.41, bf16[192,2048]{1,0:T(8,128)(2,1)S(1)} %bitcast.13, bf16[192,2048]{1,0:T(8,128)(2,1)S(1)} %get-tuple-element.42, bf16[192,2048]{1,0:T(8,128)(2,1)S(1)} %bitcast.16, bf16[256,384]{1,0:T(8,128)(2,1)S(1)} %get-tuple-element.44, ...), kind=kOutput, calls=%fused_computation.1 | convolution fusion | flops 819200000 | bytes 4587520 | tf_op jit(solution)/shard_map/dot_general | solution.py:332
  44.6 1.6 %collective-permute-start.18 = (bf16[64,2048]{1,0:T(8,128)(2,1)S(1)}, bf16[64,2048]{1,0:T(8,128)(2,1)S(1)}, u32[]{:S(2)}, u32[]{:S(2)}) collective-permute-start(bf16[64,2048]{1,0:T(8,128)(2,1)S(1)} %get-tuple-element.46), channel_id=1, source_target_pairs={{0,3},{1,2},{2,1},{3,0},{4,7},{5,6},{6,5},{7,4},{8,11},{9,10},{10,... | collective-permute-start | bytes 786440 | tf_op jit(solution)/shard_map/ppermute | solution.py:143
  46.1 1.5 %collective-permute-start.17 = (bf16[64,2048]{1,0:T(8,128)(2,1)S(1)}, bf16[64,2048]{1,0:T(8,128)(2,1)S(1)}, u32[]{:S(2)}, u32[]{:S(2)}) collective-permute-start(bf16[64,2048]{1,0:T(8,128)(2,1)S(1)} %get-tuple-element.47), channel_id=1, source_target_pairs={{0,2},{1,3},{2,0},{3,1},{4,6},{5,7},{6,4},{7,5},{8,10},{9,11},{10,... | collective-permute-start | bytes 786440 | tf_op jit(solution)/shard_map/ppermute | solution.py:143
  48.1 6.6 %collective-permute-done.18 = bf16[64,2048]{1,0:T(8,128)(2,1)S(1)} collective-permute-done((bf16[64,2048]{1,0:T(8,128)(2,1)S(1)}, bf16[64,2048]{1,0:T(8,128)(2,1)S(1)}, u32[]{:S(2)}, u32[]{:S(2)}) %collective-permute-start.18) | collective-permute-done | bytes 262176 | tf_op jit(solution)/shard_map/ppermute | solution.py:143
  54.7 5.2 %collective-permute-done.17 = bf16[64,2048]{1,0:T(8,128)(2,1)S(1)} collective-permute-done((bf16[64,2048]{1,0:T(8,128)(2,1)S(1)}, bf16[64,2048]{1,0:T(8,128)(2,1)S(1)}, u32[]{:S(2)}, u32[]{:S(2)}) %collective-permute-start.17) | collective-permute-done | bytes 262176 | tf_op jit(solution)/shard_map/ppermute | solution.py:143
  60.2 2.0 %collective-permute-start.24 = (bf16[16,2048]{1,0:T(8,128)(2,1)S(1)}, bf16[16,2048]{1,0:T(8,128)(2,1)S(1)}, u32[]{:S(2)}, u32[]{:S(2)}) collective-permute-start(bf16[16,2048]{1,0:T(8,128)(2,1)S(1)} %get-tuple-element.50), channel_id=1, source_target_pairs={{0,4},{1,5},{2,6},{3,7},{4,8},{5,9},{6,10},{7,11},{8,12},{9,13},{1... | collective-permute-start | bytes 196616 | tf_op jit(solution)/shard_map/ppermute | solution.py:137
  63.4 1.3 %collective-permute-start.22 = (bf16[16,2048]{1,0:T(8,128)(2,1)S(1)}, bf16[16,2048]{1,0:T(8,128)(2,1)S(1)}, u32[]{:S(2)}, u32[]{:S(2)}) collective-permute-start(bf16[16,2048]{1,0:T(8,128)(2,1)S(1)} %get-tuple-element.49), channel_id=1, source_target_pairs={{0,12},{1,13},{2,14},{3,15},{4,0},{5,1},{6,2},{7,3},{8,4},{9,5},{1... | collective-permute-start | bytes 196616 | tf_op jit(solution)/shard_map/ppermute | solution.py:137
  64.7 2.5 %shard_map.113 = (bf16[1,192,2048]{2,1,0:T(8,128)(2,1)}, bf16[1,192,2048]{2,1,0:T(8,128)(2,1)}, bf16[1,192,2048]{2,1,0:T(8,128)(2,1)}) custom-call(bf16[256,576]{1,0:T(8,128)(2,1)S(1)} %pad_maximum_fusion.5.own_grads, bf16[256,576]{1,0:T(8,128)(2,1)S(1)} %collective-permute-done.19.other_grads, ...), custom_call_target="tpu_custom_call" | custom-call | bytes 7143424 | tf_op jit(solution)/shard_map/pallas_call | solution.py:156
  67.2 1.7 %collective-permute-done.23 = bf16[16,2048]{1,0:T(8,128)(2,1)S(1)} collective-permute-done((bf16[16,2048]{1,0:T(8,128)(2,1)S(1)}, bf16[16,2048]{1,0:T(8,128)(2,1)S(1)}, u32[]{:S(2)}, u32[]{:S(2)}) %collective-permute-start.23) | collective-permute-done | bytes 65568 | tf_op jit(solution)/shard_map/ppermute | solution.py:137
  (76 shorter events, 12.4 us)
Async XLA Ops:
  0.6 9.8 %collective-permute-start.3 = (bf16[16,2048]{1,0:T(8,128)(2,1)}, bf16[16,2048]{1,0:T(8,128)(2,1)S(1)}, u32[]{:S(2)}, u32[]{:S(2)}) collective-permute-start(bf16[16,2048]{1,0:T(8,128)(2,1)} %tokens_hbm.1), channel_id=1, source_target_pairs={{0,12},{1,13},{2,14},{3,15},{4,0},{5,1},{6,2},{7,3},{8,4},{9,5},{1... | collective-permute-start | bytes 196616 | tf_op jit(solution)/shard_map/ppermute | solution.py:137
  5.7 6.7 %collective-permute-start.2 = (bf16[16,2048]{1,0:T(8,128)(2,1)}, bf16[16,2048]{1,0:T(8,128)(2,1)S(1)}, u32[]{:S(2)}, u32[]{:S(2)}) collective-permute-start(bf16[16,2048]{1,0:T(8,128)(2,1)} %tokens_hbm.1), channel_id=1, source_target_pairs={{0,8},{1,9},{2,10},{3,11},{4,12},{5,13},{6,14},{7,15},{8,0},{9,1},... | collective-permute-start | bytes 196616 | tf_op jit(solution)/shard_map/ppermute | solution.py:137
  5.7 6.7 %collective-permute-start.1 = (bf16[16,2048]{1,0:T(8,128)(2,1)}, bf16[16,2048]{1,0:T(8,128)(2,1)S(1)}, u32[]{:S(2)}, u32[]{:S(2)}) collective-permute-start(bf16[16,2048]{1,0:T(8,128)(2,1)} %tokens_hbm.1), channel_id=1, source_target_pairs={{0,4},{1,5},{2,6},{3,7},{4,8},{5,9},{6,10},{7,11},{8,12},{9,13},{1... | collective-permute-start | bytes 196616 | tf_op jit(solution)/shard_map/ppermute | solution.py:137
  12.4 12.5 %collective-permute-start.11 = (bf16[64,2048]{1,0:T(8,128)(2,1)S(1)}, bf16[64,2048]{1,0:T(8,128)(2,1)S(1)}, u32[]{:S(2)}, u32[]{:S(2)}) collective-permute-start(bf16[64,2048]{1,0:T(8,128)(2,1)S(1)} %pad_maximum_fusion.6), channel_id=1, source_target_pairs={{0,1},{1,0},{2,3},{3,2},{4,5},{5,4},{6,7},{7,6},{8,9},{9,8},{10,11... | collective-permute-start | bytes 786440 | tf_op jit(solution)/shard_map/ppermute | solution.py:143
  14.0 12.6 %collective-permute-start.13 = (bf16[64,2048]{1,0:T(8,128)(2,1)S(1)}, bf16[64,2048]{1,0:T(8,128)(2,1)S(1)}, u32[]{:S(2)}, u32[]{:S(2)}) collective-permute-start(bf16[64,2048]{1,0:T(8,128)(2,1)S(1)} %pad_maximum_fusion.6), channel_id=1, source_target_pairs={{0,2},{1,3},{2,0},{3,1},{4,6},{5,7},{6,4},{7,5},{8,10},{9,11},{10,... | collective-permute-start | bytes 786440 | tf_op jit(solution)/shard_map/ppermute | solution.py:143
  15.6 6.7 %collective-permute-start.4 = (bf16[16,2064]{1,0:T(8,128)(2,1)S(1)}, bf16[16,2064]{1,0:T(8,128)(2,1)S(1)}, u32[]{:S(2)}, u32[]{:S(2)}) collective-permute-start(bf16[16,2064]{1,0:T(8,128)(2,1)S(1)} %get-tuple-element.26), channel_id=1, source_target_pairs={{0,4},{1,5},{2,6},{3,7},{4,8},{5,9},{6,10},{7,11},{8,12},{9,13},{1... | collective-permute-start | bytes 198152 | tf_op jit(solution)/shard_map/ppermute | solution.py:137
  16.2 7.7 %collective-permute-start.5 = (bf16[16,2064]{1,0:T(8,128)(2,1)S(1)}, bf16[16,2064]{1,0:T(8,128)(2,1)S(1)}, u32[]{:S(2)}, u32[]{:S(2)}) collective-permute-start(bf16[16,2064]{1,0:T(8,128)(2,1)S(1)} %get-tuple-element.26), channel_id=1, source_target_pairs={{0,8},{1,9},{2,10},{3,11},{4,12},{5,13},{6,14},{7,15},{8,0},{9,1},... | collective-permute-start | bytes 198152 | tf_op jit(solution)/shard_map/ppermute | solution.py:137
  18.1 5.7 %collective-permute-start.6 = (bf16[16,2064]{1,0:T(8,128)(2,1)S(1)}, bf16[16,2064]{1,0:T(8,128)(2,1)S(1)}, u32[]{:S(2)}, u32[]{:S(2)}) collective-permute-start(bf16[16,2064]{1,0:T(8,128)(2,1)S(1)} %get-tuple-element.26), channel_id=1, source_target_pairs={{0,12},{1,13},{2,14},{3,15},{4,0},{5,1},{6,2},{7,3},{8,4},{9,5},{1... | collective-permute-start | bytes 198152 | tf_op jit(solution)/shard_map/ppermute | solution.py:137
  23.9 9.6 %collective-permute-start.7 = (bf16[64,2064]{1,0:T(8,128)(2,1)S(1)}, bf16[64,2064]{1,0:T(8,128)(2,1)S(1)}, u32[]{:S(2)}, u32[]{:S(2)}) collective-permute-start(bf16[64,2064]{1,0:T(8,128)(2,1)S(1)} %get-tuple-element.58), channel_id=1, source_target_pairs={{0,1},{1,0},{2,3},{3,2},{4,5},{5,4},{6,7},{7,6},{8,9},{9,8},{10,11... | collective-permute-start | bytes 792584 | tf_op jit(solution)/shard_map/ppermute | solution.py:143
  24.5 9.6 %collective-permute-start.8 = (bf16[64,2064]{1,0:T(8,128)(2,1)S(1)}, bf16[64,2064]{1,0:T(8,128)(2,1)S(1)}, u32[]{:S(2)}, u32[]{:S(2)}) collective-permute-start(bf16[64,2064]{1,0:T(8,128)(2,1)S(1)} %get-tuple-element.58), channel_id=1, source_target_pairs={{0,2},{1,3},{2,0},{3,1},{4,6},{5,7},{6,4},{7,5},{8,10},{9,11},{10,... | collective-permute-start | bytes 792584 | tf_op jit(solution)/shard_map/ppermute | solution.py:143
  25.0 14.5 %collective-permute-start.12 = (bf16[576,2048]{1,0:T(8,128)(2,1)S(1)}, bf16[576,2048]{1,0:T(8,128)(2,1)S(1)}, u32[]{:S(2)}, u32[]{:S(2)}) collective-permute-start(bf16[576,2048]{1,0:T(8,128)(2,1)S(1)} %pad_maximum_fusion.1), channel_id=1, source_target_pairs={{0,16},{16,0},{1,17},{17,1},{2,18},{18,2},{3,19},{19,3},{4,20},{20... | collective-permute-start | bytes 7077896 | tf_op jit(solution)/shard_map/ppermute | solution.py:133
  25.0 11.7 %collective-permute-start.14 = (bf16[32,2048]{1,0:T(8,128)(2,1)S(1)}, bf16[32,2048]{1,0:T(8,128)(2,1)S(1)}, u32[]{:S(2)}, u32[]{:S(2)}) collective-permute-start(bf16[32,2048]{1,0:T(8,128)(2,1)S(1)} %slice.117), channel_id=1, source_target_pairs={{0,2},{1,3},{2,0},{3,1},{4,6},{5,7},{6,4},{7,5},{8,10},{9,11},{10,... | collective-permute-start | bytes 393224 | tf_op jit(solution)/shard_map/ppermute | solution.py:143
  26.6 10.2 %collective-permute-start.15 = (bf16[32,2048]{1,0:T(8,128)(2,1)S(1)}, bf16[32,2048]{1,0:T(8,128)(2,1)S(1)}, u32[]{:S(2)}, u32[]{:S(2)}) collective-permute-start(bf16[32,2048]{1,0:T(8,128)(2,1)S(1)} %slice.118), channel_id=1, source_target_pairs={{0,1},{1,0},{2,3},{3,2},{4,5},{5,4},{6,7},{7,6},{8,9},{9,8},{10,11... | collective-permute-start | bytes 393224 | tf_op jit(solution)/shard_map/ppermute | solution.py:143
  33.5 5.1 %collective-permute-start.9 = (bf16[32,2064]{1,0:T(8,128)(2,1)S(1)}, bf16[32,2064]{1,0:T(8,128)(2,1)S(1)}, u32[]{:S(2)}, u32[]{:S(2)}) collective-permute-start(bf16[32,2064]{1,0:T(8,128)(2,1)S(1)} %slice.112), channel_id=1, source_target_pairs={{0,2},{1,3},{2,0},{3,1},{4,6},{5,7},{6,4},{7,5},{8,10},{9,11},{10,... | collective-permute-start | bytes 396296 | tf_op jit(solution)/shard_map/ppermute | solution.py:143
  34.1 5.1 %collective-permute-start.10 = (bf16[32,2064]{1,0:T(8,128)(2,1)S(1)}, bf16[32,2064]{1,0:T(8,128)(2,1)S(1)}, u32[]{:S(2)}, u32[]{:S(2)}) collective-permute-start(bf16[32,2064]{1,0:T(8,128)(2,1)S(1)} %slice.113), channel_id=1, source_target_pairs={{0,1},{1,0},{2,3},{3,2},{4,5},{5,4},{6,7},{7,6},{8,9},{9,8},{10,11... | collective-permute-start | bytes 396296 | tf_op jit(solution)/shard_map/ppermute | solution.py:143
  36.8 23.3 %collective-permute-start.20 = (bf16[256,2048]{1,0:T(8,128)(2,1)S(1)}, bf16[256,2048]{1,0:T(8,128)(2,1)S(1)}, u32[]{:S(2)}, u32[]{:S(2)}) collective-permute-start(bf16[256,2048]{1,0:T(8,128)(2,1)S(1)} %constant_dynamic-update-slice_fusion.12.rows), channel_id=1, source_target_pairs={{0,16},{16,0},{1,17},{17,1},{2,18},{18,2},{3,19},{19,3},{4,20},{20... | collective-permute-start | bytes 3145736 | tf_op jit(solution)/shard_map/ppermute | solution.py:133
  44.4 15.7 %collective-permute-start.21 = (bf16[256,2048]{1,0:T(8,128)(2,1)S(1)}, bf16[256,2048]{1,0:T(8,128)(2,1)S(1)}, u32[]{:S(2)}, u32[]{:S(2)}) collective-permute-start(bf16[256,2048]{1,0:T(8,128)(2,1)S(1)} %slice.115.upstream), channel_id=1, source_target_pairs={{0,16},{16,0},{1,17},{17,1},{2,18},{18,2},{3,19},{19,3},{4,20},{20... | collective-permute-start | bytes 3145736 | tf_op jit(solution)/shard_map/ppermute | solution.py:133
  44.6 10.1 %collective-permute-start.18 = (bf16[64,2048]{1,0:T(8,128)(2,1)S(1)}, bf16[64,2048]{1,0:T(8,128)(2,1)S(1)}, u32[]{:S(2)}, u32[]{:S(2)}) collective-permute-start(bf16[64,2048]{1,0:T(8,128)(2,1)S(1)} %get-tuple-element.46), channel_id=1, source_target_pairs={{0,3},{1,2},{2,1},{3,0},{4,7},{5,6},{6,5},{7,4},{8,11},{9,10},{10,... | collective-permute-start | bytes 786440 | tf_op jit(solution)/shard_map/ppermute | solution.py:143
  46.1 13.7 %collective-permute-start.17 = (bf16[64,2048]{1,0:T(8,128)(2,1)S(1)}, bf16[64,2048]{1,0:T(8,128)(2,1)S(1)}, u32[]{:S(2)}, u32[]{:S(2)}) collective-permute-start(bf16[64,2048]{1,0:T(8,128)(2,1)S(1)} %get-tuple-element.47), channel_id=1, source_target_pairs={{0,2},{1,3},{2,0},{3,1},{4,6},{5,7},{6,4},{7,5},{8,10},{9,11},{10,... | collective-permute-start | bytes 786440 | tf_op jit(solution)/shard_map/ppermute | solution.py:143
  47.6 12.4 %collective-permute-start.16 = (bf16[64,2048]{1,0:T(8,128)(2,1)S(1)}, bf16[64,2048]{1,0:T(8,128)(2,1)S(1)}, u32[]{:S(2)}, u32[]{:S(2)}) collective-permute-start(bf16[64,2048]{1,0:T(8,128)(2,1)S(1)} %get-tuple-element.45), channel_id=1, source_target_pairs={{0,1},{1,0},{2,3},{3,2},{4,5},{5,4},{6,7},{7,6},{8,9},{9,8},{10,11... | collective-permute-start | bytes 786440 | tf_op jit(solution)/shard_map/ppermute | solution.py:143
  54.7 5.4 %collective-permute-start.19 = (bf16[256,576]{1,0:T(8,128)(2,1)S(1)}, bf16[256,576]{1,0:T(8,128)(2,1)S(1)}, u32[]{:S(2)}, u32[]{:S(2)}) collective-permute-start(bf16[256,576]{1,0:T(8,128)(2,1)S(1)} %pad_maximum_fusion.4), channel_id=1, source_target_pairs={{0,16},{16,0},{1,17},{17,1},{2,18},{18,2},{3,19},{19,3},{4,20},{20... | collective-permute-start | bytes 884744 | tf_op jit(solution)/shard_map/ppermute | solution.py:133
  60.2 7.0 %collective-permute-start.24 = (bf16[16,2048]{1,0:T(8,128)(2,1)S(1)}, bf16[16,2048]{1,0:T(8,128)(2,1)S(1)}, u32[]{:S(2)}, u32[]{:S(2)}) collective-permute-start(bf16[16,2048]{1,0:T(8,128)(2,1)S(1)} %get-tuple-element.50), channel_id=1, source_target_pairs={{0,4},{1,5},{2,6},{3,7},{4,8},{5,9},{6,10},{7,11},{8,12},{9,13},{1... | collective-permute-start | bytes 196616 | tf_op jit(solution)/shard_map/ppermute | solution.py:137
  62.2 6.7 %collective-permute-start.23 = (bf16[16,2048]{1,0:T(8,128)(2,1)S(1)}, bf16[16,2048]{1,0:T(8,128)(2,1)S(1)}, u32[]{:S(2)}, u32[]{:S(2)}) collective-permute-start(bf16[16,2048]{1,0:T(8,128)(2,1)S(1)} %get-tuple-element.51), channel_id=1, source_target_pairs={{0,8},{1,9},{2,10},{3,11},{4,12},{5,13},{6,14},{7,15},{8,0},{9,1},... | collective-permute-start | bytes 196616 | tf_op jit(solution)/shard_map/ppermute | solution.py:137
  63.4 5.6 %collective-permute-start.22 = (bf16[16,2048]{1,0:T(8,128)(2,1)S(1)}, bf16[16,2048]{1,0:T(8,128)(2,1)S(1)}, u32[]{:S(2)}, u32[]{:S(2)}) collective-permute-start(bf16[16,2048]{1,0:T(8,128)(2,1)S(1)} %get-tuple-element.49), channel_id=1, source_target_pairs={{0,12},{1,13},{2,14},{3,15},{4,0},{5,1},{6,2},{7,3},{8,4},{9,5},{1... | collective-permute-start | bytes 196616 | tf_op jit(solution)/shard_map/ppermute | solution.py:137
  (7 other events, 13.2 us)

commit v12 on v11

--- a/solution.py
+++ b/solution.py
@@ -145,6 +145,7 @@
 
 VMEM = pl.BlockSpec(memory_space=pltpu.VMEM)
 ANY = pl.BlockSpec(memory_space=pl.ANY)
+LANES = 128
 NT = (((1,), (1,)), ((), ()))
 TN = (((0,), (0,)), ((), ()))
 
@@ -164,18 +165,7 @@
     )(*args)
 
 
-def read_kernel(
-    ids_hbm, gates_hbm, packing_hbm, tokens_hbm, cotangent_hbm,
-    table_ref, tokens_ref, cotangent_ref,
-    ids_ref, gates_ref, packing_ref, ready,
-):
-    pairs = [
-        (ids_hbm, ids_ref),
-        (gates_hbm, gates_ref),
-        (packing_hbm, packing_ref),
-        (tokens_hbm, tokens_ref),
-        (cotangent_hbm, cotangent_ref),
-    ]
+def fetch(ready, *pairs):
     copies = [
         pltpu.make_async_copy(source, target, ready.at[index])
         for index, (source, target) in enumerate(pairs)
@@ -184,40 +174,81 @@
         copy.start()
     for copy in copies:
         copy.wait()
+
+
+def weights_kernel(gate_hbm, up_hbm, down_hbm, weights_ref, ready):
+    half = gate_hbm.shape[1]
+    sources = (gate_hbm, up_hbm, down_hbm)
+    fetch(
+        ready,
+        *(
+            (source.at[0], weights_ref.at[index * half : (index + 1) * half])
+            for index, source in enumerate(sources)
+        ),
+    )
+
+
+def rows_kernel(
+    ids_hbm, gates_hbm, packing_hbm, tokens_hbm, cotangent_hbm, rows_ref,
+    ids_ref, gates_ref, packing_ref, ready,
+):
+    width = tokens_hbm.shape[1]
+    fetch(
+        ready,
+        (tokens_hbm, rows_ref.at[:, :width]),
+        (cotangent_hbm, rows_ref.at[:, width : 2 * width]),
+        (ids_hbm, ids_ref),
+        (gates_hbm, gates_ref),
+        (packing_hbm, packing_ref),
+    )
     slots = packing_ref.shape[1]
-    count = table_ref.shape[0] - 16
-    labels = lax.broadcasted_iota(jnp.int32, (count, slots), 0)
-    total = jnp.zeros((count, slots), jnp.float32)
+    labels = lax.broadcasted_iota(jnp.int32, (LANES, slots), 0)
+    table = jnp.where(labels == LANES - 1, packing_ref[...].astype(jnp.float32), 0.0)
     for k in range(ids_ref.shape[0]):
         named = labels == ids_ref[k : k + 1, :]
-        total = total + jnp.where(named, gates_ref[k : k + 1, :].astype(jnp.float32), 0.0)
-    table_ref[:count, :] = total.astype(jnp.bfloat16)
-    lists = jnp.broadcast_to(packing_ref[...], (16, slots)).astype(jnp.float32)
-    table_ref[count:, :] = lists.astype(jnp.bfloat16)
-
-
-def payload_kernel(table_ref, other_ref, cotangent_ref, payload_ref, here_ref):
-    rows, width = cotangent_ref.shape
-    count = table_ref.shape[0] - 16
-    slots = table_ref.shape[1]
-    homes = lax.broadcasted_iota(jnp.int32, (rows, slots), 0) + lax.axis_index("dp") * rows
-    gates = jnp.zeros((rows, count), jnp.float32)
-    for ref in (table_ref, other_ref):
-        lists = ref[count:, :].astype(jnp.float32)[:1, :]
-        matched = (lists == homes.astype(jnp.float32)).astype(jnp.float32).astype(jnp.bfloat16)
-        gates = gates + lax.dot_general(
-            matched, ref[:count, :], NT, preferred_element_type=jnp.float32
-        )
-    payload_ref[:, :width] = cotangent_ref[...]
-    payload_ref[:, width:] = gates.astype(jnp.bfloat16)
+        table = table + jnp.where(named, gates_ref[k : k + 1, :].astype(jnp.float32), 0.0)
+    across = lax.broadcasted_iota(jnp.int32, (slots, slots), 0)
+    down = lax.broadcasted_iota(jnp.int32, (slots, slots), 1)
+    same = (across == down).astype(jnp.float32).astype(jnp.bfloat16)
+    routing = lax.dot_general(
+        same, table.astype(jnp.bfloat16), NT, preferred_element_type=jnp.float32
+    )
+    rows_ref[:, 2 * width :] = routing.astype(jnp.bfloat16)
+
+
+def column_kernel(*refs):
+    column_ref, routing_ref = refs[-2:]
+    depth = refs[0].shape[0]
+    for index, ref in enumerate(refs[:-2]):
+        span = slice(index * depth, (index + 1) * depth)
+        column_ref[span, :] = ref[...]
+        routing_ref[span, :] = ref[:, ref.shape[1] - LANES :]
+
+
+def gates_kernel(own_ref, other_ref, gates_ref, here_ref):
+    outer = 4
+    depth = own_ref.shape[0] // outer
+    homes = lax.broadcasted_iota(jnp.int32, (depth, depth), 1) + lax.axis_index("dp") * depth
+    for index in range(outer):
+        span = slice(index * depth, (index + 1) * depth)
+        gates = jnp.zeros((depth, LANES), jnp.float32)
+        for ref in (own_ref, other_ref):
+            routing = ref[span, :]
+            held = routing.astype(jnp.float32)[:, LANES - 1 :]
+            matched = (held == homes.astype(jnp.float32)).astype(jnp.float32)
+            gates = gates + lax.dot_general(
+                matched.astype(jnp.bfloat16), routing, TN, preferred_element_type=jnp.float32
+            )
+        gates_ref[span, :] = gates.astype(jnp.bfloat16)
     lanes = lax.broadcasted_iota(jnp.int32, here_ref.shape, 1)
     here_ref[...] = (lanes == lax.axis_index("expert")).astype(jnp.float32)
 
 
-def weight_kernel(own_grads, other_grads, rows, other_rows, upstream, other_upstream, *outs):
-    half = outs[0].shape[1]
+def weight_kernel(own_grads, other_grads, rows, other_rows, *outs):
+    half, width = outs[0].shape[1:]
     for index, out in enumerate(outs):
-        own, other = (upstream, other_upstream) if index == 2 else (rows, other_rows)
+        side = slice(width, 2 * width) if index == 2 else slice(0, width)
+        own, other = rows.at[:, side], other_rows.at[:, side]
         span = slice(index * half, (index + 1) * half)
         step = min(out.shape[-1], 1024)
         for left in range(0, out.shape[-1], step):
@@ -271,49 +302,52 @@
     row_count = tokens.shape[0]
     low = jnp.bfloat16
     ids, gates, lists = expert_ids.T, gate_values.T, packing.reshape(1, row_count)
-    token_blocks = along_outer(tokens, count, inner)
-    table, own_tokens, own_cotangent = on_chip(
-        read_kernel,
-        [
-            ((count + 16, row_count), low),
-            (tokens.shape, low),
-            (cotangent.shape, low),
-        ],
+    copies = dict(spec=ANY, limit=False)
+    (own_rows,) = on_chip(
+        rows_kernel,
+        [((row_count, 2 * model_width + LANES), low)],
         ids,
         gates,
         lists,
         tokens,
         cotangent,
-        spec=ANY,
-        limit=False,
         scratch=[
             pltpu.VMEM(ids.shape, ids.dtype),
             pltpu.VMEM(gates.shape, gates.dtype),
             pltpu.VMEM(lists.shape, lists.dtype),
             pltpu.SemaphoreType.DMA((5,)),
         ],
-    )
-    payload, here = on_chip(
-        payload_kernel,
-        [((row_count, model_width + count), low), ((8, count), jnp.float32)],
-        table,
-        swap(table),
-        own_cotangent,
-    )
-    token_column = jnp.concatenate([own_tokens, *token_blocks[1:]], axis=0)
-    payload, token_column = lax.optimization_barrier((payload, token_column))
-    upstream_column = jnp.concatenate(along_outer(payload, count, inner), axis=0)
-    token_columns = across_inner(token_column, count, inner)
-    own_weights = jnp.concatenate([w_gate[0], w_up[0], w_down[0]], axis=0)
-    sent_weights, token_columns[1] = lax.optimization_barrier((own_weights, token_columns[1]))
-    other = swap(sent_weights)
-    inputs = jnp.concatenate(token_columns, axis=0)
-    other_inputs = swap(inputs)
-    upstream = jnp.concatenate(across_inner(upstream_column, count, inner), axis=0)
-    gate = jnp.sum(
-        upstream[:, model_width:].astype(jnp.float32) * here[:1], axis=1, keepdims=True
-    )
-    upstream = upstream[:, :model_width]
+        **copies,
+    )
+    (own_weights,) = on_chip(
+        weights_kernel,
+        [((3 * half, model_width), low)],
+        w_gate,
+        w_up,
+        w_down,
+        scratch=[pltpu.SemaphoreType.DMA((3,))],
+        **copies,
+    )
+    depth = row_count * count // inner
+    column, routing = on_chip(
+        column_kernel,
+        [((depth, 2 * model_width + LANES), low), ((depth, LANES), low)],
+        *along_outer(own_rows, count, inner),
+    )
+    gates, here = on_chip(
+        gates_kernel,
+        [((depth, LANES), low), ((8, LANES), jnp.float32)],
+        routing,
+        swap(routing),
+    )
+    gates = jnp.concatenate(
+        [gates] + [swap_inner(gates, count, partner) for partner in range(1, inner)], axis=0
+    )
+    own_weights, column = lax.optimization_barrier((own_weights, column))
+    other = swap(own_weights)
+    rows = jnp.concatenate(across_inner(column, count, inner), axis=0)
+    inputs, upstream = rows[:, :model_width], rows[:, model_width : 2 * model_width]
+    gate = jnp.sum(gates.astype(jnp.float32) * here[:1], axis=1, keepdims=True)
     gate_up = jnp.concatenate(
         [own_weights[:half], other[:half], own_weights[half : 2 * half], other[half : 2 * half]],
         axis=0,
@@ -335,11 +369,11 @@
     grads = (gate_grad, up_grad, hidden)
     own_grads = jnp.concatenate([grad[:, :half] for grad in grads], axis=1)
     sent_grads = jnp.concatenate([grad[:, half:] for grad in grads], axis=1)
-    sent_grads, upstream, _ = lax.optimization_barrier((sent_grads, upstream, partial_grad))
+    sent_grads, rows, _ = lax.optimization_barrier((sent_grads, rows, partial_grad))
     other_grads = swap(sent_grads)
-    other_upstream = swap(upstream)
-    column_sum, other_grads, other_inputs, other_upstream = lax.optimization_barrier(
-        (column_sum, other_grads, other_inputs, other_upstream)
+    other_rows = swap(rows)
+    column_sum, other_grads, other_rows = lax.optimization_barrier(
+        (column_sum, other_grads, other_rows)
     )
     input_grad = return_outer(column_sum, count, inner)
     weight_grads = on_chip(
@@ -347,10 +381,8 @@
         [((1, half, model_width), low)] * 3,
         own_grads,
         other_grads,
-        inputs,
-        other_inputs,
-        upstream,
-        other_upstream,
+        rows,
+        other_rows,
     )
     return (input_grad, *weight_grads)
 

time: 69.9 us -> 75.9 us (1.086)
  waiting for transfers between devices: 27.6 us -> 36.2 us
  starting transfers between devices: 28.6 us -> 24 us
  Pallas kernels: 4.21 us -> 7.57 us
  other arithmetic: 3.01 us -> 1.18 us
    ppermute x11 -> x10, waiting for transfers between devices: 20.5 us -> 26.8 us  [swap_inner(): lax.ppermute(value, 'expert', [(place, place ^ partner) for place in rang...]
    ppermute x9 -> x6, starting transfers between devices: 15.3 us -> 10.8 us  [shift_outer(): lax.ppermute(value, 'expert', [(place, (place + step * inner) % count) fo...]
    pallas_call x3 -> x5, Pallas kernels: 4.21 us -> 7.57 us  [on_chip(): pl.pallas_call(body, out_shape=[jax.ShapeDtypeStruct(shape, dtype) for sh...]
    ppermute x9 -> x6, waiting for transfers between devices: 7.12 us -> 9.42 us  [shift_outer(): lax.ppermute(value, 'expert', [(place, (place + step * inner) % count) fo...]
    slice x1 -> x2, local copies, waits for them, and re-layouts: 0.16 us -> 2.19 us  [dense_local(): down = jnp.concatenate([own_weights[2 * half:], other[2 * half:]], axis=0)]
    concatenate x2 -> x0, other arithmetic: 1.83 us -> none  [the longest x1 1.81 us: dense_local(): own_weights = jnp.concatenate([w_gate[0], w_up[0], w_down[0]], axis=0)]
    unnamed x22 -> x8, local copies, waits for them, and re-layouts: 1.48 us -> 0.17 us
    ppermute x11 -> x10, starting transfers between devices: 13.1 us -> 13.1 us  [swap_inner(): lax.ppermute(value, 'expert', [(place, place ^ partner) for place in rang...]
  transfers between devices with their start and end apart: 25 -> 20, of which waited for: 12 -> 10; matrix products, arithmetic and copies ran while one was open for 9% -> 3% of each run, Pallas kernels for 6% -> 8%
where the time goes in v12:
time: 75.9 us; the launch traced here: 75.7 us
  waiting for transfers between devices  36.2 us (48%)
  starting transfers between devices  24 us (32%)
  Pallas kernels  7.57 us (10%)
  matrix products  3.06 us (4%)
  local copies, waits for them, and re-layouts  2.77 us (4%)
  other arithmetic  1.18 us (2%)
  between operations  0.88 us (1%)
    ppermute x10, waiting for transfers between devices, swap_inner(): lax.ppermute(value, 'expert', [(place, place ^ partner) for place in rang...  26.8 us
    ppermute x10, starting transfers between devices, swap_inner(): lax.ppermute(value, 'expert', [(place, place ^ partner) for place in rang...  13.1 us
    ppermute x6, starting transfers between devices, shift_outer(): lax.ppermute(value, 'expert', [(place, (place + step * inner) % count) fo...  10.8 us
    ppermute x6, waiting for transfers between devices, shift_outer(): lax.ppermute(value, 'expert', [(place, (place + step * inner) % count) fo...  9.42 us
    pallas_call x5, Pallas kernels, on_chip(): pl.pallas_call(body, out_shape=[jax.ShapeDtypeStruct(shape, dtype) for sh...  7.57 us
    slice x2, local copies, waits for them, and re-layouts, dense_local(): down = jnp.concatenate([own_weights[2 * half:], other[2 * half:]], axis=0)  2.19 us
  transfers between devices with their start and end apart: 20, of which 10 were waited for; matrix products, arithmetic and copies ran while one was open for 3% of the time, Pallas kernels for 8%

profile of v12, /device:TPU:0, one launch (start us, length us, event | category | flops | bytes accessed | tf_op | source)
XLA Modules:
  0.0 75.7 jit_solution(13081339626655772304)
XLA Ops:
  0.6 1.8 %shard_map.111.refs_0_ = bf16[16,4224]{1,0:T(8,128)(2,1)} custom-call(s32[8,16]{1,0:T(8,128)} %bitcast.5, bf16[8,16]{1,0:T(8,128)(2,1)} %bitcast.6, s32[1,16]{1,0:T(1,128)} %bitcast.7, bf16[16,2048]{1,0:T(8,128)(2,1)} %tokens_hbm.1, bf16[16,2048]{1,0:T(8,128)(2,1)} %cotangent_hbm.1), custom_call_target="tpu_custom_call" | custom-call | bytes 267072 | tf_op jit(solution)/shard_map/pallas_call | solution.py:157
  2.4 5.1 %collective-permute-start.2 = (bf16[16,4224]{1,0:T(8,128)(2,1)}, bf16[16,4224]{1,0:T(8,128)(2,1)S(1)}, u32[]{:S(2)}, u32[]{:S(2)}) collective-permute-start(bf16[16,4224]{1,0:T(8,128)(2,1)} %shard_map.111.refs_0_), channel_id=1, source_target_pairs={{0,12},{1,13},{2,14},{3,15},{4,0},{5,1},{6,2},{7,3},{8,4},{9,5},{1... | collective-permute-start | bytes 405512 | tf_op jit(solution)/shard_map/ppermute | solution.py:137
  7.5 1.0 %collective-permute-start = (bf16[16,4224]{1,0:T(8,128)(2,1)}, bf16[16,4224]{1,0:T(8,128)(2,1)S(1)}, u32[]{:S(2)}, u32[]{:S(2)}) collective-permute-start(bf16[16,4224]{1,0:T(8,128)(2,1)} %shard_map.111.refs_0_), channel_id=1, source_target_pairs={{0,4},{1,5},{2,6},{3,7},{4,8},{5,9},{6,10},{7,11},{8,12},{9,13},{1... | collective-permute-start | bytes 405512 | tf_op jit(solution)/shard_map/ppermute | solution.py:137
  8.5 3.1 %shard_map.114 = bf16[576,2048]{1,0:T(8,128)(2,1)} custom-call(bf16[1,192,2048]{2,1,0:T(8,128)(2,1)} %gate_hbm.1, bf16[1,192,2048]{2,1,0:T(8,128)(2,1)} %up_hbm.1, bf16[1,192,2048]{2,1,0:T(8,128)(2,1)} %down_hbm.1), custom_call_target="tpu_custom_call" | custom-call | bytes 4718592 | tf_op jit(solution)/shard_map/pallas_call | solution.py:157
  11.8 7.4 %collective-permute-done.1.refs_2_ = bf16[16,4224]{1,0:T(8,128)(2,1)S(1)} collective-permute-done((bf16[16,4224]{1,0:T(8,128)(2,1)}, bf16[16,4224]{1,0:T(8,128)(2,1)S(1)}, u32[]{:S(2)}, u32[]{:S(2)}) %collective-permute-start.1) | collective-permute-done | bytes 135200 | tf_op jit(solution)/shard_map/ppermute | solution.py:137
  19.3 1.6 %collective-permute-start.8 = (bf16[64,4224]{1,0:T(8,128)(2,1)S(1)}, bf16[64,4224]{1,0:T(8,128)(2,1)S(1)}, u32[]{:S(2)}, u32[]{:S(2)}) collective-permute-start(bf16[64,4224]{1,0:T(8,128)(2,1)S(1)} %get-tuple-element.22), channel_id=1, source_target_pairs={{0,2},{1,3},{2,0},{3,1},{4,6},{5,7},{6,4},{7,5},{8,10},{9,11},{10,... | collective-permute-start | bytes 1622024 | tf_op jit(solution)/shard_map/ppermute | solution.py:143
  20.9 1.5 %collective-permute-start.7 = (bf16[64,4224]{1,0:T(8,128)(2,1)S(1)}, bf16[64,4224]{1,0:T(8,128)(2,1)S(1)}, u32[]{:S(2)}, u32[]{:S(2)}) collective-permute-start(bf16[64,4224]{1,0:T(8,128)(2,1)S(1)} %get-tuple-element.22), channel_id=1, source_target_pairs={{0,1},{1,0},{2,3},{3,2},{4,5},{5,4},{6,7},{7,6},{8,9},{9,8},{10,11... | collective-permute-start | bytes 1622024 | tf_op jit(solution)/shard_map/ppermute | solution.py:143
  22.5 1.9 %fusion.17 = (bf16[192,2048]{1,0:T(8,128)(2,1)S(1)}, bf16[192,2048]{1,0:T(8,128)(2,1)S(1)}, bf16[192,2048]{1,0:T(8,128)(2,1)S(1)}) fusion(bf16[576,2048]{1,0:T(8,128)(2,1)} %shard_map.114), kind=kLoop, calls=%fused_computation.32 | loop fusion | bytes 4718592 | tf_op jit(solution)/shard_map/slice | solution.py:355
  25.2 1.5 %collective-permute-start.5 = (bf16[64,128]{1,0:T(8,128)(2,1)S(1)}, bf16[64,128]{1,0:T(8,128)(2,1)S(1)}, u32[]{:S(2)}, u32[]{:S(2)}) collective-permute-start(bf16[64,128]{1,0:T(8,128)(2,1)S(1)} %get-tuple-element.19), channel_id=1, source_target_pairs={{0,2},{1,3},{2,0},{3,1},{4,6},{5,7},{6,4},{7,5},{8,10},{9,11},{10,... | collective-permute-start | bytes 49160 | tf_op jit(solution)/shard_map/ppermute | solution.py:143
  26.7 1.5 %collective-permute-start.4 = (bf16[64,128]{1,0:T(8,128)(2,1)S(1)}, bf16[64,128]{1,0:T(8,128)(2,1)S(1)}, u32[]{:S(2)}, u32[]{:S(2)}) collective-permute-start(bf16[64,128]{1,0:T(8,128)(2,1)S(1)} %get-tuple-element.19), channel_id=1, source_target_pairs={{0,1},{1,0},{2,3},{3,2},{4,5},{5,4},{6,7},{7,6},{8,9},{9,8},{10,11... | collective-permute-start | bytes 49160 | tf_op jit(solution)/shard_map/ppermute | solution.py:143
  28.2 6.4 %collective-permute-done.6 = bf16[64,128]{1,0:T(8,128)(2,1)S(1)} collective-permute-done((bf16[64,128]{1,0:T(8,128)(2,1)S(1)}, bf16[64,128]{1,0:T(8,128)(2,1)S(1)}, u32[]{:S(2)}, u32[]{:S(2)}) %collective-permute-start.6) | collective-permute-done | bytes 16416 | tf_op jit(solution)/shard_map/ppermute | solution.py:143
  35.0 1.6 %collective-permute-start.10 = (bf16[32,4224]{1,0:T(8,128)(2,1)S(1)}, bf16[32,4224]{1,0:T(8,128)(2,1)S(1)}, u32[]{:S(2)}, u32[]{:S(2)}) collective-permute-start(bf16[32,4224]{1,0:T(8,128)(2,1)S(1)} %slice.117), channel_id=1, source_target_pairs={{0,1},{1,0},{2,3},{3,2},{4,5},{5,4},{6,7},{7,6},{8,9},{9,8},{10,11... | collective-permute-start | bytes 811016 | tf_op jit(solution)/shard_map/ppermute | solution.py:143
  36.6 1.4 %collective-permute-start.9 = (bf16[32,4224]{1,0:T(8,128)(2,1)S(1)}, bf16[32,4224]{1,0:T(8,128)(2,1)S(1)}, u32[]{:S(2)}, u32[]{:S(2)}) collective-permute-start(bf16[32,4224]{1,0:T(8,128)(2,1)S(1)} %slice.116), channel_id=1, source_target_pairs={{0,2},{1,3},{2,0},{3,1},{4,6},{5,7},{6,4},{7,5},{8,10},{9,11},{10,... | collective-permute-start | bytes 811016 | tf_op jit(solution)/shard_map/ppermute | solution.py:143
  38.0 7.0 %collective-permute-done.9 = bf16[32,4224]{1,0:T(8,128)(2,1)S(1)} collective-permute-done((bf16[32,4224]{1,0:T(8,128)(2,1)S(1)}, bf16[32,4224]{1,0:T(8,128)(2,1)S(1)}, u32[]{:S(2)}, u32[]{:S(2)}) %collective-permute-start.9) | collective-permute-done | bytes 270368 | tf_op jit(solution)/shard_map/ppermute | solution.py:143
  45.4 1.0 %fusion.7 = f32[256,768]{1,0:T(8,128)S(1)} fusion(bf16[256,4224]{1,0:T(8,128)(2,1)S(1)} %constant_dynamic-update-slice_fusion.rows, bf16[192,2048]{1,0:T(8,128)(2,1)S(1)} %get-tuple-element.36, bf16[192,2048]{1,0:T(8,128)(2,1)S(1)} %get-tuple-element.33, bf16[192,2048]{1,0:T(8,128)(2,1)S(1)} %get-tuple-element.37, bf16[192,2048]{1,0:T(8,128)(2,1)S(1)} %get-tuple-element.34), kind=kOutput, calls=%fused_computation.7 | convolution fusion | flops 817889280 | bytes 4980736 | tf_op jit(solution)/shard_map/dot_general | solution.py:356
  47.3 1.2 %convolution_convert_fusion = bf16[256,2048]{1,0:T(8,128)(2,1)S(1)} fusion(bf16[192,2048]{1,0:T(8,128)(2,1)S(1)} %get-tuple-element.36, bf16[192,2048]{1,0:T(8,128)(2,1)S(1)} %get-tuple-element.33, bf16[192,2048]{1,0:T(8,128)(2,1)S(1)} %get-tuple-element.37, bf16[192,2048]{1,0:T(8,128)(2,1)S(1)} %get-tuple-element.34, ...), kind=kOutput, calls=%fused_computation.1 | convolution fusion | flops 819200000 | bytes 4587520 | tf_op jit(solution)/shard_map/dot_general | solution.py:366
  49.6 2.4 %collective-permute-start.14 = (bf16[64,2048]{1,0:T(8,128)(2,1)S(1)}, bf16[64,2048]{1,0:T(8,128)(2,1)S(1)}, u32[]{:S(2)}, u32[]{:S(2)}) collective-permute-start(bf16[64,2048]{1,0:T(8,128)(2,1)S(1)} %get-tuple-element.41), channel_id=1, source_target_pairs={{0,3},{1,2},{2,1},{3,0},{4,7},{5,6},{6,5},{7,4},{8,11},{9,10},{10,... | collective-permute-start | bytes 786440 | tf_op jit(solution)/shard_map/ppermute | solution.py:143
  52.6 5.6 %collective-permute-done.12 = bf16[64,2048]{1,0:T(8,128)(2,1)S(1)} collective-permute-done((bf16[64,2048]{1,0:T(8,128)(2,1)S(1)}, bf16[64,2048]{1,0:T(8,128)(2,1)S(1)}, u32[]{:S(2)}, u32[]{:S(2)}) %collective-permute-start.12) | collective-permute-done | bytes 262176 | tf_op jit(solution)/shard_map/ppermute | solution.py:143
  58.2 6.3 %collective-permute-done.14 = bf16[64,2048]{1,0:T(8,128)(2,1)S(1)} collective-permute-done((bf16[64,2048]{1,0:T(8,128)(2,1)S(1)}, bf16[64,2048]{1,0:T(8,128)(2,1)S(1)}, u32[]{:S(2)}, u32[]{:S(2)}) %collective-permute-start.14) | collective-permute-done | bytes 262176 | tf_op jit(solution)/shard_map/ppermute | solution.py:143
  64.5 1.4 %collective-permute-done.13 = bf16[64,2048]{1,0:T(8,128)(2,1)S(1)} collective-permute-done((bf16[64,2048]{1,0:T(8,128)(2,1)S(1)}, bf16[64,2048]{1,0:T(8,128)(2,1)S(1)}, u32[]{:S(2)}, u32[]{:S(2)}) %collective-permute-start.13) | collective-permute-done | bytes 262176 | tf_op jit(solution)/shard_map/ppermute | solution.py:143
  66.7 1.5 %collective-permute-start.19 = (bf16[16,2048]{1,0:T(8,128)(2,1)S(1)}, bf16[16,2048]{1,0:T(8,128)(2,1)S(1)}, u32[]{:S(2)}, u32[]{:S(2)}) collective-permute-start(bf16[16,2048]{1,0:T(8,128)(2,1)S(1)} %get-tuple-element.45), channel_id=1, source_target_pairs={{0,4},{1,5},{2,6},{3,7},{4,8},{5,9},{6,10},{7,11},{8,12},{9,13},{1... | collective-permute-start | bytes 196616 | tf_op jit(solution)/shard_map/ppermute | solution.py:137
  68.1 2.6 %collective-permute-start.18 = (bf16[16,2048]{1,0:T(8,128)(2,1)S(1)}, bf16[16,2048]{1,0:T(8,128)(2,1)S(1)}, u32[]{:S(2)}, u32[]{:S(2)}) collective-permute-start(bf16[16,2048]{1,0:T(8,128)(2,1)S(1)} %get-tuple-element.46), channel_id=1, source_target_pairs={{0,8},{1,9},{2,10},{3,11},{4,12},{5,13},{6,14},{7,15},{8,0},{9,1},... | collective-permute-start | bytes 196616 | tf_op jit(solution)/shard_map/ppermute | solution.py:137
  70.8 2.5 %shard_map.115 = (bf16[1,192,2048]{2,1,0:T(8,128)(2,1)}, bf16[1,192,2048]{2,1,0:T(8,128)(2,1)}, bf16[1,192,2048]{2,1,0:T(8,128)(2,1)}) custom-call(bf16[256,576]{1,0:T(8,128)(2,1)S(1)} %pad_maximum_fusion.4.own_grads, bf16[256,576]{1,0:T(8,128)(2,1)S(1)} %collective-permute-done.15.other_grads, bf16[256,4224]{1,0:T(8,128)(2,1)S(1)} %constant_dynamic-update-slice_fusion.rows, ...), custom_call_target="tpu_custom_call" | custom-call | bytes 7274496 | tf_op jit(solution)/shard_map/pallas_call | solution.py:157
  73.4 1.6 %collective-permute-done.18 = bf16[16,2048]{1,0:T(8,128)(2,1)S(1)} collective-permute-done((bf16[16,2048]{1,0:T(8,128)(2,1)S(1)}, bf16[16,2048]{1,0:T(8,128)(2,1)S(1)}, u32[]{:S(2)}, u32[]{:S(2)}) %collective-permute-start.18) | collective-permute-done | bytes 65568 | tf_op jit(solution)/shard_map/ppermute | solution.py:137
  (48 shorter events, 6.2 us)
Async XLA Ops:
  2.4 16.8 %copy-start = (bf16[16,4224]{1,0:T(8,128)(2,1)S(1)}, bf16[16,4224]{1,0:T(8,128)(2,1)}, u32[]{:S(2)}) copy-start(bf16[16,4224]{1,0:T(8,128)(2,1)} %shard_map.111.refs_0_) | copy-start | bytes 405508
  2.4 9.4 %collective-permute-start.2 = (bf16[16,4224]{1,0:T(8,128)(2,1)}, bf16[16,4224]{1,0:T(8,128)(2,1)S(1)}, u32[]{:S(2)}, u32[]{:S(2)}) collective-permute-start(bf16[16,4224]{1,0:T(8,128)(2,1)} %shard_map.111.refs_0_), channel_id=1, source_target_pairs={{0,12},{1,13},{2,14},{3,15},{4,0},{5,1},{6,2},{7,3},{8,4},{9,5},{1... | collective-permute-start | bytes 405512 | tf_op jit(solution)/shard_map/ppermute | solution.py:137
  7.5 11.7 %collective-permute-start.1 = (bf16[16,4224]{1,0:T(8,128)(2,1)}, bf16[16,4224]{1,0:T(8,128)(2,1)S(1)}, u32[]{:S(2)}, u32[]{:S(2)}) collective-permute-start(bf16[16,4224]{1,0:T(8,128)(2,1)} %shard_map.111.refs_0_), channel_id=1, source_target_pairs={{0,8},{1,9},{2,10},{3,11},{4,12},{5,13},{6,14},{7,15},{8,0},{9,1},... | collective-permute-start | bytes 405512 | tf_op jit(solution)/shard_map/ppermute | solution.py:137
  7.5 11.7 %collective-permute-start = (bf16[16,4224]{1,0:T(8,128)(2,1)}, bf16[16,4224]{1,0:T(8,128)(2,1)S(1)}, u32[]{:S(2)}, u32[]{:S(2)}) collective-permute-start(bf16[16,4224]{1,0:T(8,128)(2,1)} %shard_map.111.refs_0_), channel_id=1, source_target_pairs={{0,4},{1,5},{2,6},{3,7},{4,8},{5,9},{6,10},{7,11},{8,12},{9,13},{1... | collective-permute-start | bytes 405512 | tf_op jit(solution)/shard_map/ppermute | solution.py:137
  19.3 15.7 %collective-permute-start.8 = (bf16[64,4224]{1,0:T(8,128)(2,1)S(1)}, bf16[64,4224]{1,0:T(8,128)(2,1)S(1)}, u32[]{:S(2)}, u32[]{:S(2)}) collective-permute-start(bf16[64,4224]{1,0:T(8,128)(2,1)S(1)} %get-tuple-element.22), channel_id=1, source_target_pairs={{0,2},{1,3},{2,0},{3,1},{4,6},{5,7},{6,4},{7,5},{8,10},{9,11},{10,... | collective-permute-start | bytes 1622024 | tf_op jit(solution)/shard_map/ppermute | solution.py:143
  20.9 15.7 %collective-permute-start.7 = (bf16[64,4224]{1,0:T(8,128)(2,1)S(1)}, bf16[64,4224]{1,0:T(8,128)(2,1)S(1)}, u32[]{:S(2)}, u32[]{:S(2)}) collective-permute-start(bf16[64,4224]{1,0:T(8,128)(2,1)S(1)} %get-tuple-element.22), channel_id=1, source_target_pairs={{0,1},{1,0},{2,3},{3,2},{4,5},{5,4},{6,7},{7,6},{8,9},{9,8},{10,11... | collective-permute-start | bytes 1622024 | tf_op jit(solution)/shard_map/ppermute | solution.py:143
  22.4 12.2 %copy-start.1 = (bf16[576,2048]{1,0:T(8,128)(2,1)S(1)}, bf16[576,2048]{1,0:T(8,128)(2,1)}, u32[]{:S(2)}) copy-start(bf16[576,2048]{1,0:T(8,128)(2,1)} %shard_map.114) | copy-start | bytes 7077892
  22.4 2.0 %collective-permute-start.3 = (bf16[64,128]{1,0:T(8,128)(2,1)S(1)}, bf16[64,128]{1,0:T(8,128)(2,1)S(1)}, u32[]{:S(2)}, u32[]{:S(2)}) collective-permute-start(bf16[64,128]{1,0:T(8,128)(2,1)S(1)} %get-tuple-element.18.own_ref), channel_id=1, source_target_pairs={{0,16},{16,0},{1,17},{17,1},{2,18},{18,2},{3,19},{19,3},{4,20},{20... | collective-permute-start | bytes 49160 | tf_op jit(solution)/shard_map/ppermute | solution.py:133
  24.7 9.9 %collective-permute-start.6 = (bf16[64,128]{1,0:T(8,128)(2,1)S(1)}, bf16[64,128]{1,0:T(8,128)(2,1)S(1)}, u32[]{:S(2)}, u32[]{:S(2)}) collective-permute-start(bf16[64,128]{1,0:T(8,128)(2,1)S(1)} %get-tuple-element.19), channel_id=1, source_target_pairs={{0,3},{1,2},{2,1},{3,0},{4,7},{5,6},{6,5},{7,4},{8,11},{9,10},{10,... | collective-permute-start | bytes 49160 | tf_op jit(solution)/shard_map/ppermute | solution.py:143
  25.2 9.4 %collective-permute-start.5 = (bf16[64,128]{1,0:T(8,128)(2,1)S(1)}, bf16[64,128]{1,0:T(8,128)(2,1)S(1)}, u32[]{:S(2)}, u32[]{:S(2)}) collective-permute-start(bf16[64,128]{1,0:T(8,128)(2,1)S(1)} %get-tuple-element.19), channel_id=1, source_target_pairs={{0,2},{1,3},{2,0},{3,1},{4,6},{5,7},{6,4},{7,5},{8,10},{9,11},{10,... | collective-permute-start | bytes 49160 | tf_op jit(solution)/shard_map/ppermute | solution.py:143
  26.7 8.1 %collective-permute-start.4 = (bf16[64,128]{1,0:T(8,128)(2,1)S(1)}, bf16[64,128]{1,0:T(8,128)(2,1)S(1)}, u32[]{:S(2)}, u32[]{:S(2)}) collective-permute-start(bf16[64,128]{1,0:T(8,128)(2,1)S(1)} %get-tuple-element.19), channel_id=1, source_target_pairs={{0,1},{1,0},{2,3},{3,2},{4,5},{5,4},{6,7},{7,6},{8,9},{9,8},{10,11... | collective-permute-start | bytes 49160 | tf_op jit(solution)/shard_map/ppermute | solution.py:143
  34.6 10.5 %collective-permute-start.11 = (bf16[576,2048]{1,0:T(8,128)(2,1)S(1)}, bf16[576,2048]{1,0:T(8,128)(2,1)S(1)}, u32[]{:S(2)}, u32[]{:S(2)}) collective-permute-start(bf16[576,2048]{1,0:T(8,128)(2,1)S(1)} %copy-done.1), channel_id=1, source_target_pairs={{0,16},{16,0},{1,17},{17,1},{2,18},{18,2},{3,19},{19,3},{4,20},{20... | collective-permute-start | bytes 7077896 | tf_op jit(solution)/shard_map/ppermute | solution.py:133
  35.0 10.1 %collective-permute-start.10 = (bf16[32,4224]{1,0:T(8,128)(2,1)S(1)}, bf16[32,4224]{1,0:T(8,128)(2,1)S(1)}, u32[]{:S(2)}, u32[]{:S(2)}) collective-permute-start(bf16[32,4224]{1,0:T(8,128)(2,1)S(1)} %slice.117), channel_id=1, source_target_pairs={{0,1},{1,0},{2,3},{3,2},{4,5},{5,4},{6,7},{7,6},{8,9},{9,8},{10,11... | collective-permute-start | bytes 811016 | tf_op jit(solution)/shard_map/ppermute | solution.py:143
  36.6 8.5 %collective-permute-start.9 = (bf16[32,4224]{1,0:T(8,128)(2,1)S(1)}, bf16[32,4224]{1,0:T(8,128)(2,1)S(1)}, u32[]{:S(2)}, u32[]{:S(2)}) collective-permute-start(bf16[32,4224]{1,0:T(8,128)(2,1)S(1)} %slice.116), channel_id=1, source_target_pairs={{0,2},{1,3},{2,0},{3,1},{4,6},{5,7},{6,4},{7,5},{8,10},{9,11},{10,... | collective-permute-start | bytes 811016 | tf_op jit(solution)/shard_map/ppermute | solution.py:143
  48.9 17.1 %collective-permute-start.16 = (bf16[256,4224]{1,0:T(8,128)(2,1)S(1)}, bf16[256,4224]{1,0:T(8,128)(2,1)S(1)}, u32[]{:S(2)}, u32[]{:S(2)}) collective-permute-start(bf16[256,4224]{1,0:T(8,128)(2,1)S(1)} %constant_dynamic-update-slice_fusion.rows), channel_id=1, source_target_pairs={{0,16},{16,0},{1,17},{17,1},{2,18},{18,2},{3,19},{19,3},{4,20},{20... | collective-permute-start | bytes 6488072 | tf_op jit(solution)/shard_map/ppermute | solution.py:133
  49.0 9.2 %collective-permute-start.12 = (bf16[64,2048]{1,0:T(8,128)(2,1)S(1)}, bf16[64,2048]{1,0:T(8,128)(2,1)S(1)}, u32[]{:S(2)}, u32[]{:S(2)}) collective-permute-start(bf16[64,2048]{1,0:T(8,128)(2,1)S(1)} %get-tuple-element.40), channel_id=1, source_target_pairs={{0,1},{1,0},{2,3},{3,2},{4,5},{5,4},{6,7},{7,6},{8,9},{9,8},{10,11... | collective-permute-start | bytes 786440 | tf_op jit(solution)/shard_map/ppermute | solution.py:143
  49.6 14.8 %collective-permute-start.14 = (bf16[64,2048]{1,0:T(8,128)(2,1)S(1)}, bf16[64,2048]{1,0:T(8,128)(2,1)S(1)}, u32[]{:S(2)}, u32[]{:S(2)}) collective-permute-start(bf16[64,2048]{1,0:T(8,128)(2,1)S(1)} %get-tuple-element.41), channel_id=1, source_target_pairs={{0,3},{1,2},{2,1},{3,0},{4,7},{5,6},{6,5},{7,4},{8,11},{9,10},{10,... | collective-permute-start | bytes 786440 | tf_op jit(solution)/shard_map/ppermute | solution.py:143
  52.1 13.8 %collective-permute-start.13 = (bf16[64,2048]{1,0:T(8,128)(2,1)S(1)}, bf16[64,2048]{1,0:T(8,128)(2,1)S(1)}, u32[]{:S(2)}, u32[]{:S(2)}) collective-permute-start(bf16[64,2048]{1,0:T(8,128)(2,1)S(1)} %get-tuple-element.42), channel_id=1, source_target_pairs={{0,2},{1,3},{2,0},{3,1},{4,6},{5,7},{6,4},{7,5},{8,10},{9,11},{10,... | collective-permute-start | bytes 786440 | tf_op jit(solution)/shard_map/ppermute | solution.py:143
  52.6 13.4 %collective-permute-start.15 = (bf16[256,576]{1,0:T(8,128)(2,1)S(1)}, bf16[256,576]{1,0:T(8,128)(2,1)S(1)}, u32[]{:S(2)}, u32[]{:S(2)}) collective-permute-start(bf16[256,576]{1,0:T(8,128)(2,1)S(1)} %pad_maximum_fusion.3), channel_id=1, source_target_pairs={{0,16},{16,0},{1,17},{17,1},{2,18},{18,2},{3,19},{19,3},{4,20},{20... | collective-permute-start | bytes 884744 | tf_op jit(solution)/shard_map/ppermute | solution.py:133
  66.0 7.2 %collective-permute-start.17 = (bf16[16,2048]{1,0:T(8,128)(2,1)S(1)}, bf16[16,2048]{1,0:T(8,128)(2,1)S(1)}, u32[]{:S(2)}, u32[]{:S(2)}) collective-permute-start(bf16[16,2048]{1,0:T(8,128)(2,1)S(1)} %get-tuple-element.44), channel_id=1, source_target_pairs={{0,12},{1,13},{2,14},{3,15},{4,0},{5,1},{6,2},{7,3},{8,4},{9,5},{1... | collective-permute-start | bytes 196616 | tf_op jit(solution)/shard_map/ppermute | solution.py:137
  66.7 6.8 %collective-permute-start.19 = (bf16[16,2048]{1,0:T(8,128)(2,1)S(1)}, bf16[16,2048]{1,0:T(8,128)(2,1)S(1)}, u32[]{:S(2)}, u32[]{:S(2)}) collective-permute-start(bf16[16,2048]{1,0:T(8,128)(2,1)S(1)} %get-tuple-element.45), channel_id=1, source_target_pairs={{0,4},{1,5},{2,6},{3,7},{4,8},{5,9},{6,10},{7,11},{8,12},{9,13},{1... | collective-permute-start | bytes 196616 | tf_op jit(solution)/shard_map/ppermute | solution.py:137
  68.1 6.9 %collective-permute-start.18 = (bf16[16,2048]{1,0:T(8,128)(2,1)S(1)}, bf16[16,2048]{1,0:T(8,128)(2,1)S(1)}, u32[]{:S(2)}, u32[]{:S(2)}) collective-permute-start(bf16[16,2048]{1,0:T(8,128)(2,1)S(1)} %get-tuple-element.46), channel_id=1, source_target_pairs={{0,8},{1,9},{2,10},{3,11},{4,12},{5,13},{6,14},{7,15},{8,0},{9,1},... | collective-permute-start | bytes 196616 | tf_op jit(solution)/shard_map/ppermute | solution.py:137

commit v13 on v11

--- a/solution.py
+++ b/solution.py
@@ -214,35 +214,47 @@
     here_ref[...] = (lanes == lax.axis_index("expert")).astype(jnp.float32)
 
 
-def weight_kernel(own_grads, other_grads, rows, other_rows, upstream, other_upstream, *outs):
-    half = outs[0].shape[1]
+def weight_kernel(own_grads, other_grads, rows, other_rows, upstream, other_near, other_far, *outs):
+    half, width = outs[0].shape[1:]
+    height, cut = rows.shape[0], other_near.shape[0]
+    step = min(width, 1024)
     for index, out in enumerate(outs):
-        own, other = (upstream, other_upstream) if index == 2 else (rows, other_rows)
         span = slice(index * half, (index + 1) * half)
-        step = min(out.shape[-1], 1024)
-        for left in range(0, out.shape[-1], step):
+        terms = [(own_grads, slice(0, height), rows), (other_grads, slice(0, height), other_rows)]
+        if index == 2:
+            terms = [
+                (own_grads, slice(0, height), upstream),
+                (other_grads, slice(0, cut), other_near),
+                (other_grads, slice(cut, height), other_far),
+            ]
+        for left in range(0, width, step):
             columns = slice(left, left + step)
-            total = lax.dot_general(
-                own_grads[:, span], own[:, columns], TN, preferred_element_type=jnp.float32
-            ) + lax.dot_general(
-                other_grads[:, span], other[:, columns], TN, preferred_element_type=jnp.float32
-            )
+            total = jnp.zeros((half, step), jnp.float32)
+            for grads, part, values in terms:
+                total = total + lax.dot_general(
+                    grads[part, span], values[:, columns], TN, preferred_element_type=jnp.float32
+                )
             out[0, :, columns] = total.astype(jnp.bfloat16)
+
+
+def stack_kernel(*refs):
+    low = 0
+    for ref in refs[:-1]:
+        refs[-1][low : low + ref.shape[0], :] = ref[...]
+        low += ref.shape[0]
 
 
 def along_outer(value, count, inner):
     return [value] + [shift_outer(value, count, inner, step) for step in range(1, count // inner)]
 
 
-def across_inner(column, count, inner):
-    if inner < 4:
-        return [column] + [swap_inner(column, count, partner) for partner in range(1, inner)]
-    cut = column.shape[0] // 2
-    first = swap_inner(column, count, 1)
-    second = swap_inner(column, count, 2)
-    far_top = swap_inner(first[:cut], count, 2)
-    far_bottom = swap_inner(second[cut:], count, 1)
-    return [column, first, second, far_top, far_bottom]
+def near_inner(column, count):
+    return [swap_inner(column, count, 1), swap_inner(column, count, 2)]
+
+
+def far_inner(near, count):
+    cut = near[0].shape[0] // 2
+    return [swap_inner(near[0][:cut], count, 2), swap_inner(near[1][cut:], count, 1)]
 
 
 def return_inner(value, count, inner):
@@ -301,24 +313,35 @@
         own_cotangent,
     )
     token_column = jnp.concatenate([own_tokens, *token_blocks[1:]], axis=0)
-    payload, token_column = lax.optimization_barrier((payload, token_column))
+    others = [swap(weights[0]) for weights in (w_gate, w_up)]
+    payload, token_column, others = lax.optimization_barrier((payload, token_column, others))
     upstream_column = jnp.concatenate(along_outer(payload, count, inner), axis=0)
-    token_columns = across_inner(token_column, count, inner)
-    own_weights = jnp.concatenate([w_gate[0], w_up[0], w_down[0]], axis=0)
-    sent_weights, token_columns[1] = lax.optimization_barrier((own_weights, token_columns[1]))
-    other = swap(sent_weights)
+    token_near = near_inner(token_column, count)
+    token_near, upstream_column, sent_down = lax.optimization_barrier(
+        (token_near, upstream_column, w_down[0])
+    )
+    upstream_near = near_inner(upstream_column, count)
+    token_columns = [token_column, *token_near, *far_inner(token_near, count)]
+    other_down = swap(sent_down)
+    (gate_up,) = on_chip(
+        stack_kernel,
+        [((4 * half, model_width), low)],
+        w_gate[0],
+        others[0],
+        w_up[0],
+        others[1],
+    )
+    down = jnp.concatenate([w_down[0], other_down], axis=0)
     inputs = jnp.concatenate(token_columns, axis=0)
     other_inputs = swap(inputs)
-    upstream = jnp.concatenate(across_inner(upstream_column, count, inner), axis=0)
+    near = jnp.concatenate([upstream_column, *upstream_near], axis=0)
+    other_near = swap(near)
+    far = jnp.concatenate(far_inner(upstream_near, count), axis=0)
+    upstream = jnp.concatenate([near, far], axis=0)
     gate = jnp.sum(
         upstream[:, model_width:].astype(jnp.float32) * here[:1], axis=1, keepdims=True
     )
     upstream = upstream[:, :model_width]
-    gate_up = jnp.concatenate(
-        [own_weights[:half], other[:half], own_weights[half : 2 * half], other[half : 2 * half]],
-        axis=0,
-    )
-    down = jnp.concatenate([own_weights[2 * half :], other[2 * half :]], axis=0)
     pre = jnp.dot(inputs, gate_up.T, preferred_element_type=jnp.float32)
     gate_pre, up_pre = pre[:, : 2 * half], pre[:, 2 * half :]
     hidden_grad = gate * jnp.dot(upstream, down.T, preferred_element_type=jnp.float32)
@@ -335,11 +358,11 @@
     grads = (gate_grad, up_grad, hidden)
     own_grads = jnp.concatenate([grad[:, :half] for grad in grads], axis=1)
     sent_grads = jnp.concatenate([grad[:, half:] for grad in grads], axis=1)
-    sent_grads, upstream, _ = lax.optimization_barrier((sent_grads, upstream, partial_grad))
+    sent_grads, far, _ = lax.optimization_barrier((sent_grads, far, partial_grad))
     other_grads = swap(sent_grads)
-    other_upstream = swap(upstream)
-    column_sum, other_grads, other_inputs, other_upstream = lax.optimization_barrier(
-        (column_sum, other_grads, other_inputs, other_upstream)
+    other_far = swap(far)
+    column_sum, other_grads, other_inputs, other_near, other_far = lax.optimization_barrier(
+        (column_sum, other_grads, other_inputs, other_near, other_far)
     )
     input_grad = return_outer(column_sum, count, inner)
     weight_grads = on_chip(
@@ -350,7 +373,8 @@
         inputs,
         other_inputs,
         upstream,
-        other_upstream,
+        other_near,
+        other_far,
     )
     return (input_grad, *weight_grads)
 

time: 69.9 us -> 75.7 us (1.083)
  waiting for transfers between devices: 27.6 us -> 31.9 us
  local copies, waits for them, and re-layouts: 2.18 us -> 3.35 us
  starting transfers between devices: 28.6 us -> 29.7 us
  other arithmetic: 3.01 us -> 2.15 us
    concatenate x1 -> x3, other arithmetic: 1.81 us -> 0.11 us  [the longest x1 0.06 us: dense_local(): near = jnp.concatenate([upstream_column, *upstream_near], axis=0)]
    ppermute x9, waiting for transfers between devices: 7.12 us -> 8.75 us  [shift_outer(): lax.ppermute(value, 'expert', [(place, (place + step * inner) % count) fo...]
    ppermute x5 -> x8, waiting for transfers between devices: 0.01 us -> 1.44 us  [swap(): return lax.ppermute(value, 'dp', [(0, 1), (1, 0)])]
    unnamed x22 -> x18, local copies, waits for them, and re-layouts: 1.48 us -> 2.83 us
    ppermute x11, waiting for transfers between devices: 20.5 us -> 21.7 us  [swap_inner(): lax.ppermute(value, 'expert', [(place, place ^ partner) for place in rang...]
    ppermute x5 -> x8, starting transfers between devices: 0.22 us -> 1.24 us  [swap(): return lax.ppermute(value, 'dp', [(0, 1), (1, 0)])]
    ppermute x11, starting transfers between devices: 13.1 us -> 13.9 us  [swap_inner(): lax.ppermute(value, 'expert', [(place, place ^ partner) for place in rang...]
    concatenate x1, other arithmetic: 0.02 us -> 0.86 us  [dense_local(): token_column = jnp.concatenate([own_tokens, *token_blocks[1:]], axis=0)]
  transfers between devices with their start and end apart: 25 -> 28, of which waited for: 12 -> 13; matrix products, arithmetic and copies ran while one was open for 9% -> 7% of each run, Pallas kernels for 6% -> 6%
where the time goes in v13:
time: 75.7 us; the launch traced here: 75.4 us
  waiting for transfers between devices  31.9 us (42%)
  starting transfers between devices  29.7 us (39%)
  Pallas kernels  4.5 us (6%)
  local copies, waits for them, and re-layouts  3.35 us (4%)
  matrix products  2.83 us (4%)
  other arithmetic  2.15 us (3%)
  between operations  0.94 us (1%)
    ppermute x11, waiting for transfers between devices, swap_inner(): lax.ppermute(value, 'expert', [(place, place ^ partner) for place in rang...  21.7 us
    ppermute x9, starting transfers between devices, shift_outer(): lax.ppermute(value, 'expert', [(place, (place + step * inner) % count) fo...  14.5 us
    ppermute x11, starting transfers between devices, swap_inner(): lax.ppermute(value, 'expert', [(place, place ^ partner) for place in rang...  13.9 us
    ppermute x9, waiting for transfers between devices, shift_outer(): lax.ppermute(value, 'expert', [(place, (place + step * inner) % count) fo...  8.75 us
    pallas_call x4, Pallas kernels, on_chip(): pl.pallas_call(body, out_shape=[jax.ShapeDtypeStruct(shape, dtype) for sh...  4.5 us
    unnamed x18, local copies, waits for them, and re-layouts  2.83 us
  transfers between devices with their start and end apart: 28, of which 13 were waited for; matrix products, arithmetic and copies ran while one was open for 7% of the time, Pallas kernels for 6%

profile of v13, /device:TPU:0, one launch (start us, length us, event | category | flops | bytes accessed | tf_op | source)
XLA Modules:
  0.0 75.4 jit_solution(15645513957485102763)
XLA Ops:
  1.2 1.6 %shard_map.111 = (bf16[32,16]{1,0:T(8,128)(2,1)}, bf16[16,2048]{1,0:T(8,128)(2,1)}, bf16[16,2048]{1,0:T(8,128)(2,1)}) custom-call(s32[8,16]{1,0:T(8,128)} %bitcast.15, bf16[8,16]{1,0:T(8,128)(2,1)} %bitcast.16, s32[1,16]{1,0:T(1,128)} %bitcast.17, bf16[16,2048]{1,0:T(8,128)(2,1)} %tokens_hbm.1, bf16[16,2048]{1,0:T(8,128)(2,1)} %cotangent_hbm.1), custom_call_target="tpu_custom_call" | custom-call | bytes 264000 | tf_op jit(solution)/shard_map/pallas_call | solution.py:156
  3.4 2.6 %collective-permute-start.1 = (bf16[16,2048]{1,0:T(8,128)(2,1)}, bf16[16,2048]{1,0:T(8,128)(2,1)S(1)}, u32[]{:S(2)}, u32[]{:S(2)}) collective-permute-start(bf16[16,2048]{1,0:T(8,128)(2,1)} %tokens_hbm.1), channel_id=1, source_target_pairs={{0,4},{1,5},{2,6},{3,7},{4,8},{5,9},{6,10},{7,11},{8,12},{9,13},{1... | collective-permute-start | bytes 196616 | tf_op jit(solution)/shard_map/ppermute | solution.py:137
  6.0 2.6 %collective-permute-start.2 = (bf16[16,2048]{1,0:T(8,128)(2,1)}, bf16[16,2048]{1,0:T(8,128)(2,1)S(1)}, u32[]{:S(2)}, u32[]{:S(2)}) collective-permute-start(bf16[16,2048]{1,0:T(8,128)(2,1)} %tokens_hbm.1), channel_id=1, source_target_pairs={{0,8},{1,9},{2,10},{3,11},{4,12},{5,13},{6,14},{7,15},{8,0},{9,1},... | collective-permute-start | bytes 196616 | tf_op jit(solution)/shard_map/ppermute | solution.py:137
  8.6 1.3 %collective-permute-start.3 = (bf16[16,2048]{1,0:T(8,128)(2,1)}, bf16[16,2048]{1,0:T(8,128)(2,1)S(1)}, u32[]{:S(2)}, u32[]{:S(2)}) collective-permute-start(bf16[16,2048]{1,0:T(8,128)(2,1)} %tokens_hbm.1), channel_id=1, source_target_pairs={{0,12},{1,13},{2,14},{3,15},{4,0},{5,1},{6,2},{7,3},{8,4},{9,5},{1... | collective-permute-start | bytes 196616 | tf_op jit(solution)/shard_map/ppermute | solution.py:137
  11.6 2.2 %collective-permute-done.2 = bf16[16,2048]{1,0:T(8,128)(2,1)S(1)} collective-permute-done((bf16[16,2048]{1,0:T(8,128)(2,1)}, bf16[16,2048]{1,0:T(8,128)(2,1)S(1)}, u32[]{:S(2)}, u32[]{:S(2)}) %collective-permute-start.2) | collective-permute-done | bytes 65568 | tf_op jit(solution)/shard_map/ppermute | solution.py:137
  15.0 2.8 %collective-permute-start.10 = (bf16[16,2064]{1,0:T(8,128)(2,1)S(1)}, bf16[16,2064]{1,0:T(8,128)(2,1)S(1)}, u32[]{:S(2)}, u32[]{:S(2)}) collective-permute-start(bf16[16,2064]{1,0:T(8,128)(2,1)S(1)} %get-tuple-element.32), channel_id=1, source_target_pairs={{0,12},{1,13},{2,14},{3,15},{4,0},{5,1},{6,2},{7,3},{8,4},{9,5},{1... | collective-permute-start | bytes 198152 | tf_op jit(solution)/shard_map/ppermute | solution.py:137
  18.4 1.5 %collective-permute-start.6 = (bf16[64,2048]{1,0:T(8,128)(2,1)S(1)}, bf16[64,2048]{1,0:T(8,128)(2,1)S(1)}, u32[]{:S(2)}, u32[]{:S(2)}) collective-permute-start(bf16[64,2048]{1,0:T(8,128)(2,1)S(1)} %pad_maximum_fusion.5), channel_id=1, source_target_pairs={{0,1},{1,0},{2,3},{3,2},{4,5},{5,4},{6,7},{7,6},{8,9},{9,8},{10,11... | collective-permute-start | bytes 786440 | tf_op jit(solution)/shard_map/ppermute | solution.py:143
  19.8 1.5 %collective-permute-start.7 = (bf16[64,2048]{1,0:T(8,128)(2,1)S(1)}, bf16[64,2048]{1,0:T(8,128)(2,1)S(1)}, u32[]{:S(2)}, u32[]{:S(2)}) collective-permute-start(bf16[64,2048]{1,0:T(8,128)(2,1)S(1)} %pad_maximum_fusion.5), channel_id=1, source_target_pairs={{0,2},{1,3},{2,0},{3,1},{4,6},{5,7},{6,4},{7,5},{8,10},{9,11},{10,... | collective-permute-start | bytes 786440 | tf_op jit(solution)/shard_map/ppermute | solution.py:143
  23.9 1.4 %collective-permute-done.9 = bf16[16,2064]{1,0:T(8,128)(2,1)S(1)} collective-permute-done((bf16[16,2064]{1,0:T(8,128)(2,1)S(1)}, bf16[16,2064]{1,0:T(8,128)(2,1)S(1)}, u32[]{:S(2)}, u32[]{:S(2)}) %collective-permute-start.9) | collective-permute-done | bytes 66080 | tf_op jit(solution)/shard_map/ppermute | solution.py:137
  27.6 1.6 %collective-permute-start.12 = (bf16[64,2064]{1,0:T(8,128)(2,1)S(1)}, bf16[64,2064]{1,0:T(8,128)(2,1)S(1)}, u32[]{:S(2)}, u32[]{:S(2)}) collective-permute-start(bf16[64,2064]{1,0:T(8,128)(2,1)S(1)} %pad_maximum_fusion.3), channel_id=1, source_target_pairs={{0,2},{1,3},{2,0},{3,1},{4,6},{5,7},{6,4},{7,5},{8,10},{9,11},{10,... | collective-permute-start | bytes 792584 | tf_op jit(solution)/shard_map/ppermute | solution.py:143
  29.8 1.6 %collective-permute-start.17 = (bf16[32,2048]{1,0:T(8,128)(2,1)S(1)}, bf16[32,2048]{1,0:T(8,128)(2,1)S(1)}, u32[]{:S(2)}, u32[]{:S(2)}) collective-permute-start(bf16[32,2048]{1,0:T(8,128)(2,1)S(1)} %slice.83), channel_id=1, source_target_pairs={{0,1},{1,0},{2,3},{3,2},{4,5},{5,4},{6,7},{7,6},{8,9},{9,8},{10,11... | collective-permute-start | bytes 393224 | tf_op jit(solution)/shard_map/ppermute | solution.py:143
  31.4 5.4 %collective-permute-done.16 = bf16[32,2048]{1,0:T(8,128)(2,1)S(1)} collective-permute-done((bf16[32,2048]{1,0:T(8,128)(2,1)S(1)}, bf16[32,2048]{1,0:T(8,128)(2,1)S(1)}, u32[]{:S(2)}, u32[]{:S(2)}) %collective-permute-start.16) | collective-permute-done | bytes 131104 | tf_op jit(solution)/shard_map/ppermute | solution.py:143
  38.0 1.6 %collective-permute-start.13 = (bf16[32,2064]{1,0:T(8,128)(2,1)S(1)}, bf16[32,2064]{1,0:T(8,128)(2,1)S(1)}, u32[]{:S(2)}, u32[]{:S(2)}) collective-permute-start(bf16[32,2064]{1,0:T(8,128)(2,1)S(1)} %slice.100), channel_id=1, source_target_pairs={{0,2},{1,3},{2,0},{3,1},{4,6},{5,7},{6,4},{7,5},{8,10},{9,11},{10,... | collective-permute-start | bytes 396296 | tf_op jit(solution)/shard_map/ppermute | solution.py:143
  39.6 1.5 %collective-permute-start.14 = (bf16[32,2064]{1,0:T(8,128)(2,1)S(1)}, bf16[32,2064]{1,0:T(8,128)(2,1)S(1)}, u32[]{:S(2)}, u32[]{:S(2)}) collective-permute-start(bf16[32,2064]{1,0:T(8,128)(2,1)S(1)} %slice.101), channel_id=1, source_target_pairs={{0,1},{1,0},{2,3},{3,2},{4,5},{5,4},{6,7},{7,6},{8,9},{9,8},{10,11... | collective-permute-start | bytes 396296 | tf_op jit(solution)/shard_map/ppermute | solution.py:143
  41.3 2.8 %collective-permute-done.13 = bf16[32,2064]{1,0:T(8,128)(2,1)S(1)} collective-permute-done((bf16[32,2064]{1,0:T(8,128)(2,1)S(1)}, bf16[32,2064]{1,0:T(8,128)(2,1)S(1)}, u32[]{:S(2)}, u32[]{:S(2)}) %collective-permute-start.13) | collective-permute-done | bytes 132128 | tf_op jit(solution)/shard_map/ppermute | solution.py:143
  47.6 1.5 %collective-permute-start.18 = (bf16[64,2048]{1,0:T(8,128)(2,1)S(1)}, bf16[64,2048]{1,0:T(8,128)(2,1)S(1)}, u32[]{:S(2)}, u32[]{:S(2)}) collective-permute-start(bf16[64,2048]{1,0:T(8,128)(2,1)S(1)} %get-tuple-element.52), channel_id=1, source_target_pairs={{0,1},{1,0},{2,3},{3,2},{4,5},{5,4},{6,7},{7,6},{8,9},{9,8},{10,11... | collective-permute-start | bytes 786440 | tf_op jit(solution)/shard_map/ppermute | solution.py:143
  49.7 1.5 %collective-permute-start.20 = (bf16[64,2048]{1,0:T(8,128)(2,1)S(1)}, bf16[64,2048]{1,0:T(8,128)(2,1)S(1)}, u32[]{:S(2)}, u32[]{:S(2)}) collective-permute-start(bf16[64,2048]{1,0:T(8,128)(2,1)S(1)} %get-tuple-element.53), channel_id=1, source_target_pairs={{0,3},{1,2},{2,1},{3,0},{4,7},{5,6},{6,5},{7,4},{8,11},{9,10},{10,... | collective-permute-start | bytes 786440 | tf_op jit(solution)/shard_map/ppermute | solution.py:143
  51.6 5.4 %collective-permute-done.18 = bf16[64,2048]{1,0:T(8,128)(2,1)S(1)} collective-permute-done((bf16[64,2048]{1,0:T(8,128)(2,1)S(1)}, bf16[64,2048]{1,0:T(8,128)(2,1)S(1)}, u32[]{:S(2)}, u32[]{:S(2)}) %collective-permute-start.18) | collective-permute-done | bytes 262176 | tf_op jit(solution)/shard_map/ppermute | solution.py:143
  56.9 5.2 %collective-permute-done.19 = bf16[64,2048]{1,0:T(8,128)(2,1)S(1)} collective-permute-done((bf16[64,2048]{1,0:T(8,128)(2,1)S(1)}, bf16[64,2048]{1,0:T(8,128)(2,1)S(1)}, u32[]{:S(2)}, u32[]{:S(2)}) %collective-permute-start.19) | collective-permute-done | bytes 262176 | tf_op jit(solution)/shard_map/ppermute | solution.py:143
  62.2 1.4 %collective-permute-done.24.other_far = bf16[64,2064]{1,0:T(8,128)(2,1)S(1)} collective-permute-done((bf16[64,2064]{1,0:T(8,128)(2,1)S(1)}, bf16[64,2064]{1,0:T(8,128)(2,1)S(1)}, u32[]{:S(2)}, u32[]{:S(2)}) %collective-permute-start.24) | collective-permute-done | bytes 264224 | tf_op jit(solution)/shard_map/ppermute | solution.py:133
  63.7 3.1 %collective-permute-start.25 = (bf16[16,2048]{1,0:T(8,128)(2,1)S(1)}, bf16[16,2048]{1,0:T(8,128)(2,1)S(1)}, u32[]{:S(2)}, u32[]{:S(2)}) collective-permute-start(bf16[16,2048]{1,0:T(8,128)(2,1)S(1)} %get-tuple-element.56), channel_id=1, source_target_pairs={{0,12},{1,13},{2,14},{3,15},{4,0},{5,1},{6,2},{7,3},{8,4},{9,5},{1... | collective-permute-start | bytes 196616 | tf_op jit(solution)/shard_map/ppermute | solution.py:137
  66.8 1.5 %collective-permute-start.26 = (bf16[16,2048]{1,0:T(8,128)(2,1)S(1)}, bf16[16,2048]{1,0:T(8,128)(2,1)S(1)}, u32[]{:S(2)}, u32[]{:S(2)}) collective-permute-start(bf16[16,2048]{1,0:T(8,128)(2,1)S(1)} %get-tuple-element.58), channel_id=1, source_target_pairs={{0,8},{1,9},{2,10},{3,11},{4,12},{5,13},{6,14},{7,15},{8,0},{9,1},... | collective-permute-start | bytes 196616 | tf_op jit(solution)/shard_map/ppermute | solution.py:137
  68.4 2.6 %shard_map.114 = (bf16[1,192,2048]{2,1,0:T(8,128)(2,1)}, bf16[1,192,2048]{2,1,0:T(8,128)(2,1)}, bf16[1,192,2048]{2,1,0:T(8,128)(2,1)}) custom-call(bf16[256,576]{1,0:T(8,128)(2,1)S(1)} %pad_maximum_fusion.2.own_grads, bf16[256,576]{1,0:T(8,128)(2,1)S(1)} %collective-permute-done.21.other_grads, ...), custom_call_target="tpu_custom_call" | custom-call | bytes 7151616 | tf_op jit(solution)/shard_map/pallas_call | solution.py:156
  71.0 3.8 %collective-permute-done.26 = bf16[16,2048]{1,0:T(8,128)(2,1)S(1)} collective-permute-done((bf16[16,2048]{1,0:T(8,128)(2,1)S(1)}, bf16[16,2048]{1,0:T(8,128)(2,1)S(1)}, u32[]{:S(2)}, u32[]{:S(2)}) %collective-permute-start.26) | collective-permute-done | bytes 65568 | tf_op jit(solution)/shard_map/ppermute | solution.py:137
  (79 shorter events, 16.6 us)
Async XLA Ops:
  0.6 14.3 %collective-permute-start.4 = (bf16[192,2048]{1,0:T(8,128)(2,1)}, bf16[192,2048]{1,0:T(8,128)(2,1)S(1)}, u32[]{:S(2)}, u32[]{:S(2)}) collective-permute-start(bf16[192,2048]{1,0:T(8,128)(2,1)} %bitcast.11), channel_id=1, source_target_pairs={{0,16},{16,0},{1,17},{17,1},{2,18},{18,2},{3,19},{19,3},{4,20},{20... | collective-permute-start | bytes 2359304 | tf_op jit(solution)/shard_map/ppermute | solution.py:133
  1.2 13.8 %collective-permute-start.5 = (bf16[192,2048]{1,0:T(8,128)(2,1)}, bf16[192,2048]{1,0:T(8,128)(2,1)S(1)}, u32[]{:S(2)}, u32[]{:S(2)}) collective-permute-start(bf16[192,2048]{1,0:T(8,128)(2,1)} %bitcast.13), channel_id=1, source_target_pairs={{0,16},{16,0},{1,17},{17,1},{2,18},{18,2},{3,19},{19,3},{4,20},{20... | collective-permute-start | bytes 2359304 | tf_op jit(solution)/shard_map/ppermute | solution.py:133
  3.4 8.3 %collective-permute-start.1 = (bf16[16,2048]{1,0:T(8,128)(2,1)}, bf16[16,2048]{1,0:T(8,128)(2,1)S(1)}, u32[]{:S(2)}, u32[]{:S(2)}) collective-permute-start(bf16[16,2048]{1,0:T(8,128)(2,1)} %tokens_hbm.1), channel_id=1, source_target_pairs={{0,4},{1,5},{2,6},{3,7},{4,8},{5,9},{6,10},{7,11},{8,12},{9,13},{1... | collective-permute-start | bytes 196616 | tf_op jit(solution)/shard_map/ppermute | solution.py:137
  6.0 7.8 %collective-permute-start.2 = (bf16[16,2048]{1,0:T(8,128)(2,1)}, bf16[16,2048]{1,0:T(8,128)(2,1)S(1)}, u32[]{:S(2)}, u32[]{:S(2)}) collective-permute-start(bf16[16,2048]{1,0:T(8,128)(2,1)} %tokens_hbm.1), channel_id=1, source_target_pairs={{0,8},{1,9},{2,10},{3,11},{4,12},{5,13},{6,14},{7,15},{8,0},{9,1},... | collective-permute-start | bytes 196616 | tf_op jit(solution)/shard_map/ppermute | solution.py:137
  15.0 7.8 %collective-permute-start.10 = (bf16[16,2064]{1,0:T(8,128)(2,1)S(1)}, bf16[16,2064]{1,0:T(8,128)(2,1)S(1)}, u32[]{:S(2)}, u32[]{:S(2)}) collective-permute-start(bf16[16,2064]{1,0:T(8,128)(2,1)S(1)} %get-tuple-element.32), channel_id=1, source_target_pairs={{0,12},{1,13},{2,14},{3,15},{4,0},{5,1},{6,2},{7,3},{8,4},{9,5},{1... | collective-permute-start | bytes 198152 | tf_op jit(solution)/shard_map/ppermute | solution.py:137
  17.7 6.2 %collective-permute-start.8 = (bf16[16,2064]{1,0:T(8,128)(2,1)S(1)}, bf16[16,2064]{1,0:T(8,128)(2,1)S(1)}, u32[]{:S(2)}, u32[]{:S(2)}) collective-permute-start(bf16[16,2064]{1,0:T(8,128)(2,1)S(1)} %get-tuple-element.32), channel_id=1, source_target_pairs={{0,4},{1,5},{2,6},{3,7},{4,8},{5,9},{6,10},{7,11},{8,12},{9,13},{1... | collective-permute-start | bytes 198152 | tf_op jit(solution)/shard_map/ppermute | solution.py:137
  17.7 7.5 %collective-permute-start.9 = (bf16[16,2064]{1,0:T(8,128)(2,1)S(1)}, bf16[16,2064]{1,0:T(8,128)(2,1)S(1)}, u32[]{:S(2)}, u32[]{:S(2)}) collective-permute-start(bf16[16,2064]{1,0:T(8,128)(2,1)S(1)} %get-tuple-element.32), channel_id=1, source_target_pairs={{0,8},{1,9},{2,10},{3,11},{4,12},{5,13},{6,14},{7,15},{8,0},{9,1},... | collective-permute-start | bytes 198152 | tf_op jit(solution)/shard_map/ppermute | solution.py:137
  18.4 7.4 %collective-permute-start.6 = (bf16[64,2048]{1,0:T(8,128)(2,1)S(1)}, bf16[64,2048]{1,0:T(8,128)(2,1)S(1)}, u32[]{:S(2)}, u32[]{:S(2)}) collective-permute-start(bf16[64,2048]{1,0:T(8,128)(2,1)S(1)} %pad_maximum_fusion.5), channel_id=1, source_target_pairs={{0,1},{1,0},{2,3},{3,2},{4,5},{5,4},{6,7},{7,6},{8,9},{9,8},{10,11... | collective-permute-start | bytes 786440 | tf_op jit(solution)/shard_map/ppermute | solution.py:143
  19.8 7.2 %collective-permute-start.7 = (bf16[64,2048]{1,0:T(8,128)(2,1)S(1)}, bf16[64,2048]{1,0:T(8,128)(2,1)S(1)}, u32[]{:S(2)}, u32[]{:S(2)}) collective-permute-start(bf16[64,2048]{1,0:T(8,128)(2,1)S(1)} %pad_maximum_fusion.5), channel_id=1, source_target_pairs={{0,2},{1,3},{2,0},{3,1},{4,6},{5,7},{6,4},{7,5},{8,10},{9,11},{10,... | collective-permute-start | bytes 786440 | tf_op jit(solution)/shard_map/ppermute | solution.py:143
  27.0 10.9 %collective-permute-start.11 = (bf16[64,2064]{1,0:T(8,128)(2,1)S(1)}, bf16[64,2064]{1,0:T(8,128)(2,1)S(1)}, u32[]{:S(2)}, u32[]{:S(2)}) collective-permute-start(bf16[64,2064]{1,0:T(8,128)(2,1)S(1)} %pad_maximum_fusion.3), channel_id=1, source_target_pairs={{0,1},{1,0},{2,3},{3,2},{4,5},{5,4},{6,7},{7,6},{8,9},{9,8},{10,11... | collective-permute-start | bytes 792584 | tf_op jit(solution)/shard_map/ppermute | solution.py:143
  27.6 12.0 %collective-permute-start.12 = (bf16[64,2064]{1,0:T(8,128)(2,1)S(1)}, bf16[64,2064]{1,0:T(8,128)(2,1)S(1)}, u32[]{:S(2)}, u32[]{:S(2)}) collective-permute-start(bf16[64,2064]{1,0:T(8,128)(2,1)S(1)} %pad_maximum_fusion.3), channel_id=1, source_target_pairs={{0,2},{1,3},{2,0},{3,1},{4,6},{5,7},{6,4},{7,5},{8,10},{9,11},{10,... | collective-permute-start | bytes 792584 | tf_op jit(solution)/shard_map/ppermute | solution.py:143
  29.2 7.6 %collective-permute-start.16 = (bf16[32,2048]{1,0:T(8,128)(2,1)S(1)}, bf16[32,2048]{1,0:T(8,128)(2,1)S(1)}, u32[]{:S(2)}, u32[]{:S(2)}) collective-permute-start(bf16[32,2048]{1,0:T(8,128)(2,1)S(1)} %slice.82), channel_id=1, source_target_pairs={{0,2},{1,3},{2,0},{3,1},{4,6},{5,7},{6,4},{7,5},{8,10},{9,11},{10,... | collective-permute-start | bytes 393224 | tf_op jit(solution)/shard_map/ppermute | solution.py:143
  29.8 7.0 %collective-permute-start.17 = (bf16[32,2048]{1,0:T(8,128)(2,1)S(1)}, bf16[32,2048]{1,0:T(8,128)(2,1)S(1)}, u32[]{:S(2)}, u32[]{:S(2)}) collective-permute-start(bf16[32,2048]{1,0:T(8,128)(2,1)S(1)} %slice.83), channel_id=1, source_target_pairs={{0,1},{1,0},{2,3},{3,2},{4,5},{5,4},{6,7},{7,6},{8,9},{9,8},{10,11... | collective-permute-start | bytes 393224 | tf_op jit(solution)/shard_map/ppermute | solution.py:143
  31.3 14.4 %collective-permute-start.15 = (bf16[192,2048]{1,0:T(8,128)(2,1)S(1)}, bf16[192,2048]{1,0:T(8,128)(2,1)S(1)}, u32[]{:S(2)}, u32[]{:S(2)}) collective-permute-start(bf16[192,2048]{1,0:T(8,128)(2,1)S(1)} %bitcast.18), channel_id=1, source_target_pairs={{0,16},{16,0},{1,17},{17,1},{2,18},{18,2},{3,19},{19,3},{4,20},{20... | collective-permute-start | bytes 2359304 | tf_op jit(solution)/shard_map/ppermute | solution.py:133
  36.8 26.8 %collective-permute-start.22 = (bf16[256,2048]{1,0:T(8,128)(2,1)S(1)}, bf16[256,2048]{1,0:T(8,128)(2,1)S(1)}, u32[]{:S(2)}, u32[]{:S(2)}) collective-permute-start(bf16[256,2048]{1,0:T(8,128)(2,1)S(1)} %constant_dynamic-update-slice_fusion.5.rows), channel_id=1, source_target_pairs={{0,16},{16,0},{1,17},{17,1},{2,18},{18,2},{3,19},{19,3},{4,20},{20... | collective-permute-start | bytes 3145736 | tf_op jit(solution)/shard_map/ppermute | solution.py:133
  38.0 6.1 %collective-permute-start.13 = (bf16[32,2064]{1,0:T(8,128)(2,1)S(1)}, bf16[32,2064]{1,0:T(8,128)(2,1)S(1)}, u32[]{:S(2)}, u32[]{:S(2)}) collective-permute-start(bf16[32,2064]{1,0:T(8,128)(2,1)S(1)} %slice.100), channel_id=1, source_target_pairs={{0,2},{1,3},{2,0},{3,1},{4,6},{5,7},{6,4},{7,5},{8,10},{9,11},{10,... | collective-permute-start | bytes 396296 | tf_op jit(solution)/shard_map/ppermute | solution.py:143
  41.2 22.5 %collective-permute-start.23 = (bf16[192,2064]{1,0:T(8,128)(2,1)S(1)}, bf16[192,2064]{1,0:T(8,128)(2,1)S(1)}, u32[]{:S(2)}, u32[]{:S(2)}) collective-permute-start(bf16[192,2064]{1,0:T(8,128)(2,1)S(1)} %pad_maximum_fusion), channel_id=1, source_target_pairs={{0,16},{16,0},{1,17},{17,1},{2,18},{18,2},{3,19},{19,3},{4,20},{20... | collective-permute-start | bytes 2377736 | tf_op jit(solution)/shard_map/ppermute | solution.py:133
  47.6 9.3 %collective-permute-start.18 = (bf16[64,2048]{1,0:T(8,128)(2,1)S(1)}, bf16[64,2048]{1,0:T(8,128)(2,1)S(1)}, u32[]{:S(2)}, u32[]{:S(2)}) collective-permute-start(bf16[64,2048]{1,0:T(8,128)(2,1)S(1)} %get-tuple-element.52), channel_id=1, source_target_pairs={{0,1},{1,0},{2,3},{3,2},{4,5},{5,4},{6,7},{7,6},{8,9},{9,8},{10,11... | collective-permute-start | bytes 786440 | tf_op jit(solution)/shard_map/ppermute | solution.py:143
  49.1 12.9 %collective-permute-start.19 = (bf16[64,2048]{1,0:T(8,128)(2,1)S(1)}, bf16[64,2048]{1,0:T(8,128)(2,1)S(1)}, u32[]{:S(2)}, u32[]{:S(2)}) collective-permute-start(bf16[64,2048]{1,0:T(8,128)(2,1)S(1)} %get-tuple-element.54), channel_id=1, source_target_pairs={{0,2},{1,3},{2,0},{3,1},{4,6},{5,7},{6,4},{7,5},{8,10},{9,11},{10,... | collective-permute-start | bytes 786440 | tf_op jit(solution)/shard_map/ppermute | solution.py:143
  49.7 12.4 %collective-permute-start.20 = (bf16[64,2048]{1,0:T(8,128)(2,1)S(1)}, bf16[64,2048]{1,0:T(8,128)(2,1)S(1)}, u32[]{:S(2)}, u32[]{:S(2)}) collective-permute-start(bf16[64,2048]{1,0:T(8,128)(2,1)S(1)} %get-tuple-element.53), channel_id=1, source_target_pairs={{0,3},{1,2},{2,1},{3,0},{4,7},{5,6},{6,5},{7,4},{8,11},{9,10},{10,... | collective-permute-start | bytes 786440 | tf_op jit(solution)/shard_map/ppermute | solution.py:143
  56.9 6.7 %collective-permute-start.21 = (bf16[256,576]{1,0:T(8,128)(2,1)S(1)}, bf16[256,576]{1,0:T(8,128)(2,1)S(1)}, u32[]{:S(2)}, u32[]{:S(2)}) collective-permute-start(bf16[256,576]{1,0:T(8,128)(2,1)S(1)} %pad_maximum_fusion.1), channel_id=1, source_target_pairs={{0,16},{16,0},{1,17},{17,1},{2,18},{18,2},{3,19},{19,3},{4,20},{20... | collective-permute-start | bytes 884744 | tf_op jit(solution)/shard_map/ppermute | solution.py:133
  63.7 7.3 %collective-permute-start.25 = (bf16[16,2048]{1,0:T(8,128)(2,1)S(1)}, bf16[16,2048]{1,0:T(8,128)(2,1)S(1)}, u32[]{:S(2)}, u32[]{:S(2)}) collective-permute-start(bf16[16,2048]{1,0:T(8,128)(2,1)S(1)} %get-tuple-element.56), channel_id=1, source_target_pairs={{0,12},{1,13},{2,14},{3,15},{4,0},{5,1},{6,2},{7,3},{8,4},{9,5},{1... | collective-permute-start | bytes 196616 | tf_op jit(solution)/shard_map/ppermute | solution.py:137
  66.8 7.9 %collective-permute-start.26 = (bf16[16,2048]{1,0:T(8,128)(2,1)S(1)}, bf16[16,2048]{1,0:T(8,128)(2,1)S(1)}, u32[]{:S(2)}, u32[]{:S(2)}) collective-permute-start(bf16[16,2048]{1,0:T(8,128)(2,1)S(1)} %get-tuple-element.58), channel_id=1, source_target_pairs={{0,8},{1,9},{2,10},{3,11},{4,12},{5,13},{6,14},{7,15},{8,0},{9,1},... | collective-permute-start | bytes 196616 | tf_op jit(solution)/shard_map/ppermute | solution.py:137
  68.3 6.5 %collective-permute-start.27 = (bf16[16,2048]{1,0:T(8,128)(2,1)S(1)}, bf16[16,2048]{1,0:T(8,128)(2,1)S(1)}, u32[]{:S(2)}, u32[]{:S(2)}) collective-permute-start(bf16[16,2048]{1,0:T(8,128)(2,1)S(1)} %get-tuple-element.57), channel_id=1, source_target_pairs={{0,4},{1,5},{2,6},{3,7},{4,8},{5,9},{6,10},{7,11},{8,12},{9,13},{1... | collective-permute-start | bytes 196616 | tf_op jit(solution)/shard_map/ppermute | solution.py:137
  (9 other events, 50.7 us)

commit v14 on v11

--- a/solution.py
+++ b/solution.py
@@ -133,10 +133,8 @@
     return lax.ppermute(value, "dp", [(0, 1), (1, 0)])
 
 
-def shift_outer(value, count, inner, step):
-    return lax.ppermute(
-        value, "expert", [(place, (place + step * inner) % count) for place in range(count)]
-    )
+def swap_outer(value, count, inner, partner):
+    return swap_inner(value, count, partner * inner)
 
 
 def swap_inner(value, count, partner):
@@ -164,18 +162,7 @@
     )(*args)
 
 
-def read_kernel(
-    ids_hbm, gates_hbm, packing_hbm, tokens_hbm, cotangent_hbm,
-    table_ref, tokens_ref, cotangent_ref,
-    ids_ref, gates_ref, packing_ref, ready,
-):
-    pairs = [
-        (ids_hbm, ids_ref),
-        (gates_hbm, gates_ref),
-        (packing_hbm, packing_ref),
-        (tokens_hbm, tokens_ref),
-        (cotangent_hbm, cotangent_ref),
-    ]
+def fetch(ready, *pairs):
     copies = [
         pltpu.make_async_copy(source, target, ready.at[index])
         for index, (source, target) in enumerate(pairs)
@@ -184,6 +171,33 @@
         copy.start()
     for copy in copies:
         copy.wait()
+
+
+def weights_kernel(gate_hbm, up_hbm, down_hbm, weights_ref, ready):
+    half = gate_hbm.shape[1]
+    sources = (gate_hbm, up_hbm, down_hbm)
+    fetch(
+        ready,
+        *(
+            (source.at[0], weights_ref.at[index * half : (index + 1) * half])
+            for index, source in enumerate(sources)
+        ),
+    )
+
+
+def read_kernel(
+    ids_hbm, gates_hbm, packing_hbm, tokens_hbm, cotangent_hbm,
+    table_ref, tokens_ref, cotangent_ref,
+    ids_ref, gates_ref, packing_ref, ready,
+):
+    fetch(
+        ready,
+        (ids_hbm, ids_ref),
+        (gates_hbm, gates_ref),
+        (packing_hbm, packing_ref),
+        (tokens_hbm, tokens_ref),
+        (cotangent_hbm, cotangent_ref),
+    )
     slots = packing_ref.shape[1]
     count = table_ref.shape[0] - 16
     labels = lax.broadcasted_iota(jnp.int32, (count, slots), 0)
@@ -231,7 +245,7 @@
 
 
 def along_outer(value, count, inner):
-    return [value] + [shift_outer(value, count, inner, step) for step in range(1, count // inner)]
+    return [value] + [swap_outer(value, count, inner, step) for step in range(1, count // inner)]
 
 
 def across_inner(column, count, inner):
@@ -259,7 +273,7 @@
     rounded = blocks.astype(jnp.bfloat16)
     total = blocks[0]
     for step in range(1, outer):
-        total = total + shift_outer(rounded[step], count, inner, -step).astype(jnp.float32)
+        total = total + swap_outer(rounded[step], count, inner, step).astype(jnp.float32)
     return total.astype(jnp.bfloat16)
 
 
@@ -302,9 +316,18 @@
     )
     token_column = jnp.concatenate([own_tokens, *token_blocks[1:]], axis=0)
     payload, token_column = lax.optimization_barrier((payload, token_column))
+    (own_weights,) = on_chip(
+        weights_kernel,
+        [((3 * half, model_width), low)],
+        w_gate,
+        w_up,
+        w_down,
+        spec=ANY,
+        limit=False,
+        scratch=[pltpu.SemaphoreType.DMA((3,))],
+    )
     upstream_column = jnp.concatenate(along_outer(payload, count, inner), axis=0)
     token_columns = across_inner(token_column, count, inner)
-    own_weights = jnp.concatenate([w_gate[0], w_up[0], w_down[0]], axis=0)
     sent_weights, token_columns[1] = lax.optimization_barrier((own_weights, token_columns[1]))
     other = swap(sent_weights)
     inputs = jnp.concatenate(token_columns, axis=0)

time: 69.9 us -> 70.9 us (1.014)
  Pallas kernels: 4.21 us -> 7.29 us
  waiting for transfers between devices: 27.6 us -> 25.3 us
  other arithmetic: 3.01 us -> 1.2 us
  starting transfers between devices: 28.6 us -> 30.1 us
    ppermute x11 -> x20, starting transfers between devices: 13.1 us -> 29.9 us  [swap_inner(): lax.ppermute(value, 'expert', [(place, place ^ partner) for place in rang...]
    ppermute x9 -> x0, starting transfers between devices: 15.3 us -> none  [shift_outer(): lax.ppermute(value, 'expert', [(place, (place + step * inner) % count) fo...]
    ppermute x9 -> x0, waiting for transfers between devices: 7.12 us -> none  [shift_outer(): lax.ppermute(value, 'expert', [(place, (place + step * inner) % count) fo...]
    ppermute x11 -> x20, waiting for transfers between devices: 20.5 us -> 25.3 us  [swap_inner(): lax.ppermute(value, 'expert', [(place, place ^ partner) for place in rang...]
    pallas_call x3 -> x4, Pallas kernels: 4.21 us -> 7.29 us  [on_chip(): pl.pallas_call(body, out_shape=[jax.ShapeDtypeStruct(shape, dtype) for sh...]
    concatenate x1 -> x0, other arithmetic: 1.81 us -> none  [dense_local(): own_weights = jnp.concatenate([w_gate[0], w_up[0], w_down[0]], axis=0)]
    slice x1 -> x2, local copies, waits for them, and re-layouts: 0.16 us -> 1.96 us  [dense_local(): down = jnp.concatenate([own_weights[2 * half:], other[2 * half:]], axis=0)]
    unnamed x22 -> x18, local copies, waits for them, and re-layouts: 1.48 us -> 0.2 us
  transfers between devices with their start and end apart: 25 -> 25, of which waited for: 12 -> 12; matrix products, arithmetic and copies ran while one was open for 9% -> 9% of each run, Pallas kernels for 6% -> 10%
where the time goes in v14:
time: 70.9 us; the launch traced here: 70.7 us
  starting transfers between devices  30.1 us (42%)
  waiting for transfers between devices  25.3 us (36%)
  Pallas kernels  7.29 us (10%)
  matrix products  3.05 us (4%)
  local copies, waits for them, and re-layouts  2.71 us (4%)
  other arithmetic  1.2 us (2%)
  between operations  0.97 us (1%)
    ppermute x20, starting transfers between devices, swap_inner(): lax.ppermute(value, 'expert', [(place, place ^ partner) for place in rang...  29.9 us
    ppermute x20, waiting for transfers between devices, swap_inner(): lax.ppermute(value, 'expert', [(place, place ^ partner) for place in rang...  25.3 us
    pallas_call x4, Pallas kernels, on_chip(): pl.pallas_call(body, out_shape=[jax.ShapeDtypeStruct(shape, dtype) for sh...  7.29 us
    slice x2, local copies, waits for them, and re-layouts, dense_local(): down = jnp.concatenate([own_weights[2 * half:], other[2 * half:]], axis=0)  1.96 us
  transfers between devices with their start and end apart: 25, of which 12 were waited for; matrix products, arithmetic and copies ran while one was open for 9% of the time, Pallas kernels for 10%

profile of v14, /device:TPU:0, one launch (start us, length us, event | category | flops | bytes accessed | tf_op | source)
XLA Modules:
  0.0 70.7 jit_solution(6769946917939581573)
XLA Ops:
  0.6 3.1 %collective-permute-start.1 = (bf16[16,2048]{1,0:T(8,128)(2,1)}, bf16[16,2048]{1,0:T(8,128)(2,1)S(1)}, u32[]{:S(2)}, u32[]{:S(2)}) collective-permute-start(bf16[16,2048]{1,0:T(8,128)(2,1)} %tokens_hbm.1), channel_id=1, source_target_pairs={{0,4},{1,5},{2,6},{3,7},{4,0},{5,1},{6,2},{7,3},{8,12},{9,13},{10,... | collective-permute-start | bytes 196616 | tf_op jit(solution)/shard_map/ppermute | solution.py:141
  3.7 2.6 %collective-permute-start.2 = (bf16[16,2048]{1,0:T(8,128)(2,1)}, bf16[16,2048]{1,0:T(8,128)(2,1)S(1)}, u32[]{:S(2)}, u32[]{:S(2)}) collective-permute-start(bf16[16,2048]{1,0:T(8,128)(2,1)} %tokens_hbm.1), channel_id=1, source_target_pairs={{0,8},{1,9},{2,10},{3,11},{4,12},{5,13},{6,14},{7,15},{8,0},{9,1},... | collective-permute-start | bytes 196616 | tf_op jit(solution)/shard_map/ppermute | solution.py:141
  6.3 1.6 %shard_map.111 = (bf16[32,16]{1,0:T(8,128)(2,1)}, bf16[16,2048]{1,0:T(8,128)(2,1)}, bf16[16,2048]{1,0:T(8,128)(2,1)}) custom-call(s32[8,16]{1,0:T(8,128)} %bitcast.6, bf16[8,16]{1,0:T(8,128)(2,1)} %bitcast.7, s32[1,16]{1,0:T(1,128)} %bitcast.8, bf16[16,2048]{1,0:T(8,128)(2,1)} %tokens_hbm.1, bf16[16,2048]{1,0:T(8,128)(2,1)} %cotangent_hbm.1), custom_call_target="tpu_custom_call" | custom-call | bytes 264000 | tf_op jit(solution)/shard_map/pallas_call | solution.py:154
  8.0 3.1 %shard_map.113 = bf16[576,2048]{1,0:T(8,128)(2,1)} custom-call(bf16[1,192,2048]{2,1,0:T(8,128)(2,1)} %gate_hbm.1, bf16[1,192,2048]{2,1,0:T(8,128)(2,1)} %up_hbm.1, bf16[1,192,2048]{2,1,0:T(8,128)(2,1)} %down_hbm.1), custom_call_target="tpu_custom_call" | custom-call | bytes 4718592 | tf_op jit(solution)/shard_map/pallas_call | solution.py:154
  11.1 1.8 %fusion.16 = (bf16[192,2048]{1,0:T(8,128)(2,1)S(1)}, bf16[192,2048]{1,0:T(8,128)(2,1)S(1)}, bf16[192,2048]{1,0:T(8,128)(2,1)S(1)}) fusion(bf16[576,2048]{1,0:T(8,128)(2,1)} %shard_map.113), kind=kLoop, calls=%fused_computation.44 | loop fusion | bytes 4718592 | tf_op jit(solution)/shard_map/slice | solution.py:344
  14.1 3.5 %collective-permute-start.5 = (bf16[16,2064]{1,0:T(8,128)(2,1)S(1)}, bf16[16,2064]{1,0:T(8,128)(2,1)S(1)}, u32[]{:S(2)}, u32[]{:S(2)}) collective-permute-start(bf16[16,2064]{1,0:T(8,128)(2,1)S(1)} %get-tuple-element.26), channel_id=1, source_target_pairs={{0,8},{1,9},{2,10},{3,11},{4,12},{5,13},{6,14},{7,15},{8,0},{9,1},... | collective-permute-start | bytes 198152 | tf_op jit(solution)/shard_map/ppermute | solution.py:141
  17.6 1.7 %collective-permute-start.11 = (bf16[64,2048]{1,0:T(8,128)(2,1)S(1)}, bf16[64,2048]{1,0:T(8,128)(2,1)S(1)}, u32[]{:S(2)}, u32[]{:S(2)}) collective-permute-start(bf16[64,2048]{1,0:T(8,128)(2,1)S(1)} %pad_maximum_fusion.5), channel_id=1, source_target_pairs={{0,1},{1,0},{2,3},{3,2},{4,5},{5,4},{6,7},{7,6},{8,9},{9,8},{10,11... | collective-permute-start | bytes 786440 | tf_op jit(solution)/shard_map/ppermute | solution.py:141
  19.4 1.6 %collective-permute-start.13 = (bf16[64,2048]{1,0:T(8,128)(2,1)S(1)}, bf16[64,2048]{1,0:T(8,128)(2,1)S(1)}, u32[]{:S(2)}, u32[]{:S(2)}) collective-permute-start(bf16[64,2048]{1,0:T(8,128)(2,1)S(1)} %pad_maximum_fusion.5), channel_id=1, source_target_pairs={{0,2},{1,3},{2,0},{3,1},{4,6},{5,7},{6,4},{7,5},{8,10},{9,11},{10,... | collective-permute-start | bytes 786440 | tf_op jit(solution)/shard_map/ppermute | solution.py:141
  21.0 1.8 %collective-permute-done.5 = bf16[16,2064]{1,0:T(8,128)(2,1)S(1)} collective-permute-done((bf16[16,2064]{1,0:T(8,128)(2,1)S(1)}, bf16[16,2064]{1,0:T(8,128)(2,1)S(1)}, u32[]{:S(2)}, u32[]{:S(2)}) %collective-permute-start.5) | collective-permute-done | bytes 66080 | tf_op jit(solution)/shard_map/ppermute | solution.py:141
  23.8 1.6 %collective-permute-start.7 = (bf16[64,2064]{1,0:T(8,128)(2,1)S(1)}, bf16[64,2064]{1,0:T(8,128)(2,1)S(1)}, u32[]{:S(2)}, u32[]{:S(2)}) collective-permute-start(bf16[64,2064]{1,0:T(8,128)(2,1)S(1)} %get-tuple-element.61), channel_id=1, source_target_pairs={{0,1},{1,0},{2,3},{3,2},{4,5},{5,4},{6,7},{7,6},{8,9},{9,8},{10,11... | collective-permute-start | bytes 792584 | tf_op jit(solution)/shard_map/ppermute | solution.py:141
  25.4 1.5 %collective-permute-start.8 = (bf16[64,2064]{1,0:T(8,128)(2,1)S(1)}, bf16[64,2064]{1,0:T(8,128)(2,1)S(1)}, u32[]{:S(2)}, u32[]{:S(2)}) collective-permute-start(bf16[64,2064]{1,0:T(8,128)(2,1)S(1)} %get-tuple-element.61), channel_id=1, source_target_pairs={{0,2},{1,3},{2,0},{3,1},{4,6},{5,7},{6,4},{7,5},{8,10},{9,11},{10,... | collective-permute-start | bytes 792584 | tf_op jit(solution)/shard_map/ppermute | solution.py:141
  27.8 1.6 %collective-permute-start.15 = (bf16[32,2048]{1,0:T(8,128)(2,1)S(1)}, bf16[32,2048]{1,0:T(8,128)(2,1)S(1)}, u32[]{:S(2)}, u32[]{:S(2)}) collective-permute-start(bf16[32,2048]{1,0:T(8,128)(2,1)S(1)} %slice.131), channel_id=1, source_target_pairs={{0,1},{1,0},{2,3},{3,2},{4,5},{5,4},{6,7},{7,6},{8,9},{9,8},{10,11... | collective-permute-start | bytes 393224 | tf_op jit(solution)/shard_map/ppermute | solution.py:141
  29.4 3.7 %collective-permute-done.7 = bf16[64,2064]{1,0:T(8,128)(2,1)S(1)} collective-permute-done((bf16[64,2064]{1,0:T(8,128)(2,1)S(1)}, bf16[64,2064]{1,0:T(8,128)(2,1)S(1)}, u32[]{:S(2)}, u32[]{:S(2)}) %collective-permute-start.7) | collective-permute-done | bytes 264224 | tf_op jit(solution)/shard_map/ppermute | solution.py:141
  33.2 1.6 %collective-permute-start.9 = (bf16[32,2064]{1,0:T(8,128)(2,1)S(1)}, bf16[32,2064]{1,0:T(8,128)(2,1)S(1)}, u32[]{:S(2)}, u32[]{:S(2)}) collective-permute-start(bf16[32,2064]{1,0:T(8,128)(2,1)S(1)} %slice.124), channel_id=1, source_target_pairs={{0,2},{1,3},{2,0},{3,1},{4,6},{5,7},{6,4},{7,5},{8,10},{9,11},{10,... | collective-permute-start | bytes 396296 | tf_op jit(solution)/shard_map/ppermute | solution.py:141
  37.5 1.4 %collective-permute-done.9 = bf16[32,2064]{1,0:T(8,128)(2,1)S(1)} collective-permute-done((bf16[32,2064]{1,0:T(8,128)(2,1)S(1)}, bf16[32,2064]{1,0:T(8,128)(2,1)S(1)}, u32[]{:S(2)}, u32[]{:S(2)}) %collective-permute-start.9) | collective-permute-done | bytes 132128 | tf_op jit(solution)/shard_map/ppermute | solution.py:141
  46.3 1.4 %collective-permute-start.18 = (bf16[64,2048]{1,0:T(8,128)(2,1)S(1)}, bf16[64,2048]{1,0:T(8,128)(2,1)S(1)}, u32[]{:S(2)}, u32[]{:S(2)}) collective-permute-start(bf16[64,2048]{1,0:T(8,128)(2,1)S(1)} %get-tuple-element.49), channel_id=1, source_target_pairs={{0,3},{1,2},{2,1},{3,0},{4,7},{5,6},{6,5},{7,4},{8,11},{9,10},{10,... | collective-permute-start | bytes 786440 | tf_op jit(solution)/shard_map/ppermute | solution.py:141
  47.7 5.6 %collective-permute-done.16 = bf16[64,2048]{1,0:T(8,128)(2,1)S(1)} collective-permute-done((bf16[64,2048]{1,0:T(8,128)(2,1)S(1)}, bf16[64,2048]{1,0:T(8,128)(2,1)S(1)}, u32[]{:S(2)}, u32[]{:S(2)}) %collective-permute-start.16) | collective-permute-done | bytes 262176 | tf_op jit(solution)/shard_map/ppermute | solution.py:141
  53.3 4.5 %collective-permute-done.17 = bf16[64,2048]{1,0:T(8,128)(2,1)S(1)} collective-permute-done((bf16[64,2048]{1,0:T(8,128)(2,1)S(1)}, bf16[64,2048]{1,0:T(8,128)(2,1)S(1)}, u32[]{:S(2)}, u32[]{:S(2)}) %collective-permute-start.17) | collective-permute-done | bytes 262176 | tf_op jit(solution)/shard_map/ppermute | solution.py:141
  57.9 1.7 %collective-permute-done.18 = bf16[64,2048]{1,0:T(8,128)(2,1)S(1)} collective-permute-done((bf16[64,2048]{1,0:T(8,128)(2,1)S(1)}, bf16[64,2048]{1,0:T(8,128)(2,1)S(1)}, u32[]{:S(2)}, u32[]{:S(2)}) %collective-permute-start.18) | collective-permute-done | bytes 262176 | tf_op jit(solution)/shard_map/ppermute | solution.py:141
  59.8 1.8 %collective-permute-start.22 = (bf16[16,2048]{1,0:T(8,128)(2,1)S(1)}, bf16[16,2048]{1,0:T(8,128)(2,1)S(1)}, u32[]{:S(2)}, u32[]{:S(2)}) collective-permute-start(bf16[16,2048]{1,0:T(8,128)(2,1)S(1)} %get-tuple-element.52), channel_id=1, source_target_pairs={{0,4},{1,5},{2,6},{3,7},{4,0},{5,1},{6,2},{7,3},{8,12},{9,13},{10,... | collective-permute-start | bytes 196616 | tf_op jit(solution)/shard_map/ppermute | solution.py:141
  61.6 2.4 %collective-permute-start.23 = (bf16[16,2048]{1,0:T(8,128)(2,1)S(1)}, bf16[16,2048]{1,0:T(8,128)(2,1)S(1)}, u32[]{:S(2)}, u32[]{:S(2)}) collective-permute-start(bf16[16,2048]{1,0:T(8,128)(2,1)S(1)} %get-tuple-element.54), channel_id=1, source_target_pairs={{0,8},{1,9},{2,10},{3,11},{4,12},{5,13},{6,14},{7,15},{8,0},{9,1},... | collective-permute-start | bytes 196616 | tf_op jit(solution)/shard_map/ppermute | solution.py:141
  64.4 2.5 %shard_map.114 = (bf16[1,192,2048]{2,1,0:T(8,128)(2,1)}, bf16[1,192,2048]{2,1,0:T(8,128)(2,1)}, bf16[1,192,2048]{2,1,0:T(8,128)(2,1)}) custom-call(bf16[256,576]{1,0:T(8,128)(2,1)S(1)} %pad_maximum_fusion.4.own_grads, bf16[256,576]{1,0:T(8,128)(2,1)S(1)} %collective-permute-done.19.other_grads, ...), custom_call_target="tpu_custom_call" | custom-call | bytes 7143424 | tf_op jit(solution)/shard_map/pallas_call | solution.py:154
  66.8 1.6 %collective-permute-done.23 = bf16[16,2048]{1,0:T(8,128)(2,1)S(1)} collective-permute-done((bf16[16,2048]{1,0:T(8,128)(2,1)S(1)}, bf16[16,2048]{1,0:T(8,128)(2,1)S(1)}, u32[]{:S(2)}, u32[]{:S(2)}) %collective-permute-start.23) | collective-permute-done | bytes 65568 | tf_op jit(solution)/shard_map/ppermute | solution.py:141
  68.4 1.6 %collective-permute-done.24 = bf16[16,2048]{1,0:T(8,128)(2,1)S(1)} collective-permute-done((bf16[16,2048]{1,0:T(8,128)(2,1)S(1)}, bf16[16,2048]{1,0:T(8,128)(2,1)S(1)}, u32[]{:S(2)}, u32[]{:S(2)}) %collective-permute-start.24) | collective-permute-done | bytes 65568 | tf_op jit(solution)/shard_map/ppermute | solution.py:141
  (73 shorter events, 14.6 us)
Async XLA Ops:
  0.6 12.5 %collective-permute-start.1 = (bf16[16,2048]{1,0:T(8,128)(2,1)}, bf16[16,2048]{1,0:T(8,128)(2,1)S(1)}, u32[]{:S(2)}, u32[]{:S(2)}) collective-permute-start(bf16[16,2048]{1,0:T(8,128)(2,1)} %tokens_hbm.1), channel_id=1, source_target_pairs={{0,4},{1,5},{2,6},{3,7},{4,0},{5,1},{6,2},{7,3},{8,12},{9,13},{10,... | collective-permute-start | bytes 196616 | tf_op jit(solution)/shard_map/ppermute | solution.py:141
  3.7 9.4 %collective-permute-start.2 = (bf16[16,2048]{1,0:T(8,128)(2,1)}, bf16[16,2048]{1,0:T(8,128)(2,1)S(1)}, u32[]{:S(2)}, u32[]{:S(2)}) collective-permute-start(bf16[16,2048]{1,0:T(8,128)(2,1)} %tokens_hbm.1), channel_id=1, source_target_pairs={{0,8},{1,9},{2,10},{3,11},{4,12},{5,13},{6,14},{7,15},{8,0},{9,1},... | collective-permute-start | bytes 196616 | tf_op jit(solution)/shard_map/ppermute | solution.py:141
  6.3 6.8 %collective-permute-start.3 = (bf16[16,2048]{1,0:T(8,128)(2,1)}, bf16[16,2048]{1,0:T(8,128)(2,1)S(1)}, u32[]{:S(2)}, u32[]{:S(2)}) collective-permute-start(bf16[16,2048]{1,0:T(8,128)(2,1)} %tokens_hbm.1), channel_id=1, source_target_pairs={{0,12},{1,13},{2,14},{3,15},{4,8},{5,9},{6,10},{7,11},{8,4},{9,5},... | collective-permute-start | bytes 196616 | tf_op jit(solution)/shard_map/ppermute | solution.py:141
  13.2 7.8 %collective-permute-start.4 = (bf16[16,2064]{1,0:T(8,128)(2,1)S(1)}, bf16[16,2064]{1,0:T(8,128)(2,1)S(1)}, u32[]{:S(2)}, u32[]{:S(2)}) collective-permute-start(bf16[16,2064]{1,0:T(8,128)(2,1)S(1)} %get-tuple-element.26), channel_id=1, source_target_pairs={{0,4},{1,5},{2,6},{3,7},{4,0},{5,1},{6,2},{7,3},{8,12},{9,13},{10,... | collective-permute-start | bytes 198152 | tf_op jit(solution)/shard_map/ppermute | solution.py:141
  14.1 8.7 %collective-permute-start.5 = (bf16[16,2064]{1,0:T(8,128)(2,1)S(1)}, bf16[16,2064]{1,0:T(8,128)(2,1)S(1)}, u32[]{:S(2)}, u32[]{:S(2)}) collective-permute-start(bf16[16,2064]{1,0:T(8,128)(2,1)S(1)} %get-tuple-element.26), channel_id=1, source_target_pairs={{0,8},{1,9},{2,10},{3,11},{4,12},{5,13},{6,14},{7,15},{8,0},{9,1},... | collective-permute-start | bytes 198152 | tf_op jit(solution)/shard_map/ppermute | solution.py:141
  17.6 6.2 %collective-permute-start.6 = (bf16[16,2064]{1,0:T(8,128)(2,1)S(1)}, bf16[16,2064]{1,0:T(8,128)(2,1)S(1)}, u32[]{:S(2)}, u32[]{:S(2)}) collective-permute-start(bf16[16,2064]{1,0:T(8,128)(2,1)S(1)} %get-tuple-element.26), channel_id=1, source_target_pairs={{0,12},{1,13},{2,14},{3,15},{4,8},{5,9},{6,10},{7,11},{8,4},{9,5},... | collective-permute-start | bytes 198152 | tf_op jit(solution)/shard_map/ppermute | solution.py:141
  17.6 9.3 %collective-permute-start.11 = (bf16[64,2048]{1,0:T(8,128)(2,1)S(1)}, bf16[64,2048]{1,0:T(8,128)(2,1)S(1)}, u32[]{:S(2)}, u32[]{:S(2)}) collective-permute-start(bf16[64,2048]{1,0:T(8,128)(2,1)S(1)} %pad_maximum_fusion.5), channel_id=1, source_target_pairs={{0,1},{1,0},{2,3},{3,2},{4,5},{5,4},{6,7},{7,6},{8,9},{9,8},{10,11... | collective-permute-start | bytes 786440 | tf_op jit(solution)/shard_map/ppermute | solution.py:141
  19.4 8.4 %collective-permute-start.13 = (bf16[64,2048]{1,0:T(8,128)(2,1)S(1)}, bf16[64,2048]{1,0:T(8,128)(2,1)S(1)}, u32[]{:S(2)}, u32[]{:S(2)}) collective-permute-start(bf16[64,2048]{1,0:T(8,128)(2,1)S(1)} %pad_maximum_fusion.5), channel_id=1, source_target_pairs={{0,2},{1,3},{2,0},{3,1},{4,6},{5,7},{6,4},{7,5},{8,10},{9,11},{10,... | collective-permute-start | bytes 786440 | tf_op jit(solution)/shard_map/ppermute | solution.py:141
  23.8 9.3 %collective-permute-start.7 = (bf16[64,2064]{1,0:T(8,128)(2,1)S(1)}, bf16[64,2064]{1,0:T(8,128)(2,1)S(1)}, u32[]{:S(2)}, u32[]{:S(2)}) collective-permute-start(bf16[64,2064]{1,0:T(8,128)(2,1)S(1)} %get-tuple-element.61), channel_id=1, source_target_pairs={{0,1},{1,0},{2,3},{3,2},{4,5},{5,4},{6,7},{7,6},{8,9},{9,8},{10,11... | collective-permute-start | bytes 792584 | tf_op jit(solution)/shard_map/ppermute | solution.py:141
  25.4 9.6 %collective-permute-start.8 = (bf16[64,2064]{1,0:T(8,128)(2,1)S(1)}, bf16[64,2064]{1,0:T(8,128)(2,1)S(1)}, u32[]{:S(2)}, u32[]{:S(2)}) collective-permute-start(bf16[64,2064]{1,0:T(8,128)(2,1)S(1)} %get-tuple-element.61), channel_id=1, source_target_pairs={{0,2},{1,3},{2,0},{3,1},{4,6},{5,7},{6,4},{7,5},{8,10},{9,11},{10,... | collective-permute-start | bytes 792584 | tf_op jit(solution)/shard_map/ppermute | solution.py:141
  26.9 10.4 %collective-permute-start.14 = (bf16[32,2048]{1,0:T(8,128)(2,1)S(1)}, bf16[32,2048]{1,0:T(8,128)(2,1)S(1)}, u32[]{:S(2)}, u32[]{:S(2)}) collective-permute-start(bf16[32,2048]{1,0:T(8,128)(2,1)S(1)} %slice.130), channel_id=1, source_target_pairs={{0,2},{1,3},{2,0},{3,1},{4,6},{5,7},{6,4},{7,5},{8,10},{9,11},{10,... | collective-permute-start | bytes 393224 | tf_op jit(solution)/shard_map/ppermute | solution.py:141
  27.8 9.6 %collective-permute-start.15 = (bf16[32,2048]{1,0:T(8,128)(2,1)S(1)}, bf16[32,2048]{1,0:T(8,128)(2,1)S(1)}, u32[]{:S(2)}, u32[]{:S(2)}) collective-permute-start(bf16[32,2048]{1,0:T(8,128)(2,1)S(1)} %slice.131), channel_id=1, source_target_pairs={{0,1},{1,0},{2,3},{3,2},{4,5},{5,4},{6,7},{7,6},{8,9},{9,8},{10,11... | collective-permute-start | bytes 393224 | tf_op jit(solution)/shard_map/ppermute | solution.py:141
  29.4 11.0 %collective-permute-start.12 = (bf16[576,2048]{1,0:T(8,128)(2,1)S(1)}, bf16[576,2048]{1,0:T(8,128)(2,1)S(1)}, u32[]{:S(2)}, u32[]{:S(2)}) collective-permute-start(bf16[576,2048]{1,0:T(8,128)(2,1)S(1)} %copy-done.2), channel_id=1, source_target_pairs={{0,16},{16,0},{1,17},{17,1},{2,18},{18,2},{3,19},{19,3},{4,20},{20... | collective-permute-start | bytes 7077896 | tf_op jit(solution)/shard_map/ppermute | solution.py:133
  33.2 5.7 %collective-permute-start.9 = (bf16[32,2064]{1,0:T(8,128)(2,1)S(1)}, bf16[32,2064]{1,0:T(8,128)(2,1)S(1)}, u32[]{:S(2)}, u32[]{:S(2)}) collective-permute-start(bf16[32,2064]{1,0:T(8,128)(2,1)S(1)} %slice.124), channel_id=1, source_target_pairs={{0,2},{1,3},{2,0},{3,1},{4,6},{5,7},{6,4},{7,5},{8,10},{9,11},{10,... | collective-permute-start | bytes 396296 | tf_op jit(solution)/shard_map/ppermute | solution.py:141
  35.0 5.1 %collective-permute-start.10 = (bf16[32,2064]{1,0:T(8,128)(2,1)S(1)}, bf16[32,2064]{1,0:T(8,128)(2,1)S(1)}, u32[]{:S(2)}, u32[]{:S(2)}) collective-permute-start(bf16[32,2064]{1,0:T(8,128)(2,1)S(1)} %slice.125), channel_id=1, source_target_pairs={{0,1},{1,0},{2,3},{3,2},{4,5},{5,4},{6,7},{7,6},{8,9},{9,8},{10,11... | collective-permute-start | bytes 396296 | tf_op jit(solution)/shard_map/ppermute | solution.py:141
  37.4 22.3 %collective-permute-start.20 = (bf16[256,2048]{1,0:T(8,128)(2,1)S(1)}, bf16[256,2048]{1,0:T(8,128)(2,1)S(1)}, u32[]{:S(2)}, u32[]{:S(2)}) collective-permute-start(bf16[256,2048]{1,0:T(8,128)(2,1)S(1)} %constant_dynamic-update-slice_fusion.12.rows), channel_id=1, source_target_pairs={{0,16},{16,0},{1,17},{17,1},{2,18},{18,2},{3,19},{19,3},{4,20},{20... | collective-permute-start | bytes 3145736 | tf_op jit(solution)/shard_map/ppermute | solution.py:133
  44.0 15.7 %collective-permute-start.21 = (bf16[256,2048]{1,0:T(8,128)(2,1)S(1)}, bf16[256,2048]{1,0:T(8,128)(2,1)S(1)}, u32[]{:S(2)}, u32[]{:S(2)}) collective-permute-start(bf16[256,2048]{1,0:T(8,128)(2,1)S(1)} %slice.127.upstream), channel_id=1, source_target_pairs={{0,16},{16,0},{1,17},{17,1},{2,18},{18,2},{3,19},{19,3},{4,20},{20... | collective-permute-start | bytes 3145736 | tf_op jit(solution)/shard_map/ppermute | solution.py:133
  44.2 9.2 %collective-permute-start.16 = (bf16[64,2048]{1,0:T(8,128)(2,1)S(1)}, bf16[64,2048]{1,0:T(8,128)(2,1)S(1)}, u32[]{:S(2)}, u32[]{:S(2)}) collective-permute-start(bf16[64,2048]{1,0:T(8,128)(2,1)S(1)} %get-tuple-element.48), channel_id=1, source_target_pairs={{0,1},{1,0},{2,3},{3,2},{4,5},{5,4},{6,7},{7,6},{8,9},{9,8},{10,11... | collective-permute-start | bytes 786440 | tf_op jit(solution)/shard_map/ppermute | solution.py:141
  45.5 12.4 %collective-permute-start.17 = (bf16[64,2048]{1,0:T(8,128)(2,1)S(1)}, bf16[64,2048]{1,0:T(8,128)(2,1)S(1)}, u32[]{:S(2)}, u32[]{:S(2)}) collective-permute-start(bf16[64,2048]{1,0:T(8,128)(2,1)S(1)} %get-tuple-element.50), channel_id=1, source_target_pairs={{0,2},{1,3},{2,0},{3,1},{4,6},{5,7},{6,4},{7,5},{8,10},{9,11},{10,... | collective-permute-start | bytes 786440 | tf_op jit(solution)/shard_map/ppermute | solution.py:141
  46.3 13.3 %collective-permute-start.18 = (bf16[64,2048]{1,0:T(8,128)(2,1)S(1)}, bf16[64,2048]{1,0:T(8,128)(2,1)S(1)}, u32[]{:S(2)}, u32[]{:S(2)}) collective-permute-start(bf16[64,2048]{1,0:T(8,128)(2,1)S(1)} %get-tuple-element.49), channel_id=1, source_target_pairs={{0,3},{1,2},{2,1},{3,0},{4,7},{5,6},{6,5},{7,4},{8,11},{9,10},{10,... | collective-permute-start | bytes 786440 | tf_op jit(solution)/shard_map/ppermute | solution.py:141
  53.3 6.4 %collective-permute-start.19 = (bf16[256,576]{1,0:T(8,128)(2,1)S(1)}, bf16[256,576]{1,0:T(8,128)(2,1)S(1)}, u32[]{:S(2)}, u32[]{:S(2)}) collective-permute-start(bf16[256,576]{1,0:T(8,128)(2,1)S(1)} %pad_maximum_fusion.3), channel_id=1, source_target_pairs={{0,16},{16,0},{1,17},{17,1},{2,18},{18,2},{3,19},{19,3},{4,20},{20... | collective-permute-start | bytes 884744 | tf_op jit(solution)/shard_map/ppermute | solution.py:133
  59.8 7.1 %collective-permute-start.22 = (bf16[16,2048]{1,0:T(8,128)(2,1)S(1)}, bf16[16,2048]{1,0:T(8,128)(2,1)S(1)}, u32[]{:S(2)}, u32[]{:S(2)}) collective-permute-start(bf16[16,2048]{1,0:T(8,128)(2,1)S(1)} %get-tuple-element.52), channel_id=1, source_target_pairs={{0,4},{1,5},{2,6},{3,7},{4,0},{5,1},{6,2},{7,3},{8,12},{9,13},{10,... | collective-permute-start | bytes 196616 | tf_op jit(solution)/shard_map/ppermute | solution.py:141
  61.6 6.8 %collective-permute-start.23 = (bf16[16,2048]{1,0:T(8,128)(2,1)S(1)}, bf16[16,2048]{1,0:T(8,128)(2,1)S(1)}, u32[]{:S(2)}, u32[]{:S(2)}) collective-permute-start(bf16[16,2048]{1,0:T(8,128)(2,1)S(1)} %get-tuple-element.54), channel_id=1, source_target_pairs={{0,8},{1,9},{2,10},{3,11},{4,12},{5,13},{6,14},{7,15},{8,0},{9,1},... | collective-permute-start | bytes 196616 | tf_op jit(solution)/shard_map/ppermute | solution.py:141
  63.9 6.1 %collective-permute-start.24 = (bf16[16,2048]{1,0:T(8,128)(2,1)S(1)}, bf16[16,2048]{1,0:T(8,128)(2,1)S(1)}, u32[]{:S(2)}, u32[]{:S(2)}) collective-permute-start(bf16[16,2048]{1,0:T(8,128)(2,1)S(1)} %get-tuple-element.53), channel_id=1, source_target_pairs={{0,12},{1,13},{2,14},{3,15},{4,8},{5,9},{6,10},{7,11},{8,4},{9,5},... | collective-permute-start | bytes 196616 | tf_op jit(solution)/shard_map/ppermute | solution.py:141
  (5 other events, 27.2 us)

commit v15 on v11

--- a/solution.py
+++ b/solution.py
@@ -234,15 +234,25 @@
     return [value] + [shift_outer(value, count, inner, step) for step in range(1, count // inner)]
 
 
-def across_inner(column, count, inner):
-    if inner < 4:
-        return [column] + [swap_inner(column, count, partner) for partner in range(1, inner)]
-    cut = column.shape[0] // 2
-    first = swap_inner(column, count, 1)
-    second = swap_inner(column, count, 2)
-    far_top = swap_inner(first[:cut], count, 2)
-    far_bottom = swap_inner(second[cut:], count, 1)
-    return [column, first, second, far_top, far_bottom]
+def stack_kernel(*refs):
+    low = 0
+    for ref in refs[:-1]:
+        refs[-1][low : low + ref.shape[0], :] = ref[...]
+        low += ref.shape[0]
+
+
+def stack(blocks):
+    rows = sum(block.shape[0] for block in blocks)
+    return on_chip(stack_kernel, [((rows, blocks[0].shape[1]), blocks[0].dtype)], *blocks)[0]
+
+
+def near_inner(column, count):
+    return [swap_inner(column, count, 1), swap_inner(column, count, 2)]
+
+
+def far_inner(near, count):
+    cut = near[0].shape[0] // 2
+    return [swap_inner(near[0][:cut], count, 2), swap_inner(near[1][cut:], count, 1)]
 
 
 def return_inner(value, count, inner):
@@ -302,14 +312,24 @@
     )
     token_column = jnp.concatenate([own_tokens, *token_blocks[1:]], axis=0)
     payload, token_column = lax.optimization_barrier((payload, token_column))
-    upstream_column = jnp.concatenate(along_outer(payload, count, inner), axis=0)
-    token_columns = across_inner(token_column, count, inner)
-    own_weights = jnp.concatenate([w_gate[0], w_up[0], w_down[0]], axis=0)
-    sent_weights, token_columns[1] = lax.optimization_barrier((own_weights, token_columns[1]))
-    other = swap(sent_weights)
-    inputs = jnp.concatenate(token_columns, axis=0)
+    token_near = near_inner(token_column, count)
+    upstream_column = stack(along_outer(payload, count, inner))
+    near_rows = stack([token_column, *token_near])
+    near_rows, upstream_column, weights = lax.optimization_barrier(
+        (near_rows, upstream_column, [w_gate[0], w_up[0], w_down[0]])
+    )
+    own_weights = jnp.concatenate(weights, axis=0)
+    depth = token_column.shape[0]
+    token_near = [near_rows[depth : 2 * depth], near_rows[2 * depth :]]
+    upstream_near = near_inner(upstream_column, count)
+    token_far = far_inner(token_near, count)
+    other = swap(own_weights)
+    inputs = jnp.concatenate([near_rows, *token_far], axis=0)
+    upstream_near, inputs = lax.optimization_barrier((upstream_near, inputs))
+    upstream = jnp.concatenate(
+        [upstream_column, *upstream_near, *far_inner(upstream_near, count)], axis=0
+    )
     other_inputs = swap(inputs)
-    upstream = jnp.concatenate(across_inner(upstream_column, count, inner), axis=0)
     gate = jnp.sum(
         upstream[:, model_width:].astype(jnp.float32) * here[:1], axis=1, keepdims=True
     )

time: 69.9 us -> 71.1 us (1.017)
  waiting for transfers between devices: 27.6 us -> 29.4 us
    concatenate x1 -> x2, other arithmetic: 1.81 us -> 0.35 us  [the longest x1 0.28 us: dense_local(): own_weights = jnp.concatenate(weights, axis=0)]
    ppermute x5, waiting for transfers between devices: 0.01 us -> 1.38 us  [swap(): return lax.ppermute(value, 'dp', [(0, 1), (1, 0)])]
    ppermute x11, waiting for transfers between devices: 20.5 us -> 21.6 us  [swap_inner(): lax.ppermute(value, 'expert', [(place, place ^ partner) for place in rang...]
    concatenate x1, other arithmetic: 0.02 us -> 0.86 us  [dense_local(): token_column = jnp.concatenate([own_tokens, *token_blocks[1:]], axis=0)]
    unnamed x22 -> x14, local copies, waits for them, and re-layouts: 1.48 us -> 1.64 us
    pallas_call x3 -> x5, Pallas kernels: 4.21 us -> 4.29 us  [on_chip(): pl.pallas_call(body, out_shape=[jax.ShapeDtypeStruct(shape, dtype) for sh...]
  transfers between devices with their start and end apart: 25 -> 25, of which waited for: 12 -> 12; matrix products, arithmetic and copies ran while one was open for 9% -> 7% of each run, Pallas kernels for 6% -> 6%
where the time goes in v15:
time: 71.1 us; the launch traced here: 70.8 us
  waiting for transfers between devices  29.4 us (41%)
  starting transfers between devices  28.5 us (40%)
  Pallas kernels  4.29 us (6%)
  matrix products  3.06 us (4%)
  other arithmetic  2.39 us (3%)
  local copies, waits for them, and re-layouts  2.31 us (3%)
  between operations  0.91 us (1%)
    ppermute x11, waiting for transfers between devices, swap_inner(): lax.ppermute(value, 'expert', [(place, place ^ partner) for place in rang...  21.6 us
    ppermute x9, starting transfers between devices, shift_outer(): lax.ppermute(value, 'expert', [(place, (place + step * inner) % count) fo...  15.3 us
    ppermute x11, starting transfers between devices, swap_inner(): lax.ppermute(value, 'expert', [(place, place ^ partner) for place in rang...  12.9 us
    ppermute x9, waiting for transfers between devices, shift_outer(): lax.ppermute(value, 'expert', [(place, (place + step * inner) % count) fo...  6.42 us
    pallas_call x5, Pallas kernels, on_chip(): pl.pallas_call(body, out_shape=[jax.ShapeDtypeStruct(shape, dtype) for sh...  4.29 us
    unnamed x14, local copies, waits for them, and re-layouts  1.64 us
  transfers between devices with their start and end apart: 25, of which 12 were waited for; matrix products, arithmetic and copies ran while one was open for 7% of the time, Pallas kernels for 6%

profile of v15, /device:TPU:0, one launch (start us, length us, event | category | flops | bytes accessed | tf_op | source)
XLA Modules:
  0.0 70.8 jit_solution(14215924804907023894)
XLA Ops:
  0.6 5.1 %collective-permute-start.3 = (bf16[16,2048]{1,0:T(8,128)(2,1)}, bf16[16,2048]{1,0:T(8,128)(2,1)S(1)}, u32[]{:S(2)}, u32[]{:S(2)}) collective-permute-start(bf16[16,2048]{1,0:T(8,128)(2,1)} %tokens_hbm.1), channel_id=1, source_target_pairs={{0,12},{1,13},{2,14},{3,15},{4,0},{5,1},{6,2},{7,3},{8,4},{9,5},{1... | collective-permute-start | bytes 196616 | tf_op jit(solution)/shard_map/ppermute | solution.py:137
  5.7 1.0 %collective-permute-start.1 = (bf16[16,2048]{1,0:T(8,128)(2,1)}, bf16[16,2048]{1,0:T(8,128)(2,1)S(1)}, u32[]{:S(2)}, u32[]{:S(2)}) collective-permute-start(bf16[16,2048]{1,0:T(8,128)(2,1)} %tokens_hbm.1), channel_id=1, source_target_pairs={{0,4},{1,5},{2,6},{3,7},{4,8},{5,9},{6,10},{7,11},{8,12},{9,13},{1... | collective-permute-start | bytes 196616 | tf_op jit(solution)/shard_map/ppermute | solution.py:137
  6.7 1.6 %shard_map.111 = (bf16[32,16]{1,0:T(8,128)(2,1)}, bf16[16,2048]{1,0:T(8,128)(2,1)}, bf16[16,2048]{1,0:T(8,128)(2,1)}) custom-call(s32[8,16]{1,0:T(8,128)} %bitcast.17, bf16[8,16]{1,0:T(8,128)(2,1)} %bitcast.18, s32[1,16]{1,0:T(1,128)} %bitcast.19, bf16[16,2048]{1,0:T(8,128)(2,1)} %tokens_hbm.1, bf16[16,2048]{1,0:T(8,128)(2,1)} %cotangent_hbm.1), custom_call_target="tpu_custom_call" | custom-call | bytes 264000 | tf_op jit(solution)/shard_map/pallas_call | solution.py:156
  8.4 1.4 %collective-permute-done.other_ref = bf16[32,16]{1,0:T(8,128)(2,1)S(1)} collective-permute-done((bf16[32,16]{1,0:T(8,128)(2,1)}, bf16[32,16]{1,0:T(8,128)(2,1)S(1)}, u32[]{:S(2)}, u32[]{:S(2)}) %collective-permute-start) | collective-permute-done | bytes 1056 | tf_op jit(solution)/shard_map/ppermute | solution.py:133
  13.3 1.6 %collective-permute-start.4 = (bf16[64,2048]{1,0:T(8,128)(2,1)S(1)}, bf16[64,2048]{1,0:T(8,128)(2,1)S(1)}, u32[]{:S(2)}, u32[]{:S(2)}) collective-permute-start(bf16[64,2048]{1,0:T(8,128)(2,1)S(1)} %pad_maximum_fusion.7.refs_0_), channel_id=1, source_target_pairs={{0,1},{1,0},{2,3},{3,2},{4,5},{5,4},{6,7},{7,6},{8,9},{9,8},{10,11... | collective-permute-start | bytes 786440 | tf_op jit(solution)/shard_map/ppermute | solution.py:143
  14.8 1.5 %collective-permute-start.5 = (bf16[64,2048]{1,0:T(8,128)(2,1)S(1)}, bf16[64,2048]{1,0:T(8,128)(2,1)S(1)}, u32[]{:S(2)}, u32[]{:S(2)}) collective-permute-start(bf16[64,2048]{1,0:T(8,128)(2,1)S(1)} %pad_maximum_fusion.7.refs_0_), channel_id=1, source_target_pairs={{0,2},{1,3},{2,0},{3,1},{4,6},{5,7},{6,4},{7,5},{8,10},{9,11},{10,... | collective-permute-start | bytes 786440 | tf_op jit(solution)/shard_map/ppermute | solution.py:143
  16.4 1.7 %collective-permute-start.6 = (bf16[16,2064]{1,0:T(8,128)(2,1)S(1)}, bf16[16,2064]{1,0:T(8,128)(2,1)S(1)}, u32[]{:S(2)}, u32[]{:S(2)}) collective-permute-start(bf16[16,2064]{1,0:T(8,128)(2,1)S(1)} %get-tuple-element.33.refs_0_), channel_id=1, source_target_pairs={{0,4},{1,5},{2,6},{3,7},{4,8},{5,9},{6,10},{7,11},{8,12},{9,13},{1... | collective-permute-start | bytes 198152 | tf_op jit(solution)/shard_map/ppermute | solution.py:137
  19.0 2.1 %collective-permute-start.8 = (bf16[16,2064]{1,0:T(8,128)(2,1)S(1)}, bf16[16,2064]{1,0:T(8,128)(2,1)S(1)}, u32[]{:S(2)}, u32[]{:S(2)}) collective-permute-start(bf16[16,2064]{1,0:T(8,128)(2,1)S(1)} %get-tuple-element.33.refs_0_), channel_id=1, source_target_pairs={{0,12},{1,13},{2,14},{3,15},{4,0},{5,1},{6,2},{7,3},{8,4},{9,5},{1... | collective-permute-start | bytes 198152 | tf_op jit(solution)/shard_map/ppermute | solution.py:137
  21.1 1.8 %collective-permute-done.6.refs_1_ = bf16[16,2064]{1,0:T(8,128)(2,1)S(1)} collective-permute-done((bf16[16,2064]{1,0:T(8,128)(2,1)S(1)}, bf16[16,2064]{1,0:T(8,128)(2,1)S(1)}, u32[]{:S(2)}, u32[]{:S(2)}) %collective-permute-start.6) | collective-permute-done | bytes 66080 | tf_op jit(solution)/shard_map/ppermute | solution.py:137
  22.9 2.1 %collective-permute-done.7.refs_2_ = bf16[16,2064]{1,0:T(8,128)(2,1)S(1)} collective-permute-done((bf16[16,2064]{1,0:T(8,128)(2,1)S(1)}, bf16[16,2064]{1,0:T(8,128)(2,1)S(1)}, u32[]{:S(2)}, u32[]{:S(2)}) %collective-permute-start.7) | collective-permute-done | bytes 66080 | tf_op jit(solution)/shard_map/ppermute | solution.py:137
  26.6 1.6 %collective-permute-start.12 = (bf16[32,2048]{1,0:T(8,128)(2,1)S(1)}, bf16[32,2048]{1,0:T(8,128)(2,1)S(1)}, u32[]{:S(2)}, u32[]{:S(2)}) collective-permute-start(bf16[32,2048]{1,0:T(8,128)(2,1)S(1)} %get-tuple-element.62), channel_id=1, source_target_pairs={{0,1},{1,0},{2,3},{3,2},{4,5},{5,4},{6,7},{7,6},{8,9},{9,8},{10,11... | collective-permute-start | bytes 393224 | tf_op jit(solution)/shard_map/ppermute | solution.py:143
  28.2 1.5 %collective-permute-start.11 = (bf16[32,2048]{1,0:T(8,128)(2,1)S(1)}, bf16[32,2048]{1,0:T(8,128)(2,1)S(1)}, u32[]{:S(2)}, u32[]{:S(2)}) collective-permute-start(bf16[32,2048]{1,0:T(8,128)(2,1)S(1)} %get-tuple-element.61), channel_id=1, source_target_pairs={{0,2},{1,3},{2,0},{3,1},{4,6},{5,7},{6,4},{7,5},{8,10},{9,11},{10,... | collective-permute-start | bytes 393224 | tf_op jit(solution)/shard_map/ppermute | solution.py:143
  29.7 5.9 %collective-permute-done.12 = bf16[32,2048]{1,0:T(8,128)(2,1)S(1)} collective-permute-done((bf16[32,2048]{1,0:T(8,128)(2,1)S(1)}, bf16[32,2048]{1,0:T(8,128)(2,1)S(1)}, u32[]{:S(2)}, u32[]{:S(2)}) %collective-permute-start.12) | collective-permute-done | bytes 131104 | tf_op jit(solution)/shard_map/ppermute | solution.py:143
  36.7 1.6 %collective-permute-start.14 = (bf16[32,2064]{1,0:T(8,128)(2,1)S(1)}, bf16[32,2064]{1,0:T(8,128)(2,1)S(1)}, u32[]{:S(2)}, u32[]{:S(2)}) collective-permute-start(bf16[32,2064]{1,0:T(8,128)(2,1)S(1)} %slice.93), channel_id=1, source_target_pairs={{0,1},{1,0},{2,3},{3,2},{4,5},{5,4},{6,7},{7,6},{8,9},{9,8},{10,11... | collective-permute-start | bytes 396296 | tf_op jit(solution)/shard_map/ppermute | solution.py:143
  38.2 2.9 %collective-permute-done.13 = bf16[32,2064]{1,0:T(8,128)(2,1)S(1)} collective-permute-done((bf16[32,2064]{1,0:T(8,128)(2,1)S(1)}, bf16[32,2064]{1,0:T(8,128)(2,1)S(1)}, u32[]{:S(2)}, u32[]{:S(2)}) %collective-permute-start.13) | collective-permute-done | bytes 132128 | tf_op jit(solution)/shard_map/ppermute | solution.py:143
  42.2 1.0 %fusion.7 = f32[256,768]{1,0:T(8,128)S(1)} fusion(bf16[256,2048]{1,0:T(8,128)(2,1)S(1)} %pad_maximum_fusion.2.rows, bf16[192,2048]{1,0:T(8,128)(2,1)S(1)} %get-tuple-element.53, bf16[192,2048]{1,0:T(8,128)(2,1)S(1)} %bitcast.12, bf16[192,2048]{1,0:T(8,128)(2,1)S(1)} %get-tuple-element.54, bf16[192,2048]{1,0:T(8,128)(2,1)S(1)} %bitcast.15), kind=kOutput, calls=%fused_computation.9 | convolution fusion | flops 817889280 | bytes 4980736 | tf_op jit(solution)/shard_map/dot_general | solution.py:342
  44.1 1.2 %convolution_convert_fusion = bf16[256,2048]{1,0:T(8,128)(2,1)S(1)} fusion(bf16[192,2048]{1,0:T(8,128)(2,1)S(1)} %get-tuple-element.53, bf16[192,2048]{1,0:T(8,128)(2,1)S(1)} %bitcast.13, bf16[192,2048]{1,0:T(8,128)(2,1)S(1)} %get-tuple-element.54, bf16[192,2048]{1,0:T(8,128)(2,1)S(1)} %bitcast.16, bf16[256,384]{1,0:T(8,128)(2,1)S(1)} %get-tuple-element.56, ...), kind=kOutput, calls=%fused_computation.1 | convolution fusion | flops 819200000 | bytes 4587520 | tf_op jit(solution)/shard_map/dot_general | solution.py:352
  45.9 2.5 %collective-permute-start.18 = (bf16[64,2048]{1,0:T(8,128)(2,1)S(1)}, bf16[64,2048]{1,0:T(8,128)(2,1)S(1)}, u32[]{:S(2)}, u32[]{:S(2)}) collective-permute-start(bf16[64,2048]{1,0:T(8,128)(2,1)S(1)} %get-tuple-element.58), channel_id=1, source_target_pairs={{0,3},{1,2},{2,1},{3,0},{4,7},{5,6},{6,5},{7,4},{8,11},{9,10},{10,... | collective-permute-start | bytes 786440 | tf_op jit(solution)/shard_map/ppermute | solution.py:143
  49.4 6.6 %collective-permute-done.18 = bf16[64,2048]{1,0:T(8,128)(2,1)S(1)} collective-permute-done((bf16[64,2048]{1,0:T(8,128)(2,1)S(1)}, bf16[64,2048]{1,0:T(8,128)(2,1)S(1)}, u32[]{:S(2)}, u32[]{:S(2)}) %collective-permute-start.18) | collective-permute-done | bytes 262176 | tf_op jit(solution)/shard_map/ppermute | solution.py:143
  56.0 5.2 %collective-permute-done.17 = bf16[64,2048]{1,0:T(8,128)(2,1)S(1)} collective-permute-done((bf16[64,2048]{1,0:T(8,128)(2,1)S(1)}, bf16[64,2048]{1,0:T(8,128)(2,1)S(1)}, u32[]{:S(2)}, u32[]{:S(2)}) %collective-permute-start.17) | collective-permute-done | bytes 262176 | tf_op jit(solution)/shard_map/ppermute | solution.py:143
  61.5 2.1 %collective-permute-start.24 = (bf16[16,2048]{1,0:T(8,128)(2,1)S(1)}, bf16[16,2048]{1,0:T(8,128)(2,1)S(1)}, u32[]{:S(2)}, u32[]{:S(2)}) collective-permute-start(bf16[16,2048]{1,0:T(8,128)(2,1)S(1)} %get-tuple-element.64), channel_id=1, source_target_pairs={{0,4},{1,5},{2,6},{3,7},{4,8},{5,9},{6,10},{7,11},{8,12},{9,13},{1... | collective-permute-start | bytes 196616 | tf_op jit(solution)/shard_map/ppermute | solution.py:137
  64.5 1.5 %collective-permute-start.22 = (bf16[16,2048]{1,0:T(8,128)(2,1)S(1)}, bf16[16,2048]{1,0:T(8,128)(2,1)S(1)}, u32[]{:S(2)}, u32[]{:S(2)}) collective-permute-start(bf16[16,2048]{1,0:T(8,128)(2,1)S(1)} %get-tuple-element.63), channel_id=1, source_target_pairs={{0,12},{1,13},{2,14},{3,15},{4,0},{5,1},{6,2},{7,3},{8,4},{9,5},{1... | collective-permute-start | bytes 196616 | tf_op jit(solution)/shard_map/ppermute | solution.py:137
  66.1 2.5 %shard_map.115 = (bf16[1,192,2048]{2,1,0:T(8,128)(2,1)}, bf16[1,192,2048]{2,1,0:T(8,128)(2,1)}, bf16[1,192,2048]{2,1,0:T(8,128)(2,1)}) custom-call(bf16[256,576]{1,0:T(8,128)(2,1)S(1)} %pad_maximum_fusion.6.own_grads, bf16[256,576]{1,0:T(8,128)(2,1)S(1)} %collective-permute-done.19.other_grads, bf16[256,2048]{1,0:T(8,128)(2,1)S(1)} %pad_maximum_fusion.2.rows, ...), custom_call_target="tpu_custom_call" | custom-call | bytes 7143424 | tf_op jit(solution)/shard_map/pallas_call | solution.py:156
  68.6 1.6 %collective-permute-done.23 = bf16[16,2048]{1,0:T(8,128)(2,1)S(1)} collective-permute-done((bf16[16,2048]{1,0:T(8,128)(2,1)S(1)}, bf16[16,2048]{1,0:T(8,128)(2,1)S(1)}, u32[]{:S(2)}, u32[]{:S(2)}) %collective-permute-start.23) | collective-permute-done | bytes 65568 | tf_op jit(solution)/shard_map/ppermute | solution.py:137
  (68 shorter events, 12.4 us)
Async XLA Ops:
  0.6 10.9 %collective-permute-start.3 = (bf16[16,2048]{1,0:T(8,128)(2,1)}, bf16[16,2048]{1,0:T(8,128)(2,1)S(1)}, u32[]{:S(2)}, u32[]{:S(2)}) collective-permute-start(bf16[16,2048]{1,0:T(8,128)(2,1)} %tokens_hbm.1), channel_id=1, source_target_pairs={{0,12},{1,13},{2,14},{3,15},{4,0},{5,1},{6,2},{7,3},{8,4},{9,5},{1... | collective-permute-start | bytes 196616 | tf_op jit(solution)/shard_map/ppermute | solution.py:137
  5.7 6.7 %collective-permute-start.2 = (bf16[16,2048]{1,0:T(8,128)(2,1)}, bf16[16,2048]{1,0:T(8,128)(2,1)S(1)}, u32[]{:S(2)}, u32[]{:S(2)}) collective-permute-start(bf16[16,2048]{1,0:T(8,128)(2,1)} %tokens_hbm.1), channel_id=1, source_target_pairs={{0,8},{1,9},{2,10},{3,11},{4,12},{5,13},{6,14},{7,15},{8,0},{9,1},... | collective-permute-start | bytes 196616 | tf_op jit(solution)/shard_map/ppermute | solution.py:137
  5.7 6.7 %collective-permute-start.1 = (bf16[16,2048]{1,0:T(8,128)(2,1)}, bf16[16,2048]{1,0:T(8,128)(2,1)S(1)}, u32[]{:S(2)}, u32[]{:S(2)}) collective-permute-start(bf16[16,2048]{1,0:T(8,128)(2,1)} %tokens_hbm.1), channel_id=1, source_target_pairs={{0,4},{1,5},{2,6},{3,7},{4,8},{5,9},{6,10},{7,11},{8,12},{9,13},{1... | collective-permute-start | bytes 196616 | tf_op jit(solution)/shard_map/ppermute | solution.py:137
  13.3 11.7 %collective-permute-start.4 = (bf16[64,2048]{1,0:T(8,128)(2,1)S(1)}, bf16[64,2048]{1,0:T(8,128)(2,1)S(1)}, u32[]{:S(2)}, u32[]{:S(2)}) collective-permute-start(bf16[64,2048]{1,0:T(8,128)(2,1)S(1)} %pad_maximum_fusion.7.refs_0_), channel_id=1, source_target_pairs={{0,1},{1,0},{2,3},{3,2},{4,5},{5,4},{6,7},{7,6},{8,9},{9,8},{10,11... | collective-permute-start | bytes 786440 | tf_op jit(solution)/shard_map/ppermute | solution.py:143
  14.8 10.2 %collective-permute-start.5 = (bf16[64,2048]{1,0:T(8,128)(2,1)S(1)}, bf16[64,2048]{1,0:T(8,128)(2,1)S(1)}, u32[]{:S(2)}, u32[]{:S(2)}) collective-permute-start(bf16[64,2048]{1,0:T(8,128)(2,1)S(1)} %pad_maximum_fusion.7.refs_0_), channel_id=1, source_target_pairs={{0,2},{1,3},{2,0},{3,1},{4,6},{5,7},{6,4},{7,5},{8,10},{9,11},{10,... | collective-permute-start | bytes 786440 | tf_op jit(solution)/shard_map/ppermute | solution.py:143
  16.4 6.5 %collective-permute-start.6 = (bf16[16,2064]{1,0:T(8,128)(2,1)S(1)}, bf16[16,2064]{1,0:T(8,128)(2,1)S(1)}, u32[]{:S(2)}, u32[]{:S(2)}) collective-permute-start(bf16[16,2064]{1,0:T(8,128)(2,1)S(1)} %get-tuple-element.33.refs_0_), channel_id=1, source_target_pairs={{0,4},{1,5},{2,6},{3,7},{4,8},{5,9},{6,10},{7,11},{8,12},{9,13},{1... | collective-permute-start | bytes 198152 | tf_op jit(solution)/shard_map/ppermute | solution.py:137
  18.1 6.9 %collective-permute-start.7 = (bf16[16,2064]{1,0:T(8,128)(2,1)S(1)}, bf16[16,2064]{1,0:T(8,128)(2,1)S(1)}, u32[]{:S(2)}, u32[]{:S(2)}) collective-permute-start(bf16[16,2064]{1,0:T(8,128)(2,1)S(1)} %get-tuple-element.33.refs_0_), channel_id=1, source_target_pairs={{0,8},{1,9},{2,10},{3,11},{4,12},{5,13},{6,14},{7,15},{8,0},{9,1},... | collective-permute-start | bytes 198152 | tf_op jit(solution)/shard_map/ppermute | solution.py:137
  19.0 6.0 %collective-permute-start.8 = (bf16[16,2064]{1,0:T(8,128)(2,1)S(1)}, bf16[16,2064]{1,0:T(8,128)(2,1)S(1)}, u32[]{:S(2)}, u32[]{:S(2)}) collective-permute-start(bf16[16,2064]{1,0:T(8,128)(2,1)S(1)} %get-tuple-element.33.refs_0_), channel_id=1, source_target_pairs={{0,12},{1,13},{2,14},{3,15},{4,0},{5,1},{6,2},{7,3},{8,4},{9,5},{1... | collective-permute-start | bytes 198152 | tf_op jit(solution)/shard_map/ppermute | solution.py:137
  25.1 10.9 %collective-permute-start.9 = (bf16[64,2064]{1,0:T(8,128)(2,1)S(1)}, bf16[64,2064]{1,0:T(8,128)(2,1)S(1)}, u32[]{:S(2)}, u32[]{:S(2)}) collective-permute-start(bf16[64,2064]{1,0:T(8,128)(2,1)S(1)} %shard_map.114), channel_id=1, source_target_pairs={{0,1},{1,0},{2,3},{3,2},{4,5},{5,4},{6,7},{7,6},{8,9},{9,8},{10,11... | collective-permute-start | bytes 792584 | tf_op jit(solution)/shard_map/ppermute | solution.py:143
  25.7 10.3 %collective-permute-start.10 = (bf16[64,2064]{1,0:T(8,128)(2,1)S(1)}, bf16[64,2064]{1,0:T(8,128)(2,1)S(1)}, u32[]{:S(2)}, u32[]{:S(2)}) collective-permute-start(bf16[64,2064]{1,0:T(8,128)(2,1)S(1)} %shard_map.114), channel_id=1, source_target_pairs={{0,2},{1,3},{2,0},{3,1},{4,6},{5,7},{6,4},{7,5},{8,10},{9,11},{10,... | collective-permute-start | bytes 792584 | tf_op jit(solution)/shard_map/ppermute | solution.py:143
  26.5 15.5 %collective-permute-start.15 = (bf16[576,2048]{1,0:T(8,128)(2,1)S(1)}, bf16[576,2048]{1,0:T(8,128)(2,1)S(1)}, u32[]{:S(2)}, u32[]{:S(2)}) collective-permute-start(bf16[576,2048]{1,0:T(8,128)(2,1)S(1)} %pad_maximum_fusion.1), channel_id=1, source_target_pairs={{0,16},{16,0},{1,17},{17,1},{2,18},{18,2},{3,19},{19,3},{4,20},{20... | collective-permute-start | bytes 7077896 | tf_op jit(solution)/shard_map/ppermute | solution.py:133
  26.6 9.0 %collective-permute-start.12 = (bf16[32,2048]{1,0:T(8,128)(2,1)S(1)}, bf16[32,2048]{1,0:T(8,128)(2,1)S(1)}, u32[]{:S(2)}, u32[]{:S(2)}) collective-permute-start(bf16[32,2048]{1,0:T(8,128)(2,1)S(1)} %get-tuple-element.62), channel_id=1, source_target_pairs={{0,1},{1,0},{2,3},{3,2},{4,5},{5,4},{6,7},{7,6},{8,9},{9,8},{10,11... | collective-permute-start | bytes 393224 | tf_op jit(solution)/shard_map/ppermute | solution.py:143
  28.2 7.7 %collective-permute-start.11 = (bf16[32,2048]{1,0:T(8,128)(2,1)S(1)}, bf16[32,2048]{1,0:T(8,128)(2,1)S(1)}, u32[]{:S(2)}, u32[]{:S(2)}) collective-permute-start(bf16[32,2048]{1,0:T(8,128)(2,1)S(1)} %get-tuple-element.61), channel_id=1, source_target_pairs={{0,2},{1,3},{2,0},{3,1},{4,6},{5,7},{6,4},{7,5},{8,10},{9,11},{10,... | collective-permute-start | bytes 393224 | tf_op jit(solution)/shard_map/ppermute | solution.py:143
  36.0 5.1 %collective-permute-start.13 = (bf16[32,2064]{1,0:T(8,128)(2,1)S(1)}, bf16[32,2064]{1,0:T(8,128)(2,1)S(1)}, u32[]{:S(2)}, u32[]{:S(2)}) collective-permute-start(bf16[32,2064]{1,0:T(8,128)(2,1)S(1)} %slice.92), channel_id=1, source_target_pairs={{0,2},{1,3},{2,0},{3,1},{4,6},{5,7},{6,4},{7,5},{8,10},{9,11},{10,... | collective-permute-start | bytes 396296 | tf_op jit(solution)/shard_map/ppermute | solution.py:143
  36.7 5.1 %collective-permute-start.14 = (bf16[32,2064]{1,0:T(8,128)(2,1)S(1)}, bf16[32,2064]{1,0:T(8,128)(2,1)S(1)}, u32[]{:S(2)}, u32[]{:S(2)}) collective-permute-start(bf16[32,2064]{1,0:T(8,128)(2,1)S(1)} %slice.93), channel_id=1, source_target_pairs={{0,1},{1,0},{2,3},{3,2},{4,5},{5,4},{6,7},{7,6},{8,9},{9,8},{10,11... | collective-permute-start | bytes 396296 | tf_op jit(solution)/shard_map/ppermute | solution.py:143
  38.2 23.2 %collective-permute-start.20 = (bf16[256,2048]{1,0:T(8,128)(2,1)S(1)}, bf16[256,2048]{1,0:T(8,128)(2,1)S(1)}, u32[]{:S(2)}, u32[]{:S(2)}) collective-permute-start(bf16[256,2048]{1,0:T(8,128)(2,1)S(1)} %pad_maximum_fusion.2.rows), channel_id=1, source_target_pairs={{0,16},{16,0},{1,17},{17,1},{2,18},{18,2},{3,19},{19,3},{4,20},{20... | collective-permute-start | bytes 3145736 | tf_op jit(solution)/shard_map/ppermute | solution.py:133
  45.7 15.7 %collective-permute-start.21 = (bf16[256,2048]{1,0:T(8,128)(2,1)S(1)}, bf16[256,2048]{1,0:T(8,128)(2,1)S(1)}, u32[]{:S(2)}, u32[]{:S(2)}) collective-permute-start(bf16[256,2048]{1,0:T(8,128)(2,1)S(1)} %slice.117.upstream), channel_id=1, source_target_pairs={{0,16},{16,0},{1,17},{17,1},{2,18},{18,2},{3,19},{19,3},{4,20},{20... | collective-permute-start | bytes 3145736 | tf_op jit(solution)/shard_map/ppermute | solution.py:133
  45.9 10.1 %collective-permute-start.18 = (bf16[64,2048]{1,0:T(8,128)(2,1)S(1)}, bf16[64,2048]{1,0:T(8,128)(2,1)S(1)}, u32[]{:S(2)}, u32[]{:S(2)}) collective-permute-start(bf16[64,2048]{1,0:T(8,128)(2,1)S(1)} %get-tuple-element.58), channel_id=1, source_target_pairs={{0,3},{1,2},{2,1},{3,0},{4,7},{5,6},{6,5},{7,4},{8,11},{9,10},{10,... | collective-permute-start | bytes 786440 | tf_op jit(solution)/shard_map/ppermute | solution.py:143
  48.4 12.8 %collective-permute-start.17 = (bf16[64,2048]{1,0:T(8,128)(2,1)S(1)}, bf16[64,2048]{1,0:T(8,128)(2,1)S(1)}, u32[]{:S(2)}, u32[]{:S(2)}) collective-permute-start(bf16[64,2048]{1,0:T(8,128)(2,1)S(1)} %get-tuple-element.59), channel_id=1, source_target_pairs={{0,2},{1,3},{2,0},{3,1},{4,6},{5,7},{6,4},{7,5},{8,10},{9,11},{10,... | collective-permute-start | bytes 786440 | tf_op jit(solution)/shard_map/ppermute | solution.py:143
  48.9 12.4 %collective-permute-start.16 = (bf16[64,2048]{1,0:T(8,128)(2,1)S(1)}, bf16[64,2048]{1,0:T(8,128)(2,1)S(1)}, u32[]{:S(2)}, u32[]{:S(2)}) collective-permute-start(bf16[64,2048]{1,0:T(8,128)(2,1)S(1)} %get-tuple-element.57), channel_id=1, source_target_pairs={{0,1},{1,0},{2,3},{3,2},{4,5},{5,4},{6,7},{7,6},{8,9},{9,8},{10,11... | collective-permute-start | bytes 786440 | tf_op jit(solution)/shard_map/ppermute | solution.py:143
  56.0 5.4 %collective-permute-start.19 = (bf16[256,576]{1,0:T(8,128)(2,1)S(1)}, bf16[256,576]{1,0:T(8,128)(2,1)S(1)}, u32[]{:S(2)}, u32[]{:S(2)}) collective-permute-start(bf16[256,576]{1,0:T(8,128)(2,1)S(1)} %pad_maximum_fusion.5), channel_id=1, source_target_pairs={{0,16},{16,0},{1,17},{17,1},{2,18},{18,2},{3,19},{19,3},{4,20},{20... | collective-permute-start | bytes 884744 | tf_op jit(solution)/shard_map/ppermute | solution.py:133
  61.5 7.1 %collective-permute-start.24 = (bf16[16,2048]{1,0:T(8,128)(2,1)S(1)}, bf16[16,2048]{1,0:T(8,128)(2,1)S(1)}, u32[]{:S(2)}, u32[]{:S(2)}) collective-permute-start(bf16[16,2048]{1,0:T(8,128)(2,1)S(1)} %get-tuple-element.64), channel_id=1, source_target_pairs={{0,4},{1,5},{2,6},{3,7},{4,8},{5,9},{6,10},{7,11},{8,12},{9,13},{1... | collective-permute-start | bytes 196616 | tf_op jit(solution)/shard_map/ppermute | solution.py:137
  63.6 6.6 %collective-permute-start.23 = (bf16[16,2048]{1,0:T(8,128)(2,1)S(1)}, bf16[16,2048]{1,0:T(8,128)(2,1)S(1)}, u32[]{:S(2)}, u32[]{:S(2)}) collective-permute-start(bf16[16,2048]{1,0:T(8,128)(2,1)S(1)} %get-tuple-element.65), channel_id=1, source_target_pairs={{0,8},{1,9},{2,10},{3,11},{4,12},{5,13},{6,14},{7,15},{8,0},{9,1},... | collective-permute-start | bytes 196616 | tf_op jit(solution)/shard_map/ppermute | solution.py:137
  64.5 5.7 %collective-permute-start.22 = (bf16[16,2048]{1,0:T(8,128)(2,1)S(1)}, bf16[16,2048]{1,0:T(8,128)(2,1)S(1)}, u32[]{:S(2)}, u32[]{:S(2)}) collective-permute-start(bf16[16,2048]{1,0:T(8,128)(2,1)S(1)} %get-tuple-element.63), channel_id=1, source_target_pairs={{0,12},{1,13},{2,14},{3,15},{4,0},{5,1},{6,2},{7,3},{8,4},{9,5},{1... | collective-permute-start | bytes 196616 | tf_op jit(solution)/shard_map/ppermute | solution.py:137
  (6 other events, 47.6 us)

commit v16 on v11

--- a/solution.py
+++ b/solution.py
@@ -301,8 +301,11 @@
         own_cotangent,
     )
     token_column = jnp.concatenate([own_tokens, *token_blocks[1:]], axis=0)
+    early = shift_outer(payload, count, inner, 2)
     payload, token_column = lax.optimization_barrier((payload, token_column))
-    upstream_column = jnp.concatenate(along_outer(payload, count, inner), axis=0)
+    upstream_blocks = [payload, shift_outer(payload, count, inner, 1), early]
+    upstream_blocks.append(shift_outer(payload, count, inner, 3))
+    upstream_column = jnp.concatenate(upstream_blocks, axis=0)
     token_columns = across_inner(token_column, count, inner)
     own_weights = jnp.concatenate([w_gate[0], w_up[0], w_down[0]], axis=0)
     sent_weights, token_columns[1] = lax.optimization_barrier((own_weights, token_columns[1]))

time: 69.9 us -> 68.5 us (0.980)
  waiting for transfers between devices: 27.6 us -> 25.6 us
    ppermute x9, waiting for transfers between devices: 7.12 us -> 5.31 us  [shift_outer(): lax.ppermute(value, 'expert', [(place, (place + step * inner) % count) fo...]
  transfers between devices with their start and end apart: 25 -> 25, of which waited for: 12 -> 11; matrix products, arithmetic and copies ran while one was open for 9% -> 9% of each run, Pallas kernels for 6% -> 6%
where the time goes in v16:
time: 68.5 us; the launch traced here: 68.2 us
  starting transfers between devices  29.2 us (43%)
  waiting for transfers between devices  25.6 us (37%)
  Pallas kernels  4.22 us (6%)
  matrix products  3.05 us (4%)
  other arithmetic  3.01 us (4%)
  local copies, waits for them, and re-layouts  2.19 us (3%)
  between operations  0.97 us (1%)
    ppermute x11, waiting for transfers between devices, swap_inner(): lax.ppermute(value, 'expert', [(place, place ^ partner) for place in rang...  20.3 us
    ppermute x9, starting transfers between devices, shift_outer(): lax.ppermute(value, 'expert', [(place, (place + step * inner) % count) fo...  15.8 us
    ppermute x11, starting transfers between devices, swap_inner(): lax.ppermute(value, 'expert', [(place, place ^ partner) for place in rang...  13.1 us
    ppermute x9, waiting for transfers between devices, shift_outer(): lax.ppermute(value, 'expert', [(place, (place + step * inner) % count) fo...  5.31 us
    pallas_call x3, Pallas kernels, on_chip(): pl.pallas_call(body, out_shape=[jax.ShapeDtypeStruct(shape, dtype) for sh...  4.22 us
    concatenate x1, other arithmetic, dense_local(): own_weights = jnp.concatenate([w_gate[0], w_up[0], w_down[0]], axis=0)  1.81 us
    unnamed x22, local copies, waits for them, and re-layouts  1.49 us
  transfers between devices with their start and end apart: 25, of which 11 were waited for; matrix products, arithmetic and copies ran while one was open for 9% of the time, Pallas kernels for 6%

profile of v16, /device:TPU:0, one launch (start us, length us, event | category | flops | bytes accessed | tf_op | source)
XLA Modules:
  0.0 68.2 jit_solution(16772072504881213786)
XLA Ops:
  0.6 5.1 %collective-permute-start.3 = (bf16[16,2048]{1,0:T(8,128)(2,1)}, bf16[16,2048]{1,0:T(8,128)(2,1)S(1)}, u32[]{:S(2)}, u32[]{:S(2)}) collective-permute-start(bf16[16,2048]{1,0:T(8,128)(2,1)} %tokens_hbm.1), channel_id=1, source_target_pairs={{0,12},{1,13},{2,14},{3,15},{4,0},{5,1},{6,2},{7,3},{8,4},{9,5},{1... | collective-permute-start | bytes 196616 | tf_op jit(solution)/shard_map/ppermute | solution.py:137
  6.7 1.6 %shard_map.111 = (bf16[32,16]{1,0:T(8,128)(2,1)}, bf16[16,2048]{1,0:T(8,128)(2,1)}, bf16[16,2048]{1,0:T(8,128)(2,1)}) custom-call(s32[8,16]{1,0:T(8,128)} %bitcast.17, bf16[8,16]{1,0:T(8,128)(2,1)} %bitcast.18, s32[1,16]{1,0:T(1,128)} %bitcast.19, bf16[16,2048]{1,0:T(8,128)(2,1)} %tokens_hbm.1, bf16[16,2048]{1,0:T(8,128)(2,1)} %cotangent_hbm.1), custom_call_target="tpu_custom_call" | custom-call | bytes 264000 | tf_op jit(solution)/shard_map/pallas_call | solution.py:156
  8.5 1.8 %pad_maximum_fusion.1 = bf16[576,2048]{1,0:T(8,128)(2,1)S(1)} fusion(bf16[192,2048]{1,0:T(8,128)(2,1)} %bitcast.9, bf16[192,2048]{1,0:T(8,128)(2,1)} %bitcast.11, bf16[192,2048]{1,0:T(8,128)(2,1)} %bitcast.14), kind=kLoop, calls=%fused_computation.2 | loop fusion | flops 7077888 | bytes 4718592 | tf_op jit(solution)/shard_map/concatenate | solution.py:310
  10.5 1.9 %collective-permute-start.5 = (bf16[16,2064]{1,0:T(8,128)(2,1)S(1)}, bf16[16,2064]{1,0:T(8,128)(2,1)S(1)}, u32[]{:S(2)}, u32[]{:S(2)}) collective-permute-start(bf16[16,2064]{1,0:T(8,128)(2,1)S(1)} %get-tuple-element.26), channel_id=1, source_target_pairs={{0,8},{1,9},{2,10},{3,11},{4,12},{5,13},{6,14},{7,15},{8,0},{9,1},... | collective-permute-start | bytes 198152 | tf_op jit(solution)/shard_map/ppermute | solution.py:137
  12.4 1.6 %collective-permute-start.11 = (bf16[64,2048]{1,0:T(8,128)(2,1)S(1)}, bf16[64,2048]{1,0:T(8,128)(2,1)S(1)}, u32[]{:S(2)}, u32[]{:S(2)}) collective-permute-start(bf16[64,2048]{1,0:T(8,128)(2,1)S(1)} %pad_maximum_fusion.6), channel_id=1, source_target_pairs={{0,1},{1,0},{2,3},{3,2},{4,5},{5,4},{6,7},{7,6},{8,9},{9,8},{10,11... | collective-permute-start | bytes 786440 | tf_op jit(solution)/shard_map/ppermute | solution.py:143
  14.0 1.6 %collective-permute-start.13 = (bf16[64,2048]{1,0:T(8,128)(2,1)S(1)}, bf16[64,2048]{1,0:T(8,128)(2,1)S(1)}, u32[]{:S(2)}, u32[]{:S(2)}) collective-permute-start(bf16[64,2048]{1,0:T(8,128)(2,1)S(1)} %pad_maximum_fusion.6), channel_id=1, source_target_pairs={{0,2},{1,3},{2,0},{3,1},{4,6},{5,7},{6,4},{7,5},{8,10},{9,11},{10,... | collective-permute-start | bytes 786440 | tf_op jit(solution)/shard_map/ppermute | solution.py:143
  15.6 1.5 %collective-permute-start.4 = (bf16[16,2064]{1,0:T(8,128)(2,1)S(1)}, bf16[16,2064]{1,0:T(8,128)(2,1)S(1)}, u32[]{:S(2)}, u32[]{:S(2)}) collective-permute-start(bf16[16,2064]{1,0:T(8,128)(2,1)S(1)} %get-tuple-element.26), channel_id=1, source_target_pairs={{0,4},{1,5},{2,6},{3,7},{4,8},{5,9},{6,10},{7,11},{8,12},{9,13},{1... | collective-permute-start | bytes 198152 | tf_op jit(solution)/shard_map/ppermute | solution.py:137
  17.1 2.4 %collective-permute-start.6 = (bf16[16,2064]{1,0:T(8,128)(2,1)S(1)}, bf16[16,2064]{1,0:T(8,128)(2,1)S(1)}, u32[]{:S(2)}, u32[]{:S(2)}) collective-permute-start(bf16[16,2064]{1,0:T(8,128)(2,1)S(1)} %get-tuple-element.26), channel_id=1, source_target_pairs={{0,12},{1,13},{2,14},{3,15},{4,0},{5,1},{6,2},{7,3},{8,4},{9,5},{1... | collective-permute-start | bytes 198152 | tf_op jit(solution)/shard_map/ppermute | solution.py:137
  19.5 2.6 %collective-permute-done.4 = bf16[16,2064]{1,0:T(8,128)(2,1)S(1)} collective-permute-done((bf16[16,2064]{1,0:T(8,128)(2,1)S(1)}, bf16[16,2064]{1,0:T(8,128)(2,1)S(1)}, u32[]{:S(2)}, u32[]{:S(2)}) %collective-permute-start.4) | collective-permute-done | bytes 66080 | tf_op jit(solution)/shard_map/ppermute | solution.py:137
  23.3 1.6 %collective-permute-start.14 = (bf16[32,2048]{1,0:T(8,128)(2,1)S(1)}, bf16[32,2048]{1,0:T(8,128)(2,1)S(1)}, u32[]{:S(2)}, u32[]{:S(2)}) collective-permute-start(bf16[32,2048]{1,0:T(8,128)(2,1)S(1)} %slice.117), channel_id=1, source_target_pairs={{0,2},{1,3},{2,0},{3,1},{4,6},{5,7},{6,4},{7,5},{8,10},{9,11},{10,... | collective-permute-start | bytes 393224 | tf_op jit(solution)/shard_map/ppermute | solution.py:143
  24.9 1.6 %collective-permute-start.15 = (bf16[32,2048]{1,0:T(8,128)(2,1)S(1)}, bf16[32,2048]{1,0:T(8,128)(2,1)S(1)}, u32[]{:S(2)}, u32[]{:S(2)}) collective-permute-start(bf16[32,2048]{1,0:T(8,128)(2,1)S(1)} %slice.118), channel_id=1, source_target_pairs={{0,1},{1,0},{2,3},{3,2},{4,5},{5,4},{6,7},{7,6},{8,9},{9,8},{10,11... | collective-permute-start | bytes 393224 | tf_op jit(solution)/shard_map/ppermute | solution.py:143
  26.5 4.2 %collective-permute-done.7 = bf16[64,2064]{1,0:T(8,128)(2,1)S(1)} collective-permute-done((bf16[64,2064]{1,0:T(8,128)(2,1)S(1)}, bf16[64,2064]{1,0:T(8,128)(2,1)S(1)}, u32[]{:S(2)}, u32[]{:S(2)}) %collective-permute-start.7) | collective-permute-done | bytes 264224 | tf_op jit(solution)/shard_map/ppermute | solution.py:143
  31.3 1.0 %collective-permute-done.8 = bf16[64,2064]{1,0:T(8,128)(2,1)S(1)} collective-permute-done((bf16[64,2064]{1,0:T(8,128)(2,1)S(1)}, bf16[64,2064]{1,0:T(8,128)(2,1)S(1)}, u32[]{:S(2)}, u32[]{:S(2)}) %collective-permute-start.8) | collective-permute-done | bytes 264224 | tf_op jit(solution)/shard_map/ppermute | solution.py:143
  32.3 1.6 %collective-permute-start.10 = (bf16[32,2064]{1,0:T(8,128)(2,1)S(1)}, bf16[32,2064]{1,0:T(8,128)(2,1)S(1)}, u32[]{:S(2)}, u32[]{:S(2)}) collective-permute-start(bf16[32,2064]{1,0:T(8,128)(2,1)S(1)} %slice.113), channel_id=1, source_target_pairs={{0,1},{1,0},{2,3},{3,2},{4,5},{5,4},{6,7},{7,6},{8,9},{9,8},{10,11... | collective-permute-start | bytes 396296 | tf_op jit(solution)/shard_map/ppermute | solution.py:143
  34.2 1.7 %collective-permute-done.9 = bf16[32,2064]{1,0:T(8,128)(2,1)S(1)} collective-permute-done((bf16[32,2064]{1,0:T(8,128)(2,1)S(1)}, bf16[32,2064]{1,0:T(8,128)(2,1)S(1)}, u32[]{:S(2)}, u32[]{:S(2)}) %collective-permute-start.9) | collective-permute-done | bytes 132128 | tf_op jit(solution)/shard_map/ppermute | solution.py:143
  35.9 1.6 %collective-permute-done.10 = bf16[32,2064]{1,0:T(8,128)(2,1)S(1)} collective-permute-done((bf16[32,2064]{1,0:T(8,128)(2,1)S(1)}, bf16[32,2064]{1,0:T(8,128)(2,1)S(1)}, u32[]{:S(2)}, u32[]{:S(2)}) %collective-permute-start.10) | collective-permute-done | bytes 132128 | tf_op jit(solution)/shard_map/ppermute | solution.py:143
  39.1 1.0 %fusion.7 = f32[256,768]{1,0:T(8,128)S(1)} fusion(bf16[256,2048]{1,0:T(8,128)(2,1)S(1)} %constant_dynamic-update-slice_fusion.12.rows, bf16[192,2048]{1,0:T(8,128)(2,1)S(1)} %get-tuple-element.41, bf16[192,2048]{1,0:T(8,128)(2,1)S(1)} %bitcast.12, bf16[192,2048]{1,0:T(8,128)(2,1)S(1)} %get-tuple-element.42, bf16[192,2048]{1,0:T(8,128)(2,1)S(1)} %bitcast.15), kind=kOutput, calls=%fused_computation.8 | convolution fusion | flops 817889280 | bytes 4980736 | tf_op jit(solution)/shard_map/dot_general | solution.py:325
  41.1 1.2 %convolution_convert_fusion = bf16[256,2048]{1,0:T(8,128)(2,1)S(1)} fusion(bf16[192,2048]{1,0:T(8,128)(2,1)S(1)} %get-tuple-element.41, bf16[192,2048]{1,0:T(8,128)(2,1)S(1)} %bitcast.13, bf16[192,2048]{1,0:T(8,128)(2,1)S(1)} %get-tuple-element.42, bf16[192,2048]{1,0:T(8,128)(2,1)S(1)} %bitcast.16, bf16[256,384]{1,0:T(8,128)(2,1)S(1)} %get-tuple-element.44, ...), kind=kOutput, calls=%fused_computation.1 | convolution fusion | flops 819200000 | bytes 4587520 | tf_op jit(solution)/shard_map/dot_general | solution.py:335
  43.6 2.3 %collective-permute-start.17 = (bf16[64,2048]{1,0:T(8,128)(2,1)S(1)}, bf16[64,2048]{1,0:T(8,128)(2,1)S(1)}, u32[]{:S(2)}, u32[]{:S(2)}) collective-permute-start(bf16[64,2048]{1,0:T(8,128)(2,1)S(1)} %get-tuple-element.47), channel_id=1, source_target_pairs={{0,2},{1,3},{2,0},{3,1},{4,6},{5,7},{6,4},{7,5},{8,10},{9,11},{10,... | collective-permute-start | bytes 786440 | tf_op jit(solution)/shard_map/ppermute | solution.py:143
  46.4 6.6 %collective-permute-done.18 = bf16[64,2048]{1,0:T(8,128)(2,1)S(1)} collective-permute-done((bf16[64,2048]{1,0:T(8,128)(2,1)S(1)}, bf16[64,2048]{1,0:T(8,128)(2,1)S(1)}, u32[]{:S(2)}, u32[]{:S(2)}) %collective-permute-start.18) | collective-permute-done | bytes 262176 | tf_op jit(solution)/shard_map/ppermute | solution.py:143
  53.0 5.2 %collective-permute-done.17 = bf16[64,2048]{1,0:T(8,128)(2,1)S(1)} collective-permute-done((bf16[64,2048]{1,0:T(8,128)(2,1)S(1)}, bf16[64,2048]{1,0:T(8,128)(2,1)S(1)}, u32[]{:S(2)}, u32[]{:S(2)}) %collective-permute-start.17) | collective-permute-done | bytes 262176 | tf_op jit(solution)/shard_map/ppermute | solution.py:143
  59.0 3.3 %collective-permute-start.23 = (bf16[16,2048]{1,0:T(8,128)(2,1)S(1)}, bf16[16,2048]{1,0:T(8,128)(2,1)S(1)}, u32[]{:S(2)}, u32[]{:S(2)}) collective-permute-start(bf16[16,2048]{1,0:T(8,128)(2,1)S(1)} %get-tuple-element.51), channel_id=1, source_target_pairs={{0,8},{1,9},{2,10},{3,11},{4,12},{5,13},{6,14},{7,15},{8,0},{9,1},... | collective-permute-start | bytes 196616 | tf_op jit(solution)/shard_map/ppermute | solution.py:137
  62.4 2.5 %shard_map.113 = (bf16[1,192,2048]{2,1,0:T(8,128)(2,1)}, bf16[1,192,2048]{2,1,0:T(8,128)(2,1)}, bf16[1,192,2048]{2,1,0:T(8,128)(2,1)}) custom-call(bf16[256,576]{1,0:T(8,128)(2,1)S(1)} %pad_maximum_fusion.5.own_grads, bf16[256,576]{1,0:T(8,128)(2,1)S(1)} %collective-permute-done.19.other_grads, ...), custom_call_target="tpu_custom_call" | custom-call | bytes 7143424 | tf_op jit(solution)/shard_map/pallas_call | solution.py:156
  65.3 1.9 %collective-permute-done.23 = bf16[16,2048]{1,0:T(8,128)(2,1)S(1)} collective-permute-done((bf16[16,2048]{1,0:T(8,128)(2,1)S(1)}, bf16[16,2048]{1,0:T(8,128)(2,1)S(1)}, u32[]{:S(2)}, u32[]{:S(2)}) %collective-permute-start.23) | collective-permute-done | bytes 65568 | tf_op jit(solution)/shard_map/ppermute | solution.py:137
  (76 shorter events, 10.0 us)
Async XLA Ops:
  0.6 11.7 %collective-permute-start.3 = (bf16[16,2048]{1,0:T(8,128)(2,1)}, bf16[16,2048]{1,0:T(8,128)(2,1)S(1)}, u32[]{:S(2)}, u32[]{:S(2)}) collective-permute-start(bf16[16,2048]{1,0:T(8,128)(2,1)} %tokens_hbm.1), channel_id=1, source_target_pairs={{0,12},{1,13},{2,14},{3,15},{4,0},{5,1},{6,2},{7,3},{8,4},{9,5},{1... | collective-permute-start | bytes 196616 | tf_op jit(solution)/shard_map/ppermute | solution.py:137
  5.7 6.7 %collective-permute-start.2 = (bf16[16,2048]{1,0:T(8,128)(2,1)}, bf16[16,2048]{1,0:T(8,128)(2,1)S(1)}, u32[]{:S(2)}, u32[]{:S(2)}) collective-permute-start(bf16[16,2048]{1,0:T(8,128)(2,1)} %tokens_hbm.1), channel_id=1, source_target_pairs={{0,8},{1,9},{2,10},{3,11},{4,12},{5,13},{6,14},{7,15},{8,0},{9,1},... | collective-permute-start | bytes 196616 | tf_op jit(solution)/shard_map/ppermute | solution.py:137
  5.7 6.7 %collective-permute-start.1 = (bf16[16,2048]{1,0:T(8,128)(2,1)}, bf16[16,2048]{1,0:T(8,128)(2,1)S(1)}, u32[]{:S(2)}, u32[]{:S(2)}) collective-permute-start(bf16[16,2048]{1,0:T(8,128)(2,1)} %tokens_hbm.1), channel_id=1, source_target_pairs={{0,4},{1,5},{2,6},{3,7},{4,8},{5,9},{6,10},{7,11},{8,12},{9,13},{1... | collective-permute-start | bytes 196616 | tf_op jit(solution)/shard_map/ppermute | solution.py:137
  10.5 11.6 %collective-permute-start.5 = (bf16[16,2064]{1,0:T(8,128)(2,1)S(1)}, bf16[16,2064]{1,0:T(8,128)(2,1)S(1)}, u32[]{:S(2)}, u32[]{:S(2)}) collective-permute-start(bf16[16,2064]{1,0:T(8,128)(2,1)S(1)} %get-tuple-element.26), channel_id=1, source_target_pairs={{0,8},{1,9},{2,10},{3,11},{4,12},{5,13},{6,14},{7,15},{8,0},{9,1},... | collective-permute-start | bytes 198152 | tf_op jit(solution)/shard_map/ppermute | solution.py:137
  12.4 10.9 %collective-permute-start.11 = (bf16[64,2048]{1,0:T(8,128)(2,1)S(1)}, bf16[64,2048]{1,0:T(8,128)(2,1)S(1)}, u32[]{:S(2)}, u32[]{:S(2)}) collective-permute-start(bf16[64,2048]{1,0:T(8,128)(2,1)S(1)} %pad_maximum_fusion.6), channel_id=1, source_target_pairs={{0,1},{1,0},{2,3},{3,2},{4,5},{5,4},{6,7},{7,6},{8,9},{9,8},{10,11... | collective-permute-start | bytes 786440 | tf_op jit(solution)/shard_map/ppermute | solution.py:143
  14.0 10.9 %collective-permute-start.13 = (bf16[64,2048]{1,0:T(8,128)(2,1)S(1)}, bf16[64,2048]{1,0:T(8,128)(2,1)S(1)}, u32[]{:S(2)}, u32[]{:S(2)}) collective-permute-start(bf16[64,2048]{1,0:T(8,128)(2,1)S(1)} %pad_maximum_fusion.6), channel_id=1, source_target_pairs={{0,2},{1,3},{2,0},{3,1},{4,6},{5,7},{6,4},{7,5},{8,10},{9,11},{10,... | collective-permute-start | bytes 786440 | tf_op jit(solution)/shard_map/ppermute | solution.py:143
  15.6 6.4 %collective-permute-start.4 = (bf16[16,2064]{1,0:T(8,128)(2,1)S(1)}, bf16[16,2064]{1,0:T(8,128)(2,1)S(1)}, u32[]{:S(2)}, u32[]{:S(2)}) collective-permute-start(bf16[16,2064]{1,0:T(8,128)(2,1)S(1)} %get-tuple-element.26), channel_id=1, source_target_pairs={{0,4},{1,5},{2,6},{3,7},{4,8},{5,9},{6,10},{7,11},{8,12},{9,13},{1... | collective-permute-start | bytes 198152 | tf_op jit(solution)/shard_map/ppermute | solution.py:137
  17.1 5.1 %collective-permute-start.6 = (bf16[16,2064]{1,0:T(8,128)(2,1)S(1)}, bf16[16,2064]{1,0:T(8,128)(2,1)S(1)}, u32[]{:S(2)}, u32[]{:S(2)}) collective-permute-start(bf16[16,2064]{1,0:T(8,128)(2,1)S(1)} %get-tuple-element.26), channel_id=1, source_target_pairs={{0,12},{1,13},{2,14},{3,15},{4,0},{5,1},{6,2},{7,3},{8,4},{9,5},{1... | collective-permute-start | bytes 198152 | tf_op jit(solution)/shard_map/ppermute | solution.py:137
  22.2 8.5 %collective-permute-start.7 = (bf16[64,2064]{1,0:T(8,128)(2,1)S(1)}, bf16[64,2064]{1,0:T(8,128)(2,1)S(1)}, u32[]{:S(2)}, u32[]{:S(2)}) collective-permute-start(bf16[64,2064]{1,0:T(8,128)(2,1)S(1)} %get-tuple-element.58), channel_id=1, source_target_pairs={{0,1},{1,0},{2,3},{3,2},{4,5},{5,4},{6,7},{7,6},{8,9},{9,8},{10,11... | collective-permute-start | bytes 792584 | tf_op jit(solution)/shard_map/ppermute | solution.py:143
  22.8 9.5 %collective-permute-start.8 = (bf16[64,2064]{1,0:T(8,128)(2,1)S(1)}, bf16[64,2064]{1,0:T(8,128)(2,1)S(1)}, u32[]{:S(2)}, u32[]{:S(2)}) collective-permute-start(bf16[64,2064]{1,0:T(8,128)(2,1)S(1)} %get-tuple-element.58), channel_id=1, source_target_pairs={{0,2},{1,3},{2,0},{3,1},{4,6},{5,7},{6,4},{7,5},{8,10},{9,11},{10,... | collective-permute-start | bytes 792584 | tf_op jit(solution)/shard_map/ppermute | solution.py:143
  23.3 14.5 %collective-permute-start.12 = (bf16[576,2048]{1,0:T(8,128)(2,1)S(1)}, bf16[576,2048]{1,0:T(8,128)(2,1)S(1)}, u32[]{:S(2)}, u32[]{:S(2)}) collective-permute-start(bf16[576,2048]{1,0:T(8,128)(2,1)S(1)} %pad_maximum_fusion.1), channel_id=1, source_target_pairs={{0,16},{16,0},{1,17},{17,1},{2,18},{18,2},{3,19},{19,3},{4,20},{20... | collective-permute-start | bytes 7077896 | tf_op jit(solution)/shard_map/ppermute | solution.py:133
  23.3 10.7 %collective-permute-start.14 = (bf16[32,2048]{1,0:T(8,128)(2,1)S(1)}, bf16[32,2048]{1,0:T(8,128)(2,1)S(1)}, u32[]{:S(2)}, u32[]{:S(2)}) collective-permute-start(bf16[32,2048]{1,0:T(8,128)(2,1)S(1)} %slice.117), channel_id=1, source_target_pairs={{0,2},{1,3},{2,0},{3,1},{4,6},{5,7},{6,4},{7,5},{8,10},{9,11},{10,... | collective-permute-start | bytes 393224 | tf_op jit(solution)/shard_map/ppermute | solution.py:143
  24.9 9.1 %collective-permute-start.15 = (bf16[32,2048]{1,0:T(8,128)(2,1)S(1)}, bf16[32,2048]{1,0:T(8,128)(2,1)S(1)}, u32[]{:S(2)}, u32[]{:S(2)}) collective-permute-start(bf16[32,2048]{1,0:T(8,128)(2,1)S(1)} %slice.118), channel_id=1, source_target_pairs={{0,1},{1,0},{2,3},{3,2},{4,5},{5,4},{6,7},{7,6},{8,9},{9,8},{10,11... | collective-permute-start | bytes 393224 | tf_op jit(solution)/shard_map/ppermute | solution.py:143
  30.7 5.1 %collective-permute-start.9 = (bf16[32,2064]{1,0:T(8,128)(2,1)S(1)}, bf16[32,2064]{1,0:T(8,128)(2,1)S(1)}, u32[]{:S(2)}, u32[]{:S(2)}) collective-permute-start(bf16[32,2064]{1,0:T(8,128)(2,1)S(1)} %slice.112), channel_id=1, source_target_pairs={{0,2},{1,3},{2,0},{3,1},{4,6},{5,7},{6,4},{7,5},{8,10},{9,11},{10,... | collective-permute-start | bytes 396296 | tf_op jit(solution)/shard_map/ppermute | solution.py:143
  32.3 5.1 %collective-permute-start.10 = (bf16[32,2064]{1,0:T(8,128)(2,1)S(1)}, bf16[32,2064]{1,0:T(8,128)(2,1)S(1)}, u32[]{:S(2)}, u32[]{:S(2)}) collective-permute-start(bf16[32,2064]{1,0:T(8,128)(2,1)S(1)} %slice.113), channel_id=1, source_target_pairs={{0,1},{1,0},{2,3},{3,2},{4,5},{5,4},{6,7},{7,6},{8,9},{9,8},{10,11... | collective-permute-start | bytes 396296 | tf_op jit(solution)/shard_map/ppermute | solution.py:143
  34.1 24.2 %collective-permute-start.20 = (bf16[256,2048]{1,0:T(8,128)(2,1)S(1)}, bf16[256,2048]{1,0:T(8,128)(2,1)S(1)}, u32[]{:S(2)}, u32[]{:S(2)}) collective-permute-start(bf16[256,2048]{1,0:T(8,128)(2,1)S(1)} %constant_dynamic-update-slice_fusion.12.rows), channel_id=1, source_target_pairs={{0,16},{16,0},{1,17},{17,1},{2,18},{18,2},{3,19},{19,3},{4,20},{20... | collective-permute-start | bytes 3145736 | tf_op jit(solution)/shard_map/ppermute | solution.py:133
  42.7 15.6 %collective-permute-start.21 = (bf16[256,2048]{1,0:T(8,128)(2,1)S(1)}, bf16[256,2048]{1,0:T(8,128)(2,1)S(1)}, u32[]{:S(2)}, u32[]{:S(2)}) collective-permute-start(bf16[256,2048]{1,0:T(8,128)(2,1)S(1)} %slice.115.upstream), channel_id=1, source_target_pairs={{0,16},{16,0},{1,17},{17,1},{2,18},{18,2},{3,19},{19,3},{4,20},{20... | collective-permute-start | bytes 3145736 | tf_op jit(solution)/shard_map/ppermute | solution.py:133
  42.8 10.1 %collective-permute-start.18 = (bf16[64,2048]{1,0:T(8,128)(2,1)S(1)}, bf16[64,2048]{1,0:T(8,128)(2,1)S(1)}, u32[]{:S(2)}, u32[]{:S(2)}) collective-permute-start(bf16[64,2048]{1,0:T(8,128)(2,1)S(1)} %get-tuple-element.46), channel_id=1, source_target_pairs={{0,3},{1,2},{2,1},{3,0},{4,7},{5,6},{6,5},{7,4},{8,11},{9,10},{10,... | collective-permute-start | bytes 786440 | tf_op jit(solution)/shard_map/ppermute | solution.py:143
  43.6 14.5 %collective-permute-start.17 = (bf16[64,2048]{1,0:T(8,128)(2,1)S(1)}, bf16[64,2048]{1,0:T(8,128)(2,1)S(1)}, u32[]{:S(2)}, u32[]{:S(2)}) collective-permute-start(bf16[64,2048]{1,0:T(8,128)(2,1)S(1)} %get-tuple-element.47), channel_id=1, source_target_pairs={{0,2},{1,3},{2,0},{3,1},{4,6},{5,7},{6,4},{7,5},{8,10},{9,11},{10,... | collective-permute-start | bytes 786440 | tf_op jit(solution)/shard_map/ppermute | solution.py:143
  45.9 12.2 %collective-permute-start.16 = (bf16[64,2048]{1,0:T(8,128)(2,1)S(1)}, bf16[64,2048]{1,0:T(8,128)(2,1)S(1)}, u32[]{:S(2)}, u32[]{:S(2)}) collective-permute-start(bf16[64,2048]{1,0:T(8,128)(2,1)S(1)} %get-tuple-element.45), channel_id=1, source_target_pairs={{0,1},{1,0},{2,3},{3,2},{4,5},{5,4},{6,7},{7,6},{8,9},{9,8},{10,11... | collective-permute-start | bytes 786440 | tf_op jit(solution)/shard_map/ppermute | solution.py:143
  52.9 5.3 %collective-permute-start.19 = (bf16[256,576]{1,0:T(8,128)(2,1)S(1)}, bf16[256,576]{1,0:T(8,128)(2,1)S(1)}, u32[]{:S(2)}, u32[]{:S(2)}) collective-permute-start(bf16[256,576]{1,0:T(8,128)(2,1)S(1)} %pad_maximum_fusion.4), channel_id=1, source_target_pairs={{0,16},{16,0},{1,17},{17,1},{2,18},{18,2},{3,19},{19,3},{4,20},{20... | collective-permute-start | bytes 884744 | tf_op jit(solution)/shard_map/ppermute | solution.py:133
  58.4 6.9 %collective-permute-start.24 = (bf16[16,2048]{1,0:T(8,128)(2,1)S(1)}, bf16[16,2048]{1,0:T(8,128)(2,1)S(1)}, u32[]{:S(2)}, u32[]{:S(2)}) collective-permute-start(bf16[16,2048]{1,0:T(8,128)(2,1)S(1)} %get-tuple-element.50), channel_id=1, source_target_pairs={{0,4},{1,5},{2,6},{3,7},{4,8},{5,9},{6,10},{7,11},{8,12},{9,13},{1... | collective-permute-start | bytes 196616 | tf_op jit(solution)/shard_map/ppermute | solution.py:137
  59.0 8.2 %collective-permute-start.23 = (bf16[16,2048]{1,0:T(8,128)(2,1)S(1)}, bf16[16,2048]{1,0:T(8,128)(2,1)S(1)}, u32[]{:S(2)}, u32[]{:S(2)}) collective-permute-start(bf16[16,2048]{1,0:T(8,128)(2,1)S(1)} %get-tuple-element.51), channel_id=1, source_target_pairs={{0,8},{1,9},{2,10},{3,11},{4,12},{5,13},{6,14},{7,15},{8,0},{9,1},... | collective-permute-start | bytes 196616 | tf_op jit(solution)/shard_map/ppermute | solution.py:137
  62.3 5.3 %collective-permute-start.22 = (bf16[16,2048]{1,0:T(8,128)(2,1)S(1)}, bf16[16,2048]{1,0:T(8,128)(2,1)S(1)}, u32[]{:S(2)}, u32[]{:S(2)}) collective-permute-start(bf16[16,2048]{1,0:T(8,128)(2,1)S(1)} %get-tuple-element.49), channel_id=1, source_target_pairs={{0,12},{1,13},{2,14},{3,15},{4,0},{5,1},{6,2},{7,3},{8,4},{9,5},{1... | collective-permute-start | bytes 196616 | tf_op jit(solution)/shard_map/ppermute | solution.py:137
  (7 other events, 13.2 us)

commit v17 on v16

--- a/solution.py
+++ b/solution.py
@@ -230,6 +230,15 @@
             out[0, :, columns] = total.astype(jnp.bfloat16)
 
 
+def join_kernel(own_ref, other_ref, gate_up_ref, down_ref):
+    half = own_ref.shape[0] // 3
+    for index, ref in enumerate((own_ref, other_ref)):
+        for kind in range(2):
+            low = (2 * kind + index) * half
+            gate_up_ref[low : low + half, :] = ref[kind * half : (kind + 1) * half, :]
+        down_ref[index * half : (index + 1) * half, :] = ref[2 * half :, :]
+
+
 def along_outer(value, count, inner):
     return [value] + [shift_outer(value, count, inner, step) for step in range(1, count // inner)]
 
@@ -317,11 +326,12 @@
         upstream[:, model_width:].astype(jnp.float32) * here[:1], axis=1, keepdims=True
     )
     upstream = upstream[:, :model_width]
-    gate_up = jnp.concatenate(
-        [own_weights[:half], other[:half], own_weights[half : 2 * half], other[half : 2 * half]],
-        axis=0,
-    )
-    down = jnp.concatenate([own_weights[2 * half :], other[2 * half :]], axis=0)
+    gate_up, down = on_chip(
+        join_kernel,
+        [((4 * half, model_width), low), ((2 * half, model_width), low)],
+        own_weights,
+        other,
+    )
     pre = jnp.dot(inputs, gate_up.T, preferred_element_type=jnp.float32)
     gate_pre, up_pre = pre[:, : 2 * half], pre[:, 2 * half :]
     hidden_grad = gate * jnp.dot(upstream, down.T, preferred_element_type=jnp.float32)

time: 68.5 us -> 67.1 us (0.980)
  local copies, waits for them, and re-layouts: 2.19 us -> 0.73 us
    unnamed x22 -> x16, local copies, waits for them, and re-layouts: 1.49 us -> 0.2 us
    pallas_call x3 -> x4, Pallas kernels: 4.22 us -> 4.51 us  [on_chip(): pl.pallas_call(body, out_shape=[jax.ShapeDtypeStruct(shape, dtype) for sh...]
  transfers between devices with their start and end apart: 25 -> 25, of which waited for: 11 -> 11; matrix products, arithmetic and copies ran while one was open for 9% -> 9% of each run, Pallas kernels for 6% -> 7%
where the time goes in v17:
time: 67.1 us; the launch traced here: 66.9 us
  starting transfers between devices  29.2 us (44%)
  waiting for transfers between devices  25.5 us (38%)
  Pallas kernels  4.51 us (7%)
  other arithmetic  3.13 us (5%)
  matrix products  2.8 us (4%)
  between operations  0.98 us (1%)
  local copies, waits for them, and re-layouts  0.73 us (1%)
    ppermute x11, waiting for transfers between devices, swap_inner(): lax.ppermute(value, 'expert', [(place, place ^ partner) for place in rang...  20.3 us
    ppermute x9, starting transfers between devices, shift_outer(): lax.ppermute(value, 'expert', [(place, (place + step * inner) % count) fo...  15.9 us
    ppermute x11, starting transfers between devices, swap_inner(): lax.ppermute(value, 'expert', [(place, place ^ partner) for place in rang...  13.1 us
    ppermute x9, waiting for transfers between devices, shift_outer(): lax.ppermute(value, 'expert', [(place, (place + step * inner) % count) fo...  5.28 us
    pallas_call x4, Pallas kernels, on_chip(): pl.pallas_call(body, out_shape=[jax.ShapeDtypeStruct(shape, dtype) for sh...  4.51 us
    concatenate x1, other arithmetic, dense_local(): own_weights = jnp.concatenate([w_gate[0], w_up[0], w_down[0]], axis=0)  1.93 us
  transfers between devices with their start and end apart: 25, of which 11 were waited for; matrix products, arithmetic and copies ran while one was open for 9% of the time, Pallas kernels for 7%

profile of v17, /device:TPU:0, one launch (start us, length us, event | category | flops | bytes accessed | tf_op | source)
XLA Modules:
  0.0 66.9 jit_solution(3903830043297377308)
XLA Ops:
  0.6 5.1 %collective-permute-start.3 = (bf16[16,2048]{1,0:T(8,128)(2,1)}, bf16[16,2048]{1,0:T(8,128)(2,1)S(1)}, u32[]{:S(2)}, u32[]{:S(2)}) collective-permute-start(bf16[16,2048]{1,0:T(8,128)(2,1)} %tokens_hbm.1), channel_id=1, source_target_pairs={{0,12},{1,13},{2,14},{3,15},{4,0},{5,1},{6,2},{7,3},{8,4},{9,5},{1... | collective-permute-start | bytes 196616 | tf_op jit(solution)/shard_map/ppermute | solution.py:137
  5.7 1.0 %collective-permute-start.1 = (bf16[16,2048]{1,0:T(8,128)(2,1)}, bf16[16,2048]{1,0:T(8,128)(2,1)S(1)}, u32[]{:S(2)}, u32[]{:S(2)}) collective-permute-start(bf16[16,2048]{1,0:T(8,128)(2,1)} %tokens_hbm.1), channel_id=1, source_target_pairs={{0,4},{1,5},{2,6},{3,7},{4,8},{5,9},{6,10},{7,11},{8,12},{9,13},{1... | collective-permute-start | bytes 196616 | tf_op jit(solution)/shard_map/ppermute | solution.py:137
  6.7 1.6 %shard_map.111 = (bf16[32,16]{1,0:T(8,128)(2,1)}, bf16[16,2048]{1,0:T(8,128)(2,1)}, bf16[16,2048]{1,0:T(8,128)(2,1)}) custom-call(s32[8,16]{1,0:T(8,128)} %bitcast.15, bf16[8,16]{1,0:T(8,128)(2,1)} %bitcast.16, s32[1,16]{1,0:T(1,128)} %bitcast.17, bf16[16,2048]{1,0:T(8,128)(2,1)} %tokens_hbm.1, bf16[16,2048]{1,0:T(8,128)(2,1)} %cotangent_hbm.1), custom_call_target="tpu_custom_call" | custom-call | bytes 264000 | tf_op jit(solution)/shard_map/pallas_call | solution.py:156
  8.5 1.9 %pad_maximum_fusion.own_ref = bf16[576,2048]{1,0:T(8,128)(2,1)S(1)} fusion(bf16[192,2048]{1,0:T(8,128)(2,1)} %bitcast.12, bf16[192,2048]{1,0:T(8,128)(2,1)} %bitcast.13, bf16[192,2048]{1,0:T(8,128)(2,1)} %bitcast.14), kind=kLoop, calls=%fused_computation.1 | loop fusion | flops 7077888 | bytes 4718592 | tf_op jit(solution)/shard_map/concatenate | solution.py:319
  10.6 1.9 %collective-permute-start.5 = (bf16[16,2064]{1,0:T(8,128)(2,1)S(1)}, bf16[16,2064]{1,0:T(8,128)(2,1)S(1)}, u32[]{:S(2)}, u32[]{:S(2)}) collective-permute-start(bf16[16,2064]{1,0:T(8,128)(2,1)S(1)} %get-tuple-element.28), channel_id=1, source_target_pairs={{0,8},{1,9},{2,10},{3,11},{4,12},{5,13},{6,14},{7,15},{8,0},{9,1},... | collective-permute-start | bytes 198152 | tf_op jit(solution)/shard_map/ppermute | solution.py:137
  12.6 1.6 %collective-permute-start.11 = (bf16[64,2048]{1,0:T(8,128)(2,1)S(1)}, bf16[64,2048]{1,0:T(8,128)(2,1)S(1)}, u32[]{:S(2)}, u32[]{:S(2)}) collective-permute-start(bf16[64,2048]{1,0:T(8,128)(2,1)S(1)} %pad_maximum_fusion.3), channel_id=1, source_target_pairs={{0,1},{1,0},{2,3},{3,2},{4,5},{5,4},{6,7},{7,6},{8,9},{9,8},{10,11... | collective-permute-start | bytes 786440 | tf_op jit(solution)/shard_map/ppermute | solution.py:143
  14.1 1.6 %collective-permute-start.13 = (bf16[64,2048]{1,0:T(8,128)(2,1)S(1)}, bf16[64,2048]{1,0:T(8,128)(2,1)S(1)}, u32[]{:S(2)}, u32[]{:S(2)}) collective-permute-start(bf16[64,2048]{1,0:T(8,128)(2,1)S(1)} %pad_maximum_fusion.3), channel_id=1, source_target_pairs={{0,2},{1,3},{2,0},{3,1},{4,6},{5,7},{6,4},{7,5},{8,10},{9,11},{10,... | collective-permute-start | bytes 786440 | tf_op jit(solution)/shard_map/ppermute | solution.py:143
  15.7 1.5 %collective-permute-start.4 = (bf16[16,2064]{1,0:T(8,128)(2,1)S(1)}, bf16[16,2064]{1,0:T(8,128)(2,1)S(1)}, u32[]{:S(2)}, u32[]{:S(2)}) collective-permute-start(bf16[16,2064]{1,0:T(8,128)(2,1)S(1)} %get-tuple-element.28), channel_id=1, source_target_pairs={{0,4},{1,5},{2,6},{3,7},{4,8},{5,9},{6,10},{7,11},{8,12},{9,13},{1... | collective-permute-start | bytes 198152 | tf_op jit(solution)/shard_map/ppermute | solution.py:137
  17.2 2.4 %collective-permute-start.6 = (bf16[16,2064]{1,0:T(8,128)(2,1)S(1)}, bf16[16,2064]{1,0:T(8,128)(2,1)S(1)}, u32[]{:S(2)}, u32[]{:S(2)}) collective-permute-start(bf16[16,2064]{1,0:T(8,128)(2,1)S(1)} %get-tuple-element.28), channel_id=1, source_target_pairs={{0,12},{1,13},{2,14},{3,15},{4,0},{5,1},{6,2},{7,3},{8,4},{9,5},{1... | collective-permute-start | bytes 198152 | tf_op jit(solution)/shard_map/ppermute | solution.py:137
  19.6 2.6 %collective-permute-done.4 = bf16[16,2064]{1,0:T(8,128)(2,1)S(1)} collective-permute-done((bf16[16,2064]{1,0:T(8,128)(2,1)S(1)}, bf16[16,2064]{1,0:T(8,128)(2,1)S(1)}, u32[]{:S(2)}, u32[]{:S(2)}) %collective-permute-start.4) | collective-permute-done | bytes 66080 | tf_op jit(solution)/shard_map/ppermute | solution.py:137
  23.5 1.6 %collective-permute-start.14 = (bf16[32,2048]{1,0:T(8,128)(2,1)S(1)}, bf16[32,2048]{1,0:T(8,128)(2,1)S(1)}, u32[]{:S(2)}, u32[]{:S(2)}) collective-permute-start(bf16[32,2048]{1,0:T(8,128)(2,1)S(1)} %slice.104), channel_id=1, source_target_pairs={{0,2},{1,3},{2,0},{3,1},{4,6},{5,7},{6,4},{7,5},{8,10},{9,11},{10,... | collective-permute-start | bytes 393224 | tf_op jit(solution)/shard_map/ppermute | solution.py:143
  25.1 1.6 %collective-permute-start.15 = (bf16[32,2048]{1,0:T(8,128)(2,1)S(1)}, bf16[32,2048]{1,0:T(8,128)(2,1)S(1)}, u32[]{:S(2)}, u32[]{:S(2)}) collective-permute-start(bf16[32,2048]{1,0:T(8,128)(2,1)S(1)} %slice.105), channel_id=1, source_target_pairs={{0,1},{1,0},{2,3},{3,2},{4,5},{5,4},{6,7},{7,6},{8,9},{9,8},{10,11... | collective-permute-start | bytes 393224 | tf_op jit(solution)/shard_map/ppermute | solution.py:143
  26.7 4.2 %collective-permute-done.7 = bf16[64,2064]{1,0:T(8,128)(2,1)S(1)} collective-permute-done((bf16[64,2064]{1,0:T(8,128)(2,1)S(1)}, bf16[64,2064]{1,0:T(8,128)(2,1)S(1)}, u32[]{:S(2)}, u32[]{:S(2)}) %collective-permute-start.7) | collective-permute-done | bytes 264224 | tf_op jit(solution)/shard_map/ppermute | solution.py:143
  31.4 1.0 %collective-permute-done.8 = bf16[64,2064]{1,0:T(8,128)(2,1)S(1)} collective-permute-done((bf16[64,2064]{1,0:T(8,128)(2,1)S(1)}, bf16[64,2064]{1,0:T(8,128)(2,1)S(1)}, u32[]{:S(2)}, u32[]{:S(2)}) %collective-permute-start.8) | collective-permute-done | bytes 264224 | tf_op jit(solution)/shard_map/ppermute | solution.py:143
  32.5 1.6 %collective-permute-start.10 = (bf16[32,2064]{1,0:T(8,128)(2,1)S(1)}, bf16[32,2064]{1,0:T(8,128)(2,1)S(1)}, u32[]{:S(2)}, u32[]{:S(2)}) collective-permute-start(bf16[32,2064]{1,0:T(8,128)(2,1)S(1)} %slice.101), channel_id=1, source_target_pairs={{0,1},{1,0},{2,3},{3,2},{4,5},{5,4},{6,7},{7,6},{8,9},{9,8},{10,11... | collective-permute-start | bytes 396296 | tf_op jit(solution)/shard_map/ppermute | solution.py:143
  34.3 1.7 %collective-permute-done.9 = bf16[32,2064]{1,0:T(8,128)(2,1)S(1)} collective-permute-done((bf16[32,2064]{1,0:T(8,128)(2,1)S(1)}, bf16[32,2064]{1,0:T(8,128)(2,1)S(1)}, u32[]{:S(2)}, u32[]{:S(2)}) %collective-permute-start.9) | collective-permute-done | bytes 132128 | tf_op jit(solution)/shard_map/ppermute | solution.py:143
  36.0 1.6 %collective-permute-done.10 = bf16[32,2064]{1,0:T(8,128)(2,1)S(1)} collective-permute-done((bf16[32,2064]{1,0:T(8,128)(2,1)S(1)}, bf16[32,2064]{1,0:T(8,128)(2,1)S(1)}, u32[]{:S(2)}, u32[]{:S(2)}) %collective-permute-start.10) | collective-permute-done | bytes 132128 | tf_op jit(solution)/shard_map/ppermute | solution.py:143
  38.2 1.0 %fusion.11 = f32[256,768]{1,0:T(8,128)S(1)} fusion(bf16[256,2048]{1,0:T(8,128)(2,1)S(1)} %constant_dynamic-update-slice_fusion.12.rows, bf16[768,2048]{1,0:T(8,128)(2,1)S(1)} %get-tuple-element.34), kind=kOutput, calls=%fused_computation.42 | convolution fusion | flops 805306368 | bytes 4980736 | tf_op jit(solution)/shard_map/dot_general | solution.py:335
  42.3 2.3 %collective-permute-start.17 = (bf16[64,2048]{1,0:T(8,128)(2,1)S(1)}, bf16[64,2048]{1,0:T(8,128)(2,1)S(1)}, u32[]{:S(2)}, u32[]{:S(2)}) collective-permute-start(bf16[64,2048]{1,0:T(8,128)(2,1)S(1)} %get-tuple-element.48), channel_id=1, source_target_pairs={{0,2},{1,3},{2,0},{3,1},{4,6},{5,7},{6,4},{7,5},{8,10},{9,11},{10,... | collective-permute-start | bytes 786440 | tf_op jit(solution)/shard_map/ppermute | solution.py:143
  45.1 6.6 %collective-permute-done.18 = bf16[64,2048]{1,0:T(8,128)(2,1)S(1)} collective-permute-done((bf16[64,2048]{1,0:T(8,128)(2,1)S(1)}, bf16[64,2048]{1,0:T(8,128)(2,1)S(1)}, u32[]{:S(2)}, u32[]{:S(2)}) %collective-permute-start.18) | collective-permute-done | bytes 262176 | tf_op jit(solution)/shard_map/ppermute | solution.py:143
  51.7 5.2 %collective-permute-done.17 = bf16[64,2048]{1,0:T(8,128)(2,1)S(1)} collective-permute-done((bf16[64,2048]{1,0:T(8,128)(2,1)S(1)}, bf16[64,2048]{1,0:T(8,128)(2,1)S(1)}, u32[]{:S(2)}, u32[]{:S(2)}) %collective-permute-start.17) | collective-permute-done | bytes 262176 | tf_op jit(solution)/shard_map/ppermute | solution.py:143
  57.4 3.5 %collective-permute-start.23 = (bf16[16,2048]{1,0:T(8,128)(2,1)S(1)}, bf16[16,2048]{1,0:T(8,128)(2,1)S(1)}, u32[]{:S(2)}, u32[]{:S(2)}) collective-permute-start(bf16[16,2048]{1,0:T(8,128)(2,1)S(1)} %get-tuple-element.52), channel_id=1, source_target_pairs={{0,8},{1,9},{2,10},{3,11},{4,12},{5,13},{6,14},{7,15},{8,0},{9,1},... | collective-permute-start | bytes 196616 | tf_op jit(solution)/shard_map/ppermute | solution.py:137
  61.1 2.5 %shard_map.114 = (bf16[1,192,2048]{2,1,0:T(8,128)(2,1)}, bf16[1,192,2048]{2,1,0:T(8,128)(2,1)}, bf16[1,192,2048]{2,1,0:T(8,128)(2,1)}) custom-call(bf16[256,576]{1,0:T(8,128)(2,1)S(1)} %pad_maximum_fusion.2.own_grads, bf16[256,576]{1,0:T(8,128)(2,1)S(1)} %collective-permute-done.19.other_grads, ...), custom_call_target="tpu_custom_call" | custom-call | bytes 7143424 | tf_op jit(solution)/shard_map/pallas_call | solution.py:156
  64.0 1.9 %collective-permute-done.23 = bf16[16,2048]{1,0:T(8,128)(2,1)S(1)} collective-permute-done((bf16[16,2048]{1,0:T(8,128)(2,1)S(1)}, bf16[16,2048]{1,0:T(8,128)(2,1)S(1)}, u32[]{:S(2)}, u32[]{:S(2)}) %collective-permute-start.23) | collective-permute-done | bytes 65568 | tf_op jit(solution)/shard_map/ppermute | solution.py:137
  (70 shorter events, 8.6 us)
Async XLA Ops:
  0.6 11.9 %collective-permute-start.3 = (bf16[16,2048]{1,0:T(8,128)(2,1)}, bf16[16,2048]{1,0:T(8,128)(2,1)S(1)}, u32[]{:S(2)}, u32[]{:S(2)}) collective-permute-start(bf16[16,2048]{1,0:T(8,128)(2,1)} %tokens_hbm.1), channel_id=1, source_target_pairs={{0,12},{1,13},{2,14},{3,15},{4,0},{5,1},{6,2},{7,3},{8,4},{9,5},{1... | collective-permute-start | bytes 196616 | tf_op jit(solution)/shard_map/ppermute | solution.py:137
  5.7 6.8 %collective-permute-start.2 = (bf16[16,2048]{1,0:T(8,128)(2,1)}, bf16[16,2048]{1,0:T(8,128)(2,1)S(1)}, u32[]{:S(2)}, u32[]{:S(2)}) collective-permute-start(bf16[16,2048]{1,0:T(8,128)(2,1)} %tokens_hbm.1), channel_id=1, source_target_pairs={{0,8},{1,9},{2,10},{3,11},{4,12},{5,13},{6,14},{7,15},{8,0},{9,1},... | collective-permute-start | bytes 196616 | tf_op jit(solution)/shard_map/ppermute | solution.py:137
  5.7 6.8 %collective-permute-start.1 = (bf16[16,2048]{1,0:T(8,128)(2,1)}, bf16[16,2048]{1,0:T(8,128)(2,1)S(1)}, u32[]{:S(2)}, u32[]{:S(2)}) collective-permute-start(bf16[16,2048]{1,0:T(8,128)(2,1)} %tokens_hbm.1), channel_id=1, source_target_pairs={{0,4},{1,5},{2,6},{3,7},{4,8},{5,9},{6,10},{7,11},{8,12},{9,13},{1... | collective-permute-start | bytes 196616 | tf_op jit(solution)/shard_map/ppermute | solution.py:137
  10.6 11.6 %collective-permute-start.5 = (bf16[16,2064]{1,0:T(8,128)(2,1)S(1)}, bf16[16,2064]{1,0:T(8,128)(2,1)S(1)}, u32[]{:S(2)}, u32[]{:S(2)}) collective-permute-start(bf16[16,2064]{1,0:T(8,128)(2,1)S(1)} %get-tuple-element.28), channel_id=1, source_target_pairs={{0,8},{1,9},{2,10},{3,11},{4,12},{5,13},{6,14},{7,15},{8,0},{9,1},... | collective-permute-start | bytes 198152 | tf_op jit(solution)/shard_map/ppermute | solution.py:137
  12.6 10.9 %collective-permute-start.11 = (bf16[64,2048]{1,0:T(8,128)(2,1)S(1)}, bf16[64,2048]{1,0:T(8,128)(2,1)S(1)}, u32[]{:S(2)}, u32[]{:S(2)}) collective-permute-start(bf16[64,2048]{1,0:T(8,128)(2,1)S(1)} %pad_maximum_fusion.3), channel_id=1, source_target_pairs={{0,1},{1,0},{2,3},{3,2},{4,5},{5,4},{6,7},{7,6},{8,9},{9,8},{10,11... | collective-permute-start | bytes 786440 | tf_op jit(solution)/shard_map/ppermute | solution.py:143
  14.1 10.9 %collective-permute-start.13 = (bf16[64,2048]{1,0:T(8,128)(2,1)S(1)}, bf16[64,2048]{1,0:T(8,128)(2,1)S(1)}, u32[]{:S(2)}, u32[]{:S(2)}) collective-permute-start(bf16[64,2048]{1,0:T(8,128)(2,1)S(1)} %pad_maximum_fusion.3), channel_id=1, source_target_pairs={{0,2},{1,3},{2,0},{3,1},{4,6},{5,7},{6,4},{7,5},{8,10},{9,11},{10,... | collective-permute-start | bytes 786440 | tf_op jit(solution)/shard_map/ppermute | solution.py:143
  15.7 6.5 %collective-permute-start.4 = (bf16[16,2064]{1,0:T(8,128)(2,1)S(1)}, bf16[16,2064]{1,0:T(8,128)(2,1)S(1)}, u32[]{:S(2)}, u32[]{:S(2)}) collective-permute-start(bf16[16,2064]{1,0:T(8,128)(2,1)S(1)} %get-tuple-element.28), channel_id=1, source_target_pairs={{0,4},{1,5},{2,6},{3,7},{4,8},{5,9},{6,10},{7,11},{8,12},{9,13},{1... | collective-permute-start | bytes 198152 | tf_op jit(solution)/shard_map/ppermute | solution.py:137
  17.2 5.1 %collective-permute-start.6 = (bf16[16,2064]{1,0:T(8,128)(2,1)S(1)}, bf16[16,2064]{1,0:T(8,128)(2,1)S(1)}, u32[]{:S(2)}, u32[]{:S(2)}) collective-permute-start(bf16[16,2064]{1,0:T(8,128)(2,1)S(1)} %get-tuple-element.28), channel_id=1, source_target_pairs={{0,12},{1,13},{2,14},{3,15},{4,0},{5,1},{6,2},{7,3},{8,4},{9,5},{1... | collective-permute-start | bytes 198152 | tf_op jit(solution)/shard_map/ppermute | solution.py:137
  22.3 8.5 %collective-permute-start.7 = (bf16[64,2064]{1,0:T(8,128)(2,1)S(1)}, bf16[64,2064]{1,0:T(8,128)(2,1)S(1)}, u32[]{:S(2)}, u32[]{:S(2)}) collective-permute-start(bf16[64,2064]{1,0:T(8,128)(2,1)S(1)} %get-tuple-element.59), channel_id=1, source_target_pairs={{0,1},{1,0},{2,3},{3,2},{4,5},{5,4},{6,7},{7,6},{8,9},{9,8},{10,11... | collective-permute-start | bytes 792584 | tf_op jit(solution)/shard_map/ppermute | solution.py:143
  22.9 9.5 %collective-permute-start.8 = (bf16[64,2064]{1,0:T(8,128)(2,1)S(1)}, bf16[64,2064]{1,0:T(8,128)(2,1)S(1)}, u32[]{:S(2)}, u32[]{:S(2)}) collective-permute-start(bf16[64,2064]{1,0:T(8,128)(2,1)S(1)} %get-tuple-element.59), channel_id=1, source_target_pairs={{0,2},{1,3},{2,0},{3,1},{4,6},{5,7},{6,4},{7,5},{8,10},{9,11},{10,... | collective-permute-start | bytes 792584 | tf_op jit(solution)/shard_map/ppermute | solution.py:143
  23.4 14.4 %collective-permute-start.12 = (bf16[576,2048]{1,0:T(8,128)(2,1)S(1)}, bf16[576,2048]{1,0:T(8,128)(2,1)S(1)}, u32[]{:S(2)}, u32[]{:S(2)}) collective-permute-start(bf16[576,2048]{1,0:T(8,128)(2,1)S(1)} %pad_maximum_fusion.own_ref), channel_id=1, source_target_pairs={{0,16},{16,0},{1,17},{17,1},{2,18},{18,2},{3,19},{19,3},{4,20},{20... | collective-permute-start | bytes 7077896 | tf_op jit(solution)/shard_map/ppermute | solution.py:133
  23.5 10.7 %collective-permute-start.14 = (bf16[32,2048]{1,0:T(8,128)(2,1)S(1)}, bf16[32,2048]{1,0:T(8,128)(2,1)S(1)}, u32[]{:S(2)}, u32[]{:S(2)}) collective-permute-start(bf16[32,2048]{1,0:T(8,128)(2,1)S(1)} %slice.104), channel_id=1, source_target_pairs={{0,2},{1,3},{2,0},{3,1},{4,6},{5,7},{6,4},{7,5},{8,10},{9,11},{10,... | collective-permute-start | bytes 393224 | tf_op jit(solution)/shard_map/ppermute | solution.py:143
  25.1 9.1 %collective-permute-start.15 = (bf16[32,2048]{1,0:T(8,128)(2,1)S(1)}, bf16[32,2048]{1,0:T(8,128)(2,1)S(1)}, u32[]{:S(2)}, u32[]{:S(2)}) collective-permute-start(bf16[32,2048]{1,0:T(8,128)(2,1)S(1)} %slice.105), channel_id=1, source_target_pairs={{0,1},{1,0},{2,3},{3,2},{4,5},{5,4},{6,7},{7,6},{8,9},{9,8},{10,11... | collective-permute-start | bytes 393224 | tf_op jit(solution)/shard_map/ppermute | solution.py:143
  30.9 5.1 %collective-permute-start.9 = (bf16[32,2064]{1,0:T(8,128)(2,1)S(1)}, bf16[32,2064]{1,0:T(8,128)(2,1)S(1)}, u32[]{:S(2)}, u32[]{:S(2)}) collective-permute-start(bf16[32,2064]{1,0:T(8,128)(2,1)S(1)} %slice.100), channel_id=1, source_target_pairs={{0,2},{1,3},{2,0},{3,1},{4,6},{5,7},{6,4},{7,5},{8,10},{9,11},{10,... | collective-permute-start | bytes 396296 | tf_op jit(solution)/shard_map/ppermute | solution.py:143
  32.5 5.1 %collective-permute-start.10 = (bf16[32,2064]{1,0:T(8,128)(2,1)S(1)}, bf16[32,2064]{1,0:T(8,128)(2,1)S(1)}, u32[]{:S(2)}, u32[]{:S(2)}) collective-permute-start(bf16[32,2064]{1,0:T(8,128)(2,1)S(1)} %slice.101), channel_id=1, source_target_pairs={{0,1},{1,0},{2,3},{3,2},{4,5},{5,4},{6,7},{7,6},{8,9},{9,8},{10,11... | collective-permute-start | bytes 396296 | tf_op jit(solution)/shard_map/ppermute | solution.py:143
  34.2 22.8 %collective-permute-start.20 = (bf16[256,2048]{1,0:T(8,128)(2,1)S(1)}, bf16[256,2048]{1,0:T(8,128)(2,1)S(1)}, u32[]{:S(2)}, u32[]{:S(2)}) collective-permute-start(bf16[256,2048]{1,0:T(8,128)(2,1)S(1)} %constant_dynamic-update-slice_fusion.12.rows), channel_id=1, source_target_pairs={{0,16},{16,0},{1,17},{17,1},{2,18},{18,2},{3,19},{19,3},{4,20},{20... | collective-permute-start | bytes 3145736 | tf_op jit(solution)/shard_map/ppermute | solution.py:133
  41.4 15.6 %collective-permute-start.21 = (bf16[256,2048]{1,0:T(8,128)(2,1)S(1)}, bf16[256,2048]{1,0:T(8,128)(2,1)S(1)}, u32[]{:S(2)}, u32[]{:S(2)}) collective-permute-start(bf16[256,2048]{1,0:T(8,128)(2,1)S(1)} %slice.103.upstream), channel_id=1, source_target_pairs={{0,16},{16,0},{1,17},{17,1},{2,18},{18,2},{3,19},{19,3},{4,20},{20... | collective-permute-start | bytes 3145736 | tf_op jit(solution)/shard_map/ppermute | solution.py:133
  41.6 10.1 %collective-permute-start.18 = (bf16[64,2048]{1,0:T(8,128)(2,1)S(1)}, bf16[64,2048]{1,0:T(8,128)(2,1)S(1)}, u32[]{:S(2)}, u32[]{:S(2)}) collective-permute-start(bf16[64,2048]{1,0:T(8,128)(2,1)S(1)} %get-tuple-element.47), channel_id=1, source_target_pairs={{0,3},{1,2},{2,1},{3,0},{4,7},{5,6},{6,5},{7,4},{8,11},{9,10},{10,... | collective-permute-start | bytes 786440 | tf_op jit(solution)/shard_map/ppermute | solution.py:143
  42.3 14.5 %collective-permute-start.17 = (bf16[64,2048]{1,0:T(8,128)(2,1)S(1)}, bf16[64,2048]{1,0:T(8,128)(2,1)S(1)}, u32[]{:S(2)}, u32[]{:S(2)}) collective-permute-start(bf16[64,2048]{1,0:T(8,128)(2,1)S(1)} %get-tuple-element.48), channel_id=1, source_target_pairs={{0,2},{1,3},{2,0},{3,1},{4,6},{5,7},{6,4},{7,5},{8,10},{9,11},{10,... | collective-permute-start | bytes 786440 | tf_op jit(solution)/shard_map/ppermute | solution.py:143
  44.6 12.2 %collective-permute-start.16 = (bf16[64,2048]{1,0:T(8,128)(2,1)S(1)}, bf16[64,2048]{1,0:T(8,128)(2,1)S(1)}, u32[]{:S(2)}, u32[]{:S(2)}) collective-permute-start(bf16[64,2048]{1,0:T(8,128)(2,1)S(1)} %get-tuple-element.46), channel_id=1, source_target_pairs={{0,1},{1,0},{2,3},{3,2},{4,5},{5,4},{6,7},{7,6},{8,9},{9,8},{10,11... | collective-permute-start | bytes 786440 | tf_op jit(solution)/shard_map/ppermute | solution.py:143
  51.7 5.3 %collective-permute-start.19 = (bf16[256,576]{1,0:T(8,128)(2,1)S(1)}, bf16[256,576]{1,0:T(8,128)(2,1)S(1)}, u32[]{:S(2)}, u32[]{:S(2)}) collective-permute-start(bf16[256,576]{1,0:T(8,128)(2,1)S(1)} %pad_maximum_fusion.1), channel_id=1, source_target_pairs={{0,16},{16,0},{1,17},{17,1},{2,18},{18,2},{3,19},{19,3},{4,20},{20... | collective-permute-start | bytes 884744 | tf_op jit(solution)/shard_map/ppermute | solution.py:133
  57.1 6.9 %collective-permute-start.24 = (bf16[16,2048]{1,0:T(8,128)(2,1)S(1)}, bf16[16,2048]{1,0:T(8,128)(2,1)S(1)}, u32[]{:S(2)}, u32[]{:S(2)}) collective-permute-start(bf16[16,2048]{1,0:T(8,128)(2,1)S(1)} %get-tuple-element.51), channel_id=1, source_target_pairs={{0,4},{1,5},{2,6},{3,7},{4,8},{5,9},{6,10},{7,11},{8,12},{9,13},{1... | collective-permute-start | bytes 196616 | tf_op jit(solution)/shard_map/ppermute | solution.py:137
  57.4 8.4 %collective-permute-start.23 = (bf16[16,2048]{1,0:T(8,128)(2,1)S(1)}, bf16[16,2048]{1,0:T(8,128)(2,1)S(1)}, u32[]{:S(2)}, u32[]{:S(2)}) collective-permute-start(bf16[16,2048]{1,0:T(8,128)(2,1)S(1)} %get-tuple-element.52), channel_id=1, source_target_pairs={{0,8},{1,9},{2,10},{3,11},{4,12},{5,13},{6,14},{7,15},{8,0},{9,1},... | collective-permute-start | bytes 196616 | tf_op jit(solution)/shard_map/ppermute | solution.py:137
  61.0 5.3 %collective-permute-start.22 = (bf16[16,2048]{1,0:T(8,128)(2,1)S(1)}, bf16[16,2048]{1,0:T(8,128)(2,1)S(1)}, u32[]{:S(2)}, u32[]{:S(2)}) collective-permute-start(bf16[16,2048]{1,0:T(8,128)(2,1)S(1)} %get-tuple-element.50), channel_id=1, source_target_pairs={{0,12},{1,13},{2,14},{3,15},{4,0},{5,1},{6,2},{7,3},{8,4},{9,5},{1... | collective-permute-start | bytes 196616 | tf_op jit(solution)/shard_map/ppermute | solution.py:137
  (4 other events, 10.1 us)

commit v18 on v17

--- a/solution.py
+++ b/solution.py
@@ -239,6 +239,15 @@
         down_ref[index * half : (index + 1) * half, :] = ref[2 * half :, :]
 
 
+def pair_kernel(left_ref, right_ref, other_left_ref, other_right_ref, sum_ref, other_sum_ref):
+    for one, two, out in (
+        (left_ref, right_ref, sum_ref),
+        (other_left_ref, other_right_ref, other_sum_ref),
+    ):
+        total = one[...].astype(jnp.float32) + two[...].astype(jnp.float32)
+        out[...] = total.astype(out.dtype)
+
+
 def along_outer(value, count, inner):
     return [value] + [shift_outer(value, count, inner, step) for step in range(1, count // inner)]
 
@@ -254,11 +263,21 @@
     return [column, first, second, far_top, far_bottom]
 
 
-def return_inner(value, count, inner):
-    blocks = value.reshape(inner, -1, value.shape[-1])
-    total = blocks[0].astype(jnp.float32)
-    for partner in range(1, inner):
-        total = total + swap_inner(blocks[partner], count, partner).astype(jnp.float32)
+def return_inner(value, count):
+    own, first, second, far = jnp.split(value, 4, axis=0)
+    cut = own.shape[0] // 2
+    top = swap_inner(far[:cut], count, 2)
+    bottom = swap_inner(far[cut:], count, 1)
+    first_bottom = swap_inner(first[cut:], count, 1)
+    second_top = swap_inner(second[:cut], count, 2)
+    sent_first, sent_second = on_chip(
+        pair_kernel, [(top.shape, top.dtype)] * 2, first[:cut], top, second[cut:], bottom
+    )
+    first_top = swap_inner(sent_first, count, 1)
+    second_bottom = swap_inner(sent_second, count, 2)
+    total = own.astype(jnp.float32)
+    for upper, lower in ((first_top, first_bottom), (second_top, second_bottom)):
+        total = total + jnp.concatenate([upper, lower], axis=0).astype(jnp.float32)
     return total
 
 
@@ -344,15 +363,16 @@
     both_grad = jnp.concatenate([gate_grad, up_grad], axis=1)
     partial_grad = jnp.dot(both_grad, gate_up, preferred_element_type=jnp.float32)
     partial_grad = partial_grad.astype(jnp.bfloat16)
-    column_sum = return_inner(partial_grad, count, inner)
+    partial_grad, other_inputs = lax.optimization_barrier((partial_grad, other_inputs))
+    column_sum = return_inner(partial_grad, count)
     grads = (gate_grad, up_grad, hidden)
     own_grads = jnp.concatenate([grad[:, :half] for grad in grads], axis=1)
     sent_grads = jnp.concatenate([grad[:, half:] for grad in grads], axis=1)
     sent_grads, upstream, _ = lax.optimization_barrier((sent_grads, upstream, partial_grad))
     other_grads = swap(sent_grads)
     other_upstream = swap(upstream)
-    column_sum, other_grads, other_inputs, other_upstream = lax.optimization_barrier(
-        (column_sum, other_grads, other_inputs, other_upstream)
+    column_sum, other_grads, other_upstream = lax.optimization_barrier(
+        (column_sum, other_grads, other_upstream)
     )
     input_grad = return_outer(column_sum, count, inner)
     weight_grads = on_chip(

time: 67.1 us -> 64.2 us (0.957)
  waiting for transfers between devices: 25.5 us -> 19 us
  starting transfers between devices: 29.2 us -> 32.8 us
    ppermute x11 -> x14, waiting for transfers between devices: 20.3 us -> 14.3 us  [swap_inner(): lax.ppermute(value, 'expert', [(place, place ^ partner) for place in rang...]
    ppermute x11 -> x14, starting transfers between devices: 13.1 us -> 16.8 us  [swap_inner(): lax.ppermute(value, 'expert', [(place, place ^ partner) for place in rang...]
    pallas_call x4 -> x5, Pallas kernels: 4.51 us -> 4.58 us  [on_chip(): pl.pallas_call(body, out_shape=[jax.ShapeDtypeStruct(shape, dtype) for sh...]
  transfers between devices with their start and end apart: 25 -> 28, of which waited for: 11 -> 12; matrix products, arithmetic and copies ran while one was open for 9% -> 9% of each run, Pallas kernels for 7% -> 7%
where the time goes in v18:
time: 64.2 us; the launch traced here: 64 us
  starting transfers between devices  32.8 us (51%)
  waiting for transfers between devices  19 us (30%)
  Pallas kernels  4.58 us (7%)
  other arithmetic  3.1 us (5%)
  matrix products  2.81 us (4%)
  between operations  0.98 us (2%)
  local copies, waits for them, and re-layouts  0.74 us (1%)
    ppermute x14, starting transfers between devices, swap_inner(): lax.ppermute(value, 'expert', [(place, place ^ partner) for place in rang...  16.8 us
    ppermute x9, starting transfers between devices, shift_outer(): lax.ppermute(value, 'expert', [(place, (place + step * inner) % count) fo...  15.8 us
    ppermute x14, waiting for transfers between devices, swap_inner(): lax.ppermute(value, 'expert', [(place, place ^ partner) for place in rang...  14.3 us
    ppermute x9, waiting for transfers between devices, shift_outer(): lax.ppermute(value, 'expert', [(place, (place + step * inner) % count) fo...  4.72 us
    pallas_call x5, Pallas kernels, on_chip(): pl.pallas_call(body, out_shape=[jax.ShapeDtypeStruct(shape, dtype) for sh...  4.58 us
    concatenate x1, other arithmetic, dense_local(): own_weights = jnp.concatenate([w_gate[0], w_up[0], w_down[0]], axis=0)  1.93 us
  transfers between devices with their start and end apart: 28, of which 12 were waited for; matrix products, arithmetic and copies ran while one was open for 9% of the time, Pallas kernels for 7%

profile of v18, /device:TPU:0, one launch (start us, length us, event | category | flops | bytes accessed | tf_op | source)
XLA Modules:
  0.0 64.0 jit_solution(13618538866908143937)
XLA Ops:
  0.6 5.1 %collective-permute-start.3 = (bf16[16,2048]{1,0:T(8,128)(2,1)}, bf16[16,2048]{1,0:T(8,128)(2,1)S(1)}, u32[]{:S(2)}, u32[]{:S(2)}) collective-permute-start(bf16[16,2048]{1,0:T(8,128)(2,1)} %tokens_hbm.1), channel_id=1, source_target_pairs={{0,12},{1,13},{2,14},{3,15},{4,0},{5,1},{6,2},{7,3},{8,4},{9,5},{1... | collective-permute-start | bytes 196616 | tf_op jit(solution)/shard_map/ppermute | solution.py:137
  6.7 1.6 %shard_map.111 = (bf16[32,16]{1,0:T(8,128)(2,1)}, bf16[16,2048]{1,0:T(8,128)(2,1)}, bf16[16,2048]{1,0:T(8,128)(2,1)}) custom-call(s32[8,16]{1,0:T(8,128)} %bitcast.15, bf16[8,16]{1,0:T(8,128)(2,1)} %bitcast.16, s32[1,16]{1,0:T(1,128)} %bitcast.17, bf16[16,2048]{1,0:T(8,128)(2,1)} %tokens_hbm.1, bf16[16,2048]{1,0:T(8,128)(2,1)} %cotangent_hbm.1), custom_call_target="tpu_custom_call" | custom-call | bytes 264000 | tf_op jit(solution)/shard_map/pallas_call | solution.py:156
  8.5 1.9 %pad_maximum_fusion.own_ref = bf16[576,2048]{1,0:T(8,128)(2,1)S(1)} fusion(bf16[192,2048]{1,0:T(8,128)(2,1)} %bitcast.12, bf16[192,2048]{1,0:T(8,128)(2,1)} %bitcast.13, bf16[192,2048]{1,0:T(8,128)(2,1)} %bitcast.14), kind=kLoop, calls=%fused_computation.1 | loop fusion | flops 7077888 | bytes 4718592 | tf_op jit(solution)/shard_map/concatenate | solution.py:338
  10.6 1.9 %collective-permute-start.5 = (bf16[16,2064]{1,0:T(8,128)(2,1)S(1)}, bf16[16,2064]{1,0:T(8,128)(2,1)S(1)}, u32[]{:S(2)}, u32[]{:S(2)}) collective-permute-start(bf16[16,2064]{1,0:T(8,128)(2,1)S(1)} %get-tuple-element.31), channel_id=1, source_target_pairs={{0,8},{1,9},{2,10},{3,11},{4,12},{5,13},{6,14},{7,15},{8,0},{9,1},... | collective-permute-start | bytes 198152 | tf_op jit(solution)/shard_map/ppermute | solution.py:137
  12.6 1.6 %collective-permute-start.11 = (bf16[64,2048]{1,0:T(8,128)(2,1)S(1)}, bf16[64,2048]{1,0:T(8,128)(2,1)S(1)}, u32[]{:S(2)}, u32[]{:S(2)}) collective-permute-start(bf16[64,2048]{1,0:T(8,128)(2,1)S(1)} %pad_maximum_fusion.3), channel_id=1, source_target_pairs={{0,1},{1,0},{2,3},{3,2},{4,5},{5,4},{6,7},{7,6},{8,9},{9,8},{10,11... | collective-permute-start | bytes 786440 | tf_op jit(solution)/shard_map/ppermute | solution.py:143
  14.1 1.6 %collective-permute-start.13 = (bf16[64,2048]{1,0:T(8,128)(2,1)S(1)}, bf16[64,2048]{1,0:T(8,128)(2,1)S(1)}, u32[]{:S(2)}, u32[]{:S(2)}) collective-permute-start(bf16[64,2048]{1,0:T(8,128)(2,1)S(1)} %pad_maximum_fusion.3), channel_id=1, source_target_pairs={{0,2},{1,3},{2,0},{3,1},{4,6},{5,7},{6,4},{7,5},{8,10},{9,11},{10,... | collective-permute-start | bytes 786440 | tf_op jit(solution)/shard_map/ppermute | solution.py:143
  15.7 1.5 %collective-permute-start.4 = (bf16[16,2064]{1,0:T(8,128)(2,1)S(1)}, bf16[16,2064]{1,0:T(8,128)(2,1)S(1)}, u32[]{:S(2)}, u32[]{:S(2)}) collective-permute-start(bf16[16,2064]{1,0:T(8,128)(2,1)S(1)} %get-tuple-element.31), channel_id=1, source_target_pairs={{0,4},{1,5},{2,6},{3,7},{4,8},{5,9},{6,10},{7,11},{8,12},{9,13},{1... | collective-permute-start | bytes 198152 | tf_op jit(solution)/shard_map/ppermute | solution.py:137
  17.2 2.4 %collective-permute-start.6 = (bf16[16,2064]{1,0:T(8,128)(2,1)S(1)}, bf16[16,2064]{1,0:T(8,128)(2,1)S(1)}, u32[]{:S(2)}, u32[]{:S(2)}) collective-permute-start(bf16[16,2064]{1,0:T(8,128)(2,1)S(1)} %get-tuple-element.31), channel_id=1, source_target_pairs={{0,12},{1,13},{2,14},{3,15},{4,0},{5,1},{6,2},{7,3},{8,4},{9,5},{1... | collective-permute-start | bytes 198152 | tf_op jit(solution)/shard_map/ppermute | solution.py:137
  19.6 2.6 %collective-permute-done.4 = bf16[16,2064]{1,0:T(8,128)(2,1)S(1)} collective-permute-done((bf16[16,2064]{1,0:T(8,128)(2,1)S(1)}, bf16[16,2064]{1,0:T(8,128)(2,1)S(1)}, u32[]{:S(2)}, u32[]{:S(2)}) %collective-permute-start.4) | collective-permute-done | bytes 66080 | tf_op jit(solution)/shard_map/ppermute | solution.py:137
  23.5 1.6 %collective-permute-start.14 = (bf16[32,2048]{1,0:T(8,128)(2,1)S(1)}, bf16[32,2048]{1,0:T(8,128)(2,1)S(1)}, u32[]{:S(2)}, u32[]{:S(2)}) collective-permute-start(bf16[32,2048]{1,0:T(8,128)(2,1)S(1)} %slice.114), channel_id=1, source_target_pairs={{0,2},{1,3},{2,0},{3,1},{4,6},{5,7},{6,4},{7,5},{8,10},{9,11},{10,... | collective-permute-start | bytes 393224 | tf_op jit(solution)/shard_map/ppermute | solution.py:143
  25.1 1.6 %collective-permute-start.15 = (bf16[32,2048]{1,0:T(8,128)(2,1)S(1)}, bf16[32,2048]{1,0:T(8,128)(2,1)S(1)}, u32[]{:S(2)}, u32[]{:S(2)}) collective-permute-start(bf16[32,2048]{1,0:T(8,128)(2,1)S(1)} %slice.115), channel_id=1, source_target_pairs={{0,1},{1,0},{2,3},{3,2},{4,5},{5,4},{6,7},{7,6},{8,9},{9,8},{10,11... | collective-permute-start | bytes 393224 | tf_op jit(solution)/shard_map/ppermute | solution.py:143
  26.7 4.2 %collective-permute-done.7 = bf16[64,2064]{1,0:T(8,128)(2,1)S(1)} collective-permute-done((bf16[64,2064]{1,0:T(8,128)(2,1)S(1)}, bf16[64,2064]{1,0:T(8,128)(2,1)S(1)}, u32[]{:S(2)}, u32[]{:S(2)}) %collective-permute-start.7) | collective-permute-done | bytes 264224 | tf_op jit(solution)/shard_map/ppermute | solution.py:143
  32.5 1.6 %collective-permute-start.10 = (bf16[32,2064]{1,0:T(8,128)(2,1)S(1)}, bf16[32,2064]{1,0:T(8,128)(2,1)S(1)}, u32[]{:S(2)}, u32[]{:S(2)}) collective-permute-start(bf16[32,2064]{1,0:T(8,128)(2,1)S(1)} %slice.111), channel_id=1, source_target_pairs={{0,1},{1,0},{2,3},{3,2},{4,5},{5,4},{6,7},{7,6},{8,9},{9,8},{10,11... | collective-permute-start | bytes 396296 | tf_op jit(solution)/shard_map/ppermute | solution.py:143
  34.3 1.7 %collective-permute-done.9 = bf16[32,2064]{1,0:T(8,128)(2,1)S(1)} collective-permute-done((bf16[32,2064]{1,0:T(8,128)(2,1)S(1)}, bf16[32,2064]{1,0:T(8,128)(2,1)S(1)}, u32[]{:S(2)}, u32[]{:S(2)}) %collective-permute-start.9) | collective-permute-done | bytes 132128 | tf_op jit(solution)/shard_map/ppermute | solution.py:143
  36.0 1.6 %collective-permute-done.10 = bf16[32,2064]{1,0:T(8,128)(2,1)S(1)} collective-permute-done((bf16[32,2064]{1,0:T(8,128)(2,1)S(1)}, bf16[32,2064]{1,0:T(8,128)(2,1)S(1)}, u32[]{:S(2)}, u32[]{:S(2)}) %collective-permute-start.10) | collective-permute-done | bytes 132128 | tf_op jit(solution)/shard_map/ppermute | solution.py:143
  42.1 1.1 %collective-permute-start.18 = (bf16[32,2048]{1,0:T(8,128)(2,1)S(1)}, bf16[32,2048]{1,0:T(8,128)(2,1)S(1)}, u32[]{:S(2)}, u32[]{:S(2)}) collective-permute-start(bf16[32,2048]{1,0:T(8,128)(2,1)S(1)} %get-tuple-element.54), channel_id=1, source_target_pairs={{0,1},{1,0},{2,3},{3,2},{4,5},{5,4},{6,7},{7,6},{8,9},{9,8},{10,11... | collective-permute-start | bytes 393224 | tf_op jit(solution)/shard_map/ppermute | solution.py:143
  44.2 1.5 %collective-permute-start.21 = (bf16[32,2048]{1,0:T(8,128)(2,1)S(1)}, bf16[32,2048]{1,0:T(8,128)(2,1)S(1)}, u32[]{:S(2)}, u32[]{:S(2)}) collective-permute-start(bf16[32,2048]{1,0:T(8,128)(2,1)S(1)} %get-tuple-element.52), channel_id=1, source_target_pairs={{0,2},{1,3},{2,0},{3,1},{4,6},{5,7},{6,4},{7,5},{8,10},{9,11},{10,... | collective-permute-start | bytes 393224 | tf_op jit(solution)/shard_map/ppermute | solution.py:143
  45.7 2.2 %collective-permute-done.17.right_ref = bf16[32,2048]{1,0:T(8,128)(2,1)S(1)} collective-permute-done((bf16[32,2048]{1,0:T(8,128)(2,1)S(1)}, bf16[32,2048]{1,0:T(8,128)(2,1)S(1)}, u32[]{:S(2)}, u32[]{:S(2)}) %collective-permute-start.17) | collective-permute-done | bytes 131104 | tf_op jit(solution)/shard_map/ppermute | solution.py:143
  48.5 1.1 %collective-permute-start.19 = (bf16[32,2048]{1,0:T(8,128)(2,1)S(1)}, bf16[32,2048]{1,0:T(8,128)(2,1)S(1)}, u32[]{:S(2)}, u32[]{:S(2)}) collective-permute-start(bf16[32,2048]{1,0:T(8,128)(2,1)S(1)} %get-tuple-element.39), channel_id=1, source_target_pairs={{0,1},{1,0},{2,3},{3,2},{4,5},{5,4},{6,7},{7,6},{8,9},{9,8},{10,11... | collective-permute-start | bytes 393224 | tf_op jit(solution)/shard_map/ppermute | solution.py:143
  49.7 2.0 %collective-permute-start.22 = (bf16[32,2048]{1,0:T(8,128)(2,1)S(1)}, bf16[32,2048]{1,0:T(8,128)(2,1)S(1)}, u32[]{:S(2)}, u32[]{:S(2)}) collective-permute-start(bf16[32,2048]{1,0:T(8,128)(2,1)S(1)} %get-tuple-element.40), channel_id=1, source_target_pairs={{0,2},{1,3},{2,0},{3,1},{4,6},{5,7},{6,4},{7,5},{8,10},{9,11},{10,... | collective-permute-start | bytes 393224 | tf_op jit(solution)/shard_map/ppermute | solution.py:143
  51.7 1.9 %collective-permute-done.19 = bf16[32,2048]{1,0:T(8,128)(2,1)S(1)} collective-permute-done((bf16[32,2048]{1,0:T(8,128)(2,1)S(1)}, bf16[32,2048]{1,0:T(8,128)(2,1)S(1)}, u32[]{:S(2)}, u32[]{:S(2)}) %collective-permute-start.19) | collective-permute-done | bytes 131104 | tf_op jit(solution)/shard_map/ppermute | solution.py:143
  55.1 3.5 %collective-permute-start.26 = (bf16[16,2048]{1,0:T(8,128)(2,1)S(1)}, bf16[16,2048]{1,0:T(8,128)(2,1)S(1)}, u32[]{:S(2)}, u32[]{:S(2)}) collective-permute-start(bf16[16,2048]{1,0:T(8,128)(2,1)S(1)} %get-tuple-element.61), channel_id=1, source_target_pairs={{0,8},{1,9},{2,10},{3,11},{4,12},{5,13},{6,14},{7,15},{8,0},{9,1},... | collective-permute-start | bytes 196616 | tf_op jit(solution)/shard_map/ppermute | solution.py:137
  58.8 2.5 %shard_map.115 = (bf16[1,192,2048]{2,1,0:T(8,128)(2,1)}, bf16[1,192,2048]{2,1,0:T(8,128)(2,1)}, bf16[1,192,2048]{2,1,0:T(8,128)(2,1)}) custom-call(bf16[256,576]{1,0:T(8,128)(2,1)S(1)} %pad_maximum_fusion.2.own_grads, bf16[256,576]{1,0:T(8,128)(2,1)S(1)} %collective-permute-done.23.other_grads, ...), custom_call_target="tpu_custom_call" | custom-call | bytes 7143424 | tf_op jit(solution)/shard_map/pallas_call | solution.py:156
  61.3 1.6 %collective-permute-done.26 = bf16[16,2048]{1,0:T(8,128)(2,1)S(1)} collective-permute-done((bf16[16,2048]{1,0:T(8,128)(2,1)S(1)}, bf16[16,2048]{1,0:T(8,128)(2,1)S(1)}, u32[]{:S(2)}, u32[]{:S(2)}) %collective-permute-start.26) | collective-permute-done | bytes 65568 | tf_op jit(solution)/shard_map/ppermute | solution.py:137
  (77 shorter events, 13.2 us)
Async XLA Ops:
  0.6 11.9 %collective-permute-start.3 = (bf16[16,2048]{1,0:T(8,128)(2,1)}, bf16[16,2048]{1,0:T(8,128)(2,1)S(1)}, u32[]{:S(2)}, u32[]{:S(2)}) collective-permute-start(bf16[16,2048]{1,0:T(8,128)(2,1)} %tokens_hbm.1), channel_id=1, source_target_pairs={{0,12},{1,13},{2,14},{3,15},{4,0},{5,1},{6,2},{7,3},{8,4},{9,5},{1... | collective-permute-start | bytes 196616 | tf_op jit(solution)/shard_map/ppermute | solution.py:137
  5.7 6.8 %collective-permute-start.2 = (bf16[16,2048]{1,0:T(8,128)(2,1)}, bf16[16,2048]{1,0:T(8,128)(2,1)S(1)}, u32[]{:S(2)}, u32[]{:S(2)}) collective-permute-start(bf16[16,2048]{1,0:T(8,128)(2,1)} %tokens_hbm.1), channel_id=1, source_target_pairs={{0,8},{1,9},{2,10},{3,11},{4,12},{5,13},{6,14},{7,15},{8,0},{9,1},... | collective-permute-start | bytes 196616 | tf_op jit(solution)/shard_map/ppermute | solution.py:137
  5.7 6.8 %collective-permute-start.1 = (bf16[16,2048]{1,0:T(8,128)(2,1)}, bf16[16,2048]{1,0:T(8,128)(2,1)S(1)}, u32[]{:S(2)}, u32[]{:S(2)}) collective-permute-start(bf16[16,2048]{1,0:T(8,128)(2,1)} %tokens_hbm.1), channel_id=1, source_target_pairs={{0,4},{1,5},{2,6},{3,7},{4,8},{5,9},{6,10},{7,11},{8,12},{9,13},{1... | collective-permute-start | bytes 196616 | tf_op jit(solution)/shard_map/ppermute | solution.py:137
  10.6 11.6 %collective-permute-start.5 = (bf16[16,2064]{1,0:T(8,128)(2,1)S(1)}, bf16[16,2064]{1,0:T(8,128)(2,1)S(1)}, u32[]{:S(2)}, u32[]{:S(2)}) collective-permute-start(bf16[16,2064]{1,0:T(8,128)(2,1)S(1)} %get-tuple-element.31), channel_id=1, source_target_pairs={{0,8},{1,9},{2,10},{3,11},{4,12},{5,13},{6,14},{7,15},{8,0},{9,1},... | collective-permute-start | bytes 198152 | tf_op jit(solution)/shard_map/ppermute | solution.py:137
  12.6 10.9 %collective-permute-start.11 = (bf16[64,2048]{1,0:T(8,128)(2,1)S(1)}, bf16[64,2048]{1,0:T(8,128)(2,1)S(1)}, u32[]{:S(2)}, u32[]{:S(2)}) collective-permute-start(bf16[64,2048]{1,0:T(8,128)(2,1)S(1)} %pad_maximum_fusion.3), channel_id=1, source_target_pairs={{0,1},{1,0},{2,3},{3,2},{4,5},{5,4},{6,7},{7,6},{8,9},{9,8},{10,11... | collective-permute-start | bytes 786440 | tf_op jit(solution)/shard_map/ppermute | solution.py:143
  14.1 10.9 %collective-permute-start.13 = (bf16[64,2048]{1,0:T(8,128)(2,1)S(1)}, bf16[64,2048]{1,0:T(8,128)(2,1)S(1)}, u32[]{:S(2)}, u32[]{:S(2)}) collective-permute-start(bf16[64,2048]{1,0:T(8,128)(2,1)S(1)} %pad_maximum_fusion.3), channel_id=1, source_target_pairs={{0,2},{1,3},{2,0},{3,1},{4,6},{5,7},{6,4},{7,5},{8,10},{9,11},{10,... | collective-permute-start | bytes 786440 | tf_op jit(solution)/shard_map/ppermute | solution.py:143
  15.7 6.5 %collective-permute-start.4 = (bf16[16,2064]{1,0:T(8,128)(2,1)S(1)}, bf16[16,2064]{1,0:T(8,128)(2,1)S(1)}, u32[]{:S(2)}, u32[]{:S(2)}) collective-permute-start(bf16[16,2064]{1,0:T(8,128)(2,1)S(1)} %get-tuple-element.31), channel_id=1, source_target_pairs={{0,4},{1,5},{2,6},{3,7},{4,8},{5,9},{6,10},{7,11},{8,12},{9,13},{1... | collective-permute-start | bytes 198152 | tf_op jit(solution)/shard_map/ppermute | solution.py:137
  17.2 5.1 %collective-permute-start.6 = (bf16[16,2064]{1,0:T(8,128)(2,1)S(1)}, bf16[16,2064]{1,0:T(8,128)(2,1)S(1)}, u32[]{:S(2)}, u32[]{:S(2)}) collective-permute-start(bf16[16,2064]{1,0:T(8,128)(2,1)S(1)} %get-tuple-element.31), channel_id=1, source_target_pairs={{0,12},{1,13},{2,14},{3,15},{4,0},{5,1},{6,2},{7,3},{8,4},{9,5},{1... | collective-permute-start | bytes 198152 | tf_op jit(solution)/shard_map/ppermute | solution.py:137
  22.3 8.5 %collective-permute-start.7 = (bf16[64,2064]{1,0:T(8,128)(2,1)S(1)}, bf16[64,2064]{1,0:T(8,128)(2,1)S(1)}, u32[]{:S(2)}, u32[]{:S(2)}) collective-permute-start(bf16[64,2064]{1,0:T(8,128)(2,1)S(1)} %get-tuple-element.68), channel_id=1, source_target_pairs={{0,1},{1,0},{2,3},{3,2},{4,5},{5,4},{6,7},{7,6},{8,9},{9,8},{10,11... | collective-permute-start | bytes 792584 | tf_op jit(solution)/shard_map/ppermute | solution.py:143
  22.9 9.5 %collective-permute-start.8 = (bf16[64,2064]{1,0:T(8,128)(2,1)S(1)}, bf16[64,2064]{1,0:T(8,128)(2,1)S(1)}, u32[]{:S(2)}, u32[]{:S(2)}) collective-permute-start(bf16[64,2064]{1,0:T(8,128)(2,1)S(1)} %get-tuple-element.68), channel_id=1, source_target_pairs={{0,2},{1,3},{2,0},{3,1},{4,6},{5,7},{6,4},{7,5},{8,10},{9,11},{10,... | collective-permute-start | bytes 792584 | tf_op jit(solution)/shard_map/ppermute | solution.py:143
  23.4 14.4 %collective-permute-start.12 = (bf16[576,2048]{1,0:T(8,128)(2,1)S(1)}, bf16[576,2048]{1,0:T(8,128)(2,1)S(1)}, u32[]{:S(2)}, u32[]{:S(2)}) collective-permute-start(bf16[576,2048]{1,0:T(8,128)(2,1)S(1)} %pad_maximum_fusion.own_ref), channel_id=1, source_target_pairs={{0,16},{16,0},{1,17},{17,1},{2,18},{18,2},{3,19},{19,3},{4,20},{20... | collective-permute-start | bytes 7077896 | tf_op jit(solution)/shard_map/ppermute | solution.py:133
  23.5 10.7 %collective-permute-start.14 = (bf16[32,2048]{1,0:T(8,128)(2,1)S(1)}, bf16[32,2048]{1,0:T(8,128)(2,1)S(1)}, u32[]{:S(2)}, u32[]{:S(2)}) collective-permute-start(bf16[32,2048]{1,0:T(8,128)(2,1)S(1)} %slice.114), channel_id=1, source_target_pairs={{0,2},{1,3},{2,0},{3,1},{4,6},{5,7},{6,4},{7,5},{8,10},{9,11},{10,... | collective-permute-start | bytes 393224 | tf_op jit(solution)/shard_map/ppermute | solution.py:143
  25.1 9.1 %collective-permute-start.15 = (bf16[32,2048]{1,0:T(8,128)(2,1)S(1)}, bf16[32,2048]{1,0:T(8,128)(2,1)S(1)}, u32[]{:S(2)}, u32[]{:S(2)}) collective-permute-start(bf16[32,2048]{1,0:T(8,128)(2,1)S(1)} %slice.115), channel_id=1, source_target_pairs={{0,1},{1,0},{2,3},{3,2},{4,5},{5,4},{6,7},{7,6},{8,9},{9,8},{10,11... | collective-permute-start | bytes 393224 | tf_op jit(solution)/shard_map/ppermute | solution.py:143
  30.9 5.1 %collective-permute-start.9 = (bf16[32,2064]{1,0:T(8,128)(2,1)S(1)}, bf16[32,2064]{1,0:T(8,128)(2,1)S(1)}, u32[]{:S(2)}, u32[]{:S(2)}) collective-permute-start(bf16[32,2064]{1,0:T(8,128)(2,1)S(1)} %slice.110), channel_id=1, source_target_pairs={{0,2},{1,3},{2,0},{3,1},{4,6},{5,7},{6,4},{7,5},{8,10},{9,11},{10,... | collective-permute-start | bytes 396296 | tf_op jit(solution)/shard_map/ppermute | solution.py:143
  32.5 5.1 %collective-permute-start.10 = (bf16[32,2064]{1,0:T(8,128)(2,1)S(1)}, bf16[32,2064]{1,0:T(8,128)(2,1)S(1)}, u32[]{:S(2)}, u32[]{:S(2)}) collective-permute-start(bf16[32,2064]{1,0:T(8,128)(2,1)S(1)} %slice.111), channel_id=1, source_target_pairs={{0,1},{1,0},{2,3},{3,2},{4,5},{5,4},{6,7},{7,6},{8,9},{9,8},{10,11... | collective-permute-start | bytes 396296 | tf_op jit(solution)/shard_map/ppermute | solution.py:143
  34.2 6.9 %collective-permute-start.16 = (bf16[256,2048]{1,0:T(8,128)(2,1)S(1)}, bf16[256,2048]{1,0:T(8,128)(2,1)S(1)}, u32[]{:S(2)}, u32[]{:S(2)}) collective-permute-start(bf16[256,2048]{1,0:T(8,128)(2,1)S(1)} %constant_dynamic-update-slice_fusion.12.rows), channel_id=1, source_target_pairs={{0,16},{16,0},{1,17},{17,1},{2,18},{18,2},{3,19},{19,3},{4,20},{20... | collective-permute-start | bytes 3145736 | tf_op jit(solution)/shard_map/ppermute | solution.py:133
  41.4 13.4 %collective-permute-start.24 = (bf16[256,2048]{1,0:T(8,128)(2,1)S(1)}, bf16[256,2048]{1,0:T(8,128)(2,1)S(1)}, u32[]{:S(2)}, u32[]{:S(2)}) collective-permute-start(bf16[256,2048]{1,0:T(8,128)(2,1)S(1)} %slice.113.upstream), channel_id=1, source_target_pairs={{0,16},{16,0},{1,17},{17,1},{2,18},{18,2},{3,19},{19,3},{4,20},{20... | collective-permute-start | bytes 3145736 | tf_op jit(solution)/shard_map/ppermute | solution.py:133
  41.6 6.4 %collective-permute-start.17 = (bf16[32,2048]{1,0:T(8,128)(2,1)S(1)}, bf16[32,2048]{1,0:T(8,128)(2,1)S(1)}, u32[]{:S(2)}, u32[]{:S(2)}) collective-permute-start(bf16[32,2048]{1,0:T(8,128)(2,1)S(1)} %get-tuple-element.56), channel_id=1, source_target_pairs={{0,2},{1,3},{2,0},{3,1},{4,6},{5,7},{6,4},{7,5},{8,10},{9,11},{10,... | collective-permute-start | bytes 393224 | tf_op jit(solution)/shard_map/ppermute | solution.py:143
  42.1 6.3 %collective-permute-start.18 = (bf16[32,2048]{1,0:T(8,128)(2,1)S(1)}, bf16[32,2048]{1,0:T(8,128)(2,1)S(1)}, u32[]{:S(2)}, u32[]{:S(2)}) collective-permute-start(bf16[32,2048]{1,0:T(8,128)(2,1)S(1)} %get-tuple-element.54), channel_id=1, source_target_pairs={{0,1},{1,0},{2,3},{3,2},{4,5},{5,4},{6,7},{7,6},{8,9},{9,8},{10,11... | collective-permute-start | bytes 393224 | tf_op jit(solution)/shard_map/ppermute | solution.py:143
  43.3 8.4 %collective-permute-start.20 = (bf16[32,2048]{1,0:T(8,128)(2,1)S(1)}, bf16[32,2048]{1,0:T(8,128)(2,1)S(1)}, u32[]{:S(2)}, u32[]{:S(2)}) collective-permute-start(bf16[32,2048]{1,0:T(8,128)(2,1)S(1)} %get-tuple-element.53), channel_id=1, source_target_pairs={{0,1},{1,0},{2,3},{3,2},{4,5},{5,4},{6,7},{7,6},{8,9},{9,8},{10,11... | collective-permute-start | bytes 393224 | tf_op jit(solution)/shard_map/ppermute | solution.py:143
  44.2 7.5 %collective-permute-start.21 = (bf16[32,2048]{1,0:T(8,128)(2,1)S(1)}, bf16[32,2048]{1,0:T(8,128)(2,1)S(1)}, u32[]{:S(2)}, u32[]{:S(2)}) collective-permute-start(bf16[32,2048]{1,0:T(8,128)(2,1)S(1)} %get-tuple-element.52), channel_id=1, source_target_pairs={{0,2},{1,3},{2,0},{3,1},{4,6},{5,7},{6,4},{7,5},{8,10},{9,11},{10,... | collective-permute-start | bytes 393224 | tf_op jit(solution)/shard_map/ppermute | solution.py:143
  48.5 5.0 %collective-permute-start.19 = (bf16[32,2048]{1,0:T(8,128)(2,1)S(1)}, bf16[32,2048]{1,0:T(8,128)(2,1)S(1)}, u32[]{:S(2)}, u32[]{:S(2)}) collective-permute-start(bf16[32,2048]{1,0:T(8,128)(2,1)S(1)} %get-tuple-element.39), channel_id=1, source_target_pairs={{0,1},{1,0},{2,3},{3,2},{4,5},{5,4},{6,7},{7,6},{8,9},{9,8},{10,11... | collective-permute-start | bytes 393224 | tf_op jit(solution)/shard_map/ppermute | solution.py:143
  54.8 6.5 %collective-permute-start.27 = (bf16[16,2048]{1,0:T(8,128)(2,1)S(1)}, bf16[16,2048]{1,0:T(8,128)(2,1)S(1)}, u32[]{:S(2)}, u32[]{:S(2)}) collective-permute-start(bf16[16,2048]{1,0:T(8,128)(2,1)S(1)} %get-tuple-element.60), channel_id=1, source_target_pairs={{0,4},{1,5},{2,6},{3,7},{4,8},{5,9},{6,10},{7,11},{8,12},{9,13},{1... | collective-permute-start | bytes 196616 | tf_op jit(solution)/shard_map/ppermute | solution.py:137
  55.1 7.8 %collective-permute-start.26 = (bf16[16,2048]{1,0:T(8,128)(2,1)S(1)}, bf16[16,2048]{1,0:T(8,128)(2,1)S(1)}, u32[]{:S(2)}, u32[]{:S(2)}) collective-permute-start(bf16[16,2048]{1,0:T(8,128)(2,1)S(1)} %get-tuple-element.61), channel_id=1, source_target_pairs={{0,8},{1,9},{2,10},{3,11},{4,12},{5,13},{6,14},{7,15},{8,0},{9,1},... | collective-permute-start | bytes 196616 | tf_op jit(solution)/shard_map/ppermute | solution.py:137
  (7 other events, 22.8 us)

commit v19 on v18

--- a/solution.py
+++ b/solution.py
@@ -253,14 +253,24 @@
 
 
 def across_inner(column, count, inner):
-    if inner < 4:
-        return [column] + [swap_inner(column, count, partner) for partner in range(1, inner)]
     cut = column.shape[0] // 2
     first = swap_inner(column, count, 1)
     second = swap_inner(column, count, 2)
     far_top = swap_inner(first[:cut], count, 2)
     far_bottom = swap_inner(second[cut:], count, 1)
     return [column, first, second, far_top, far_bottom]
+
+
+def across_halves(column, count):
+    cut = column.shape[0] // 2
+    top, bottom = column[:cut], column[cut:]
+    first_top = swap_inner(top, count, 1)
+    second_bottom = swap_inner(bottom, count, 2)
+    first_bottom = swap_inner(bottom, count, 1)
+    second_top = swap_inner(top, count, 2)
+    far_top = swap_inner(first_top, count, 2)
+    far_bottom = swap_inner(second_bottom, count, 1)
+    return [column, first_top, first_bottom, second_top, second_bottom, far_top, far_bottom]
 
 
 def return_inner(value, count):
@@ -340,7 +350,7 @@
     other = swap(sent_weights)
     inputs = jnp.concatenate(token_columns, axis=0)
     other_inputs = swap(inputs)
-    upstream = jnp.concatenate(across_inner(upstream_column, count, inner), axis=0)
+    upstream = jnp.concatenate(across_halves(upstream_column, count), axis=0)
     gate = jnp.sum(
         upstream[:, model_width:].astype(jnp.float32) * here[:1], axis=1, keepdims=True
     )

time: 64.2 us -> 68.2 us (1.062)
  waiting for transfers between devices: 19 us -> 21.5 us
  starting transfers between devices: 32.8 us -> 34.3 us
    ppermute x14 -> x16, waiting for transfers between devices: 14.3 us -> 18.7 us  [swap_inner(): lax.ppermute(value, 'expert', [(place, place ^ partner) for place in rang...]
    ppermute x9, waiting for transfers between devices: 4.72 us -> 2.81 us  [shift_outer(): lax.ppermute(value, 'expert', [(place, (place + step * inner) % count) fo...]
    ppermute x9, starting transfers between devices: 15.8 us -> 17.3 us  [shift_outer(): lax.ppermute(value, 'expert', [(place, (place + step * inner) % count) fo...]
    ppermute x14 -> x16, starting transfers between devices: 16.8 us -> 16.3 us  [swap_inner(): lax.ppermute(value, 'expert', [(place, place ^ partner) for place in rang...]
  transfers between devices with their start and end apart: 28 -> 30, of which waited for: 12 -> 13; matrix products, arithmetic and copies ran while one was open for 9% -> 8% of each run, Pallas kernels for 7% -> 7%
where the time goes in v19:
time: 68.2 us; the launch traced here: 68 us
  starting transfers between devices  34.3 us (50%)
  waiting for transfers between devices  21.5 us (32%)
  Pallas kernels  4.58 us (7%)
  other arithmetic  3.1 us (5%)
  matrix products  2.81 us (4%)
  between operations  0.98 us (1%)
  local copies, waits for them, and re-layouts  0.73 us (1%)
    ppermute x16, waiting for transfers between devices, swap_inner(): lax.ppermute(value, 'expert', [(place, place ^ partner) for place in rang...  18.7 us
    ppermute x9, starting transfers between devices, shift_outer(): lax.ppermute(value, 'expert', [(place, (place + step * inner) % count) fo...  17.3 us
    ppermute x16, starting transfers between devices, swap_inner(): lax.ppermute(value, 'expert', [(place, place ^ partner) for place in rang...  16.3 us
    pallas_call x5, Pallas kernels, on_chip(): pl.pallas_call(body, out_shape=[jax.ShapeDtypeStruct(shape, dtype) for sh...  4.58 us
    ppermute x9, waiting for transfers between devices, shift_outer(): lax.ppermute(value, 'expert', [(place, (place + step * inner) % count) fo...  2.81 us
    concatenate x1, other arithmetic, dense_local(): own_weights = jnp.concatenate([w_gate[0], w_up[0], w_down[0]], axis=0)  1.93 us
  transfers between devices with their start and end apart: 30, of which 13 were waited for; matrix products, arithmetic and copies ran while one was open for 8% of the time, Pallas kernels for 7%

profile of v19, /device:TPU:0, one launch (start us, length us, event | category | flops | bytes accessed | tf_op | source)
XLA Modules:
  0.0 68.0 jit_solution(1101632487981878332)
XLA Ops:
  0.6 5.1 %collective-permute-start.3 = (bf16[16,2048]{1,0:T(8,128)(2,1)}, bf16[16,2048]{1,0:T(8,128)(2,1)S(1)}, u32[]{:S(2)}, u32[]{:S(2)}) collective-permute-start(bf16[16,2048]{1,0:T(8,128)(2,1)} %tokens_hbm.1), channel_id=1, source_target_pairs={{0,12},{1,13},{2,14},{3,15},{4,0},{5,1},{6,2},{7,3},{8,4},{9,5},{1... | collective-permute-start | bytes 196616 | tf_op jit(solution)/shard_map/ppermute | solution.py:137
  6.7 1.6 %shard_map.111 = (bf16[32,16]{1,0:T(8,128)(2,1)}, bf16[16,2048]{1,0:T(8,128)(2,1)}, bf16[16,2048]{1,0:T(8,128)(2,1)}) custom-call(s32[8,16]{1,0:T(8,128)} %bitcast.15, bf16[8,16]{1,0:T(8,128)(2,1)} %bitcast.16, s32[1,16]{1,0:T(1,128)} %bitcast.17, bf16[16,2048]{1,0:T(8,128)(2,1)} %tokens_hbm.1, bf16[16,2048]{1,0:T(8,128)(2,1)} %cotangent_hbm.1), custom_call_target="tpu_custom_call" | custom-call | bytes 264000 | tf_op jit(solution)/shard_map/pallas_call | solution.py:156
  8.5 1.9 %pad_maximum_fusion.own_ref = bf16[576,2048]{1,0:T(8,128)(2,1)S(1)} fusion(bf16[192,2048]{1,0:T(8,128)(2,1)} %bitcast.12, bf16[192,2048]{1,0:T(8,128)(2,1)} %bitcast.13, bf16[192,2048]{1,0:T(8,128)(2,1)} %bitcast.14), kind=kLoop, calls=%fused_computation.1 | loop fusion | flops 7077888 | bytes 4718592 | tf_op jit(solution)/shard_map/concatenate | solution.py:348
  10.6 1.9 %collective-permute-start.5 = (bf16[16,2064]{1,0:T(8,128)(2,1)S(1)}, bf16[16,2064]{1,0:T(8,128)(2,1)S(1)}, u32[]{:S(2)}, u32[]{:S(2)}) collective-permute-start(bf16[16,2064]{1,0:T(8,128)(2,1)S(1)} %get-tuple-element.31), channel_id=1, source_target_pairs={{0,8},{1,9},{2,10},{3,11},{4,12},{5,13},{6,14},{7,15},{8,0},{9,1},... | collective-permute-start | bytes 198152 | tf_op jit(solution)/shard_map/ppermute | solution.py:137
  12.6 1.6 %collective-permute-start.13 = (bf16[64,2048]{1,0:T(8,128)(2,1)S(1)}, bf16[64,2048]{1,0:T(8,128)(2,1)S(1)}, u32[]{:S(2)}, u32[]{:S(2)}) collective-permute-start(bf16[64,2048]{1,0:T(8,128)(2,1)S(1)} %pad_maximum_fusion.3), channel_id=1, source_target_pairs={{0,1},{1,0},{2,3},{3,2},{4,5},{5,4},{6,7},{7,6},{8,9},{9,8},{10,11... | collective-permute-start | bytes 786440 | tf_op jit(solution)/shard_map/ppermute | solution.py:143
  14.1 1.6 %collective-permute-start.15 = (bf16[64,2048]{1,0:T(8,128)(2,1)S(1)}, bf16[64,2048]{1,0:T(8,128)(2,1)S(1)}, u32[]{:S(2)}, u32[]{:S(2)}) collective-permute-start(bf16[64,2048]{1,0:T(8,128)(2,1)S(1)} %pad_maximum_fusion.3), channel_id=1, source_target_pairs={{0,2},{1,3},{2,0},{3,1},{4,6},{5,7},{6,4},{7,5},{8,10},{9,11},{10,... | collective-permute-start | bytes 786440 | tf_op jit(solution)/shard_map/ppermute | solution.py:143
  15.7 1.5 %collective-permute-start.4 = (bf16[16,2064]{1,0:T(8,128)(2,1)S(1)}, bf16[16,2064]{1,0:T(8,128)(2,1)S(1)}, u32[]{:S(2)}, u32[]{:S(2)}) collective-permute-start(bf16[16,2064]{1,0:T(8,128)(2,1)S(1)} %get-tuple-element.31), channel_id=1, source_target_pairs={{0,4},{1,5},{2,6},{3,7},{4,8},{5,9},{6,10},{7,11},{8,12},{9,13},{1... | collective-permute-start | bytes 198152 | tf_op jit(solution)/shard_map/ppermute | solution.py:137
  17.2 2.4 %collective-permute-start.6 = (bf16[16,2064]{1,0:T(8,128)(2,1)S(1)}, bf16[16,2064]{1,0:T(8,128)(2,1)S(1)}, u32[]{:S(2)}, u32[]{:S(2)}) collective-permute-start(bf16[16,2064]{1,0:T(8,128)(2,1)S(1)} %get-tuple-element.31), channel_id=1, source_target_pairs={{0,12},{1,13},{2,14},{3,15},{4,0},{5,1},{6,2},{7,3},{8,4},{9,5},{1... | collective-permute-start | bytes 198152 | tf_op jit(solution)/shard_map/ppermute | solution.py:137
  19.6 2.6 %collective-permute-done.4 = bf16[16,2064]{1,0:T(8,128)(2,1)S(1)} collective-permute-done((bf16[16,2064]{1,0:T(8,128)(2,1)S(1)}, bf16[16,2064]{1,0:T(8,128)(2,1)S(1)}, u32[]{:S(2)}, u32[]{:S(2)}) %collective-permute-start.4) | collective-permute-done | bytes 66080 | tf_op jit(solution)/shard_map/ppermute | solution.py:137
  23.4 1.5 %collective-permute-start.8 = (bf16[32,2064]{1,0:T(8,128)(2,1)S(1)}, bf16[32,2064]{1,0:T(8,128)(2,1)S(1)}, u32[]{:S(2)}, u32[]{:S(2)}) collective-permute-start(bf16[32,2064]{1,0:T(8,128)(2,1)S(1)} %get-tuple-element.68), channel_id=1, source_target_pairs={{0,1},{1,0},{2,3},{3,2},{4,5},{5,4},{6,7},{7,6},{8,9},{9,8},{10,11... | collective-permute-start | bytes 396296 | tf_op jit(solution)/shard_map/ppermute | solution.py:143
  24.9 2.7 %collective-permute-done.7 = bf16[32,2064]{1,0:T(8,128)(2,1)S(1)} collective-permute-done((bf16[32,2064]{1,0:T(8,128)(2,1)S(1)}, bf16[32,2064]{1,0:T(8,128)(2,1)S(1)}, u32[]{:S(2)}, u32[]{:S(2)}) %collective-permute-start.7) | collective-permute-done | bytes 132128 | tf_op jit(solution)/shard_map/ppermute | solution.py:143
  30.0 2.7 %collective-permute-done.10 = bf16[32,2064]{1,0:T(8,128)(2,1)S(1)} collective-permute-done((bf16[32,2064]{1,0:T(8,128)(2,1)S(1)}, bf16[32,2064]{1,0:T(8,128)(2,1)S(1)}, u32[]{:S(2)}, u32[]{:S(2)}) %collective-permute-start.10) | collective-permute-done | bytes 132128 | tf_op jit(solution)/shard_map/ppermute | solution.py:143
  33.7 1.8 %collective-permute-start.16 = (bf16[32,2048]{1,0:T(8,128)(2,1)S(1)}, bf16[32,2048]{1,0:T(8,128)(2,1)S(1)}, u32[]{:S(2)}, u32[]{:S(2)}) collective-permute-start(bf16[32,2048]{1,0:T(8,128)(2,1)S(1)} %slice.108), channel_id=1, source_target_pairs={{0,2},{1,3},{2,0},{3,1},{4,6},{5,7},{6,4},{7,5},{8,10},{9,11},{10,... | collective-permute-start | bytes 393224 | tf_op jit(solution)/shard_map/ppermute | solution.py:143
  35.7 2.0 %collective-permute-done.12 = bf16[32,2064]{1,0:T(8,128)(2,1)S(1)} collective-permute-done((bf16[32,2064]{1,0:T(8,128)(2,1)S(1)}, bf16[32,2064]{1,0:T(8,128)(2,1)S(1)}, u32[]{:S(2)}, u32[]{:S(2)}) %collective-permute-start.12) | collective-permute-done | bytes 132128 | tf_op jit(solution)/shard_map/ppermute | solution.py:143
  38.0 1.7 %collective-permute-done.16 = bf16[32,2048]{1,0:T(8,128)(2,1)S(1)} collective-permute-done((bf16[32,2048]{1,0:T(8,128)(2,1)S(1)}, bf16[32,2048]{1,0:T(8,128)(2,1)S(1)}, u32[]{:S(2)}, u32[]{:S(2)}) %collective-permute-start.16) | collective-permute-done | bytes 131104 | tf_op jit(solution)/shard_map/ppermute | solution.py:143
  39.7 1.5 %collective-permute-done.17 = bf16[32,2048]{1,0:T(8,128)(2,1)S(1)} collective-permute-done((bf16[32,2048]{1,0:T(8,128)(2,1)S(1)}, bf16[32,2048]{1,0:T(8,128)(2,1)S(1)}, u32[]{:S(2)}, u32[]{:S(2)}) %collective-permute-start.17) | collective-permute-done | bytes 131104 | tf_op jit(solution)/shard_map/ppermute | solution.py:143
  45.9 1.6 %collective-permute-start.20 = (bf16[32,2048]{1,0:T(8,128)(2,1)S(1)}, bf16[32,2048]{1,0:T(8,128)(2,1)S(1)}, u32[]{:S(2)}, u32[]{:S(2)}) collective-permute-start(bf16[32,2048]{1,0:T(8,128)(2,1)S(1)} %get-tuple-element.54), channel_id=1, source_target_pairs={{0,1},{1,0},{2,3},{3,2},{4,5},{5,4},{6,7},{7,6},{8,9},{9,8},{10,11... | collective-permute-start | bytes 393224 | tf_op jit(solution)/shard_map/ppermute | solution.py:143
  47.9 1.7 %collective-permute-start.23 = (bf16[32,2048]{1,0:T(8,128)(2,1)S(1)}, bf16[32,2048]{1,0:T(8,128)(2,1)S(1)}, u32[]{:S(2)}, u32[]{:S(2)}) collective-permute-start(bf16[32,2048]{1,0:T(8,128)(2,1)S(1)} %get-tuple-element.52), channel_id=1, source_target_pairs={{0,2},{1,3},{2,0},{3,1},{4,6},{5,7},{6,4},{7,5},{8,10},{9,11},{10,... | collective-permute-start | bytes 393224 | tf_op jit(solution)/shard_map/ppermute | solution.py:143
  49.6 2.3 %collective-permute-done.19.right_ref = bf16[32,2048]{1,0:T(8,128)(2,1)S(1)} collective-permute-done((bf16[32,2048]{1,0:T(8,128)(2,1)S(1)}, bf16[32,2048]{1,0:T(8,128)(2,1)S(1)}, u32[]{:S(2)}, u32[]{:S(2)}) %collective-permute-start.19) | collective-permute-done | bytes 131104 | tf_op jit(solution)/shard_map/ppermute | solution.py:143
  52.3 1.7 %collective-permute-start.21 = (bf16[32,2048]{1,0:T(8,128)(2,1)S(1)}, bf16[32,2048]{1,0:T(8,128)(2,1)S(1)}, u32[]{:S(2)}, u32[]{:S(2)}) collective-permute-start(bf16[32,2048]{1,0:T(8,128)(2,1)S(1)} %get-tuple-element.39), channel_id=1, source_target_pairs={{0,1},{1,0},{2,3},{3,2},{4,5},{5,4},{6,7},{7,6},{8,9},{9,8},{10,11... | collective-permute-start | bytes 393224 | tf_op jit(solution)/shard_map/ppermute | solution.py:143
  54.8 2.6 %collective-permute-done.21 = bf16[32,2048]{1,0:T(8,128)(2,1)S(1)} collective-permute-done((bf16[32,2048]{1,0:T(8,128)(2,1)S(1)}, bf16[32,2048]{1,0:T(8,128)(2,1)S(1)}, u32[]{:S(2)}, u32[]{:S(2)}) %collective-permute-start.21) | collective-permute-done | bytes 131104 | tf_op jit(solution)/shard_map/ppermute | solution.py:143
  57.3 1.6 %collective-permute-done.24 = bf16[32,2048]{1,0:T(8,128)(2,1)S(1)} collective-permute-done((bf16[32,2048]{1,0:T(8,128)(2,1)S(1)}, bf16[32,2048]{1,0:T(8,128)(2,1)S(1)}, u32[]{:S(2)}, u32[]{:S(2)}) %collective-permute-start.24) | collective-permute-done | bytes 131104 | tf_op jit(solution)/shard_map/ppermute | solution.py:143
  60.0 3.1 %collective-permute-start.28 = (bf16[16,2048]{1,0:T(8,128)(2,1)S(1)}, bf16[16,2048]{1,0:T(8,128)(2,1)S(1)}, u32[]{:S(2)}, u32[]{:S(2)}) collective-permute-start(bf16[16,2048]{1,0:T(8,128)(2,1)S(1)} %get-tuple-element.61), channel_id=1, source_target_pairs={{0,8},{1,9},{2,10},{3,11},{4,12},{5,13},{6,14},{7,15},{8,0},{9,1},... | collective-permute-start | bytes 196616 | tf_op jit(solution)/shard_map/ppermute | solution.py:137
  64.7 2.5 %shard_map.115 = (bf16[1,192,2048]{2,1,0:T(8,128)(2,1)}, bf16[1,192,2048]{2,1,0:T(8,128)(2,1)}, bf16[1,192,2048]{2,1,0:T(8,128)(2,1)}) custom-call(bf16[256,576]{1,0:T(8,128)(2,1)S(1)} %pad_maximum_fusion.2.own_grads, bf16[256,576]{1,0:T(8,128)(2,1)S(1)} %collective-permute-done.25.other_grads, ...), custom_call_target="tpu_custom_call" | custom-call | bytes 7143424 | tf_op jit(solution)/shard_map/pallas_call | solution.py:156
  (81 shorter events, 15.9 us)
Async XLA Ops:
  0.6 11.9 %collective-permute-start.3 = (bf16[16,2048]{1,0:T(8,128)(2,1)}, bf16[16,2048]{1,0:T(8,128)(2,1)S(1)}, u32[]{:S(2)}, u32[]{:S(2)}) collective-permute-start(bf16[16,2048]{1,0:T(8,128)(2,1)} %tokens_hbm.1), channel_id=1, source_target_pairs={{0,12},{1,13},{2,14},{3,15},{4,0},{5,1},{6,2},{7,3},{8,4},{9,5},{1... | collective-permute-start | bytes 196616 | tf_op jit(solution)/shard_map/ppermute | solution.py:137
  5.7 6.8 %collective-permute-start.2 = (bf16[16,2048]{1,0:T(8,128)(2,1)}, bf16[16,2048]{1,0:T(8,128)(2,1)S(1)}, u32[]{:S(2)}, u32[]{:S(2)}) collective-permute-start(bf16[16,2048]{1,0:T(8,128)(2,1)} %tokens_hbm.1), channel_id=1, source_target_pairs={{0,8},{1,9},{2,10},{3,11},{4,12},{5,13},{6,14},{7,15},{8,0},{9,1},... | collective-permute-start | bytes 196616 | tf_op jit(solution)/shard_map/ppermute | solution.py:137
  5.7 6.8 %collective-permute-start.1 = (bf16[16,2048]{1,0:T(8,128)(2,1)}, bf16[16,2048]{1,0:T(8,128)(2,1)S(1)}, u32[]{:S(2)}, u32[]{:S(2)}) collective-permute-start(bf16[16,2048]{1,0:T(8,128)(2,1)} %tokens_hbm.1), channel_id=1, source_target_pairs={{0,4},{1,5},{2,6},{3,7},{4,8},{5,9},{6,10},{7,11},{8,12},{9,13},{1... | collective-permute-start | bytes 196616 | tf_op jit(solution)/shard_map/ppermute | solution.py:137
  10.6 12.2 %collective-permute-start.5 = (bf16[16,2064]{1,0:T(8,128)(2,1)S(1)}, bf16[16,2064]{1,0:T(8,128)(2,1)S(1)}, u32[]{:S(2)}, u32[]{:S(2)}) collective-permute-start(bf16[16,2064]{1,0:T(8,128)(2,1)S(1)} %get-tuple-element.31), channel_id=1, source_target_pairs={{0,8},{1,9},{2,10},{3,11},{4,12},{5,13},{6,14},{7,15},{8,0},{9,1},... | collective-permute-start | bytes 198152 | tf_op jit(solution)/shard_map/ppermute | solution.py:137
  12.6 21.0 %collective-permute-start.13 = (bf16[64,2048]{1,0:T(8,128)(2,1)S(1)}, bf16[64,2048]{1,0:T(8,128)(2,1)S(1)}, u32[]{:S(2)}, u32[]{:S(2)}) collective-permute-start(bf16[64,2048]{1,0:T(8,128)(2,1)S(1)} %pad_maximum_fusion.3), channel_id=1, source_target_pairs={{0,1},{1,0},{2,3},{3,2},{4,5},{5,4},{6,7},{7,6},{8,9},{9,8},{10,11... | collective-permute-start | bytes 786440 | tf_op jit(solution)/shard_map/ppermute | solution.py:143
  14.1 21.4 %collective-permute-start.15 = (bf16[64,2048]{1,0:T(8,128)(2,1)S(1)}, bf16[64,2048]{1,0:T(8,128)(2,1)S(1)}, u32[]{:S(2)}, u32[]{:S(2)}) collective-permute-start(bf16[64,2048]{1,0:T(8,128)(2,1)S(1)} %pad_maximum_fusion.3), channel_id=1, source_target_pairs={{0,2},{1,3},{2,0},{3,1},{4,6},{5,7},{6,4},{7,5},{8,10},{9,11},{10,... | collective-permute-start | bytes 786440 | tf_op jit(solution)/shard_map/ppermute | solution.py:143
  15.7 6.5 %collective-permute-start.4 = (bf16[16,2064]{1,0:T(8,128)(2,1)S(1)}, bf16[16,2064]{1,0:T(8,128)(2,1)S(1)}, u32[]{:S(2)}, u32[]{:S(2)}) collective-permute-start(bf16[16,2064]{1,0:T(8,128)(2,1)S(1)} %get-tuple-element.31), channel_id=1, source_target_pairs={{0,4},{1,5},{2,6},{3,7},{4,8},{5,9},{6,10},{7,11},{8,12},{9,13},{1... | collective-permute-start | bytes 198152 | tf_op jit(solution)/shard_map/ppermute | solution.py:137
  17.2 6.1 %collective-permute-start.6 = (bf16[16,2064]{1,0:T(8,128)(2,1)S(1)}, bf16[16,2064]{1,0:T(8,128)(2,1)S(1)}, u32[]{:S(2)}, u32[]{:S(2)}) collective-permute-start(bf16[16,2064]{1,0:T(8,128)(2,1)S(1)} %get-tuple-element.31), channel_id=1, source_target_pairs={{0,12},{1,13},{2,14},{3,15},{4,0},{5,1},{6,2},{7,3},{8,4},{9,5},{1... | collective-permute-start | bytes 198152 | tf_op jit(solution)/shard_map/ppermute | solution.py:137
  22.2 5.4 %collective-permute-start.7 = (bf16[32,2064]{1,0:T(8,128)(2,1)S(1)}, bf16[32,2064]{1,0:T(8,128)(2,1)S(1)}, u32[]{:S(2)}, u32[]{:S(2)}) collective-permute-start(bf16[32,2064]{1,0:T(8,128)(2,1)S(1)} %get-tuple-element.72), channel_id=1, source_target_pairs={{0,1},{1,0},{2,3},{3,2},{4,5},{5,4},{6,7},{7,6},{8,9},{9,8},{10,11... | collective-permute-start | bytes 396296 | tf_op jit(solution)/shard_map/ppermute | solution.py:143
  22.8 10.9 %collective-permute-start.9 = (bf16[32,2064]{1,0:T(8,128)(2,1)S(1)}, bf16[32,2064]{1,0:T(8,128)(2,1)S(1)}, u32[]{:S(2)}, u32[]{:S(2)}) collective-permute-start(bf16[32,2064]{1,0:T(8,128)(2,1)S(1)} %get-tuple-element.72), channel_id=1, source_target_pairs={{0,2},{1,3},{2,0},{3,1},{4,6},{5,7},{6,4},{7,5},{8,10},{9,11},{10,... | collective-permute-start | bytes 396296 | tf_op jit(solution)/shard_map/ppermute | solution.py:143
  23.4 5.7 %collective-permute-start.8 = (bf16[32,2064]{1,0:T(8,128)(2,1)S(1)}, bf16[32,2064]{1,0:T(8,128)(2,1)S(1)}, u32[]{:S(2)}, u32[]{:S(2)}) collective-permute-start(bf16[32,2064]{1,0:T(8,128)(2,1)S(1)} %get-tuple-element.68), channel_id=1, source_target_pairs={{0,1},{1,0},{2,3},{3,2},{4,5},{5,4},{6,7},{7,6},{8,9},{9,8},{10,11... | collective-permute-start | bytes 396296 | tf_op jit(solution)/shard_map/ppermute | solution.py:143
  27.6 5.1 %collective-permute-start.10 = (bf16[32,2064]{1,0:T(8,128)(2,1)S(1)}, bf16[32,2064]{1,0:T(8,128)(2,1)S(1)}, u32[]{:S(2)}, u32[]{:S(2)}) collective-permute-start(bf16[32,2064]{1,0:T(8,128)(2,1)S(1)} %get-tuple-element.68), channel_id=1, source_target_pairs={{0,2},{1,3},{2,0},{3,1},{4,6},{5,7},{6,4},{7,5},{8,10},{9,11},{10,... | collective-permute-start | bytes 396296 | tf_op jit(solution)/shard_map/ppermute | solution.py:143
  29.1 6.6 %collective-permute-start.11 = (bf16[32,2064]{1,0:T(8,128)(2,1)S(1)}, bf16[32,2064]{1,0:T(8,128)(2,1)S(1)}, u32[]{:S(2)}, u32[]{:S(2)}) collective-permute-start(bf16[32,2064]{1,0:T(8,128)(2,1)S(1)} %collective-permute-done.7), channel_id=1, source_target_pairs={{0,2},{1,3},{2,0},{3,1},{4,6},{5,7},{6,4},{7,5},{8,10},{9,11},{10,... | collective-permute-start | bytes 396296 | tf_op jit(solution)/shard_map/ppermute | solution.py:143
  32.7 5.1 %collective-permute-start.12 = (bf16[32,2064]{1,0:T(8,128)(2,1)S(1)}, bf16[32,2064]{1,0:T(8,128)(2,1)S(1)}, u32[]{:S(2)}, u32[]{:S(2)}) collective-permute-start(bf16[32,2064]{1,0:T(8,128)(2,1)S(1)} %collective-permute-done.10), channel_id=1, source_target_pairs={{0,1},{1,0},{2,3},{3,2},{4,5},{5,4},{6,7},{7,6},{8,9},{9,8},{10,11... | collective-permute-start | bytes 396296 | tf_op jit(solution)/shard_map/ppermute | solution.py:143
  33.6 7.7 %collective-permute-start.14 = (bf16[576,2048]{1,0:T(8,128)(2,1)S(1)}, bf16[576,2048]{1,0:T(8,128)(2,1)S(1)}, u32[]{:S(2)}, u32[]{:S(2)}) collective-permute-start(bf16[576,2048]{1,0:T(8,128)(2,1)S(1)} %pad_maximum_fusion.own_ref), channel_id=1, source_target_pairs={{0,16},{16,0},{1,17},{17,1},{2,18},{18,2},{3,19},{19,3},{4,20},{20... | collective-permute-start | bytes 7077896 | tf_op jit(solution)/shard_map/ppermute | solution.py:133
  33.7 6.0 %collective-permute-start.16 = (bf16[32,2048]{1,0:T(8,128)(2,1)S(1)}, bf16[32,2048]{1,0:T(8,128)(2,1)S(1)}, u32[]{:S(2)}, u32[]{:S(2)}) collective-permute-start(bf16[32,2048]{1,0:T(8,128)(2,1)S(1)} %slice.108), channel_id=1, source_target_pairs={{0,2},{1,3},{2,0},{3,1},{4,6},{5,7},{6,4},{7,5},{8,10},{9,11},{10,... | collective-permute-start | bytes 393224 | tf_op jit(solution)/shard_map/ppermute | solution.py:143
  35.5 5.7 %collective-permute-start.17 = (bf16[32,2048]{1,0:T(8,128)(2,1)S(1)}, bf16[32,2048]{1,0:T(8,128)(2,1)S(1)}, u32[]{:S(2)}, u32[]{:S(2)}) collective-permute-start(bf16[32,2048]{1,0:T(8,128)(2,1)S(1)} %slice.109), channel_id=1, source_target_pairs={{0,1},{1,0},{2,3},{3,2},{4,5},{5,4},{6,7},{7,6},{8,9},{9,8},{10,11... | collective-permute-start | bytes 393224 | tf_op jit(solution)/shard_map/ppermute | solution.py:143
  44.9 14.2 %collective-permute-start.26 = (bf16[256,2048]{1,0:T(8,128)(2,1)S(1)}, bf16[256,2048]{1,0:T(8,128)(2,1)S(1)}, u32[]{:S(2)}, u32[]{:S(2)}) collective-permute-start(bf16[256,2048]{1,0:T(8,128)(2,1)S(1)} %slice.107.upstream), channel_id=1, source_target_pairs={{0,16},{16,0},{1,17},{17,1},{2,18},{18,2},{3,19},{19,3},{4,20},{20... | collective-permute-start | bytes 3145736 | tf_op jit(solution)/shard_map/ppermute | solution.py:133
  45.5 6.4 %collective-permute-start.19 = (bf16[32,2048]{1,0:T(8,128)(2,1)S(1)}, bf16[32,2048]{1,0:T(8,128)(2,1)S(1)}, u32[]{:S(2)}, u32[]{:S(2)}) collective-permute-start(bf16[32,2048]{1,0:T(8,128)(2,1)S(1)} %get-tuple-element.56), channel_id=1, source_target_pairs={{0,2},{1,3},{2,0},{3,1},{4,6},{5,7},{6,4},{7,5},{8,10},{9,11},{10,... | collective-permute-start | bytes 393224 | tf_op jit(solution)/shard_map/ppermute | solution.py:143
  45.9 6.4 %collective-permute-start.20 = (bf16[32,2048]{1,0:T(8,128)(2,1)S(1)}, bf16[32,2048]{1,0:T(8,128)(2,1)S(1)}, u32[]{:S(2)}, u32[]{:S(2)}) collective-permute-start(bf16[32,2048]{1,0:T(8,128)(2,1)S(1)} %get-tuple-element.54), channel_id=1, source_target_pairs={{0,1},{1,0},{2,3},{3,2},{4,5},{5,4},{6,7},{7,6},{8,9},{9,8},{10,11... | collective-permute-start | bytes 393224 | tf_op jit(solution)/shard_map/ppermute | solution.py:143
  47.5 7.3 %collective-permute-start.22 = (bf16[32,2048]{1,0:T(8,128)(2,1)S(1)}, bf16[32,2048]{1,0:T(8,128)(2,1)S(1)}, u32[]{:S(2)}, u32[]{:S(2)}) collective-permute-start(bf16[32,2048]{1,0:T(8,128)(2,1)S(1)} %get-tuple-element.53), channel_id=1, source_target_pairs={{0,1},{1,0},{2,3},{3,2},{4,5},{5,4},{6,7},{7,6},{8,9},{9,8},{10,11... | collective-permute-start | bytes 393224 | tf_op jit(solution)/shard_map/ppermute | solution.py:143
  47.9 6.9 %collective-permute-start.23 = (bf16[32,2048]{1,0:T(8,128)(2,1)S(1)}, bf16[32,2048]{1,0:T(8,128)(2,1)S(1)}, u32[]{:S(2)}, u32[]{:S(2)}) collective-permute-start(bf16[32,2048]{1,0:T(8,128)(2,1)S(1)} %get-tuple-element.52), channel_id=1, source_target_pairs={{0,2},{1,3},{2,0},{3,1},{4,6},{5,7},{6,4},{7,5},{8,10},{9,11},{10,... | collective-permute-start | bytes 393224 | tf_op jit(solution)/shard_map/ppermute | solution.py:143
  59.2 8.0 %collective-permute-start.29 = (bf16[16,2048]{1,0:T(8,128)(2,1)S(1)}, bf16[16,2048]{1,0:T(8,128)(2,1)S(1)}, u32[]{:S(2)}, u32[]{:S(2)}) collective-permute-start(bf16[16,2048]{1,0:T(8,128)(2,1)S(1)} %get-tuple-element.60), channel_id=1, source_target_pairs={{0,4},{1,5},{2,6},{3,7},{4,8},{5,9},{6,10},{7,11},{8,12},{9,13},{1... | collective-permute-start | bytes 196616 | tf_op jit(solution)/shard_map/ppermute | solution.py:137
  60.0 7.1 %collective-permute-start.28 = (bf16[16,2048]{1,0:T(8,128)(2,1)S(1)}, bf16[16,2048]{1,0:T(8,128)(2,1)S(1)}, u32[]{:S(2)}, u32[]{:S(2)}) collective-permute-start(bf16[16,2048]{1,0:T(8,128)(2,1)S(1)} %get-tuple-element.61), channel_id=1, source_target_pairs={{0,8},{1,9},{2,10},{3,11},{4,12},{5,13},{6,14},{7,15},{8,0},{9,1},... | collective-permute-start | bytes 196616 | tf_op jit(solution)/shard_map/ppermute | solution.py:137
  (9 other events, 32.0 us)

commit v20 on v18

--- a/solution.py
+++ b/solution.py
@@ -263,8 +263,8 @@
     return [column, first, second, far_top, far_bottom]
 
 
-def return_inner(value, count):
-    own, first, second, far = jnp.split(value, 4, axis=0)
+def return_inner(near, far, count):
+    own, first, second = jnp.split(near, 3, axis=0)
     cut = own.shape[0] // 2
     top = swap_inner(far[:cut], count, 2)
     bottom = swap_inner(far[cut:], count, 1)
@@ -361,14 +361,18 @@
     gate_grad = (hidden_grad * up_pre * silu_slope).astype(jnp.bfloat16)
     up_grad = (hidden_grad * activated).astype(jnp.bfloat16)
     both_grad = jnp.concatenate([gate_grad, up_grad], axis=1)
-    partial_grad = jnp.dot(both_grad, gate_up, preferred_element_type=jnp.float32)
-    partial_grad = partial_grad.astype(jnp.bfloat16)
-    partial_grad, other_inputs = lax.optimization_barrier((partial_grad, other_inputs))
-    column_sum = return_inner(partial_grad, count)
+    cut = both_grad.shape[0] // inner * (inner - 1)
+    far = jnp.dot(both_grad[cut:], gate_up, preferred_element_type=jnp.float32)
+    far = far.astype(jnp.bfloat16)
+    near_grad, far = lax.optimization_barrier((both_grad[:cut], far))
+    near = jnp.dot(near_grad, gate_up, preferred_element_type=jnp.float32)
+    near = near.astype(jnp.bfloat16)
+    far, other_inputs = lax.optimization_barrier((far, other_inputs))
+    column_sum = return_inner(near, far, count)
     grads = (gate_grad, up_grad, hidden)
     own_grads = jnp.concatenate([grad[:, :half] for grad in grads], axis=1)
     sent_grads = jnp.concatenate([grad[:, half:] for grad in grads], axis=1)
-    sent_grads, upstream, _ = lax.optimization_barrier((sent_grads, upstream, partial_grad))
+    sent_grads, upstream, _ = lax.optimization_barrier((sent_grads, upstream, near))
     other_grads = swap(sent_grads)
     other_upstream = swap(upstream)
     column_sum, other_grads, other_upstream = lax.optimization_barrier(

time: 64.2 us -> 64.1 us (level)
    dot_general x1 -> x2, matrix products: 0.98 us -> 1.45 us  [the longest x1 0.79 us: dense_local(): near = jnp.dot(near_grad, gate_up, preferred_element_type=jnp.float32)]
  transfers between devices with their start and end apart: 28 -> 28, of which waited for: 12 -> 12; matrix products, arithmetic and copies ran while one was open for 9% -> 10% of each run, Pallas kernels for 7% -> 7%
where the time goes in v20:
time: 64.1 us; the launch traced here: 63.9 us
  starting transfers between devices  32.6 us (51%)
  waiting for transfers between devices  18.5 us (29%)
  Pallas kernels  4.58 us (7%)
  matrix products  3.27 us (5%)
  other arithmetic  3.13 us (5%)
  between operations  1.02 us (2%)
  local copies, waits for them, and re-layouts  0.72 us (1%)
    ppermute x14, starting transfers between devices, swap_inner(): lax.ppermute(value, 'expert', [(place, place ^ partner) for place in rang...  16.6 us
    ppermute x9, starting transfers between devices, shift_outer(): lax.ppermute(value, 'expert', [(place, (place + step * inner) % count) fo...  15.8 us
    ppermute x14, waiting for transfers between devices, swap_inner(): lax.ppermute(value, 'expert', [(place, place ^ partner) for place in rang...  13.8 us
    ppermute x9, waiting for transfers between devices, shift_outer(): lax.ppermute(value, 'expert', [(place, (place + step * inner) % count) fo...  4.73 us
    pallas_call x5, Pallas kernels, on_chip(): pl.pallas_call(body, out_shape=[jax.ShapeDtypeStruct(shape, dtype) for sh...  4.58 us
    concatenate x1, other arithmetic, dense_local(): own_weights = jnp.concatenate([w_gate[0], w_up[0], w_down[0]], axis=0)  1.93 us
  transfers between devices with their start and end apart: 28, of which 12 were waited for; matrix products, arithmetic and copies ran while one was open for 10% of the time, Pallas kernels for 7%

profile of v20, /device:TPU:0, one launch (start us, length us, event | category | flops | bytes accessed | tf_op | source)
XLA Modules:
  0.0 63.9 jit_solution(570025826976218676)
XLA Ops:
  0.6 5.1 %collective-permute-start.3 = (bf16[16,2048]{1,0:T(8,128)(2,1)}, bf16[16,2048]{1,0:T(8,128)(2,1)S(1)}, u32[]{:S(2)}, u32[]{:S(2)}) collective-permute-start(bf16[16,2048]{1,0:T(8,128)(2,1)} %tokens_hbm.1), channel_id=1, source_target_pairs={{0,12},{1,13},{2,14},{3,15},{4,0},{5,1},{6,2},{7,3},{8,4},{9,5},{1... | collective-permute-start | bytes 196616 | tf_op jit(solution)/shard_map/ppermute | solution.py:137
  6.7 1.6 %shard_map.111 = (bf16[32,16]{1,0:T(8,128)(2,1)}, bf16[16,2048]{1,0:T(8,128)(2,1)}, bf16[16,2048]{1,0:T(8,128)(2,1)}) custom-call(s32[8,16]{1,0:T(8,128)} %bitcast.17, bf16[8,16]{1,0:T(8,128)(2,1)} %bitcast.18, s32[1,16]{1,0:T(1,128)} %bitcast.19, bf16[16,2048]{1,0:T(8,128)(2,1)} %tokens_hbm.1, bf16[16,2048]{1,0:T(8,128)(2,1)} %cotangent_hbm.1), custom_call_target="tpu_custom_call" | custom-call | bytes 264000 | tf_op jit(solution)/shard_map/pallas_call | solution.py:156
  8.5 1.9 %pad_maximum_fusion.own_ref = bf16[576,2048]{1,0:T(8,128)(2,1)S(1)} fusion(bf16[192,2048]{1,0:T(8,128)(2,1)} %bitcast.14, bf16[192,2048]{1,0:T(8,128)(2,1)} %bitcast.15, bf16[192,2048]{1,0:T(8,128)(2,1)} %bitcast.16), kind=kLoop, calls=%fused_computation.1 | loop fusion | flops 7077888 | bytes 4718592 | tf_op jit(solution)/shard_map/concatenate | solution.py:338
  10.6 1.9 %collective-permute-start.5 = (bf16[16,2064]{1,0:T(8,128)(2,1)S(1)}, bf16[16,2064]{1,0:T(8,128)(2,1)S(1)}, u32[]{:S(2)}, u32[]{:S(2)}) collective-permute-start(bf16[16,2064]{1,0:T(8,128)(2,1)S(1)} %get-tuple-element.33), channel_id=1, source_target_pairs={{0,8},{1,9},{2,10},{3,11},{4,12},{5,13},{6,14},{7,15},{8,0},{9,1},... | collective-permute-start | bytes 198152 | tf_op jit(solution)/shard_map/ppermute | solution.py:137
  12.6 1.6 %collective-permute-start.11 = (bf16[64,2048]{1,0:T(8,128)(2,1)S(1)}, bf16[64,2048]{1,0:T(8,128)(2,1)S(1)}, u32[]{:S(2)}, u32[]{:S(2)}) collective-permute-start(bf16[64,2048]{1,0:T(8,128)(2,1)S(1)} %pad_maximum_fusion.3), channel_id=1, source_target_pairs={{0,1},{1,0},{2,3},{3,2},{4,5},{5,4},{6,7},{7,6},{8,9},{9,8},{10,11... | collective-permute-start | bytes 786440 | tf_op jit(solution)/shard_map/ppermute | solution.py:143
  14.1 1.5 %collective-permute-start.13 = (bf16[64,2048]{1,0:T(8,128)(2,1)S(1)}, bf16[64,2048]{1,0:T(8,128)(2,1)S(1)}, u32[]{:S(2)}, u32[]{:S(2)}) collective-permute-start(bf16[64,2048]{1,0:T(8,128)(2,1)S(1)} %pad_maximum_fusion.3), channel_id=1, source_target_pairs={{0,2},{1,3},{2,0},{3,1},{4,6},{5,7},{6,4},{7,5},{8,10},{9,11},{10,... | collective-permute-start | bytes 786440 | tf_op jit(solution)/shard_map/ppermute | solution.py:143
  15.7 1.5 %collective-permute-start.4 = (bf16[16,2064]{1,0:T(8,128)(2,1)S(1)}, bf16[16,2064]{1,0:T(8,128)(2,1)S(1)}, u32[]{:S(2)}, u32[]{:S(2)}) collective-permute-start(bf16[16,2064]{1,0:T(8,128)(2,1)S(1)} %get-tuple-element.33), channel_id=1, source_target_pairs={{0,4},{1,5},{2,6},{3,7},{4,8},{5,9},{6,10},{7,11},{8,12},{9,13},{1... | collective-permute-start | bytes 198152 | tf_op jit(solution)/shard_map/ppermute | solution.py:137
  17.1 2.4 %collective-permute-start.6 = (bf16[16,2064]{1,0:T(8,128)(2,1)S(1)}, bf16[16,2064]{1,0:T(8,128)(2,1)S(1)}, u32[]{:S(2)}, u32[]{:S(2)}) collective-permute-start(bf16[16,2064]{1,0:T(8,128)(2,1)S(1)} %get-tuple-element.33), channel_id=1, source_target_pairs={{0,12},{1,13},{2,14},{3,15},{4,0},{5,1},{6,2},{7,3},{8,4},{9,5},{1... | collective-permute-start | bytes 198152 | tf_op jit(solution)/shard_map/ppermute | solution.py:137
  19.6 2.6 %collective-permute-done.4 = bf16[16,2064]{1,0:T(8,128)(2,1)S(1)} collective-permute-done((bf16[16,2064]{1,0:T(8,128)(2,1)S(1)}, bf16[16,2064]{1,0:T(8,128)(2,1)S(1)}, u32[]{:S(2)}, u32[]{:S(2)}) %collective-permute-start.4) | collective-permute-done | bytes 66080 | tf_op jit(solution)/shard_map/ppermute | solution.py:137
  23.4 1.6 %collective-permute-start.14 = (bf16[32,2048]{1,0:T(8,128)(2,1)S(1)}, bf16[32,2048]{1,0:T(8,128)(2,1)S(1)}, u32[]{:S(2)}, u32[]{:S(2)}) collective-permute-start(bf16[32,2048]{1,0:T(8,128)(2,1)S(1)} %slice.120), channel_id=1, source_target_pairs={{0,2},{1,3},{2,0},{3,1},{4,6},{5,7},{6,4},{7,5},{8,10},{9,11},{10,... | collective-permute-start | bytes 393224 | tf_op jit(solution)/shard_map/ppermute | solution.py:143
  25.0 1.6 %collective-permute-start.15 = (bf16[32,2048]{1,0:T(8,128)(2,1)S(1)}, bf16[32,2048]{1,0:T(8,128)(2,1)S(1)}, u32[]{:S(2)}, u32[]{:S(2)}) collective-permute-start(bf16[32,2048]{1,0:T(8,128)(2,1)S(1)} %slice.121), channel_id=1, source_target_pairs={{0,1},{1,0},{2,3},{3,2},{4,5},{5,4},{6,7},{7,6},{8,9},{9,8},{10,11... | collective-permute-start | bytes 393224 | tf_op jit(solution)/shard_map/ppermute | solution.py:143
  26.6 4.8 %collective-permute-done.7 = bf16[64,2064]{1,0:T(8,128)(2,1)S(1)} collective-permute-done((bf16[64,2064]{1,0:T(8,128)(2,1)S(1)}, bf16[64,2064]{1,0:T(8,128)(2,1)S(1)}, u32[]{:S(2)}, u32[]{:S(2)}) %collective-permute-start.7) | collective-permute-done | bytes 264224 | tf_op jit(solution)/shard_map/ppermute | solution.py:143
  32.2 1.8 %collective-permute-start.10 = (bf16[32,2064]{1,0:T(8,128)(2,1)S(1)}, bf16[32,2064]{1,0:T(8,128)(2,1)S(1)}, u32[]{:S(2)}, u32[]{:S(2)}) collective-permute-start(bf16[32,2064]{1,0:T(8,128)(2,1)S(1)} %slice.117), channel_id=1, source_target_pairs={{0,1},{1,0},{2,3},{3,2},{4,5},{5,4},{6,7},{7,6},{8,9},{9,8},{10,11... | collective-permute-start | bytes 396296 | tf_op jit(solution)/shard_map/ppermute | solution.py:143
  34.2 2.3 %collective-permute-done.9 = bf16[32,2064]{1,0:T(8,128)(2,1)S(1)} collective-permute-done((bf16[32,2064]{1,0:T(8,128)(2,1)S(1)}, bf16[32,2064]{1,0:T(8,128)(2,1)S(1)}, u32[]{:S(2)}, u32[]{:S(2)}) %collective-permute-start.9) | collective-permute-done | bytes 132128 | tf_op jit(solution)/shard_map/ppermute | solution.py:143
  37.9 1.0 %fusion.11 = f32[256,768]{1,0:T(8,128)S(1)} fusion(bf16[256,2048]{1,0:T(8,128)(2,1)S(1)} %constant_dynamic-update-slice_fusion.12.rows, bf16[768,2048]{1,0:T(8,128)(2,1)S(1)} %get-tuple-element.39), kind=kOutput, calls=%fused_computation.46 | convolution fusion | flops 805306368 | bytes 4980736 | tf_op jit(solution)/shard_map/dot_general | solution.py:354
  41.4 1.4 %collective-permute-start.17 = (bf16[32,2048]{1,0:T(8,128)(2,1)S(1)}, bf16[32,2048]{1,0:T(8,128)(2,1)S(1)}, u32[]{:S(2)}, u32[]{:S(2)}) collective-permute-start(bf16[32,2048]{1,0:T(8,128)(2,1)S(1)} %get-tuple-element.65), channel_id=1, source_target_pairs={{0,2},{1,3},{2,0},{3,1},{4,6},{5,7},{6,4},{7,5},{8,10},{9,11},{10,... | collective-permute-start | bytes 393224 | tf_op jit(solution)/shard_map/ppermute | solution.py:143
  44.1 1.1 %collective-permute-start.20 = (bf16[32,2048]{1,0:T(8,128)(2,1)S(1)}, bf16[32,2048]{1,0:T(8,128)(2,1)S(1)}, u32[]{:S(2)}, u32[]{:S(2)}) collective-permute-start(bf16[32,2048]{1,0:T(8,128)(2,1)S(1)} %get-tuple-element.58), channel_id=1, source_target_pairs={{0,1},{1,0},{2,3},{3,2},{4,5},{5,4},{6,7},{7,6},{8,9},{9,8},{10,11... | collective-permute-start | bytes 393224 | tf_op jit(solution)/shard_map/ppermute | solution.py:143
  46.5 1.8 %collective-permute-done.18.other_right_ref = bf16[32,2048]{1,0:T(8,128)(2,1)S(1)} collective-permute-done((bf16[32,2048]{1,0:T(8,128)(2,1)S(1)}, bf16[32,2048]{1,0:T(8,128)(2,1)S(1)}, u32[]{:S(2)}, u32[]{:S(2)}) %collective-permute-start.18) | collective-permute-done | bytes 131104 | tf_op jit(solution)/shard_map/ppermute | solution.py:143
  49.3 2.3 %collective-permute-start.22 = (bf16[32,2048]{1,0:T(8,128)(2,1)S(1)}, bf16[32,2048]{1,0:T(8,128)(2,1)S(1)}, u32[]{:S(2)}, u32[]{:S(2)}) collective-permute-start(bf16[32,2048]{1,0:T(8,128)(2,1)S(1)} %get-tuple-element.44), channel_id=1, source_target_pairs={{0,2},{1,3},{2,0},{3,1},{4,6},{5,7},{6,4},{7,5},{8,10},{9,11},{10,... | collective-permute-start | bytes 393224 | tf_op jit(solution)/shard_map/ppermute | solution.py:143
  51.6 1.8 %collective-permute-done.19 = bf16[32,2048]{1,0:T(8,128)(2,1)S(1)} collective-permute-done((bf16[32,2048]{1,0:T(8,128)(2,1)S(1)}, bf16[32,2048]{1,0:T(8,128)(2,1)S(1)}, u32[]{:S(2)}, u32[]{:S(2)}) %collective-permute-start.19) | collective-permute-done | bytes 131104 | tf_op jit(solution)/shard_map/ppermute | solution.py:143
  53.4 1.1 %collective-permute-done.22 = bf16[32,2048]{1,0:T(8,128)(2,1)S(1)} collective-permute-done((bf16[32,2048]{1,0:T(8,128)(2,1)S(1)}, bf16[32,2048]{1,0:T(8,128)(2,1)S(1)}, u32[]{:S(2)}, u32[]{:S(2)}) %collective-permute-start.22) | collective-permute-done | bytes 131104 | tf_op jit(solution)/shard_map/ppermute | solution.py:143
  55.0 3.5 %collective-permute-start.26 = (bf16[16,2048]{1,0:T(8,128)(2,1)S(1)}, bf16[16,2048]{1,0:T(8,128)(2,1)S(1)}, u32[]{:S(2)}, u32[]{:S(2)}) collective-permute-start(bf16[16,2048]{1,0:T(8,128)(2,1)S(1)} %get-tuple-element.63), channel_id=1, source_target_pairs={{0,8},{1,9},{2,10},{3,11},{4,12},{5,13},{6,14},{7,15},{8,0},{9,1},... | collective-permute-start | bytes 196616 | tf_op jit(solution)/shard_map/ppermute | solution.py:137
  58.7 2.5 %shard_map.115 = (bf16[1,192,2048]{2,1,0:T(8,128)(2,1)}, bf16[1,192,2048]{2,1,0:T(8,128)(2,1)}, bf16[1,192,2048]{2,1,0:T(8,128)(2,1)}) custom-call(bf16[256,576]{1,0:T(8,128)(2,1)S(1)} %pad_maximum_fusion.2.own_grads, bf16[256,576]{1,0:T(8,128)(2,1)S(1)} %collective-permute-done.23.other_grads, ...), custom_call_target="tpu_custom_call" | custom-call | bytes 7143424 | tf_op jit(solution)/shard_map/pallas_call | solution.py:156
  61.2 1.6 %collective-permute-done.26 = bf16[16,2048]{1,0:T(8,128)(2,1)S(1)} collective-permute-done((bf16[16,2048]{1,0:T(8,128)(2,1)S(1)}, bf16[16,2048]{1,0:T(8,128)(2,1)S(1)}, u32[]{:S(2)}, u32[]{:S(2)}) %collective-permute-start.26) | collective-permute-done | bytes 65568 | tf_op jit(solution)/shard_map/ppermute | solution.py:137
  (80 shorter events, 12.6 us)
Async XLA Ops:
  0.6 11.9 %collective-permute-start.3 = (bf16[16,2048]{1,0:T(8,128)(2,1)}, bf16[16,2048]{1,0:T(8,128)(2,1)S(1)}, u32[]{:S(2)}, u32[]{:S(2)}) collective-permute-start(bf16[16,2048]{1,0:T(8,128)(2,1)} %tokens_hbm.1), channel_id=1, source_target_pairs={{0,12},{1,13},{2,14},{3,15},{4,0},{5,1},{6,2},{7,3},{8,4},{9,5},{1... | collective-permute-start | bytes 196616 | tf_op jit(solution)/shard_map/ppermute | solution.py:137
  5.7 6.8 %collective-permute-start.2 = (bf16[16,2048]{1,0:T(8,128)(2,1)}, bf16[16,2048]{1,0:T(8,128)(2,1)S(1)}, u32[]{:S(2)}, u32[]{:S(2)}) collective-permute-start(bf16[16,2048]{1,0:T(8,128)(2,1)} %tokens_hbm.1), channel_id=1, source_target_pairs={{0,8},{1,9},{2,10},{3,11},{4,12},{5,13},{6,14},{7,15},{8,0},{9,1},... | collective-permute-start | bytes 196616 | tf_op jit(solution)/shard_map/ppermute | solution.py:137
  5.7 6.8 %collective-permute-start.1 = (bf16[16,2048]{1,0:T(8,128)(2,1)}, bf16[16,2048]{1,0:T(8,128)(2,1)S(1)}, u32[]{:S(2)}, u32[]{:S(2)}) collective-permute-start(bf16[16,2048]{1,0:T(8,128)(2,1)} %tokens_hbm.1), channel_id=1, source_target_pairs={{0,4},{1,5},{2,6},{3,7},{4,8},{5,9},{6,10},{7,11},{8,12},{9,13},{1... | collective-permute-start | bytes 196616 | tf_op jit(solution)/shard_map/ppermute | solution.py:137
  10.6 11.6 %collective-permute-start.5 = (bf16[16,2064]{1,0:T(8,128)(2,1)S(1)}, bf16[16,2064]{1,0:T(8,128)(2,1)S(1)}, u32[]{:S(2)}, u32[]{:S(2)}) collective-permute-start(bf16[16,2064]{1,0:T(8,128)(2,1)S(1)} %get-tuple-element.33), channel_id=1, source_target_pairs={{0,8},{1,9},{2,10},{3,11},{4,12},{5,13},{6,14},{7,15},{8,0},{9,1},... | collective-permute-start | bytes 198152 | tf_op jit(solution)/shard_map/ppermute | solution.py:137
  12.6 10.8 %collective-permute-start.11 = (bf16[64,2048]{1,0:T(8,128)(2,1)S(1)}, bf16[64,2048]{1,0:T(8,128)(2,1)S(1)}, u32[]{:S(2)}, u32[]{:S(2)}) collective-permute-start(bf16[64,2048]{1,0:T(8,128)(2,1)S(1)} %pad_maximum_fusion.3), channel_id=1, source_target_pairs={{0,1},{1,0},{2,3},{3,2},{4,5},{5,4},{6,7},{7,6},{8,9},{9,8},{10,11... | collective-permute-start | bytes 786440 | tf_op jit(solution)/shard_map/ppermute | solution.py:143
  14.1 10.8 %collective-permute-start.13 = (bf16[64,2048]{1,0:T(8,128)(2,1)S(1)}, bf16[64,2048]{1,0:T(8,128)(2,1)S(1)}, u32[]{:S(2)}, u32[]{:S(2)}) collective-permute-start(bf16[64,2048]{1,0:T(8,128)(2,1)S(1)} %pad_maximum_fusion.3), channel_id=1, source_target_pairs={{0,2},{1,3},{2,0},{3,1},{4,6},{5,7},{6,4},{7,5},{8,10},{9,11},{10,... | collective-permute-start | bytes 786440 | tf_op jit(solution)/shard_map/ppermute | solution.py:143
  15.7 6.5 %collective-permute-start.4 = (bf16[16,2064]{1,0:T(8,128)(2,1)S(1)}, bf16[16,2064]{1,0:T(8,128)(2,1)S(1)}, u32[]{:S(2)}, u32[]{:S(2)}) collective-permute-start(bf16[16,2064]{1,0:T(8,128)(2,1)S(1)} %get-tuple-element.33), channel_id=1, source_target_pairs={{0,4},{1,5},{2,6},{3,7},{4,8},{5,9},{6,10},{7,11},{8,12},{9,13},{1... | collective-permute-start | bytes 198152 | tf_op jit(solution)/shard_map/ppermute | solution.py:137
  17.1 5.1 %collective-permute-start.6 = (bf16[16,2064]{1,0:T(8,128)(2,1)S(1)}, bf16[16,2064]{1,0:T(8,128)(2,1)S(1)}, u32[]{:S(2)}, u32[]{:S(2)}) collective-permute-start(bf16[16,2064]{1,0:T(8,128)(2,1)S(1)} %get-tuple-element.33), channel_id=1, source_target_pairs={{0,12},{1,13},{2,14},{3,15},{4,0},{5,1},{6,2},{7,3},{8,4},{9,5},{1... | collective-permute-start | bytes 198152 | tf_op jit(solution)/shard_map/ppermute | solution.py:137
  22.3 9.1 %collective-permute-start.7 = (bf16[64,2064]{1,0:T(8,128)(2,1)S(1)}, bf16[64,2064]{1,0:T(8,128)(2,1)S(1)}, u32[]{:S(2)}, u32[]{:S(2)}) collective-permute-start(bf16[64,2064]{1,0:T(8,128)(2,1)S(1)} %get-tuple-element.72), channel_id=1, source_target_pairs={{0,1},{1,0},{2,3},{3,2},{4,5},{5,4},{6,7},{7,6},{8,9},{9,8},{10,11... | collective-permute-start | bytes 792584 | tf_op jit(solution)/shard_map/ppermute | solution.py:143
  22.9 9.3 %collective-permute-start.8 = (bf16[64,2064]{1,0:T(8,128)(2,1)S(1)}, bf16[64,2064]{1,0:T(8,128)(2,1)S(1)}, u32[]{:S(2)}, u32[]{:S(2)}) collective-permute-start(bf16[64,2064]{1,0:T(8,128)(2,1)S(1)} %get-tuple-element.72), channel_id=1, source_target_pairs={{0,2},{1,3},{2,0},{3,1},{4,6},{5,7},{6,4},{7,5},{8,10},{9,11},{10,... | collective-permute-start | bytes 792584 | tf_op jit(solution)/shard_map/ppermute | solution.py:143
  23.4 10.7 %collective-permute-start.14 = (bf16[32,2048]{1,0:T(8,128)(2,1)S(1)}, bf16[32,2048]{1,0:T(8,128)(2,1)S(1)}, u32[]{:S(2)}, u32[]{:S(2)}) collective-permute-start(bf16[32,2048]{1,0:T(8,128)(2,1)S(1)} %slice.120), channel_id=1, source_target_pairs={{0,2},{1,3},{2,0},{3,1},{4,6},{5,7},{6,4},{7,5},{8,10},{9,11},{10,... | collective-permute-start | bytes 393224 | tf_op jit(solution)/shard_map/ppermute | solution.py:143
  25.0 9.1 %collective-permute-start.15 = (bf16[32,2048]{1,0:T(8,128)(2,1)S(1)}, bf16[32,2048]{1,0:T(8,128)(2,1)S(1)}, u32[]{:S(2)}, u32[]{:S(2)}) collective-permute-start(bf16[32,2048]{1,0:T(8,128)(2,1)S(1)} %slice.121), channel_id=1, source_target_pairs={{0,1},{1,0},{2,3},{3,2},{4,5},{5,4},{6,7},{7,6},{8,9},{9,8},{10,11... | collective-permute-start | bytes 393224 | tf_op jit(solution)/shard_map/ppermute | solution.py:143
  26.6 11.0 %collective-permute-start.12 = (bf16[576,2048]{1,0:T(8,128)(2,1)S(1)}, bf16[576,2048]{1,0:T(8,128)(2,1)S(1)}, u32[]{:S(2)}, u32[]{:S(2)}) collective-permute-start(bf16[576,2048]{1,0:T(8,128)(2,1)S(1)} %pad_maximum_fusion.own_ref), channel_id=1, source_target_pairs={{0,16},{16,0},{1,17},{17,1},{2,18},{18,2},{3,19},{19,3},{4,20},{20... | collective-permute-start | bytes 7077896 | tf_op jit(solution)/shard_map/ppermute | solution.py:133
  31.4 5.1 %collective-permute-start.9 = (bf16[32,2064]{1,0:T(8,128)(2,1)S(1)}, bf16[32,2064]{1,0:T(8,128)(2,1)S(1)}, u32[]{:S(2)}, u32[]{:S(2)}) collective-permute-start(bf16[32,2064]{1,0:T(8,128)(2,1)S(1)} %slice.116), channel_id=1, source_target_pairs={{0,2},{1,3},{2,0},{3,1},{4,6},{5,7},{6,4},{7,5},{8,10},{9,11},{10,... | collective-permute-start | bytes 396296 | tf_op jit(solution)/shard_map/ppermute | solution.py:143
  32.2 5.1 %collective-permute-start.10 = (bf16[32,2064]{1,0:T(8,128)(2,1)S(1)}, bf16[32,2064]{1,0:T(8,128)(2,1)S(1)}, u32[]{:S(2)}, u32[]{:S(2)}) collective-permute-start(bf16[32,2064]{1,0:T(8,128)(2,1)S(1)} %slice.117), channel_id=1, source_target_pairs={{0,1},{1,0},{2,3},{3,2},{4,5},{5,4},{6,7},{7,6},{8,9},{9,8},{10,11... | collective-permute-start | bytes 396296 | tf_op jit(solution)/shard_map/ppermute | solution.py:143
  34.2 7.2 %collective-permute-start.16 = (bf16[256,2048]{1,0:T(8,128)(2,1)S(1)}, bf16[256,2048]{1,0:T(8,128)(2,1)S(1)}, u32[]{:S(2)}, u32[]{:S(2)}) collective-permute-start(bf16[256,2048]{1,0:T(8,128)(2,1)S(1)} %constant_dynamic-update-slice_fusion.12.rows), channel_id=1, source_target_pairs={{0,16},{16,0},{1,17},{17,1},{2,18},{18,2},{3,19},{19,3},{4,20},{20... | collective-permute-start | bytes 3145736 | tf_op jit(solution)/shard_map/ppermute | solution.py:133
  42.8 5.5 %collective-permute-start.18 = (bf16[32,2048]{1,0:T(8,128)(2,1)S(1)}, bf16[32,2048]{1,0:T(8,128)(2,1)S(1)}, u32[]{:S(2)}, u32[]{:S(2)}) collective-permute-start(bf16[32,2048]{1,0:T(8,128)(2,1)S(1)} %get-tuple-element.64), channel_id=1, source_target_pairs={{0,1},{1,0},{2,3},{3,2},{4,5},{5,4},{6,7},{7,6},{8,9},{9,8},{10,11... | collective-permute-start | bytes 393224 | tf_op jit(solution)/shard_map/ppermute | solution.py:143
  44.0 10.6 %collective-permute-start.24 = (bf16[256,2048]{1,0:T(8,128)(2,1)S(1)}, bf16[256,2048]{1,0:T(8,128)(2,1)S(1)}, u32[]{:S(2)}, u32[]{:S(2)}) collective-permute-start(bf16[256,2048]{1,0:T(8,128)(2,1)S(1)} %slice.119.upstream), channel_id=1, source_target_pairs={{0,16},{16,0},{1,17},{17,1},{2,18},{18,2},{3,19},{19,3},{4,20},{20... | collective-permute-start | bytes 3145736 | tf_op jit(solution)/shard_map/ppermute | solution.py:133
  44.1 7.4 %collective-permute-start.20 = (bf16[32,2048]{1,0:T(8,128)(2,1)S(1)}, bf16[32,2048]{1,0:T(8,128)(2,1)S(1)}, u32[]{:S(2)}, u32[]{:S(2)}) collective-permute-start(bf16[32,2048]{1,0:T(8,128)(2,1)S(1)} %get-tuple-element.58), channel_id=1, source_target_pairs={{0,1},{1,0},{2,3},{3,2},{4,5},{5,4},{6,7},{7,6},{8,9},{9,8},{10,11... | collective-permute-start | bytes 393224 | tf_op jit(solution)/shard_map/ppermute | solution.py:143
  45.3 6.3 %collective-permute-start.21 = (bf16[32,2048]{1,0:T(8,128)(2,1)S(1)}, bf16[32,2048]{1,0:T(8,128)(2,1)S(1)}, u32[]{:S(2)}, u32[]{:S(2)}) collective-permute-start(bf16[32,2048]{1,0:T(8,128)(2,1)S(1)} %get-tuple-element.57), channel_id=1, source_target_pairs={{0,2},{1,3},{2,0},{3,1},{4,6},{5,7},{6,4},{7,5},{8,10},{9,11},{10,... | collective-permute-start | bytes 393224 | tf_op jit(solution)/shard_map/ppermute | solution.py:143
  48.4 5.0 %collective-permute-start.19 = (bf16[32,2048]{1,0:T(8,128)(2,1)S(1)}, bf16[32,2048]{1,0:T(8,128)(2,1)S(1)}, u32[]{:S(2)}, u32[]{:S(2)}) collective-permute-start(bf16[32,2048]{1,0:T(8,128)(2,1)S(1)} %get-tuple-element.43), channel_id=1, source_target_pairs={{0,1},{1,0},{2,3},{3,2},{4,5},{5,4},{6,7},{7,6},{8,9},{9,8},{10,11... | collective-permute-start | bytes 393224 | tf_op jit(solution)/shard_map/ppermute | solution.py:143
  49.3 5.3 %collective-permute-start.22 = (bf16[32,2048]{1,0:T(8,128)(2,1)S(1)}, bf16[32,2048]{1,0:T(8,128)(2,1)S(1)}, u32[]{:S(2)}, u32[]{:S(2)}) collective-permute-start(bf16[32,2048]{1,0:T(8,128)(2,1)S(1)} %get-tuple-element.44), channel_id=1, source_target_pairs={{0,2},{1,3},{2,0},{3,1},{4,6},{5,7},{6,4},{7,5},{8,10},{9,11},{10,... | collective-permute-start | bytes 393224 | tf_op jit(solution)/shard_map/ppermute | solution.py:143
  54.7 6.5 %collective-permute-start.27 = (bf16[16,2048]{1,0:T(8,128)(2,1)S(1)}, bf16[16,2048]{1,0:T(8,128)(2,1)S(1)}, u32[]{:S(2)}, u32[]{:S(2)}) collective-permute-start(bf16[16,2048]{1,0:T(8,128)(2,1)S(1)} %get-tuple-element.62), channel_id=1, source_target_pairs={{0,4},{1,5},{2,6},{3,7},{4,8},{5,9},{6,10},{7,11},{8,12},{9,13},{1... | collective-permute-start | bytes 196616 | tf_op jit(solution)/shard_map/ppermute | solution.py:137
  55.0 7.7 %collective-permute-start.26 = (bf16[16,2048]{1,0:T(8,128)(2,1)S(1)}, bf16[16,2048]{1,0:T(8,128)(2,1)S(1)}, u32[]{:S(2)}, u32[]{:S(2)}) collective-permute-start(bf16[16,2048]{1,0:T(8,128)(2,1)S(1)} %get-tuple-element.63), channel_id=1, source_target_pairs={{0,8},{1,9},{2,10},{3,11},{4,12},{5,13},{6,14},{7,15},{8,0},{9,1},... | collective-permute-start | bytes 196616 | tf_op jit(solution)/shard_map/ppermute | solution.py:137
  (7 other events, 22.8 us)

commit v21 on v20

--- a/solution.py
+++ b/solution.py
@@ -286,7 +286,7 @@
     blocks = value.reshape(outer, -1, value.shape[-1])
     rounded = blocks.astype(jnp.bfloat16)
     total = blocks[0]
-    for step in range(1, outer):
+    for step in sorted(range(1, outer), key=lambda step: step != outer // 2):
         total = total + shift_outer(rounded[step], count, inner, -step).astype(jnp.float32)
     return total.astype(jnp.bfloat16)
 

time: 64.1 us -> 64.7 us (level)
  waiting for transfers between devices: 18.5 us -> 19.2 us
  transfers between devices with their start and end apart: 28 -> 28, of which waited for: 12 -> 11; matrix products, arithmetic and copies ran while one was open for 10% -> 10% of each run, Pallas kernels for 7% -> 7%
where the time goes in v21:
time: 64.7 us; the launch traced here: 64.5 us
  starting transfers between devices  32.6 us (50%)
  waiting for transfers between devices  19.2 us (30%)
  Pallas kernels  4.57 us (7%)
  matrix products  3.27 us (5%)
  other arithmetic  3.13 us (5%)
  between operations  1.02 us (2%)
  local copies, waits for them, and re-layouts  0.72 us (1%)
    ppermute x14, starting transfers between devices, swap_inner(): lax.ppermute(value, 'expert', [(place, place ^ partner) for place in rang...  16.6 us
    ppermute x9, starting transfers between devices, shift_outer(): lax.ppermute(value, 'expert', [(place, (place + step * inner) % count) fo...  15.8 us
    ppermute x14, waiting for transfers between devices, swap_inner(): lax.ppermute(value, 'expert', [(place, place ^ partner) for place in rang...  13.8 us
    ppermute x9, waiting for transfers between devices, shift_outer(): lax.ppermute(value, 'expert', [(place, (place + step * inner) % count) fo...  5.33 us
    pallas_call x5, Pallas kernels, on_chip(): pl.pallas_call(body, out_shape=[jax.ShapeDtypeStruct(shape, dtype) for sh...  4.57 us
    concatenate x1, other arithmetic, dense_local(): own_weights = jnp.concatenate([w_gate[0], w_up[0], w_down[0]], axis=0)  1.93 us
  transfers between devices with their start and end apart: 28, of which 11 were waited for; matrix products, arithmetic and copies ran while one was open for 10% of the time, Pallas kernels for 7%

profile of v21, /device:TPU:0, one launch (start us, length us, event | category | flops | bytes accessed | tf_op | source)
XLA Modules:
  0.0 64.5 jit_solution(13354087019118157670)
XLA Ops:
  0.6 5.1 %collective-permute-start.3 = (bf16[16,2048]{1,0:T(8,128)(2,1)}, bf16[16,2048]{1,0:T(8,128)(2,1)S(1)}, u32[]{:S(2)}, u32[]{:S(2)}) collective-permute-start(bf16[16,2048]{1,0:T(8,128)(2,1)} %tokens_hbm.1), channel_id=1, source_target_pairs={{0,12},{1,13},{2,14},{3,15},{4,0},{5,1},{6,2},{7,3},{8,4},{9,5},{1... | collective-permute-start | bytes 196616 | tf_op jit(solution)/shard_map/ppermute | solution.py:137
  6.7 1.6 %shard_map.111 = (bf16[32,16]{1,0:T(8,128)(2,1)}, bf16[16,2048]{1,0:T(8,128)(2,1)}, bf16[16,2048]{1,0:T(8,128)(2,1)}) custom-call(s32[8,16]{1,0:T(8,128)} %bitcast.17, bf16[8,16]{1,0:T(8,128)(2,1)} %bitcast.18, s32[1,16]{1,0:T(1,128)} %bitcast.19, bf16[16,2048]{1,0:T(8,128)(2,1)} %tokens_hbm.1, bf16[16,2048]{1,0:T(8,128)(2,1)} %cotangent_hbm.1), custom_call_target="tpu_custom_call" | custom-call | bytes 264000 | tf_op jit(solution)/shard_map/pallas_call | solution.py:156
  8.5 1.9 %pad_maximum_fusion.own_ref = bf16[576,2048]{1,0:T(8,128)(2,1)S(1)} fusion(bf16[192,2048]{1,0:T(8,128)(2,1)} %bitcast.14, bf16[192,2048]{1,0:T(8,128)(2,1)} %bitcast.15, bf16[192,2048]{1,0:T(8,128)(2,1)} %bitcast.16), kind=kLoop, calls=%fused_computation.1 | loop fusion | flops 7077888 | bytes 4718592 | tf_op jit(solution)/shard_map/concatenate | solution.py:338
  10.6 1.9 %collective-permute-start.5 = (bf16[16,2064]{1,0:T(8,128)(2,1)S(1)}, bf16[16,2064]{1,0:T(8,128)(2,1)S(1)}, u32[]{:S(2)}, u32[]{:S(2)}) collective-permute-start(bf16[16,2064]{1,0:T(8,128)(2,1)S(1)} %get-tuple-element.33), channel_id=1, source_target_pairs={{0,8},{1,9},{2,10},{3,11},{4,12},{5,13},{6,14},{7,15},{8,0},{9,1},... | collective-permute-start | bytes 198152 | tf_op jit(solution)/shard_map/ppermute | solution.py:137
  12.6 1.6 %collective-permute-start.11 = (bf16[64,2048]{1,0:T(8,128)(2,1)S(1)}, bf16[64,2048]{1,0:T(8,128)(2,1)S(1)}, u32[]{:S(2)}, u32[]{:S(2)}) collective-permute-start(bf16[64,2048]{1,0:T(8,128)(2,1)S(1)} %pad_maximum_fusion.3), channel_id=1, source_target_pairs={{0,1},{1,0},{2,3},{3,2},{4,5},{5,4},{6,7},{7,6},{8,9},{9,8},{10,11... | collective-permute-start | bytes 786440 | tf_op jit(solution)/shard_map/ppermute | solution.py:143
  14.1 1.5 %collective-permute-start.13 = (bf16[64,2048]{1,0:T(8,128)(2,1)S(1)}, bf16[64,2048]{1,0:T(8,128)(2,1)S(1)}, u32[]{:S(2)}, u32[]{:S(2)}) collective-permute-start(bf16[64,2048]{1,0:T(8,128)(2,1)S(1)} %pad_maximum_fusion.3), channel_id=1, source_target_pairs={{0,2},{1,3},{2,0},{3,1},{4,6},{5,7},{6,4},{7,5},{8,10},{9,11},{10,... | collective-permute-start | bytes 786440 | tf_op jit(solution)/shard_map/ppermute | solution.py:143
  15.7 1.5 %collective-permute-start.4 = (bf16[16,2064]{1,0:T(8,128)(2,1)S(1)}, bf16[16,2064]{1,0:T(8,128)(2,1)S(1)}, u32[]{:S(2)}, u32[]{:S(2)}) collective-permute-start(bf16[16,2064]{1,0:T(8,128)(2,1)S(1)} %get-tuple-element.33), channel_id=1, source_target_pairs={{0,4},{1,5},{2,6},{3,7},{4,8},{5,9},{6,10},{7,11},{8,12},{9,13},{1... | collective-permute-start | bytes 198152 | tf_op jit(solution)/shard_map/ppermute | solution.py:137
  17.1 2.4 %collective-permute-start.6 = (bf16[16,2064]{1,0:T(8,128)(2,1)S(1)}, bf16[16,2064]{1,0:T(8,128)(2,1)S(1)}, u32[]{:S(2)}, u32[]{:S(2)}) collective-permute-start(bf16[16,2064]{1,0:T(8,128)(2,1)S(1)} %get-tuple-element.33), channel_id=1, source_target_pairs={{0,12},{1,13},{2,14},{3,15},{4,0},{5,1},{6,2},{7,3},{8,4},{9,5},{1... | collective-permute-start | bytes 198152 | tf_op jit(solution)/shard_map/ppermute | solution.py:137
  19.6 2.6 %collective-permute-done.4 = bf16[16,2064]{1,0:T(8,128)(2,1)S(1)} collective-permute-done((bf16[16,2064]{1,0:T(8,128)(2,1)S(1)}, bf16[16,2064]{1,0:T(8,128)(2,1)S(1)}, u32[]{:S(2)}, u32[]{:S(2)}) %collective-permute-start.4) | collective-permute-done | bytes 66080 | tf_op jit(solution)/shard_map/ppermute | solution.py:137
  23.4 1.6 %collective-permute-start.14 = (bf16[32,2048]{1,0:T(8,128)(2,1)S(1)}, bf16[32,2048]{1,0:T(8,128)(2,1)S(1)}, u32[]{:S(2)}, u32[]{:S(2)}) collective-permute-start(bf16[32,2048]{1,0:T(8,128)(2,1)S(1)} %slice.120), channel_id=1, source_target_pairs={{0,2},{1,3},{2,0},{3,1},{4,6},{5,7},{6,4},{7,5},{8,10},{9,11},{10,... | collective-permute-start | bytes 393224 | tf_op jit(solution)/shard_map/ppermute | solution.py:143
  25.0 1.6 %collective-permute-start.15 = (bf16[32,2048]{1,0:T(8,128)(2,1)S(1)}, bf16[32,2048]{1,0:T(8,128)(2,1)S(1)}, u32[]{:S(2)}, u32[]{:S(2)}) collective-permute-start(bf16[32,2048]{1,0:T(8,128)(2,1)S(1)} %slice.121), channel_id=1, source_target_pairs={{0,1},{1,0},{2,3},{3,2},{4,5},{5,4},{6,7},{7,6},{8,9},{9,8},{10,11... | collective-permute-start | bytes 393224 | tf_op jit(solution)/shard_map/ppermute | solution.py:143
  26.6 4.8 %collective-permute-done.7 = bf16[64,2064]{1,0:T(8,128)(2,1)S(1)} collective-permute-done((bf16[64,2064]{1,0:T(8,128)(2,1)S(1)}, bf16[64,2064]{1,0:T(8,128)(2,1)S(1)}, u32[]{:S(2)}, u32[]{:S(2)}) %collective-permute-start.7) | collective-permute-done | bytes 264224 | tf_op jit(solution)/shard_map/ppermute | solution.py:143
  32.2 1.8 %collective-permute-start.10 = (bf16[32,2064]{1,0:T(8,128)(2,1)S(1)}, bf16[32,2064]{1,0:T(8,128)(2,1)S(1)}, u32[]{:S(2)}, u32[]{:S(2)}) collective-permute-start(bf16[32,2064]{1,0:T(8,128)(2,1)S(1)} %slice.117), channel_id=1, source_target_pairs={{0,1},{1,0},{2,3},{3,2},{4,5},{5,4},{6,7},{7,6},{8,9},{9,8},{10,11... | collective-permute-start | bytes 396296 | tf_op jit(solution)/shard_map/ppermute | solution.py:143
  34.2 2.3 %collective-permute-done.9 = bf16[32,2064]{1,0:T(8,128)(2,1)S(1)} collective-permute-done((bf16[32,2064]{1,0:T(8,128)(2,1)S(1)}, bf16[32,2064]{1,0:T(8,128)(2,1)S(1)}, u32[]{:S(2)}, u32[]{:S(2)}) %collective-permute-start.9) | collective-permute-done | bytes 132128 | tf_op jit(solution)/shard_map/ppermute | solution.py:143
  37.9 1.0 %fusion.11 = f32[256,768]{1,0:T(8,128)S(1)} fusion(bf16[256,2048]{1,0:T(8,128)(2,1)S(1)} %constant_dynamic-update-slice_fusion.12.rows, bf16[768,2048]{1,0:T(8,128)(2,1)S(1)} %get-tuple-element.39), kind=kOutput, calls=%fused_computation.46 | convolution fusion | flops 805306368 | bytes 4980736 | tf_op jit(solution)/shard_map/dot_general | solution.py:354
  41.4 1.4 %collective-permute-start.17 = (bf16[32,2048]{1,0:T(8,128)(2,1)S(1)}, bf16[32,2048]{1,0:T(8,128)(2,1)S(1)}, u32[]{:S(2)}, u32[]{:S(2)}) collective-permute-start(bf16[32,2048]{1,0:T(8,128)(2,1)S(1)} %get-tuple-element.65), channel_id=1, source_target_pairs={{0,2},{1,3},{2,0},{3,1},{4,6},{5,7},{6,4},{7,5},{8,10},{9,11},{10,... | collective-permute-start | bytes 393224 | tf_op jit(solution)/shard_map/ppermute | solution.py:143
  44.1 1.1 %collective-permute-start.20 = (bf16[32,2048]{1,0:T(8,128)(2,1)S(1)}, bf16[32,2048]{1,0:T(8,128)(2,1)S(1)}, u32[]{:S(2)}, u32[]{:S(2)}) collective-permute-start(bf16[32,2048]{1,0:T(8,128)(2,1)S(1)} %get-tuple-element.58), channel_id=1, source_target_pairs={{0,1},{1,0},{2,3},{3,2},{4,5},{5,4},{6,7},{7,6},{8,9},{9,8},{10,11... | collective-permute-start | bytes 393224 | tf_op jit(solution)/shard_map/ppermute | solution.py:143
  46.5 1.8 %collective-permute-done.18.other_right_ref = bf16[32,2048]{1,0:T(8,128)(2,1)S(1)} collective-permute-done((bf16[32,2048]{1,0:T(8,128)(2,1)S(1)}, bf16[32,2048]{1,0:T(8,128)(2,1)S(1)}, u32[]{:S(2)}, u32[]{:S(2)}) %collective-permute-start.18) | collective-permute-done | bytes 131104 | tf_op jit(solution)/shard_map/ppermute | solution.py:143
  49.3 2.3 %collective-permute-start.22 = (bf16[32,2048]{1,0:T(8,128)(2,1)S(1)}, bf16[32,2048]{1,0:T(8,128)(2,1)S(1)}, u32[]{:S(2)}, u32[]{:S(2)}) collective-permute-start(bf16[32,2048]{1,0:T(8,128)(2,1)S(1)} %get-tuple-element.44), channel_id=1, source_target_pairs={{0,2},{1,3},{2,0},{3,1},{4,6},{5,7},{6,4},{7,5},{8,10},{9,11},{10,... | collective-permute-start | bytes 393224 | tf_op jit(solution)/shard_map/ppermute | solution.py:143
  51.6 1.8 %collective-permute-done.19 = bf16[32,2048]{1,0:T(8,128)(2,1)S(1)} collective-permute-done((bf16[32,2048]{1,0:T(8,128)(2,1)S(1)}, bf16[32,2048]{1,0:T(8,128)(2,1)S(1)}, u32[]{:S(2)}, u32[]{:S(2)}) %collective-permute-start.19) | collective-permute-done | bytes 131104 | tf_op jit(solution)/shard_map/ppermute | solution.py:143
  53.4 1.1 %collective-permute-done.22 = bf16[32,2048]{1,0:T(8,128)(2,1)S(1)} collective-permute-done((bf16[32,2048]{1,0:T(8,128)(2,1)S(1)}, bf16[32,2048]{1,0:T(8,128)(2,1)S(1)}, u32[]{:S(2)}, u32[]{:S(2)}) %collective-permute-start.22) | collective-permute-done | bytes 131104 | tf_op jit(solution)/shard_map/ppermute | solution.py:143
  55.0 3.5 %collective-permute-start.26 = (bf16[16,2048]{1,0:T(8,128)(2,1)S(1)}, bf16[16,2048]{1,0:T(8,128)(2,1)S(1)}, u32[]{:S(2)}, u32[]{:S(2)}) collective-permute-start(bf16[16,2048]{1,0:T(8,128)(2,1)S(1)} %get-tuple-element.63), channel_id=1, source_target_pairs={{0,12},{1,13},{2,14},{3,15},{4,0},{5,1},{6,2},{7,3},{8,4},{9,5},{1... | collective-permute-start | bytes 196616 | tf_op jit(solution)/shard_map/ppermute | solution.py:137
  58.7 2.5 %shard_map.115 = (bf16[1,192,2048]{2,1,0:T(8,128)(2,1)}, bf16[1,192,2048]{2,1,0:T(8,128)(2,1)}, bf16[1,192,2048]{2,1,0:T(8,128)(2,1)}) custom-call(bf16[256,576]{1,0:T(8,128)(2,1)S(1)} %pad_maximum_fusion.2.own_grads, bf16[256,576]{1,0:T(8,128)(2,1)S(1)} %collective-permute-done.23.other_grads, ...), custom_call_target="tpu_custom_call" | custom-call | bytes 7143424 | tf_op jit(solution)/shard_map/pallas_call | solution.py:156
  61.2 2.7 %collective-permute-done.25 = bf16[16,2048]{1,0:T(8,128)(2,1)S(1)} collective-permute-done((bf16[16,2048]{1,0:T(8,128)(2,1)S(1)}, bf16[16,2048]{1,0:T(8,128)(2,1)S(1)}, u32[]{:S(2)}, u32[]{:S(2)}) %collective-permute-start.25) | collective-permute-done | bytes 65568 | tf_op jit(solution)/shard_map/ppermute | solution.py:137
  (80 shorter events, 12.1 us)
Async XLA Ops:
  0.6 11.9 %collective-permute-start.3 = (bf16[16,2048]{1,0:T(8,128)(2,1)}, bf16[16,2048]{1,0:T(8,128)(2,1)S(1)}, u32[]{:S(2)}, u32[]{:S(2)}) collective-permute-start(bf16[16,2048]{1,0:T(8,128)(2,1)} %tokens_hbm.1), channel_id=1, source_target_pairs={{0,12},{1,13},{2,14},{3,15},{4,0},{5,1},{6,2},{7,3},{8,4},{9,5},{1... | collective-permute-start | bytes 196616 | tf_op jit(solution)/shard_map/ppermute | solution.py:137
  5.7 6.8 %collective-permute-start.2 = (bf16[16,2048]{1,0:T(8,128)(2,1)}, bf16[16,2048]{1,0:T(8,128)(2,1)S(1)}, u32[]{:S(2)}, u32[]{:S(2)}) collective-permute-start(bf16[16,2048]{1,0:T(8,128)(2,1)} %tokens_hbm.1), channel_id=1, source_target_pairs={{0,8},{1,9},{2,10},{3,11},{4,12},{5,13},{6,14},{7,15},{8,0},{9,1},... | collective-permute-start | bytes 196616 | tf_op jit(solution)/shard_map/ppermute | solution.py:137
  5.7 6.8 %collective-permute-start.1 = (bf16[16,2048]{1,0:T(8,128)(2,1)}, bf16[16,2048]{1,0:T(8,128)(2,1)S(1)}, u32[]{:S(2)}, u32[]{:S(2)}) collective-permute-start(bf16[16,2048]{1,0:T(8,128)(2,1)} %tokens_hbm.1), channel_id=1, source_target_pairs={{0,4},{1,5},{2,6},{3,7},{4,8},{5,9},{6,10},{7,11},{8,12},{9,13},{1... | collective-permute-start | bytes 196616 | tf_op jit(solution)/shard_map/ppermute | solution.py:137
  10.6 11.6 %collective-permute-start.5 = (bf16[16,2064]{1,0:T(8,128)(2,1)S(1)}, bf16[16,2064]{1,0:T(8,128)(2,1)S(1)}, u32[]{:S(2)}, u32[]{:S(2)}) collective-permute-start(bf16[16,2064]{1,0:T(8,128)(2,1)S(1)} %get-tuple-element.33), channel_id=1, source_target_pairs={{0,8},{1,9},{2,10},{3,11},{4,12},{5,13},{6,14},{7,15},{8,0},{9,1},... | collective-permute-start | bytes 198152 | tf_op jit(solution)/shard_map/ppermute | solution.py:137
  12.6 10.8 %collective-permute-start.11 = (bf16[64,2048]{1,0:T(8,128)(2,1)S(1)}, bf16[64,2048]{1,0:T(8,128)(2,1)S(1)}, u32[]{:S(2)}, u32[]{:S(2)}) collective-permute-start(bf16[64,2048]{1,0:T(8,128)(2,1)S(1)} %pad_maximum_fusion.3), channel_id=1, source_target_pairs={{0,1},{1,0},{2,3},{3,2},{4,5},{5,4},{6,7},{7,6},{8,9},{9,8},{10,11... | collective-permute-start | bytes 786440 | tf_op jit(solution)/shard_map/ppermute | solution.py:143
  14.1 10.8 %collective-permute-start.13 = (bf16[64,2048]{1,0:T(8,128)(2,1)S(1)}, bf16[64,2048]{1,0:T(8,128)(2,1)S(1)}, u32[]{:S(2)}, u32[]{:S(2)}) collective-permute-start(bf16[64,2048]{1,0:T(8,128)(2,1)S(1)} %pad_maximum_fusion.3), channel_id=1, source_target_pairs={{0,2},{1,3},{2,0},{3,1},{4,6},{5,7},{6,4},{7,5},{8,10},{9,11},{10,... | collective-permute-start | bytes 786440 | tf_op jit(solution)/shard_map/ppermute | solution.py:143
  15.7 6.5 %collective-permute-start.4 = (bf16[16,2064]{1,0:T(8,128)(2,1)S(1)}, bf16[16,2064]{1,0:T(8,128)(2,1)S(1)}, u32[]{:S(2)}, u32[]{:S(2)}) collective-permute-start(bf16[16,2064]{1,0:T(8,128)(2,1)S(1)} %get-tuple-element.33), channel_id=1, source_target_pairs={{0,4},{1,5},{2,6},{3,7},{4,8},{5,9},{6,10},{7,11},{8,12},{9,13},{1... | collective-permute-start | bytes 198152 | tf_op jit(solution)/shard_map/ppermute | solution.py:137
  17.1 5.1 %collective-permute-start.6 = (bf16[16,2064]{1,0:T(8,128)(2,1)S(1)}, bf16[16,2064]{1,0:T(8,128)(2,1)S(1)}, u32[]{:S(2)}, u32[]{:S(2)}) collective-permute-start(bf16[16,2064]{1,0:T(8,128)(2,1)S(1)} %get-tuple-element.33), channel_id=1, source_target_pairs={{0,12},{1,13},{2,14},{3,15},{4,0},{5,1},{6,2},{7,3},{8,4},{9,5},{1... | collective-permute-start | bytes 198152 | tf_op jit(solution)/shard_map/ppermute | solution.py:137
  22.3 9.1 %collective-permute-start.7 = (bf16[64,2064]{1,0:T(8,128)(2,1)S(1)}, bf16[64,2064]{1,0:T(8,128)(2,1)S(1)}, u32[]{:S(2)}, u32[]{:S(2)}) collective-permute-start(bf16[64,2064]{1,0:T(8,128)(2,1)S(1)} %get-tuple-element.72), channel_id=1, source_target_pairs={{0,1},{1,0},{2,3},{3,2},{4,5},{5,4},{6,7},{7,6},{8,9},{9,8},{10,11... | collective-permute-start | bytes 792584 | tf_op jit(solution)/shard_map/ppermute | solution.py:143
  22.9 9.3 %collective-permute-start.8 = (bf16[64,2064]{1,0:T(8,128)(2,1)S(1)}, bf16[64,2064]{1,0:T(8,128)(2,1)S(1)}, u32[]{:S(2)}, u32[]{:S(2)}) collective-permute-start(bf16[64,2064]{1,0:T(8,128)(2,1)S(1)} %get-tuple-element.72), channel_id=1, source_target_pairs={{0,2},{1,3},{2,0},{3,1},{4,6},{5,7},{6,4},{7,5},{8,10},{9,11},{10,... | collective-permute-start | bytes 792584 | tf_op jit(solution)/shard_map/ppermute | solution.py:143
  23.4 10.7 %collective-permute-start.14 = (bf16[32,2048]{1,0:T(8,128)(2,1)S(1)}, bf16[32,2048]{1,0:T(8,128)(2,1)S(1)}, u32[]{:S(2)}, u32[]{:S(2)}) collective-permute-start(bf16[32,2048]{1,0:T(8,128)(2,1)S(1)} %slice.120), channel_id=1, source_target_pairs={{0,2},{1,3},{2,0},{3,1},{4,6},{5,7},{6,4},{7,5},{8,10},{9,11},{10,... | collective-permute-start | bytes 393224 | tf_op jit(solution)/shard_map/ppermute | solution.py:143
  25.0 9.1 %collective-permute-start.15 = (bf16[32,2048]{1,0:T(8,128)(2,1)S(1)}, bf16[32,2048]{1,0:T(8,128)(2,1)S(1)}, u32[]{:S(2)}, u32[]{:S(2)}) collective-permute-start(bf16[32,2048]{1,0:T(8,128)(2,1)S(1)} %slice.121), channel_id=1, source_target_pairs={{0,1},{1,0},{2,3},{3,2},{4,5},{5,4},{6,7},{7,6},{8,9},{9,8},{10,11... | collective-permute-start | bytes 393224 | tf_op jit(solution)/shard_map/ppermute | solution.py:143
  26.6 11.0 %collective-permute-start.12 = (bf16[576,2048]{1,0:T(8,128)(2,1)S(1)}, bf16[576,2048]{1,0:T(8,128)(2,1)S(1)}, u32[]{:S(2)}, u32[]{:S(2)}) collective-permute-start(bf16[576,2048]{1,0:T(8,128)(2,1)S(1)} %pad_maximum_fusion.own_ref), channel_id=1, source_target_pairs={{0,16},{16,0},{1,17},{17,1},{2,18},{18,2},{3,19},{19,3},{4,20},{20... | collective-permute-start | bytes 7077896 | tf_op jit(solution)/shard_map/ppermute | solution.py:133
  31.4 5.1 %collective-permute-start.9 = (bf16[32,2064]{1,0:T(8,128)(2,1)S(1)}, bf16[32,2064]{1,0:T(8,128)(2,1)S(1)}, u32[]{:S(2)}, u32[]{:S(2)}) collective-permute-start(bf16[32,2064]{1,0:T(8,128)(2,1)S(1)} %slice.116), channel_id=1, source_target_pairs={{0,2},{1,3},{2,0},{3,1},{4,6},{5,7},{6,4},{7,5},{8,10},{9,11},{10,... | collective-permute-start | bytes 396296 | tf_op jit(solution)/shard_map/ppermute | solution.py:143
  32.2 5.1 %collective-permute-start.10 = (bf16[32,2064]{1,0:T(8,128)(2,1)S(1)}, bf16[32,2064]{1,0:T(8,128)(2,1)S(1)}, u32[]{:S(2)}, u32[]{:S(2)}) collective-permute-start(bf16[32,2064]{1,0:T(8,128)(2,1)S(1)} %slice.117), channel_id=1, source_target_pairs={{0,1},{1,0},{2,3},{3,2},{4,5},{5,4},{6,7},{7,6},{8,9},{9,8},{10,11... | collective-permute-start | bytes 396296 | tf_op jit(solution)/shard_map/ppermute | solution.py:143
  34.2 7.2 %collective-permute-start.16 = (bf16[256,2048]{1,0:T(8,128)(2,1)S(1)}, bf16[256,2048]{1,0:T(8,128)(2,1)S(1)}, u32[]{:S(2)}, u32[]{:S(2)}) collective-permute-start(bf16[256,2048]{1,0:T(8,128)(2,1)S(1)} %constant_dynamic-update-slice_fusion.12.rows), channel_id=1, source_target_pairs={{0,16},{16,0},{1,17},{17,1},{2,18},{18,2},{3,19},{19,3},{4,20},{20... | collective-permute-start | bytes 3145736 | tf_op jit(solution)/shard_map/ppermute | solution.py:133
  42.8 5.5 %collective-permute-start.18 = (bf16[32,2048]{1,0:T(8,128)(2,1)S(1)}, bf16[32,2048]{1,0:T(8,128)(2,1)S(1)}, u32[]{:S(2)}, u32[]{:S(2)}) collective-permute-start(bf16[32,2048]{1,0:T(8,128)(2,1)S(1)} %get-tuple-element.64), channel_id=1, source_target_pairs={{0,1},{1,0},{2,3},{3,2},{4,5},{5,4},{6,7},{7,6},{8,9},{9,8},{10,11... | collective-permute-start | bytes 393224 | tf_op jit(solution)/shard_map/ppermute | solution.py:143
  44.0 10.6 %collective-permute-start.24 = (bf16[256,2048]{1,0:T(8,128)(2,1)S(1)}, bf16[256,2048]{1,0:T(8,128)(2,1)S(1)}, u32[]{:S(2)}, u32[]{:S(2)}) collective-permute-start(bf16[256,2048]{1,0:T(8,128)(2,1)S(1)} %slice.119.upstream), channel_id=1, source_target_pairs={{0,16},{16,0},{1,17},{17,1},{2,18},{18,2},{3,19},{19,3},{4,20},{20... | collective-permute-start | bytes 3145736 | tf_op jit(solution)/shard_map/ppermute | solution.py:133
  44.1 7.4 %collective-permute-start.20 = (bf16[32,2048]{1,0:T(8,128)(2,1)S(1)}, bf16[32,2048]{1,0:T(8,128)(2,1)S(1)}, u32[]{:S(2)}, u32[]{:S(2)}) collective-permute-start(bf16[32,2048]{1,0:T(8,128)(2,1)S(1)} %get-tuple-element.58), channel_id=1, source_target_pairs={{0,1},{1,0},{2,3},{3,2},{4,5},{5,4},{6,7},{7,6},{8,9},{9,8},{10,11... | collective-permute-start | bytes 393224 | tf_op jit(solution)/shard_map/ppermute | solution.py:143
  45.3 6.3 %collective-permute-start.21 = (bf16[32,2048]{1,0:T(8,128)(2,1)S(1)}, bf16[32,2048]{1,0:T(8,128)(2,1)S(1)}, u32[]{:S(2)}, u32[]{:S(2)}) collective-permute-start(bf16[32,2048]{1,0:T(8,128)(2,1)S(1)} %get-tuple-element.57), channel_id=1, source_target_pairs={{0,2},{1,3},{2,0},{3,1},{4,6},{5,7},{6,4},{7,5},{8,10},{9,11},{10,... | collective-permute-start | bytes 393224 | tf_op jit(solution)/shard_map/ppermute | solution.py:143
  49.3 5.3 %collective-permute-start.22 = (bf16[32,2048]{1,0:T(8,128)(2,1)S(1)}, bf16[32,2048]{1,0:T(8,128)(2,1)S(1)}, u32[]{:S(2)}, u32[]{:S(2)}) collective-permute-start(bf16[32,2048]{1,0:T(8,128)(2,1)S(1)} %get-tuple-element.44), channel_id=1, source_target_pairs={{0,2},{1,3},{2,0},{3,1},{4,6},{5,7},{6,4},{7,5},{8,10},{9,11},{10,... | collective-permute-start | bytes 393224 | tf_op jit(solution)/shard_map/ppermute | solution.py:143
  54.7 6.5 %collective-permute-start.27 = (bf16[16,2048]{1,0:T(8,128)(2,1)S(1)}, bf16[16,2048]{1,0:T(8,128)(2,1)S(1)}, u32[]{:S(2)}, u32[]{:S(2)}) collective-permute-start(bf16[16,2048]{1,0:T(8,128)(2,1)S(1)} %get-tuple-element.62), channel_id=1, source_target_pairs={{0,4},{1,5},{2,6},{3,7},{4,8},{5,9},{6,10},{7,11},{8,12},{9,13},{1... | collective-permute-start | bytes 196616 | tf_op jit(solution)/shard_map/ppermute | solution.py:137
  55.0 6.1 %collective-permute-start.26 = (bf16[16,2048]{1,0:T(8,128)(2,1)S(1)}, bf16[16,2048]{1,0:T(8,128)(2,1)S(1)}, u32[]{:S(2)}, u32[]{:S(2)}) collective-permute-start(bf16[16,2048]{1,0:T(8,128)(2,1)S(1)} %get-tuple-element.63), channel_id=1, source_target_pairs={{0,12},{1,13},{2,14},{3,15},{4,0},{5,1},{6,2},{7,3},{8,4},{9,5},{1... | collective-permute-start | bytes 196616 | tf_op jit(solution)/shard_map/ppermute | solution.py:137
  58.6 5.3 %collective-permute-start.25 = (bf16[16,2048]{1,0:T(8,128)(2,1)S(1)}, bf16[16,2048]{1,0:T(8,128)(2,1)S(1)}, u32[]{:S(2)}, u32[]{:S(2)}) collective-permute-start(bf16[16,2048]{1,0:T(8,128)(2,1)S(1)} %get-tuple-element.61), channel_id=1, source_target_pairs={{0,8},{1,9},{2,10},{3,11},{4,12},{5,13},{6,14},{7,15},{8,0},{9,1},... | collective-permute-start | bytes 196616 | tf_op jit(solution)/shard_map/ppermute | solution.py:137
  (7 other events, 23.2 us)
